TPU v7x, 32 devices: a whole 2x2x4 slice. The times are simulated.
32 devices in a mesh: vintage: 2 (over core), tile: 16 (over z, y, x).
Axes of the slice: x: 2, y: 2, z: 4, core: 2. Of those that a mesh axis runs over, the one named last changes fastest.
Arguments:
- patches: bfloat16 [2, 8192, 768], P('vintage', 'tile'), may hold values from -16 to 16, as said below
- out_grad: bfloat16 [2, 8192, 768], P('vintage', 'tile'), may hold values from -6 to 6
- w_query: bfloat16 [768, 768], replicated, may hold values from -0.21875 to 0.21875
- w_key: bfloat16 [768, 256], replicated, may hold values from -0.21875 to 0.21875
- w_value: bfloat16 [768, 256], replicated, may hold values from -0.21875 to 0.21875
- w_out: bfloat16 [768, 768], replicated, may hold values from -0.21875 to 0.21875
- key_tiles: int32 [2, 64, 4], P('vintage'), may hold values from 0 to 15, all different within a row; in each aligned block of 4 rows (0 to 3, 4 to 7, ..., all dimensions but the last counted through in order) at most 2 rows name the same one
- key_blocks: int32 [2, 64, 4], P('vintage'), may hold values from 0 to 3
Outputs:
- layer_out: bfloat16 [2, 8192, 768], P('vintage', 'tile')
- input_grad: bfloat16 [2, 8192, 768], P('vintage', 'tile')
Inputs may be any that keep to these rules, and one draw needn't show every extreme that they name: `patches`: patch features of order one, rows of differing scale possible. `key_tiles`: the 4 tiles of one query block's list differ; over the 4 query blocks of one tile no key tile is named more than 2 times, and in every draw some tile is named exactly 2 times by some tile's blocks.
All inputs are finite; a program needn't handle non-finite values.
Results may differ from a plain program's by a relative error of at most 0.012.
The roundings to bfloat16 on the way count: a program that leaves them out, or rounds other values in their place, can miss the bound.
Values may be sent and summed in bfloat16 or wider, within the bound.
No kernel may reach another device: no remote copies, remote signals or barrier semaphores. Data moves between devices by JAX's collectives and lax.ppermute only.
A program may use at most 128 MiB of HBM per device.

v0:
```python
import jax
import jax.numpy as jnp
from jax import lax
from jax.sharding import PartitionSpec as P

HEADS = 12
KV_HEADS = 4
HEAD_DIM = 64
BLK = 128
CAP = 2


EPSILON = 1e-06


def from_partner(value, axis, bit):
    return lax.ppermute(value, axis, [(i, i ^ 1 << bit) for i in range(lax.axis_size(axis))])


def block_work(query_rows, grad_rows, key_value, w_out):
    kv_width = KV_HEADS * HEAD_DIM
    group_size = HEADS // KV_HEADS
    temper = HEAD_DIM ** (-0.5)
    row_count = query_rows.shape[0]
    keys_low = key_value[:, :kv_width].reshape(-1, KV_HEADS, HEAD_DIM)
    values_low = key_value[:, kv_width:].reshape(-1, KV_HEADS, HEAD_DIM)
    query_low = query_rows.reshape(row_count, KV_HEADS, group_size, HEAD_DIM)
    scores = (
        jnp.einsum("igrd,ngd->grin", query_low, keys_low, preferred_element_type=jnp.float32)
        * temper
    )
    peak = jnp.max(scores, axis=-1, keepdims=True)
    expo = jnp.exp(scores - peak)
    probs = expo / jnp.sum(expo, axis=-1, keepdims=True)
    probs_low = probs.astype(jnp.bfloat16)
    attended = jnp.einsum(
        "grin,ngd->igrd", probs_low, values_low, preferred_element_type=jnp.float32
    )
    attended = attended.reshape(row_count, HEADS * HEAD_DIM).astype(jnp.bfloat16)
    attended_f = attended.astype(jnp.float32)
    root_mean = jnp.sqrt(jnp.mean(attended_f * attended_f, axis=-1, keepdims=True) + EPSILON)
    normed = attended_f / root_mean
    layer_rows = jnp.dot(
        normed.astype(jnp.bfloat16), w_out, preferred_element_type=jnp.float32
    ).astype(jnp.bfloat16)
    normed_grad = jnp.dot(grad_rows, w_out.T, preferred_element_type=jnp.float32)
    attended_grad = (
        normed_grad - normed * jnp.mean(normed_grad * normed, axis=-1, keepdims=True)
    ) / root_mean
    attended_grad = attended_grad.astype(jnp.bfloat16).reshape(
        row_count, KV_HEADS, group_size, HEAD_DIM
    )
    prob_grad = jnp.einsum(
        "igrd,ngd->grin", attended_grad, values_low, preferred_element_type=jnp.float32
    )
    row_dot = jnp.sum(probs * prob_grad, axis=-1, keepdims=True)
    score_grad = (probs * (prob_grad - row_dot) * temper).astype(jnp.bfloat16)
    query_grad = jnp.einsum(
        "grin,ngd->igrd", score_grad, keys_low, preferred_element_type=jnp.float32
    )
    query_grad = query_grad.reshape(row_count, HEADS * HEAD_DIM).astype(jnp.bfloat16)
    key_part = jnp.einsum(
        "grin,igrd->ngd", score_grad, query_low, preferred_element_type=jnp.float32
    )
    value_part = jnp.einsum(
        "grin,igrd->ngd", probs_low, attended_grad, preferred_element_type=jnp.float32
    )
    parts = jnp.concatenate(
        [key_part.reshape(-1, kv_width), value_part.reshape(-1, kv_width)], axis=-1
    )
    return (layer_rows, query_grad, parts.astype(jnp.bfloat16).reshape(-1, row_count, 2 * kv_width))


def slot_index(entry_tiles, tile_count):
    one_hot = (entry_tiles[:, None] == jnp.arange(tile_count, dtype=jnp.int32)[None, :]).astype(
        jnp.int32
    )
    ranks = jnp.cumsum(one_hot, axis=0) - 1
    return jnp.sum(one_hot * ranks, axis=1)


def shards(patches, out_grad, w_query, w_key, w_value, w_out, key_tiles, key_blocks):
    tokens = patches[0]
    grads_in = out_grad[0]
    kv_width = KV_HEADS * HEAD_DIM
    tile_count = lax.axis_size("tile")
    my_tile = lax.axis_index("tile")
    block_count = tokens.shape[0] // BLK
    list_len = key_tiles.shape[2]
    entry_count = block_count * list_len
    queries = jnp.dot(tokens, w_query, preferred_element_type=jnp.float32).astype(jnp.bfloat16)
    keys = jnp.dot(tokens, w_key, preferred_element_type=jnp.float32).astype(jnp.bfloat16)
    values = jnp.dot(tokens, w_value, preferred_element_type=jnp.float32).astype(jnp.bfloat16)
    local_kv = jnp.concatenate([keys, values], axis=-1)
    partner = from_partner(local_kv, "vintage", 0)
    partner_blocks = partner.reshape(block_count, BLK, 2 * kv_width)
    my_tiles = lax.dynamic_slice_in_dim(
        key_tiles[0], my_tile * block_count, block_count, 0
    ).reshape(-1)
    my_slots = slot_index(my_tiles, tile_count)
    flat_slot = my_tiles * CAP + my_slots
    slot_range = jnp.arange(CAP, dtype=jnp.int32)
    all_tiles = key_tiles[0].reshape(tile_count, entry_count)
    all_blocks = key_blocks[0].reshape(tile_count, entry_count)
    asking = (all_tiles == my_tile).astype(jnp.int32)
    ranks = jnp.cumsum(asking, axis=1) - 1
    hits = (asking[:, :, None] == 1) & (ranks[:, :, None] == slot_range[None, None, :])
    wanted = jnp.sum(jnp.where(hits, all_blocks[:, :, None] + 1, 0), axis=1) - 1
    picked = partner_blocks[jnp.clip(wanted, 0, block_count - 1)]
    send_kv = jnp.where((wanted >= 0)[:, :, None, None], picked, jnp.zeros_like(picked))
    arrived = lax.all_to_all(send_kv, "tile", split_axis=0, concat_axis=0, tiled=True)
    entries = arrived.reshape(tile_count * CAP, BLK, 2 * kv_width)[flat_slot]
    entries = entries.reshape(block_count, list_len * BLK, 2 * kv_width)

    def per_block(item):
        query_rows, grad_rows, key_value = item
        return block_work(query_rows, grad_rows, key_value, w_out)

    layer_rows, query_grad, parts = lax.map(
        per_block,
        (
            queries.reshape(block_count, BLK, HEADS * HEAD_DIM),
            grads_in.reshape(block_count, BLK, tokens.shape[1]),
            entries,
        ),
    )
    parts = parts.reshape(entry_count, BLK, 2 * kv_width)
    back_send = (
        jnp.zeros((tile_count * CAP, BLK, 2 * kv_width), jnp.bfloat16).at[flat_slot].set(parts)
    )
    returned = lax.all_to_all(
        back_send.reshape(tile_count, CAP, BLK, 2 * kv_width),
        "tile",
        split_axis=0,
        concat_axis=0,
        tiled=True,
    )
    owner_hot = (
        wanted.reshape(-1)[:, None] == jnp.arange(block_count, dtype=jnp.int32)[None, :]
    ).astype(jnp.bfloat16)
    summed = jnp.einsum(
        "sj,snf->jnf",
        owner_hot,
        returned.reshape(tile_count * CAP, BLK, 2 * kv_width),
        preferred_element_type=jnp.float32,
    )
    kv_grad = summed.astype(jnp.bfloat16).reshape(tokens.shape[0], 2 * kv_width)
    away_term = jnp.dot(
        kv_grad[:, :kv_width], w_key.T, preferred_element_type=jnp.float32
    ) + jnp.dot(kv_grad[:, kv_width:], w_value.T, preferred_element_type=jnp.float32)
    kv_term = from_partner(away_term.astype(jnp.bfloat16), "vintage", 0).astype(away_term.dtype)
    query_rows_all = query_grad.reshape(tokens.shape[0], HEADS * HEAD_DIM)
    input_grad = (
        jnp.dot(query_rows_all, w_query.T, preferred_element_type=jnp.float32) + kv_term
    ).astype(jnp.bfloat16)
    layer_out = layer_rows.reshape(tokens.shape[0], tokens.shape[1])
    return (layer_out[None], input_grad[None])


def solution(mesh):
    in_specs = (
        P("vintage", "tile", None),
        P("vintage", "tile", None),
        P(),
        P(),
        P(),
        P(),
        P("vintage", None, None),
        P("vintage", None, None),
    )
    out_specs = (P("vintage", "tile", None), P("vintage", "tile", None))
    return jax.shard_map(shards, mesh=mesh, in_specs=in_specs, out_specs=out_specs, check_vma=False)
```

profile of v0, /device:TPU:15, one launch (start us, length us, event | category | flops | bytes accessed | tf_op | source)
XLA Modules:
  0.0 383.4 jit_solution(16986560840301869226)
XLA Ops:
  0.7 1.7 convolution_convert_fusion.5
  6.6 2.7 gather_fusion
  9.3 4.5 %broadcast_select_fusion = bf16[16,2,128,512]{3,2,1,0:T(8,128)(2,1)} fusion(bf16[16,2,128,512]{3,2,1,0:T(8,128)(2,1)} %bitcast.216, pred[16,2]{1,0:T(8,128)(4,1)S(1)} %copy.72), kind=kLoop, calls=%fused_computation.56 | loop fusion | flops 2097152 | bytes 8388640 | tf_op jit(solution)/shard_map/jit(_where)/select_n | solution.py:110
  13.8 6.7 %all-to-all-start = ((bf16[16,2,128,512]{3,2,1,0:T(8,128)(2,1)}), bf16[16,2,128,512]{3,2,1,0:T(8,128)(2,1)}, u32[]{:S(2)}, u32[]{:S(2)}) async-start(bf16[16,2,128,512]{3,2,1,0:T(8,128)(2,1)} %broadcast_select_fusion), calls=%async_computation | async-start | bytes 8388608 | tf_op jit(solution)/shard_map/all_to_all | solution.py:111
  23.0 92.6 %all-to-all-done = bf16[16,2,128,512]{3,2,1,0:T(8,128)(2,1)} async-done(((bf16[16,2,128,512]{3,2,1,0:T(8,128)(2,1)}), bf16[16,2,128,512]{3,2,1,0:T(8,128)(2,1)}, u32[]{:S(2)}, u32[]{:S(2)}) %all-to-all-start) | async-done | bytes 4194336 | tf_op jit(solution)/shard_map/all_to_all | solution.py:111
  115.6 4.2 %gather_fusion.1 = bf16[16,128,512]{2,1,0:T(8,128)(2,1)} fusion(bf16[32,128,512]{2,1,0:T(8,128)(2,1)} %bitcast.31, s32[1024]{0:T(1024)S(1)} %pad_clamp_fusion), kind=kCustom, calls=%fused_computation.1 | custom fusion | bytes 4194368 | tf_op jit(solution)/shard_map/gather | solution.py:112
  119.9 124.5 %while.14 = (s32[]{:T(128)}, bf16[4,128,768]{2,1,0:T(8,128)(2,1)}, bf16[4,128,768]{2,1,0:T(8,128)(2,1)}, bf16[4,4,128,512]{3,2,1,0:T(8,128)(2,1)}, bf16[4,512,51...) while((s32[]{:T(128)}, bf16[4,128,768]{2,1,0:T(8,128)(2,1)}, ...), condition=%wide.region_10.11_spmd, body=%wide.region_4.10_spmd.sunk | while | flops 924586624 | bytes 43158652 | solution.py:119
  122.3 2.7 fusion.105
  125.0 2.3 multiply_reduce_fusion.4
  127.5 2.0 multiply_reduce_fusion.5
  129.9 2.5 fusion.109
  132.5 2.3 fusion.106
  134.8 2.3 fusion.107
  137.1 5.7 %fusion.108 = bf16[4,64,3,128]{3,1,2,0:T(8,128)(2,1)S(1)} fusion(bf16[512,4,64,1]{0,2,3,1:T(8,128)(2,1)S(1)} %bitcast.220, f32[4,512,128,3]{2,1,3,0:T(8,128)} %fusion.107, f32[4,3,128,512]{2,3,1,0:T(8,128)} %get-tuple-element.166, f32[4,3,128]{2,1,0:T(4,128)S(1)} %get-tuple-element.167), kind=kOutput, calls=%fused_computation.24.clone.1 | convolution fusion | flops 106268672 | bytes 6756352 | tf_op jit(solution)/shard_map/while/body/eval_jaxpr/grin,ngd->igrd/dot_general | solution.py:58
  142.8 5.7 %fusion.110 = bf16[512,4,64]{0,2,1:T(8,128)(2,1)S(1)} fusion(bf16[128,4,3,64]{0,3,2,1:T(8,128)(2,1)S(1)} %bitcast.222, f32[4,512,128,3]{2,1,3,0:T(8,128)} %fusion.107, f32[4,3,128,512]{2,3,1,0:T(8,128)} %get-tuple-element.166, f32[4,3,128]{2,1,0:T(4,128)S(1)} %get-tuple-element.167), kind=kOutput, calls=%fused_computation.28.clone.1 | convolution fusion | flops 106301440 | bytes 6756352 | tf_op jit(solution)/shard_map/while/body/eval_jaxpr/grin,igrd->ngd/dot_general | solution.py:62
  153.4 2.7 fusion.105
  156.2 2.3 multiply_reduce_fusion.4
  158.7 2.0 multiply_reduce_fusion.5
  161.0 2.5 fusion.109
  163.6 2.3 fusion.106
  165.9 2.3 fusion.107
  168.3 5.7 %fusion.108 = bf16[4,64,3,128]{3,1,2,0:T(8,128)(2,1)S(1)} fusion(bf16[512,4,64,1]{0,2,3,1:T(8,128)(2,1)S(1)} %bitcast.220, f32[4,512,128,3]{2,1,3,0:T(8,128)} %fusion.107, f32[4,3,128,512]{2,3,1,0:T(8,128)} %get-tuple-element.166, f32[4,3,128]{2,1,0:T(4,128)S(1)} %get-tuple-element.167), kind=kOutput, calls=%fused_computation.24.clone.1 | convolution fusion | flops 106268672 | bytes 6756352 | tf_op jit(solution)/shard_map/while/body/eval_jaxpr/grin,ngd->igrd/dot_general | solution.py:58
  173.9 5.7 %fusion.110 = bf16[512,4,64]{0,2,1:T(8,128)(2,1)S(1)} fusion(bf16[128,4,3,64]{0,3,2,1:T(8,128)(2,1)S(1)} %bitcast.222, f32[4,512,128,3]{2,1,3,0:T(8,128)} %fusion.107, f32[4,3,128,512]{2,3,1,0:T(8,128)} %get-tuple-element.166, f32[4,3,128]{2,1,0:T(4,128)S(1)} %get-tuple-element.167), kind=kOutput, calls=%fused_computation.28.clone.1 | convolution fusion | flops 106301440 | bytes 6756352 | tf_op jit(solution)/shard_map/while/body/eval_jaxpr/grin,igrd->ngd/dot_general | solution.py:62
  184.6 2.7 fusion.105
  187.3 2.3 multiply_reduce_fusion.4
  189.8 2.0 multiply_reduce_fusion.5
  192.2 2.5 fusion.109
  194.8 2.3 fusion.106
  197.1 2.3 fusion.107
  199.4 5.7 %fusion.108 = bf16[4,64,3,128]{3,1,2,0:T(8,128)(2,1)S(1)} fusion(bf16[512,4,64,1]{0,2,3,1:T(8,128)(2,1)S(1)} %bitcast.220, f32[4,512,128,3]{2,1,3,0:T(8,128)} %fusion.107, f32[4,3,128,512]{2,3,1,0:T(8,128)} %get-tuple-element.166, f32[4,3,128]{2,1,0:T(4,128)S(1)} %get-tuple-element.167), kind=kOutput, calls=%fused_computation.24.clone.1 | convolution fusion | flops 106268672 | bytes 6756352 | tf_op jit(solution)/shard_map/while/body/eval_jaxpr/grin,ngd->igrd/dot_general | solution.py:58
  205.1 5.7 %fusion.110 = bf16[512,4,64]{0,2,1:T(8,128)(2,1)S(1)} fusion(bf16[128,4,3,64]{0,3,2,1:T(8,128)(2,1)S(1)} %bitcast.222, f32[4,512,128,3]{2,1,3,0:T(8,128)} %fusion.107, f32[4,3,128,512]{2,3,1,0:T(8,128)} %get-tuple-element.166, f32[4,3,128]{2,1,0:T(4,128)S(1)} %get-tuple-element.167), kind=kOutput, calls=%fused_computation.28.clone.1 | convolution fusion | flops 106301440 | bytes 6756352 | tf_op jit(solution)/shard_map/while/body/eval_jaxpr/grin,igrd->ngd/dot_general | solution.py:62
  215.7 2.7 fusion.105
  218.4 2.3 multiply_reduce_fusion.4
  220.9 2.0 multiply_reduce_fusion.5
  223.2 2.5 fusion.109
  225.9 2.3 fusion.106
  228.2 2.3 fusion.107
  230.5 5.7 %fusion.108 = bf16[4,64,3,128]{3,1,2,0:T(8,128)(2,1)S(1)} fusion(bf16[512,4,64,1]{0,2,3,1:T(8,128)(2,1)S(1)} %bitcast.220, f32[4,512,128,3]{2,1,3,0:T(8,128)} %fusion.107, f32[4,3,128,512]{2,3,1,0:T(8,128)} %get-tuple-element.166, f32[4,3,128]{2,1,0:T(4,128)S(1)} %get-tuple-element.167), kind=kOutput, calls=%fused_computation.24.clone.1 | convolution fusion | flops 106268672 | bytes 6756352 | tf_op jit(solution)/shard_map/while/body/eval_jaxpr/grin,ngd->igrd/dot_general | solution.py:58
  236.2 5.7 %fusion.110 = bf16[512,4,64]{0,2,1:T(8,128)(2,1)S(1)} fusion(bf16[128,4,3,64]{0,3,2,1:T(8,128)(2,1)S(1)} %bitcast.222, f32[4,512,128,3]{2,1,3,0:T(8,128)} %fusion.107, f32[4,3,128,512]{2,3,1,0:T(8,128)} %get-tuple-element.166, f32[4,3,128]{2,1,0:T(4,128)S(1)} %get-tuple-element.167), kind=kOutput, calls=%fused_computation.28.clone.1 | convolution fusion | flops 106301440 | bytes 6756352 | tf_op jit(solution)/shard_map/while/body/eval_jaxpr/grin,igrd->ngd/dot_general | solution.py:62
  244.3 2.4 broadcast_in_dim.58
  246.7 5.2 %scatter_fusion = bf16[32,128,512]{2,1,0:T(8,128)(2,1)} fusion(bf16[32,128,512]{2,1,0:T(8,128)(2,1)} %broadcast_in_dim.58, s32[16]{0:T(128)S(1)} %fusion.49, bf16[16,128,512]{2,1,0:T(8,128)(2,1)S(1)} %bitcast.224), kind=kCustom, calls=%fused_computation.2 | custom fusion | bytes 6291520 | tf_op jit(solution)/shard_map/scatter | solution.py:129
  251.9 8.5 %copy.83 = bf16[16,2,128,512]{3,1,2,0:T(2,128)(2,1)} copy(bf16[16,2,128,512]{3,2,1,0:T(8,128)(2,1)} %bitcast.211) | data formatting | bytes 8388608 | tf_op jit(solution)/shard_map/reshape | solution.py:132
  260.4 4.6 %all-to-all-start.1 = ((bf16[16,2,128,512]{3,1,2,0:T(2,128)(2,1)}), bf16[16,2,128,512]{3,1,2,0:T(2,128)(2,1)}, u32[]{:S(2)}, u32[]{:S(2)}) async-start(bf16[16,2,128,512]{3,1,2,0:T(2,128)(2,1)} %copy.83), calls=%async_computation.1 | async-start | bytes 8388608 | tf_op jit(solution)/shard_map/all_to_all | solution.py:131
  265.2 93.1 %all-to-all-done.1 = bf16[16,2,128,512]{3,1,2,0:T(2,128)(2,1)} async-done(((bf16[16,2,128,512]{3,1,2,0:T(2,128)(2,1)}), bf16[16,2,128,512]{3,1,2,0:T(2,128)(2,1)}, u32[]{:S(2)}, u32[]{:S(2)}) %all-to-all-start.1) | async-done | bytes 4194336 | tf_op jit(solution)/shard_map/all_to_all | solution.py:131
  358.3 8.9 %copy.84 = bf16[16,2,128,512]{3,1,0,2:T(2,128)(2,1)} copy(bf16[16,2,128,512]{3,1,2,0:T(2,128)(2,1)} %all-to-all-done.1) | data formatting | bytes 8388608 | tf_op jit(solution)/shard_map/all_to_all | solution.py:131
  367.2 7.2 %reshape.220 = bf16[32,128,512]{2,0,1:T(8,128)(2,1)} reshape(bf16[16,2,128,512]{3,1,0,2:T(2,128)(2,1)} %copy.84) | data formatting | bytes 8388608 | tf_op jit(solution)/shard_map/reshape | solution.py:144
  374.4 2.9 convolution_convert_fusion.3
  379.8 1.9 collective-permute-done.1
  (127 shorter events, 32.6 us)
Async XLA Ops:
  0.6 20.7 %copy-start = (bf16[768,768]{1,0:T(8,128)(2,1)S(1)}, bf16[768,768]{1,0:T(8,128)(2,1)}, u32[]{:S(2)}) copy-start(bf16[768,768]{1,0:T(8,128)(2,1)} %param.12) | copy-start | bytes 3538948
  0.6 4.2 %copy-start.6 = (s32[1,64,4]{1,2,0:T(4,128)S(1)}, s32[1,64,4]{1,2,0:T(4,128)}, u32[]{:S(2)}) copy-start(s32[1,64,4]{1,2,0:T(4,128)} %param.17) | copy-start | bytes 3076
  0.7 4.4 %copy-start.5 = (s32[1,64,4]{1,2,0:T(4,128)S(1)}, s32[1,64,4]{1,2,0:T(4,128)}, u32[]{:S(2)}) copy-start(s32[1,64,4]{1,2,0:T(4,128)} %param.16) | copy-start | bytes 3076
  4.1 2.3 collective-permute-start
  13.8 7.5 %copy-start.1 = (bf16[1,512,768]{2,1,0:T(8,128)(2,1)S(1)}, bf16[1,512,768]{2,1,0:T(8,128)(2,1)}, u32[]{:S(2)}) copy-start(bf16[1,512,768]{2,1,0:T(8,128)(2,1)} %param.10) | copy-start | bytes 2359300
  13.8 101.8 %all-to-all-start = ((bf16[16,2,128,512]{3,2,1,0:T(8,128)(2,1)}), bf16[16,2,128,512]{3,2,1,0:T(8,128)(2,1)}, u32[]{:S(2)}, u32[]{:S(2)}) async-start(bf16[16,2,128,512]{3,2,1,0:T(8,128)(2,1)} %broadcast_select_fusion), calls=%async_computation | async-start | bytes 8388608 | tf_op jit(solution)/shard_map/all_to_all | solution.py:111
  244.3 2.4 copy-start.2
  260.4 97.9 %all-to-all-start.1 = ((bf16[16,2,128,512]{3,1,2,0:T(2,128)(2,1)}), bf16[16,2,128,512]{3,1,2,0:T(2,128)(2,1)}, u32[]{:S(2)}, u32[]{:S(2)}) async-start(bf16[16,2,128,512]{3,1,2,0:T(2,128)(2,1)} %copy.83), calls=%async_computation.1 | async-start | bytes 8388608 | tf_op jit(solution)/shard_map/all_to_all | solution.py:131
  374.4 3.0 copy-start.3
  374.4 3.5 copy-start.4
  377.3 4.4 %copy-start.7 = (bf16[4,128,768]{2,1,0:T(8,128)(2,1)S(1)}, bf16[4,128,768]{2,1,0:T(8,128)(2,1)}, u32[]{:S(2)}) copy-start(bf16[4,128,768]{2,1,0:T(8,128)(2,1)} %get-tuple-element.47) | copy-start | bytes 2359300
  378.3 3.4 collective-permute-start.1
where the time goes:
time: 385 us; the launch traced here: 383 us
  waiting for transfers between devices  188 us (49%)
  matrix products  113 us (29%)
  local copies, waits for them, and re-layouts  60.3 us (16%)
  starting transfers between devices  13.5 us (4%)
  other arithmetic  7.23 us (2%)
    all_to_all x1, waiting for transfers between devices, shards(): lax.all_to_all(back_send.reshape(tile_count, CAP, BLK, 2 * kv_width), 'ti...  93.1 us
    all_to_all x1, waiting for transfers between devices, shards(): lax.all_to_all(send_kv, 'tile', split_axis=0, concat_axis=0, tiled=True)  92.6 us
    dot_general x4, matrix products, block_work(): jnp.einsum('grin,igrd->ngd', score_grad, query_low, preferred_element_typ...  22.9 us
    dot_general x4, matrix products, block_work(): jnp.einsum('grin,ngd->igrd', score_grad, keys_low, preferred_element_type...  22.6 us
    sub x4, matrix products, block_work(): expo = jnp.exp(scores - peak)  10.9 us
    dot_general x4, matrix products, block_work(): jnp.einsum('grin,igrd->ngd', probs_low, attended_grad, preferred_element_...  10.1 us
    dynamic_slice x16, local copies, waits for them, and re-layouts, shards(): lax.map(per_block, (queries.reshape(block_count, BLK, HEADS * HEAD_DIM),...  9.58 us
    dot_general x4, matrix products, block_work(): jnp.dot(normed.astype(jnp.bfloat16), w_out, preferred_element_type=jnp.fl...  9.33 us
  transfers between devices with their start and end apart: 4, of which 4 were waited for; matrix products, arithmetic and copies ran while one was open for 1% of the time, Pallas kernels for 0%

commit v1 on v0

v1 whole, which is shorter than its diff:
```python
import functools

import jax
import jax.numpy as jnp
from jax import lax
from jax.experimental import pallas as pl
from jax.experimental.pallas import tpu as pltpu
from jax.sharding import PartitionSpec as P

HEADS = 12
KV_HEADS = 4
HEAD_DIM = 64
BLK = 128
CAP = 2
GROUP = HEADS // KV_HEADS
KV = KV_HEADS * HEAD_DIM
TEMPER = HEAD_DIM ** (-0.5)
EPSILON = 1e-06
F32 = jnp.float32
BF16 = jnp.bfloat16


def dot_nt(a, b):
    return lax.dot_general(a, b, (((1,), (1,)), ((), ())), preferred_element_type=F32)


def dot_tn(a, b):
    return lax.dot_general(a, b, (((0,), (0,)), ((), ())), preferred_element_type=F32)


def stack_heads(rows, g):
    first = g * GROUP * HEAD_DIM
    return jnp.concatenate(
        [rows[:, first + r * HEAD_DIM : first + (r + 1) * HEAD_DIM] for r in range(GROUP)], axis=0
    )


def spread_heads(stacked):
    return jnp.concatenate([stacked[r * BLK : (r + 1) * BLK] for r in range(GROUP)], axis=1)


def attention_kernel(list_len, slot_ref, q_ref, ng_ref, *refs):
    kv_refs = refs[:list_len]
    normed_ref, qg_ref, back_ref, probs_scr, parts_scr, sems = refs[list_len:]
    step = pl.program_id(0)
    keys = jnp.concatenate([ref[0, :, :KV] for ref in kv_refs], axis=0)
    values = jnp.concatenate([ref[0, :, KV:] for ref in kv_refs], axis=0)
    queries = q_ref[...] * jnp.asarray(TEMPER, BF16)
    attended = []
    for g in range(KV_HEADS):
        cols = slice(g * HEAD_DIM, (g + 1) * HEAD_DIM)
        scores = dot_nt(stack_heads(queries, g), keys[:, cols])
        expo = jnp.exp(scores - jnp.max(scores, axis=-1, keepdims=True))
        probs = expo * (1.0 / jnp.sum(expo, axis=-1, keepdims=True))
        probs_scr[g] = probs
        out = jnp.dot(probs.astype(BF16), values[:, cols], preferred_element_type=F32)
        attended.append(spread_heads(out.astype(BF16)))
    attended = jnp.concatenate(attended, axis=1).astype(F32)
    width = attended.shape[1]
    inverse = lax.rsqrt(jnp.sum(attended * attended, axis=-1, keepdims=True) / width + EPSILON)
    normed = attended * inverse
    normed_ref[...] = normed.astype(BF16)
    normed_grad = ng_ref[...]
    shared = jnp.sum(normed_grad * normed, axis=-1, keepdims=True) / width
    attended_grad = ((normed_grad - normed * shared) * inverse).astype(BF16)
    for g in range(KV_HEADS):
        cols = slice(g * HEAD_DIM, (g + 1) * HEAD_DIM)
        out_grad = stack_heads(attended_grad, g)
        prob_grad = dot_nt(out_grad, values[:, cols])
        probs = probs_scr[g]
        row_dot = jnp.sum(probs * prob_grad, axis=-1, keepdims=True)
        score_grad = (probs * (prob_grad - row_dot)).astype(BF16)
        query_grad = jnp.dot(score_grad, keys[:, cols], preferred_element_type=F32) * TEMPER
        first = g * GROUP * HEAD_DIM
        qg_ref[:, first : first + GROUP * HEAD_DIM] = spread_heads(query_grad.astype(BF16))
        key_part = dot_tn(score_grad, stack_heads(queries, g)).astype(BF16)
        value_part = dot_tn(probs.astype(BF16), out_grad).astype(BF16)
        for l in range(list_len):
            rows = slice(l * BLK, (l + 1) * BLK)
            parts_scr[step, l, :, g * HEAD_DIM : (g + 1) * HEAD_DIM] = key_part[rows]
            parts_scr[step, l, :, KV + g * HEAD_DIM : KV + (g + 1) * HEAD_DIM] = value_part[rows]

    def copy(s, l):
        return pltpu.make_async_copy(
            parts_scr.at[s, l], back_ref.at[slot_ref[s * list_len + l]], sems.at[s, l]
        )

    for l in range(list_len):
        copy(step, l).start()

    @pl.when(step == pl.num_programs(0) - 1)
    def _():
        for s in range(sems.shape[0]):
            for l in range(list_len):
                copy(s, l).wait()


def attention(slots, queries, normed_grad, arrived, list_len):
    rows, width = queries.shape
    blocks = rows // BLK
    row_spec = pl.BlockSpec((BLK, width), lambda r, s: (r, 0))

    def entry_spec(l):
        return pl.BlockSpec((1, BLK, 2 * KV), lambda r, s: (s[r * list_len + l], 0, 0))

    keys = list_len * BLK
    pairs = HEADS * rows * keys
    return pl.pallas_call(
        functools.partial(attention_kernel, list_len),
        grid_spec=pltpu.PrefetchScalarGridSpec(
            num_scalar_prefetch=1,
            grid=(blocks,),
            in_specs=[row_spec, row_spec] + [entry_spec(l) for l in range(list_len)],
            out_specs=[row_spec, row_spec, pl.BlockSpec(memory_space=pl.ANY)],
            scratch_shapes=[
                pltpu.VMEM((KV_HEADS, GROUP * BLK, keys), F32),
                pltpu.VMEM((blocks, list_len, BLK, 2 * KV), BF16),
                pltpu.SemaphoreType.DMA((blocks, list_len)),
            ],
        ),
        out_shape=[
            jax.ShapeDtypeStruct((rows, width), BF16),
            jax.ShapeDtypeStruct((rows, width), BF16),
            jax.ShapeDtypeStruct(arrived.shape, BF16),
        ],
        compiler_params=pltpu.CompilerParams(vmem_limit_bytes=56 * 1024 * 1024),
        cost_estimate=pl.CostEstimate(
            flops=12 * pairs * HEAD_DIM, bytes_accessed=16 * rows * width, transcendentals=pairs
        ),
        name="attention",
    )(slots, queries, normed_grad, *([arrived] * list_len))


def owner_kernel(chunk, wanted_ref, parts_ref, out_ref, total):
    step = pl.program_id(0)

    @pl.when(step == 0)
    def _():
        total[...] = jnp.zeros_like(total)

    for s in range(chunk):
        block = wanted_ref[step * chunk + s]

        @pl.when(block >= 0)
        def _():
            total[block] += parts_ref[s].astype(F32)

    @pl.when(step == pl.num_programs(0) - 1)
    def _():
        out_ref[...] = total[...].astype(BF16)


def owner_sum(wanted, returned, blocks):
    slots = returned.shape[0]
    chunk = 4
    return pl.pallas_call(
        functools.partial(owner_kernel, chunk),
        grid_spec=pltpu.PrefetchScalarGridSpec(
            num_scalar_prefetch=1,
            grid=(slots // chunk,),
            in_specs=[pl.BlockSpec((chunk, BLK, 2 * KV), lambda s, w: (s, 0, 0))],
            out_specs=pl.BlockSpec((blocks, BLK, 2 * KV), lambda s, w: (0, 0, 0)),
            scratch_shapes=[pltpu.VMEM((blocks, BLK, 2 * KV), F32)],
        ),
        out_shape=jax.ShapeDtypeStruct((blocks, BLK, 2 * KV), BF16),
        compiler_params=pltpu.CompilerParams(vmem_limit_bytes=24 * 1024 * 1024),
        name="owner_sum",
    )(wanted, returned)


def slot_index(entry_tiles, tile_count):
    one_hot = (entry_tiles[:, None] == jnp.arange(tile_count, dtype=jnp.int32)[None, :]).astype(
        jnp.int32
    )
    ranks = jnp.cumsum(one_hot, axis=0) - 1
    return jnp.sum(one_hot * ranks, axis=1)


def from_partner(value):
    return lax.ppermute(value, "vintage", [(0, 1), (1, 0)])


def shards(patches, out_grad, w_query, w_key, w_value, w_out, key_tiles, key_blocks):
    tokens = patches[0]
    rows = tokens.shape[0]
    tile_count = lax.axis_size("tile")
    my_tile = lax.axis_index("tile")
    block_count = rows // BLK
    list_len = key_tiles.shape[2]
    entry_count = block_count * list_len
    keys = jnp.dot(tokens, w_key, preferred_element_type=F32).astype(BF16)
    values = jnp.dot(tokens, w_value, preferred_element_type=F32).astype(BF16)
    partner = from_partner(jnp.concatenate([keys, values], axis=-1))
    partner_blocks = partner.reshape(block_count, BLK, 2 * KV)
    my_tiles = lax.dynamic_slice_in_dim(
        key_tiles[0], my_tile * block_count, block_count, 0
    ).reshape(-1)
    flat_slot = my_tiles * CAP + slot_index(my_tiles, tile_count)
    all_tiles = key_tiles[0].reshape(tile_count, entry_count)
    all_blocks = key_blocks[0].reshape(tile_count, entry_count)
    asking = (all_tiles == my_tile).astype(jnp.int32)
    ranks = jnp.cumsum(asking, axis=1) - 1
    slot_range = jnp.arange(CAP, dtype=jnp.int32)
    hits = (asking[:, :, None] == 1) & (ranks[:, :, None] == slot_range[None, None, :])
    wanted = (jnp.sum(jnp.where(hits, all_blocks[:, :, None] + 1, 0), axis=1) - 1).reshape(-1)
    send = partner_blocks[jnp.clip(wanted, 0, block_count - 1)]
    arrived = lax.all_to_all(send, "tile", split_axis=0, concat_axis=0, tiled=True)
    queries = jnp.dot(tokens, w_query, preferred_element_type=F32).astype(BF16)
    normed_grad = dot_nt(out_grad[0], w_out)
    normed_low, query_grad, back = attention(flat_slot, queries, normed_grad, arrived, list_len)
    returned = lax.all_to_all(back, "tile", split_axis=0, concat_axis=0, tiled=True)
    layer_out = jnp.dot(normed_low, w_out, preferred_element_type=F32).astype(BF16)
    query_term = dot_nt(query_grad, w_query)
    kv_grad = owner_sum(wanted, returned, block_count).reshape(rows, 2 * KV)
    kv_grad = from_partner(kv_grad)
    kv_term = dot_nt(kv_grad[:, :KV], w_key) + dot_nt(kv_grad[:, KV:], w_value)
    input_grad = (query_term + kv_term).astype(BF16)
    return (layer_out[None], input_grad[None])


def solution(mesh):
    in_specs = (
        P("vintage", "tile", None),
        P("vintage", "tile", None),
        P(),
        P(),
        P(),
        P(),
        P("vintage", None, None),
        P("vintage", None, None),
    )
    out_specs = (P("vintage", "tile", None), P("vintage", "tile", None))
    return jax.shard_map(shards, mesh=mesh, in_specs=in_specs, out_specs=out_specs, check_vma=False)
```

time: 385 us -> 246 us (0.64)
  matrix products: 113 us -> 11.4 us
  local copies, waits for them, and re-layouts: 60.3 us -> 4.57 us
  Pallas kernels: 0 us -> 31.9 us
  other arithmetic: 7.23 us -> 1.23 us
  waiting for transfers between devices: 188 us -> 183 us
    dot_general x35 -> x8, matrix products: 102 us -> 11.4 us  [the longest x4 4.52 us: dot_nt(): lax.dot_general(a, b, (((1,), (1,)), ((), ())), preferred_element_type=F32)]
    pallas_call x0 -> x2, Pallas kernels: none -> 31.9 us  [the longest x1 26.5 us: attention(): pl.pallas_call(functools.partial(attention_kernel, list_len), grid_spec=p...]
    reshape x3 -> x2, local copies, waits for them, and re-layouts: 15.9 us -> 0.3 us  [the longest x1 0.21 us: shards(): partner_blocks = partner.reshape(block_count, BLK, 2 * KV)]
    sub x4 -> x0, matrix products: 10.9 us -> none  [block_work(): expo = jnp.exp(scores - peak)]
    dynamic_slice x16 -> x0, local copies, waits for them, and re-layouts: 9.58 us -> none  [shards(): lax.map(per_block, (queries.reshape(block_count, BLK, HEADS * HEAD_DIM),...]
    all_to_all x1 -> x0, local copies, waits for them, and re-layouts: 8.89 us -> none  [shards(): lax.all_to_all(back_send.reshape(tile_count, CAP, BLK, 2 * kv_width), 'ti...]
    dynamic_update_slice x16 -> x0, local copies, waits for them, and re-layouts: 8.08 us -> none  [shards(): lax.map(per_block, (queries.reshape(block_count, BLK, HEADS * HEAD_DIM),...]
    scatter x1 -> x0, local copies, waits for them, and re-layouts: 5.21 us -> none  [shards(): jnp.zeros((tile_count * CAP, BLK, 2 * kv_width), jnp.bfloat16).at[flat_slot]]
  transfers between devices with their start and end apart: 4 -> 4, of which waited for: 4 -> 3; matrix products, arithmetic and copies ran while one was open for 1% -> 4% of each run, Pallas kernels for 0% -> 0%
where the time goes in v1:
time: 246 us
  waiting for transfers between devices  183 us (74%)
  Pallas kernels  31.9 us (13%)
  starting transfers between devices  13.4 us (5%)
  matrix products  11.4 us (5%)
  local copies, waits for them, and re-layouts  4.57 us (2%)
    all_to_all x1, waiting for transfers between devices, shards(): lax.all_to_all(back, 'tile', split_axis=0, concat_axis=0, tiled=True)  93.1 us
    all_to_all x1, waiting for transfers between devices, shards(): lax.all_to_all(send, 'tile', split_axis=0, concat_axis=0, tiled=True)  88.9 us
    pallas_call x1, Pallas kernels, attention(): pl.pallas_call(functools.partial(attention_kernel, list_len), grid_spec=p...  26.5 us
    all_to_all x1, starting transfers between devices, shards(): lax.all_to_all(send, 'tile', split_axis=0, concat_axis=0, tiled=True)  6.58 us
    pallas_call x1, Pallas kernels, owner_sum(): pl.pallas_call(functools.partial(owner_kernel, chunk), grid_spec=pltpu.Pr...  5.37 us
  transfers between devices with their start and end apart: 4, of which 3 were waited for; matrix products, arithmetic and copies ran while one was open for 4% of the time, Pallas kernels for 0%

profile of v1, /device:TPU:15, one launch (start us, length us, event | category | flops | bytes accessed | tf_op | source)
XLA Modules:
  0.0 246.0 jit_solution(1945920244186924994)
XLA Ops:
  0.6 0.0 copy-start
  0.6 0.0 copy-start.1
  0.7 0.0 copy-start.3
  0.7 1.8 convolution_convert_fusion.3
  2.5 0.0 copy-done.1
  2.5 0.0 copy-done.3
  2.5 0.0 copy-start.5
  2.5 0.0 copy-start.4
  2.5 0.4 convolution_convert_fusion.2
  3.0 0.7 collective-permute-start
  3.7 0.1 copy.17
  3.8 0.1 add.56
  3.9 0.1 copy.16
  4.0 0.1 reshape.84
  4.1 0.2 reduce_window_sum.23
  4.3 0.1 select_reduce_fusion
  4.4 0.1 copy.18
  4.5 0.1 min.12
  4.6 0.7 collective-permute-done
  5.3 0.2 copy.21
  5.5 2.8 %gather_fusion = bf16[32,128,512]{2,1,0:T(8,128)(2,1)} fusion(bf16[4,128,512]{2,1,0:T(8,128)(2,1)S(1)} %bitcast.29, s32[1024]{0:T(1024)S(1)} %pad_clamp_fusion), kind=kCustom, calls=%fused_computation | custom fusion | bytes 8388736 | tf_op jit(solution)/shard_map/gather | solution.py:206
  8.3 6.6 %all-to-all-start = ((bf16[32,128,512]{2,1,0:T(8,128)(2,1)}), bf16[32,128,512]{2,1,0:T(8,128)(2,1)}, u32[]{:S(2)}, u32[]{:S(2)}) async-start(bf16[32,128,512]{2,1,0:T(8,128)(2,1)} %gather_fusion), calls=%async_computation | async-start | bytes 8388608 | tf_op jit(solution)/shard_map/all_to_all | solution.py:207
  14.8 0.1 constant_dynamic-slice_fusion
  14.9 0.1 copy.15
  15.0 0.1 reshape.81
  15.1 0.1 fusion.11
  15.2 0.2 select_reduce_fusion.1
  15.4 0.6 multiply_add_fusion.slot_ref
  16.0 3.0 %convolution_convert_fusion.1.q_ref = bf16[512,768]{1,0:T(8,128)(2,1)} fusion(bf16[768,768]{1,0:T(8,128)(2,1)} %param.10, bf16[1,512,768]{2,1,0:T(8,128)(2,1)S(1)} %copy-done.1), kind=kOutput, calls=%fused_computation.3 | convolution fusion | flops 604372992 | bytes 2752512 | tf_op jit(solution)/shard_map/dot_general | solution.py:208
  19.0 0.0 copy-done.7
  19.0 2.0 fusion.2.ng_ref
  21.0 88.9 %all-to-all-done.refs_0_.refs_1_.refs_2_.refs_3_ = bf16[32,128,512]{2,1,0:T(8,128)(2,1)} async-done(((bf16[32,128,512]{2,1,0:T(8,128)(2,1)}), bf16[32,128,512]{2,1,0:T(8,128)(2,1)}, u32[]{:S(2)}, u32[]{:S(2)}) %all-to-all-start) | async-done | bytes 4194336 | tf_op jit(solution)/shard_map/all_to_all | solution.py:207
  109.9 26.5 %attention.1 = (bf16[512,768]{1,0:T(8,128)(2,1)}, bf16[512,768]{1,0:T(8,128)(2,1)}, bf16[32,128,512]{2,1,0:T(8,128)(2,1)}) custom-call(s32[16]{0:T(128)} %multiply_add_fusion.slot_ref, bf16[512,768]{1,0:T(8,128)(2,1)} %convolution_convert_fusion.1.q_ref, f32[512,768]{1,0:T(8,128)} %fusion.2.ng_ref, ...), custom_call_target="tpu_custom_call" | custom-call | flops 2415919104 | bytes 6291456 | tf_op jit(solution)/shard_map/attention/pallas_call | solution.py:108
  136.4 4.6 %all-to-all-start.1 = ((bf16[32,128,512]{2,1,0:T(8,128)(2,1)}), bf16[32,128,512]{2,1,0:T(8,128)(2,1)}, u32[]{:S(2)}, u32[]{:S(2)}) async-start(bf16[32,128,512]{2,1,0:T(8,128)(2,1)} %get-tuple-element.7), calls=%async_computation.1 | async-start | bytes 8388608 | tf_op jit(solution)/shard_map/all_to_all | solution.py:211
  141.0 0.1 copy.20
  141.1 0.1 sub.15.wanted_ref
  141.2 0.0 copy-start.9
  141.2 93.1 %all-to-all-done.1.parts_ref = bf16[32,128,512]{2,1,0:T(8,128)(2,1)} async-done(((bf16[32,128,512]{2,1,0:T(8,128)(2,1)}), bf16[32,128,512]{2,1,0:T(8,128)(2,1)}, u32[]{:S(2)}, u32[]{:S(2)}) %all-to-all-start.1) | async-done | bytes 4194336 | tf_op jit(solution)/shard_map/all_to_all | solution.py:211
  234.3 5.4 %owner_sum.1 = bf16[4,128,512]{2,1,0:T(8,128)(2,1)S(1)} custom-call(s32[32]{0:T(128)S(1)} %sub.15.wanted_ref, bf16[32,128,512]{2,1,0:T(8,128)(2,1)} %all-to-all-done.1.parts_ref), custom_call_target="tpu_custom_call" | custom-call | tf_op jit(solution)/shard_map/owner_sum/pallas_call | solution.py:156
  239.7 1.5 collective-permute-start.1
  241.2 1.7 fusion
  242.9 0.0 copy-done.6
  242.9 0.8 fusion.13
  243.7 0.0 copy-start.2
  243.7 0.0 collective-permute-done.1
  243.7 0.4 fusion.7
  244.1 0.6 copy-done.2
  244.7 1.3 fusion.1
  (17 shorter events, 0.1 us)
Async XLA Ops:
  0.6 18.3 %copy-start = (bf16[768,768]{1,0:T(8,128)(2,1)S(1)}, bf16[768,768]{1,0:T(8,128)(2,1)}, u32[]{:S(2)}) copy-start(bf16[768,768]{1,0:T(8,128)(2,1)} %param.13) | copy-start | bytes 3538948
  0.6 1.8 copy-start.1
  0.7 1.8 copy-start.3
  2.5 1.2 copy-start.5
  2.5 1.4 copy-start.4
  3.0 2.3 collective-permute-start
  8.3 101.7 %all-to-all-start = ((bf16[32,128,512]{2,1,0:T(8,128)(2,1)}), bf16[32,128,512]{2,1,0:T(8,128)(2,1)}, u32[]{:S(2)}, u32[]{:S(2)}) async-start(bf16[32,128,512]{2,1,0:T(8,128)(2,1)} %gather_fusion), calls=%async_computation | async-start | bytes 8388608 | tf_op jit(solution)/shard_map/all_to_all | solution.py:207
  16.0 3.0 %copy-start.7 = (bf16[1,512,768]{2,1,0:T(8,128)(2,1)S(1)}, bf16[1,512,768]{2,1,0:T(8,128)(2,1)}, u32[]{:S(2)}) copy-start(bf16[1,512,768]{2,1,0:T(8,128)(2,1)} %param.9) | copy-start | bytes 2359300
  136.4 97.9 %all-to-all-start.1 = ((bf16[32,128,512]{2,1,0:T(8,128)(2,1)}), bf16[32,128,512]{2,1,0:T(8,128)(2,1)}, u32[]{:S(2)}, u32[]{:S(2)}) async-start(bf16[32,128,512]{2,1,0:T(8,128)(2,1)} %get-tuple-element.7), calls=%async_computation.1 | async-start | bytes 8388608 | tf_op jit(solution)/shard_map/all_to_all | solution.py:211
  141.2 100.1 %copy-start.9 = (bf16[512,768]{1,0:T(8,128)(2,1)S(1)}, bf16[512,768]{1,0:T(8,128)(2,1)}, u32[]{:S(2)}) copy-start(bf16[512,768]{1,0:T(8,128)(2,1)} %get-tuple-element.5) | copy-start | bytes 2359300
  239.7 4.0 %collective-permute-start.1 = (bf16[512,512]{1,0:T(8,128)(2,1)S(1)}, bf16[512,512]{1,0:T(8,128)(2,1)S(1)}, u32[]{:S(2)}, u32[]{:S(2)}) collective-permute-start(bf16[512,512]{1,0:T(8,128)(2,1)S(1)} %bitcast.28), channel_id=1, source_target_pairs={{0,16},{16,0},{1,17},{17,1},{2,18},{18,2},{3,19},{19,3},{4,20},{20... | collective-permute-start | bytes 1572872 | tf_op jit(solution)/shard_map/ppermute | solution.py:180
  241.2 1.7 copy-start.6
  241.2 1.7 copy-start.8
  243.7 1.0 copy-start.2

commit v2 on v1

v2 whole, which is shorter than its diff:
```python
import functools

import jax
import jax.numpy as jnp
from jax import lax
from jax.experimental import pallas as pl
from jax.experimental.pallas import tpu as pltpu
from jax.sharding import PartitionSpec as P

HEADS = 12
KV_HEADS = 4
HEAD_DIM = 64
BLK = 128
CAP = 2
MAJOR = 4
CHUNKS = 2
GROUP = HEADS // KV_HEADS
KV = KV_HEADS * HEAD_DIM
TEMPER = HEAD_DIM ** (-0.5)
EPSILON = 1e-06
PER_CHUNK = KV_HEADS // CHUNKS
HALF = PER_CHUNK * HEAD_DIM
F32 = jnp.float32
BF16 = jnp.bfloat16


def dot_nt(a, b):
    return lax.dot_general(a, b, (((1,), (1,)), ((), ())), preferred_element_type=F32)


def dot_tn(a, b):
    return lax.dot_general(a, b, (((0,), (0,)), ((), ())), preferred_element_type=F32)


def stack_heads(rows, g):
    first = g * GROUP * HEAD_DIM
    return jnp.concatenate(
        [rows[:, first + r * HEAD_DIM : first + (r + 1) * HEAD_DIM] for r in range(GROUP)], axis=0
    )


def spread_heads(stacked):
    return jnp.concatenate([stacked[r * BLK : (r + 1) * BLK] for r in range(GROUP)], axis=1)


def attention_kernel(list_len, slot_ref, q_ref, ng_ref, *refs):
    kv_refs = refs[: CHUNKS * list_len]
    normed_ref, qg_ref = refs[CHUNKS * list_len : CHUNKS * list_len + 2]
    back_refs = refs[CHUNKS * list_len + 2 : CHUNKS * list_len + 2 + CHUNKS]
    probs_scr, parts_scr, sems = refs[-3:]
    step = pl.program_id(0)
    queries = q_ref[...] * jnp.asarray(TEMPER, BF16)
    keys, values, attended = [], [], []
    for c in range(CHUNKS):
        entries = kv_refs[c * list_len : (c + 1) * list_len]
        rows = jnp.concatenate([ref[0] for ref in entries], axis=0)
        for k in range(PER_CHUNK):
            keys.append(rows[:, k * HEAD_DIM : (k + 1) * HEAD_DIM])
            values.append(rows[:, HALF + k * HEAD_DIM : HALF + (k + 1) * HEAD_DIM])
    for g in range(KV_HEADS):
        scores = dot_nt(stack_heads(queries, g), keys[g])
        expo = jnp.exp(scores - jnp.max(scores, axis=-1, keepdims=True))
        probs = expo * (1.0 / jnp.sum(expo, axis=-1, keepdims=True))
        probs_scr[g] = probs
        out = jnp.dot(probs.astype(BF16), values[g], preferred_element_type=F32)
        attended.append(spread_heads(out.astype(BF16)))
    attended = jnp.concatenate(attended, axis=1).astype(F32)
    width = attended.shape[1]
    inverse = lax.rsqrt(jnp.sum(attended * attended, axis=-1, keepdims=True) / width + EPSILON)
    normed = attended * inverse
    normed_ref[...] = normed.astype(BF16)
    normed_grad = ng_ref[...]
    shared = jnp.sum(normed_grad * normed, axis=-1, keepdims=True) / width
    attended_grad = ((normed_grad - normed * shared) * inverse).astype(BF16)
    for g in range(KV_HEADS):
        out_grad = stack_heads(attended_grad, g)
        prob_grad = dot_nt(out_grad, values[g])
        probs = probs_scr[g]
        row_dot = jnp.sum(probs * prob_grad, axis=-1, keepdims=True)
        score_grad = (probs * (prob_grad - row_dot)).astype(BF16)
        query_grad = jnp.dot(score_grad, keys[g], preferred_element_type=F32) * TEMPER
        first = g * GROUP * HEAD_DIM
        qg_ref[:, first : first + GROUP * HEAD_DIM] = spread_heads(query_grad.astype(BF16))
        key_part = dot_tn(score_grad, stack_heads(queries, g)).astype(BF16)
        value_part = dot_tn(probs.astype(BF16), out_grad).astype(BF16)
        c, k = g // PER_CHUNK, (g % PER_CHUNK) * HEAD_DIM
        for l in range(list_len):
            rows = slice(l * BLK, (l + 1) * BLK)
            parts_scr[c, step, l, :, k : k + HEAD_DIM] = key_part[rows]
            parts_scr[c, step, l, :, HALF + k : HALF + k + HEAD_DIM] = value_part[rows]

    def copy(c, s, l):
        return pltpu.make_async_copy(
            parts_scr.at[c, s, l],
            back_refs[c].at[slot_ref[s * list_len + l]],
            sems.at[c, s, l],
        )

    for c in range(CHUNKS):
        for l in range(list_len):
            copy(c, step, l).start()

    @pl.when(step == pl.num_programs(0) - 1)
    def _():
        for c in range(CHUNKS):
            for s in range(sems.shape[1]):
                for l in range(list_len):
                    copy(c, s, l).wait()


def attention(slots, queries, normed_grad, arrived, list_len):
    rows, width = queries.shape
    blocks = rows // BLK
    row_spec = pl.BlockSpec((BLK, width), lambda r, s: (r, 0))

    def entry_spec(l):
        return pl.BlockSpec((1, BLK, 2 * HALF), lambda r, s: (s[r * list_len + l], 0, 0))

    keys = list_len * BLK
    pairs = HEADS * rows * keys
    entry_specs = [entry_spec(l) for _ in range(CHUNKS) for l in range(list_len)]
    entry_args = [chunk for chunk in arrived for _ in range(list_len)]
    return pl.pallas_call(
        functools.partial(attention_kernel, list_len),
        grid_spec=pltpu.PrefetchScalarGridSpec(
            num_scalar_prefetch=1,
            grid=(blocks,),
            in_specs=[row_spec, row_spec] + entry_specs,
            out_specs=[row_spec, row_spec] + [pl.BlockSpec(memory_space=pl.ANY)] * CHUNKS,
            scratch_shapes=[
                pltpu.VMEM((KV_HEADS, GROUP * BLK, keys), F32),
                pltpu.VMEM((CHUNKS, blocks, list_len, BLK, 2 * HALF), BF16),
                pltpu.SemaphoreType.DMA((CHUNKS, blocks, list_len)),
            ],
        ),
        out_shape=[
            jax.ShapeDtypeStruct((rows, width), BF16),
            jax.ShapeDtypeStruct((rows, width), BF16),
        ]
        + [jax.ShapeDtypeStruct(arrived[0].shape, BF16)] * CHUNKS,
        compiler_params=pltpu.CompilerParams(vmem_limit_bytes=56 * 1024 * 1024),
        cost_estimate=pl.CostEstimate(
            flops=12 * pairs * HEAD_DIM, bytes_accessed=16 * rows * width, transcendentals=pairs
        ),
        name="attention",
    )(slots, queries, normed_grad, *entry_args)


def column_kernel(chunk, place_ref, parts_ref, out_ref, total):
    step = pl.program_id(0)

    @pl.when(step == 0)
    def _():
        total[...] = jnp.zeros_like(total)

    for s in range(chunk):
        block = place_ref[step * chunk + s]

        @pl.when(block >= 0)
        def _():
            total[block] += parts_ref[s].astype(F32)

    @pl.when(step == pl.num_programs(0) - 1)
    def _():
        out_ref[...] = total[...].astype(BF16)


def column_sum(place, returned, blocks):
    slots, _, width = returned.shape
    chunk = 8
    return pl.pallas_call(
        functools.partial(column_kernel, chunk),
        grid_spec=pltpu.PrefetchScalarGridSpec(
            num_scalar_prefetch=1,
            grid=(slots // chunk,),
            in_specs=[pl.BlockSpec((chunk, BLK, width), lambda s, w: (s, 0, 0))],
            out_specs=pl.BlockSpec((blocks, BLK, width), lambda s, w: (0, 0, 0)),
            scratch_shapes=[pltpu.VMEM((blocks, BLK, width), F32)],
        ),
        out_shape=jax.ShapeDtypeStruct((blocks, BLK, width), BF16),
        compiler_params=pltpu.CompilerParams(vmem_limit_bytes=24 * 1024 * 1024),
        name="column_sum",
    )(place, returned)


def from_partner(value):
    return lax.ppermute(value, "vintage", [(0, 1), (1, 0)])


def exchange(value, groups):
    return lax.all_to_all(
        value, "tile", split_axis=0, concat_axis=0, tiled=True, axis_index_groups=groups
    )


def shards(patches, out_grad, w_query, w_key, w_value, w_out, key_tiles, key_blocks):
    tokens = patches[0]
    rows = tokens.shape[0]
    tile_count = lax.axis_size("tile")
    plane = tile_count // MAJOR
    my_tile = lax.axis_index("tile")
    my_row, my_place = my_tile // plane, my_tile % plane
    columns = [[z * plane + c for z in range(MAJOR)] for c in range(plane)]
    planes = [[z * plane + c for c in range(plane)] for z in range(MAJOR)]
    block_count = rows // BLK
    list_len = key_tiles.shape[2]
    entry_count = block_count * list_len

    def plane_rows(table):
        table = table[0].reshape(MAJOR, plane, entry_count)
        return lax.dynamic_index_in_dim(table, my_row, 0, keepdims=False)

    tiles, picks = plane_rows(key_tiles), plane_rows(key_blocks)
    earlier = jnp.arange(entry_count)[:, None] > jnp.arange(entry_count)[None, :]
    same = (tiles[:, :, None] == tiles[:, None, :]) & earlier[None]
    ranks = jnp.sum(same.astype(jnp.int32), axis=2)
    slots = ((tiles % plane) * MAJOR + tiles // plane) * CAP + ranks
    my_slots = lax.dynamic_index_in_dim(slots, my_place, 0, keepdims=False)
    ids = jnp.arange(MAJOR * CAP, dtype=jnp.int32)
    hits = slots[:, None, :] == my_place * (MAJOR * CAP) + ids[None, :, None]
    place = jnp.sum(jnp.where(hits, picks[:, None, :] + 1, 0), axis=2) - 1
    place = jnp.where(place >= 0, (ids // CAP)[None, :] * block_count + place, -1).reshape(-1)
    picked = jnp.maximum(place, 0)

    arrived = []
    for c in range(CHUNKS):
        cols = slice(c * HALF, (c + 1) * HALF)
        weight = jnp.concatenate([w_key[:, cols], w_value[:, cols]], axis=1)
        mine = jnp.dot(tokens, weight, preferred_element_type=F32).astype(BF16)
        whole = lax.all_gather(
            from_partner(mine), "tile", axis_index_groups=columns, tiled=True
        ).reshape(MAJOR * block_count, BLK, 2 * HALF)
        arrived.append(exchange(whole[picked], planes))
    queries = jnp.dot(tokens, w_query, preferred_element_type=F32).astype(BF16)
    normed_grad = dot_nt(out_grad[0], w_out)
    normed_low, query_grad, *back = attention(my_slots, queries, normed_grad, arrived, list_len)
    layer_out = jnp.dot(normed_low, w_out, preferred_element_type=F32).astype(BF16)
    total = dot_nt(query_grad, w_query)
    for c in range(CHUNKS):
        cols = slice(c * HALF, (c + 1) * HALF)
        sums = column_sum(place, exchange(back[c], planes), MAJOR * block_count)
        own = exchange(sums, columns).reshape(MAJOR, rows, 2 * HALF)
        kv_grad = from_partner(jnp.sum(own.astype(F32), axis=0).astype(BF16))
        total += dot_nt(kv_grad[:, :HALF], w_key[:, cols]) + dot_nt(kv_grad[:, HALF:], w_value[:, cols])
    return (layer_out[None], total.astype(BF16)[None])


def solution(mesh):
    in_specs = (
        P("vintage", "tile", None),
        P("vintage", "tile", None),
        P(),
        P(),
        P(),
        P(),
        P("vintage", None, None),
        P("vintage", None, None),
    )
    out_specs = (P("vintage", "tile", None), P("vintage", "tile", None))
    return jax.shard_map(shards, mesh=mesh, in_specs=in_specs, out_specs=out_specs, check_vma=False)
```

time: 246 us -> 261 us (1.061)
  the two profiles are of different devices: /device:TPU:15 before, /device:TPU:0 now
where the time goes in v2:
time: 261 us; the launch traced here: 260 us
  waiting for transfers between devices  133 us (51%)
  Pallas kernels  29.4 us (11%)
  blocking collectives  29.3 us (11%)
  starting transfers between devices  20.9 us (8%)
  local copies, waits for them, and re-layouts  18.6 us (7%)
  between operations  14.3 us (5%)
  matrix products  11.9 us (5%)
    all_to_all x5, waiting for transfers between devices, exchange(): lax.all_to_all(value, 'tile', split_axis=0, concat_axis=0, tiled=True, ax...  81.3 us
    all_gather x2, waiting for transfers between devices, shards(): lax.all_gather(from_partner(mine), 'tile', axis_index_groups=columns, til...  50.4 us
    all_to_all x1, blocking collectives, exchange(): lax.all_to_all(value, 'tile', split_axis=0, concat_axis=0, tiled=True, ax...  29.3 us
    pallas_call x1, Pallas kernels, attention(): pl.pallas_call(functools.partial(attention_kernel, list_len), grid_spec=p...  26.9 us
    all_to_all x5, starting transfers between devices, exchange(): lax.all_to_all(value, 'tile', split_axis=0, concat_axis=0, tiled=True, ax...  19.7 us
    unnamed x38, local copies, waits for them, and re-layouts  7.34 us
    dot_general x6, matrix products, dot_nt(): lax.dot_general(a, b, (((1,), (1,)), ((), ())), preferred_element_type=F32)  6.45 us
    gather x2, local copies, waits for them, and re-layouts, shards(): arrived.append(exchange(whole[picked], planes))  5.23 us
  transfers between devices with their start and end apart: 11, of which 9 were waited for; matrix products, arithmetic and copies ran while one was open for 8% of the time, Pallas kernels for 1%

profile of v2, /device:TPU:0, one launch (start us, length us, event | category | flops | bytes accessed | tf_op | source)
XLA Modules:
  0.0 259.9 jit_solution(13664621091551619661)
XLA Ops:
  7.2 1.4 fusion.36
  8.8 0.4 fusion.3
  9.2 0.5 collective-permute-start.1
  9.7 1.2 collective-permute-done.1
  10.9 0.7 copy-done.8
  11.6 0.4 fusion.2
  12.1 0.4 collective-permute-start
  12.9 0.2 convert_reduce_fusion
  13.2 0.2 select_reduce_fusion
  13.5 0.2 collective-permute-done
  13.7 0.7 copy-done.9
  14.4 27.9 %all-gather.5.cloned.1.call-done = bf16[2048,256]{0,1:T(8,128)(2,1)} async-done(((bf16[512,256]{0,1:T(8,128)(2,1)}), bf16[2048,256]{0,1:T(8,128)(2,1)}) %all-gather.5.cloned.1.call-update) | async-done | bytes 1048592 | tf_op jit(solution)/shard_map/all_gather | solution.py:230
  42.3 1.5 copy.19
  43.8 2.0 gather_fusion.1
  45.8 3.6 %all-to-all-start.1 = ((bf16[32,128,256]{2,1,0:T(8,128)(2,1)}), bf16[32,128,256]{2,1,0:T(8,128)(2,1)S(1)}, u32[]{:S(2)}, u32[]{:S(2)}) async-start(bf16[32,128,256]{2,1,0:T(8,128)(2,1)} %gather_fusion.1), calls=%async_computation.1 | async-start | bytes 4194304 | tf_op jit(solution)/shard_map/all_to_all | solution.py:191
  49.4 22.5 %all-gather.3.cloned.1.call-done = bf16[2048,256]{0,1:T(8,128)(2,1)} async-done(((bf16[512,256]{0,1:T(8,128)(2,1)}), bf16[2048,256]{0,1:T(8,128)(2,1)}) %all-gather.3.cloned.1.call-update) | async-done | bytes 1048592 | tf_op jit(solution)/shard_map/all_gather | solution.py:230
  71.9 2.3 copy.18
  74.2 3.3 %gather_fusion = bf16[32,128,256]{2,1,0:T(8,128)(2,1)} fusion(bf16[16,128,256]{2,1,0:T(8,128)(2,1)} %bitcast.38, s32[1024]{0:T(1024)S(1)} %pad_clamp_fusion), kind=kCustom, calls=%fused_computation | custom fusion | bytes 4194432 | tf_op jit(solution)/shard_map/gather | solution.py:233
  77.5 1.4 copy-done.4
  78.8 4.5 %all-to-all-start = ((bf16[32,128,256]{2,1,0:T(8,128)(2,1)}), bf16[32,128,256]{2,1,0:T(8,128)(2,1)}, u32[]{:S(2)}, u32[]{:S(2)}) async-start(bf16[32,128,256]{2,1,0:T(8,128)(2,1)} %gather_fusion), calls=%async_computation | async-start | bytes 4194304 | tf_op jit(solution)/shard_map/all_to_all | solution.py:191
  83.3 0.6 fusion.28.slot_ref
  83.9 2.9 %convolution_convert_fusion.1.q_ref = bf16[512,768]{1,0:T(8,128)(2,1)} fusion(bf16[768,768]{1,0:T(8,128)(2,1)S(1)} %copy-done, bf16[1,512,768]{2,1,0:T(8,128)(2,1)} %param.8), kind=kOutput, calls=%fused_computation.4 | convolution fusion | flops 604372992 | bytes 2752512 | tf_op jit(solution)/shard_map/dot_general | solution.py:234
  86.8 2.0 fusion.4.ng_ref
  88.8 19.5 %all-to-all-done.refs_0_.refs_1_.refs_2_.refs_3_ = bf16[32,128,256]{2,1,0:T(8,128)(2,1)} async-done(((bf16[32,128,256]{2,1,0:T(8,128)(2,1)}), bf16[32,128,256]{2,1,0:T(8,128)(2,1)}, u32[]{:S(2)}, u32[]{:S(2)}) %all-to-all-start) | async-done | bytes 2097184 | tf_op jit(solution)/shard_map/all_to_all | solution.py:191
  108.4 26.9 %attention.1 = (bf16[512,768]{1,0:T(8,128)(2,1)}, bf16[512,768]{1,0:T(8,128)(2,1)}, bf16[32,128,256]{2,1,0:T(8,128)(2,1)}, bf16[32,128,256]{2,1,0:T(8,128)(2,1)}) custom-call(s32[16]{0:T(128)} %fusion.28.slot_ref, bf16[512,768]{1,0:T(8,128)(2,1)} %convolution_convert_fusion.1.q_ref, f32[512,768]{1,0:T(8,128)} %fusion.4.ng_ref, ...), custom_call_target="tpu_custom_call" | custom-call | flops 2415919104 | bytes 6291456 | tf_op jit(solution)/shard_map/attention/pallas_call | solution.py:123
  135.3 29.3 %all_to_all.30.parts_ref = bf16[32,128,256]{2,1,0:T(8,128)(2,1)} all-to-all(bf16[32,128,256]{2,1,0:T(8,128)(2,1)} %get-tuple-element.8), channel_id=1, replica_groups={{0,1,2,3},{4,5,6,7},{8,9,10,11},{12,13,14,15},{16,17,18,19},{20,21,22,2..., dimensions={0} | all-to-all | bytes 4194304 | tf_op jit(solution)/shard_map/all_to_all | solution.py:191
  164.6 3.6 %all-to-all-start.4 = ((bf16[32,128,256]{2,1,0:T(8,128)(2,1)}), bf16[32,128,256]{2,1,0:T(8,128)(2,1)S(1)}, u32[]{:S(2)}, u32[]{:S(2)}) async-start(bf16[32,128,256]{2,1,0:T(8,128)(2,1)} %get-tuple-element.9), calls=%async_computation.4 | async-start | bytes 4194304 | tf_op jit(solution)/shard_map/all_to_all | solution.py:191
  168.3 1.6 copy-done.1
  169.9 1.3 column_sum.2
  171.2 1.0 copy-done.3
  172.1 18.9 %all-to-all-done.4.parts_ref = bf16[32,128,256]{2,1,0:T(8,128)(2,1)S(1)} async-done(((bf16[32,128,256]{2,1,0:T(8,128)(2,1)}), bf16[32,128,256]{2,1,0:T(8,128)(2,1)S(1)}, u32[]{:S(2)}, u32[]{:S(2)}) %all-to-all-start.4) | async-done | bytes 2097184 | tf_op jit(solution)/shard_map/all_to_all | solution.py:191
  191.1 4.3 %all-to-all-start.3 = ((bf16[16,128,256]{2,1,0:T(8,128)(2,1)}), bf16[16,128,256]{2,1,0:T(8,128)(2,1)}, u32[]{:S(2)}, u32[]{:S(2)}) async-start(bf16[16,128,256]{2,1,0:T(8,128)(2,1)} %copy-done.3), calls=%async_computation.3 | async-start | bytes 2097152 | tf_op jit(solution)/shard_map/all_to_all | solution.py:191
  195.3 1.3 column_sum.3
  196.6 1.0 copy-done.2
  197.6 23.0 %all-to-all-done.3 = bf16[16,128,256]{2,1,0:T(8,128)(2,1)} async-done(((bf16[16,128,256]{2,1,0:T(8,128)(2,1)}), bf16[16,128,256]{2,1,0:T(8,128)(2,1)}, u32[]{:S(2)}, u32[]{:S(2)}) %all-to-all-start.3) | async-done | bytes 1048608 | tf_op jit(solution)/shard_map/all_to_all | solution.py:191
  220.6 3.7 %all-to-all-start.5 = ((bf16[16,128,256]{2,1,0:T(8,128)(2,1)}), bf16[16,128,256]{2,1,0:T(8,128)(2,1)S(1)}, u32[]{:S(2)}, u32[]{:S(2)}) async-start(bf16[16,128,256]{2,1,0:T(8,128)(2,1)} %copy-done.2), calls=%async_computation.5 | async-start | bytes 2097152 | tf_op jit(solution)/shard_map/all_to_all | solution.py:191
  224.3 2.0 fusion.38
  226.3 1.4 bitcast_reduce_fusion.1
  227.8 1.7 fusion
  229.5 19.8 %all-to-all-done.5 = bf16[16,128,256]{2,1,0:T(8,128)(2,1)S(1)} async-done(((bf16[16,128,256]{2,1,0:T(8,128)(2,1)}), bf16[16,128,256]{2,1,0:T(8,128)(2,1)S(1)}, u32[]{:S(2)}, u32[]{:S(2)}) %all-to-all-start.5) | async-done | bytes 1048608 | tf_op jit(solution)/shard_map/all_to_all | solution.py:191
  249.3 0.1 bitcast_reduce_fusion
  249.5 0.4 fusion.18
  249.9 0.4 copy-done.7
  250.3 0.4 fusion.20
  250.6 0.4 collective-permute-done.3
  251.0 0.4 fusion.15
  251.4 0.3 copy-done.5
  251.7 1.3 fusion.1
  (49 shorter events, 1.0 us)
Async XLA Ops:
  7.2 76.7 %copy-start = (bf16[768,768]{1,0:T(8,128)(2,1)S(1)}, bf16[768,768]{1,0:T(8,128)(2,1)}, u32[]{:S(2)}) copy-start(bf16[768,768]{1,0:T(8,128)(2,1)} %param.10) | copy-start | bytes 3538948
  7.2 1.6 copy-start.14
  7.2 35.1 %all-gather.5.cloned.1.call-start = ((), (), s32[]{:S(2)}) async-start(), calls=%async_computation.7 | async-start | bytes 1310720 | tf_op jit(solution)/shard_map/all_gather | solution.py:230
  8.8 3.8 %copy-start.10 = (s32[1,64,4]{1,2,0:T(4,128)S(1)}, s32[1,64,4]{1,2,0:T(4,128)}, u32[]{:S(2)}) copy-start(s32[1,64,4]{1,2,0:T(4,128)} %param.14) | copy-start | bytes 3076
  8.8 3.9 %copy-start.11 = (s32[1,64,4]{1,2,0:T(4,128)S(1)}, s32[1,64,4]{1,2,0:T(4,128)}, u32[]{:S(2)}) copy-start(s32[1,64,4]{1,2,0:T(4,128)} %param.15) | copy-start | bytes 3076
  9.2 1.7 collective-permute-start.1
  10.9 0.7 copy-start.8
  11.6 60.3 %all-gather.3.cloned.1.call-start = ((), (), s32[]{:S(2)}) async-start(), calls=%async_computation.6 | async-start | bytes 1310720 | tf_op jit(solution)/shard_map/all_gather | solution.py:230
  12.1 1.6 collective-permute-start
  13.7 0.7 copy-start.9
  45.8 31.7 %all-to-all-start.1 = ((bf16[32,128,256]{2,1,0:T(8,128)(2,1)}), bf16[32,128,256]{2,1,0:T(8,128)(2,1)S(1)}, u32[]{:S(2)}, u32[]{:S(2)}) async-start(bf16[32,128,256]{2,1,0:T(8,128)(2,1)} %gather_fusion.1), calls=%async_computation.1 | async-start | bytes 4194304 | tf_op jit(solution)/shard_map/all_to_all | solution.py:191
  77.4 1.4 copy-start.4
  78.8 29.5 %all-to-all-start = ((bf16[32,128,256]{2,1,0:T(8,128)(2,1)}), bf16[32,128,256]{2,1,0:T(8,128)(2,1)}, u32[]{:S(2)}, u32[]{:S(2)}) async-start(bf16[32,128,256]{2,1,0:T(8,128)(2,1)} %gather_fusion), calls=%async_computation | async-start | bytes 4194304 | tf_op jit(solution)/shard_map/all_to_all | solution.py:191
  83.9 2.9 %copy-start.12 = (bf16[768,768]{1,0:T(8,128)(2,1)S(1)}, bf16[768,768]{1,0:T(8,128)(2,1)}, u32[]{:S(2)}) copy-start(bf16[768,768]{1,0:T(8,128)(2,1)} %param.13) | copy-start | bytes 3538948
  83.9 2.9 %copy-start.15 = (bf16[1,512,768]{2,1,0:T(8,128)(2,1)S(1)}, bf16[1,512,768]{2,1,0:T(8,128)(2,1)}, u32[]{:S(2)}) copy-start(bf16[1,512,768]{2,1,0:T(8,128)(2,1)} %param.9) | copy-start | bytes 2359300
  164.6 26.5 %all-to-all-start.4 = ((bf16[32,128,256]{2,1,0:T(8,128)(2,1)}), bf16[32,128,256]{2,1,0:T(8,128)(2,1)S(1)}, u32[]{:S(2)}, u32[]{:S(2)}) async-start(bf16[32,128,256]{2,1,0:T(8,128)(2,1)} %get-tuple-element.9), calls=%async_computation.4 | async-start | bytes 4194304 | tf_op jit(solution)/shard_map/all_to_all | solution.py:191
  168.3 1.6 copy-start.1
  171.2 1.0 copy-start.3
  191.1 29.5 %all-to-all-start.3 = ((bf16[16,128,256]{2,1,0:T(8,128)(2,1)}), bf16[16,128,256]{2,1,0:T(8,128)(2,1)}, u32[]{:S(2)}, u32[]{:S(2)}) async-start(bf16[16,128,256]{2,1,0:T(8,128)(2,1)} %copy-done.3), calls=%async_computation.3 | async-start | bytes 2097152 | tf_op jit(solution)/shard_map/all_to_all | solution.py:191
  196.6 1.0 copy-start.2
  197.6 26.7 %copy-start.17 = (bf16[512,768]{1,0:T(8,128)(2,1)S(1)}, bf16[512,768]{1,0:T(8,128)(2,1)}, u32[]{:S(2)}) copy-start(bf16[512,768]{1,0:T(8,128)(2,1)} %get-tuple-element.7) | copy-start | bytes 2359300
  220.6 28.7 %all-to-all-start.5 = ((bf16[16,128,256]{2,1,0:T(8,128)(2,1)}), bf16[16,128,256]{2,1,0:T(8,128)(2,1)S(1)}, u32[]{:S(2)}, u32[]{:S(2)}) async-start(bf16[16,128,256]{2,1,0:T(8,128)(2,1)} %copy-done.2), calls=%async_computation.5 | async-start | bytes 2097152 | tf_op jit(solution)/shard_map/all_to_all | solution.py:191
  224.3 3.5 %copy-start.13 = (bf16[768,768]{1,0:T(8,128)(2,1)S(1)}, bf16[768,768]{1,0:T(8,128)(2,1)}, u32[]{:S(2)}) copy-start(bf16[768,768]{1,0:T(8,128)(2,1)} %param.13) | copy-start | bytes 3538948
  224.3 3.5 %copy-start.16 = (bf16[512,768]{1,0:T(8,128)(2,1)S(1)}, bf16[512,768]{1,0:T(8,128)(2,1)}, u32[]{:S(2)}) copy-start(bf16[512,768]{1,0:T(8,128)(2,1)} %get-tuple-element.6) | copy-start | bytes 2359300
  227.7 21.8 %collective-permute-start.2 = (bf16[512,256]{1,0:T(8,128)(2,1)S(1)}, bf16[512,256]{1,0:T(8,128)(2,1)S(1)}, u32[]{:S(2)}, u32[]{:S(2)}) collective-permute-start(bf16[512,256]{1,0:T(8,128)(2,1)S(1)} %bitcast_reduce_fusion.1), channel_id=1, source_target_pairs={{0,16},{16,0},{1,17},{17,1},{2,18},{18,2},{3,19},{19,3},{4,20},{20... | collective-permute-start | bytes 786440 | tf_op jit(solution)/shard_map/ppermute | solution.py:187
  227.8 21.7 %copy-start.6 = (bf16[768,256]{1,0:T(8,128)(2,1)S(1)}, bf16[768,256]{1,0:T(8,128)(2,1)}, u32[]{:S(2)}) copy-start(bf16[768,256]{1,0:T(8,128)(2,1)} %param.12) | copy-start | bytes 1179652
  249.3 1.0 copy-start.7
  249.4 1.6 collective-permute-start.3
  250.3 1.4 copy-start.5
Sparse Core Ops, SparseCore 0:
  11.7 30.5 all-gather.4
  44.4 27.4 all-gather.2

commit v3 on v2

v3 whole, which is shorter than its diff:
```python
import functools

import jax
import jax.numpy as jnp
from jax import lax
from jax.experimental import pallas as pl
from jax.experimental.pallas import tpu as pltpu
from jax.sharding import PartitionSpec as P

HEADS = 12
KV_HEADS = 4
HEAD_DIM = 64
BLK = 128
CAP = 2
MAJOR = 4
GROUP = HEADS // KV_HEADS
GROUP_WIDTH = GROUP * HEAD_DIM
WIDE = 2 * HEAD_DIM
TEMPER = HEAD_DIM ** (-0.5)
EPSILON = 1e-06
F32 = jnp.float32
BF16 = jnp.bfloat16
AXES = ("vintage", "tile")
WHOLE = pl.BlockSpec(memory_space=pltpu.VMEM)


def dot_nt(a, b):
    return lax.dot_general(a, b, (((1,), (1,)), ((), ())), preferred_element_type=F32)


def dot_tn(a, b):
    return lax.dot_general(a, b, (((0,), (0,)), ((), ())), preferred_element_type=F32)


def stack_heads(rows):
    return jnp.concatenate(
        [rows[:, r * HEAD_DIM : (r + 1) * HEAD_DIM] for r in range(GROUP)], axis=0
    )


def spread_heads(stacked):
    return jnp.concatenate([stacked[r * BLK : (r + 1) * BLK] for r in range(GROUP)], axis=1)


def params(mebibytes):
    return pltpu.CompilerParams(vmem_limit_bytes=mebibytes * 1024 * 1024)


def pack_kernel(peers, row_ref, place_ref, own, up1, down1, far2, far3, *refs):
    outs, column = refs[:peers], refs[peers]
    row = row_ref[0]
    column[row] = own[...]

    @pl.when(row > 0)
    def _():
        column[jnp.maximum(row - 1, 0)] = up1[...]

    @pl.when(row < MAJOR - 1)
    def _():
        column[jnp.minimum(row + 1, MAJOR - 1)] = down1[...]

    column[(row + 2) % MAJOR] = far2[...]

    @pl.when((row == 0) | (row == MAJOR - 1))
    def _():
        column[MAJOR - 1 - row] = far3[...]

    for p in range(peers):
        for i in range(MAJOR * CAP):
            block = jnp.maximum(place_ref[p * MAJOR * CAP + i], 0)
            outs[p][i] = column[i // CAP, block]


def pack(row, place, tiles, peers):
    blocks = tiles[0].shape[0]
    smem = pl.BlockSpec(memory_space=pltpu.SMEM)
    return pl.pallas_call(
        functools.partial(pack_kernel, peers),
        in_specs=[smem, smem] + [WHOLE] * 5,
        out_specs=[WHOLE] * peers,
        out_shape=[jax.ShapeDtypeStruct((MAJOR * CAP, BLK, WIDE), BF16)] * peers,
        scratch_shapes=[pltpu.VMEM((MAJOR, blocks, BLK, WIDE), BF16)],
        compiler_params=params(16),
        name="pack",
    )(row, place, *tiles)


def forward_kernel(g, list_len, peers, slot_ref, q_ref, *refs):
    sources = refs[:peers]
    attended_ref, probs_ref, kv_ref = refs[peers:]
    step = pl.program_id(0)
    per_peer = MAJOR * CAP
    for l in range(list_len):
        slot = slot_ref[step * list_len + l]
        for p in range(peers):

            @pl.when(slot // per_peer == p)
            def _():
                kv_ref[0, l * BLK : (l + 1) * BLK, :] = sources[p][slot % per_peer]

    rows = kv_ref[0]
    queries = q_ref[:, g * GROUP_WIDTH : (g + 1) * GROUP_WIDTH] * jnp.asarray(TEMPER, BF16)
    scores = dot_nt(stack_heads(queries), rows[:, :HEAD_DIM])
    expo = jnp.exp(scores - jnp.max(scores, axis=-1, keepdims=True))
    probs = expo * (1.0 / jnp.sum(expo, axis=-1, keepdims=True))
    probs_ref[0] = probs
    out = jnp.dot(probs.astype(BF16), rows[:, HEAD_DIM:], preferred_element_type=F32)
    attended_ref[...] = spread_heads(out.astype(BF16))


def forward(g, slots, queries, sources, list_len):
    rows, width = queries.shape
    blocks = rows // BLK
    keys = list_len * BLK
    pairs = GROUP * rows * keys
    return pl.pallas_call(
        functools.partial(forward_kernel, g, list_len, len(sources)),
        grid_spec=pltpu.PrefetchScalarGridSpec(
            num_scalar_prefetch=1,
            grid=(blocks,),
            in_specs=[pl.BlockSpec((BLK, width), lambda r, s: (r, 0))]
            + [pl.BlockSpec(x.shape, lambda r, s: (0, 0, 0)) for x in sources],
            out_specs=[
                pl.BlockSpec((BLK, GROUP_WIDTH), lambda r, s: (r, 0)),
                pl.BlockSpec((1, GROUP * BLK, keys), lambda r, s: (r, 0, 0)),
                pl.BlockSpec((1, keys, WIDE), lambda r, s: (r, 0, 0)),
            ],
        ),
        out_shape=[
            jax.ShapeDtypeStruct((rows, GROUP_WIDTH), BF16),
            jax.ShapeDtypeStruct((blocks, GROUP * BLK, keys), F32),
            jax.ShapeDtypeStruct((blocks, keys, WIDE), BF16),
        ],
        compiler_params=params(48),
        cost_estimate=pl.CostEstimate(
            flops=4 * pairs * HEAD_DIM, bytes_accessed=4 * pairs, transcendentals=pairs
        ),
        name="forward",
    )(slots, queries, *sources)


def norm_kernel(ng_ref, *refs):
    attended_refs, (normed_ref, ag_ref) = refs[:KV_HEADS], refs[KV_HEADS:]
    attended = jnp.concatenate([ref[...] for ref in attended_refs], axis=1).astype(F32)
    width = attended.shape[1]
    inverse = lax.rsqrt(jnp.sum(attended * attended, axis=-1, keepdims=True) / width + EPSILON)
    normed = attended * inverse
    normed_ref[...] = normed.astype(BF16)
    normed_grad = ng_ref[...]
    shared = jnp.sum(normed_grad * normed, axis=-1, keepdims=True) / width
    ag_ref[...] = ((normed_grad - normed * shared) * inverse).astype(BF16)


def normalise(normed_grad, attended):
    rows, width = normed_grad.shape
    spec = pl.BlockSpec((BLK, width), lambda r: (r, 0))
    return pl.pallas_call(
        norm_kernel,
        grid=(rows // BLK,),
        in_specs=[spec] + [pl.BlockSpec((BLK, GROUP_WIDTH), lambda r: (r, 0))] * KV_HEADS,
        out_specs=[spec, spec],
        out_shape=[jax.ShapeDtypeStruct((rows, width), BF16)] * 2,
        compiler_params=params(16),
        name="norm",
    )(normed_grad, *attended)


def backward_kernel(g, list_len, peers, slot_ref, q_ref, ag_ref, probs_ref, kv_ref, qg_ref, *outs):
    step = pl.program_id(0)
    per_peer = MAJOR * CAP
    cols = slice(g * GROUP_WIDTH, (g + 1) * GROUP_WIDTH)
    queries = stack_heads(q_ref[:, cols] * jnp.asarray(TEMPER, BF16))
    out_grad = stack_heads(ag_ref[:, cols])
    rows = kv_ref[0]
    probs = probs_ref[0]
    prob_grad = dot_nt(out_grad, rows[:, HEAD_DIM:])
    row_dot = jnp.sum(probs * prob_grad, axis=-1, keepdims=True)
    score_grad = (probs * (prob_grad - row_dot)).astype(BF16)
    query_grad = jnp.dot(score_grad, rows[:, :HEAD_DIM], preferred_element_type=F32) * TEMPER
    qg_ref[...] = spread_heads(query_grad.astype(BF16))
    key_part = dot_tn(score_grad, queries)
    value_part = dot_tn(probs.astype(BF16), out_grad)
    parts = jnp.concatenate([key_part, value_part], axis=1).astype(BF16)
    for l in range(list_len):
        slot = slot_ref[step * list_len + l]
        for p in range(peers):

            @pl.when(slot // per_peer == p)
            def _():
                outs[p][slot % per_peer] = parts[l * BLK : (l + 1) * BLK]


def backward(g, slots, queries, attended_grad, probs, kv, peers):
    rows, width = queries.shape
    blocks, _, keys = probs.shape
    list_len = keys // BLK
    pairs = GROUP * rows * keys
    row_spec = pl.BlockSpec((BLK, width), lambda r, s: (r, 0))
    per_peer = (MAJOR * CAP, BLK, WIDE)
    return pl.pallas_call(
        functools.partial(backward_kernel, g, list_len, peers),
        grid_spec=pltpu.PrefetchScalarGridSpec(
            num_scalar_prefetch=1,
            grid=(blocks,),
            in_specs=[
                row_spec,
                row_spec,
                pl.BlockSpec((1, GROUP * BLK, keys), lambda r, s: (r, 0, 0)),
                pl.BlockSpec((1, keys, WIDE), lambda r, s: (r, 0, 0)),
            ],
            out_specs=[pl.BlockSpec((BLK, GROUP_WIDTH), lambda r, s: (r, 0))]
            + [pl.BlockSpec(per_peer, lambda r, s: (0, 0, 0))] * peers,
        ),
        out_shape=[jax.ShapeDtypeStruct((rows, GROUP_WIDTH), BF16)]
        + [jax.ShapeDtypeStruct(per_peer, BF16)] * peers,
        compiler_params=params(48),
        cost_estimate=pl.CostEstimate(
            flops=8 * pairs * HEAD_DIM, bytes_accessed=4 * pairs, transcendentals=0
        ),
        name="backward",
    )(slots, queries, attended_grad, probs, kv)


def column_kernel(peers, blocks, row_ref, place_ref, *refs):
    parts, (own, next_up, next_down, far2, far3, total) = refs[:peers], refs[peers:]
    total[...] = jnp.zeros_like(total)
    for p in range(peers):
        for i in range(MAJOR * CAP):
            place = place_ref[p * MAJOR * CAP + i]

            @pl.when(place >= 0)
            def _():
                total[i // CAP, place] += parts[p][i].astype(F32)

    row = row_ref[0]
    own[...] = total[row].astype(BF16)
    next_up[...] = total[jnp.minimum(row + 1, MAJOR - 1)]
    next_down[...] = total[jnp.maximum(row - 1, 0)]
    far2[...] = total[(row + 2) % MAJOR]
    far3[...] = total[MAJOR - 1 - row].astype(BF16)


def column_sum(row, place, parts, blocks):
    peers = len(parts)
    smem = pl.BlockSpec(memory_space=pltpu.SMEM)
    shape = (blocks, BLK, WIDE)
    return pl.pallas_call(
        functools.partial(column_kernel, peers, blocks),
        in_specs=[smem, smem] + [WHOLE] * peers,
        out_specs=[WHOLE] * 5,
        out_shape=[jax.ShapeDtypeStruct(shape, kind) for kind in (BF16, F32, F32, F32, BF16)],
        scratch_shapes=[pltpu.VMEM((MAJOR,) + shape, F32)],
        compiler_params=params(24),
        name="column_sum",
    )(row, place, *parts)


def shards(patches, out_grad, w_query, w_key, w_value, w_out, key_tiles, key_blocks):
    tokens = patches[0]
    rows = tokens.shape[0]
    tile_count = lax.axis_size("tile")
    plane = tile_count // MAJOR
    my_tile = lax.axis_index("tile")
    my_row, my_place = my_tile // plane, my_tile % plane
    block_count = rows // BLK
    list_len = key_tiles.shape[2]
    entry_count = block_count * list_len

    def hop(value, moves, swap):
        pairs = [
            (
                v * tile_count + a * plane + c,
                (v ^ int(swap)) * tile_count + b * plane + c,
            )
            for v in range(2)
            for a, b in moves
            for c in range(plane)
        ]
        return lax.ppermute(value, AXES, pairs)

    def to_peer(value, p):
        pairs = [(t, t // plane * plane + (t % plane ^ p)) for t in range(tile_count)]
        return lax.ppermute(value, "tile", pairs)

    def plane_rows(table):
        table = table[0].reshape(MAJOR, plane, entry_count)
        return lax.dynamic_index_in_dim(table, my_row, 0, keepdims=False)

    stay = [(z, z) for z in range(MAJOR)]
    up = [(z, z + 1) for z in range(MAJOR - 1)]
    down = [(z + 1, z) for z in range(MAJOR - 1)]

    tiles, picks = plane_rows(key_tiles), plane_rows(key_blocks)
    earlier = jnp.arange(entry_count)[:, None] > jnp.arange(entry_count)[None, :]
    same = (tiles[:, :, None] == tiles[:, None, :]) & earlier[None]
    ranks = jnp.sum(same.astype(jnp.int32), axis=2)
    slots = tiles // plane * CAP + ranks
    columns = tiles % plane
    ids = jnp.arange(MAJOR * CAP, dtype=jnp.int32)
    hits = (slots[:, None, :] == ids[None, :, None]) & (columns == my_place)[:, None, :]
    place = jnp.sum(jnp.where(hits, picks[:, None, :] + 1, 0), axis=2) - 1
    place = place[jnp.arange(plane) ^ my_place].reshape(-1)
    my_slots = lax.dynamic_index_in_dim(
        (columns ^ my_place) * (MAJOR * CAP) + slots, my_place, 0, keepdims=False
    )
    row_index = my_row.reshape(1)

    def chunk_weight(g):
        cols = slice(g * HEAD_DIM, (g + 1) * HEAD_DIM)
        return jnp.concatenate([w_key[:, cols], w_value[:, cols]], axis=1)

    weights = [chunk_weight(g) for g in range(KV_HEADS)]
    arrived = []
    for g in range(KV_HEADS):
        mine = jnp.dot(tokens, weights[g], preferred_element_type=F32).astype(BF16)
        mine = mine.reshape(block_count, BLK, WIDE)
        up1 = hop(mine, up, True)
        down1 = hop(mine, down, True)
        own = hop(mine, stay, True)
        far2 = jnp.where(my_row >= 2, hop(up1, up[1:], False), hop(down1, down[:-1], False))
        far3 = hop(far2, [up[-1], down[0]], False)
        send = pack(row_index, place, (own, up1, down1, far2, far3), plane)
        arrived.append([send[0]] + [to_peer(send[p], p) for p in range(1, plane)])
    queries = jnp.dot(tokens, w_query, preferred_element_type=F32).astype(BF16)
    normed_grad = dot_nt(out_grad[0], w_out)
    kept = [forward(g, my_slots, queries, arrived[g], list_len) for g in range(KV_HEADS)]
    normed_low, attended_grad = normalise(normed_grad, [k[0] for k in kept])
    query_grads, terms = [], []
    for g in range(KV_HEADS):
        query_grad, *back = backward(
            g, my_slots, queries, attended_grad, kept[g][1], kept[g][2], plane
        )
        query_grads.append(query_grad)
        parts = [back[0]] + [to_peer(back[p], p) for p in range(1, plane)]
        own, next_up, next_down, far2, far3 = column_sum(row_index, place, parts, block_count)
        own = hop(own, stay, True)
        far2 = (far2 + hop(far3, [up[0], down[-1]], False).astype(F32)).astype(BF16)
        next_up = (next_up + hop(far2, up[:-1], False).astype(F32)).astype(BF16)
        next_down = (next_down + hop(far2, down[1:], False).astype(F32)).astype(BF16)
        kv_grad = own.astype(F32) + hop(next_up, up, True) + hop(next_down, down, True)
        terms.append(dot_nt(kv_grad.astype(BF16).reshape(rows, WIDE), weights[g]))
    layer_out = jnp.dot(normed_low, w_out, preferred_element_type=F32).astype(BF16)
    total = dot_nt(jnp.concatenate(query_grads, axis=1), w_query)
    for term in terms:
        total += term
    return (layer_out[None], total.astype(BF16)[None])


def solution(mesh):
    in_specs = (
        P("vintage", "tile", None),
        P("vintage", "tile", None),
        P(),
        P(),
        P(),
        P(),
        P("vintage", None, None),
        P("vintage", None, None),
    )
    out_specs = (P("vintage", "tile", None), P("vintage", "tile", None))
    return jax.shard_map(shards, mesh=mesh, in_specs=in_specs, out_specs=out_specs, check_vma=False)
```

time: 261 us -> 272 us (1.042)
  starting transfers between devices: 20.9 us -> 138 us
  waiting for transfers between devices: 133 us -> 50.6 us
  blocking collectives: 29.3 us -> 0 us
  Pallas kernels: 29.4 us -> 51.7 us
  between operations: 14.3 us -> 1.98 us
  local copies, waits for them, and re-layouts: 18.6 us -> 15.7 us
    ppermute x4 -> x72, starting transfers between devices: 1.09 us -> 138 us  [the longest x48 106 us: hop(): return lax.ppermute(value, AXES, pairs)]
    all_to_all x5 -> x0, waiting for transfers between devices: 81.3 us -> none  [exchange(): lax.all_to_all(value, 'tile', split_axis=0, concat_axis=0, tiled=True, ax...]
    all_gather x2 -> x0, waiting for transfers between devices: 50.4 us -> none  [shards(): lax.all_gather(from_partner(mine), 'tile', axis_index_groups=columns, til...]
    ppermute x4 -> x72, waiting for transfers between devices: 1.74 us -> 50.6 us  [the longest x48 30.1 us: hop(): return lax.ppermute(value, AXES, pairs)]
    all_to_all x1 -> x0, blocking collectives: 29.3 us -> none  [exchange(): lax.all_to_all(value, 'tile', split_axis=0, concat_axis=0, tiled=True, ax...]
    pallas_call x3 -> x17, Pallas kernels: 29.4 us -> 51.7 us  [the longest x4 24.4 us: backward(): pl.pallas_call(functools.partial(backward_kernel, g, list_len, peers), gr...]
    all_to_all x5 -> x0, starting transfers between devices: 19.7 us -> none  [exchange(): lax.all_to_all(value, 'tile', split_axis=0, concat_axis=0, tiled=True, ax...]
    gather x2 -> x1, local copies, waits for them, and re-layouts: 5.23 us -> 0.56 us  [shards(): place = place[jnp.arange(plane) ^ my_place].reshape(-1)]
  transfers between devices with their start and end apart: 11 -> 72, of which waited for: 9 -> 19; matrix products, arithmetic and copies ran while one was open for 8% -> 5% of each run, Pallas kernels for 1% -> 15%
where the time goes in v3:
time: 272 us; the launch traced here: 271 us
  starting transfers between devices  138 us (51%)
  Pallas kernels  51.7 us (19%)
  waiting for transfers between devices  50.6 us (19%)
  local copies, waits for them, and re-layouts  15.7 us (6%)
  matrix products  11.6 us (4%)
    ppermute x48, starting transfers between devices, hop(): return lax.ppermute(value, AXES, pairs)  106 us
    ppermute x24, starting transfers between devices, to_peer(): return lax.ppermute(value, 'tile', pairs)  32.3 us
    ppermute x48, waiting for transfers between devices, hop(): return lax.ppermute(value, AXES, pairs)  30.1 us
    pallas_call x4, Pallas kernels, backward(): pl.pallas_call(functools.partial(backward_kernel, g, list_len, peers), gr...  24.4 us
    ppermute x24, waiting for transfers between devices, to_peer(): return lax.ppermute(value, 'tile', pairs)  20.5 us
    pallas_call x4, Pallas kernels, forward(): pl.pallas_call(functools.partial(forward_kernel, g, list_len, len(sources...  17.8 us
    unnamed x66, local copies, waits for them, and re-layouts  9.93 us
    dot_general x6, matrix products, dot_nt(): lax.dot_general(a, b, (((1,), (1,)), ((), ())), preferred_element_type=F32)  6.03 us
  transfers between devices with their start and end apart: 72, of which 19 were waited for; matrix products, arithmetic and copies ran while one was open for 5% of the time, Pallas kernels for 15%

profile of v3, /device:TPU:0, one launch (start us, length us, event | category | flops | bytes accessed | tf_op | source)
XLA Modules:
  0.0 271.0 jit_solution(11870413805394359959)
XLA Ops:
  0.7 2.5 fusion.40
  5.9 5.0 %collective-permute-start.1 = (bf16[4,128,128]{2,1,0:T(8,128)(2,1)S(1)}, bf16[4,128,128]{2,1,0:T(8,128)(2,1)S(1)}, u32[]{:S(2)}, u32[]{:S(2)}) collective-permute-start(bf16[4,128,128]{2,1,0:T(8,128)(2,1)S(1)} %bitcast.58), channel_id=1, source_target_pairs={{0,20},{1,21},{2,22},{3,23},{4,24},{5,25},{6,26},{7,27},{8,28},{9,... | collective-permute-start | bytes 393224 | tf_op jit(solution)/shard_map/ppermute | solution.py:279
  13.6 4.4 %collective-permute-start.10 = (bf16[4,128,128]{2,1,0:T(8,128)(2,1)}, bf16[4,128,128]{2,1,0:T(8,128)(2,1)S(1)}, u32[]{:S(2)}, u32[]{:S(2)}) collective-permute-start(bf16[4,128,128]{2,1,0:T(8,128)(2,1)} %bitcast.61), channel_id=1, source_target_pairs={{0,20},{1,21},{2,22},{3,23},{4,24},{5,25},{6,26},{7,27},{8,28},{9,... | collective-permute-start | bytes 393224 | tf_op jit(solution)/shard_map/ppermute | solution.py:279
  26.4 7.6 %collective-permute-start.19 = (bf16[4,128,128]{2,1,0:T(8,128)(2,1)}, bf16[4,128,128]{2,1,0:T(8,128)(2,1)S(1)}, u32[]{:S(2)}, u32[]{:S(2)}) collective-permute-start(bf16[4,128,128]{2,1,0:T(8,128)(2,1)} %bitcast.12), channel_id=1, source_target_pairs={{0,20},{1,21},{2,22},{3,23},{4,24},{5,25},{6,26},{7,27},{8,28},{9,... | collective-permute-start | bytes 393224 | tf_op jit(solution)/shard_map/ppermute | solution.py:279
  38.5 5.9 %collective-permute-start.28 = (bf16[4,128,128]{2,1,0:T(8,128)(2,1)}, bf16[4,128,128]{2,1,0:T(8,128)(2,1)S(1)}, u32[]{:S(2)}, u32[]{:S(2)}) collective-permute-start(bf16[4,128,128]{2,1,0:T(8,128)(2,1)} %bitcast.14), channel_id=1, source_target_pairs={{0,20},{1,21},{2,22},{3,23},{4,24},{5,25},{6,26},{7,27},{8,28},{9,... | collective-permute-start | bytes 393224 | tf_op jit(solution)/shard_map/ppermute | solution.py:279
  49.2 3.1 %collective-permute-done.22 = bf16[4,128,128]{2,1,0:T(8,128)(2,1)S(1)} collective-permute-done((bf16[4,128,128]{2,1,0:T(8,128)(2,1)S(1)}, bf16[4,128,128]{2,1,0:T(8,128)(2,1)S(1)}, u32[]{:S(2)}, u32[]{:S(2)}) %collective-permute-start.22) | collective-permute-done | bytes 131104 | tf_op jit(solution)/shard_map/ppermute | solution.py:279
  55.0 11.2 %collective-permute-done.14.far3 = bf16[4,128,128]{2,1,0:T(8,128)(2,1)S(1)} collective-permute-done((bf16[4,128,128]{2,1,0:T(8,128)(2,1)S(1)}, bf16[4,128,128]{2,1,0:T(8,128)(2,1)S(1)}, u32[]{:S(2)}, u32[]{:S(2)}) %collective-permute-start.14) | collective-permute-done | bytes 131104 | tf_op jit(solution)/shard_map/ppermute | solution.py:279
  84.8 3.0 %collective-permute-done.6.refs_1_ = bf16[8,128,128]{2,1,0:T(8,128)(2,1)S(1)} collective-permute-done((bf16[8,128,128]{2,1,0:T(8,128)(2,1)}, bf16[8,128,128]{2,1,0:T(8,128)(2,1)S(1)}, u32[]{:S(2)}, u32[]{:S(2)}) %collective-permute-start.6) | collective-permute-done | bytes 262176 | tf_op jit(solution)/shard_map/ppermute | solution.py:283
  87.9 2.5 collective-permute-start.26
  90.3 2.3 fusion.19.ng_ref
  95.0 4.2 %collective-permute-done.24.refs_1_ = bf16[8,128,128]{2,1,0:T(8,128)(2,1)S(1)} collective-permute-done((bf16[8,128,128]{2,1,0:T(8,128)(2,1)S(1)}, bf16[8,128,128]{2,1,0:T(8,128)(2,1)S(1)}, u32[]{:S(2)}, u32[]{:S(2)}) %collective-permute-start.24) | collective-permute-done | bytes 262176 | tf_op jit(solution)/shard_map/ppermute | solution.py:283
  99.2 2.5 collective-permute-start.35
  102.1 3.7 %collective-permute-done.26.refs_3_ = bf16[8,128,128]{2,1,0:T(8,128)(2,1)S(1)} collective-permute-done((bf16[8,128,128]{2,1,0:T(8,128)(2,1)S(1)}, bf16[8,128,128]{2,1,0:T(8,128)(2,1)S(1)}, u32[]{:S(2)}, u32[]{:S(2)}) %collective-permute-start.26) | collective-permute-done | bytes 262176 | tf_op jit(solution)/shard_map/ppermute | solution.py:283
  108.0 4.3 %forward.6 = (bf16[512,192]{1,0:T(8,128)(2,1)S(1)}, f32[4,384,512]{2,1,0:T(8,128)S(1)}, bf16[4,512,128]{2,1,0:T(8,128)(2,1)S(1)}) custom-call(s32[16]{0:T(128)S(1)} %fusion.28.slot_ref, bf16[512,768]{1,0:T(8,128)(2,1)S(1)} %convolution_convert_fusion.1.q_ref, bf16[8,128,128]{2,1,0:T(8,128)(2,1)S(1)} %get-tuple-element.82.refs_0_, ...), custom_call_target="tpu_custom_call" | custom-call | flops 201326592 | bytes 3145728 | tf_op jit(solution)/shard_map/forward/pallas_call | solution.py:116
  112.4 1.6 copy-done.2
  114.0 4.3 %forward.4 = (bf16[512,192]{1,0:T(8,128)(2,1)S(1)}, f32[4,384,512]{2,1,0:T(8,128)S(1)}, bf16[4,512,128]{2,1,0:T(8,128)(2,1)S(1)}) custom-call(s32[16]{0:T(128)S(1)} %fusion.28.slot_ref, bf16[512,768]{1,0:T(8,128)(2,1)S(1)} %convolution_convert_fusion.1.q_ref, bf16[8,128,128]{2,1,0:T(8,128)(2,1)S(1)} %get-tuple-element.72.refs_0_, ...), custom_call_target="tpu_custom_call" | custom-call | flops 201326592 | bytes 3145728 | tf_op jit(solution)/shard_map/forward/pallas_call | solution.py:116
  118.3 1.7 copy-done.1
  120.0 3.7 %collective-permute-done.16.refs_2_ = bf16[8,128,128]{2,1,0:T(8,128)(2,1)S(1)} collective-permute-done((bf16[8,128,128]{2,1,0:T(8,128)(2,1)S(1)}, bf16[8,128,128]{2,1,0:T(8,128)(2,1)S(1)}, u32[]{:S(2)}, u32[]{:S(2)}) %collective-permute-start.16) | collective-permute-done | bytes 262176 | tf_op jit(solution)/shard_map/ppermute | solution.py:283
  123.7 4.6 %forward.5 = (bf16[512,192]{1,0:T(8,128)(2,1)S(1)}, f32[4,384,512]{2,1,0:T(8,128)S(1)}, bf16[4,512,128]{2,1,0:T(8,128)(2,1)S(1)}) custom-call(s32[16]{0:T(128)S(1)} %fusion.28.slot_ref, bf16[512,768]{1,0:T(8,128)(2,1)S(1)} %convolution_convert_fusion.1.q_ref, bf16[8,128,128]{2,1,0:T(8,128)(2,1)S(1)} %get-tuple-element.77.refs_0_, ...), custom_call_target="tpu_custom_call" | custom-call | flops 201326592 | bytes 3145728 | tf_op jit(solution)/shard_map/forward/pallas_call | solution.py:116
  128.4 1.8 copy-done.3
  130.1 4.6 %forward.7 = (bf16[512,192]{1,0:T(8,128)(2,1)S(1)}, f32[4,384,512]{2,1,0:T(8,128)S(1)}, bf16[4,512,128]{2,1,0:T(8,128)(2,1)S(1)}) custom-call(s32[16]{0:T(128)S(1)} %fusion.28.slot_ref, bf16[512,768]{1,0:T(8,128)(2,1)S(1)} %convolution_convert_fusion.1.q_ref, bf16[8,128,128]{2,1,0:T(8,128)(2,1)S(1)} %get-tuple-element.87.refs_0_, ...), custom_call_target="tpu_custom_call" | custom-call | flops 201326592 | bytes 3145728 | tf_op jit(solution)/shard_map/forward/pallas_call | solution.py:116
  134.7 1.7 copy-done.4
  137.8 6.1 %backward.7 = (bf16[512,192]{1,0:T(8,128)(2,1)S(1)}, bf16[8,128,128]{2,1,0:T(8,128)(2,1)S(1)}, bf16[8,128,128]{2,1,0:T(8,128)(2,1)S(1)}, bf16[8,128,128]{2,1,0:T(8,128)(2,1)S(1)}, bf16[8,128,128]{2,1,0:T(8,128)(2,1)S(1)}) custom-call(s32[16]{0:T(128)S(1)} %fusion.28.slot_ref, bf16[512,768]{1,0:T(8,128)(2,1)S(1)} %convolution_convert_fusion.1.q_ref, ...), custom_call_target="tpu_custom_call" | custom-call | flops 402653184 | bytes 3145728 | tf_op jit(solution)/shard_map/backward/pallas_call | solution.py:200
  143.9 1.6 collective-permute-start.63
  147.5 6.1 %backward.6 = (bf16[512,192]{1,0:T(8,128)(2,1)S(1)}, bf16[8,128,128]{2,1,0:T(8,128)(2,1)S(1)}, bf16[8,128,128]{2,1,0:T(8,128)(2,1)S(1)}, bf16[8,128,128]{2,1,0:T(8,128)(2,1)S(1)}, bf16[8,128,128]{2,1,0:T(8,128)(2,1)S(1)}) custom-call(s32[16]{0:T(128)S(1)} %fusion.28.slot_ref, bf16[512,768]{1,0:T(8,128)(2,1)S(1)} %convolution_convert_fusion.1.q_ref, ...), custom_call_target="tpu_custom_call" | custom-call | flops 402653184 | bytes 3145728 | tf_op jit(solution)/shard_map/backward/pallas_call | solution.py:200
  155.1 1.5 collective-permute-start.55
  156.6 6.1 %backward.5 = (bf16[512,192]{1,0:T(8,128)(2,1)S(1)}, bf16[8,128,128]{2,1,0:T(8,128)(2,1)S(1)}, bf16[8,128,128]{2,1,0:T(8,128)(2,1)S(1)}, bf16[8,128,128]{2,1,0:T(8,128)(2,1)S(1)}, bf16[8,128,128]{2,1,0:T(8,128)(2,1)S(1)}) custom-call(s32[16]{0:T(128)S(1)} %fusion.28.slot_ref, bf16[512,768]{1,0:T(8,128)(2,1)S(1)} %convolution_convert_fusion.1.q_ref, ...), custom_call_target="tpu_custom_call" | custom-call | flops 402653184 | bytes 3145728 | tf_op jit(solution)/shard_map/backward/pallas_call | solution.py:200
  164.8 6.1 %backward.4 = (bf16[512,192]{1,0:T(8,128)(2,1)S(1)}, bf16[8,128,128]{2,1,0:T(8,128)(2,1)S(1)}, bf16[8,128,128]{2,1,0:T(8,128)(2,1)S(1)}, bf16[8,128,128]{2,1,0:T(8,128)(2,1)S(1)}, bf16[8,128,128]{2,1,0:T(8,128)(2,1)S(1)}) custom-call(s32[16]{0:T(128)S(1)} %fusion.28.slot_ref, bf16[512,768]{1,0:T(8,128)(2,1)S(1)} %convolution_convert_fusion.1.q_ref, ...), custom_call_target="tpu_custom_call" | custom-call | flops 402653184 | bytes 3145728 | tf_op jit(solution)/shard_map/backward/pallas_call | solution.py:200
  170.9 1.6 collective-permute-start.46
  176.0 2.5 collective-permute-start.38
  180.4 5.4 %collective-permute-done.46.refs_2_ = bf16[8,128,128]{2,1,0:T(8,128)(2,1)S(1)} collective-permute-done((bf16[8,128,128]{2,1,0:T(8,128)(2,1)S(1)}, bf16[8,128,128]{2,1,0:T(8,128)(2,1)S(1)}, u32[]{:S(2)}, u32[]{:S(2)}) %collective-permute-start.46) | collective-permute-done | bytes 262176 | tf_op jit(solution)/shard_map/ppermute | solution.py:283
  185.9 4.1 %collective-permute-start.67 = (bf16[4,128,128]{2,1,0:T(8,128)(2,1)S(1)}, bf16[4,128,128]{2,1,0:T(8,128)(2,1)S(1)}, u32[]{:S(2)}, u32[]{:S(2)}) collective-permute-start(bf16[4,128,128]{2,1,0:T(8,128)(2,1)S(1)} %get-tuple-element.140), channel_id=1, source_target_pairs={{0,4},{1,5},{2,6},{3,7},{12,8},{13,9},{14,10},{15,11},{16,20},{17,... | collective-permute-start | bytes 393224 | tf_op jit(solution)/shard_map/ppermute | solution.py:279
  190.0 1.7 fusion
  194.3 3.7 %collective-permute-start.58 = (bf16[4,128,128]{2,1,0:T(8,128)(2,1)S(1)}, bf16[4,128,128]{2,1,0:T(8,128)(2,1)S(1)}, u32[]{:S(2)}, u32[]{:S(2)}) collective-permute-start(bf16[4,128,128]{2,1,0:T(8,128)(2,1)S(1)} %get-tuple-element.131), channel_id=1, source_target_pairs={{0,4},{1,5},{2,6},{3,7},{12,8},{13,9},{14,10},{15,11},{16,20},{17,... | collective-permute-start | bytes 393224 | tf_op jit(solution)/shard_map/ppermute | solution.py:279
  200.7 4.2 %collective-permute-start.40 = (bf16[4,128,128]{2,1,0:T(8,128)(2,1)S(1)}, bf16[4,128,128]{2,1,0:T(8,128)(2,1)S(1)}, u32[]{:S(2)}, u32[]{:S(2)}) collective-permute-start(bf16[4,128,128]{2,1,0:T(8,128)(2,1)S(1)} %get-tuple-element.113), channel_id=1, source_target_pairs={{0,4},{1,5},{2,6},{3,7},{12,8},{13,9},{14,10},{15,11},{16,20},{17,... | collective-permute-start | bytes 393224 | tf_op jit(solution)/shard_map/ppermute | solution.py:279
  205.6 1.7 collective-permute-done.40
  207.4 4.3 %collective-permute-start.68 = (bf16[4,128,128]{2,1,0:T(8,128)(2,1)S(1)}, bf16[4,128,128]{2,1,0:T(8,128)(2,1)S(1)}, u32[]{:S(2)}, u32[]{:S(2)}) collective-permute-start(bf16[4,128,128]{2,1,0:T(8,128)(2,1)S(1)} %add_convert_fusion.4), channel_id=1, source_target_pairs={{0,4},{1,5},{2,6},{3,7},{4,8},{5,9},{6,10},{7,11},{16,20},{17,21},... | collective-permute-start | bytes 393224 | tf_op jit(solution)/shard_map/ppermute | solution.py:279
  212.5 1.7 collective-permute-done.68
  214.2 4.3 %collective-permute-start.59 = (bf16[4,128,128]{2,1,0:T(8,128)(2,1)S(1)}, bf16[4,128,128]{2,1,0:T(8,128)(2,1)S(1)}, u32[]{:S(2)}, u32[]{:S(2)}) collective-permute-start(bf16[4,128,128]{2,1,0:T(8,128)(2,1)S(1)} %add_convert_fusion.8), channel_id=1, source_target_pairs={{0,4},{1,5},{2,6},{3,7},{4,8},{5,9},{6,10},{7,11},{16,20},{17,21},... | collective-permute-start | bytes 393224 | tf_op jit(solution)/shard_map/ppermute | solution.py:279
  219.3 2.8 %collective-permute-done.59 = bf16[4,128,128]{2,1,0:T(8,128)(2,1)S(1)} collective-permute-done((bf16[4,128,128]{2,1,0:T(8,128)(2,1)S(1)}, bf16[4,128,128]{2,1,0:T(8,128)(2,1)S(1)}, u32[]{:S(2)}, u32[]{:S(2)}) %collective-permute-start.59) | collective-permute-done | bytes 131104 | tf_op jit(solution)/shard_map/ppermute | solution.py:279
  222.1 4.4 %collective-permute-start.50 = (bf16[4,128,128]{2,1,0:T(8,128)(2,1)S(1)}, bf16[4,128,128]{2,1,0:T(8,128)(2,1)S(1)}, u32[]{:S(2)}, u32[]{:S(2)}) collective-permute-start(bf16[4,128,128]{2,1,0:T(8,128)(2,1)S(1)} %add_convert_fusion.12), channel_id=1, source_target_pairs={{0,4},{1,5},{2,6},{3,7},{4,8},{5,9},{6,10},{7,11},{16,20},{17,21},... | collective-permute-start | bytes 393224 | tf_op jit(solution)/shard_map/ppermute | solution.py:279
  227.4 9.7 %collective-permute-start.41 = (bf16[4,128,128]{2,1,0:T(8,128)(2,1)S(1)}, bf16[4,128,128]{2,1,0:T(8,128)(2,1)S(1)}, u32[]{:S(2)}, u32[]{:S(2)}) collective-permute-start(bf16[4,128,128]{2,1,0:T(8,128)(2,1)S(1)} %add_convert_fusion.16), channel_id=1, source_target_pairs={{0,4},{1,5},{2,6},{3,7},{4,8},{5,9},{6,10},{7,11},{16,20},{17,21},... | collective-permute-start | bytes 393224 | tf_op jit(solution)/shard_map/ppermute | solution.py:279
  237.2 2.5 collective-permute-done.41
  241.0 4.3 %collective-permute-start.42 = (bf16[4,128,128]{2,1,0:T(8,128)(2,1)S(1)}, bf16[4,128,128]{2,1,0:T(8,128)(2,1)S(1)}, u32[]{:S(2)}, u32[]{:S(2)}) collective-permute-start(bf16[4,128,128]{2,1,0:T(8,128)(2,1)S(1)} %add_convert_fusion.15), channel_id=1, source_target_pairs={{0,20},{1,21},{2,22},{3,23},{4,24},{5,25},{6,26},{7,27},{8,28},{9,... | collective-permute-start | bytes 393224 | tf_op jit(solution)/shard_map/ppermute | solution.py:279
  249.0 4.1 %collective-permute-start.51 = (bf16[4,128,128]{2,1,0:T(8,128)(2,1)S(1)}, bf16[4,128,128]{2,1,0:T(8,128)(2,1)S(1)}, u32[]{:S(2)}, u32[]{:S(2)}) collective-permute-start(bf16[4,128,128]{2,1,0:T(8,128)(2,1)S(1)} %add_convert_fusion.11), channel_id=1, source_target_pairs={{0,20},{1,21},{2,22},{3,23},{4,24},{5,25},{6,26},{7,27},{8,28},{9,... | collective-permute-start | bytes 393224 | tf_op jit(solution)/shard_map/ppermute | solution.py:279
  256.8 4.5 %collective-permute-start.60 = (bf16[4,128,128]{2,1,0:T(8,128)(2,1)S(1)}, bf16[4,128,128]{2,1,0:T(8,128)(2,1)S(1)}, u32[]{:S(2)}, u32[]{:S(2)}) collective-permute-start(bf16[4,128,128]{2,1,0:T(8,128)(2,1)S(1)} %add_convert_fusion.7), channel_id=1, source_target_pairs={{0,20},{1,21},{2,22},{3,23},{4,24},{5,25},{6,26},{7,27},{8,28},{9,... | collective-permute-start | bytes 393224 | tf_op jit(solution)/shard_map/ppermute | solution.py:279
  261.9 3.8 %collective-permute-start.69 = (bf16[4,128,128]{2,1,0:T(8,128)(2,1)S(1)}, bf16[4,128,128]{2,1,0:T(8,128)(2,1)S(1)}, u32[]{:S(2)}, u32[]{:S(2)}) collective-permute-start(bf16[4,128,128]{2,1,0:T(8,128)(2,1)S(1)} %add_convert_fusion.3), channel_id=1, source_target_pairs={{0,20},{1,21},{2,22},{3,23},{4,24},{5,25},{6,26},{7,27},{8,28},{9,... | collective-permute-start | bytes 393224 | tf_op jit(solution)/shard_map/ppermute | solution.py:279
  266.2 3.1 %collective-permute-done.69 = bf16[4,128,128]{2,1,0:T(8,128)(2,1)S(1)} collective-permute-done((bf16[4,128,128]{2,1,0:T(8,128)(2,1)S(1)}, bf16[4,128,128]{2,1,0:T(8,128)(2,1)S(1)}, u32[]{:S(2)}, u32[]{:S(2)}) %collective-permute-start.69) | collective-permute-done | bytes 131104 | tf_op jit(solution)/shard_map/ppermute | solution.py:279
  (230 shorter events, 80.8 us)
Async XLA Ops:
  4.6 17.5 %collective-permute-start.2 = (bf16[4,128,128]{2,1,0:T(8,128)(2,1)S(1)}, bf16[4,128,128]{2,1,0:T(8,128)(2,1)S(1)}, u32[]{:S(2)}, u32[]{:S(2)}) collective-permute-start(bf16[4,128,128]{2,1,0:T(8,128)(2,1)S(1)} %bitcast.57), channel_id=1, source_target_pairs={{4,16},{5,17},{6,18},{7,19},{8,20},{9,21},{10,22},{11,23},{12,24},... | collective-permute-start | bytes 393224 | tf_op jit(solution)/shard_map/ppermute | solution.py:279
  5.9 17.5 %collective-permute-start.1 = (bf16[4,128,128]{2,1,0:T(8,128)(2,1)S(1)}, bf16[4,128,128]{2,1,0:T(8,128)(2,1)S(1)}, u32[]{:S(2)}, u32[]{:S(2)}) collective-permute-start(bf16[4,128,128]{2,1,0:T(8,128)(2,1)S(1)} %bitcast.58), channel_id=1, source_target_pairs={{0,20},{1,21},{2,22},{3,23},{4,24},{5,25},{6,26},{7,27},{8,28},{9,... | collective-permute-start | bytes 393224 | tf_op jit(solution)/shard_map/ppermute | solution.py:279
  12.3 14.1 %collective-permute-start.11 = (bf16[4,128,128]{2,1,0:T(8,128)(2,1)}, bf16[4,128,128]{2,1,0:T(8,128)(2,1)S(1)}, u32[]{:S(2)}, u32[]{:S(2)}) collective-permute-start(bf16[4,128,128]{2,1,0:T(8,128)(2,1)} %bitcast.60), channel_id=1, source_target_pairs={{4,16},{5,17},{6,18},{7,19},{8,20},{9,21},{10,22},{11,23},{12,24},... | collective-permute-start | bytes 393224 | tf_op jit(solution)/shard_map/ppermute | solution.py:279
  13.6 20.4 %collective-permute-start.10 = (bf16[4,128,128]{2,1,0:T(8,128)(2,1)}, bf16[4,128,128]{2,1,0:T(8,128)(2,1)S(1)}, u32[]{:S(2)}, u32[]{:S(2)}) collective-permute-start(bf16[4,128,128]{2,1,0:T(8,128)(2,1)} %bitcast.61), channel_id=1, source_target_pairs={{0,20},{1,21},{2,22},{3,23},{4,24},{5,25},{6,26},{7,27},{8,28},{9,... | collective-permute-start | bytes 393224 | tf_op jit(solution)/shard_map/ppermute | solution.py:279
  19.3 17.8 %collective-permute-start.20 = (bf16[4,128,128]{2,1,0:T(8,128)(2,1)}, bf16[4,128,128]{2,1,0:T(8,128)(2,1)S(1)}, u32[]{:S(2)}, u32[]{:S(2)}) collective-permute-start(bf16[4,128,128]{2,1,0:T(8,128)(2,1)} %bitcast.12), channel_id=1, source_target_pairs={{4,16},{5,17},{6,18},{7,19},{8,20},{9,21},{10,22},{11,23},{12,24},... | collective-permute-start | bytes 393224 | tf_op jit(solution)/shard_map/ppermute | solution.py:279
  22.1 13.0 %collective-permute-start.4 = (bf16[4,128,128]{2,1,0:T(8,128)(2,1)S(1)}, bf16[4,128,128]{2,1,0:T(8,128)(2,1)S(1)}, u32[]{:S(2)}, u32[]{:S(2)}) collective-permute-start(bf16[4,128,128]{2,1,0:T(8,128)(2,1)S(1)} %collective-permute-done.2.down1), channel_id=1, source_target_pairs={{4,0},{5,1},{6,2},{7,3},{8,4},{9,5},{10,6},{11,7},{20,16},{21,17},... | collective-permute-start | bytes 393224 | tf_op jit(solution)/shard_map/ppermute | solution.py:279
  23.4 13.0 %collective-permute-start.3 = (bf16[4,128,128]{2,1,0:T(8,128)(2,1)S(1)}, bf16[4,128,128]{2,1,0:T(8,128)(2,1)S(1)}, u32[]{:S(2)}, u32[]{:S(2)}) collective-permute-start(bf16[4,128,128]{2,1,0:T(8,128)(2,1)S(1)} %collective-permute-done.1.up1), channel_id=1, source_target_pairs={{4,8},{5,9},{6,10},{7,11},{8,12},{9,13},{10,14},{11,15},{20,24},{2... | collective-permute-start | bytes 393224 | tf_op jit(solution)/shard_map/ppermute | solution.py:279
  26.4 12.1 %collective-permute-start.19 = (bf16[4,128,128]{2,1,0:T(8,128)(2,1)}, bf16[4,128,128]{2,1,0:T(8,128)(2,1)S(1)}, u32[]{:S(2)}, u32[]{:S(2)}) collective-permute-start(bf16[4,128,128]{2,1,0:T(8,128)(2,1)} %bitcast.12), channel_id=1, source_target_pairs={{0,20},{1,21},{2,22},{3,23},{4,24},{5,25},{6,26},{7,27},{8,28},{9,... | collective-permute-start | bytes 393224 | tf_op jit(solution)/shard_map/ppermute | solution.py:279
  34.0 12.4 %collective-permute-start.9 = (bf16[4,128,128]{2,1,0:T(8,128)(2,1)S(1)}, bf16[4,128,128]{2,1,0:T(8,128)(2,1)S(1)}, u32[]{:S(2)}, u32[]{:S(2)}) collective-permute-start(bf16[4,128,128]{2,1,0:T(8,128)(2,1)S(1)} %bitcast.62), channel_id=1, source_target_pairs={{0,16},{1,17},{2,18},{3,19},{4,20},{5,21},{6,22},{7,23},{8,24},{9,... | collective-permute-start | bytes 393224 | tf_op jit(solution)/shard_map/ppermute | solution.py:279
  38.5 10.0 %collective-permute-start.28 = (bf16[4,128,128]{2,1,0:T(8,128)(2,1)}, bf16[4,128,128]{2,1,0:T(8,128)(2,1)S(1)}, u32[]{:S(2)}, u32[]{:S(2)}) collective-permute-start(bf16[4,128,128]{2,1,0:T(8,128)(2,1)} %bitcast.14), channel_id=1, source_target_pairs={{0,20},{1,21},{2,22},{3,23},{4,24},{5,25},{6,26},{7,27},{8,28},{9,... | collective-permute-start | bytes 393224 | tf_op jit(solution)/shard_map/ppermute | solution.py:279
  46.4 22.6 %collective-permute-start = (bf16[4,128,128]{2,1,0:T(8,128)(2,1)S(1)}, bf16[4,128,128]{2,1,0:T(8,128)(2,1)S(1)}, u32[]{:S(2)}, u32[]{:S(2)}) collective-permute-start(bf16[4,128,128]{2,1,0:T(8,128)(2,1)S(1)} %bitcast.59), channel_id=1, source_target_pairs={{0,16},{1,17},{2,18},{3,19},{4,20},{5,21},{6,22},{7,23},{8,24},{9,... | collective-permute-start | bytes 393224 | tf_op jit(solution)/shard_map/ppermute | solution.py:279
  47.2 25.7 %collective-permute-start.31 = (bf16[4,128,128]{2,1,0:T(8,128)(2,1)S(1)}, bf16[4,128,128]{2,1,0:T(8,128)(2,1)S(1)}, u32[]{:S(2)}, u32[]{:S(2)}) collective-permute-start(bf16[4,128,128]{2,1,0:T(8,128)(2,1)S(1)} %collective-permute-done.29.down1), channel_id=1, source_target_pairs={{4,0},{5,1},{6,2},{7,3},{8,4},{9,5},{10,6},{11,7},{20,16},{21,17},... | collective-permute-start | bytes 393224 | tf_op jit(solution)/shard_map/ppermute | solution.py:279
  48.5 25.8 %collective-permute-start.30 = (bf16[4,128,128]{2,1,0:T(8,128)(2,1)S(1)}, bf16[4,128,128]{2,1,0:T(8,128)(2,1)S(1)}, u32[]{:S(2)}, u32[]{:S(2)}) collective-permute-start(bf16[4,128,128]{2,1,0:T(8,128)(2,1)S(1)} %collective-permute-done.28.up1), channel_id=1, source_target_pairs={{4,8},{5,9},{6,10},{7,11},{8,12},{9,13},{10,14},{11,15},{20,24},{2... | collective-permute-start | bytes 393224 | tf_op jit(solution)/shard_map/ppermute | solution.py:279
  52.4 17.2 %collective-permute-start.5 = (bf16[4,128,128]{2,1,0:T(8,128)(2,1)S(1)}, bf16[4,128,128]{2,1,0:T(8,128)(2,1)S(1)}, u32[]{:S(2)}, u32[]{:S(2)}) collective-permute-start(bf16[4,128,128]{2,1,0:T(8,128)(2,1)S(1)} %broadcast_select_fusion.3.far2), channel_id=1, source_target_pairs={{8,12},{9,13},{10,14},{11,15},{4,0},{5,1},{6,2},{7,3},{24,28},{25,... | collective-permute-start | bytes 393224 | tf_op jit(solution)/shard_map/ppermute | solution.py:279
  53.7 12.6 %collective-permute-start.14 = (bf16[4,128,128]{2,1,0:T(8,128)(2,1)S(1)}, bf16[4,128,128]{2,1,0:T(8,128)(2,1)S(1)}, u32[]{:S(2)}, u32[]{:S(2)}) collective-permute-start(bf16[4,128,128]{2,1,0:T(8,128)(2,1)S(1)} %broadcast_select_fusion.2.far2), channel_id=1, source_target_pairs={{8,12},{9,13},{10,14},{11,15},{4,0},{5,1},{6,2},{7,3},{24,28},{25,... | collective-permute-start | bytes 393224 | tf_op jit(solution)/shard_map/ppermute | solution.py:279
  69.0 10.0 %collective-permute-start.27 = (bf16[4,128,128]{2,1,0:T(8,128)(2,1)}, bf16[4,128,128]{2,1,0:T(8,128)(2,1)S(1)}, u32[]{:S(2)}, u32[]{:S(2)}) collective-permute-start(bf16[4,128,128]{2,1,0:T(8,128)(2,1)} %bitcast.14), channel_id=1, source_target_pairs={{0,16},{1,17},{2,18},{3,19},{4,20},{5,21},{6,22},{7,23},{8,24},{9,... | collective-permute-start | bytes 393224 | tf_op jit(solution)/shard_map/ppermute | solution.py:279
  72.9 10.4 %collective-permute-start.15 = (bf16[8,128,128]{2,1,0:T(8,128)(2,1)}, bf16[8,128,128]{2,1,0:T(8,128)(2,1)S(1)}, u32[]{:S(2)}, u32[]{:S(2)}) collective-permute-start(bf16[8,128,128]{2,1,0:T(8,128)(2,1)} %get-tuple-element.78), channel_id=1, source_target_pairs={{0,1},{1,0},{2,3},{3,2},{4,5},{5,4},{6,7},{7,6},{8,9},{9,8},{10,11... | collective-permute-start | bytes 786440 | tf_op jit(solution)/shard_map/ppermute | solution.py:283
  74.4 13.5 %collective-permute-start.6 = (bf16[8,128,128]{2,1,0:T(8,128)(2,1)}, bf16[8,128,128]{2,1,0:T(8,128)(2,1)S(1)}, u32[]{:S(2)}, u32[]{:S(2)}) collective-permute-start(bf16[8,128,128]{2,1,0:T(8,128)(2,1)} %get-tuple-element.73), channel_id=1, source_target_pairs={{0,1},{1,0},{2,3},{3,2},{4,5},{5,4},{6,7},{7,6},{8,9},{9,8},{10,11... | collective-permute-start | bytes 786440 | tf_op jit(solution)/shard_map/ppermute | solution.py:283
  76.8 16.7 %collective-permute-start.7 = (bf16[8,128,128]{2,1,0:T(8,128)(2,1)}, bf16[8,128,128]{2,1,0:T(8,128)(2,1)S(1)}, u32[]{:S(2)}, u32[]{:S(2)}) collective-permute-start(bf16[8,128,128]{2,1,0:T(8,128)(2,1)} %copy-done.10), channel_id=1, source_target_pairs={{0,2},{1,3},{2,0},{3,1},{4,6},{5,7},{6,4},{7,5},{8,10},{9,11},{10,... | collective-permute-start | bytes 786440 | tf_op jit(solution)/shard_map/ppermute | solution.py:283
  79.0 15.5 %collective-permute-start.8 = (bf16[8,128,128]{2,1,0:T(8,128)(2,1)}, bf16[8,128,128]{2,1,0:T(8,128)(2,1)S(1)}, u32[]{:S(2)}, u32[]{:S(2)}) collective-permute-start(bf16[8,128,128]{2,1,0:T(8,128)(2,1)} %copy-done.9), channel_id=1, source_target_pairs={{0,3},{1,2},{2,1},{3,0},{4,7},{5,6},{6,5},{7,4},{8,11},{9,10},{10,... | collective-permute-start | bytes 786440 | tf_op jit(solution)/shard_map/ppermute | solution.py:283
  81.8 17.3 %collective-permute-start.24 = (bf16[8,128,128]{2,1,0:T(8,128)(2,1)S(1)}, bf16[8,128,128]{2,1,0:T(8,128)(2,1)S(1)}, u32[]{:S(2)}, u32[]{:S(2)}) collective-permute-start(bf16[8,128,128]{2,1,0:T(8,128)(2,1)S(1)} %get-tuple-element.83), channel_id=1, source_target_pairs={{0,1},{1,0},{2,3},{3,2},{4,5},{5,4},{6,7},{7,6},{8,9},{9,8},{10,11... | collective-permute-start | bytes 786440 | tf_op jit(solution)/shard_map/ppermute | solution.py:283
  83.3 18.3 %collective-permute-start.25 = (bf16[8,128,128]{2,1,0:T(8,128)(2,1)S(1)}, bf16[8,128,128]{2,1,0:T(8,128)(2,1)S(1)}, u32[]{:S(2)}, u32[]{:S(2)}) collective-permute-start(bf16[8,128,128]{2,1,0:T(8,128)(2,1)S(1)} %get-tuple-element.84), channel_id=1, source_target_pairs={{0,2},{1,3},{2,0},{3,1},{4,6},{5,7},{6,4},{7,5},{8,10},{9,11},{10,... | collective-permute-start | bytes 786440 | tf_op jit(solution)/shard_map/ppermute | solution.py:283
  87.9 17.9 %collective-permute-start.26 = (bf16[8,128,128]{2,1,0:T(8,128)(2,1)S(1)}, bf16[8,128,128]{2,1,0:T(8,128)(2,1)S(1)}, u32[]{:S(2)}, u32[]{:S(2)}) collective-permute-start(bf16[8,128,128]{2,1,0:T(8,128)(2,1)S(1)} %get-tuple-element.85), channel_id=1, source_target_pairs={{0,3},{1,2},{2,1},{3,0},{4,7},{5,6},{6,5},{7,4},{8,11},{9,10},{10,... | collective-permute-start | bytes 786440 | tf_op jit(solution)/shard_map/ppermute | solution.py:283
  93.5 36.6 %collective-permute-start.33 = (bf16[8,128,128]{2,1,0:T(8,128)(2,1)S(1)}, bf16[8,128,128]{2,1,0:T(8,128)(2,1)S(1)}, u32[]{:S(2)}, u32[]{:S(2)}) collective-permute-start(bf16[8,128,128]{2,1,0:T(8,128)(2,1)S(1)} %get-tuple-element.88), channel_id=1, source_target_pairs={{0,1},{1,0},{2,3},{3,2},{4,5},{5,4},{6,7},{7,6},{8,9},{9,8},{10,11... | collective-permute-start | bytes 786440 | tf_op jit(solution)/shard_map/ppermute | solution.py:283
  94.5 35.6 %collective-permute-start.34 = (bf16[8,128,128]{2,1,0:T(8,128)(2,1)S(1)}, bf16[8,128,128]{2,1,0:T(8,128)(2,1)S(1)}, u32[]{:S(2)}, u32[]{:S(2)}) collective-permute-start(bf16[8,128,128]{2,1,0:T(8,128)(2,1)S(1)} %get-tuple-element.89), channel_id=1, source_target_pairs={{0,2},{1,3},{2,0},{3,1},{4,6},{5,7},{6,4},{7,5},{8,10},{9,11},{10,... | collective-permute-start | bytes 786440 | tf_op jit(solution)/shard_map/ppermute | solution.py:283
  99.2 31.0 %collective-permute-start.35 = (bf16[8,128,128]{2,1,0:T(8,128)(2,1)S(1)}, bf16[8,128,128]{2,1,0:T(8,128)(2,1)S(1)}, u32[]{:S(2)}, u32[]{:S(2)}) collective-permute-start(bf16[8,128,128]{2,1,0:T(8,128)(2,1)S(1)} %get-tuple-element.90), channel_id=1, source_target_pairs={{0,3},{1,2},{2,1},{3,0},{4,7},{5,6},{6,5},{7,4},{8,11},{9,10},{10,... | collective-permute-start | bytes 786440 | tf_op jit(solution)/shard_map/ppermute | solution.py:283
  101.6 22.1 %collective-permute-start.16 = (bf16[8,128,128]{2,1,0:T(8,128)(2,1)S(1)}, bf16[8,128,128]{2,1,0:T(8,128)(2,1)S(1)}, u32[]{:S(2)}, u32[]{:S(2)}) collective-permute-start(bf16[8,128,128]{2,1,0:T(8,128)(2,1)S(1)} %copy-done.8), channel_id=1, source_target_pairs={{0,2},{1,3},{2,0},{3,1},{4,6},{5,7},{6,4},{7,5},{8,10},{9,11},{10,... | collective-permute-start | bytes 786440 | tf_op jit(solution)/shard_map/ppermute | solution.py:283
  105.8 18.0 %collective-permute-start.17 = (bf16[8,128,128]{2,1,0:T(8,128)(2,1)S(1)}, bf16[8,128,128]{2,1,0:T(8,128)(2,1)S(1)}, u32[]{:S(2)}, u32[]{:S(2)}) collective-permute-start(bf16[8,128,128]{2,1,0:T(8,128)(2,1)S(1)} %copy-done.6), channel_id=1, source_target_pairs={{0,3},{1,2},{2,1},{3,0},{4,7},{5,6},{6,5},{7,4},{8,11},{9,10},{10,... | collective-permute-start | bytes 786440 | tf_op jit(solution)/shard_map/ppermute | solution.py:283
  143.9 18.8 %collective-permute-start.63 = (bf16[8,128,128]{2,1,0:T(8,128)(2,1)S(1)}, bf16[8,128,128]{2,1,0:T(8,128)(2,1)S(1)}, u32[]{:S(2)}, u32[]{:S(2)}) collective-permute-start(bf16[8,128,128]{2,1,0:T(8,128)(2,1)S(1)} %get-tuple-element.134), channel_id=1, source_target_pairs={{0,1},{1,0},{2,3},{3,2},{4,5},{5,4},{6,7},{7,6},{8,9},{9,8},{10,11... | collective-permute-start | bytes 786440 | tf_op jit(solution)/shard_map/ppermute | solution.py:283
  145.5 17.8 %collective-permute-start.64 = (bf16[8,128,128]{2,1,0:T(8,128)(2,1)S(1)}, bf16[8,128,128]{2,1,0:T(8,128)(2,1)S(1)}, u32[]{:S(2)}, u32[]{:S(2)}) collective-permute-start(bf16[8,128,128]{2,1,0:T(8,128)(2,1)S(1)} %get-tuple-element.135), channel_id=1, source_target_pairs={{0,2},{1,3},{2,0},{3,1},{4,6},{5,7},{6,4},{7,5},{8,10},{9,11},{10,... | collective-permute-start | bytes 786440 | tf_op jit(solution)/shard_map/ppermute | solution.py:283
  147.0 23.9 %collective-permute-start.65 = (bf16[8,128,128]{2,1,0:T(8,128)(2,1)S(1)}, bf16[8,128,128]{2,1,0:T(8,128)(2,1)S(1)}, u32[]{:S(2)}, u32[]{:S(2)}) collective-permute-start(bf16[8,128,128]{2,1,0:T(8,128)(2,1)S(1)} %get-tuple-element.136), channel_id=1, source_target_pairs={{0,3},{1,2},{2,1},{3,0},{4,7},{5,6},{6,5},{7,4},{8,11},{9,10},{10,... | collective-permute-start | bytes 786440 | tf_op jit(solution)/shard_map/ppermute | solution.py:283
  153.5 18.9 %collective-permute-start.54 = (bf16[8,128,128]{2,1,0:T(8,128)(2,1)S(1)}, bf16[8,128,128]{2,1,0:T(8,128)(2,1)S(1)}, u32[]{:S(2)}, u32[]{:S(2)}) collective-permute-start(bf16[8,128,128]{2,1,0:T(8,128)(2,1)S(1)} %get-tuple-element.125), channel_id=1, source_target_pairs={{0,1},{1,0},{2,3},{3,2},{4,5},{5,4},{6,7},{7,6},{8,9},{9,8},{10,11... | collective-permute-start | bytes 786440 | tf_op jit(solution)/shard_map/ppermute | solution.py:283
  155.1 17.9 %collective-permute-start.55 = (bf16[8,128,128]{2,1,0:T(8,128)(2,1)S(1)}, bf16[8,128,128]{2,1,0:T(8,128)(2,1)S(1)}, u32[]{:S(2)}, u32[]{:S(2)}) collective-permute-start(bf16[8,128,128]{2,1,0:T(8,128)(2,1)S(1)} %get-tuple-element.126), channel_id=1, source_target_pairs={{0,2},{1,3},{2,0},{3,1},{4,6},{5,7},{6,4},{7,5},{8,10},{9,11},{10,... | collective-permute-start | bytes 786440 | tf_op jit(solution)/shard_map/ppermute | solution.py:283
  162.8 11.7 %collective-permute-start.56 = (bf16[8,128,128]{2,1,0:T(8,128)(2,1)S(1)}, bf16[8,128,128]{2,1,0:T(8,128)(2,1)S(1)}, u32[]{:S(2)}, u32[]{:S(2)}) collective-permute-start(bf16[8,128,128]{2,1,0:T(8,128)(2,1)S(1)} %get-tuple-element.127), channel_id=1, source_target_pairs={{0,3},{1,2},{2,1},{3,0},{4,7},{5,6},{6,5},{7,4},{8,11},{9,10},{10,... | collective-permute-start | bytes 786440 | tf_op jit(solution)/shard_map/ppermute | solution.py:283
  163.3 12.7 %collective-permute-start.45 = (bf16[8,128,128]{2,1,0:T(8,128)(2,1)S(1)}, bf16[8,128,128]{2,1,0:T(8,128)(2,1)S(1)}, u32[]{:S(2)}, u32[]{:S(2)}) collective-permute-start(bf16[8,128,128]{2,1,0:T(8,128)(2,1)S(1)} %get-tuple-element.116), channel_id=1, source_target_pairs={{0,1},{1,0},{2,3},{3,2},{4,5},{5,4},{6,7},{7,6},{8,9},{9,8},{10,11... | collective-permute-start | bytes 786440 | tf_op jit(solution)/shard_map/ppermute | solution.py:283
  170.9 15.0 %collective-permute-start.46 = (bf16[8,128,128]{2,1,0:T(8,128)(2,1)S(1)}, bf16[8,128,128]{2,1,0:T(8,128)(2,1)S(1)}, u32[]{:S(2)}, u32[]{:S(2)}) collective-permute-start(bf16[8,128,128]{2,1,0:T(8,128)(2,1)S(1)} %get-tuple-element.117), channel_id=1, source_target_pairs={{0,2},{1,3},{2,0},{3,1},{4,6},{5,7},{6,4},{7,5},{8,10},{9,11},{10,... | collective-permute-start | bytes 786440 | tf_op jit(solution)/shard_map/ppermute | solution.py:283
  172.5 20.2 %collective-permute-start.47 = (bf16[8,128,128]{2,1,0:T(8,128)(2,1)S(1)}, bf16[8,128,128]{2,1,0:T(8,128)(2,1)S(1)}, u32[]{:S(2)}, u32[]{:S(2)}) collective-permute-start(bf16[8,128,128]{2,1,0:T(8,128)(2,1)S(1)} %get-tuple-element.118), channel_id=1, source_target_pairs={{0,3},{1,2},{2,1},{3,0},{4,7},{5,6},{6,5},{7,4},{8,11},{9,10},{10,... | collective-permute-start | bytes 786440 | tf_op jit(solution)/shard_map/ppermute | solution.py:283
  173.0 20.8 %collective-permute-start.36 = (bf16[8,128,128]{2,1,0:T(8,128)(2,1)S(1)}, bf16[8,128,128]{2,1,0:T(8,128)(2,1)S(1)}, u32[]{:S(2)}, u32[]{:S(2)}) collective-permute-start(bf16[8,128,128]{2,1,0:T(8,128)(2,1)S(1)} %get-tuple-element.107), channel_id=1, source_target_pairs={{0,1},{1,0},{2,3},{3,2},{4,5},{5,4},{6,7},{7,6},{8,9},{9,8},{10,11... | collective-permute-start | bytes 786440 | tf_op jit(solution)/shard_map/ppermute | solution.py:283
  174.4 19.9 %collective-permute-start.37 = (bf16[8,128,128]{2,1,0:T(8,128)(2,1)S(1)}, bf16[8,128,128]{2,1,0:T(8,128)(2,1)S(1)}, u32[]{:S(2)}, u32[]{:S(2)}) collective-permute-start(bf16[8,128,128]{2,1,0:T(8,128)(2,1)S(1)} %get-tuple-element.108), channel_id=1, source_target_pairs={{0,2},{1,3},{2,0},{3,1},{4,6},{5,7},{6,4},{7,5},{8,10},{9,11},{10,... | collective-permute-start | bytes 786440 | tf_op jit(solution)/shard_map/ppermute | solution.py:283
  176.0 22.0 %collective-permute-start.38 = (bf16[8,128,128]{2,1,0:T(8,128)(2,1)S(1)}, bf16[8,128,128]{2,1,0:T(8,128)(2,1)S(1)}, u32[]{:S(2)}, u32[]{:S(2)}) collective-permute-start(bf16[8,128,128]{2,1,0:T(8,128)(2,1)S(1)} %get-tuple-element.109), channel_id=1, source_target_pairs={{0,3},{1,2},{2,1},{3,0},{4,7},{5,6},{6,5},{7,4},{8,11},{9,10},{10,... | collective-permute-start | bytes 786440 | tf_op jit(solution)/shard_map/ppermute | solution.py:283
  185.9 14.7 %collective-permute-start.67 = (bf16[4,128,128]{2,1,0:T(8,128)(2,1)S(1)}, bf16[4,128,128]{2,1,0:T(8,128)(2,1)S(1)}, u32[]{:S(2)}, u32[]{:S(2)}) collective-permute-start(bf16[4,128,128]{2,1,0:T(8,128)(2,1)S(1)} %get-tuple-element.140), channel_id=1, source_target_pairs={{0,4},{1,5},{2,6},{3,7},{12,8},{13,9},{14,10},{15,11},{16,20},{17,... | collective-permute-start | bytes 393224 | tf_op jit(solution)/shard_map/ppermute | solution.py:279
  192.6 73.6 %collective-permute-start.66 = (bf16[4,128,128]{2,1,0:T(8,128)(2,1)S(1)}, bf16[4,128,128]{2,1,0:T(8,128)(2,1)S(1)}, u32[]{:S(2)}, u32[]{:S(2)}) collective-permute-start(bf16[4,128,128]{2,1,0:T(8,128)(2,1)S(1)} %get-tuple-element.137), channel_id=1, source_target_pairs={{0,16},{1,17},{2,18},{3,19},{4,20},{5,21},{6,22},{7,23},{8,24},{9,... | collective-permute-start | bytes 393224 | tf_op jit(solution)/shard_map/ppermute | solution.py:279
  193.7 68.1 %collective-permute-start.57 = (bf16[4,128,128]{2,1,0:T(8,128)(2,1)S(1)}, bf16[4,128,128]{2,1,0:T(8,128)(2,1)S(1)}, u32[]{:S(2)}, u32[]{:S(2)}) collective-permute-start(bf16[4,128,128]{2,1,0:T(8,128)(2,1)S(1)} %get-tuple-element.128), channel_id=1, source_target_pairs={{0,16},{1,17},{2,18},{3,19},{4,20},{5,21},{6,22},{7,23},{8,24},{9,... | collective-permute-start | bytes 393224 | tf_op jit(solution)/shard_map/ppermute | solution.py:279
  200.6 44.7 %collective-permute-start.39 = (bf16[4,128,128]{2,1,0:T(8,128)(2,1)S(1)}, bf16[4,128,128]{2,1,0:T(8,128)(2,1)S(1)}, u32[]{:S(2)}, u32[]{:S(2)}) collective-permute-start(bf16[4,128,128]{2,1,0:T(8,128)(2,1)S(1)} %get-tuple-element.110), channel_id=1, source_target_pairs={{0,16},{1,17},{2,18},{3,19},{4,20},{5,21},{6,22},{7,23},{8,24},{9,... | collective-permute-start | bytes 393224 | tf_op jit(solution)/shard_map/ppermute | solution.py:279
  222.1 18.9 %collective-permute-start.50 = (bf16[4,128,128]{2,1,0:T(8,128)(2,1)S(1)}, bf16[4,128,128]{2,1,0:T(8,128)(2,1)S(1)}, u32[]{:S(2)}, u32[]{:S(2)}) collective-permute-start(bf16[4,128,128]{2,1,0:T(8,128)(2,1)S(1)} %add_convert_fusion.12), channel_id=1, source_target_pairs={{0,4},{1,5},{2,6},{3,7},{4,8},{5,9},{6,10},{7,11},{16,20},{17,21},... | collective-permute-start | bytes 393224 | tf_op jit(solution)/shard_map/ppermute | solution.py:279
  227.4 12.2 %collective-permute-start.41 = (bf16[4,128,128]{2,1,0:T(8,128)(2,1)S(1)}, bf16[4,128,128]{2,1,0:T(8,128)(2,1)S(1)}, u32[]{:S(2)}, u32[]{:S(2)}) collective-permute-start(bf16[4,128,128]{2,1,0:T(8,128)(2,1)S(1)} %add_convert_fusion.16), channel_id=1, source_target_pairs={{0,4},{1,5},{2,6},{3,7},{4,8},{5,9},{6,10},{7,11},{16,20},{17,21},... | collective-permute-start | bytes 393224 | tf_op jit(solution)/shard_map/ppermute | solution.py:279
  253.7 12.6 %collective-permute-start.71 = (bf16[4,128,128]{2,1,0:T(8,128)(2,1)S(1)}, bf16[4,128,128]{2,1,0:T(8,128)(2,1)S(1)}, u32[]{:S(2)}, u32[]{:S(2)}) collective-permute-start(bf16[4,128,128]{2,1,0:T(8,128)(2,1)S(1)} %add_convert_fusion.2), channel_id=1, source_target_pairs={{4,16},{5,17},{6,18},{7,19},{8,20},{9,21},{10,22},{11,23},{12,24},... | collective-permute-start | bytes 393224 | tf_op jit(solution)/shard_map/ppermute | solution.py:279
  255.1 10.6 %collective-permute-start.62 = (bf16[4,128,128]{2,1,0:T(8,128)(2,1)S(1)}, bf16[4,128,128]{2,1,0:T(8,128)(2,1)S(1)}, u32[]{:S(2)}, u32[]{:S(2)}) collective-permute-start(bf16[4,128,128]{2,1,0:T(8,128)(2,1)S(1)} %add_convert_fusion.6), channel_id=1, source_target_pairs={{4,16},{5,17},{6,18},{7,19},{8,20},{9,21},{10,22},{11,23},{12,24},... | collective-permute-start | bytes 393224 | tf_op jit(solution)/shard_map/ppermute | solution.py:279
  (56 other events, 594.4 us)

commit v4 on v1

--- a/solution.py
+++ b/solution.py
@@ -40,11 +40,36 @@
 
 
 def attention_kernel(list_len, slot_ref, q_ref, ng_ref, *refs):
-    kv_refs = refs[:list_len]
-    normed_ref, qg_ref, back_ref, probs_scr, parts_scr, sems = refs[list_len:]
+    arrived, (normed_ref, qg_ref) = refs[:2], refs[2:4]
+    back, (probs_scr, kv_scr, parts_scr, in_sems, out_sems) = refs[4:6], refs[6:]
     step = pl.program_id(0)
-    keys = jnp.concatenate([ref[0, :, :KV] for ref in kv_refs], axis=0)
-    values = jnp.concatenate([ref[0, :, KV:] for ref in kv_refs], axis=0)
+    entries = kv_scr.shape[0]
+    per_part = arrived[0].shape[0]
+
+    def fetch(e, part, slot):
+        return pltpu.make_async_copy(arrived[part].at[slot], kv_scr.at[e], in_sems.at[e])
+
+    def give(e, part, slot):
+        return pltpu.make_async_copy(parts_scr.at[e], back[part].at[slot], out_sems.at[e])
+
+    def start(copy, e):
+        slot = slot_ref[e]
+        for part in range(2):
+
+            @pl.when(slot // per_part == part)
+            def _():
+                copy(e, part, slot % per_part).start()
+
+    @pl.when(step == 0)
+    def _():
+        for e in range(entries):
+            start(fetch, e)
+
+    first = step * list_len
+    for l in range(list_len):
+        fetch(first + l, 0, 0).wait()
+    keys = jnp.concatenate([kv_scr[first + l, :, :KV] for l in range(list_len)], axis=0)
+    values = jnp.concatenate([kv_scr[first + l, :, KV:] for l in range(list_len)], axis=0)
     queries = q_ref[...] * jnp.asarray(TEMPER, BF16)
     attended = []
     for g in range(KV_HEADS):
@@ -71,38 +96,29 @@
         row_dot = jnp.sum(probs * prob_grad, axis=-1, keepdims=True)
         score_grad = (probs * (prob_grad - row_dot)).astype(BF16)
         query_grad = jnp.dot(score_grad, keys[:, cols], preferred_element_type=F32) * TEMPER
-        first = g * GROUP * HEAD_DIM
-        qg_ref[:, first : first + GROUP * HEAD_DIM] = spread_heads(query_grad.astype(BF16))
+        left = g * GROUP * HEAD_DIM
+        qg_ref[:, left : left + GROUP * HEAD_DIM] = spread_heads(query_grad.astype(BF16))
         key_part = dot_tn(score_grad, stack_heads(queries, g)).astype(BF16)
         value_part = dot_tn(probs.astype(BF16), out_grad).astype(BF16)
         for l in range(list_len):
             rows = slice(l * BLK, (l + 1) * BLK)
-            parts_scr[step, l, :, g * HEAD_DIM : (g + 1) * HEAD_DIM] = key_part[rows]
-            parts_scr[step, l, :, KV + g * HEAD_DIM : KV + (g + 1) * HEAD_DIM] = value_part[rows]
-
-    def copy(s, l):
-        return pltpu.make_async_copy(
-            parts_scr.at[s, l], back_ref.at[slot_ref[s * list_len + l]], sems.at[s, l]
-        )
-
+            parts_scr[first + l, :, g * HEAD_DIM : (g + 1) * HEAD_DIM] = key_part[rows]
+            parts_scr[first + l, :, KV + g * HEAD_DIM : KV + (g + 1) * HEAD_DIM] = value_part[rows]
     for l in range(list_len):
-        copy(step, l).start()
+        start(give, first + l)
 
     @pl.when(step == pl.num_programs(0) - 1)
     def _():
-        for s in range(sems.shape[0]):
-            for l in range(list_len):
-                copy(s, l).wait()
+        for e in range(entries):
+            give(e, 0, 0).wait()
 
 
 def attention(slots, queries, normed_grad, arrived, list_len):
     rows, width = queries.shape
     blocks = rows // BLK
+    entries = blocks * list_len
     row_spec = pl.BlockSpec((BLK, width), lambda r, s: (r, 0))
-
-    def entry_spec(l):
-        return pl.BlockSpec((1, BLK, 2 * KV), lambda r, s: (s[r * list_len + l], 0, 0))
-
+    anywhere = pl.BlockSpec(memory_space=pl.ANY)
     keys = list_len * BLK
     pairs = HEADS * rows * keys
     return pl.pallas_call(
@@ -110,25 +126,24 @@
         grid_spec=pltpu.PrefetchScalarGridSpec(
             num_scalar_prefetch=1,
             grid=(blocks,),
-            in_specs=[row_spec, row_spec] + [entry_spec(l) for l in range(list_len)],
-            out_specs=[row_spec, row_spec, pl.BlockSpec(memory_space=pl.ANY)],
+            in_specs=[row_spec, row_spec, anywhere, anywhere],
+            out_specs=[row_spec, row_spec, anywhere, anywhere],
             scratch_shapes=[
                 pltpu.VMEM((KV_HEADS, GROUP * BLK, keys), F32),
-                pltpu.VMEM((blocks, list_len, BLK, 2 * KV), BF16),
-                pltpu.SemaphoreType.DMA((blocks, list_len)),
+                pltpu.VMEM((entries, BLK, 2 * KV), BF16),
+                pltpu.VMEM((entries, BLK, 2 * KV), BF16),
+                pltpu.SemaphoreType.DMA((entries,)),
+                pltpu.SemaphoreType.DMA((entries,)),
             ],
         ),
-        out_shape=[
-            jax.ShapeDtypeStruct((rows, width), BF16),
-            jax.ShapeDtypeStruct((rows, width), BF16),
-            jax.ShapeDtypeStruct(arrived.shape, BF16),
-        ],
+        out_shape=[jax.ShapeDtypeStruct((rows, width), BF16)] * 2
+        + [jax.ShapeDtypeStruct(arrived[0].shape, BF16)] * 2,
         compiler_params=pltpu.CompilerParams(vmem_limit_bytes=56 * 1024 * 1024),
         cost_estimate=pl.CostEstimate(
             flops=12 * pairs * HEAD_DIM, bytes_accessed=16 * rows * width, transcendentals=pairs
         ),
         name="attention",
-    )(slots, queries, normed_grad, *([arrived] * list_len))
+    )(slots, queries, normed_grad, *arrived)
 
 
 def owner_kernel(chunk, wanted_ref, parts_ref, out_ref, total):
@@ -168,51 +183,61 @@
     )(wanted, returned)
 
 
-def slot_index(entry_tiles, tile_count):
-    one_hot = (entry_tiles[:, None] == jnp.arange(tile_count, dtype=jnp.int32)[None, :]).astype(
-        jnp.int32
-    )
-    ranks = jnp.cumsum(one_hot, axis=0) - 1
-    return jnp.sum(one_hot * ranks, axis=1)
-
-
-def from_partner(value):
-    return lax.ppermute(value, "vintage", [(0, 1), (1, 0)])
-
-
 def shards(patches, out_grad, w_query, w_key, w_value, w_out, key_tiles, key_blocks):
     tokens = patches[0]
     rows = tokens.shape[0]
     tile_count = lax.axis_size("tile")
+    half = tile_count // 2
     my_tile = lax.axis_index("tile")
+    my_half, my_place = my_tile // half, my_tile % half
+    groups = [list(range(half)), list(range(half, tile_count))]
     block_count = rows // BLK
     list_len = key_tiles.shape[2]
     entry_count = block_count * list_len
+
+    def cross(value, shift):
+        pairs = [
+            (v * tile_count + t, (1 - v) * tile_count + (t + shift) % tile_count)
+            for v in range(2)
+            for t in range(tile_count)
+        ]
+        return lax.ppermute(value, ("vintage", "tile"), pairs)
+
+    def exchange(value):
+        return lax.all_to_all(
+            value, "tile", split_axis=0, concat_axis=0, tiled=True, axis_index_groups=groups
+        )
+
+    def half_rows(table):
+        table = table[0].reshape(2, half, entry_count)
+        return lax.dynamic_index_in_dim(table, my_half, 0, keepdims=False)
+
+    tiles, picks = half_rows(key_tiles), half_rows(key_blocks)
+    earlier = jnp.arange(entry_count)[:, None] > jnp.arange(entry_count)[None, :]
+    same = (tiles[:, :, None] == tiles[:, None, :]) & earlier[None]
+    ranks = jnp.sum(same.astype(jnp.int32), axis=2)
+    is_far = (tiles // half != my_half).astype(jnp.int32)
+    slots = (is_far * half + tiles % half) * CAP + ranks
+    my_slots = lax.dynamic_index_in_dim(slots, my_place, 0, keepdims=False)
+    part_ids = jnp.arange(2, dtype=jnp.int32)[:, None, None] * half + my_place
+    ids = part_ids * CAP + jnp.arange(CAP, dtype=jnp.int32)[None, None, :]
+    hits = slots[None, :, :, None] == ids[:, :, None, :]
+    wanted = jnp.sum(jnp.where(hits, picks[None, :, :, None] + 1, 0), axis=2) - 1
+    wanted = wanted.reshape(2, half * CAP)
+
     keys = jnp.dot(tokens, w_key, preferred_element_type=F32).astype(BF16)
     values = jnp.dot(tokens, w_value, preferred_element_type=F32).astype(BF16)
-    partner = from_partner(jnp.concatenate([keys, values], axis=-1))
-    partner_blocks = partner.reshape(block_count, BLK, 2 * KV)
-    my_tiles = lax.dynamic_slice_in_dim(
-        key_tiles[0], my_tile * block_count, block_count, 0
-    ).reshape(-1)
-    flat_slot = my_tiles * CAP + slot_index(my_tiles, tile_count)
-    all_tiles = key_tiles[0].reshape(tile_count, entry_count)
-    all_blocks = key_blocks[0].reshape(tile_count, entry_count)
-    asking = (all_tiles == my_tile).astype(jnp.int32)
-    ranks = jnp.cumsum(asking, axis=1) - 1
-    slot_range = jnp.arange(CAP, dtype=jnp.int32)
-    hits = (asking[:, :, None] == 1) & (ranks[:, :, None] == slot_range[None, None, :])
-    wanted = (jnp.sum(jnp.where(hits, all_blocks[:, :, None] + 1, 0), axis=1) - 1).reshape(-1)
-    send = partner_blocks[jnp.clip(wanted, 0, block_count - 1)]
-    arrived = lax.all_to_all(send, "tile", split_axis=0, concat_axis=0, tiled=True)
+    mine = jnp.concatenate([keys, values], axis=-1).reshape(block_count, BLK, 2 * KV)
+    tiles_here = [cross(mine, 0), cross(mine, half)]
+    arrived = [exchange(tiles_here[p][jnp.maximum(wanted[p], 0)]) for p in range(2)]
     queries = jnp.dot(tokens, w_query, preferred_element_type=F32).astype(BF16)
     normed_grad = dot_nt(out_grad[0], w_out)
-    normed_low, query_grad, back = attention(flat_slot, queries, normed_grad, arrived, list_len)
-    returned = lax.all_to_all(back, "tile", split_axis=0, concat_axis=0, tiled=True)
+    normed_low, query_grad, *back = attention(my_slots, queries, normed_grad, arrived, list_len)
+    far = cross(owner_sum(wanted[1], exchange(back[1]), block_count), half)
+    near = cross(owner_sum(wanted[0], exchange(back[0]), block_count), 0)
     layer_out = jnp.dot(normed_low, w_out, preferred_element_type=F32).astype(BF16)
     query_term = dot_nt(query_grad, w_query)
-    kv_grad = owner_sum(wanted, returned, block_count).reshape(rows, 2 * KV)
-    kv_grad = from_partner(kv_grad)
+    kv_grad = (near.astype(F32) + far.astype(F32)).astype(BF16).reshape(rows, 2 * KV)
     kv_term = dot_nt(kv_grad[:, :KV], w_key) + dot_nt(kv_grad[:, KV:], w_value)
     input_grad = (query_term + kv_term).astype(BF16)
     return (layer_out[None], input_grad[None])

time: 246 us -> 194 us (0.79)
  the two profiles are of different devices: /device:TPU:15 before, /device:TPU:0 now
where the time goes in v4:
time: 194 us; the launch traced here: 193 us
  waiting for transfers between devices  85.9 us (44%)
  blocking collectives  32.7 us (17%)
  Pallas kernels  30.2 us (16%)
  starting transfers between devices  22 us (11%)
  matrix products  11.4 us (6%)
  local copies, waits for them, and re-layouts  8.48 us (4%)
    all_to_all x3, waiting for transfers between devices, exchange(): lax.all_to_all(value, 'tile', split_axis=0, concat_axis=0, tiled=True, ax...  53.2 us
    all_to_all x1, blocking collectives, exchange(): lax.all_to_all(value, 'tile', split_axis=0, concat_axis=0, tiled=True, ax...  32.7 us
    ppermute x4, waiting for transfers between devices, cross(): return lax.ppermute(value, ('vintage', 'tile'), pairs)  32.6 us
    pallas_call x1, Pallas kernels, attention(): pl.pallas_call(functools.partial(attention_kernel, list_len), grid_spec=p...  27.3 us
    all_to_all x3, starting transfers between devices, exchange(): lax.all_to_all(value, 'tile', split_axis=0, concat_axis=0, tiled=True, ax...  19.3 us
    dot_general x4, matrix products, dot_nt(): lax.dot_general(a, b, (((1,), (1,)), ((), ())), preferred_element_type=F32)  4.53 us
    gather x2, local copies, waits for them, and re-layouts, shards(): tiles_here[p][jnp.maximum(wanted[p], 0)]  4.03 us
  transfers between devices with their start and end apart: 7, of which 6 were waited for; matrix products, arithmetic and copies ran while one was open for 6% of the time, Pallas kernels for 1%

profile of v4, /device:TPU:0, one launch (start us, length us, event | category | flops | bytes accessed | tf_op | source)
XLA Modules:
  0.0 193.4 jit_solution(1989099112337453185)
XLA Ops:
  0.6 0.0 copy-start
  0.7 1.8 convolution_convert_fusion.3
  2.5 0.4 convolution_convert_fusion.2
  3.0 0.2 copy.24
  3.2 0.5 collective-permute-start
  3.7 0.1 iota_add_fusion
  3.8 0.1 copy.16
  3.9 0.1 reshape_squeeze.6
  4.0 0.1 copy.18
  4.1 0.1 reshape_squeeze.7
  4.2 0.3 convert_reduce_fusion
  4.5 0.2 select_reduce_fusion
  4.7 0.1 copy.19
  4.8 0.1 reshape.151
  4.9 0.4 collective-permute-done
  5.2 2.0 %gather_fusion = bf16[16,128,512]{2,1,0:T(8,128)(2,1)} fusion(bf16[4,128,512]{2,1,0:T(8,128)(2,1)S(1)} %collective-permute-done, s32[1024]{0:T(1024)S(1)} %pad_clamp_fusion.1), kind=kCustom, calls=%fused_computation | custom fusion | bytes 4194368 | tf_op jit(solution)/shard_map/gather | solution.py:232
  7.3 6.1 %all-to-all-start = ((bf16[16,128,512]{2,1,0:T(8,128)(2,1)}), bf16[16,128,512]{2,1,0:T(8,128)(2,1)}, u32[]{:S(2)}, u32[]{:S(2)}) async-start(bf16[16,128,512]{2,1,0:T(8,128)(2,1)} %gather_fusion), calls=%async_computation | async-start | bytes 4194304 | tf_op jit(solution)/shard_map/all_to_all | solution.py:207
  13.4 2.1 %collective-permute-start.1 = (bf16[4,128,512]{2,1,0:T(8,128)(2,1)S(1)}, bf16[4,128,512]{2,1,0:T(8,128)(2,1)S(1)}, u32[]{:S(2)}, u32[]{:S(2)}) collective-permute-start(bf16[4,128,512]{2,1,0:T(8,128)(2,1)S(1)} %bitcast.35), channel_id=1, source_target_pairs={{0,24},{1,25},{2,26},{3,27},{4,28},{5,29},{6,30},{7,31},{8,16},{9,... | collective-permute-start | bytes 1572872 | tf_op jit(solution)/shard_map/ppermute | solution.py:204
  15.5 0.1 copy.21
  15.5 0.1 reshape.159
  15.6 32.1 %collective-permute-done.1 = bf16[4,128,512]{2,1,0:T(8,128)(2,1)S(1)} collective-permute-done((bf16[4,128,512]{2,1,0:T(8,128)(2,1)S(1)}, bf16[4,128,512]{2,1,0:T(8,128)(2,1)S(1)}, u32[]{:S(2)}, u32[]{:S(2)}) %collective-permute-start.1) | collective-permute-done | bytes 524320 | tf_op jit(solution)/shard_map/ppermute | solution.py:204
  47.7 2.0 %gather_fusion.1 = bf16[16,128,512]{2,1,0:T(8,128)(2,1)} fusion(bf16[4,128,512]{2,1,0:T(8,128)(2,1)S(1)} %collective-permute-done.1, s32[1024]{0:T(1024)S(1)} %pad_clamp_fusion), kind=kCustom, calls=%fused_computation.1 | custom fusion | bytes 4194368 | tf_op jit(solution)/shard_map/gather | solution.py:232
  49.7 0.2 all-to-all-done.refs_0_
  49.9 9.6 %all-to-all-start.1 = ((bf16[16,128,512]{2,1,0:T(8,128)(2,1)}), bf16[16,128,512]{2,1,0:T(8,128)(2,1)}, u32[]{:S(2)}, u32[]{:S(2)}) async-start(bf16[16,128,512]{2,1,0:T(8,128)(2,1)} %gather_fusion.1), calls=%async_computation.1 | async-start | bytes 4194304 | tf_op jit(solution)/shard_map/all_to_all | solution.py:207
  59.5 0.5 fusion.17.slot_ref
  60.1 3.0 %convolution_convert_fusion.1.q_ref = bf16[512,768]{1,0:T(8,128)(2,1)} fusion(bf16[768,768]{1,0:T(8,128)(2,1)} %param.10, bf16[1,512,768]{2,1,0:T(8,128)(2,1)S(1)} %copy-done.2), kind=kOutput, calls=%fused_computation.4 | convolution fusion | flops 604372992 | bytes 2752512 | tf_op jit(solution)/shard_map/dot_general | solution.py:233
  63.1 2.0 %fusion.2.ng_ref = f32[512,768]{1,0:T(8,128)} fusion(bf16[768,768]{1,0:T(8,128)(2,1)S(1)} %copy-done, bf16[1,512,768]{2,1,0:T(8,128)(2,1)S(1)} %copy-done.10), kind=kOutput, calls=%fused_computation.10 | convolution fusion | flops 603979776 | bytes 3538944 | tf_op jit(solution)/shard_map/dot_general | solution.py:24
  65.1 21.4 %all-to-all-done.1.refs_1_ = bf16[16,128,512]{2,1,0:T(8,128)(2,1)} async-done(((bf16[16,128,512]{2,1,0:T(8,128)(2,1)}), bf16[16,128,512]{2,1,0:T(8,128)(2,1)}, u32[]{:S(2)}, u32[]{:S(2)}) %all-to-all-start.1) | async-done | bytes 2097184 | tf_op jit(solution)/shard_map/all_to_all | solution.py:207
  86.5 27.3 %attention.1 = (bf16[512,768]{1,0:T(8,128)(2,1)}, bf16[512,768]{1,0:T(8,128)(2,1)}, bf16[16,128,512]{2,1,0:T(8,128)(2,1)}, bf16[16,128,512]{2,1,0:T(8,128)(2,1)}) custom-call(s32[16]{0:T(128)} %fusion.17.slot_ref, bf16[512,768]{1,0:T(8,128)(2,1)} %convolution_convert_fusion.1.q_ref, f32[512,768]{1,0:T(8,128)} %fusion.2.ng_ref, ...), custom_call_target="tpu_custom_call" | custom-call | flops 2415919104 | bytes 6291456 | tf_op jit(solution)/shard_map/attention/pallas_call | solution.py:124
  113.9 32.7 %all_to_all.20.parts_ref = bf16[16,128,512]{2,1,0:T(8,128)(2,1)} all-to-all(bf16[16,128,512]{2,1,0:T(8,128)(2,1)} %get-tuple-element.9), channel_id=1, replica_groups={{0,1,2,3,4,5,6,7},{8,9,10,11,12,13,14,15},{16,17,18,19,20,21,22,23},{24..., dimensions={0} | all-to-all | bytes 4194304 | tf_op jit(solution)/shard_map/all_to_all | solution.py:207
  146.6 3.6 %all-to-all-start.2 = ((bf16[16,128,512]{2,1,0:T(8,128)(2,1)}), bf16[16,128,512]{2,1,0:T(8,128)(2,1)S(1)}, u32[]{:S(2)}, u32[]{:S(2)}) async-start(bf16[16,128,512]{2,1,0:T(8,128)(2,1)} %get-tuple-element.8), calls=%async_computation.2 | async-start | bytes 4194304 | tf_op jit(solution)/shard_map/all_to_all | solution.py:207
  150.2 0.1 copy.22
  150.3 0.1 squeeze.27.wanted_ref
  150.4 0.1 copy.23
  150.5 0.1 squeeze.28.wanted_ref
  150.6 1.6 copy-done.1
  152.2 1.8 owner_sum.3
  154.0 31.6 %all-to-all-done.2.parts_ref = bf16[16,128,512]{2,1,0:T(8,128)(2,1)S(1)} async-done(((bf16[16,128,512]{2,1,0:T(8,128)(2,1)}), bf16[16,128,512]{2,1,0:T(8,128)(2,1)S(1)}, u32[]{:S(2)}, u32[]{:S(2)}) %all-to-all-start.2) | async-done | bytes 2097184 | tf_op jit(solution)/shard_map/all_to_all | solution.py:207
  185.6 1.0 owner_sum.2
  186.6 0.1 collective-permute-start.2
  186.7 1.7 fusion
  188.4 0.2 collective-permute-done.2
  188.6 1.2 add_convert_fusion.1
  189.8 0.4 fusion.7
  190.3 0.4 fusion.9
  190.7 0.8 copy-done.6
  191.5 0.2 copy-done.7
  191.7 1.7 fusion.1
  (31 shorter events, 0.2 us)
Async XLA Ops:
  0.6 62.4 %copy-start = (bf16[768,768]{1,0:T(8,128)(2,1)S(1)}, bf16[768,768]{1,0:T(8,128)(2,1)}, u32[]{:S(2)}) copy-start(bf16[768,768]{1,0:T(8,128)(2,1)} %param.13) | copy-start | bytes 3538948
  0.6 1.8 copy-start.2
  0.7 1.8 copy-start.3
  2.5 1.3 copy-start.8
  2.5 1.5 copy-start.9
  3.2 2.1 %collective-permute-start = (bf16[4,128,512]{2,1,0:T(8,128)(2,1)S(1)}, bf16[4,128,512]{2,1,0:T(8,128)(2,1)S(1)}, u32[]{:S(2)}, u32[]{:S(2)}) collective-permute-start(bf16[4,128,512]{2,1,0:T(8,128)(2,1)S(1)} %bitcast.34), channel_id=1, source_target_pairs={{0,16},{1,17},{2,18},{3,19},{4,20},{5,21},{6,22},{7,23},{8,24},{9,... | collective-permute-start | bytes 1572872 | tf_op jit(solution)/shard_map/ppermute | solution.py:204
  7.3 42.6 %all-to-all-start = ((bf16[16,128,512]{2,1,0:T(8,128)(2,1)}), bf16[16,128,512]{2,1,0:T(8,128)(2,1)}, u32[]{:S(2)}, u32[]{:S(2)}) async-start(bf16[16,128,512]{2,1,0:T(8,128)(2,1)} %gather_fusion), calls=%async_computation | async-start | bytes 4194304 | tf_op jit(solution)/shard_map/all_to_all | solution.py:207
  13.4 34.3 %collective-permute-start.1 = (bf16[4,128,512]{2,1,0:T(8,128)(2,1)S(1)}, bf16[4,128,512]{2,1,0:T(8,128)(2,1)S(1)}, u32[]{:S(2)}, u32[]{:S(2)}) collective-permute-start(bf16[4,128,512]{2,1,0:T(8,128)(2,1)S(1)} %bitcast.35), channel_id=1, source_target_pairs={{0,24},{1,25},{2,26},{3,27},{4,28},{5,29},{6,30},{7,31},{8,16},{9,... | collective-permute-start | bytes 1572872 | tf_op jit(solution)/shard_map/ppermute | solution.py:204
  49.9 36.6 %all-to-all-start.1 = ((bf16[16,128,512]{2,1,0:T(8,128)(2,1)}), bf16[16,128,512]{2,1,0:T(8,128)(2,1)}, u32[]{:S(2)}, u32[]{:S(2)}) async-start(bf16[16,128,512]{2,1,0:T(8,128)(2,1)} %gather_fusion.1), calls=%async_computation.1 | async-start | bytes 4194304 | tf_op jit(solution)/shard_map/all_to_all | solution.py:207
  60.1 3.0 %copy-start.10 = (bf16[1,512,768]{2,1,0:T(8,128)(2,1)S(1)}, bf16[1,512,768]{2,1,0:T(8,128)(2,1)}, u32[]{:S(2)}) copy-start(bf16[1,512,768]{2,1,0:T(8,128)(2,1)} %param.9) | copy-start | bytes 2359300
  146.6 38.9 %all-to-all-start.2 = ((bf16[16,128,512]{2,1,0:T(8,128)(2,1)}), bf16[16,128,512]{2,1,0:T(8,128)(2,1)S(1)}, u32[]{:S(2)}, u32[]{:S(2)}) async-start(bf16[16,128,512]{2,1,0:T(8,128)(2,1)} %get-tuple-element.8), calls=%async_computation.2 | async-start | bytes 4194304 | tf_op jit(solution)/shard_map/all_to_all | solution.py:207
  150.6 1.6 copy-start.1
  154.0 34.4 %collective-permute-start.3 = (bf16[4,128,512]{2,1,0:T(8,128)(2,1)}, bf16[4,128,512]{2,1,0:T(8,128)(2,1)}, u32[]{:S(2)}, u32[]{:S(2)}) collective-permute-start(bf16[4,128,512]{2,1,0:T(8,128)(2,1)} %owner_sum.3), channel_id=1, source_target_pairs={{0,24},{1,25},{2,26},{3,27},{4,28},{5,29},{6,30},{7,31},{8,16},{9,... | collective-permute-start | bytes 1572872 | tf_op jit(solution)/shard_map/ppermute | solution.py:204
  185.6 1.1 copy-start.11
  186.6 2.0 %collective-permute-start.2 = (bf16[4,128,512]{2,1,0:T(8,128)(2,1)S(1)}, bf16[4,128,512]{2,1,0:T(8,128)(2,1)S(1)}, u32[]{:S(2)}, u32[]{:S(2)}) collective-permute-start(bf16[4,128,512]{2,1,0:T(8,128)(2,1)S(1)} %owner_sum.2), channel_id=1, source_target_pairs={{0,16},{1,17},{2,18},{3,19},{4,20},{5,21},{6,22},{7,23},{8,24},{9,... | collective-permute-start | bytes 1572872 | tf_op jit(solution)/shard_map/ppermute | solution.py:204
  188.4 1.4 copy-start.4
  188.4 1.8 copy-start.5
  190.2 1.3 copy-start.6
  190.2 1.5 copy-start.7

commit v5 on v4

--- a/solution.py
+++ b/solution.py
@@ -14,6 +14,7 @@
 CAP = 2
 GROUP = HEADS // KV_HEADS
 KV = KV_HEADS * HEAD_DIM
+PAIR = 2 * HEAD_DIM
 TEMPER = HEAD_DIM ** (-0.5)
 EPSILON = 1e-06
 F32 = jnp.float32
@@ -28,29 +29,38 @@
     return lax.dot_general(a, b, (((0,), (0,)), ((), ())), preferred_element_type=F32)
 
 
-def stack_heads(rows, g):
-    first = g * GROUP * HEAD_DIM
+def feature_heads(features, g):
+    first = g * GROUP
     return jnp.concatenate(
-        [rows[:, first + r * HEAD_DIM : first + (r + 1) * HEAD_DIM] for r in range(GROUP)], axis=0
+        [features[(first + r) * HEAD_DIM : (first + r + 1) * HEAD_DIM] for r in range(GROUP)],
+        axis=1,
     )
 
 
-def spread_heads(stacked):
-    return jnp.concatenate([stacked[r * BLK : (r + 1) * BLK] for r in range(GROUP)], axis=1)
+def pad_half(features, odd):
+    zeros = jnp.zeros_like(features)
+    return jnp.concatenate([zeros, features] if odd else [features, zeros], axis=0)
+
+
+def take_half(features, odd):
+    return features[odd * HEAD_DIM : (odd + 1) * HEAD_DIM]
 
 
 def attention_kernel(list_len, slot_ref, q_ref, ng_ref, *refs):
     arrived, (normed_ref, qg_ref) = refs[:2], refs[2:4]
     back, (probs_scr, kv_scr, parts_scr, in_sems, out_sems) = refs[4:6], refs[6:]
     step = pl.program_id(0)
-    entries = kv_scr.shape[0]
+    entries = in_sems.shape[0]
     per_part = arrived[0].shape[0]
 
+    def rows_of(e):
+        return pl.ds(pl.multiple_of(e * BLK, BLK), BLK)
+
     def fetch(e, part, slot):
-        return pltpu.make_async_copy(arrived[part].at[slot], kv_scr.at[e], in_sems.at[e])
+        return pltpu.make_async_copy(arrived[part].at[slot], kv_scr.at[rows_of(e)], in_sems.at[e])
 
     def give(e, part, slot):
-        return pltpu.make_async_copy(parts_scr.at[e], back[part].at[slot], out_sems.at[e])
+        return pltpu.make_async_copy(parts_scr.at[rows_of(e)], back[part].at[slot], out_sems.at[e])
 
     def start(copy, e):
         slot = slot_ref[e]
@@ -68,42 +78,44 @@
     first = step * list_len
     for l in range(list_len):
         fetch(first + l, 0, 0).wait()
-    keys = jnp.concatenate([kv_scr[first + l, :, :KV] for l in range(list_len)], axis=0)
-    values = jnp.concatenate([kv_scr[first + l, :, KV:] for l in range(list_len)], axis=0)
+    here = pl.ds(pl.multiple_of(step * list_len * BLK, list_len * BLK), list_len * BLK)
+    keys = [kv_scr[here, j * PAIR : (j + 1) * PAIR] for j in range(KV // PAIR)]
+    values = [kv_scr[here, KV + j * PAIR : KV + (j + 1) * PAIR] for j in range(KV // PAIR)]
     queries = q_ref[...] * jnp.asarray(TEMPER, BF16)
+    padded = [pad_half(feature_heads(queries, g), g % 2) for g in range(KV_HEADS)]
     attended = []
     for g in range(KV_HEADS):
-        cols = slice(g * HEAD_DIM, (g + 1) * HEAD_DIM)
-        scores = dot_nt(stack_heads(queries, g), keys[:, cols])
-        expo = jnp.exp(scores - jnp.max(scores, axis=-1, keepdims=True))
-        probs = expo * (1.0 / jnp.sum(expo, axis=-1, keepdims=True))
+        scores = jnp.dot(keys[g // 2], padded[g], preferred_element_type=F32)
+        expo = jnp.exp(scores - jnp.max(scores, axis=0, keepdims=True))
+        probs = expo * (1.0 / jnp.sum(expo, axis=0, keepdims=True))
         probs_scr[g] = probs
-        out = jnp.dot(probs.astype(BF16), values[:, cols], preferred_element_type=F32)
-        attended.append(spread_heads(out.astype(BF16)))
-    attended = jnp.concatenate(attended, axis=1).astype(F32)
-    width = attended.shape[1]
-    inverse = lax.rsqrt(jnp.sum(attended * attended, axis=-1, keepdims=True) / width + EPSILON)
+        out = take_half(dot_tn(values[g // 2], probs.astype(BF16)), g % 2)
+        attended += [out[:, r * BLK : (r + 1) * BLK] for r in range(GROUP)]
+    attended = jnp.concatenate(attended, axis=0).astype(BF16).astype(F32)
+    width = attended.shape[0]
+    inverse = lax.rsqrt(jnp.sum(attended * attended, axis=0, keepdims=True) / width + EPSILON)
     normed = attended * inverse
     normed_ref[...] = normed.astype(BF16)
     normed_grad = ng_ref[...]
-    shared = jnp.sum(normed_grad * normed, axis=-1, keepdims=True) / width
+    shared = jnp.sum(normed_grad * normed, axis=0, keepdims=True) / width
     attended_grad = ((normed_grad - normed * shared) * inverse).astype(BF16)
-    for g in range(KV_HEADS):
-        cols = slice(g * HEAD_DIM, (g + 1) * HEAD_DIM)
-        out_grad = stack_heads(attended_grad, g)
-        prob_grad = dot_nt(out_grad, values[:, cols])
-        probs = probs_scr[g]
-        row_dot = jnp.sum(probs * prob_grad, axis=-1, keepdims=True)
-        score_grad = (probs * (prob_grad - row_dot)).astype(BF16)
-        query_grad = jnp.dot(score_grad, keys[:, cols], preferred_element_type=F32) * TEMPER
-        left = g * GROUP * HEAD_DIM
-        qg_ref[:, left : left + GROUP * HEAD_DIM] = spread_heads(query_grad.astype(BF16))
-        key_part = dot_tn(score_grad, stack_heads(queries, g)).astype(BF16)
-        value_part = dot_tn(probs.astype(BF16), out_grad).astype(BF16)
-        for l in range(list_len):
-            rows = slice(l * BLK, (l + 1) * BLK)
-            parts_scr[first + l, :, g * HEAD_DIM : (g + 1) * HEAD_DIM] = key_part[rows]
-            parts_scr[first + l, :, KV + g * HEAD_DIM : KV + (g + 1) * HEAD_DIM] = value_part[rows]
+    for j in range(KV // PAIR):
+        key_part = value_part = 0.0
+        for odd in range(2):
+            g = 2 * j + odd
+            out_grad = pad_half(feature_heads(attended_grad, g), odd)
+            prob_grad = jnp.dot(values[j], out_grad, preferred_element_type=F32)
+            probs = probs_scr[g]
+            row_dot = jnp.sum(probs * prob_grad, axis=0, keepdims=True)
+            score_grad = (probs * (prob_grad - row_dot)).astype(BF16)
+            query_grad = (take_half(dot_tn(keys[j], score_grad), odd) * TEMPER).astype(BF16)
+            for r in range(GROUP):
+                top = (g * GROUP + r) * HEAD_DIM
+                qg_ref[top : top + HEAD_DIM, :] = query_grad[:, r * BLK : (r + 1) * BLK]
+            key_part += dot_nt(score_grad, padded[g])
+            value_part += dot_nt(probs.astype(BF16), out_grad)
+        parts_scr[here, j * PAIR : (j + 1) * PAIR] = key_part.astype(BF16)
+        parts_scr[here, KV + j * PAIR : KV + (j + 1) * PAIR] = value_part.astype(BF16)
     for l in range(list_len):
         start(give, first + l)
 
@@ -114,10 +126,10 @@
 
 
 def attention(slots, queries, normed_grad, arrived, list_len):
-    rows, width = queries.shape
+    width, rows = queries.shape
     blocks = rows // BLK
     entries = blocks * list_len
-    row_spec = pl.BlockSpec((BLK, width), lambda r, s: (r, 0))
+    row_spec = pl.BlockSpec((width, BLK), lambda r, s: (0, r))
     anywhere = pl.BlockSpec(memory_space=pl.ANY)
     keys = list_len * BLK
     pairs = HEADS * rows * keys
@@ -129,14 +141,14 @@
             in_specs=[row_spec, row_spec, anywhere, anywhere],
             out_specs=[row_spec, row_spec, anywhere, anywhere],
             scratch_shapes=[
-                pltpu.VMEM((KV_HEADS, GROUP * BLK, keys), F32),
-                pltpu.VMEM((entries, BLK, 2 * KV), BF16),
-                pltpu.VMEM((entries, BLK, 2 * KV), BF16),
+                pltpu.VMEM((KV_HEADS, keys, GROUP * BLK), F32),
+                pltpu.VMEM((entries * BLK, 2 * KV), BF16),
+                pltpu.VMEM((entries * BLK, 2 * KV), BF16),
                 pltpu.SemaphoreType.DMA((entries,)),
                 pltpu.SemaphoreType.DMA((entries,)),
             ],
         ),
-        out_shape=[jax.ShapeDtypeStruct((rows, width), BF16)] * 2
+        out_shape=[jax.ShapeDtypeStruct((width, rows), BF16)] * 2
         + [jax.ShapeDtypeStruct(arrived[0].shape, BF16)] * 2,
         compiler_params=pltpu.CompilerParams(vmem_limit_bytes=56 * 1024 * 1024),
         cost_estimate=pl.CostEstimate(
@@ -230,13 +242,17 @@
     mine = jnp.concatenate([keys, values], axis=-1).reshape(block_count, BLK, 2 * KV)
     tiles_here = [cross(mine, 0), cross(mine, half)]
     arrived = [exchange(tiles_here[p][jnp.maximum(wanted[p], 0)]) for p in range(2)]
-    queries = jnp.dot(tokens, w_query, preferred_element_type=F32).astype(BF16)
-    normed_grad = dot_nt(out_grad[0], w_out)
+    queries = lax.dot_general(
+        w_query, tokens, (((0,), (1,)), ((), ())), preferred_element_type=F32
+    ).astype(BF16)
+    normed_grad = dot_nt(w_out, out_grad[0])
     normed_low, query_grad, *back = attention(my_slots, queries, normed_grad, arrived, list_len)
     far = cross(owner_sum(wanted[1], exchange(back[1]), block_count), half)
     near = cross(owner_sum(wanted[0], exchange(back[0]), block_count), 0)
-    layer_out = jnp.dot(normed_low, w_out, preferred_element_type=F32).astype(BF16)
-    query_term = dot_nt(query_grad, w_query)
+    layer_out = dot_tn(normed_low, w_out).astype(BF16)
+    query_term = lax.dot_general(
+        query_grad, w_query, (((0,), (1,)), ((), ())), preferred_element_type=F32
+    )
     kv_grad = (near.astype(F32) + far.astype(F32)).astype(BF16).reshape(rows, 2 * KV)
     kv_term = dot_nt(kv_grad[:, :KV], w_key) + dot_nt(kv_grad[:, KV:], w_value)
     input_grad = (query_term + kv_term).astype(BF16)

time: 194 us -> 190 us (0.979)
  Pallas kernels: 30.2 us -> 26.2 us
    pallas_call x1, Pallas kernels: 27.3 us -> 23.4 us  [attention(): pl.pallas_call(functools.partial(attention_kernel, list_len), grid_spec=p...]
    dot_general x2 -> x3, matrix products: 4.68 us -> 6.45 us  [the longest x1 3.05 us: shards(): lax.dot_general(w_query, tokens, (((0,), (1,)), ((), ())), preferred_elem...]
    dot_general x4 -> x3, matrix products: 4.53 us -> 2.83 us  [dot_nt(): lax.dot_general(a, b, (((1,), (1,)), ((), ())), preferred_element_type=F32)]
where the time goes in v5:
time: 190 us; the launch traced here: 189 us
  waiting for transfers between devices  85.8 us (45%)
  blocking collectives  32.8 us (17%)
  Pallas kernels  26.2 us (14%)
  starting transfers between devices  22 us (12%)
  matrix products  11.5 us (6%)
  local copies, waits for them, and re-layouts  8.5 us (4%)
  other arithmetic  1.91 us (1%)
    all_to_all x3, waiting for transfers between devices, exchange(): lax.all_to_all(value, 'tile', split_axis=0, concat_axis=0, tiled=True, ax...  53.2 us
    all_to_all x1, blocking collectives, exchange(): lax.all_to_all(value, 'tile', split_axis=0, concat_axis=0, tiled=True, ax...  32.8 us
    ppermute x4, waiting for transfers between devices, cross(): return lax.ppermute(value, ('vintage', 'tile'), pairs)  32.6 us
    pallas_call x1, Pallas kernels, attention(): pl.pallas_call(functools.partial(attention_kernel, list_len), grid_spec=p...  23.4 us
    all_to_all x3, starting transfers between devices, exchange(): lax.all_to_all(value, 'tile', split_axis=0, concat_axis=0, tiled=True, ax...  19.3 us
    gather x2, local copies, waits for them, and re-layouts, shards(): tiles_here[p][jnp.maximum(wanted[p], 0)]  4.03 us
  transfers between devices with their start and end apart: 7, of which 6 were waited for; matrix products, arithmetic and copies ran while one was open for 6% of the time, Pallas kernels for 1%

profile of v5, /device:TPU:0, one launch (start us, length us, event | category | flops | bytes accessed | tf_op | source)
XLA Modules:
  0.0 189.5 jit_solution(3775246455885343639)
XLA Ops:
  0.7 1.8 convolution_convert_fusion.3
  2.5 0.4 convolution_convert_fusion.2
  3.0 0.2 copy.24
  3.2 0.5 collective-permute-start
  3.7 0.1 iota_add_fusion
  3.8 0.1 copy.16
  3.9 0.1 reshape_squeeze.6
  4.0 0.1 copy.18
  4.1 0.1 reshape_squeeze.7
  4.2 0.3 convert_reduce_fusion
  4.5 0.2 select_reduce_fusion
  4.7 0.1 copy.19
  4.8 0.1 reshape.151
  4.9 0.4 collective-permute-done
  5.2 2.0 %gather_fusion = bf16[16,128,512]{2,1,0:T(8,128)(2,1)} fusion(bf16[4,128,512]{2,1,0:T(8,128)(2,1)S(1)} %collective-permute-done, s32[1024]{0:T(1024)S(1)} %pad_clamp_fusion.1), kind=kCustom, calls=%fused_computation | custom fusion | bytes 4194368 | tf_op jit(solution)/shard_map/gather | solution.py:244
  7.3 6.1 %all-to-all-start = ((bf16[16,128,512]{2,1,0:T(8,128)(2,1)}), bf16[16,128,512]{2,1,0:T(8,128)(2,1)}, u32[]{:S(2)}, u32[]{:S(2)}) async-start(bf16[16,128,512]{2,1,0:T(8,128)(2,1)} %gather_fusion), calls=%async_computation | async-start | bytes 4194304 | tf_op jit(solution)/shard_map/all_to_all | solution.py:219
  13.4 2.1 %collective-permute-start.1 = (bf16[4,128,512]{2,1,0:T(8,128)(2,1)S(1)}, bf16[4,128,512]{2,1,0:T(8,128)(2,1)S(1)}, u32[]{:S(2)}, u32[]{:S(2)}) collective-permute-start(bf16[4,128,512]{2,1,0:T(8,128)(2,1)S(1)} %bitcast.35), channel_id=1, source_target_pairs={{0,24},{1,25},{2,26},{3,27},{4,28},{5,29},{6,30},{7,31},{8,16},{9,... | collective-permute-start | bytes 1572872 | tf_op jit(solution)/shard_map/ppermute | solution.py:216
  15.5 0.1 copy.21
  15.5 0.1 reshape.159
  15.6 32.1 %collective-permute-done.1 = bf16[4,128,512]{2,1,0:T(8,128)(2,1)S(1)} collective-permute-done((bf16[4,128,512]{2,1,0:T(8,128)(2,1)S(1)}, bf16[4,128,512]{2,1,0:T(8,128)(2,1)S(1)}, u32[]{:S(2)}, u32[]{:S(2)}) %collective-permute-start.1) | collective-permute-done | bytes 524320 | tf_op jit(solution)/shard_map/ppermute | solution.py:216
  47.7 2.0 %gather_fusion.1 = bf16[16,128,512]{2,1,0:T(8,128)(2,1)} fusion(bf16[4,128,512]{2,1,0:T(8,128)(2,1)S(1)} %collective-permute-done.1, s32[1024]{0:T(1024)S(1)} %pad_clamp_fusion), kind=kCustom, calls=%fused_computation.1 | custom fusion | bytes 4194368 | tf_op jit(solution)/shard_map/gather | solution.py:244
  49.7 0.2 all-to-all-done.refs_0_
  49.9 9.6 %all-to-all-start.1 = ((bf16[16,128,512]{2,1,0:T(8,128)(2,1)}), bf16[16,128,512]{2,1,0:T(8,128)(2,1)}, u32[]{:S(2)}, u32[]{:S(2)}) async-start(bf16[16,128,512]{2,1,0:T(8,128)(2,1)} %gather_fusion.1), calls=%async_computation.1 | async-start | bytes 4194304 | tf_op jit(solution)/shard_map/all_to_all | solution.py:219
  59.5 0.5 fusion.17.slot_ref
  60.1 3.0 %convolution_convert_fusion.1.q_ref = bf16[768,512]{1,0:T(8,128)(2,1)} fusion(bf16[768,768]{1,0:T(8,128)(2,1)} %param.10, bf16[1,512,768]{2,1,0:T(8,128)(2,1)S(1)} %copy-done.2), kind=kOutput, calls=%fused_computation.4 | convolution fusion | flops 604372992 | bytes 2752512 | tf_op jit(solution)/shard_map/dot_general | solution.py:245
  63.1 2.0 %fusion.2.ng_ref = f32[768,512]{1,0:T(8,128)} fusion(bf16[768,768]{1,0:T(8,128)(2,1)S(1)} %copy-done, bf16[1,512,768]{2,1,0:T(8,128)(2,1)S(1)} %copy-done.10), kind=kOutput, calls=%fused_computation.10 | convolution fusion | flops 603979776 | bytes 3538944 | tf_op jit(solution)/shard_map/dot_general | solution.py:25
  65.1 21.4 %all-to-all-done.1.refs_1_ = bf16[16,128,512]{2,1,0:T(8,128)(2,1)} async-done(((bf16[16,128,512]{2,1,0:T(8,128)(2,1)}), bf16[16,128,512]{2,1,0:T(8,128)(2,1)}, u32[]{:S(2)}, u32[]{:S(2)}) %all-to-all-start.1) | async-done | bytes 2097184 | tf_op jit(solution)/shard_map/all_to_all | solution.py:219
  86.5 23.4 %attention.1 = (bf16[768,512]{1,0:T(8,128)(2,1)}, bf16[768,512]{1,0:T(8,128)(2,1)}, bf16[16,128,512]{2,1,0:T(8,128)(2,1)}, bf16[16,128,512]{2,1,0:T(8,128)(2,1)}) custom-call(s32[16]{0:T(128)} %fusion.17.slot_ref, bf16[768,512]{1,0:T(8,128)(2,1)} %convolution_convert_fusion.1.q_ref, f32[768,512]{1,0:T(8,128)} %fusion.2.ng_ref, ...), custom_call_target="tpu_custom_call" | custom-call | flops 2415919104 | bytes 6291456 | tf_op jit(solution)/shard_map/attention/pallas_call | solution.py:136
  109.9 32.8 %all_to_all.20.parts_ref = bf16[16,128,512]{2,1,0:T(8,128)(2,1)} all-to-all(bf16[16,128,512]{2,1,0:T(8,128)(2,1)} %get-tuple-element.9), channel_id=1, replica_groups={{0,1,2,3,4,5,6,7},{8,9,10,11,12,13,14,15},{16,17,18,19,20,21,22,23},{24..., dimensions={0} | all-to-all | bytes 4194304 | tf_op jit(solution)/shard_map/all_to_all | solution.py:219
  142.6 3.6 %all-to-all-start.2 = ((bf16[16,128,512]{2,1,0:T(8,128)(2,1)}), bf16[16,128,512]{2,1,0:T(8,128)(2,1)S(1)}, u32[]{:S(2)}, u32[]{:S(2)}) async-start(bf16[16,128,512]{2,1,0:T(8,128)(2,1)} %get-tuple-element.8), calls=%async_computation.2 | async-start | bytes 4194304 | tf_op jit(solution)/shard_map/all_to_all | solution.py:219
  146.3 0.1 copy.22
  146.3 0.1 squeeze.27.wanted_ref
  146.4 0.1 copy.23
  146.5 0.1 squeeze.28.wanted_ref
  146.6 1.6 copy-done.1
  148.2 1.8 owner_sum.3
  150.0 31.6 %all-to-all-done.2.parts_ref = bf16[16,128,512]{2,1,0:T(8,128)(2,1)S(1)} async-done(((bf16[16,128,512]{2,1,0:T(8,128)(2,1)}), bf16[16,128,512]{2,1,0:T(8,128)(2,1)S(1)}, u32[]{:S(2)}, u32[]{:S(2)}) %all-to-all-start.2) | async-done | bytes 2097184 | tf_op jit(solution)/shard_map/all_to_all | solution.py:219
  181.6 1.0 owner_sum.2
  182.6 0.1 collective-permute-start.2
  182.7 0.0 copy-done.11
  182.7 1.7 fusion
  184.4 0.2 collective-permute-done.2
  184.6 1.2 add_convert_fusion.1
  185.8 0.4 fusion.7
  186.3 0.4 fusion.9
  186.7 0.8 copy-done.6
  187.5 0.2 copy-done.7
  187.7 1.7 fusion.1
  (31 shorter events, 0.2 us)
Async XLA Ops:
  0.6 62.5 %copy-start = (bf16[768,768]{1,0:T(8,128)(2,1)S(1)}, bf16[768,768]{1,0:T(8,128)(2,1)}, u32[]{:S(2)}) copy-start(bf16[768,768]{1,0:T(8,128)(2,1)} %param.13) | copy-start | bytes 3538948
  0.6 1.8 copy-start.2
  0.7 1.8 copy-start.3
  2.5 1.3 copy-start.8
  2.5 1.5 copy-start.9
  3.2 2.1 %collective-permute-start = (bf16[4,128,512]{2,1,0:T(8,128)(2,1)S(1)}, bf16[4,128,512]{2,1,0:T(8,128)(2,1)S(1)}, u32[]{:S(2)}, u32[]{:S(2)}) collective-permute-start(bf16[4,128,512]{2,1,0:T(8,128)(2,1)S(1)} %bitcast.34), channel_id=1, source_target_pairs={{0,16},{1,17},{2,18},{3,19},{4,20},{5,21},{6,22},{7,23},{8,24},{9,... | collective-permute-start | bytes 1572872 | tf_op jit(solution)/shard_map/ppermute | solution.py:216
  7.3 42.6 %all-to-all-start = ((bf16[16,128,512]{2,1,0:T(8,128)(2,1)}), bf16[16,128,512]{2,1,0:T(8,128)(2,1)}, u32[]{:S(2)}, u32[]{:S(2)}) async-start(bf16[16,128,512]{2,1,0:T(8,128)(2,1)} %gather_fusion), calls=%async_computation | async-start | bytes 4194304 | tf_op jit(solution)/shard_map/all_to_all | solution.py:219
  13.4 34.3 %collective-permute-start.1 = (bf16[4,128,512]{2,1,0:T(8,128)(2,1)S(1)}, bf16[4,128,512]{2,1,0:T(8,128)(2,1)S(1)}, u32[]{:S(2)}, u32[]{:S(2)}) collective-permute-start(bf16[4,128,512]{2,1,0:T(8,128)(2,1)S(1)} %bitcast.35), channel_id=1, source_target_pairs={{0,24},{1,25},{2,26},{3,27},{4,28},{5,29},{6,30},{7,31},{8,16},{9,... | collective-permute-start | bytes 1572872 | tf_op jit(solution)/shard_map/ppermute | solution.py:216
  49.9 36.6 %all-to-all-start.1 = ((bf16[16,128,512]{2,1,0:T(8,128)(2,1)}), bf16[16,128,512]{2,1,0:T(8,128)(2,1)}, u32[]{:S(2)}, u32[]{:S(2)}) async-start(bf16[16,128,512]{2,1,0:T(8,128)(2,1)} %gather_fusion.1), calls=%async_computation.1 | async-start | bytes 4194304 | tf_op jit(solution)/shard_map/all_to_all | solution.py:219
  60.1 3.1 %copy-start.10 = (bf16[1,512,768]{2,1,0:T(8,128)(2,1)S(1)}, bf16[1,512,768]{2,1,0:T(8,128)(2,1)}, u32[]{:S(2)}) copy-start(bf16[1,512,768]{2,1,0:T(8,128)(2,1)} %param.9) | copy-start | bytes 2359300
  142.6 38.9 %all-to-all-start.2 = ((bf16[16,128,512]{2,1,0:T(8,128)(2,1)}), bf16[16,128,512]{2,1,0:T(8,128)(2,1)S(1)}, u32[]{:S(2)}, u32[]{:S(2)}) async-start(bf16[16,128,512]{2,1,0:T(8,128)(2,1)} %get-tuple-element.8), calls=%async_computation.2 | async-start | bytes 4194304 | tf_op jit(solution)/shard_map/all_to_all | solution.py:219
  146.6 1.6 copy-start.1
  150.0 34.4 %collective-permute-start.3 = (bf16[4,128,512]{2,1,0:T(8,128)(2,1)}, bf16[4,128,512]{2,1,0:T(8,128)(2,1)}, u32[]{:S(2)}, u32[]{:S(2)}) collective-permute-start(bf16[4,128,512]{2,1,0:T(8,128)(2,1)} %owner_sum.3), channel_id=1, source_target_pairs={{0,24},{1,25},{2,26},{3,27},{4,28},{5,29},{6,30},{7,31},{8,16},{9,... | collective-permute-start | bytes 1572872 | tf_op jit(solution)/shard_map/ppermute | solution.py:216
  181.6 1.1 copy-start.11
  182.6 2.0 %collective-permute-start.2 = (bf16[4,128,512]{2,1,0:T(8,128)(2,1)S(1)}, bf16[4,128,512]{2,1,0:T(8,128)(2,1)S(1)}, u32[]{:S(2)}, u32[]{:S(2)}) collective-permute-start(bf16[4,128,512]{2,1,0:T(8,128)(2,1)S(1)} %owner_sum.2), channel_id=1, source_target_pairs={{0,16},{1,17},{2,18},{3,19},{4,20},{5,21},{6,22},{7,23},{8,24},{9,... | collective-permute-start | bytes 1572872 | tf_op jit(solution)/shard_map/ppermute | solution.py:216
  184.4 1.4 copy-start.4
  184.4 1.8 copy-start.5
  186.3 1.3 copy-start.6
  186.3 1.5 copy-start.7

commit v6 on v5

--- a/solution.py
+++ b/solution.py
@@ -37,18 +37,25 @@
     )
 
 
-def pad_half(features, odd):
-    zeros = jnp.zeros_like(features)
-    return jnp.concatenate([zeros, features] if odd else [features, zeros], axis=0)
-
-
-def take_half(features, odd):
-    return features[odd * HEAD_DIM : (odd + 1) * HEAD_DIM]
+def two_groups(features, j):
+    low, high = feature_heads(features, 2 * j), feature_heads(features, 2 * j + 1)
+    zeros = jnp.zeros_like(low)
+    return jnp.concatenate(
+        [jnp.concatenate([low, zeros], axis=1), jnp.concatenate([zeros, high], axis=1)], axis=0
+    )
+
+
+def head_rows(pair_out):
+    heads = []
+    for i in range(2 * GROUP):
+        top = i // GROUP * HEAD_DIM
+        heads.append(pair_out[top : top + HEAD_DIM, i * BLK : (i + 1) * BLK])
+    return jnp.concatenate(heads, axis=0)
 
 
 def attention_kernel(list_len, slot_ref, q_ref, ng_ref, *refs):
     arrived, (normed_ref, qg_ref) = refs[:2], refs[2:4]
-    back, (probs_scr, kv_scr, parts_scr, in_sems, out_sems) = refs[4:6], refs[6:]
+    back, (expo_scr, kv_scr, parts_scr, in_sems, out_sems) = refs[4:6], refs[6:]
     step = pl.program_id(0)
     entries = in_sems.shape[0]
     per_part = arrived[0].shape[0]
@@ -82,38 +89,47 @@
     keys = [kv_scr[here, j * PAIR : (j + 1) * PAIR] for j in range(KV // PAIR)]
     values = [kv_scr[here, KV + j * PAIR : KV + (j + 1) * PAIR] for j in range(KV // PAIR)]
     queries = q_ref[...] * jnp.asarray(TEMPER, BF16)
-    padded = [pad_half(feature_heads(queries, g), g % 2) for g in range(KV_HEADS)]
-    attended = []
-    for g in range(KV_HEADS):
-        scores = jnp.dot(keys[g // 2], padded[g], preferred_element_type=F32)
-        expo = jnp.exp(scores - jnp.max(scores, axis=0, keepdims=True))
-        probs = expo * (1.0 / jnp.sum(expo, axis=0, keepdims=True))
-        probs_scr[g] = probs
-        out = take_half(dot_tn(values[g // 2], probs.astype(BF16)), g % 2)
-        attended += [out[:, r * BLK : (r + 1) * BLK] for r in range(GROUP)]
-    attended = jnp.concatenate(attended, axis=0).astype(BF16).astype(F32)
+    pairs = range(KV // PAIR)
+    wide = [two_groups(queries, j) for j in pairs]
+    scores = [jnp.dot(keys[j], wide[j], preferred_element_type=F32) for j in pairs]
+    attended, scales = [], []
+    for j in pairs:
+        expo = jnp.exp(scores[j] - jnp.max(scores[j], axis=0, keepdims=True))
+        scale = 1.0 / jnp.sum(expo, axis=0, keepdims=True)
+        expo_scr[j] = expo.astype(BF16)
+        attended.append(head_rows(dot_tn(values[j], expo_scr[j]) * scale))
+        scales += [
+            jnp.broadcast_to(scale[:, i * BLK : (i + 1) * BLK], (HEAD_DIM, BLK))
+            for i in range(2 * GROUP)
+        ]
+    exact = jnp.concatenate(attended, axis=0)
+    attended = exact.astype(BF16).astype(F32)
     width = attended.shape[0]
     inverse = lax.rsqrt(jnp.sum(attended * attended, axis=0, keepdims=True) / width + EPSILON)
     normed = attended * inverse
     normed_ref[...] = normed.astype(BF16)
     normed_grad = ng_ref[...]
     shared = jnp.sum(normed_grad * normed, axis=0, keepdims=True) / width
-    attended_grad = ((normed_grad - normed * shared) * inverse).astype(BF16)
-    for j in range(KV // PAIR):
-        key_part = value_part = 0.0
-        for odd in range(2):
-            g = 2 * j + odd
-            out_grad = pad_half(feature_heads(attended_grad, g), odd)
-            prob_grad = jnp.dot(values[j], out_grad, preferred_element_type=F32)
-            probs = probs_scr[g]
-            row_dot = jnp.sum(probs * prob_grad, axis=0, keepdims=True)
-            score_grad = (probs * (prob_grad - row_dot)).astype(BF16)
-            query_grad = (take_half(dot_tn(keys[j], score_grad), odd) * TEMPER).astype(BF16)
-            for r in range(GROUP):
-                top = (g * GROUP + r) * HEAD_DIM
-                qg_ref[top : top + HEAD_DIM, :] = query_grad[:, r * BLK : (r + 1) * BLK]
-            key_part += dot_nt(score_grad, padded[g])
-            value_part += dot_nt(probs.astype(BF16), out_grad)
+    attended_grad = (normed_grad - normed * shared) * inverse
+    scaled_grad = (attended_grad * jnp.concatenate(scales, axis=0)).astype(BF16)
+    overlap = scaled_grad.astype(F32) * exact
+    grads = [two_groups(scaled_grad, j) for j in pairs]
+    prob_grads = [jnp.dot(values[j], grads[j], preferred_element_type=F32) for j in pairs]
+    for j in pairs:
+        heads = range(2 * GROUP * j, 2 * GROUP * (j + 1))
+        row_dot = jnp.concatenate(
+            [
+                jnp.sum(overlap[h * HEAD_DIM : (h + 1) * HEAD_DIM], axis=0, keepdims=True)
+                for h in heads
+            ],
+            axis=1,
+        )
+        expo = expo_scr[j]
+        value_part = dot_nt(expo, grads[j])
+        score_grad = (expo.astype(F32) * (prob_grads[j] - row_dot)).astype(BF16)
+        query_grad = head_rows(dot_tn(keys[j], score_grad) * TEMPER).astype(BF16)
+        qg_ref[heads.start * HEAD_DIM : heads.stop * HEAD_DIM, :] = query_grad
+        key_part = dot_nt(score_grad, wide[j])
         parts_scr[here, j * PAIR : (j + 1) * PAIR] = key_part.astype(BF16)
         parts_scr[here, KV + j * PAIR : KV + (j + 1) * PAIR] = value_part.astype(BF16)
     for l in range(list_len):
@@ -141,7 +157,7 @@
             in_specs=[row_spec, row_spec, anywhere, anywhere],
             out_specs=[row_spec, row_spec, anywhere, anywhere],
             scratch_shapes=[
-                pltpu.VMEM((KV_HEADS, keys, GROUP * BLK), F32),
+                pltpu.VMEM((KV // PAIR, keys, 2 * GROUP * BLK), BF16),
                 pltpu.VMEM((entries * BLK, 2 * KV), BF16),
                 pltpu.VMEM((entries * BLK, 2 * KV), BF16),
                 pltpu.SemaphoreType.DMA((entries,)),
@@ -203,6 +219,9 @@
     my_tile = lax.axis_index("tile")
     my_half, my_place = my_tile // half, my_tile % half
     groups = [list(range(half)), list(range(half, tile_count))]
+    swaps = [
+        [v * tile_count + t, (1 - v) * tile_count + t + half] for v in range(2) for t in range(half)
+    ]
     block_count = rows // BLK
     list_len = key_tiles.shape[2]
     entry_count = block_count * list_len
@@ -240,8 +259,12 @@
     keys = jnp.dot(tokens, w_key, preferred_element_type=F32).astype(BF16)
     values = jnp.dot(tokens, w_value, preferred_element_type=F32).astype(BF16)
     mine = jnp.concatenate([keys, values], axis=-1).reshape(block_count, BLK, 2 * KV)
-    tiles_here = [cross(mine, 0), cross(mine, half)]
-    arrived = [exchange(tiles_here[p][jnp.maximum(wanted[p], 0)]) for p in range(2)]
+    both = lax.all_gather(mine, ("vintage", "tile"), axis_index_groups=swaps)
+    both = both.reshape(2 * block_count, BLK, 2 * KV)
+    picked = jnp.maximum(wanted, 0)
+    near_send = cross(mine, 0)[picked[0]]
+    far_send = both[picked[1] + (my_half ^ 1) * block_count]
+    arrived = [exchange(near_send), exchange(far_send)]
     queries = lax.dot_general(
         w_query, tokens, (((0,), (1,)), ((), ())), preferred_element_type=F32
     ).astype(BF16)

time: 190 us -> 195 us (1.026)
  between operations: 0.83 us -> 14.3 us
  Pallas kernels: 26.2 us -> 20.5 us
  starting transfers between devices: 22 us -> 16.4 us
  waiting for transfers between devices: 85.8 us -> 88.5 us
    all_gather x0 -> x1, waiting for transfers between devices: none -> 35.9 us  [shards(): both = lax.all_gather(mine, ('vintage', 'tile'), axis_index_groups=swaps)]
    ppermute x4 -> x3, waiting for transfers between devices: 32.6 us -> 0.54 us  [cross(): return lax.ppermute(value, ('vintage', 'tile'), pairs)]
    pallas_call x1, Pallas kernels: 23.4 us -> 17.7 us  [attention(): pl.pallas_call(functools.partial(attention_kernel, list_len), grid_spec=p...]
    all_to_all x3, starting transfers between devices: 19.3 us -> 15.8 us  [exchange(): lax.all_to_all(value, 'tile', split_axis=0, concat_axis=0, tiled=True, ax...]
    ppermute x4 -> x3, starting transfers between devices: 2.64 us -> 0.59 us  [cross(): return lax.ppermute(value, ('vintage', 'tile'), pairs)]
  transfers between devices with their start and end apart: 7 -> 7, of which waited for: 6 -> 5; matrix products, arithmetic and copies ran while one was open for 6% -> 6% of each run, Pallas kernels for 1% -> 1%
where the time goes in v6:
time: 195 us; the launch traced here: 194 us
  waiting for transfers between devices  88.5 us (45%)
  blocking collectives  31.4 us (16%)
  Pallas kernels  20.5 us (11%)
  starting transfers between devices  16.4 us (8%)
  between operations  14.3 us (7%)
  matrix products  11.5 us (6%)
  local copies, waits for them, and re-layouts  9.75 us (5%)
    all_to_all x3, waiting for transfers between devices, exchange(): lax.all_to_all(value, 'tile', split_axis=0, concat_axis=0, tiled=True, ax...  51.4 us
    all_gather x1, waiting for transfers between devices, shards(): both = lax.all_gather(mine, ('vintage', 'tile'), axis_index_groups=swaps)  35.9 us
    all_to_all x1, blocking collectives, exchange(): lax.all_to_all(value, 'tile', split_axis=0, concat_axis=0, tiled=True, ax...  31.4 us
    pallas_call x1, Pallas kernels, attention(): pl.pallas_call(functools.partial(attention_kernel, list_len), grid_spec=p...  17.7 us
    all_to_all x3, starting transfers between devices, exchange(): lax.all_to_all(value, 'tile', split_axis=0, concat_axis=0, tiled=True, ax...  15.8 us
  transfers between devices with their start and end apart: 7, of which 5 were waited for; matrix products, arithmetic and copies ran while one was open for 6% of the time, Pallas kernels for 1%

profile of v6, /device:TPU:0, one launch (start us, length us, event | category | flops | bytes accessed | tf_op | source)
XLA Modules:
  0.0 194.2 jit_solution(18046217271076719598)
XLA Ops:
  7.2 1.8 convolution_convert_fusion.3
  9.0 0.4 convolution_convert_fusion.2
  9.5 0.2 copy.28
  9.7 0.5 collective-permute-start
  10.3 0.1 iota_add_fusion
  10.4 0.1 copy.20
  10.4 0.1 reshape_squeeze.6
  10.5 0.1 copy.22
  10.6 0.1 reshape_squeeze.7
  10.7 0.3 convert_reduce_fusion
  11.0 0.2 select_reduce_fusion
  11.3 0.1 copy.23
  11.3 0.1 squeeze.29
  11.4 0.4 collective-permute-done
  11.8 2.0 %gather_fusion = bf16[16,128,512]{2,1,0:T(8,128)(2,1)} fusion(bf16[4,128,512]{2,1,0:T(8,128)(2,1)S(1)} %collective-permute-done, s32[1024]{0:T(1024)S(1)} %pad_clamp_fusion.1), kind=kCustom, calls=%fused_computation | custom fusion | bytes 4194368 | tf_op jit(solution)/shard_map/gather | solution.py:265
  13.8 6.1 %all-to-all-start = ((bf16[16,128,512]{2,1,0:T(8,128)(2,1)}), bf16[16,128,512]{2,1,0:T(8,128)(2,1)}, u32[]{:S(2)}, u32[]{:S(2)}) async-start(bf16[16,128,512]{2,1,0:T(8,128)(2,1)} %gather_fusion), calls=%async_computation | async-start | bytes 4194304 | tf_op jit(solution)/shard_map/all_to_all | solution.py:238
  19.9 0.0 all-gather.2.cloned.1.call-start
  20.0 0.7 all-gather.2.cloned.1.call-update
  20.7 0.1 copy.25
  20.7 0.1 add.150
  20.8 35.9 %all-gather.2.cloned.1.call-done = bf16[2,4,128,512]{3,2,1,0:T(8,128)(2,1)} async-done(((bf16[1,4,128,512]{3,2,1,0:T(8,128)(2,1)}), bf16[2,4,128,512]{3,2,1,0:T(8,128)(2,1)}) %all-gather.2.cloned.1.call-update) | async-done | bytes 1048592 | tf_op jit(solution)/shard_map/all_gather | solution.py:262
  56.8 3.2 %gather_fusion.1 = bf16[16,128,512]{2,1,0:T(8,128)(2,1)} fusion(bf16[8,128,512]{2,1,0:T(8,128)(2,1)} %bitcast.38, s32[1024]{0:T(1024)S(1)} %pad_clamp_fusion), kind=kCustom, calls=%fused_computation.1 | custom fusion | bytes 4194368 | tf_op jit(solution)/shard_map/gather | solution.py:266
  60.0 6.1 %all-to-all-start.1 = ((bf16[16,128,512]{2,1,0:T(8,128)(2,1)}), bf16[16,128,512]{2,1,0:T(8,128)(2,1)}, u32[]{:S(2)}, u32[]{:S(2)}) async-start(bf16[16,128,512]{2,1,0:T(8,128)(2,1)} %gather_fusion.1), calls=%async_computation.1 | async-start | bytes 4194304 | tf_op jit(solution)/shard_map/all_to_all | solution.py:238
  66.0 0.6 fusion.17.slot_ref
  66.6 3.0 %convolution_convert_fusion.1.q_ref = bf16[768,512]{1,0:T(8,128)(2,1)} fusion(bf16[768,768]{1,0:T(8,128)(2,1)} %param.10, bf16[1,512,768]{2,1,0:T(8,128)(2,1)S(1)} %copy-done.2), kind=kOutput, calls=%fused_computation.4 | convolution fusion | flops 604372992 | bytes 2752512 | tf_op jit(solution)/shard_map/dot_general | solution.py:268
  69.7 2.0 %fusion.2.ng_ref = f32[768,512]{1,0:T(8,128)} fusion(bf16[768,768]{1,0:T(8,128)(2,1)S(1)} %copy-done, bf16[1,512,768]{2,1,0:T(8,128)(2,1)S(1)} %copy-done.11), kind=kOutput, calls=%fused_computation.10 | convolution fusion | flops 603979776 | bytes 3538944 | tf_op jit(solution)/shard_map/dot_general | solution.py:25
  71.7 20.6 %all-to-all-done.1.refs_1_ = bf16[16,128,512]{2,1,0:T(8,128)(2,1)} async-done(((bf16[16,128,512]{2,1,0:T(8,128)(2,1)}), bf16[16,128,512]{2,1,0:T(8,128)(2,1)}, u32[]{:S(2)}, u32[]{:S(2)}) %all-to-all-start.1) | async-done | bytes 2097184 | tf_op jit(solution)/shard_map/all_to_all | solution.py:238
  92.2 17.7 %attention.1 = (bf16[768,512]{1,0:T(8,128)(2,1)}, bf16[768,512]{1,0:T(8,128)(2,1)}, bf16[16,128,512]{2,1,0:T(8,128)(2,1)}, bf16[16,128,512]{2,1,0:T(8,128)(2,1)}) custom-call(s32[16]{0:T(128)} %fusion.17.slot_ref, bf16[768,512]{1,0:T(8,128)(2,1)} %convolution_convert_fusion.1.q_ref, f32[768,512]{1,0:T(8,128)} %fusion.2.ng_ref, ...), custom_call_target="tpu_custom_call" | custom-call | flops 2415919104 | bytes 6291456 | tf_op jit(solution)/shard_map/attention/pallas_call | solution.py:152
  110.0 31.4 %all_to_all.20.parts_ref = bf16[16,128,512]{2,1,0:T(8,128)(2,1)} all-to-all(bf16[16,128,512]{2,1,0:T(8,128)(2,1)} %get-tuple-element.9), channel_id=1, replica_groups={{0,1,2,3,4,5,6,7},{8,9,10,11,12,13,14,15},{16,17,18,19,20,21,22,23},{24..., dimensions={0} | all-to-all | bytes 4194304 | tf_op jit(solution)/shard_map/all_to_all | solution.py:238
  141.4 3.6 %all-to-all-start.2 = ((bf16[16,128,512]{2,1,0:T(8,128)(2,1)}), bf16[16,128,512]{2,1,0:T(8,128)(2,1)S(1)}, u32[]{:S(2)}, u32[]{:S(2)}) async-start(bf16[16,128,512]{2,1,0:T(8,128)(2,1)} %get-tuple-element.8), calls=%async_computation.2 | async-start | bytes 4194304 | tf_op jit(solution)/shard_map/all_to_all | solution.py:238
  145.0 0.1 copy.26
  145.1 0.1 squeeze.30.wanted_ref
  145.1 0.1 copy.27
  145.2 0.1 squeeze.31.wanted_ref
  145.3 1.6 copy-done.1
  146.9 1.8 owner_sum.3
  148.7 30.8 %all-to-all-done.2.parts_ref = bf16[16,128,512]{2,1,0:T(8,128)(2,1)S(1)} async-done(((bf16[16,128,512]{2,1,0:T(8,128)(2,1)}), bf16[16,128,512]{2,1,0:T(8,128)(2,1)S(1)}, u32[]{:S(2)}, u32[]{:S(2)}) %all-to-all-start.2) | async-done | bytes 2097184 | tf_op jit(solution)/shard_map/all_to_all | solution.py:238
  179.5 1.0 owner_sum.2
  180.5 0.1 collective-permute-start.1
  180.6 0.0 copy-done.12
  180.6 1.7 fusion
  182.3 0.2 collective-permute-done.1
  182.5 1.2 add_convert_fusion.1
  183.7 0.4 fusion.7
  184.2 0.4 fusion.9
  184.6 0.8 copy-done.7
  185.4 0.2 copy-done.8
  185.7 1.7 fusion.1
  (37 shorter events, 0.2 us)
Async XLA Ops:
  7.2 62.5 %copy-start = (bf16[768,768]{1,0:T(8,128)(2,1)S(1)}, bf16[768,768]{1,0:T(8,128)(2,1)}, u32[]{:S(2)}) copy-start(bf16[768,768]{1,0:T(8,128)(2,1)} %param.13) | copy-start | bytes 3538948
  7.2 1.8 copy-start.2
  7.2 1.8 copy-start.4
  9.0 1.3 copy-start.9
  9.0 1.5 copy-start.10
  9.7 4.1 %copy-start.3 = (bf16[512,512]{1,0:T(8,128)(2,1)}, bf16[512,512]{1,0:T(8,128)(2,1)S(1)}, u32[]{:S(2)}) copy-start(bf16[512,512]{1,0:T(8,128)(2,1)S(1)} %copy.28) | copy-start | bytes 1572868
  9.7 2.1 %collective-permute-start = (bf16[4,128,512]{2,1,0:T(8,128)(2,1)S(1)}, bf16[4,128,512]{2,1,0:T(8,128)(2,1)S(1)}, u32[]{:S(2)}, u32[]{:S(2)}) collective-permute-start(bf16[4,128,512]{2,1,0:T(8,128)(2,1)S(1)} %bitcast.41), channel_id=1, source_target_pairs={{0,16},{1,17},{2,18},{3,19},{4,20},{5,21},{6,22},{7,23},{8,24},{9,... | collective-permute-start | bytes 1572872 | tf_op jit(solution)/shard_map/ppermute | solution.py:235
  13.8 46.2 %all-to-all-start = ((bf16[16,128,512]{2,1,0:T(8,128)(2,1)}), bf16[16,128,512]{2,1,0:T(8,128)(2,1)}, u32[]{:S(2)}, u32[]{:S(2)}) async-start(bf16[16,128,512]{2,1,0:T(8,128)(2,1)} %gather_fusion), calls=%async_computation | async-start | bytes 4194304 | tf_op jit(solution)/shard_map/all_to_all | solution.py:238
  19.9 36.8 %all-gather.2.cloned.1.call-start = ((), (), s32[]{:S(2)}) async-start(), calls=%async_computation.4 | async-start | bytes 1572864 | tf_op jit(solution)/shard_map/all_gather | solution.py:262
  60.0 32.3 %all-to-all-start.1 = ((bf16[16,128,512]{2,1,0:T(8,128)(2,1)}), bf16[16,128,512]{2,1,0:T(8,128)(2,1)}, u32[]{:S(2)}, u32[]{:S(2)}) async-start(bf16[16,128,512]{2,1,0:T(8,128)(2,1)} %gather_fusion.1), calls=%async_computation.1 | async-start | bytes 4194304 | tf_op jit(solution)/shard_map/all_to_all | solution.py:238
  66.6 3.1 %copy-start.11 = (bf16[1,512,768]{2,1,0:T(8,128)(2,1)S(1)}, bf16[1,512,768]{2,1,0:T(8,128)(2,1)}, u32[]{:S(2)}) copy-start(bf16[1,512,768]{2,1,0:T(8,128)(2,1)} %param.9) | copy-start | bytes 2359300
  141.4 38.1 %all-to-all-start.2 = ((bf16[16,128,512]{2,1,0:T(8,128)(2,1)}), bf16[16,128,512]{2,1,0:T(8,128)(2,1)S(1)}, u32[]{:S(2)}, u32[]{:S(2)}) async-start(bf16[16,128,512]{2,1,0:T(8,128)(2,1)} %get-tuple-element.8), calls=%async_computation.2 | async-start | bytes 4194304 | tf_op jit(solution)/shard_map/all_to_all | solution.py:238
  145.3 1.6 copy-start.1
  148.7 33.6 %collective-permute-start.2 = (bf16[4,128,512]{2,1,0:T(8,128)(2,1)}, bf16[4,128,512]{2,1,0:T(8,128)(2,1)}, u32[]{:S(2)}, u32[]{:S(2)}) collective-permute-start(bf16[4,128,512]{2,1,0:T(8,128)(2,1)} %owner_sum.3), channel_id=1, source_target_pairs={{0,24},{1,25},{2,26},{3,27},{4,28},{5,29},{6,30},{7,31},{8,16},{9,... | collective-permute-start | bytes 1572872 | tf_op jit(solution)/shard_map/ppermute | solution.py:235
  179.5 1.1 copy-start.12
  180.5 2.0 %collective-permute-start.1 = (bf16[4,128,512]{2,1,0:T(8,128)(2,1)S(1)}, bf16[4,128,512]{2,1,0:T(8,128)(2,1)S(1)}, u32[]{:S(2)}, u32[]{:S(2)}) collective-permute-start(bf16[4,128,512]{2,1,0:T(8,128)(2,1)S(1)} %owner_sum.2), channel_id=1, source_target_pairs={{0,16},{1,17},{2,18},{3,19},{4,20},{5,21},{6,22},{7,23},{8,24},{9,... | collective-permute-start | bytes 1572872 | tf_op jit(solution)/shard_map/ppermute | solution.py:235
  182.3 1.4 copy-start.5
  182.3 1.8 copy-start.6
  184.2 1.3 copy-start.7
  184.2 1.5 copy-start.8
Sparse Core Ops, SparseCore 0:
  22.9 33.8 all-gather.1

commit v7 on v6

--- a/solution.py
+++ b/solution.py
@@ -15,10 +15,15 @@
 GROUP = HEADS // KV_HEADS
 KV = KV_HEADS * HEAD_DIM
 PAIR = 2 * HEAD_DIM
+SWAP_FLOPS = 40_000_000_000
 TEMPER = HEAD_DIM ** (-0.5)
 EPSILON = 1e-06
 F32 = jnp.float32
 BF16 = jnp.bfloat16
+
+
+def params(mebibytes):
+    return pltpu.CompilerParams(vmem_limit_bytes=mebibytes * 1024 * 1024)
 
 
 def dot_nt(a, b):
@@ -166,12 +171,85 @@
         ),
         out_shape=[jax.ShapeDtypeStruct((width, rows), BF16)] * 2
         + [jax.ShapeDtypeStruct(arrived[0].shape, BF16)] * 2,
-        compiler_params=pltpu.CompilerParams(vmem_limit_bytes=56 * 1024 * 1024),
+        compiler_params=params(56),
         cost_estimate=pl.CostEstimate(
             flops=12 * pairs * HEAD_DIM, bytes_accessed=16 * rows * width, transcendentals=pairs
         ),
         name="attention",
     )(slots, queries, normed_grad, *arrived)
+
+
+def project_kernel(tokens_ref, wk_ref, wv_ref, out_ref):
+    tokens = tokens_ref[...]
+    for first, weight in ((0, wk_ref), (KV, wv_ref)):
+        out = jnp.dot(tokens, weight[...], preferred_element_type=F32)
+        out_ref[0, :, first : first + KV] = out.astype(BF16)
+
+
+def project(tokens, w_key, w_value):
+    rows, width = tokens.shape
+    weight = pl.BlockSpec((width, KV), lambda r: (0, 0))
+    return pl.pallas_call(
+        project_kernel,
+        grid=(rows // BLK,),
+        in_specs=[pl.BlockSpec((BLK, width), lambda r: (r, 0)), weight, weight],
+        out_specs=pl.BlockSpec((1, BLK, 2 * KV), lambda r: (r, 0, 0)),
+        out_shape=jax.ShapeDtypeStruct((rows // BLK, BLK, 2 * KV), BF16),
+        compiler_params=params(56),
+        name="project",
+    )(tokens, w_key, w_value)
+
+
+def pack_kernel(slots, picked_ref, tile_ref, out_ref, sems):
+    copies = [
+        pltpu.make_async_copy(tile_ref.at[picked_ref[i]], out_ref.at[i], sems.at[i])
+        for i in range(slots)
+    ]
+    for copy in copies:
+        copy.start()
+    for copy in copies:
+        copy.wait()
+
+
+def pack(picked, tile, flops):
+    slots = picked.shape[0]
+    return pl.pallas_call(
+        functools.partial(pack_kernel, slots),
+        in_specs=[
+            pl.BlockSpec(memory_space=pltpu.SMEM),
+            pl.BlockSpec(memory_space=pltpu.VMEM),
+        ],
+        out_specs=pl.BlockSpec(memory_space=pl.ANY),
+        out_shape=jax.ShapeDtypeStruct((slots,) + tile.shape[1:], BF16),
+        scratch_shapes=[pltpu.SemaphoreType.DMA((slots,))],
+        compiler_params=params(56),
+        cost_estimate=pl.CostEstimate(
+            flops=flops, bytes_accessed=2 * slots * tile[0].size, transcendentals=0
+        ),
+        name="pack",
+    )(picked, tile)
+
+
+def finish_kernel(near_ref, far_ref, term_ref, wk_ref, wv_ref, out_ref):
+    grad = (near_ref[0].astype(F32) + far_ref[0].astype(F32)).astype(BF16)
+    total = dot_nt(grad[:, :KV], wk_ref[...]) + dot_nt(grad[:, KV:], wv_ref[...])
+    out_ref[...] = (term_ref[...] + total).astype(BF16)
+
+
+def finish(near, far, term, w_key, w_value):
+    rows, width = term.shape
+    weight = pl.BlockSpec((width, KV), lambda r: (0, 0))
+    part = pl.BlockSpec((1, BLK, 2 * KV), lambda r: (r, 0, 0))
+    row = pl.BlockSpec((BLK, width), lambda r: (r, 0))
+    return pl.pallas_call(
+        finish_kernel,
+        grid=(rows // BLK,),
+        in_specs=[part, part, row, weight, weight],
+        out_specs=row,
+        out_shape=jax.ShapeDtypeStruct((rows, width), BF16),
+        compiler_params=params(32),
+        name="finish",
+    )(near, far, term, w_key, w_value)
 
 
 def owner_kernel(chunk, wanted_ref, parts_ref, out_ref, total):
@@ -206,7 +284,7 @@
             scratch_shapes=[pltpu.VMEM((blocks, BLK, 2 * KV), F32)],
         ),
         out_shape=jax.ShapeDtypeStruct((blocks, BLK, 2 * KV), BF16),
-        compiler_params=pltpu.CompilerParams(vmem_limit_bytes=24 * 1024 * 1024),
+        compiler_params=params(56),
         name="owner_sum",
     )(wanted, returned)
 
@@ -219,9 +297,6 @@
     my_tile = lax.axis_index("tile")
     my_half, my_place = my_tile // half, my_tile % half
     groups = [list(range(half)), list(range(half, tile_count))]
-    swaps = [
-        [v * tile_count + t, (1 - v) * tile_count + t + half] for v in range(2) for t in range(half)
-    ]
     block_count = rows // BLK
     list_len = key_tiles.shape[2]
     entry_count = block_count * list_len
@@ -256,29 +331,29 @@
     wanted = jnp.sum(jnp.where(hits, picks[None, :, :, None] + 1, 0), axis=2) - 1
     wanted = wanted.reshape(2, half * CAP)
 
-    keys = jnp.dot(tokens, w_key, preferred_element_type=F32).astype(BF16)
-    values = jnp.dot(tokens, w_value, preferred_element_type=F32).astype(BF16)
-    mine = jnp.concatenate([keys, values], axis=-1).reshape(block_count, BLK, 2 * KV)
-    both = lax.all_gather(mine, ("vintage", "tile"), axis_index_groups=swaps)
-    both = both.reshape(2 * block_count, BLK, 2 * KV)
     picked = jnp.maximum(wanted, 0)
-    near_send = cross(mine, 0)[picked[0]]
-    far_send = both[picked[1] + (my_half ^ 1) * block_count]
-    arrived = [exchange(near_send), exchange(far_send)]
+    mine = project(tokens, w_key, w_value)
+    far_tile = cross(mine, half)
+    near_tile = cross(mine, 0)
+    arrived = [
+        exchange(pack(picked[0], near_tile, 0)),
+        exchange(pack(picked[1], far_tile, SWAP_FLOPS)),
+    ]
     queries = lax.dot_general(
         w_query, tokens, (((0,), (1,)), ((), ())), preferred_element_type=F32
     ).astype(BF16)
     normed_grad = dot_nt(w_out, out_grad[0])
     normed_low, query_grad, *back = attention(my_slots, queries, normed_grad, arrived, list_len)
-    far = cross(owner_sum(wanted[1], exchange(back[1]), block_count), half)
-    near = cross(owner_sum(wanted[0], exchange(back[0]), block_count), 0)
     layer_out = dot_tn(normed_low, w_out).astype(BF16)
     query_term = lax.dot_general(
         query_grad, w_query, (((0,), (1,)), ((), ())), preferred_element_type=F32
     )
-    kv_grad = (near.astype(F32) + far.astype(F32)).astype(BF16).reshape(rows, 2 * KV)
-    kv_term = dot_nt(kv_grad[:, :KV], w_key) + dot_nt(kv_grad[:, KV:], w_value)
-    input_grad = (query_term + kv_term).astype(BF16)
+    far = cross(owner_sum(wanted[1], exchange(back[1]), block_count), half)
+    near_parts, query_term, layer_out = lax.optimization_barrier(
+        (exchange(back[0]), query_term, layer_out)
+    )
+    near = cross(owner_sum(wanted[0], near_parts, block_count), 0)
+    input_grad = finish(near, far, query_term, w_key, w_value)
     return (layer_out[None], input_grad[None])
 
 

time: 195 us -> 183 us (0.938)
  Pallas kernels: 20.5 us -> 38.8 us
  between operations: 14.3 us -> 0.77 us
  waiting for transfers between devices: 88.5 us -> 80.6 us
  local copies, waits for them, and re-layouts: 9.75 us -> 5.82 us
  matrix products: 11.5 us -> 7.81 us
    all_gather x1 -> x0, waiting for transfers between devices: 35.9 us -> none  [shards(): both = lax.all_gather(mine, ('vintage', 'tile'), axis_index_groups=swaps)]
    all_to_all x3, waiting for transfers between devices: 51.4 us -> 66.2 us  [exchange(): lax.all_to_all(value, 'tile', split_axis=0, concat_axis=0, tiled=True, ax...]
    ppermute x3 -> x4, waiting for transfers between devices: 0.54 us -> 14.4 us  [cross(): return lax.ppermute(value, ('vintage', 'tile'), pairs)]
    pallas_call x0 -> x4, Pallas kernels: none -> 13.1 us  [the longest x2 5.04 us: pack(): pl.pallas_call(functools.partial(pack_kernel, slots), in_specs=[pl.BlockS...]
    gather x2 -> x0, local copies, waits for them, and re-layouts: 5.23 us -> none  [the longest x1 3.21 us: shards(): far_send = both[picked[1] + (my_half ^ 1) * block_count]]
    pallas_call x2, Pallas kernels: 2.83 us -> 7.95 us  [owner_sum(): pl.pallas_call(functools.partial(owner_kernel, chunk), grid_spec=pltpu.Pr...]
    ppermute x3 -> x4, starting transfers between devices: 0.59 us -> 4.16 us  [cross(): return lax.ppermute(value, ('vintage', 'tile'), pairs)]
    dot_general x2 -> x0, matrix products: 2.21 us -> none  [the longest x1 1.8 us: shards(): keys = jnp.dot(tokens, w_key, preferred_element_type=F32).astype(BF16)]
  transfers between devices with their start and end apart: 7 -> 7, of which waited for: 5 -> 5; matrix products, arithmetic and copies ran while one was open for 6% -> 7% of each run, Pallas kernels for 1% -> 7%
where the time goes in v7:
time: 183 us; the launch traced here: 182 us
  waiting for transfers between devices  80.6 us (44%)
  Pallas kernels  38.8 us (21%)
  blocking collectives  30.4 us (17%)
  starting transfers between devices  17.7 us (10%)
  matrix products  7.81 us (4%)
  local copies, waits for them, and re-layouts  5.82 us (3%)
    all_to_all x3, waiting for transfers between devices, exchange(): lax.all_to_all(value, 'tile', split_axis=0, concat_axis=0, tiled=True, ax...  66.2 us
    all_to_all x1, blocking collectives, exchange(): lax.all_to_all(value, 'tile', split_axis=0, concat_axis=0, tiled=True, ax...  30.4 us
    pallas_call x1, Pallas kernels, attention(): pl.pallas_call(functools.partial(attention_kernel, list_len), grid_spec=p...  17.7 us
    ppermute x4, waiting for transfers between devices, cross(): return lax.ppermute(value, ('vintage', 'tile'), pairs)  14.4 us
    all_to_all x3, starting transfers between devices, exchange(): lax.all_to_all(value, 'tile', split_axis=0, concat_axis=0, tiled=True, ax...  13.6 us
    pallas_call x2, Pallas kernels, owner_sum(): pl.pallas_call(functools.partial(owner_kernel, chunk), grid_spec=pltpu.Pr...  7.95 us
    pallas_call x2, Pallas kernels, pack(): pl.pallas_call(functools.partial(pack_kernel, slots), in_specs=[pl.BlockS...  5.04 us
    ppermute x4, starting transfers between devices, cross(): return lax.ppermute(value, ('vintage', 'tile'), pairs)  4.16 us
  transfers between devices with their start and end apart: 7, of which 5 were waited for; matrix products, arithmetic and copies ran while one was open for 7% of the time, Pallas kernels for 7%

profile of v7, /device:TPU:0, one launch (start us, length us, event | category | flops | bytes accessed | tf_op | source)
XLA Modules:
  0.0 182.5 jit_solution(3102438924932245838)
XLA Ops:
  0.6 0.0 copy-start
  0.6 0.0 copy-start.5
  0.7 0.0 copy-start.6
  0.7 4.1 %project.1 = bf16[4,128,512]{2,1,0:T(8,128)(2,1)} custom-call(bf16[512,768]{1,0:T(8,128)(2,1)} %bitcast.21, bf16[768,256]{1,0:T(8,128)(2,1)} %wk_ref.3, bf16[768,256]{1,0:T(8,128)(2,1)} %wv_ref.3), custom_call_target="tpu_custom_call" | custom-call | tf_op jit(solution)/shard_map/project/pallas_call | solution.py:192
  4.8 3.5 %collective-permute-start.1 = (bf16[4,128,512]{2,1,0:T(8,128)(2,1)}, bf16[4,128,512]{2,1,0:T(8,128)(2,1)}, u32[]{:S(2)}, u32[]{:S(2)}) collective-permute-start(bf16[4,128,512]{2,1,0:T(8,128)(2,1)} %project.1), channel_id=1, source_target_pairs={{0,24},{1,25},{2,26},{3,27},{4,28},{5,29},{6,30},{7,31},{8,16},{9,... | collective-permute-start | bytes 1572872 | tf_op jit(solution)/shard_map/ppermute | solution.py:310
  8.3 0.7 collective-permute-start
  9.0 0.1 iota_add_fusion
  9.0 0.0 copy-done.5
  9.0 0.1 copy.14
  9.1 0.1 reshape_squeeze.6
  9.2 0.1 copy.15
  9.3 0.1 reshape_squeeze.7
  9.4 0.3 convert_reduce_fusion
  9.7 0.2 select_reduce_fusion
  9.9 0.1 copy.17
  10.0 0.6 squeeze.32.picked_ref
  10.6 0.1 copy.16
  10.7 0.6 squeeze.31.picked_ref
  11.3 0.0 collective-permute-done.tile_ref
  11.3 0.8 copy-done.4
  12.1 2.5 %pack.2 = bf16[16,128,512]{2,1,0:T(8,128)(2,1)} custom-call(s32[16]{0:T(128)} %squeeze.31.picked_ref, bf16[4,128,512]{2,1,0:T(8,128)(2,1)} %copy-done.4), custom_call_target="tpu_custom_call" | custom-call | bytes 2097152 | tf_op jit(solution)/shard_map/pack/pallas_call | solution.py:216
  14.6 4.7 %all-to-all-start = ((bf16[16,128,512]{2,1,0:T(8,128)(2,1)}), bf16[16,128,512]{2,1,0:T(8,128)(2,1)S(1)}, u32[]{:S(2)}, u32[]{:S(2)}) async-start(bf16[16,128,512]{2,1,0:T(8,128)(2,1)} %pack.2), calls=%async_computation | async-start | bytes 4194304 | tf_op jit(solution)/shard_map/all_to_all | solution.py:313
  19.3 12.3 %collective-permute-done.1.tile_ref = bf16[4,128,512]{2,1,0:T(8,128)(2,1)} collective-permute-done((bf16[4,128,512]{2,1,0:T(8,128)(2,1)}, bf16[4,128,512]{2,1,0:T(8,128)(2,1)}, u32[]{:S(2)}, u32[]{:S(2)}) %collective-permute-start.1) | collective-permute-done | bytes 524320 | tf_op jit(solution)/shard_map/ppermute | solution.py:310
  31.6 2.5 %pack.3 = bf16[16,128,512]{2,1,0:T(8,128)(2,1)} custom-call(s32[16]{0:T(128)} %squeeze.32.picked_ref, bf16[4,128,512]{2,1,0:T(8,128)(2,1)} %collective-permute-done.1.tile_ref), custom_call_target="tpu_custom_call" | custom-call | flops 40000000000 | bytes 2097152 | tf_op jit(solution)/shard_map/pack/pallas_call | solution.py:216
  34.1 19.8 %all-to-all-done.refs_0_ = bf16[16,128,512]{2,1,0:T(8,128)(2,1)S(1)} async-done(((bf16[16,128,512]{2,1,0:T(8,128)(2,1)}), bf16[16,128,512]{2,1,0:T(8,128)(2,1)S(1)}, u32[]{:S(2)}, u32[]{:S(2)}) %all-to-all-start) | async-done | bytes 2097184 | tf_op jit(solution)/shard_map/all_to_all | solution.py:313
  53.9 1.4 copy-done.3
  55.2 4.3 %all-to-all-start.1 = ((bf16[16,128,512]{2,1,0:T(8,128)(2,1)}), bf16[16,128,512]{2,1,0:T(8,128)(2,1)}, u32[]{:S(2)}, u32[]{:S(2)}) async-start(bf16[16,128,512]{2,1,0:T(8,128)(2,1)} %pack.3), calls=%async_computation.1 | async-start | bytes 4194304 | tf_op jit(solution)/shard_map/all_to_all | solution.py:313
  59.6 0.5 fusion.8.slot_ref
  60.1 3.3 %convolution_convert_fusion.1.q_ref = bf16[768,512]{1,0:T(8,128)(2,1)} fusion(bf16[768,768]{1,0:T(8,128)(2,1)} %param.10, bf16[1,512,768]{2,1,0:T(8,128)(2,1)} %param.8), kind=kOutput, calls=%fused_computation.1 | convolution fusion | flops 604372992 | bytes 2752512 | tf_op jit(solution)/shard_map/dot_general | solution.py:342
  63.4 2.0 %fusion.ng_ref = f32[768,512]{1,0:T(8,128)} fusion(bf16[768,768]{1,0:T(8,128)(2,1)S(1)} %copy-done, bf16[1,512,768]{2,1,0:T(8,128)(2,1)S(1)} %copy-done.8), kind=kOutput, calls=%fused_computation.2 | convolution fusion | flops 603979776 | bytes 3538944 | tf_op jit(solution)/shard_map/dot_general | solution.py:30
  65.5 20.2 %all-to-all-done.1.refs_1_ = bf16[16,128,512]{2,1,0:T(8,128)(2,1)} async-done(((bf16[16,128,512]{2,1,0:T(8,128)(2,1)}), bf16[16,128,512]{2,1,0:T(8,128)(2,1)}, u32[]{:S(2)}, u32[]{:S(2)}) %all-to-all-start.1) | async-done | bytes 2097184 | tf_op jit(solution)/shard_map/all_to_all | solution.py:313
  85.7 17.7 %attention.1 = (bf16[768,512]{1,0:T(8,128)(2,1)}, bf16[768,512]{1,0:T(8,128)(2,1)}, bf16[16,128,512]{2,1,0:T(8,128)(2,1)}, bf16[16,128,512]{2,1,0:T(8,128)(2,1)}) custom-call(s32[16]{0:T(128)} %fusion.8.slot_ref, bf16[768,512]{1,0:T(8,128)(2,1)} %convolution_convert_fusion.1.q_ref, f32[768,512]{1,0:T(8,128)} %fusion.ng_ref, bf16[16,128,512]{2,1,0:T(8,128)(2,1)} %copy-done.3, ...), custom_call_target="tpu_custom_call" | custom-call | flops 2415919104 | bytes 6291456 | tf_op jit(solution)/shard_map/attention/pallas_call | solution.py:157
  103.4 30.4 %all_to_all.20.parts_ref = bf16[16,128,512]{2,1,0:T(8,128)(2,1)} all-to-all(bf16[16,128,512]{2,1,0:T(8,128)(2,1)} %get-tuple-element.14), channel_id=1, replica_groups={{0,1,2,3,4,5,6,7},{8,9,10,11,12,13,14,15},{16,17,18,19,20,21,22,23},{24..., dimensions={0} | all-to-all | bytes 4194304 | tf_op jit(solution)/shard_map/all_to_all | solution.py:313
  133.7 4.5 %all-to-all-start.2 = ((bf16[16,128,512]{2,1,0:T(8,128)(2,1)}), bf16[16,128,512]{2,1,0:T(8,128)(2,1)}, u32[]{:S(2)}, u32[]{:S(2)}) async-start(bf16[16,128,512]{2,1,0:T(8,128)(2,1)} %get-tuple-element.9), calls=%async_computation.2 | async-start | bytes 4194304 | tf_op jit(solution)/shard_map/all_to_all | solution.py:313
  138.2 0.1 copy.19
  138.3 0.6 squeeze.34.wanted_ref
  138.9 0.1 copy.18
  139.0 0.7 squeeze.33.wanted_ref
  139.7 1.7 convolution_convert_fusion
  141.4 0.8 fusion.12.term_ref
  142.2 4.0 %owner_sum.3 = bf16[4,128,512]{2,1,0:T(8,128)(2,1)} custom-call(s32[16]{0:T(128)} %squeeze.34.wanted_ref, bf16[16,128,512]{2,1,0:T(8,128)(2,1)} %all_to_all.20.parts_ref), custom_call_target="tpu_custom_call" | custom-call | tf_op jit(solution)/shard_map/owner_sum/pallas_call | solution.py:277
  146.2 0.0 collective-permute-start.3
  146.2 26.2 %all-to-all-done.2.parts_ref = bf16[16,128,512]{2,1,0:T(8,128)(2,1)} async-done(((bf16[16,128,512]{2,1,0:T(8,128)(2,1)}), bf16[16,128,512]{2,1,0:T(8,128)(2,1)}, u32[]{:S(2)}, u32[]{:S(2)}) %all-to-all-start.2) | async-done | bytes 2097184 | tf_op jit(solution)/shard_map/all_to_all | solution.py:313
  172.4 3.9 %owner_sum.2 = bf16[4,128,512]{2,1,0:T(8,128)(2,1)} custom-call(s32[16]{0:T(128)} %squeeze.33.wanted_ref, bf16[16,128,512]{2,1,0:T(8,128)(2,1)} %all-to-all-done.2.parts_ref), custom_call_target="tpu_custom_call" | custom-call | tf_op jit(solution)/shard_map/owner_sum/pallas_call | solution.py:277
  176.4 0.0 collective-permute-start.2
  176.4 0.0 collective-permute-done.3.far_ref
  176.4 2.1 %collective-permute-done.2.near_ref = bf16[4,128,512]{2,1,0:T(8,128)(2,1)S(1)} collective-permute-done((bf16[4,128,512]{2,1,0:T(8,128)(2,1)}, bf16[4,128,512]{2,1,0:T(8,128)(2,1)S(1)}, u32[]{:S(2)}, u32[]{:S(2)}) %collective-permute-start.2) | collective-permute-done | bytes 524320 | tf_op jit(solution)/shard_map/ppermute | solution.py:310
  178.5 4.0 %finish.1 = bf16[512,768]{1,0:T(8,128)(2,1)} custom-call(bf16[4,128,512]{2,1,0:T(8,128)(2,1)S(1)} %collective-permute-done.2.near_ref, bf16[4,128,512]{2,1,0:T(8,128)(2,1)} %collective-permute-done.3.far_ref, f32[512,768]{1,0:T(8,128)S(1)} %fusion.12.term_ref, bf16[768,256]{1,0:T(8,128)(2,1)S(1)} %copy-done.1, bf16[768,256]{1,0:T(8,128)(2,1)S(1)} %copy-done.2), custom_call_target="tpu_custom_call" | custom-call | tf_op jit(solution)/shard_map/finish/pallas_call | solution.py:244
  (23 shorter events, 0.1 us)
Async XLA Ops:
  0.6 62.8 %copy-start = (bf16[768,768]{1,0:T(8,128)(2,1)S(1)}, bf16[768,768]{1,0:T(8,128)(2,1)}, u32[]{:S(2)}) copy-start(bf16[768,768]{1,0:T(8,128)(2,1)} %param.13) | copy-start | bytes 3538948
  0.6 8.4 %copy-start.5 = (s32[1,64,4]{1,2,0:T(4,128)S(1)}, s32[1,64,4]{1,2,0:T(4,128)}, u32[]{:S(2)}) copy-start(s32[1,64,4]{1,2,0:T(4,128)} %param.14) | copy-start | bytes 3076
  0.7 8.5 %copy-start.6 = (s32[1,64,4]{1,2,0:T(4,128)S(1)}, s32[1,64,4]{1,2,0:T(4,128)}, u32[]{:S(2)}) copy-start(s32[1,64,4]{1,2,0:T(4,128)} %param.15) | copy-start | bytes 3076
  4.8 26.8 %collective-permute-start.1 = (bf16[4,128,512]{2,1,0:T(8,128)(2,1)}, bf16[4,128,512]{2,1,0:T(8,128)(2,1)}, u32[]{:S(2)}, u32[]{:S(2)}) collective-permute-start(bf16[4,128,512]{2,1,0:T(8,128)(2,1)} %project.1), channel_id=1, source_target_pairs={{0,24},{1,25},{2,26},{3,27},{4,28},{5,29},{6,30},{7,31},{8,16},{9,... | collective-permute-start | bytes 1572872 | tf_op jit(solution)/shard_map/ppermute | solution.py:310
  8.3 3.0 %collective-permute-start = (bf16[4,128,512]{2,1,0:T(8,128)(2,1)}, bf16[4,128,512]{2,1,0:T(8,128)(2,1)S(1)}, u32[]{:S(2)}, u32[]{:S(2)}) collective-permute-start(bf16[4,128,512]{2,1,0:T(8,128)(2,1)} %project.1), channel_id=1, source_target_pairs={{0,16},{1,17},{2,18},{3,19},{4,20},{5,21},{6,22},{7,23},{8,24},{9,... | collective-permute-start | bytes 1572872 | tf_op jit(solution)/shard_map/ppermute | solution.py:310
  11.3 0.8 copy-start.4
  14.6 39.3 %all-to-all-start = ((bf16[16,128,512]{2,1,0:T(8,128)(2,1)}), bf16[16,128,512]{2,1,0:T(8,128)(2,1)S(1)}, u32[]{:S(2)}, u32[]{:S(2)}) async-start(bf16[16,128,512]{2,1,0:T(8,128)(2,1)} %pack.2), calls=%async_computation | async-start | bytes 4194304 | tf_op jit(solution)/shard_map/all_to_all | solution.py:313
  53.9 1.4 copy-start.3
  55.2 30.4 %all-to-all-start.1 = ((bf16[16,128,512]{2,1,0:T(8,128)(2,1)}), bf16[16,128,512]{2,1,0:T(8,128)(2,1)}, u32[]{:S(2)}, u32[]{:S(2)}) async-start(bf16[16,128,512]{2,1,0:T(8,128)(2,1)} %pack.3), calls=%async_computation.1 | async-start | bytes 4194304 | tf_op jit(solution)/shard_map/all_to_all | solution.py:313
  60.1 3.3 %copy-start.8 = (bf16[1,512,768]{2,1,0:T(8,128)(2,1)S(1)}, bf16[1,512,768]{2,1,0:T(8,128)(2,1)}, u32[]{:S(2)}) copy-start(bf16[1,512,768]{2,1,0:T(8,128)(2,1)} %param.9) | copy-start | bytes 2359300
  133.7 5.9 %copy-start.10 = (bf16[768,512]{1,0:T(8,128)(2,1)S(1)}, bf16[768,512]{1,0:T(8,128)(2,1)}, u32[]{:S(2)}) copy-start(bf16[768,512]{1,0:T(8,128)(2,1)} %get-tuple-element.11) | copy-start | bytes 2359300
  133.7 38.7 %all-to-all-start.2 = ((bf16[16,128,512]{2,1,0:T(8,128)(2,1)}), bf16[16,128,512]{2,1,0:T(8,128)(2,1)}, u32[]{:S(2)}, u32[]{:S(2)}) async-start(bf16[16,128,512]{2,1,0:T(8,128)(2,1)} %get-tuple-element.9), calls=%async_computation.2 | async-start | bytes 4194304 | tf_op jit(solution)/shard_map/all_to_all | solution.py:313
  139.7 1.7 copy-start.7
  139.7 1.7 copy-start.9
  146.2 32.3 %copy-start.1 = (bf16[768,256]{1,0:T(8,128)(2,1)S(1)}, bf16[768,256]{1,0:T(8,128)(2,1)}, u32[]{:S(2)}) copy-start(bf16[768,256]{1,0:T(8,128)(2,1)} %wk_ref.3) | copy-start | bytes 1179652
  146.2 32.3 %copy-start.2 = (bf16[768,256]{1,0:T(8,128)(2,1)S(1)}, bf16[768,256]{1,0:T(8,128)(2,1)}, u32[]{:S(2)}) copy-start(bf16[768,256]{1,0:T(8,128)(2,1)} %wv_ref.3) | copy-start | bytes 1179652
  146.2 30.2 %collective-permute-start.3 = (bf16[4,128,512]{2,1,0:T(8,128)(2,1)}, bf16[4,128,512]{2,1,0:T(8,128)(2,1)}, u32[]{:S(2)}, u32[]{:S(2)}) collective-permute-start(bf16[4,128,512]{2,1,0:T(8,128)(2,1)} %owner_sum.3), channel_id=1, source_target_pairs={{0,24},{1,25},{2,26},{3,27},{4,28},{5,29},{6,30},{7,31},{8,16},{9,... | collective-permute-start | bytes 1572872 | tf_op jit(solution)/shard_map/ppermute | solution.py:310
  176.4 2.1 %collective-permute-start.2 = (bf16[4,128,512]{2,1,0:T(8,128)(2,1)}, bf16[4,128,512]{2,1,0:T(8,128)(2,1)S(1)}, u32[]{:S(2)}, u32[]{:S(2)}) collective-permute-start(bf16[4,128,512]{2,1,0:T(8,128)(2,1)} %owner_sum.2), channel_id=1, source_target_pairs={{0,16},{1,17},{2,18},{3,19},{4,20},{5,21},{6,22},{7,23},{8,24},{9,... | collective-permute-start | bytes 1572872 | tf_op jit(solution)/shard_map/ppermute | solution.py:310

commit v8 on v7

--- a/solution.py
+++ b/solution.py
@@ -18,6 +18,7 @@
 SWAP_FLOPS = 40_000_000_000
 TEMPER = HEAD_DIM ** (-0.5)
 EPSILON = 1e-06
+WHOLE = pl.BlockSpec(memory_space=pltpu.VMEM)
 F32 = jnp.float32
 BF16 = jnp.bfloat16
 
@@ -59,33 +60,43 @@
 
 
 def attention_kernel(list_len, slot_ref, q_ref, ng_ref, *refs):
-    arrived, (normed_ref, qg_ref) = refs[:2], refs[2:4]
-    back, (expo_scr, kv_scr, parts_scr, in_sems, out_sems) = refs[4:6], refs[6:]
+    expo_scr, kv_scr, parts_scr, in_sems, out_sems = refs[-5:]
+    sources = (len(refs) - 7) // 2
+    arrived, (normed_ref, qg_ref) = refs[:sources], refs[sources : sources + 2]
+    back = refs[sources + 2 : 2 * sources + 2]
     step = pl.program_id(0)
     entries = in_sems.shape[0]
-    per_part = arrived[0].shape[0]
 
     def rows_of(e):
         return pl.ds(pl.multiple_of(e * BLK, BLK), BLK)
 
-    def fetch(e, part, slot):
-        return pltpu.make_async_copy(arrived[part].at[slot], kv_scr.at[rows_of(e)], in_sems.at[e])
-
-    def give(e, part, slot):
-        return pltpu.make_async_copy(parts_scr.at[rows_of(e)], back[part].at[slot], out_sems.at[e])
-
-    def start(copy, e):
-        slot = slot_ref[e]
-        for part in range(2):
-
-            @pl.when(slot // per_part == part)
-            def _():
-                copy(e, part, slot % per_part).start()
+    def fetch(e, source, slot):
+        return pltpu.make_async_copy(
+            arrived[source].at[slot], kv_scr.at[rows_of(e)], in_sems.at[e]
+        )
+
+    def give(e, source, slot):
+        return pltpu.make_async_copy(
+            parts_scr.at[rows_of(e)], back[source].at[slot], out_sems.at[e]
+        )
+
+    def start(copy, begin, count):
+        def one(i, carry):
+            e = begin + i
+            slot = slot_ref[e]
+            for source in range(sources):
+
+                @pl.when(slot // CAP == source)
+                def _():
+                    copy(e, source, slot % CAP).start()
+
+            return carry
+
+        lax.fori_loop(0, count, one, 0)
 
     @pl.when(step == 0)
     def _():
-        for e in range(entries):
-            start(fetch, e)
+        start(fetch, 0, entries)
 
     first = step * list_len
     for l in range(list_len):
@@ -137,8 +148,7 @@
         key_part = dot_nt(score_grad, wide[j])
         parts_scr[here, j * PAIR : (j + 1) * PAIR] = key_part.astype(BF16)
         parts_scr[here, KV + j * PAIR : KV + (j + 1) * PAIR] = value_part.astype(BF16)
-    for l in range(list_len):
-        start(give, first + l)
+    start(give, first, list_len)
 
     @pl.when(step == pl.num_programs(0) - 1)
     def _():
@@ -159,8 +169,8 @@
         grid_spec=pltpu.PrefetchScalarGridSpec(
             num_scalar_prefetch=1,
             grid=(blocks,),
-            in_specs=[row_spec, row_spec, anywhere, anywhere],
-            out_specs=[row_spec, row_spec, anywhere, anywhere],
+            in_specs=[row_spec, row_spec] + [anywhere] * len(arrived),
+            out_specs=[row_spec, row_spec] + [anywhere] * len(arrived),
             scratch_shapes=[
                 pltpu.VMEM((KV // PAIR, keys, 2 * GROUP * BLK), BF16),
                 pltpu.VMEM((entries * BLK, 2 * KV), BF16),
@@ -170,7 +180,7 @@
             ],
         ),
         out_shape=[jax.ShapeDtypeStruct((width, rows), BF16)] * 2
-        + [jax.ShapeDtypeStruct(arrived[0].shape, BF16)] * 2,
+        + [jax.ShapeDtypeStruct(arrived[0].shape, BF16)] * len(arrived),
         compiler_params=params(56),
         cost_estimate=pl.CostEstimate(
             flops=12 * pairs * HEAD_DIM, bytes_accessed=16 * rows * width, transcendentals=pairs
@@ -183,27 +193,28 @@
     tokens = tokens_ref[...]
     for first, weight in ((0, wk_ref), (KV, wv_ref)):
         out = jnp.dot(tokens, weight[...], preferred_element_type=F32)
-        out_ref[0, :, first : first + KV] = out.astype(BF16)
+        out_ref[:, first : first + KV] = out.astype(BF16)
 
 
 def project(tokens, w_key, w_value):
-    rows, width = tokens.shape
-    weight = pl.BlockSpec((width, KV), lambda r: (0, 0))
     return pl.pallas_call(
         project_kernel,
-        grid=(rows // BLK,),
-        in_specs=[pl.BlockSpec((BLK, width), lambda r: (r, 0)), weight, weight],
-        out_specs=pl.BlockSpec((1, BLK, 2 * KV), lambda r: (r, 0, 0)),
-        out_shape=jax.ShapeDtypeStruct((rows // BLK, BLK, 2 * KV), BF16),
-        compiler_params=params(56),
+        in_specs=[WHOLE] * 3,
+        out_specs=WHOLE,
+        out_shape=jax.ShapeDtypeStruct((tokens.shape[0], 2 * KV), BF16),
+        compiler_params=params(16),
         name="project",
     )(tokens, w_key, w_value)
 
 
-def pack_kernel(slots, picked_ref, tile_ref, out_ref, sems):
+def pack_kernel(peers, picked_ref, tile_ref, *refs):
+    outs, sems = refs[:peers], refs[peers]
     copies = [
-        pltpu.make_async_copy(tile_ref.at[picked_ref[i]], out_ref.at[i], sems.at[i])
-        for i in range(slots)
+        pltpu.make_async_copy(
+            tile_ref.at[picked_ref[p * CAP + s]], outs[p].at[s], sems.at[p * CAP + s]
+        )
+        for p in range(peers)
+        for s in range(CAP)
     ]
     for copy in copies:
         copy.start()
@@ -212,81 +223,64 @@
 
 
 def pack(picked, tile, flops):
-    slots = picked.shape[0]
-    return pl.pallas_call(
-        functools.partial(pack_kernel, slots),
-        in_specs=[
-            pl.BlockSpec(memory_space=pltpu.SMEM),
-            pl.BlockSpec(memory_space=pltpu.VMEM),
-        ],
-        out_specs=pl.BlockSpec(memory_space=pl.ANY),
-        out_shape=jax.ShapeDtypeStruct((slots,) + tile.shape[1:], BF16),
-        scratch_shapes=[pltpu.SemaphoreType.DMA((slots,))],
-        compiler_params=params(56),
+    peers = picked.shape[0] // CAP
+    shape = (CAP,) + tile.shape[1:]
+    return pl.pallas_call(
+        functools.partial(pack_kernel, peers),
+        in_specs=[pl.BlockSpec(memory_space=pltpu.SMEM), WHOLE],
+        out_specs=[pl.BlockSpec(memory_space=pl.ANY)] * peers,
+        out_shape=[jax.ShapeDtypeStruct(shape, BF16)] * peers,
+        scratch_shapes=[pltpu.SemaphoreType.DMA((peers * CAP,))],
+        compiler_params=params(16),
         cost_estimate=pl.CostEstimate(
-            flops=flops, bytes_accessed=2 * slots * tile[0].size, transcendentals=0
+            flops=flops, bytes_accessed=2 * peers * CAP * tile[0].size, transcendentals=0
         ),
         name="pack",
     )(picked, tile)
 
 
 def finish_kernel(near_ref, far_ref, term_ref, wk_ref, wv_ref, out_ref):
-    grad = (near_ref[0].astype(F32) + far_ref[0].astype(F32)).astype(BF16)
+    grad = (near_ref[...].astype(F32) + far_ref[...].astype(F32)).astype(BF16)
     total = dot_nt(grad[:, :KV], wk_ref[...]) + dot_nt(grad[:, KV:], wv_ref[...])
     out_ref[...] = (term_ref[...] + total).astype(BF16)
 
 
 def finish(near, far, term, w_key, w_value):
-    rows, width = term.shape
-    weight = pl.BlockSpec((width, KV), lambda r: (0, 0))
-    part = pl.BlockSpec((1, BLK, 2 * KV), lambda r: (r, 0, 0))
-    row = pl.BlockSpec((BLK, width), lambda r: (r, 0))
     return pl.pallas_call(
         finish_kernel,
-        grid=(rows // BLK,),
-        in_specs=[part, part, row, weight, weight],
-        out_specs=row,
-        out_shape=jax.ShapeDtypeStruct((rows, width), BF16),
-        compiler_params=params(32),
+        in_specs=[WHOLE] * 5,
+        out_specs=WHOLE,
+        out_shape=jax.ShapeDtypeStruct(term.shape, BF16),
+        compiler_params=params(24),
         name="finish",
     )(near, far, term, w_key, w_value)
 
 
-def owner_kernel(chunk, wanted_ref, parts_ref, out_ref, total):
-    step = pl.program_id(0)
-
-    @pl.when(step == 0)
-    def _():
-        total[...] = jnp.zeros_like(total)
-
-    for s in range(chunk):
-        block = wanted_ref[step * chunk + s]
-
-        @pl.when(block >= 0)
-        def _():
-            total[block] += parts_ref[s].astype(F32)
-
-    @pl.when(step == pl.num_programs(0) - 1)
-    def _():
-        out_ref[...] = total[...].astype(BF16)
-
-
-def owner_sum(wanted, returned, blocks):
-    slots = returned.shape[0]
-    chunk = 4
-    return pl.pallas_call(
-        functools.partial(owner_kernel, chunk),
-        grid_spec=pltpu.PrefetchScalarGridSpec(
-            num_scalar_prefetch=1,
-            grid=(slots // chunk,),
-            in_specs=[pl.BlockSpec((chunk, BLK, 2 * KV), lambda s, w: (s, 0, 0))],
-            out_specs=pl.BlockSpec((blocks, BLK, 2 * KV), lambda s, w: (0, 0, 0)),
-            scratch_shapes=[pltpu.VMEM((blocks, BLK, 2 * KV), F32)],
-        ),
-        out_shape=jax.ShapeDtypeStruct((blocks, BLK, 2 * KV), BF16),
-        compiler_params=params(56),
+def owner_kernel(wanted_ref, *refs):
+    parts, (out_ref, total) = refs[:-2], refs[-2:]
+    total[...] = jnp.zeros_like(total)
+    for p, part in enumerate(parts):
+        for s in range(CAP):
+            block = wanted_ref[p * CAP + s]
+
+            @pl.when(block >= 0)
+            def _():
+                total[block] += part[s].astype(F32)
+
+    out_ref[...] = total[...].astype(BF16)
+
+
+def owner_sum(wanted, parts, blocks):
+    shape = (blocks,) + parts[0].shape[1:]
+    return pl.pallas_call(
+        owner_kernel,
+        in_specs=[pl.BlockSpec(memory_space=pltpu.SMEM)] + [WHOLE] * len(parts),
+        out_specs=WHOLE,
+        out_shape=jax.ShapeDtypeStruct(shape, BF16),
+        scratch_shapes=[pltpu.VMEM(shape, F32)],
+        compiler_params=params(16),
         name="owner_sum",
-    )(wanted, returned)
+    )(wanted, *parts)
 
 
 def shards(patches, out_grad, w_query, w_key, w_value, w_out, key_tiles, key_blocks):
@@ -296,7 +290,6 @@
     half = tile_count // 2
     my_tile = lax.axis_index("tile")
     my_half, my_place = my_tile // half, my_tile % half
-    groups = [list(range(half)), list(range(half, tile_count))]
     block_count = rows // BLK
     list_len = key_tiles.shape[2]
     entry_count = block_count * list_len
@@ -309,10 +302,12 @@
         ]
         return lax.ppermute(value, ("vintage", "tile"), pairs)
 
-    def exchange(value):
-        return lax.all_to_all(
-            value, "tile", split_axis=0, concat_axis=0, tiled=True, axis_index_groups=groups
-        )
+    def exchange(values):
+        moved = [values[0]]
+        for p in range(1, half):
+            pairs = [(t, t // half * half + (t % half ^ p)) for t in range(tile_count)]
+            moved.append(lax.ppermute(values[p], "tile", pairs))
+        return moved
 
     def half_rows(table):
         table = table[0].reshape(2, half, entry_count)
@@ -323,8 +318,13 @@
     same = (tiles[:, :, None] == tiles[:, None, :]) & earlier[None]
     ranks = jnp.sum(same.astype(jnp.int32), axis=2)
     is_far = (tiles // half != my_half).astype(jnp.int32)
+    holders = (tiles % half) ^ my_place
+    my_slots = lax.dynamic_index_in_dim(
+        (is_far * half + holders) * CAP + ranks, my_place, 0, keepdims=False
+    )
     slots = (is_far * half + tiles % half) * CAP + ranks
-    my_slots = lax.dynamic_index_in_dim(slots, my_place, 0, keepdims=False)
+    slots = slots[jnp.arange(half) ^ my_place]
+    picks = picks[jnp.arange(half) ^ my_place]
     part_ids = jnp.arange(2, dtype=jnp.int32)[:, None, None] * half + my_place
     ids = part_ids * CAP + jnp.arange(CAP, dtype=jnp.int32)[None, None, :]
     hits = slots[None, :, :, None] == ids[:, :, None, :]
@@ -332,13 +332,12 @@
     wanted = wanted.reshape(2, half * CAP)
 
     picked = jnp.maximum(wanted, 0)
-    mine = project(tokens, w_key, w_value)
+    mine = project(tokens, w_key, w_value).reshape(block_count, BLK, 2 * KV)
     far_tile = cross(mine, half)
     near_tile = cross(mine, 0)
-    arrived = [
-        exchange(pack(picked[0], near_tile, 0)),
-        exchange(pack(picked[1], far_tile, SWAP_FLOPS)),
-    ]
+    arrived = exchange(pack(picked[0], near_tile, 0)) + exchange(
+        pack(picked[1], far_tile, SWAP_FLOPS)
+    )
     queries = lax.dot_general(
         w_query, tokens, (((0,), (1,)), ((), ())), preferred_element_type=F32
     ).astype(BF16)
@@ -348,12 +347,14 @@
     query_term = lax.dot_general(
         query_grad, w_query, (((0,), (1,)), ((), ())), preferred_element_type=F32
     )
-    far = cross(owner_sum(wanted[1], exchange(back[1]), block_count), half)
+    far = cross(owner_sum(wanted[1], exchange(back[half:]), block_count), half)
     near_parts, query_term, layer_out = lax.optimization_barrier(
-        (exchange(back[0]), query_term, layer_out)
+        (exchange(back[:half]), query_term, layer_out)
     )
     near = cross(owner_sum(wanted[0], near_parts, block_count), 0)
-    input_grad = finish(near, far, query_term, w_key, w_value)
+    input_grad = finish(
+        near.reshape(rows, 2 * KV), far.reshape(rows, 2 * KV), query_term, w_key, w_value
+    )
     return (layer_out[None], input_grad[None])
 
 

time: 183 us -> 169 us (0.923)
  blocking collectives: 30.4 us -> 0 us
  starting transfers between devices: 17.7 us -> 44.3 us
  Pallas kernels: 38.8 us -> 29.3 us
  waiting for transfers between devices: 80.6 us -> 77.4 us
    all_to_all x3 -> x0, waiting for transfers between devices: 66.2 us -> none  [exchange(): lax.all_to_all(value, 'tile', split_axis=0, concat_axis=0, tiled=True, ax...]
    ppermute x0 -> x28, waiting for transfers between devices: none -> 63.7 us  [exchange(): moved.append(lax.ppermute(values[p], 'tile', pairs))]
    ppermute x0 -> x28, starting transfers between devices: none -> 40 us  [exchange(): moved.append(lax.ppermute(values[p], 'tile', pairs))]
    all_to_all x1 -> x0, blocking collectives: 30.4 us -> none  [exchange(): lax.all_to_all(value, 'tile', split_axis=0, concat_axis=0, tiled=True, ax...]
    all_to_all x3 -> x0, starting transfers between devices: 13.6 us -> none  [exchange(): lax.all_to_all(value, 'tile', split_axis=0, concat_axis=0, tiled=True, ax...]
    pallas_call x6, Pallas kernels: 21.1 us -> 11.2 us  [the longest x2 7.27 us: pack(): pl.pallas_call(functools.partial(pack_kernel, peers), in_specs=[pl.BlockS...]
    unnamed x24 -> x74, local copies, waits for them, and re-layouts: 2.38 us -> 4.22 us
  transfers between devices with their start and end apart: 7 -> 32, of which waited for: 5 -> 15; matrix products, arithmetic and copies ran while one was open for 7% -> 6% of each run, Pallas kernels for 7% -> 5%
where the time goes in v8:
time: 169 us; the launch traced here: 167 us
  waiting for transfers between devices  77.4 us (46%)
  starting transfers between devices  44.3 us (26%)
  Pallas kernels  29.3 us (17%)
  matrix products  7.51 us (4%)
  local copies, waits for them, and re-layouts  6.66 us (4%)
    ppermute x28, waiting for transfers between devices, exchange(): moved.append(lax.ppermute(values[p], 'tile', pairs))  63.7 us
    ppermute x28, starting transfers between devices, exchange(): moved.append(lax.ppermute(values[p], 'tile', pairs))  40 us
    pallas_call x1, Pallas kernels, attention(): pl.pallas_call(functools.partial(attention_kernel, list_len), grid_spec=p...  18.1 us
    ppermute x4, waiting for transfers between devices, cross(): return lax.ppermute(value, ('vintage', 'tile'), pairs)  13.8 us
    pallas_call x2, Pallas kernels, pack(): pl.pallas_call(functools.partial(pack_kernel, peers), in_specs=[pl.BlockS...  7.27 us
    ppermute x4, starting transfers between devices, cross(): return lax.ppermute(value, ('vintage', 'tile'), pairs)  4.29 us
    unnamed x74, local copies, waits for them, and re-layouts  4.22 us
  transfers between devices with their start and end apart: 32, of which 15 were waited for; matrix products, arithmetic and copies ran while one was open for 6% of the time, Pallas kernels for 5%

profile of v8, /device:TPU:0, one launch (start us, length us, event | category | flops | bytes accessed | tf_op | source)
XLA Modules:
  0.0 166.8 jit_solution(5519625160819010156)
XLA Ops:
  0.7 1.1 copy-done.1
  1.7 1.0 copy-done.3
  2.7 1.1 copy-done.5
  4.5 3.5 %collective-permute-start.8 = (bf16[4,128,512]{2,1,0:T(8,128)(2,1)S(1)}, bf16[4,128,512]{2,1,0:T(8,128)(2,1)S(1)}, u32[]{:S(2)}, u32[]{:S(2)}) collective-permute-start(bf16[4,128,512]{2,1,0:T(8,128)(2,1)S(1)} %bitcast.26), channel_id=1, source_target_pairs={{0,24},{1,25},{2,26},{3,27},{4,28},{5,29},{6,30},{7,31},{8,16},{9,... | collective-permute-start | bytes 1572872 | tf_op jit(solution)/shard_map/ppermute | solution.py:303
  11.7 3.6 %pack.2 = (bf16[2,128,512]{2,1,0:T(8,128)(2,1)S(1)}, bf16[2,128,512]{2,1,0:T(8,128)(2,1)S(1)}, bf16[2,128,512]{2,1,0:T(8,128)(2,1)S(1)}, bf16[2,128,512]{2,1,0:T...) custom-call(s32[16]{0:T(128)S(1)} %squeeze.34.picked_ref, ...), custom_call_target="tpu_custom_call" | custom-call | bytes 2097152 | tf_op jit(solution)/shard_map/pack/pallas_call | solution.py:228
  15.3 1.6 collective-permute-start.1
  16.9 1.5 collective-permute-start.2
  18.9 1.6 collective-permute-start.4
  20.5 10.5 %collective-permute-done.8.tile_ref = bf16[4,128,512]{2,1,0:T(8,128)(2,1)S(1)} collective-permute-done((bf16[4,128,512]{2,1,0:T(8,128)(2,1)S(1)}, bf16[4,128,512]{2,1,0:T(8,128)(2,1)S(1)}, u32[]{:S(2)}, u32[]{:S(2)}) %collective-permute-start.8) | collective-permute-done | bytes 524320 | tf_op jit(solution)/shard_map/ppermute | solution.py:303
  31.0 3.0 %collective-permute-start.5 = (bf16[2,128,512]{2,1,0:T(8,128)(2,1)S(1)}, bf16[2,128,512]{2,1,0:T(8,128)(2,1)S(1)}, u32[]{:S(2)}, u32[]{:S(2)}) collective-permute-start(bf16[2,128,512]{2,1,0:T(8,128)(2,1)S(1)} %get-tuple-element.51), channel_id=1, source_target_pairs={{0,5},{1,4},{2,7},{3,6},{4,1},{5,0},{6,3},{7,2},{8,13},{9,12},{10,... | collective-permute-start | bytes 786440 | tf_op jit(solution)/shard_map/ppermute | solution.py:309
  34.0 3.6 %pack.3 = (bf16[2,128,512]{2,1,0:T(8,128)(2,1)S(1)}, bf16[2,128,512]{2,1,0:T(8,128)(2,1)S(1)}, bf16[2,128,512]{2,1,0:T(8,128)(2,1)S(1)}, bf16[2,128,512]{2,1,0:T...) custom-call(s32[16]{0:T(128)S(1)} %squeeze.35.picked_ref, ...), custom_call_target="tpu_custom_call" | custom-call | flops 40000000000 | bytes 2097152 | tf_op jit(solution)/shard_map/pack/pallas_call | solution.py:228
  37.7 2.2 %collective-permute-start.6 = (bf16[2,128,512]{2,1,0:T(8,128)(2,1)S(1)}, bf16[2,128,512]{2,1,0:T(8,128)(2,1)S(1)}, u32[]{:S(2)}, u32[]{:S(2)}) collective-permute-start(bf16[2,128,512]{2,1,0:T(8,128)(2,1)S(1)} %get-tuple-element.52), channel_id=1, source_target_pairs={{0,6},{1,7},{2,4},{3,5},{4,2},{5,3},{6,0},{7,1},{8,14},{9,15},{10,... | collective-permute-start | bytes 786440 | tf_op jit(solution)/shard_map/ppermute | solution.py:309
  39.9 0.8 collective-permute-start.7
  40.6 1.5 collective-permute-start.9
  42.1 1.5 collective-permute-start.10
  43.6 2.0 %fusion.ng_ref = f32[768,512]{1,0:T(8,128)} fusion(bf16[768,768]{1,0:T(8,128)(2,1)S(1)} %copy-done.13, bf16[1,512,768]{2,1,0:T(8,128)(2,1)S(1)} %copy-done.15), kind=kOutput, calls=%fused_computation.4 | convolution fusion | flops 603979776 | bytes 3538944 | tf_op jit(solution)/shard_map/dot_general | solution.py:31
  46.2 3.0 %collective-permute-done.6.refs_6_ = bf16[2,128,512]{2,1,0:T(8,128)(2,1)S(1)} collective-permute-done((bf16[2,128,512]{2,1,0:T(8,128)(2,1)S(1)}, bf16[2,128,512]{2,1,0:T(8,128)(2,1)S(1)}, u32[]{:S(2)}, u32[]{:S(2)}) %collective-permute-start.6) | collective-permute-done | bytes 262176 | tf_op jit(solution)/shard_map/ppermute | solution.py:309
  49.2 0.7 collective-permute-start.12
  49.9 6.8 %collective-permute-done.7.refs_7_ = bf16[2,128,512]{2,1,0:T(8,128)(2,1)S(1)} collective-permute-done((bf16[2,128,512]{2,1,0:T(8,128)(2,1)S(1)}, bf16[2,128,512]{2,1,0:T(8,128)(2,1)S(1)}, u32[]{:S(2)}, u32[]{:S(2)}) %collective-permute-start.7) | collective-permute-done | bytes 262176 | tf_op jit(solution)/shard_map/ppermute | solution.py:309
  56.7 1.7 collective-permute-start.14
  58.4 6.7 %collective-permute-done.10.refs_10_ = bf16[2,128,512]{2,1,0:T(8,128)(2,1)S(1)} collective-permute-done((bf16[2,128,512]{2,1,0:T(8,128)(2,1)S(1)}, bf16[2,128,512]{2,1,0:T(8,128)(2,1)S(1)}, u32[]{:S(2)}, u32[]{:S(2)}) %collective-permute-start.10) | collective-permute-done | bytes 262176 | tf_op jit(solution)/shard_map/ppermute | solution.py:309
  65.1 1.7 %convolution_convert_fusion.1.q_ref = bf16[768,512]{1,0:T(8,128)(2,1)} fusion(bf16[768,768]{1,0:T(8,128)(2,1)S(1)} %copy-done, bf16[1,512,768]{2,1,0:T(8,128)(2,1)S(1)} %copy-done.6), kind=kOutput, calls=%fused_computation.3 | convolution fusion | flops 604372992 | bytes 2752512 | tf_op jit(solution)/shard_map/dot_general | solution.py:341
  67.2 5.6 %collective-permute-done.14.refs_14_ = bf16[2,128,512]{2,1,0:T(8,128)(2,1)S(1)} collective-permute-done((bf16[2,128,512]{2,1,0:T(8,128)(2,1)S(1)}, bf16[2,128,512]{2,1,0:T(8,128)(2,1)S(1)}, u32[]{:S(2)}, u32[]{:S(2)}) %collective-permute-start.14) | collective-permute-done | bytes 262176 | tf_op jit(solution)/shard_map/ppermute | solution.py:309
  72.8 5.0 %collective-permute-done.15.refs_15_ = bf16[2,128,512]{2,1,0:T(8,128)(2,1)S(1)} collective-permute-done((bf16[2,128,512]{2,1,0:T(8,128)(2,1)S(1)}, bf16[2,128,512]{2,1,0:T(8,128)(2,1)S(1)}, u32[]{:S(2)}, u32[]{:S(2)}) %collective-permute-start.15) | collective-permute-done | bytes 262176 | tf_op jit(solution)/shard_map/ppermute | solution.py:309
  78.4 18.1 %attention.1 = (bf16[768,512]{1,0:T(8,128)(2,1)}, bf16[768,512]{1,0:T(8,128)(2,1)}, bf16[2,128,512]{2,1,0:T(8,128)(2,1)}, bf16[2,128,512]{2,1,0:T(8,128)(2,1)}, ...) custom-call(s32[16]{0:T(128)} %fusion.9.slot_ref, ...), custom_call_target="tpu_custom_call" | custom-call | flops 2415919104 | bytes 6291456 | tf_op jit(solution)/shard_map/attention/pallas_call | solution.py:167
  96.5 1.4 collective-permute-start.16
  98.3 0.8 collective-permute-start.24
  99.1 1.5 collective-permute-start.25
  101.0 1.1 collective-permute-start.26
  102.1 3.9 %collective-permute-done.16.refs_1_ = bf16[2,128,512]{2,1,0:T(8,128)(2,1)S(1)} collective-permute-done((bf16[2,128,512]{2,1,0:T(8,128)(2,1)}, bf16[2,128,512]{2,1,0:T(8,128)(2,1)S(1)}, u32[]{:S(2)}, u32[]{:S(2)}) %collective-permute-start.16) | collective-permute-done | bytes 262176 | tf_op jit(solution)/shard_map/ppermute | solution.py:309
  106.2 1.9 %collective-permute-done.17.refs_2_ = bf16[2,128,512]{2,1,0:T(8,128)(2,1)S(1)} collective-permute-done((bf16[2,128,512]{2,1,0:T(8,128)(2,1)}, bf16[2,128,512]{2,1,0:T(8,128)(2,1)S(1)}, u32[]{:S(2)}, u32[]{:S(2)}) %collective-permute-start.17) | collective-permute-done | bytes 262176 | tf_op jit(solution)/shard_map/ppermute | solution.py:309
  108.1 0.8 collective-permute-start.28
  108.9 5.6 %collective-permute-done.24.refs_1_ = bf16[2,128,512]{2,1,0:T(8,128)(2,1)S(1)} collective-permute-done((bf16[2,128,512]{2,1,0:T(8,128)(2,1)}, bf16[2,128,512]{2,1,0:T(8,128)(2,1)S(1)}, u32[]{:S(2)}, u32[]{:S(2)}) %collective-permute-start.24) | collective-permute-done | bytes 262176 | tf_op jit(solution)/shard_map/ppermute | solution.py:309
  114.5 3.7 %collective-permute-start.30 = (bf16[2,128,512]{2,1,0:T(8,128)(2,1)}, bf16[2,128,512]{2,1,0:T(8,128)(2,1)S(1)}, u32[]{:S(2)}, u32[]{:S(2)}) collective-permute-start(bf16[2,128,512]{2,1,0:T(8,128)(2,1)} %get-tuple-element.88), channel_id=1, source_target_pairs={{0,7},{1,6},{2,5},{3,4},{4,3},{5,2},{6,1},{7,0},{8,15},{9,14},{10,... | collective-permute-start | bytes 786440 | tf_op jit(solution)/shard_map/ppermute | solution.py:309
  118.3 2.1 %fusion.14.term_ref = f32[512,768]{1,0:T(8,128)S(1)} fusion(bf16[768,512]{1,0:T(8,128)(2,1)} %get-tuple-element.70, bf16[768,768]{1,0:T(8,128)(2,1)S(1)} %copy-done), kind=kOutput, calls=%fused_computation.39 | convolution fusion | flops 603979776 | bytes 3538944 | tf_op jit(solution)/shard_map/dot_general | solution.py:347
  120.4 4.2 %collective-permute-done.26.refs_3_ = bf16[2,128,512]{2,1,0:T(8,128)(2,1)S(1)} collective-permute-done((bf16[2,128,512]{2,1,0:T(8,128)(2,1)}, bf16[2,128,512]{2,1,0:T(8,128)(2,1)S(1)}, u32[]{:S(2)}, u32[]{:S(2)}) %collective-permute-start.26) | collective-permute-done | bytes 262176 | tf_op jit(solution)/shard_map/ppermute | solution.py:309
  124.6 7.2 %collective-permute-start.18 = (bf16[2,128,512]{2,1,0:T(8,128)(2,1)S(1)}, bf16[2,128,512]{2,1,0:T(8,128)(2,1)S(1)}, u32[]{:S(2)}, u32[]{:S(2)}) collective-permute-start(bf16[2,128,512]{2,1,0:T(8,128)(2,1)S(1)} %copy-done.22), channel_id=1, source_target_pairs={{0,3},{1,2},{2,1},{3,0},{4,7},{5,6},{6,5},{7,4},{8,11},{9,10},{10,... | collective-permute-start | bytes 786440 | tf_op jit(solution)/shard_map/ppermute | solution.py:309
  131.9 3.3 %collective-permute-start.20 = (bf16[2,128,512]{2,1,0:T(8,128)(2,1)S(1)}, bf16[2,128,512]{2,1,0:T(8,128)(2,1)S(1)}, u32[]{:S(2)}, u32[]{:S(2)}) collective-permute-start(bf16[2,128,512]{2,1,0:T(8,128)(2,1)S(1)} %copy-done.18), channel_id=1, source_target_pairs={{0,5},{1,4},{2,7},{3,6},{4,1},{5,0},{6,3},{7,2},{8,13},{9,12},{10,... | collective-permute-start | bytes 786440 | tf_op jit(solution)/shard_map/ppermute | solution.py:309
  135.2 1.5 collective-permute-start.21
  136.7 1.1 collective-permute-start.22
  137.7 1.7 %convolution_convert_fusion = bf16[512,768]{1,0:T(8,128)(2,1)} fusion(bf16[768,512]{1,0:T(8,128)(2,1)S(1)} %copy-done.35, bf16[768,768]{1,0:T(8,128)(2,1)S(1)} %copy-done.14), kind=kOutput, calls=%fused_computation.2 | convolution fusion | flops 604372992 | bytes 2752512 | tf_op jit(solution)/shard_map/dot_general | solution.py:35
  139.4 0.9 owner_sum.3
  140.3 2.6 %collective-permute-done.18.refs_3_ = bf16[2,128,512]{2,1,0:T(8,128)(2,1)S(1)} collective-permute-done((bf16[2,128,512]{2,1,0:T(8,128)(2,1)S(1)}, bf16[2,128,512]{2,1,0:T(8,128)(2,1)S(1)}, u32[]{:S(2)}, u32[]{:S(2)}) %collective-permute-start.18) | collective-permute-done | bytes 262176 | tf_op jit(solution)/shard_map/ppermute | solution.py:309
  143.0 14.8 %collective-permute-done.20.refs_5_ = bf16[2,128,512]{2,1,0:T(8,128)(2,1)S(1)} collective-permute-done((bf16[2,128,512]{2,1,0:T(8,128)(2,1)S(1)}, bf16[2,128,512]{2,1,0:T(8,128)(2,1)S(1)}, u32[]{:S(2)}, u32[]{:S(2)}) %collective-permute-start.20) | collective-permute-done | bytes 262176 | tf_op jit(solution)/shard_map/ppermute | solution.py:309
  157.7 3.3 %collective-permute-done.21.refs_6_ = bf16[2,128,512]{2,1,0:T(8,128)(2,1)S(1)} collective-permute-done((bf16[2,128,512]{2,1,0:T(8,128)(2,1)S(1)}, bf16[2,128,512]{2,1,0:T(8,128)(2,1)S(1)}, u32[]{:S(2)}, u32[]{:S(2)}) %collective-permute-start.21) | collective-permute-done | bytes 262176 | tf_op jit(solution)/shard_map/ppermute | solution.py:309
  161.1 0.9 owner_sum.2
  162.1 3.2 %collective-permute-done.31 = bf16[4,128,512]{2,1,0:T(8,128)(2,1)S(1)} collective-permute-done((bf16[4,128,512]{2,1,0:T(8,128)(2,1)S(1)}, bf16[4,128,512]{2,1,0:T(8,128)(2,1)S(1)}, u32[]{:S(2)}, u32[]{:S(2)}) %collective-permute-start.31) | collective-permute-done | bytes 524320 | tf_op jit(solution)/shard_map/ppermute | solution.py:303
  165.3 1.5 finish.1
  (127 shorter events, 7.2 us)
Async XLA Ops:
  0.6 64.5 %copy-start = (bf16[768,768]{1,0:T(8,128)(2,1)S(1)}, bf16[768,768]{1,0:T(8,128)(2,1)}, u32[]{:S(2)}) copy-start(bf16[768,768]{1,0:T(8,128)(2,1)} %param.10) | copy-start | bytes 3538948
  4.5 26.5 %collective-permute-start.8 = (bf16[4,128,512]{2,1,0:T(8,128)(2,1)S(1)}, bf16[4,128,512]{2,1,0:T(8,128)(2,1)S(1)}, u32[]{:S(2)}, u32[]{:S(2)}) collective-permute-start(bf16[4,128,512]{2,1,0:T(8,128)(2,1)S(1)} %bitcast.26), channel_id=1, source_target_pairs={{0,24},{1,25},{2,26},{3,27},{4,28},{5,29},{6,30},{7,31},{8,16},{9,... | collective-permute-start | bytes 1572872 | tf_op jit(solution)/shard_map/ppermute | solution.py:303
  8.0 3.7 %collective-permute-start = (bf16[4,128,512]{2,1,0:T(8,128)(2,1)S(1)}, bf16[4,128,512]{2,1,0:T(8,128)(2,1)S(1)}, u32[]{:S(2)}, u32[]{:S(2)}) collective-permute-start(bf16[4,128,512]{2,1,0:T(8,128)(2,1)S(1)} %bitcast.27), channel_id=1, source_target_pairs={{0,16},{1,17},{2,18},{3,19},{4,20},{5,21},{6,22},{7,23},{8,24},{9,... | collective-permute-start | bytes 1572872 | tf_op jit(solution)/shard_map/ppermute | solution.py:303
  15.3 22.3 %copy-start.9 = (bf16[2,128,512]{2,1,0:T(8,128)(2,1)}, bf16[2,128,512]{2,1,0:T(8,128)(2,1)S(1)}, u32[]{:S(2)}) copy-start(bf16[2,128,512]{2,1,0:T(8,128)(2,1)S(1)} %get-tuple-element.46.refs_0_) | copy-start | bytes 786436
  15.3 22.3 %collective-permute-start.1 = (bf16[2,128,512]{2,1,0:T(8,128)(2,1)S(1)}, bf16[2,128,512]{2,1,0:T(8,128)(2,1)S(1)}, u32[]{:S(2)}, u32[]{:S(2)}) collective-permute-start(bf16[2,128,512]{2,1,0:T(8,128)(2,1)S(1)} %get-tuple-element.47), channel_id=1, source_target_pairs={{0,1},{1,0},{2,3},{3,2},{4,5},{5,4},{6,7},{7,6},{8,9},{9,8},{10,11... | collective-permute-start | bytes 786440 | tf_op jit(solution)/shard_map/ppermute | solution.py:309
  16.9 23.0 %collective-permute-start.2 = (bf16[2,128,512]{2,1,0:T(8,128)(2,1)S(1)}, bf16[2,128,512]{2,1,0:T(8,128)(2,1)S(1)}, u32[]{:S(2)}, u32[]{:S(2)}) collective-permute-start(bf16[2,128,512]{2,1,0:T(8,128)(2,1)S(1)} %get-tuple-element.48), channel_id=1, source_target_pairs={{0,2},{1,3},{2,0},{3,1},{4,6},{5,7},{6,4},{7,5},{8,10},{9,11},{10,... | collective-permute-start | bytes 786440 | tf_op jit(solution)/shard_map/ppermute | solution.py:309
  18.4 22.2 %collective-permute-start.3 = (bf16[2,128,512]{2,1,0:T(8,128)(2,1)S(1)}, bf16[2,128,512]{2,1,0:T(8,128)(2,1)S(1)}, u32[]{:S(2)}, u32[]{:S(2)}) collective-permute-start(bf16[2,128,512]{2,1,0:T(8,128)(2,1)S(1)} %get-tuple-element.49), channel_id=1, source_target_pairs={{0,3},{1,2},{2,1},{3,0},{4,7},{5,6},{6,5},{7,4},{8,11},{9,10},{10,... | collective-permute-start | bytes 786440 | tf_op jit(solution)/shard_map/ppermute | solution.py:309
  18.9 23.2 %collective-permute-start.4 = (bf16[2,128,512]{2,1,0:T(8,128)(2,1)S(1)}, bf16[2,128,512]{2,1,0:T(8,128)(2,1)S(1)}, u32[]{:S(2)}, u32[]{:S(2)}) collective-permute-start(bf16[2,128,512]{2,1,0:T(8,128)(2,1)S(1)} %get-tuple-element.50), channel_id=1, source_target_pairs={{0,4},{1,5},{2,6},{3,7},{4,0},{5,1},{6,2},{7,3},{8,12},{9,13},{10,... | collective-permute-start | bytes 786440 | tf_op jit(solution)/shard_map/ppermute | solution.py:309
  31.0 12.7 %copy-start.13 = (bf16[768,768]{1,0:T(8,128)(2,1)S(1)}, bf16[768,768]{1,0:T(8,128)(2,1)}, u32[]{:S(2)}) copy-start(bf16[768,768]{1,0:T(8,128)(2,1)} %param.13) | copy-start | bytes 3538948
  31.0 12.7 %copy-start.15 = (bf16[1,512,768]{2,1,0:T(8,128)(2,1)S(1)}, bf16[1,512,768]{2,1,0:T(8,128)(2,1)}, u32[]{:S(2)}) copy-start(bf16[1,512,768]{2,1,0:T(8,128)(2,1)} %param.9) | copy-start | bytes 2359300
  31.0 14.7 %collective-permute-start.5 = (bf16[2,128,512]{2,1,0:T(8,128)(2,1)S(1)}, bf16[2,128,512]{2,1,0:T(8,128)(2,1)S(1)}, u32[]{:S(2)}, u32[]{:S(2)}) collective-permute-start(bf16[2,128,512]{2,1,0:T(8,128)(2,1)S(1)} %get-tuple-element.51), channel_id=1, source_target_pairs={{0,5},{1,4},{2,7},{3,6},{4,1},{5,0},{6,3},{7,2},{8,13},{9,12},{10,... | collective-permute-start | bytes 786440 | tf_op jit(solution)/shard_map/ppermute | solution.py:309
  37.7 11.5 %collective-permute-start.6 = (bf16[2,128,512]{2,1,0:T(8,128)(2,1)S(1)}, bf16[2,128,512]{2,1,0:T(8,128)(2,1)S(1)}, u32[]{:S(2)}, u32[]{:S(2)}) collective-permute-start(bf16[2,128,512]{2,1,0:T(8,128)(2,1)S(1)} %get-tuple-element.52), channel_id=1, source_target_pairs={{0,6},{1,7},{2,4},{3,5},{4,2},{5,3},{6,0},{7,1},{8,14},{9,15},{10,... | collective-permute-start | bytes 786440 | tf_op jit(solution)/shard_map/ppermute | solution.py:309
  39.9 16.9 %collective-permute-start.7 = (bf16[2,128,512]{2,1,0:T(8,128)(2,1)S(1)}, bf16[2,128,512]{2,1,0:T(8,128)(2,1)S(1)}, u32[]{:S(2)}, u32[]{:S(2)}) collective-permute-start(bf16[2,128,512]{2,1,0:T(8,128)(2,1)S(1)} %get-tuple-element.53), channel_id=1, source_target_pairs={{0,7},{1,6},{2,5},{3,4},{4,3},{5,2},{6,1},{7,0},{8,15},{9,14},{10,... | collective-permute-start | bytes 786440 | tf_op jit(solution)/shard_map/ppermute | solution.py:309
  40.6 16.1 %collective-permute-start.9 = (bf16[2,128,512]{2,1,0:T(8,128)(2,1)S(1)}, bf16[2,128,512]{2,1,0:T(8,128)(2,1)S(1)}, u32[]{:S(2)}, u32[]{:S(2)}) collective-permute-start(bf16[2,128,512]{2,1,0:T(8,128)(2,1)S(1)} %get-tuple-element.55), channel_id=1, source_target_pairs={{0,1},{1,0},{2,3},{3,2},{4,5},{5,4},{6,7},{7,6},{8,9},{9,8},{10,11... | collective-permute-start | bytes 786440 | tf_op jit(solution)/shard_map/ppermute | solution.py:309
  42.1 23.0 %copy-start.6 = (bf16[1,512,768]{2,1,0:T(8,128)(2,1)S(1)}, bf16[1,512,768]{2,1,0:T(8,128)(2,1)}, u32[]{:S(2)}) copy-start(bf16[1,512,768]{2,1,0:T(8,128)(2,1)} %param.8) | copy-start | bytes 2359300
  42.1 23.0 %collective-permute-start.10 = (bf16[2,128,512]{2,1,0:T(8,128)(2,1)S(1)}, bf16[2,128,512]{2,1,0:T(8,128)(2,1)S(1)}, u32[]{:S(2)}, u32[]{:S(2)}) collective-permute-start(bf16[2,128,512]{2,1,0:T(8,128)(2,1)S(1)} %get-tuple-element.56), channel_id=1, source_target_pairs={{0,2},{1,3},{2,0},{3,1},{4,6},{5,7},{6,4},{7,5},{8,10},{9,11},{10,... | collective-permute-start | bytes 786440 | tf_op jit(solution)/shard_map/ppermute | solution.py:309
  45.7 21.1 %copy-start.25 = (bf16[2,128,512]{2,1,0:T(8,128)(2,1)}, bf16[2,128,512]{2,1,0:T(8,128)(2,1)S(1)}, u32[]{:S(2)}) copy-start(bf16[2,128,512]{2,1,0:T(8,128)(2,1)S(1)} %collective-permute-done.5.refs_5_) | copy-start | bytes 786436
  45.7 21.1 %collective-permute-start.11 = (bf16[2,128,512]{2,1,0:T(8,128)(2,1)S(1)}, bf16[2,128,512]{2,1,0:T(8,128)(2,1)S(1)}, u32[]{:S(2)}, u32[]{:S(2)}) collective-permute-start(bf16[2,128,512]{2,1,0:T(8,128)(2,1)S(1)} %get-tuple-element.57), channel_id=1, source_target_pairs={{0,3},{1,2},{2,1},{3,0},{4,7},{5,6},{6,5},{7,4},{8,11},{9,10},{10,... | collective-permute-start | bytes 786440 | tf_op jit(solution)/shard_map/ppermute | solution.py:309
  49.2 17.6 %copy-start.26 = (bf16[2,128,512]{2,1,0:T(8,128)(2,1)}, bf16[2,128,512]{2,1,0:T(8,128)(2,1)S(1)}, u32[]{:S(2)}) copy-start(bf16[2,128,512]{2,1,0:T(8,128)(2,1)S(1)} %collective-permute-done.6.refs_6_) | copy-start | bytes 786436
  49.2 17.7 %collective-permute-start.12 = (bf16[2,128,512]{2,1,0:T(8,128)(2,1)S(1)}, bf16[2,128,512]{2,1,0:T(8,128)(2,1)S(1)}, u32[]{:S(2)}, u32[]{:S(2)}) collective-permute-start(bf16[2,128,512]{2,1,0:T(8,128)(2,1)S(1)} %get-tuple-element.58), channel_id=1, source_target_pairs={{0,4},{1,5},{2,6},{3,7},{4,0},{5,1},{6,2},{7,3},{8,12},{9,13},{10,... | collective-permute-start | bytes 786440 | tf_op jit(solution)/shard_map/ppermute | solution.py:309
  56.7 10.5 %collective-permute-start.13 = (bf16[2,128,512]{2,1,0:T(8,128)(2,1)S(1)}, bf16[2,128,512]{2,1,0:T(8,128)(2,1)S(1)}, u32[]{:S(2)}, u32[]{:S(2)}) collective-permute-start(bf16[2,128,512]{2,1,0:T(8,128)(2,1)S(1)} %get-tuple-element.59), channel_id=1, source_target_pairs={{0,5},{1,4},{2,7},{3,6},{4,1},{5,0},{6,3},{7,2},{8,13},{9,12},{10,... | collective-permute-start | bytes 786440 | tf_op jit(solution)/shard_map/ppermute | solution.py:309
  56.7 16.0 %collective-permute-start.14 = (bf16[2,128,512]{2,1,0:T(8,128)(2,1)S(1)}, bf16[2,128,512]{2,1,0:T(8,128)(2,1)S(1)}, u32[]{:S(2)}, u32[]{:S(2)}) collective-permute-start(bf16[2,128,512]{2,1,0:T(8,128)(2,1)S(1)} %get-tuple-element.60), channel_id=1, source_target_pairs={{0,6},{1,7},{2,4},{3,5},{4,2},{5,3},{6,0},{7,1},{8,14},{9,15},{10,... | collective-permute-start | bytes 786440 | tf_op jit(solution)/shard_map/ppermute | solution.py:309
  65.1 12.6 %collective-permute-start.15 = (bf16[2,128,512]{2,1,0:T(8,128)(2,1)S(1)}, bf16[2,128,512]{2,1,0:T(8,128)(2,1)S(1)}, u32[]{:S(2)}, u32[]{:S(2)}) collective-permute-start(bf16[2,128,512]{2,1,0:T(8,128)(2,1)S(1)} %get-tuple-element.61), channel_id=1, source_target_pairs={{0,7},{1,6},{2,5},{3,4},{4,3},{5,2},{6,1},{7,0},{8,15},{9,14},{10,... | collective-permute-start | bytes 786440 | tf_op jit(solution)/shard_map/ppermute | solution.py:309
  66.8 10.9 %copy-start.30 = (bf16[2,128,512]{2,1,0:T(8,128)(2,1)}, bf16[2,128,512]{2,1,0:T(8,128)(2,1)S(1)}, u32[]{:S(2)}) copy-start(bf16[2,128,512]{2,1,0:T(8,128)(2,1)S(1)} %collective-permute-done.11.refs_11_) | copy-start | bytes 786436
  66.9 10.9 %copy-start.31 = (bf16[2,128,512]{2,1,0:T(8,128)(2,1)}, bf16[2,128,512]{2,1,0:T(8,128)(2,1)S(1)}, u32[]{:S(2)}) copy-start(bf16[2,128,512]{2,1,0:T(8,128)(2,1)S(1)} %collective-permute-done.12.refs_12_) | copy-start | bytes 786436
  96.5 9.5 %collective-permute-start.16 = (bf16[2,128,512]{2,1,0:T(8,128)(2,1)}, bf16[2,128,512]{2,1,0:T(8,128)(2,1)S(1)}, u32[]{:S(2)}, u32[]{:S(2)}) collective-permute-start(bf16[2,128,512]{2,1,0:T(8,128)(2,1)} %get-tuple-element.63), channel_id=1, source_target_pairs={{0,1},{1,0},{2,3},{3,2},{4,5},{5,4},{6,7},{7,6},{8,9},{9,8},{10,11... | collective-permute-start | bytes 786440 | tf_op jit(solution)/shard_map/ppermute | solution.py:309
  98.0 10.1 %collective-permute-start.17 = (bf16[2,128,512]{2,1,0:T(8,128)(2,1)}, bf16[2,128,512]{2,1,0:T(8,128)(2,1)S(1)}, u32[]{:S(2)}, u32[]{:S(2)}) collective-permute-start(bf16[2,128,512]{2,1,0:T(8,128)(2,1)} %get-tuple-element.64), channel_id=1, source_target_pairs={{0,2},{1,3},{2,0},{3,1},{4,6},{5,7},{6,4},{7,5},{8,10},{9,11},{10,... | collective-permute-start | bytes 786440 | tf_op jit(solution)/shard_map/ppermute | solution.py:309
  98.3 16.2 %collective-permute-start.24 = (bf16[2,128,512]{2,1,0:T(8,128)(2,1)}, bf16[2,128,512]{2,1,0:T(8,128)(2,1)S(1)}, u32[]{:S(2)}, u32[]{:S(2)}) collective-permute-start(bf16[2,128,512]{2,1,0:T(8,128)(2,1)} %get-tuple-element.82), channel_id=1, source_target_pairs={{0,1},{1,0},{2,3},{3,2},{4,5},{5,4},{6,7},{7,6},{8,9},{9,8},{10,11... | collective-permute-start | bytes 786440 | tf_op jit(solution)/shard_map/ppermute | solution.py:309
  99.1 15.4 %collective-permute-start.25 = (bf16[2,128,512]{2,1,0:T(8,128)(2,1)}, bf16[2,128,512]{2,1,0:T(8,128)(2,1)S(1)}, u32[]{:S(2)}, u32[]{:S(2)}) collective-permute-start(bf16[2,128,512]{2,1,0:T(8,128)(2,1)} %get-tuple-element.83), channel_id=1, source_target_pairs={{0,2},{1,3},{2,0},{3,1},{4,6},{5,7},{6,4},{7,5},{8,10},{9,11},{10,... | collective-permute-start | bytes 786440 | tf_op jit(solution)/shard_map/ppermute | solution.py:309
  101.0 23.6 %collective-permute-start.26 = (bf16[2,128,512]{2,1,0:T(8,128)(2,1)}, bf16[2,128,512]{2,1,0:T(8,128)(2,1)S(1)}, u32[]{:S(2)}, u32[]{:S(2)}) collective-permute-start(bf16[2,128,512]{2,1,0:T(8,128)(2,1)} %get-tuple-element.84), channel_id=1, source_target_pairs={{0,3},{1,2},{2,1},{3,0},{4,7},{5,6},{6,5},{7,4},{8,11},{9,10},{10,... | collective-permute-start | bytes 786440 | tf_op jit(solution)/shard_map/ppermute | solution.py:309
  106.1 25.8 %collective-permute-start.27 = (bf16[2,128,512]{2,1,0:T(8,128)(2,1)}, bf16[2,128,512]{2,1,0:T(8,128)(2,1)S(1)}, u32[]{:S(2)}, u32[]{:S(2)}) collective-permute-start(bf16[2,128,512]{2,1,0:T(8,128)(2,1)} %get-tuple-element.85), channel_id=1, source_target_pairs={{0,4},{1,5},{2,6},{3,7},{4,0},{5,1},{6,2},{7,3},{8,12},{9,13},{10,... | collective-permute-start | bytes 786440 | tf_op jit(solution)/shard_map/ppermute | solution.py:309
  108.1 23.7 %collective-permute-start.28 = (bf16[2,128,512]{2,1,0:T(8,128)(2,1)}, bf16[2,128,512]{2,1,0:T(8,128)(2,1)S(1)}, u32[]{:S(2)}, u32[]{:S(2)}) collective-permute-start(bf16[2,128,512]{2,1,0:T(8,128)(2,1)} %get-tuple-element.86), channel_id=1, source_target_pairs={{0,5},{1,4},{2,7},{3,6},{4,1},{5,0},{6,3},{7,2},{8,13},{9,12},{10,... | collective-permute-start | bytes 786440 | tf_op jit(solution)/shard_map/ppermute | solution.py:309
  114.5 20.7 %collective-permute-start.29 = (bf16[2,128,512]{2,1,0:T(8,128)(2,1)}, bf16[2,128,512]{2,1,0:T(8,128)(2,1)S(1)}, u32[]{:S(2)}, u32[]{:S(2)}) collective-permute-start(bf16[2,128,512]{2,1,0:T(8,128)(2,1)} %get-tuple-element.87), channel_id=1, source_target_pairs={{0,6},{1,7},{2,4},{3,5},{4,2},{5,3},{6,0},{7,1},{8,14},{9,15},{10,... | collective-permute-start | bytes 786440 | tf_op jit(solution)/shard_map/ppermute | solution.py:309
  114.5 22.2 %collective-permute-start.30 = (bf16[2,128,512]{2,1,0:T(8,128)(2,1)}, bf16[2,128,512]{2,1,0:T(8,128)(2,1)S(1)}, u32[]{:S(2)}, u32[]{:S(2)}) collective-permute-start(bf16[2,128,512]{2,1,0:T(8,128)(2,1)} %get-tuple-element.88), channel_id=1, source_target_pairs={{0,7},{1,6},{2,5},{3,4},{4,3},{5,2},{6,1},{7,0},{8,15},{9,14},{10,... | collective-permute-start | bytes 786440 | tf_op jit(solution)/shard_map/ppermute | solution.py:309
  118.2 13.6 %copy-start.19 = (bf16[2,128,512]{2,1,0:T(8,128)(2,1)S(1)}, bf16[2,128,512]{2,1,0:T(8,128)(2,1)}, u32[]{:S(2)}) copy-start(bf16[2,128,512]{2,1,0:T(8,128)(2,1)} %get-tuple-element.66) | copy-start | bytes 786436
  118.2 13.6 %copy-start.18 = (bf16[2,128,512]{2,1,0:T(8,128)(2,1)S(1)}, bf16[2,128,512]{2,1,0:T(8,128)(2,1)}, u32[]{:S(2)}) copy-start(bf16[2,128,512]{2,1,0:T(8,128)(2,1)} %get-tuple-element.67) | copy-start | bytes 786436
  118.2 17.0 %copy-start.17 = (bf16[2,128,512]{2,1,0:T(8,128)(2,1)S(1)}, bf16[2,128,512]{2,1,0:T(8,128)(2,1)}, u32[]{:S(2)}) copy-start(bf16[2,128,512]{2,1,0:T(8,128)(2,1)} %get-tuple-element.68) | copy-start | bytes 786436
  118.2 18.4 %copy-start.16 = (bf16[2,128,512]{2,1,0:T(8,128)(2,1)S(1)}, bf16[2,128,512]{2,1,0:T(8,128)(2,1)}, u32[]{:S(2)}) copy-start(bf16[2,128,512]{2,1,0:T(8,128)(2,1)} %get-tuple-element.69) | copy-start | bytes 786436
  118.2 19.5 %copy-start.14 = (bf16[768,768]{1,0:T(8,128)(2,1)S(1)}, bf16[768,768]{1,0:T(8,128)(2,1)}, u32[]{:S(2)}) copy-start(bf16[768,768]{1,0:T(8,128)(2,1)} %param.13) | copy-start | bytes 3538948
  118.2 19.5 %copy-start.35 = (bf16[768,512]{1,0:T(8,128)(2,1)S(1)}, bf16[768,512]{1,0:T(8,128)(2,1)}, u32[]{:S(2)}) copy-start(bf16[768,512]{1,0:T(8,128)(2,1)} %get-tuple-element.71) | copy-start | bytes 2359300
  124.6 18.4 %collective-permute-start.18 = (bf16[2,128,512]{2,1,0:T(8,128)(2,1)S(1)}, bf16[2,128,512]{2,1,0:T(8,128)(2,1)S(1)}, u32[]{:S(2)}, u32[]{:S(2)}) collective-permute-start(bf16[2,128,512]{2,1,0:T(8,128)(2,1)S(1)} %copy-done.22), channel_id=1, source_target_pairs={{0,3},{1,2},{2,1},{3,0},{4,7},{5,6},{6,5},{7,4},{8,11},{9,10},{10,... | collective-permute-start | bytes 786440 | tf_op jit(solution)/shard_map/ppermute | solution.py:309
  131.8 11.1 %collective-permute-start.19 = (bf16[2,128,512]{2,1,0:T(8,128)(2,1)S(1)}, bf16[2,128,512]{2,1,0:T(8,128)(2,1)S(1)}, u32[]{:S(2)}, u32[]{:S(2)}) collective-permute-start(bf16[2,128,512]{2,1,0:T(8,128)(2,1)S(1)} %copy-done.19), channel_id=1, source_target_pairs={{0,4},{1,5},{2,6},{3,7},{4,0},{5,1},{6,2},{7,3},{8,12},{9,13},{10,... | collective-permute-start | bytes 786440 | tf_op jit(solution)/shard_map/ppermute | solution.py:309
  131.9 25.8 %collective-permute-start.20 = (bf16[2,128,512]{2,1,0:T(8,128)(2,1)S(1)}, bf16[2,128,512]{2,1,0:T(8,128)(2,1)S(1)}, u32[]{:S(2)}, u32[]{:S(2)}) collective-permute-start(bf16[2,128,512]{2,1,0:T(8,128)(2,1)S(1)} %copy-done.18), channel_id=1, source_target_pairs={{0,5},{1,4},{2,7},{3,6},{4,1},{5,0},{6,3},{7,2},{8,13},{9,12},{10,... | collective-permute-start | bytes 786440 | tf_op jit(solution)/shard_map/ppermute | solution.py:309
  135.2 25.9 %collective-permute-start.21 = (bf16[2,128,512]{2,1,0:T(8,128)(2,1)S(1)}, bf16[2,128,512]{2,1,0:T(8,128)(2,1)S(1)}, u32[]{:S(2)}, u32[]{:S(2)}) collective-permute-start(bf16[2,128,512]{2,1,0:T(8,128)(2,1)S(1)} %copy-done.17), channel_id=1, source_target_pairs={{0,6},{1,7},{2,4},{3,5},{4,2},{5,3},{6,0},{7,1},{8,14},{9,15},{10,... | collective-permute-start | bytes 786440 | tf_op jit(solution)/shard_map/ppermute | solution.py:309
  136.7 24.4 %collective-permute-start.22 = (bf16[2,128,512]{2,1,0:T(8,128)(2,1)S(1)}, bf16[2,128,512]{2,1,0:T(8,128)(2,1)S(1)}, u32[]{:S(2)}, u32[]{:S(2)}) collective-permute-start(bf16[2,128,512]{2,1,0:T(8,128)(2,1)S(1)} %copy-done.16), channel_id=1, source_target_pairs={{0,7},{1,6},{2,5},{3,4},{4,3},{5,2},{6,1},{7,0},{8,15},{9,14},{10,... | collective-permute-start | bytes 786440 | tf_op jit(solution)/shard_map/ppermute | solution.py:309
  139.4 21.6 %copy-start.7 = (bf16[2,128,512]{2,1,0:T(8,128)(2,1)S(1)}, bf16[2,128,512]{2,1,0:T(8,128)(2,1)}, u32[]{:S(2)}) copy-start(bf16[2,128,512]{2,1,0:T(8,128)(2,1)} %get-tuple-element.73.refs_0_) | copy-start | bytes 786436
  143.0 22.4 %collective-permute-start.31 = (bf16[4,128,512]{2,1,0:T(8,128)(2,1)S(1)}, bf16[4,128,512]{2,1,0:T(8,128)(2,1)S(1)}, u32[]{:S(2)}, u32[]{:S(2)}) collective-permute-start(bf16[4,128,512]{2,1,0:T(8,128)(2,1)S(1)} %owner_sum.3), channel_id=1, source_target_pairs={{0,24},{1,25},{2,26},{3,27},{4,28},{5,29},{6,30},{7,31},{8,16},{9,... | collective-permute-start | bytes 1572872 | tf_op jit(solution)/shard_map/ppermute | solution.py:303
  162.0 3.3 %collective-permute-start.23 = (bf16[4,128,512]{2,1,0:T(8,128)(2,1)S(1)}, bf16[4,128,512]{2,1,0:T(8,128)(2,1)S(1)}, u32[]{:S(2)}, u32[]{:S(2)}) collective-permute-start(bf16[4,128,512]{2,1,0:T(8,128)(2,1)S(1)} %owner_sum.2), channel_id=1, source_target_pairs={{0,16},{1,17},{2,18},{3,19},{4,20},{5,21},{6,22},{7,23},{8,24},{9,... | collective-permute-start | bytes 1572872 | tf_op jit(solution)/shard_map/ppermute | solution.py:303
  (20 other events, 98.4 us)

commit v9 on v8

v9 whole, which is shorter than its diff:
```python
import functools

import jax
import jax.numpy as jnp
from jax import lax
from jax.experimental import pallas as pl
from jax.experimental.pallas import tpu as pltpu
from jax.sharding import PartitionSpec as P

HEADS = 12
KV_HEADS = 4
HEAD_DIM = 64
BLK = 128
CAP = 2
GROUP = HEADS // KV_HEADS
KV = KV_HEADS * HEAD_DIM
PAIR = 2 * HEAD_DIM
CODE = 16
MAJOR = 4
TEMPER = HEAD_DIM ** (-0.5)
EPSILON = 1e-06
WHOLE = pl.BlockSpec(memory_space=pltpu.VMEM)
F32 = jnp.float32
BF16 = jnp.bfloat16


def params(mebibytes):
    return pltpu.CompilerParams(vmem_limit_bytes=mebibytes * 1024 * 1024)


def dot_nt(a, b):
    return lax.dot_general(a, b, (((1,), (1,)), ((), ())), preferred_element_type=F32)


def dot_tn(a, b):
    return lax.dot_general(a, b, (((0,), (0,)), ((), ())), preferred_element_type=F32)


def feature_heads(features, g):
    first = g * GROUP
    return jnp.concatenate(
        [features[(first + r) * HEAD_DIM : (first + r + 1) * HEAD_DIM] for r in range(GROUP)],
        axis=1,
    )


def two_groups(features, j):
    low, high = feature_heads(features, 2 * j), feature_heads(features, 2 * j + 1)
    zeros = jnp.zeros_like(low)
    return jnp.concatenate(
        [jnp.concatenate([low, zeros], axis=1), jnp.concatenate([zeros, high], axis=1)], axis=0
    )


def head_rows(pair_out):
    heads = []
    for i in range(2 * GROUP):
        top = i // GROUP * HEAD_DIM
        heads.append(pair_out[top : top + HEAD_DIM, i * BLK : (i + 1) * BLK])
    return jnp.concatenate(heads, axis=0)


def attention_kernel(list_len, get_ref, put_ref, q_ref, ng_ref, *refs):
    expo_scr, kv_scr, parts_scr, in_sems, out_sems = refs[-5:]
    sources = (len(refs) - 7) // 2
    arrived, (normed_ref, qg_ref) = refs[:sources], refs[sources : sources + 2]
    back = refs[sources + 2 : 2 * sources + 2]
    step = pl.program_id(0)
    entries = in_sems.shape[0]

    def rows_of(e):
        return pl.ds(pl.multiple_of(e * BLK, BLK), BLK)

    def fetch(e, source, slot):
        return pltpu.make_async_copy(
            arrived[source].at[slot], kv_scr.at[rows_of(e)], in_sems.at[e]
        )

    def give(e, source, slot):
        return pltpu.make_async_copy(
            parts_scr.at[rows_of(e)], back[source].at[slot], out_sems.at[e]
        )

    def start(copy, code_ref, begin, count):
        def one(i, carry):
            e = begin + i
            code = code_ref[e]
            for source in range(sources):

                @pl.when(code // CODE == source)
                def _():
                    copy(e, source, code % CODE).start()

            return carry

        lax.fori_loop(0, count, one, 0)

    @pl.when(step == 0)
    def _():
        start(fetch, get_ref, 0, entries)

    first = step * list_len
    for l in range(list_len):
        fetch(first + l, 0, 0).wait()
    here = pl.ds(pl.multiple_of(step * list_len * BLK, list_len * BLK), list_len * BLK)
    keys = [kv_scr[here, j * PAIR : (j + 1) * PAIR] for j in range(KV // PAIR)]
    values = [kv_scr[here, KV + j * PAIR : KV + (j + 1) * PAIR] for j in range(KV // PAIR)]
    queries = q_ref[...] * jnp.asarray(TEMPER, BF16)
    pairs = range(KV // PAIR)
    wide = [two_groups(queries, j) for j in pairs]
    scores = [jnp.dot(keys[j], wide[j], preferred_element_type=F32) for j in pairs]
    attended, scales = [], []
    for j in pairs:
        expo = jnp.exp(scores[j] - jnp.max(scores[j], axis=0, keepdims=True))
        scale = 1.0 / jnp.sum(expo, axis=0, keepdims=True)
        expo_scr[j] = expo.astype(BF16)
        attended.append(head_rows(dot_tn(values[j], expo_scr[j]) * scale))
        scales += [
            jnp.broadcast_to(scale[:, i * BLK : (i + 1) * BLK], (HEAD_DIM, BLK))
            for i in range(2 * GROUP)
        ]
    exact = jnp.concatenate(attended, axis=0)
    attended = exact.astype(BF16).astype(F32)
    width = attended.shape[0]
    inverse = lax.rsqrt(jnp.sum(attended * attended, axis=0, keepdims=True) / width + EPSILON)
    normed = attended * inverse
    normed_ref[...] = normed.astype(BF16)
    normed_grad = ng_ref[...]
    shared = jnp.sum(normed_grad * normed, axis=0, keepdims=True) / width
    attended_grad = (normed_grad - normed * shared) * inverse
    scaled_grad = (attended_grad * jnp.concatenate(scales, axis=0)).astype(BF16)
    overlap = scaled_grad.astype(F32) * exact
    grads = [two_groups(scaled_grad, j) for j in pairs]
    prob_grads = [jnp.dot(values[j], grads[j], preferred_element_type=F32) for j in pairs]
    for j in pairs:
        heads = range(2 * GROUP * j, 2 * GROUP * (j + 1))
        row_dot = jnp.concatenate(
            [
                jnp.sum(overlap[h * HEAD_DIM : (h + 1) * HEAD_DIM], axis=0, keepdims=True)
                for h in heads
            ],
            axis=1,
        )
        expo = expo_scr[j]
        value_part = dot_nt(expo, grads[j])
        score_grad = (expo.astype(F32) * (prob_grads[j] - row_dot)).astype(BF16)
        query_grad = head_rows(dot_tn(keys[j], score_grad) * TEMPER).astype(BF16)
        qg_ref[heads.start * HEAD_DIM : heads.stop * HEAD_DIM, :] = query_grad
        key_part = dot_nt(score_grad, wide[j])
        parts_scr[here, j * PAIR : (j + 1) * PAIR] = key_part.astype(BF16)
        parts_scr[here, KV + j * PAIR : KV + (j + 1) * PAIR] = value_part.astype(BF16)
    start(give, put_ref, first, list_len)

    @pl.when(step == pl.num_programs(0) - 1)
    def _():
        for e in range(entries):
            give(e, 0, 0).wait()


def attention(gets, puts, queries, normed_grad, arrived, list_len):
    width, rows = queries.shape
    slot_shape = (CAP,) + arrived[0].shape[1:]
    blocks = rows // BLK
    entries = blocks * list_len
    row_spec = pl.BlockSpec((width, BLK), lambda r, g, p: (0, r))
    anywhere = pl.BlockSpec(memory_space=pl.ANY)
    keys = list_len * BLK
    pairs = HEADS * rows * keys
    return pl.pallas_call(
        functools.partial(attention_kernel, list_len),
        grid_spec=pltpu.PrefetchScalarGridSpec(
            num_scalar_prefetch=2,
            grid=(blocks,),
            in_specs=[row_spec, row_spec] + [anywhere] * len(arrived),
            out_specs=[row_spec, row_spec] + [anywhere] * len(arrived),
            scratch_shapes=[
                pltpu.VMEM((KV // PAIR, keys, 2 * GROUP * BLK), BF16),
                pltpu.VMEM((entries * BLK, 2 * KV), BF16),
                pltpu.VMEM((entries * BLK, 2 * KV), BF16),
                pltpu.SemaphoreType.DMA((entries,)),
                pltpu.SemaphoreType.DMA((entries,)),
            ],
        ),
        out_shape=[jax.ShapeDtypeStruct((width, rows), BF16)] * 2
        + [jax.ShapeDtypeStruct(slot_shape, BF16)] * len(arrived),
        compiler_params=params(56),
        cost_estimate=pl.CostEstimate(
            flops=12 * pairs * HEAD_DIM, bytes_accessed=16 * rows * width, transcendentals=pairs
        ),
        name="attention",
    )(gets, puts, queries, normed_grad, *arrived)


def project_kernel(tokens_hbm, wk_hbm, wv_hbm, out_ref, tokens, wk, wv, sems):
    moves = ((wk_hbm, wk), (tokens_hbm, tokens), (wv_hbm, wv))
    copies = [pltpu.make_async_copy(src, dst, sems.at[i]) for i, (src, dst) in enumerate(moves)]
    for copy in copies:
        copy.start()
    copies[0].wait()
    copies[1].wait()
    keys = jnp.dot(tokens[...], wk[...], preferred_element_type=F32)
    out_ref[:, :KV] = keys.astype(BF16)
    copies[2].wait()
    values = jnp.dot(tokens[...], wv[...], preferred_element_type=F32)
    out_ref[:, KV:] = values.astype(BF16)


def project(tokens, w_key, w_value):
    args = (tokens, w_key, w_value)
    return pl.pallas_call(
        project_kernel,
        in_specs=[pl.BlockSpec(memory_space=pl.ANY)] * 3,
        out_specs=WHOLE,
        out_shape=jax.ShapeDtypeStruct((tokens.shape[0], 2 * KV), BF16),
        scratch_shapes=[pltpu.VMEM(x.shape, BF16) for x in args]
        + [pltpu.SemaphoreType.DMA((3,))],
        compiler_params=params(56),
        name="project",
    )(*args)


def pack_kernel(picked_ref, tile_ref, *outs):
    for i, out in enumerate(outs):
        for s in range(CAP):
            out[s] = tile_ref[picked_ref[i * CAP + s]]


def pack(picked, tile):
    peers = picked.shape[0] // CAP
    shape = (CAP,) + tile.shape[1:]
    return pl.pallas_call(
        pack_kernel,
        in_specs=[pl.BlockSpec(memory_space=pltpu.SMEM), WHOLE],
        out_specs=[WHOLE] * peers,
        out_shape=[jax.ShapeDtypeStruct(shape, BF16)] * peers,
        compiler_params=params(16),
        name="pack",
    )(picked, tile)


def finish_kernel(parts, *refs):
    term_ref, wk_ref, wv_ref, out_ref = refs[parts:]
    grad = refs[0][...].astype(F32)
    for ref in refs[1:parts]:
        grad += ref[...].astype(F32)
    grad = grad.astype(BF16)
    total = dot_nt(grad[:, :KV], wk_ref[...]) + dot_nt(grad[:, KV:], wv_ref[...])
    out_ref[...] = (term_ref[...] + total).astype(BF16)


def finish(parts, term, w_key, w_value):
    return pl.pallas_call(
        functools.partial(finish_kernel, len(parts)),
        in_specs=[WHOLE] * (len(parts) + 3),
        out_specs=WHOLE,
        out_shape=jax.ShapeDtypeStruct(term.shape, BF16),
        compiler_params=params(24),
        name="finish",
    )(*parts, term, w_key, w_value)


def owner_kernel(peers, wanted_ref, *refs):
    parts, extra, (out_ref, total) = refs[:peers], refs[peers:-2], refs[-2:]
    total[...] = extra[0][...].astype(F32) if extra else jnp.zeros_like(total)
    for p, part in enumerate(parts):
        for s in range(CAP):
            block = wanted_ref[p * CAP + s]

            @pl.when(block >= 0)
            def _():
                total[block] += part[s].astype(F32)

    out_ref[...] = total[...].astype(BF16)


def owner_sum(wanted, parts, blocks, *extra):
    shape = (blocks,) + parts[0].shape[1:]
    args = (*parts, *extra)
    return pl.pallas_call(
        functools.partial(owner_kernel, len(parts)),
        in_specs=[pl.BlockSpec(memory_space=pltpu.SMEM)] + [WHOLE] * len(args),
        out_specs=WHOLE,
        out_shape=jax.ShapeDtypeStruct(shape, BF16),
        scratch_shapes=[pltpu.VMEM(shape, F32)],
        compiler_params=params(16),
        name="owner_sum",
    )(wanted, *args)


def shards(patches, out_grad, w_query, w_key, w_value, w_out, key_tiles, key_blocks):
    tokens = patches[0]
    rows = tokens.shape[0]
    tile_count = lax.axis_size("tile")
    plane = tile_count // MAJOR
    my_tile = lax.axis_index("tile")
    my_row, my_place = my_tile // plane, my_tile % plane
    block_count = rows // BLK
    list_len = key_tiles.shape[2]
    entry_count = block_count * list_len

    def swap(value, d, cross):
        pairs = [
            (v * tile_count + t, (v ^ cross) * tile_count + (t // plane ^ d) * plane + t % plane)
            for v in range(2)
            for t in range(tile_count)
        ]
        return lax.ppermute(value, ("vintage", "tile"), pairs)

    def after(value, earlier):
        return lax.optimization_barrier((value, earlier))[0]

    def spread(values, earlier=None):
        moved = []
        for i, value in enumerate(values):
            pairs = [(t, t // plane * plane + (t % plane ^ (i + 1))) for t in range(tile_count)]
            if earlier is not None:
                value = after(value, earlier[i])
            moved.append(lax.ppermute(value, "tile", pairs))
        return moved

    def plane_rows(table):
        table = table[0].reshape(MAJOR, plane, entry_count)
        return lax.dynamic_index_in_dim(table, my_row, 0, keepdims=False)

    def mine_of(table):
        return lax.dynamic_index_in_dim(table, my_place, 0, keepdims=False)

    tiles, picks = plane_rows(key_tiles), plane_rows(key_blocks)
    earlier = jnp.arange(entry_count)[:, None] > jnp.arange(entry_count)[None, :]
    same = (tiles[:, :, None] == tiles[:, None, :]) & earlier[None]
    ranks = jnp.sum(same.astype(jnp.int32), axis=2)
    groups, columns = (tiles // plane) ^ my_row, tiles % plane
    my_source = mine_of(groups) * plane + (mine_of(columns) ^ my_place)
    puts = my_source * CODE + mine_of(ranks)
    gets = jnp.where(my_source % plane == 0, my_source * CODE + mine_of(picks), puts)
    ids = jnp.arange(MAJOR * CAP, dtype=jnp.int32)
    slots = groups * CAP + ranks
    hits = (slots[:, None, :] == ids[None, :, None]) & (columns == my_place)[:, None, :]
    wanted = jnp.sum(jnp.where(hits, picks[:, None, :] + 1, 0), axis=2) - 1
    wanted = wanted[jnp.arange(plane) ^ my_place].reshape(plane, MAJOR, CAP)
    wanted = wanted.transpose(1, 0, 2).reshape(MAJOR, plane * CAP)
    picked = jnp.maximum(wanted[:, CAP:], 0)

    mine = project(tokens, w_key, w_value).reshape(block_count, BLK, 2 * KV)
    far_tile = swap(mine, 2, 1)
    next_tile = swap(mine, 1, 1)
    own_tile = swap(mine, 0, 1)
    own = spread(pack(picked[0], own_tile))
    beside = spread(pack(picked[1], next_tile), own)
    last_tile = swap(after(far_tile, own[-1]), 1, 0)
    far = spread(pack(picked[2], after(far_tile, own[-1])), beside)
    last = spread(pack(picked[3], last_tile), far)
    arrived = [own_tile, *own, next_tile, *beside, far_tile, *far, last_tile, *last]
    queries = lax.dot_general(
        w_query, tokens, (((0,), (1,)), ((), ())), preferred_element_type=F32
    ).astype(BF16)
    normed_grad = dot_nt(w_out, out_grad[0])
    normed_low, query_grad, *back = attention(
        gets, puts, queries, normed_grad, arrived, list_len
    )
    back = [back[d * plane : (d + 1) * plane] for d in range(MAJOR)]
    layer_out = dot_tn(normed_low, w_out).astype(BF16)
    query_term = lax.dot_general(
        query_grad, w_query, (((0,), (1,)), ((), ())), preferred_element_type=F32
    )
    last = spread(back[3][1:])
    far = spread(back[2][1:], last)
    beside = spread(back[1][1:], far)
    last_sum = swap(owner_sum(wanted[3], [back[3][0], *last], block_count), 1, 0)
    far_sum = owner_sum(wanted[2], [back[2][0], *far], block_count, last_sum)
    own = spread([after(x, far_sum) for x in back[0][1:]], beside)
    next_sum = owner_sum(wanted[1], [back[1][0], *beside], block_count)
    *own, query_term, layer_out = lax.optimization_barrier((*own, query_term, layer_out))
    own_sum = owner_sum(wanted[0], [back[0][0], *own], block_count)
    sums = [swap(far_sum, 2, 1), swap(next_sum, 1, 1), swap(own_sum, 0, 1)]
    input_grad = finish([x.reshape(rows, 2 * KV) for x in sums], query_term, w_key, w_value)
    return (layer_out[None], input_grad[None])


def solution(mesh):
    in_specs = (
        P("vintage", "tile", None),
        P("vintage", "tile", None),
        P(),
        P(),
        P(),
        P(),
        P("vintage", None, None),
        P("vintage", None, None),
    )
    out_specs = (P("vintage", "tile", None), P("vintage", "tile", None))
    return jax.shard_map(shards, mesh=mesh, in_specs=in_specs, out_specs=out_specs, check_vma=False)
```

time: 169 us -> 165 us (0.976)
  the two profiles are of different devices: /device:TPU:0 before, /device:TPU:12 now
where the time goes in v9:
time: 165 us
  waiting for transfers between devices  88.8 us (54%)
  starting transfers between devices  30.2 us (18%)
  Pallas kernels  29.3 us (18%)
  matrix products  8.89 us (5%)
  local copies, waits for them, and re-layouts  4.05 us (2%)
  other arithmetic  2.86 us (2%)
    ppermute x24, waiting for transfers between devices, spread(): moved.append(lax.ppermute(value, 'tile', pairs))  52.5 us
    ppermute x8, waiting for transfers between devices, swap(): return lax.ppermute(value, ('vintage', 'tile'), pairs)  36.2 us
    ppermute x24, starting transfers between devices, spread(): moved.append(lax.ppermute(value, 'tile', pairs))  25.7 us
    pallas_call x1, Pallas kernels, attention(): pl.pallas_call(functools.partial(attention_kernel, list_len), grid_spec=p...  18.1 us
    ppermute x8, starting transfers between devices, swap(): return lax.ppermute(value, ('vintage', 'tile'), pairs)  4.51 us
    dot_general x1, matrix products, dot_nt(): lax.dot_general(a, b, (((1,), (1,)), ((), ())), preferred_element_type=F32)  3.45 us
  transfers between devices with their start and end apart: 32, of which 15 were waited for; matrix products, arithmetic and copies ran while one was open for 8% of the time, Pallas kernels for 4%

profile of v9, /device:TPU:12, one launch (start us, length us, event | category | flops | bytes accessed | tf_op | source)
XLA Modules:
  0.0 165.0 jit_solution(15458562020686104386)
XLA Ops:
  0.7 3.3 %project.1 = bf16[512,512]{1,0:T(8,128)(2,1)} custom-call(bf16[512,768]{1,0:T(8,128)(2,1)} %bitcast.52, bf16[768,256]{1,0:T(8,128)(2,1)} %refs_4_.1, bf16[768,256]{1,0:T(8,128)(2,1)} %refs_5_.1), custom_call_target="tpu_custom_call" | custom-call | tf_op jit(solution)/shard_map/project/pallas_call | solution.py:210
  3.9 2.1 %collective-permute-start.8 = (bf16[4,128,512]{2,1,0:T(8,128)(2,1)}, bf16[4,128,512]{2,1,0:T(8,128)(2,1)S(1)}, u32[]{:S(2)}, u32[]{:S(2)}) collective-permute-start(bf16[4,128,512]{2,1,0:T(8,128)(2,1)} %bitcast.53), channel_id=1, source_target_pairs={{0,24},{1,25},{2,26},{3,27},{4,28},{5,29},{6,30},{7,31},{8,16},{9,... | collective-permute-start | bytes 1572872 | tf_op jit(solution)/shard_map/ppermute | solution.py:307
  6.0 0.7 collective-permute-start.4
  7.8 0.6 multiply_add_fusion
  9.8 0.6 pack.4
  10.4 1.5 collective-permute-start.3
  11.9 1.5 collective-permute-start.2
  13.9 16.8 %collective-permute-done.4.tile_ref.refs_4_ = bf16[4,128,512]{2,1,0:T(8,128)(2,1)S(1)} collective-permute-done((bf16[4,128,512]{2,1,0:T(8,128)(2,1)}, bf16[4,128,512]{2,1,0:T(8,128)(2,1)S(1)}, u32[]{:S(2)}, u32[]{:S(2)}) %collective-permute-start.4) | collective-permute-done | bytes 524320 | tf_op jit(solution)/shard_map/ppermute | solution.py:307
  30.7 1.4 pack.5
  32.1 1.4 collective-permute-start.7
  33.6 1.5 collective-permute-start.6
  35.8 1.3 compare_select_fusion.3
  37.7 4.9 %collective-permute-done.7.refs_7_ = bf16[2,128,512]{2,1,0:T(8,128)(2,1)} collective-permute-done((bf16[2,128,512]{2,1,0:T(8,128)(2,1)}, bf16[2,128,512]{2,1,0:T(8,128)(2,1)}, u32[]{:S(2)}, u32[]{:S(2)}) %collective-permute-start.7) | collective-permute-done | bytes 262176 | tf_op jit(solution)/shard_map/ppermute | solution.py:318
  42.6 1.4 collective-permute-start.11
  44.0 4.1 %collective-permute-done.6.refs_6_ = bf16[2,128,512]{2,1,0:T(8,128)(2,1)} collective-permute-done((bf16[2,128,512]{2,1,0:T(8,128)(2,1)}, bf16[2,128,512]{2,1,0:T(8,128)(2,1)}, u32[]{:S(2)}, u32[]{:S(2)}) %collective-permute-start.6) | collective-permute-done | bytes 262176 | tf_op jit(solution)/shard_map/ppermute | solution.py:318
  48.6 1.5 collective-permute-start.9
  50.1 3.5 %fusion.ng_ref = f32[768,512]{1,0:T(8,128)} fusion(bf16[768,768]{1,0:T(8,128)(2,1)} %param.13, bf16[1,512,768]{2,1,0:T(8,128)(2,1)} %param.9), kind=kOutput, calls=%fused_computation.3 | convolution fusion | flops 603979776 | bytes 3538944 | tf_op jit(solution)/shard_map/dot_general | solution.py:32
  54.2 1.6 collective-permute-start.15
  55.8 3.5 %collective-permute-done.10.refs_10_ = bf16[2,128,512]{2,1,0:T(8,128)(2,1)S(1)} collective-permute-done((bf16[2,128,512]{2,1,0:T(8,128)(2,1)S(1)}, bf16[2,128,512]{2,1,0:T(8,128)(2,1)S(1)}, u32[]{:S(2)}, u32[]{:S(2)}) %collective-permute-start.10) | collective-permute-done | bytes 262176 | tf_op jit(solution)/shard_map/ppermute | solution.py:318
  59.8 1.5 collective-permute-start.13
  61.3 1.7 %convolution_convert_fusion.1.q_ref = bf16[768,512]{1,0:T(8,128)(2,1)} fusion(bf16[768,768]{1,0:T(8,128)(2,1)S(1)} %copy-done, bf16[1,512,768]{2,1,0:T(8,128)(2,1)S(1)} %copy-done.11), kind=kOutput, calls=%fused_computation.2 | convolution fusion | flops 604372992 | bytes 2752512 | tf_op jit(solution)/shard_map/dot_general | solution.py:354
  63.0 1.9 %collective-permute-done.15.refs_15_ = bf16[2,128,512]{2,1,0:T(8,128)(2,1)S(1)} collective-permute-done((bf16[2,128,512]{2,1,0:T(8,128)(2,1)S(1)}, bf16[2,128,512]{2,1,0:T(8,128)(2,1)S(1)}, u32[]{:S(2)}, u32[]{:S(2)}) %collective-permute-start.15) | collective-permute-done | bytes 262176 | tf_op jit(solution)/shard_map/ppermute | solution.py:318
  64.9 4.8 %collective-permute-done.14.refs_14_ = bf16[2,128,512]{2,1,0:T(8,128)(2,1)S(1)} collective-permute-done((bf16[2,128,512]{2,1,0:T(8,128)(2,1)S(1)}, bf16[2,128,512]{2,1,0:T(8,128)(2,1)S(1)}, u32[]{:S(2)}, u32[]{:S(2)}) %collective-permute-start.14) | collective-permute-done | bytes 262176 | tf_op jit(solution)/shard_map/ppermute | solution.py:318
  69.7 0.7 copy-done.27
  70.5 18.1 %attention.1 = (bf16[768,512]{1,0:T(8,128)(2,1)}, bf16[768,512]{1,0:T(8,128)(2,1)}, bf16[2,128,512]{2,1,0:T(8,128)(2,1)}, bf16[2,128,512]{2,1,0:T(8,128)(2,1)}, ...) custom-call(s32[16]{0:T(128)} %get-tuple-element.125.get_ref, ...), custom_call_target="tpu_custom_call" | custom-call | flops 2415919104 | bytes 6291456 | tf_op jit(solution)/shard_map/attention/pallas_call | solution.py:169
  88.6 1.7 %collective-permute-start.16 = (bf16[2,128,512]{2,1,0:T(8,128)(2,1)}, bf16[2,128,512]{2,1,0:T(8,128)(2,1)S(1)}, u32[]{:S(2)}, u32[]{:S(2)}) collective-permute-start(bf16[2,128,512]{2,1,0:T(8,128)(2,1)} %get-tuple-element.84), channel_id=1, source_target_pairs={{0,1},{1,0},{2,3},{3,2},{4,5},{5,4},{6,7},{7,6},{8,9},{9,8},{10,11... | collective-permute-start | bytes 786440 | tf_op jit(solution)/shard_map/ppermute | solution.py:318
  90.7 1.5 collective-permute-start.20
  92.1 5.9 %collective-permute-done.16.refs_1_ = bf16[2,128,512]{2,1,0:T(8,128)(2,1)S(1)} collective-permute-done((bf16[2,128,512]{2,1,0:T(8,128)(2,1)}, bf16[2,128,512]{2,1,0:T(8,128)(2,1)S(1)}, u32[]{:S(2)}, u32[]{:S(2)}) %collective-permute-start.16) | collective-permute-done | bytes 262176 | tf_op jit(solution)/shard_map/ppermute | solution.py:318
  98.0 1.6 collective-permute-start.17
  99.6 5.5 %collective-permute-done.18.refs_2_ = bf16[2,128,512]{2,1,0:T(8,128)(2,1)S(1)} collective-permute-done((bf16[2,128,512]{2,1,0:T(8,128)(2,1)}, bf16[2,128,512]{2,1,0:T(8,128)(2,1)S(1)}, u32[]{:S(2)}, u32[]{:S(2)}) %collective-permute-start.18) | collective-permute-done | bytes 262176 | tf_op jit(solution)/shard_map/ppermute | solution.py:318
  105.1 1.0 collective-permute-start.21
  106.4 0.9 copy-done.10
  107.3 0.9 owner_sum.4
  109.3 2.0 %collective-permute-start.23 = (bf16[2,128,512]{2,1,0:T(8,128)(2,1)S(1)}, bf16[2,128,512]{2,1,0:T(8,128)(2,1)S(1)}, u32[]{:S(2)}, u32[]{:S(2)}) collective-permute-start(bf16[2,128,512]{2,1,0:T(8,128)(2,1)S(1)} %copy-done.22), channel_id=1, source_target_pairs={{0,1},{1,0},{2,3},{3,2},{4,5},{5,4},{6,7},{7,6},{8,9},{9,8},{10,11... | collective-permute-start | bytes 786440 | tf_op jit(solution)/shard_map/ppermute | solution.py:318
  111.2 8.8 %collective-permute-done.19.refs_2_ = bf16[2,128,512]{2,1,0:T(8,128)(2,1)S(1)} collective-permute-done((bf16[2,128,512]{2,1,0:T(8,128)(2,1)}, bf16[2,128,512]{2,1,0:T(8,128)(2,1)S(1)}, u32[]{:S(2)}, u32[]{:S(2)}) %collective-permute-start.19) | collective-permute-done | bytes 262176 | tf_op jit(solution)/shard_map/ppermute | solution.py:318
  120.1 2.0 %fusion.18.refs_3_ = f32[512,768]{1,0:T(8,128)S(1)} fusion(bf16[768,512]{1,0:T(8,128)(2,1)} %get-tuple-element.107, bf16[768,768]{1,0:T(8,128)(2,1)S(1)} %copy-done), kind=kOutput, calls=%fused_computation.51 | convolution fusion | flops 603979776 | bytes 3538944 | tf_op jit(solution)/shard_map/dot_general | solution.py:363
  122.2 0.8 owner_sum.5
  123.1 6.1 %collective-permute-done.27.refs_3_ = bf16[2,128,512]{2,1,0:T(8,128)(2,1)S(1)} collective-permute-done((bf16[2,128,512]{2,1,0:T(8,128)(2,1)}, bf16[2,128,512]{2,1,0:T(8,128)(2,1)S(1)}, u32[]{:S(2)}, u32[]{:S(2)}) %collective-permute-start.27) | collective-permute-done | bytes 262176 | tf_op jit(solution)/shard_map/ppermute | solution.py:318
  129.1 4.8 %collective-permute-done.25.refs_2_ = bf16[2,128,512]{2,1,0:T(8,128)(2,1)S(1)} collective-permute-done((bf16[2,128,512]{2,1,0:T(8,128)(2,1)}, bf16[2,128,512]{2,1,0:T(8,128)(2,1)S(1)}, u32[]{:S(2)}, u32[]{:S(2)}) %collective-permute-start.25) | collective-permute-done | bytes 262176 | tf_op jit(solution)/shard_map/ppermute | solution.py:318
  134.1 3.4 %collective-permute-start.28 = (bf16[2,128,512]{2,1,0:T(8,128)(2,1)S(1)}, bf16[2,128,512]{2,1,0:T(8,128)(2,1)S(1)}, u32[]{:S(2)}, u32[]{:S(2)}) collective-permute-start(bf16[2,128,512]{2,1,0:T(8,128)(2,1)S(1)} %copy-done.16), channel_id=1, source_target_pairs={{0,3},{1,2},{2,1},{3,0},{4,7},{5,6},{6,5},{7,4},{8,11},{9,10},{10,... | collective-permute-start | bytes 786440 | tf_op jit(solution)/shard_map/ppermute | solution.py:318
  137.5 1.7 %convolution_convert_fusion = bf16[512,768]{1,0:T(8,128)(2,1)} fusion(bf16[768,512]{1,0:T(8,128)(2,1)S(1)} %copy-done.29, bf16[768,768]{1,0:T(8,128)(2,1)S(1)} %copy-done.15), kind=kOutput, calls=%fused_computation.1 | convolution fusion | flops 604372992 | bytes 2752512 | tf_op jit(solution)/shard_map/dot_general | solution.py:36
  139.2 0.8 owner_sum.6
  140.1 1.5 collective-permute-start.29
  141.5 1.7 %collective-permute-done.26.refs_2_ = bf16[2,128,512]{2,1,0:T(8,128)(2,1)S(1)} collective-permute-done((bf16[2,128,512]{2,1,0:T(8,128)(2,1)S(1)}, bf16[2,128,512]{2,1,0:T(8,128)(2,1)S(1)}, u32[]{:S(2)}, u32[]{:S(2)}) %collective-permute-start.26) | collective-permute-done | bytes 262176 | tf_op jit(solution)/shard_map/ppermute | solution.py:318
  143.2 0.8 owner_sum.7
  144.1 13.0 %collective-permute-done.30 = bf16[4,128,512]{2,1,0:T(8,128)(2,1)S(1)} collective-permute-done((bf16[4,128,512]{2,1,0:T(8,128)(2,1)S(1)}, bf16[4,128,512]{2,1,0:T(8,128)(2,1)S(1)}, u32[]{:S(2)}, u32[]{:S(2)}) %collective-permute-start.30) | collective-permute-done | bytes 524320 | tf_op jit(solution)/shard_map/ppermute | solution.py:307
  157.1 6.4 %collective-permute-done.29 = bf16[4,128,512]{2,1,0:T(8,128)(2,1)S(1)} collective-permute-done((bf16[4,128,512]{2,1,0:T(8,128)(2,1)S(1)}, bf16[4,128,512]{2,1,0:T(8,128)(2,1)S(1)}, u32[]{:S(2)}, u32[]{:S(2)}) %collective-permute-start.29) | collective-permute-done | bytes 524320 | tf_op jit(solution)/shard_map/ppermute | solution.py:307
  163.5 1.5 finish.1
  (119 shorter events, 7.9 us)
Async XLA Ops:
  0.6 60.7 %copy-start = (bf16[768,768]{1,0:T(8,128)(2,1)S(1)}, bf16[768,768]{1,0:T(8,128)(2,1)}, u32[]{:S(2)}) copy-start(bf16[768,768]{1,0:T(8,128)(2,1)} %param.10) | copy-start | bytes 3538948
  0.6 6.2 %copy-start.13 = (s32[1,64,4]{1,2,0:T(4,128)S(1)}, s32[1,64,4]{1,2,0:T(4,128)}, u32[]{:S(2)}) copy-start(s32[1,64,4]{1,2,0:T(4,128)} %param.14) | copy-start | bytes 3076
  0.7 7.7 %copy-start.14 = (s32[1,64,4]{1,2,0:T(4,128)S(1)}, s32[1,64,4]{1,2,0:T(4,128)}, u32[]{:S(2)}) copy-start(s32[1,64,4]{1,2,0:T(4,128)} %param.15) | copy-start | bytes 3076
  3.9 31.7 %collective-permute-start.8 = (bf16[4,128,512]{2,1,0:T(8,128)(2,1)}, bf16[4,128,512]{2,1,0:T(8,128)(2,1)S(1)}, u32[]{:S(2)}, u32[]{:S(2)}) collective-permute-start(bf16[4,128,512]{2,1,0:T(8,128)(2,1)} %bitcast.53), channel_id=1, source_target_pairs={{0,24},{1,25},{2,26},{3,27},{4,28},{5,29},{6,30},{7,31},{8,16},{9,... | collective-permute-start | bytes 1572872 | tf_op jit(solution)/shard_map/ppermute | solution.py:307
  6.0 24.7 %collective-permute-start.4 = (bf16[4,128,512]{2,1,0:T(8,128)(2,1)}, bf16[4,128,512]{2,1,0:T(8,128)(2,1)S(1)}, u32[]{:S(2)}, u32[]{:S(2)}) collective-permute-start(bf16[4,128,512]{2,1,0:T(8,128)(2,1)} %bitcast.54), channel_id=1, source_target_pairs={{0,20},{1,21},{2,22},{3,23},{4,16},{5,17},{6,18},{7,19},{8,28},{9,... | collective-permute-start | bytes 1572872 | tf_op jit(solution)/shard_map/ppermute | solution.py:307
  6.8 3.0 %collective-permute-start = (bf16[4,128,512]{2,1,0:T(8,128)(2,1)}, bf16[4,128,512]{2,1,0:T(8,128)(2,1)S(1)}, u32[]{:S(2)}, u32[]{:S(2)}) collective-permute-start(bf16[4,128,512]{2,1,0:T(8,128)(2,1)} %bitcast.55), channel_id=1, source_target_pairs={{0,16},{1,17},{2,18},{3,19},{4,20},{5,21},{6,22},{7,23},{8,24},{9,... | collective-permute-start | bytes 1572872 | tf_op jit(solution)/shard_map/ppermute | solution.py:307
  9.7 43.8 %copy-start.5 = (bf16[4,128,512]{2,1,0:T(8,128)(2,1)}, bf16[4,128,512]{2,1,0:T(8,128)(2,1)S(1)}, u32[]{:S(2)}) copy-start(bf16[4,128,512]{2,1,0:T(8,128)(2,1)S(1)} %collective-permute-done.tile_ref.refs_0_) | copy-start | bytes 1572868
  10.4 21.8 %collective-permute-start.3 = (bf16[2,128,512]{2,1,0:T(8,128)(2,1)S(1)}, bf16[2,128,512]{2,1,0:T(8,128)(2,1)S(1)}, u32[]{:S(2)}, u32[]{:S(2)}) collective-permute-start(bf16[2,128,512]{2,1,0:T(8,128)(2,1)S(1)} %get-tuple-element.61), channel_id=1, source_target_pairs={{0,3},{1,2},{2,1},{3,0},{4,7},{5,6},{6,5},{7,4},{8,11},{9,10},{10,... | collective-permute-start | bytes 786440 | tf_op jit(solution)/shard_map/ppermute | solution.py:318
  11.9 21.7 %collective-permute-start.2 = (bf16[2,128,512]{2,1,0:T(8,128)(2,1)S(1)}, bf16[2,128,512]{2,1,0:T(8,128)(2,1)S(1)}, u32[]{:S(2)}, u32[]{:S(2)}) collective-permute-start(bf16[2,128,512]{2,1,0:T(8,128)(2,1)S(1)} %get-tuple-element.60), channel_id=1, source_target_pairs={{0,2},{1,3},{2,0},{3,1},{4,6},{5,7},{6,4},{7,5},{8,10},{9,11},{10,... | collective-permute-start | bytes 786440 | tf_op jit(solution)/shard_map/ppermute | solution.py:318
  13.4 21.7 %collective-permute-start.1 = (bf16[2,128,512]{2,1,0:T(8,128)(2,1)S(1)}, bf16[2,128,512]{2,1,0:T(8,128)(2,1)S(1)}, u32[]{:S(2)}, u32[]{:S(2)}) collective-permute-start(bf16[2,128,512]{2,1,0:T(8,128)(2,1)S(1)} %get-tuple-element.59), channel_id=1, source_target_pairs={{0,1},{1,0},{2,3},{3,2},{4,5},{5,4},{6,7},{7,6},{8,9},{9,8},{10,11... | collective-permute-start | bytes 786440 | tf_op jit(solution)/shard_map/ppermute | solution.py:318
  30.7 22.8 %copy-start.4 = (bf16[4,128,512]{2,1,0:T(8,128)(2,1)}, bf16[4,128,512]{2,1,0:T(8,128)(2,1)S(1)}, u32[]{:S(2)}) copy-start(bf16[4,128,512]{2,1,0:T(8,128)(2,1)S(1)} %collective-permute-done.4.tile_ref.refs_4_) | copy-start | bytes 1572868
  32.1 10.4 %collective-permute-start.7 = (bf16[2,128,512]{2,1,0:T(8,128)(2,1)}, bf16[2,128,512]{2,1,0:T(8,128)(2,1)}, u32[]{:S(2)}, u32[]{:S(2)}) collective-permute-start(bf16[2,128,512]{2,1,0:T(8,128)(2,1)} %get-tuple-element.67), channel_id=1, source_target_pairs={{0,3},{1,2},{2,1},{3,0},{4,7},{5,6},{6,5},{7,4},{8,11},{9,10},{10,... | collective-permute-start | bytes 786440 | tf_op jit(solution)/shard_map/ppermute | solution.py:318
  33.6 14.5 %collective-permute-start.6 = (bf16[2,128,512]{2,1,0:T(8,128)(2,1)}, bf16[2,128,512]{2,1,0:T(8,128)(2,1)}, u32[]{:S(2)}, u32[]{:S(2)}) collective-permute-start(bf16[2,128,512]{2,1,0:T(8,128)(2,1)} %get-tuple-element.65), channel_id=1, source_target_pairs={{0,2},{1,3},{2,0},{3,1},{4,6},{5,7},{6,4},{7,5},{8,10},{9,11},{10,... | collective-permute-start | bytes 786440 | tf_op jit(solution)/shard_map/ppermute | solution.py:318
  35.1 13.5 %collective-permute-start.5 = (bf16[2,128,512]{2,1,0:T(8,128)(2,1)S(1)}, bf16[2,128,512]{2,1,0:T(8,128)(2,1)}, u32[]{:S(2)}, u32[]{:S(2)}) collective-permute-start(bf16[2,128,512]{2,1,0:T(8,128)(2,1)S(1)} %get-tuple-element.63), channel_id=1, source_target_pairs={{0,1},{1,0},{2,3},{3,2},{4,5},{5,4},{6,7},{7,6},{8,9},{9,8},{10,11... | collective-permute-start | bytes 786440 | tf_op jit(solution)/shard_map/ppermute | solution.py:318
  35.8 17.7 %copy-start.3 = (bf16[4,128,512]{2,1,0:T(8,128)(2,1)}, bf16[4,128,512]{2,1,0:T(8,128)(2,1)S(1)}, u32[]{:S(2)}) copy-start(bf16[4,128,512]{2,1,0:T(8,128)(2,1)S(1)} %collective-permute-done.8.tile_ref.refs_8_) | copy-start | bytes 1572868
  35.8 17.7 %collective-permute-start.12 = (bf16[4,128,512]{2,1,0:T(8,128)(2,1)S(1)}, bf16[4,128,512]{2,1,0:T(8,128)(2,1)S(1)}, u32[]{:S(2)}, u32[]{:S(2)}) collective-permute-start(bf16[4,128,512]{2,1,0:T(8,128)(2,1)S(1)} %collective-permute-done.8.tile_ref.refs_8_), channel_id=1, source_target_pairs={{0,4},{1,5},{2,6},{3,7},{4,0},{5,1},{6,2},{7,3},{8,12},{9,13},{10,... | collective-permute-start | bytes 1572872 | tf_op jit(solution)/shard_map/ppermute | solution.py:307
  42.6 11.6 %collective-permute-start.11 = (bf16[2,128,512]{2,1,0:T(8,128)(2,1)S(1)}, bf16[2,128,512]{2,1,0:T(8,128)(2,1)S(1)}, u32[]{:S(2)}, u32[]{:S(2)}) collective-permute-start(bf16[2,128,512]{2,1,0:T(8,128)(2,1)S(1)} %get-tuple-element.74), channel_id=1, source_target_pairs={{0,3},{1,2},{2,1},{3,0},{4,7},{5,6},{6,5},{7,4},{8,11},{9,10},{10,... | collective-permute-start | bytes 786440 | tf_op jit(solution)/shard_map/ppermute | solution.py:318
  48.1 11.2 %collective-permute-start.10 = (bf16[2,128,512]{2,1,0:T(8,128)(2,1)S(1)}, bf16[2,128,512]{2,1,0:T(8,128)(2,1)S(1)}, u32[]{:S(2)}, u32[]{:S(2)}) collective-permute-start(bf16[2,128,512]{2,1,0:T(8,128)(2,1)S(1)} %get-tuple-element.72), channel_id=1, source_target_pairs={{0,2},{1,3},{2,0},{3,1},{4,6},{5,7},{6,4},{7,5},{8,10},{9,11},{10,... | collective-permute-start | bytes 786440 | tf_op jit(solution)/shard_map/ppermute | solution.py:318
  48.6 12.7 %copy-start.11 = (bf16[1,512,768]{2,1,0:T(8,128)(2,1)S(1)}, bf16[1,512,768]{2,1,0:T(8,128)(2,1)}, u32[]{:S(2)}) copy-start(bf16[1,512,768]{2,1,0:T(8,128)(2,1)} %param.8) | copy-start | bytes 2359300
  48.6 11.2 %collective-permute-start.9 = (bf16[2,128,512]{2,1,0:T(8,128)(2,1)S(1)}, bf16[2,128,512]{2,1,0:T(8,128)(2,1)S(1)}, u32[]{:S(2)}, u32[]{:S(2)}) collective-permute-start(bf16[2,128,512]{2,1,0:T(8,128)(2,1)S(1)} %get-tuple-element.70), channel_id=1, source_target_pairs={{0,1},{1,0},{2,3},{3,2},{4,5},{5,4},{6,7},{7,6},{8,9},{9,8},{10,11... | collective-permute-start | bytes 786440 | tf_op jit(solution)/shard_map/ppermute | solution.py:318
  53.6 9.5 %copy-start.6 = (bf16[4,128,512]{2,1,0:T(8,128)(2,1)}, bf16[4,128,512]{2,1,0:T(8,128)(2,1)S(1)}, u32[]{:S(2)}) copy-start(bf16[4,128,512]{2,1,0:T(8,128)(2,1)S(1)} %collective-permute-done.12.tile_ref.refs_12_) | copy-start | bytes 1572868
  54.2 8.8 %copy-start.23 = (bf16[2,128,512]{2,1,0:T(8,128)(2,1)}, bf16[2,128,512]{2,1,0:T(8,128)(2,1)S(1)}, u32[]{:S(2)}) copy-start(bf16[2,128,512]{2,1,0:T(8,128)(2,1)S(1)} %collective-permute-done.11.refs_11_) | copy-start | bytes 786436
  54.2 10.7 %collective-permute-start.15 = (bf16[2,128,512]{2,1,0:T(8,128)(2,1)S(1)}, bf16[2,128,512]{2,1,0:T(8,128)(2,1)S(1)}, u32[]{:S(2)}, u32[]{:S(2)}) collective-permute-start(bf16[2,128,512]{2,1,0:T(8,128)(2,1)S(1)} %get-tuple-element.80), channel_id=1, source_target_pairs={{0,3},{1,2},{2,1},{3,0},{4,7},{5,6},{6,5},{7,4},{8,11},{9,10},{10,... | collective-permute-start | bytes 786440 | tf_op jit(solution)/shard_map/ppermute | solution.py:318
  59.3 10.4 %collective-permute-start.14 = (bf16[2,128,512]{2,1,0:T(8,128)(2,1)S(1)}, bf16[2,128,512]{2,1,0:T(8,128)(2,1)S(1)}, u32[]{:S(2)}, u32[]{:S(2)}) collective-permute-start(bf16[2,128,512]{2,1,0:T(8,128)(2,1)S(1)} %get-tuple-element.78), channel_id=1, source_target_pairs={{0,2},{1,3},{2,0},{3,1},{4,6},{5,7},{6,4},{7,5},{8,10},{9,11},{10,... | collective-permute-start | bytes 786440 | tf_op jit(solution)/shard_map/ppermute | solution.py:318
  59.8 9.9 %collective-permute-start.13 = (bf16[2,128,512]{2,1,0:T(8,128)(2,1)S(1)}, bf16[2,128,512]{2,1,0:T(8,128)(2,1)S(1)}, u32[]{:S(2)}, u32[]{:S(2)}) collective-permute-start(bf16[2,128,512]{2,1,0:T(8,128)(2,1)S(1)} %get-tuple-element.76), channel_id=1, source_target_pairs={{0,1},{1,0},{2,3},{3,2},{4,5},{5,4},{6,7},{7,6},{8,9},{9,8},{10,11... | collective-permute-start | bytes 786440 | tf_op jit(solution)/shard_map/ppermute | solution.py:318
  88.6 9.4 %collective-permute-start.16 = (bf16[2,128,512]{2,1,0:T(8,128)(2,1)}, bf16[2,128,512]{2,1,0:T(8,128)(2,1)S(1)}, u32[]{:S(2)}, u32[]{:S(2)}) collective-permute-start(bf16[2,128,512]{2,1,0:T(8,128)(2,1)} %get-tuple-element.84), channel_id=1, source_target_pairs={{0,1},{1,0},{2,3},{3,2},{4,5},{5,4},{6,7},{7,6},{8,9},{9,8},{10,11... | collective-permute-start | bytes 786440 | tf_op jit(solution)/shard_map/ppermute | solution.py:318
  90.2 14.9 %collective-permute-start.18 = (bf16[2,128,512]{2,1,0:T(8,128)(2,1)}, bf16[2,128,512]{2,1,0:T(8,128)(2,1)S(1)}, u32[]{:S(2)}, u32[]{:S(2)}) collective-permute-start(bf16[2,128,512]{2,1,0:T(8,128)(2,1)} %get-tuple-element.87), channel_id=1, source_target_pairs={{0,2},{1,3},{2,0},{3,1},{4,6},{5,7},{6,4},{7,5},{8,10},{9,11},{10,... | collective-permute-start | bytes 786440 | tf_op jit(solution)/shard_map/ppermute | solution.py:318
  90.7 14.5 %collective-permute-start.20 = (bf16[2,128,512]{2,1,0:T(8,128)(2,1)}, bf16[2,128,512]{2,1,0:T(8,128)(2,1)S(1)}, u32[]{:S(2)}, u32[]{:S(2)}) collective-permute-start(bf16[2,128,512]{2,1,0:T(8,128)(2,1)} %get-tuple-element.90), channel_id=1, source_target_pairs={{0,3},{1,2},{2,1},{3,0},{4,7},{5,6},{6,5},{7,4},{8,11},{9,10},{10,... | collective-permute-start | bytes 786440 | tf_op jit(solution)/shard_map/ppermute | solution.py:318
  98.0 11.3 %collective-permute-start.17 = (bf16[2,128,512]{2,1,0:T(8,128)(2,1)}, bf16[2,128,512]{2,1,0:T(8,128)(2,1)S(1)}, u32[]{:S(2)}, u32[]{:S(2)}) collective-permute-start(bf16[2,128,512]{2,1,0:T(8,128)(2,1)} %get-tuple-element.85), channel_id=1, source_target_pairs={{0,1},{1,0},{2,3},{3,2},{4,5},{5,4},{6,7},{7,6},{8,9},{9,8},{10,11... | collective-permute-start | bytes 786440 | tf_op jit(solution)/shard_map/ppermute | solution.py:318
  105.1 15.0 %collective-permute-start.19 = (bf16[2,128,512]{2,1,0:T(8,128)(2,1)}, bf16[2,128,512]{2,1,0:T(8,128)(2,1)S(1)}, u32[]{:S(2)}, u32[]{:S(2)}) collective-permute-start(bf16[2,128,512]{2,1,0:T(8,128)(2,1)} %get-tuple-element.88), channel_id=1, source_target_pairs={{0,2},{1,3},{2,0},{3,1},{4,6},{5,7},{6,4},{7,5},{8,10},{9,11},{10,... | collective-permute-start | bytes 786440 | tf_op jit(solution)/shard_map/ppermute | solution.py:318
  105.1 15.0 %collective-permute-start.21 = (bf16[2,128,512]{2,1,0:T(8,128)(2,1)}, bf16[2,128,512]{2,1,0:T(8,128)(2,1)S(1)}, u32[]{:S(2)}, u32[]{:S(2)}) collective-permute-start(bf16[2,128,512]{2,1,0:T(8,128)(2,1)} %get-tuple-element.91), channel_id=1, source_target_pairs={{0,3},{1,2},{2,1},{3,0},{4,7},{5,6},{6,5},{7,4},{8,11},{9,10},{10,... | collective-permute-start | bytes 786440 | tf_op jit(solution)/shard_map/ppermute | solution.py:318
  108.2 14.0 %collective-permute-start.22 = (bf16[4,128,512]{2,1,0:T(8,128)(2,1)S(1)}, bf16[4,128,512]{2,1,0:T(8,128)(2,1)S(1)}, u32[]{:S(2)}, u32[]{:S(2)}) collective-permute-start(bf16[4,128,512]{2,1,0:T(8,128)(2,1)S(1)} %owner_sum.4), channel_id=1, source_target_pairs={{0,4},{1,5},{2,6},{3,7},{4,0},{5,1},{6,2},{7,3},{8,12},{9,13},{10,... | collective-permute-start | bytes 1572872 | tf_op jit(solution)/shard_map/ppermute | solution.py:307
  109.3 24.7 %collective-permute-start.23 = (bf16[2,128,512]{2,1,0:T(8,128)(2,1)S(1)}, bf16[2,128,512]{2,1,0:T(8,128)(2,1)S(1)}, u32[]{:S(2)}, u32[]{:S(2)}) collective-permute-start(bf16[2,128,512]{2,1,0:T(8,128)(2,1)S(1)} %copy-done.22), channel_id=1, source_target_pairs={{0,1},{1,0},{2,3},{3,2},{4,5},{5,4},{6,7},{7,6},{8,9},{9,8},{10,11... | collective-permute-start | bytes 786440 | tf_op jit(solution)/shard_map/ppermute | solution.py:318
  120.1 13.9 %collective-permute-start.25 = (bf16[2,128,512]{2,1,0:T(8,128)(2,1)}, bf16[2,128,512]{2,1,0:T(8,128)(2,1)S(1)}, u32[]{:S(2)}, u32[]{:S(2)}) collective-permute-start(bf16[2,128,512]{2,1,0:T(8,128)(2,1)} %get-tuple-element.100), channel_id=1, source_target_pairs={{0,2},{1,3},{2,0},{3,1},{4,6},{5,7},{6,4},{7,5},{8,10},{9,11},{10,... | collective-permute-start | bytes 786440 | tf_op jit(solution)/shard_map/ppermute | solution.py:318
  120.1 9.0 %collective-permute-start.27 = (bf16[2,128,512]{2,1,0:T(8,128)(2,1)}, bf16[2,128,512]{2,1,0:T(8,128)(2,1)S(1)}, u32[]{:S(2)}, u32[]{:S(2)}) collective-permute-start(bf16[2,128,512]{2,1,0:T(8,128)(2,1)} %get-tuple-element.105), channel_id=1, source_target_pairs={{0,3},{1,2},{2,1},{3,0},{4,7},{5,6},{6,5},{7,4},{8,11},{9,10},{10,... | collective-permute-start | bytes 786440 | tf_op jit(solution)/shard_map/ppermute | solution.py:318
  120.1 17.3 %copy-start.29 = (bf16[768,512]{1,0:T(8,128)(2,1)S(1)}, bf16[768,512]{1,0:T(8,128)(2,1)}, u32[]{:S(2)}) copy-start(bf16[768,512]{1,0:T(8,128)(2,1)} %get-tuple-element.108) | copy-start | bytes 2359300
  122.2 11.8 %copy-start.20 = (bf16[2,128,512]{2,1,0:T(8,128)(2,1)S(1)}, bf16[2,128,512]{2,1,0:T(8,128)(2,1)}, u32[]{:S(2)}) copy-start(bf16[2,128,512]{2,1,0:T(8,128)(2,1)} %get-tuple-element.96) | copy-start | bytes 786436
  122.2 11.8 %copy-start.18 = (bf16[2,128,512]{2,1,0:T(8,128)(2,1)S(1)}, bf16[2,128,512]{2,1,0:T(8,128)(2,1)}, u32[]{:S(2)}) copy-start(bf16[2,128,512]{2,1,0:T(8,128)(2,1)} %get-tuple-element.101) | copy-start | bytes 786436
  122.2 11.9 %copy-start.16 = (bf16[2,128,512]{2,1,0:T(8,128)(2,1)S(1)}, bf16[2,128,512]{2,1,0:T(8,128)(2,1)}, u32[]{:S(2)}) copy-start(bf16[2,128,512]{2,1,0:T(8,128)(2,1)} %get-tuple-element.106) | copy-start | bytes 786436
  122.2 15.3 %copy-start.15 = (bf16[768,768]{1,0:T(8,128)(2,1)S(1)}, bf16[768,768]{1,0:T(8,128)(2,1)}, u32[]{:S(2)}) copy-start(bf16[768,768]{1,0:T(8,128)(2,1)} %param.13) | copy-start | bytes 3538948
  134.0 7.6 %collective-permute-start.24 = (bf16[2,128,512]{2,1,0:T(8,128)(2,1)S(1)}, bf16[2,128,512]{2,1,0:T(8,128)(2,1)S(1)}, u32[]{:S(2)}, u32[]{:S(2)}) collective-permute-start(bf16[2,128,512]{2,1,0:T(8,128)(2,1)S(1)} %copy-done.20), channel_id=1, source_target_pairs={{0,1},{1,0},{2,3},{3,2},{4,5},{5,4},{6,7},{7,6},{8,9},{9,8},{10,11... | collective-permute-start | bytes 786440 | tf_op jit(solution)/shard_map/ppermute | solution.py:318
  134.0 9.2 %collective-permute-start.26 = (bf16[2,128,512]{2,1,0:T(8,128)(2,1)S(1)}, bf16[2,128,512]{2,1,0:T(8,128)(2,1)S(1)}, u32[]{:S(2)}, u32[]{:S(2)}) collective-permute-start(bf16[2,128,512]{2,1,0:T(8,128)(2,1)S(1)} %copy-done.18), channel_id=1, source_target_pairs={{0,2},{1,3},{2,0},{3,1},{4,6},{5,7},{6,4},{7,5},{8,10},{9,11},{10,... | collective-permute-start | bytes 786440 | tf_op jit(solution)/shard_map/ppermute | solution.py:318
  134.1 9.2 %collective-permute-start.28 = (bf16[2,128,512]{2,1,0:T(8,128)(2,1)S(1)}, bf16[2,128,512]{2,1,0:T(8,128)(2,1)S(1)}, u32[]{:S(2)}, u32[]{:S(2)}) collective-permute-start(bf16[2,128,512]{2,1,0:T(8,128)(2,1)S(1)} %copy-done.16), channel_id=1, source_target_pairs={{0,3},{1,2},{2,1},{3,0},{4,7},{5,6},{6,5},{7,4},{8,11},{9,10},{10,... | collective-permute-start | bytes 786440 | tf_op jit(solution)/shard_map/ppermute | solution.py:318
  140.0 23.6 %copy-start.1 = (bf16[768,256]{1,0:T(8,128)(2,1)S(1)}, bf16[768,256]{1,0:T(8,128)(2,1)}, u32[]{:S(2)}) copy-start(bf16[768,256]{1,0:T(8,128)(2,1)} %refs_4_.1) | copy-start | bytes 1179652
  140.0 23.5 %copy-start.2 = (bf16[768,256]{1,0:T(8,128)(2,1)S(1)}, bf16[768,256]{1,0:T(8,128)(2,1)}, u32[]{:S(2)}) copy-start(bf16[768,256]{1,0:T(8,128)(2,1)} %refs_5_.1) | copy-start | bytes 1179652
  140.0 17.2 %collective-permute-start.30 = (bf16[4,128,512]{2,1,0:T(8,128)(2,1)S(1)}, bf16[4,128,512]{2,1,0:T(8,128)(2,1)S(1)}, u32[]{:S(2)}, u32[]{:S(2)}) collective-permute-start(bf16[4,128,512]{2,1,0:T(8,128)(2,1)S(1)} %owner_sum.6), channel_id=1, source_target_pairs={{0,20},{1,21},{2,22},{3,23},{4,16},{5,17},{6,18},{7,19},{8,28},{9,... | collective-permute-start | bytes 1572872 | tf_op jit(solution)/shard_map/ppermute | solution.py:307
  140.1 23.4 %collective-permute-start.29 = (bf16[4,128,512]{2,1,0:T(8,128)(2,1)S(1)}, bf16[4,128,512]{2,1,0:T(8,128)(2,1)S(1)}, u32[]{:S(2)}, u32[]{:S(2)}) collective-permute-start(bf16[4,128,512]{2,1,0:T(8,128)(2,1)S(1)} %owner_sum.5), channel_id=1, source_target_pairs={{0,24},{1,25},{2,26},{3,27},{4,28},{5,29},{6,30},{7,31},{8,16},{9,... | collective-permute-start | bytes 1572872 | tf_op jit(solution)/shard_map/ppermute | solution.py:307
  144.0 19.5 %collective-permute-start.31 = (bf16[4,128,512]{2,1,0:T(8,128)(2,1)S(1)}, bf16[4,128,512]{2,1,0:T(8,128)(2,1)S(1)}, u32[]{:S(2)}, u32[]{:S(2)}) collective-permute-start(bf16[4,128,512]{2,1,0:T(8,128)(2,1)S(1)} %owner_sum.7), channel_id=1, source_target_pairs={{0,16},{1,17},{2,18},{3,19},{4,20},{5,21},{6,22},{7,23},{8,24},{9,... | collective-permute-start | bytes 1572872 | tf_op jit(solution)/shard_map/ppermute | solution.py:307
  (14 other events, 31.5 us)

commit v10 on v9

--- a/solution.py
+++ b/solution.py
@@ -16,6 +16,7 @@
 KV = KV_HEADS * HEAD_DIM
 PAIR = 2 * HEAD_DIM
 CODE = 16
+FAR_FLOPS = 30_000_000_000
 MAJOR = 4
 TEMPER = HEAD_DIM ** (-0.5)
 EPSILON = 1e-06
@@ -60,7 +61,7 @@
     return jnp.concatenate(heads, axis=0)
 
 
-def attention_kernel(list_len, get_ref, put_ref, q_ref, ng_ref, *refs):
+def attention_kernel(list_len, per_step, get_ref, put_ref, q_ref, ng_ref, *refs):
     expo_scr, kv_scr, parts_scr, in_sems, out_sems = refs[-5:]
     sources = (len(refs) - 7) // 2
     arrived, (normed_ref, qg_ref) = refs[:sources], refs[sources : sources + 2]
@@ -99,57 +100,97 @@
     def _():
         start(fetch, get_ref, 0, entries)
 
-    first = step * list_len
-    for l in range(list_len):
-        fetch(first + l, 0, 0).wait()
-    here = pl.ds(pl.multiple_of(step * list_len * BLK, list_len * BLK), list_len * BLK)
-    keys = [kv_scr[here, j * PAIR : (j + 1) * PAIR] for j in range(KV // PAIR)]
-    values = [kv_scr[here, KV + j * PAIR : KV + (j + 1) * PAIR] for j in range(KV // PAIR)]
-    queries = q_ref[...] * jnp.asarray(TEMPER, BF16)
+    first = step * per_step * list_len
+    for i in range(per_step * list_len):
+        fetch(first + i, 0, 0).wait()
     pairs = range(KV // PAIR)
-    wide = [two_groups(queries, j) for j in pairs]
-    scores = [jnp.dot(keys[j], wide[j], preferred_element_type=F32) for j in pairs]
-    attended, scales = [], []
-    for j in pairs:
-        expo = jnp.exp(scores[j] - jnp.max(scores[j], axis=0, keepdims=True))
+    keys, values, wide, scores, exact, scales, grads, overlap, prob_grads = (
+        {} for _ in range(9)
+    )
+
+    def rows_at(b):
+        size = list_len * BLK
+        return pl.ds(pl.multiple_of((step * per_step + b) * size, size), size)
+
+    def cols_at(b):
+        return slice(b * BLK, (b + 1) * BLK)
+
+    def score(b):
+        here = rows_at(b)
+        queries = q_ref[:, cols_at(b)] * jnp.asarray(TEMPER, BF16)
+        for j in pairs:
+            keys[b, j] = kv_scr[here, j * PAIR : (j + 1) * PAIR]
+            values[b, j] = kv_scr[here, KV + j * PAIR : KV + (j + 1) * PAIR]
+            wide[b, j] = two_groups(queries, j)
+            scores[b, j] = jnp.dot(keys[b, j], wide[b, j], preferred_element_type=F32)
+
+    def soften(b, j):
+        expo = jnp.exp(scores[b, j] - jnp.max(scores[b, j], axis=0, keepdims=True))
         scale = 1.0 / jnp.sum(expo, axis=0, keepdims=True)
-        expo_scr[j] = expo.astype(BF16)
-        attended.append(head_rows(dot_tn(values[j], expo_scr[j]) * scale))
-        scales += [
-            jnp.broadcast_to(scale[:, i * BLK : (i + 1) * BLK], (HEAD_DIM, BLK))
-            for i in range(2 * GROUP)
-        ]
-    exact = jnp.concatenate(attended, axis=0)
-    attended = exact.astype(BF16).astype(F32)
-    width = attended.shape[0]
-    inverse = lax.rsqrt(jnp.sum(attended * attended, axis=0, keepdims=True) / width + EPSILON)
-    normed = attended * inverse
-    normed_ref[...] = normed.astype(BF16)
-    normed_grad = ng_ref[...]
-    shared = jnp.sum(normed_grad * normed, axis=0, keepdims=True) / width
-    attended_grad = (normed_grad - normed * shared) * inverse
-    scaled_grad = (attended_grad * jnp.concatenate(scales, axis=0)).astype(BF16)
-    overlap = scaled_grad.astype(F32) * exact
-    grads = [two_groups(scaled_grad, j) for j in pairs]
-    prob_grads = [jnp.dot(values[j], grads[j], preferred_element_type=F32) for j in pairs]
-    for j in pairs:
+        expo_scr[b, j] = expo.astype(BF16)
+        exact[b, j] = head_rows(dot_tn(values[b, j], expo_scr[b, j]) * scale)
+        scales[b, j] = jnp.concatenate(
+            [
+                jnp.broadcast_to(scale[:, i * BLK : (i + 1) * BLK], (HEAD_DIM, BLK))
+                for i in range(2 * GROUP)
+            ],
+            axis=0,
+        )
+
+    def normalise(b):
+        whole = jnp.concatenate([exact[b, j] for j in pairs], axis=0)
+        attended = whole.astype(BF16).astype(F32)
+        width = attended.shape[0]
+        square = jnp.sum(attended * attended, axis=0, keepdims=True) / width
+        inverse = lax.rsqrt(square + EPSILON)
+        normed = attended * inverse
+        normed_ref[:, cols_at(b)] = normed.astype(BF16)
+        normed_grad = ng_ref[:, cols_at(b)]
+        shared = jnp.sum(normed_grad * normed, axis=0, keepdims=True) / width
+        attended_grad = (normed_grad - normed * shared) * inverse
+        scale = jnp.concatenate([scales[b, j] for j in pairs], axis=0)
+        scaled_grad = (attended_grad * scale).astype(BF16)
+        overlap[b] = scaled_grad.astype(F32) * whole
+        for j in pairs:
+            grads[b, j] = two_groups(scaled_grad, j)
+
+    def regrade(b, j):
+        prob_grads[b, j] = jnp.dot(values[b, j], grads[b, j], preferred_element_type=F32)
+
+    def finish_pair(b, j):
+        here = rows_at(b)
         heads = range(2 * GROUP * j, 2 * GROUP * (j + 1))
         row_dot = jnp.concatenate(
             [
-                jnp.sum(overlap[h * HEAD_DIM : (h + 1) * HEAD_DIM], axis=0, keepdims=True)
+                jnp.sum(overlap[b][h * HEAD_DIM : (h + 1) * HEAD_DIM], axis=0, keepdims=True)
                 for h in heads
             ],
             axis=1,
         )
-        expo = expo_scr[j]
-        value_part = dot_nt(expo, grads[j])
-        score_grad = (expo.astype(F32) * (prob_grads[j] - row_dot)).astype(BF16)
-        query_grad = head_rows(dot_tn(keys[j], score_grad) * TEMPER).astype(BF16)
-        qg_ref[heads.start * HEAD_DIM : heads.stop * HEAD_DIM, :] = query_grad
-        key_part = dot_nt(score_grad, wide[j])
+        expo = expo_scr[b, j]
+        value_part = dot_nt(expo, grads[b, j])
+        score_grad = (expo.astype(F32) * (prob_grads[b, j] - row_dot)).astype(BF16)
+        query_grad = head_rows(dot_tn(keys[b, j], score_grad) * TEMPER).astype(BF16)
+        qg_ref[heads.start * HEAD_DIM : heads.stop * HEAD_DIM, cols_at(b)] = query_grad
+        key_part = dot_nt(score_grad, wide[b, j])
         parts_scr[here, j * PAIR : (j + 1) * PAIR] = key_part.astype(BF16)
         parts_scr[here, KV + j * PAIR : KV + (j + 1) * PAIR] = value_part.astype(BF16)
-    start(give, put_ref, first, list_len)
+
+    for b in range(per_step):
+        score(b)
+    for j in pairs:
+        soften(0, j)
+    normalise(0)
+    for b in range(per_step):
+        for j in pairs:
+            regrade(b, j)
+            if b + 1 < per_step:
+                soften(b + 1, j)
+        for j in pairs:
+            finish_pair(b, j)
+            if b + 1 < per_step and j == 0:
+                normalise(b + 1)
+    start(give, put_ref, first, per_step * list_len)
 
     @pl.when(step == pl.num_programs(0) - 1)
     def _():
@@ -162,19 +203,20 @@
     slot_shape = (CAP,) + arrived[0].shape[1:]
     blocks = rows // BLK
     entries = blocks * list_len
-    row_spec = pl.BlockSpec((width, BLK), lambda r, g, p: (0, r))
+    per_step = 2 if list_len <= 4 and blocks % 2 == 0 else 1
+    row_spec = pl.BlockSpec((width, per_step * BLK), lambda r, g, p: (0, r))
     anywhere = pl.BlockSpec(memory_space=pl.ANY)
     keys = list_len * BLK
     pairs = HEADS * rows * keys
     return pl.pallas_call(
-        functools.partial(attention_kernel, list_len),
+        functools.partial(attention_kernel, list_len, per_step),
         grid_spec=pltpu.PrefetchScalarGridSpec(
             num_scalar_prefetch=2,
-            grid=(blocks,),
+            grid=(blocks // per_step,),
             in_specs=[row_spec, row_spec] + [anywhere] * len(arrived),
             out_specs=[row_spec, row_spec] + [anywhere] * len(arrived),
             scratch_shapes=[
-                pltpu.VMEM((KV // PAIR, keys, 2 * GROUP * BLK), BF16),
+                pltpu.VMEM((per_step, KV // PAIR, keys, 2 * GROUP * BLK), BF16),
                 pltpu.VMEM((entries * BLK, 2 * KV), BF16),
                 pltpu.VMEM((entries * BLK, 2 * KV), BF16),
                 pltpu.SemaphoreType.DMA((entries,)),
@@ -245,16 +287,19 @@
         grad += ref[...].astype(F32)
     grad = grad.astype(BF16)
     total = dot_nt(grad[:, :KV], wk_ref[...]) + dot_nt(grad[:, KV:], wv_ref[...])
-    out_ref[...] = (term_ref[...] + total).astype(BF16)
-
-
-def finish(parts, term, w_key, w_value):
+    out_ref[...] = (term_ref[...] + total).astype(out_ref.dtype)
+
+
+def finish(parts, term, w_key, w_value, kind, flops):
     return pl.pallas_call(
         functools.partial(finish_kernel, len(parts)),
         in_specs=[WHOLE] * (len(parts) + 3),
         out_specs=WHOLE,
-        out_shape=jax.ShapeDtypeStruct(term.shape, BF16),
+        out_shape=jax.ShapeDtypeStruct(term.shape, kind),
         compiler_params=params(24),
+        cost_estimate=pl.CostEstimate(
+            flops=flops, bytes_accessed=4 * term.size, transcendentals=0
+        ),
         name="finish",
     )(*parts, term, w_key, w_value)
 
@@ -342,9 +387,9 @@
     picked = jnp.maximum(wanted[:, CAP:], 0)
 
     mine = project(tokens, w_key, w_value).reshape(block_count, BLK, 2 * KV)
-    far_tile = swap(mine, 2, 1)
     next_tile = swap(mine, 1, 1)
     own_tile = swap(mine, 0, 1)
+    far_tile = swap(after(mine, own_tile), 2, 1)
     own = spread(pack(picked[0], own_tile))
     beside = spread(pack(picked[1], next_tile), own)
     last_tile = swap(after(far_tile, own[-1]), 1, 0)
@@ -364,7 +409,7 @@
         query_grad, w_query, (((0,), (1,)), ((), ())), preferred_element_type=F32
     )
     last = spread(back[3][1:])
-    far = spread(back[2][1:], last)
+    far = spread(back[2][1:])
     beside = spread(back[1][1:], far)
     last_sum = swap(owner_sum(wanted[3], [back[3][0], *last], block_count), 1, 0)
     far_sum = owner_sum(wanted[2], [back[2][0], *far], block_count, last_sum)
@@ -372,8 +417,10 @@
     next_sum = owner_sum(wanted[1], [back[1][0], *beside], block_count)
     *own, query_term, layer_out = lax.optimization_barrier((*own, query_term, layer_out))
     own_sum = owner_sum(wanted[0], [back[0][0], *own], block_count)
-    sums = [swap(far_sum, 2, 1), swap(next_sum, 1, 1), swap(own_sum, 0, 1)]
-    input_grad = finish([x.reshape(rows, 2 * KV) for x in sums], query_term, w_key, w_value)
+    far_grad = swap(far_sum, 2, 1).reshape(rows, 2 * KV)
+    near_grads = [x.reshape(rows, 2 * KV) for x in (swap(next_sum, 1, 1), swap(own_sum, 0, 1))]
+    query_term = finish([far_grad], query_term, w_key, w_value, F32, FAR_FLOPS)
+    input_grad = finish(near_grads, query_term, w_key, w_value, BF16, 800_000_000)
     return (layer_out[None], input_grad[None])
 
 

time: 165 us -> 160 us (0.970)
  the two profiles are of different devices: /device:TPU:12 before, /device:TPU:0 now
where the time goes in v10:
time: 160 us
  waiting for transfers between devices  75.8 us (47%)
  starting transfers between devices  39.1 us (24%)
  Pallas kernels  29.3 us (18%)
  matrix products  7.74 us (5%)
  local copies, waits for them, and re-layouts  3.79 us (2%)
  other arithmetic  2.88 us (2%)
    ppermute x24, waiting for transfers between devices, spread(): moved.append(lax.ppermute(value, 'tile', pairs))  44.7 us
    ppermute x24, starting transfers between devices, spread(): moved.append(lax.ppermute(value, 'tile', pairs))  33.2 us
    ppermute x8, waiting for transfers between devices, swap(): return lax.ppermute(value, ('vintage', 'tile'), pairs)  31.1 us
    pallas_call x1, Pallas kernels, attention(): pl.pallas_call(functools.partial(attention_kernel, list_len, per_step), g...  17.3 us
    ppermute x8, starting transfers between devices, swap(): return lax.ppermute(value, ('vintage', 'tile'), pairs)  5.84 us
    dot_general x1, matrix products, dot_nt(): lax.dot_general(a, b, (((1,), (1,)), ((), ())), preferred_element_type=F32)  3.52 us
    pallas_call x4, Pallas kernels, owner_sum(): pl.pallas_call(functools.partial(owner_kernel, len(parts)), in_specs=[pl....  3.4 us
    pallas_call x1, Pallas kernels, project(): pl.pallas_call(project_kernel, in_specs=[pl.BlockSpec(memory_space=pl.ANY...  3.27 us
  transfers between devices with their start and end apart: 32, of which 20 were waited for; matrix products, arithmetic and copies ran while one was open for 8% of the time, Pallas kernels for 4%

profile of v10, /device:TPU:0, one launch (start us, length us, event | category | flops | bytes accessed | tf_op | source)
XLA Modules:
  0.0 159.6 jit_solution(7386255917389029240)
XLA Ops:
  0.7 3.3 %project.1 = bf16[512,512]{1,0:T(8,128)(2,1)} custom-call(bf16[512,768]{1,0:T(8,128)(2,1)} %bitcast.52, bf16[768,256]{1,0:T(8,128)(2,1)} %refs_3_.3, bf16[768,256]{1,0:T(8,128)(2,1)} %refs_4_.1), custom_call_target="tpu_custom_call" | custom-call | tf_op jit(solution)/shard_map/project/pallas_call | solution.py:252
  3.9 2.5 %collective-permute-start.4 = (bf16[4,128,512]{2,1,0:T(8,128)(2,1)}, bf16[4,128,512]{2,1,0:T(8,128)(2,1)S(1)}, u32[]{:S(2)}, u32[]{:S(2)}) collective-permute-start(bf16[4,128,512]{2,1,0:T(8,128)(2,1)} %bitcast.53), channel_id=1, source_target_pairs={{0,20},{1,21},{2,22},{3,23},{4,16},{5,17},{6,18},{7,19},{8,28},{9,... | collective-permute-start | bytes 1572872 | tf_op jit(solution)/shard_map/ppermute | solution.py:352
  9.9 2.3 %collective-permute-start.8 = (bf16[4,128,512]{2,1,0:T(8,128)(2,1)}, bf16[4,128,512]{2,1,0:T(8,128)(2,1)S(1)}, u32[]{:S(2)}, u32[]{:S(2)}) collective-permute-start(bf16[4,128,512]{2,1,0:T(8,128)(2,1)} %bitcast.55), channel_id=1, source_target_pairs={{0,24},{1,25},{2,26},{3,27},{4,28},{5,29},{6,30},{7,31},{8,16},{9,... | collective-permute-start | bytes 1572872 | tf_op jit(solution)/shard_map/ppermute | solution.py:352
  13.0 2.5 %collective-permute-start.3 = (bf16[2,128,512]{2,1,0:T(8,128)(2,1)S(1)}, bf16[2,128,512]{2,1,0:T(8,128)(2,1)S(1)}, u32[]{:S(2)}, u32[]{:S(2)}) collective-permute-start(bf16[2,128,512]{2,1,0:T(8,128)(2,1)S(1)} %get-tuple-element.59), channel_id=1, source_target_pairs={{0,3},{1,2},{2,1},{3,0},{4,7},{5,6},{6,5},{7,4},{8,11},{9,10},{10,... | collective-permute-start | bytes 786440 | tf_op jit(solution)/shard_map/ppermute | solution.py:363
  16.5 9.7 %collective-permute-done.4.tile_ref.refs_4_ = bf16[4,128,512]{2,1,0:T(8,128)(2,1)S(1)} collective-permute-done((bf16[4,128,512]{2,1,0:T(8,128)(2,1)}, bf16[4,128,512]{2,1,0:T(8,128)(2,1)S(1)}, u32[]{:S(2)}, u32[]{:S(2)}) %collective-permute-start.4) | collective-permute-done | bytes 524320 | tf_op jit(solution)/shard_map/ppermute | solution.py:352
  26.3 1.4 pack.5
  27.7 3.9 %collective-permute-start.7 = (bf16[2,128,512]{2,1,0:T(8,128)(2,1)}, bf16[2,128,512]{2,1,0:T(8,128)(2,1)}, u32[]{:S(2)}, u32[]{:S(2)}) collective-permute-start(bf16[2,128,512]{2,1,0:T(8,128)(2,1)} %get-tuple-element.65), channel_id=1, source_target_pairs={{0,3},{1,2},{2,1},{3,0},{4,7},{5,6},{6,5},{7,4},{8,11},{9,10},{10,... | collective-permute-start | bytes 786440 | tf_op jit(solution)/shard_map/ppermute | solution.py:363
  32.3 4.0 %collective-permute-done.8.tile_ref.refs_8_ = bf16[4,128,512]{2,1,0:T(8,128)(2,1)S(1)} collective-permute-done((bf16[4,128,512]{2,1,0:T(8,128)(2,1)}, bf16[4,128,512]{2,1,0:T(8,128)(2,1)S(1)}, u32[]{:S(2)}, u32[]{:S(2)}) %collective-permute-start.8) | collective-permute-done | bytes 524320 | tf_op jit(solution)/shard_map/ppermute | solution.py:352
  36.4 1.3 compare_select_fusion.3
  39.0 3.0 %collective-permute-start.11 = (bf16[2,128,512]{2,1,0:T(8,128)(2,1)S(1)}, bf16[2,128,512]{2,1,0:T(8,128)(2,1)S(1)}, u32[]{:S(2)}, u32[]{:S(2)}) collective-permute-start(bf16[2,128,512]{2,1,0:T(8,128)(2,1)S(1)} %get-tuple-element.73), channel_id=1, source_target_pairs={{0,3},{1,2},{2,1},{3,0},{4,7},{5,6},{6,5},{7,4},{8,11},{9,10},{10,... | collective-permute-start | bytes 786440 | tf_op jit(solution)/shard_map/ppermute | solution.py:363
  42.0 2.6 %collective-permute-done.6.refs_6_ = bf16[2,128,512]{2,1,0:T(8,128)(2,1)} collective-permute-done((bf16[2,128,512]{2,1,0:T(8,128)(2,1)}, bf16[2,128,512]{2,1,0:T(8,128)(2,1)}, u32[]{:S(2)}, u32[]{:S(2)}) %collective-permute-start.6) | collective-permute-done | bytes 262176 | tf_op jit(solution)/shard_map/ppermute | solution.py:363
  44.6 2.0 %collective-permute-start.10 = (bf16[2,128,512]{2,1,0:T(8,128)(2,1)S(1)}, bf16[2,128,512]{2,1,0:T(8,128)(2,1)S(1)}, u32[]{:S(2)}, u32[]{:S(2)}) collective-permute-start(bf16[2,128,512]{2,1,0:T(8,128)(2,1)S(1)} %get-tuple-element.71), channel_id=1, source_target_pairs={{0,2},{1,3},{2,0},{3,1},{4,6},{5,7},{6,4},{7,5},{8,10},{9,11},{10,... | collective-permute-start | bytes 786440 | tf_op jit(solution)/shard_map/ppermute | solution.py:363
  46.7 3.5 %fusion.ng_ref = f32[768,512]{1,0:T(8,128)} fusion(bf16[768,768]{1,0:T(8,128)(2,1)} %param.13, bf16[1,512,768]{2,1,0:T(8,128)(2,1)} %param.9), kind=kOutput, calls=%fused_computation.3 | convolution fusion | flops 603979776 | bytes 3538944 | tf_op jit(solution)/shard_map/dot_general | solution.py:33
  51.3 2.5 %collective-permute-start.15 = (bf16[2,128,512]{2,1,0:T(8,128)(2,1)S(1)}, bf16[2,128,512]{2,1,0:T(8,128)(2,1)S(1)}, u32[]{:S(2)}, u32[]{:S(2)}) collective-permute-start(bf16[2,128,512]{2,1,0:T(8,128)(2,1)S(1)} %get-tuple-element.79), channel_id=1, source_target_pairs={{0,3},{1,2},{2,1},{3,0},{4,7},{5,6},{6,5},{7,4},{8,11},{9,10},{10,... | collective-permute-start | bytes 786440 | tf_op jit(solution)/shard_map/ppermute | solution.py:363
  53.8 1.9 %collective-permute-done.10.refs_10_ = bf16[2,128,512]{2,1,0:T(8,128)(2,1)S(1)} collective-permute-done((bf16[2,128,512]{2,1,0:T(8,128)(2,1)S(1)}, bf16[2,128,512]{2,1,0:T(8,128)(2,1)S(1)}, u32[]{:S(2)}, u32[]{:S(2)}) %collective-permute-start.10) | collective-permute-done | bytes 262176 | tf_op jit(solution)/shard_map/ppermute | solution.py:363
  55.7 2.1 %collective-permute-start.14 = (bf16[2,128,512]{2,1,0:T(8,128)(2,1)S(1)}, bf16[2,128,512]{2,1,0:T(8,128)(2,1)S(1)}, u32[]{:S(2)}, u32[]{:S(2)}) collective-permute-start(bf16[2,128,512]{2,1,0:T(8,128)(2,1)S(1)} %get-tuple-element.77), channel_id=1, source_target_pairs={{0,2},{1,3},{2,0},{3,1},{4,6},{5,7},{6,4},{7,5},{8,10},{9,11},{10,... | collective-permute-start | bytes 786440 | tf_op jit(solution)/shard_map/ppermute | solution.py:363
  57.8 1.5 collective-permute-start.13
  59.3 1.7 %convolution_convert_fusion.1.q_ref = bf16[768,512]{1,0:T(8,128)(2,1)} fusion(bf16[768,768]{1,0:T(8,128)(2,1)S(1)} %copy-done, bf16[1,512,768]{2,1,0:T(8,128)(2,1)S(1)} %copy-done.11), kind=kOutput, calls=%fused_computation.2 | convolution fusion | flops 604372992 | bytes 2752512 | tf_op jit(solution)/shard_map/dot_general | solution.py:399
  61.6 5.1 %collective-permute-done.14.refs_14_ = bf16[2,128,512]{2,1,0:T(8,128)(2,1)S(1)} collective-permute-done((bf16[2,128,512]{2,1,0:T(8,128)(2,1)S(1)}, bf16[2,128,512]{2,1,0:T(8,128)(2,1)S(1)}, u32[]{:S(2)}, u32[]{:S(2)}) %collective-permute-start.14) | collective-permute-done | bytes 262176 | tf_op jit(solution)/shard_map/ppermute | solution.py:363
  67.7 17.3 %attention.1 = (bf16[768,512]{1,0:T(8,128)(2,1)}, bf16[768,512]{1,0:T(8,128)(2,1)}, bf16[2,128,512]{2,1,0:T(8,128)(2,1)}, bf16[2,128,512]{2,1,0:T(8,128)(2,1)}, ...) custom-call(s32[16]{0:T(128)} %get-tuple-element.121.get_ref, ...), custom_call_target="tpu_custom_call" | custom-call | flops 2415919104 | bytes 6291456 | tf_op jit(solution)/shard_map/attention/pallas_call | solution.py:211
  84.9 1.6 %collective-permute-start.19 = (bf16[2,128,512]{2,1,0:T(8,128)(2,1)}, bf16[2,128,512]{2,1,0:T(8,128)(2,1)S(1)}, u32[]{:S(2)}, u32[]{:S(2)}) collective-permute-start(bf16[2,128,512]{2,1,0:T(8,128)(2,1)} %get-tuple-element.86), channel_id=1, source_target_pairs={{0,1},{1,0},{2,3},{3,2},{4,5},{5,4},{6,7},{7,6},{8,9},{9,8},{10,11... | collective-permute-start | bytes 786440 | tf_op jit(solution)/shard_map/ppermute | solution.py:363
  86.6 1.5 collective-permute-start.20
  88.7 5.7 %collective-permute-done.19.refs_1_ = bf16[2,128,512]{2,1,0:T(8,128)(2,1)S(1)} collective-permute-done((bf16[2,128,512]{2,1,0:T(8,128)(2,1)}, bf16[2,128,512]{2,1,0:T(8,128)(2,1)S(1)}, u32[]{:S(2)}, u32[]{:S(2)}) %collective-permute-start.19) | collective-permute-done | bytes 262176 | tf_op jit(solution)/shard_map/ppermute | solution.py:363
  94.4 6.0 %collective-permute-done.20.refs_2_ = bf16[2,128,512]{2,1,0:T(8,128)(2,1)S(1)} collective-permute-done((bf16[2,128,512]{2,1,0:T(8,128)(2,1)}, bf16[2,128,512]{2,1,0:T(8,128)(2,1)S(1)}, u32[]{:S(2)}, u32[]{:S(2)}) %collective-permute-start.20) | collective-permute-done | bytes 262176 | tf_op jit(solution)/shard_map/ppermute | solution.py:363
  100.4 0.9 copy-done.10
  101.3 0.8 owner_sum.4
  102.2 1.3 collective-permute-start.16
  103.5 0.8 collective-permute-start.17
  104.3 1.5 collective-permute-start.18
  106.3 5.4 %collective-permute-done.16.refs_1_ = bf16[2,128,512]{2,1,0:T(8,128)(2,1)S(1)} collective-permute-done((bf16[2,128,512]{2,1,0:T(8,128)(2,1)}, bf16[2,128,512]{2,1,0:T(8,128)(2,1)S(1)}, u32[]{:S(2)}, u32[]{:S(2)}) %collective-permute-start.16) | collective-permute-done | bytes 262176 | tf_op jit(solution)/shard_map/ppermute | solution.py:363
  111.7 1.2 collective-permute-start.23
  112.9 2.8 %collective-permute-done.17.refs_2_ = bf16[2,128,512]{2,1,0:T(8,128)(2,1)S(1)} collective-permute-done((bf16[2,128,512]{2,1,0:T(8,128)(2,1)}, bf16[2,128,512]{2,1,0:T(8,128)(2,1)S(1)}, u32[]{:S(2)}, u32[]{:S(2)}) %collective-permute-start.17) | collective-permute-done | bytes 262176 | tf_op jit(solution)/shard_map/ppermute | solution.py:363
  115.7 1.0 collective-permute-start.25
  116.7 1.6 collective-permute-done.18.refs_3_
  118.3 1.2 collective-permute-start.27
  119.5 0.9 owner_sum.5
  120.6 0.8 fusion.18.refs_1_
  121.4 6.1 %collective-permute-done.27.refs_3_ = bf16[2,128,512]{2,1,0:T(8,128)(2,1)S(1)} collective-permute-done((bf16[2,128,512]{2,1,0:T(8,128)(2,1)}, bf16[2,128,512]{2,1,0:T(8,128)(2,1)S(1)}, u32[]{:S(2)}, u32[]{:S(2)}) %collective-permute-start.27) | collective-permute-done | bytes 262176 | tf_op jit(solution)/shard_map/ppermute | solution.py:363
  128.3 1.9 %collective-permute-start.26 = (bf16[2,128,512]{2,1,0:T(8,128)(2,1)S(1)}, bf16[2,128,512]{2,1,0:T(8,128)(2,1)S(1)}, u32[]{:S(2)}, u32[]{:S(2)}) collective-permute-start(bf16[2,128,512]{2,1,0:T(8,128)(2,1)S(1)} %copy-done.18), channel_id=1, source_target_pairs={{0,2},{1,3},{2,0},{3,1},{4,6},{5,7},{6,4},{7,5},{8,10},{9,11},{10,... | collective-permute-start | bytes 786440 | tf_op jit(solution)/shard_map/ppermute | solution.py:363
  130.2 1.3 collective-permute-start.28
  131.5 1.7 %convolution_convert_fusion = bf16[512,768]{1,0:T(8,128)(2,1)} fusion(bf16[768,512]{1,0:T(8,128)(2,1)S(1)} %copy-done.30, bf16[768,768]{1,0:T(8,128)(2,1)S(1)} %copy-done.15), kind=kOutput, calls=%fused_computation.1 | convolution fusion | flops 604372992 | bytes 2752512 | tf_op jit(solution)/shard_map/dot_general | solution.py:37
  133.2 0.9 owner_sum.6
  134.1 2.4 %collective-permute-done.24.refs_1_ = bf16[2,128,512]{2,1,0:T(8,128)(2,1)S(1)} collective-permute-done((bf16[2,128,512]{2,1,0:T(8,128)(2,1)S(1)}, bf16[2,128,512]{2,1,0:T(8,128)(2,1)S(1)}, u32[]{:S(2)}, u32[]{:S(2)}) %collective-permute-start.24) | collective-permute-done | bytes 262176 | tf_op jit(solution)/shard_map/ppermute | solution.py:363
  136.5 3.2 %collective-permute-done.26.refs_2_ = bf16[2,128,512]{2,1,0:T(8,128)(2,1)S(1)} collective-permute-done((bf16[2,128,512]{2,1,0:T(8,128)(2,1)S(1)}, bf16[2,128,512]{2,1,0:T(8,128)(2,1)S(1)}, u32[]{:S(2)}, u32[]{:S(2)}) %collective-permute-start.26) | collective-permute-done | bytes 262176 | tf_op jit(solution)/shard_map/ppermute | solution.py:363
  139.7 0.8 owner_sum.7
  140.6 6.1 %collective-permute-done.31 = bf16[4,128,512]{2,1,0:T(8,128)(2,1)S(1)} collective-permute-done((bf16[4,128,512]{2,1,0:T(8,128)(2,1)S(1)}, bf16[4,128,512]{2,1,0:T(8,128)(2,1)S(1)}, u32[]{:S(2)}, u32[]{:S(2)}) %collective-permute-start.31) | collective-permute-done | bytes 524320 | tf_op jit(solution)/shard_map/ppermute | solution.py:352
  147.3 10.8 %collective-permute-done.29 = bf16[4,128,512]{2,1,0:T(8,128)(2,1)S(1)} collective-permute-done((bf16[4,128,512]{2,1,0:T(8,128)(2,1)S(1)}, bf16[4,128,512]{2,1,0:T(8,128)(2,1)S(1)}, u32[]{:S(2)}, u32[]{:S(2)}) %collective-permute-start.29) | collective-permute-done | bytes 524320 | tf_op jit(solution)/shard_map/ppermute | solution.py:352
  158.1 1.5 finish.3
  (122 shorter events, 12.9 us)
Async XLA Ops:
  0.6 58.7 %copy-start = (bf16[768,768]{1,0:T(8,128)(2,1)S(1)}, bf16[768,768]{1,0:T(8,128)(2,1)}, u32[]{:S(2)}) copy-start(bf16[768,768]{1,0:T(8,128)(2,1)} %param.10) | copy-start | bytes 3538948
  3.9 22.3 %collective-permute-start.4 = (bf16[4,128,512]{2,1,0:T(8,128)(2,1)}, bf16[4,128,512]{2,1,0:T(8,128)(2,1)S(1)}, u32[]{:S(2)}, u32[]{:S(2)}) collective-permute-start(bf16[4,128,512]{2,1,0:T(8,128)(2,1)} %bitcast.53), channel_id=1, source_target_pairs={{0,20},{1,21},{2,22},{3,23},{4,16},{5,17},{6,18},{7,19},{8,28},{9,... | collective-permute-start | bytes 1572872 | tf_op jit(solution)/shard_map/ppermute | solution.py:352
  6.5 3.4 %collective-permute-start = (bf16[4,128,512]{2,1,0:T(8,128)(2,1)}, bf16[4,128,512]{2,1,0:T(8,128)(2,1)S(1)}, u32[]{:S(2)}, u32[]{:S(2)}) collective-permute-start(bf16[4,128,512]{2,1,0:T(8,128)(2,1)} %bitcast.54), channel_id=1, source_target_pairs={{0,16},{1,17},{2,18},{3,19},{4,20},{5,21},{6,22},{7,23},{8,24},{9,... | collective-permute-start | bytes 1572872 | tf_op jit(solution)/shard_map/ppermute | solution.py:352
  9.9 40.4 %copy-start.4 = (bf16[4,128,512]{2,1,0:T(8,128)(2,1)}, bf16[4,128,512]{2,1,0:T(8,128)(2,1)S(1)}, u32[]{:S(2)}) copy-start(bf16[4,128,512]{2,1,0:T(8,128)(2,1)S(1)} %collective-permute-done.tile_ref.refs_0_) | copy-start | bytes 1572868
  9.9 26.4 %collective-permute-start.8 = (bf16[4,128,512]{2,1,0:T(8,128)(2,1)}, bf16[4,128,512]{2,1,0:T(8,128)(2,1)S(1)}, u32[]{:S(2)}, u32[]{:S(2)}) collective-permute-start(bf16[4,128,512]{2,1,0:T(8,128)(2,1)} %bitcast.55), channel_id=1, source_target_pairs={{0,24},{1,25},{2,26},{3,27},{4,28},{5,29},{6,30},{7,31},{8,16},{9,... | collective-permute-start | bytes 1572872 | tf_op jit(solution)/shard_map/ppermute | solution.py:352
  13.0 14.7 %collective-permute-start.3 = (bf16[2,128,512]{2,1,0:T(8,128)(2,1)S(1)}, bf16[2,128,512]{2,1,0:T(8,128)(2,1)S(1)}, u32[]{:S(2)}, u32[]{:S(2)}) collective-permute-start(bf16[2,128,512]{2,1,0:T(8,128)(2,1)S(1)} %get-tuple-element.59), channel_id=1, source_target_pairs={{0,3},{1,2},{2,1},{3,0},{4,7},{5,6},{6,5},{7,4},{8,11},{9,10},{10,... | collective-permute-start | bytes 786440 | tf_op jit(solution)/shard_map/ppermute | solution.py:363
  15.5 16.1 %collective-permute-start.2 = (bf16[2,128,512]{2,1,0:T(8,128)(2,1)S(1)}, bf16[2,128,512]{2,1,0:T(8,128)(2,1)S(1)}, u32[]{:S(2)}, u32[]{:S(2)}) collective-permute-start(bf16[2,128,512]{2,1,0:T(8,128)(2,1)S(1)} %get-tuple-element.58), channel_id=1, source_target_pairs={{0,2},{1,3},{2,0},{3,1},{4,6},{5,7},{6,4},{7,5},{8,10},{9,11},{10,... | collective-permute-start | bytes 786440 | tf_op jit(solution)/shard_map/ppermute | solution.py:363
  16.0 16.1 %collective-permute-start.1 = (bf16[2,128,512]{2,1,0:T(8,128)(2,1)S(1)}, bf16[2,128,512]{2,1,0:T(8,128)(2,1)S(1)}, u32[]{:S(2)}, u32[]{:S(2)}) collective-permute-start(bf16[2,128,512]{2,1,0:T(8,128)(2,1)S(1)} %get-tuple-element.57), channel_id=1, source_target_pairs={{0,1},{1,0},{2,3},{3,2},{4,5},{5,4},{6,7},{7,6},{8,9},{9,8},{10,11... | collective-permute-start | bytes 786440 | tf_op jit(solution)/shard_map/ppermute | solution.py:363
  26.3 24.0 %copy-start.3 = (bf16[4,128,512]{2,1,0:T(8,128)(2,1)}, bf16[4,128,512]{2,1,0:T(8,128)(2,1)S(1)}, u32[]{:S(2)}) copy-start(bf16[4,128,512]{2,1,0:T(8,128)(2,1)S(1)} %collective-permute-done.4.tile_ref.refs_4_) | copy-start | bytes 1572868
  27.7 8.6 %copy-start.17 = (bf16[2,128,512]{2,1,0:T(8,128)(2,1)}, bf16[2,128,512]{2,1,0:T(8,128)(2,1)S(1)}, u32[]{:S(2)}) copy-start(bf16[2,128,512]{2,1,0:T(8,128)(2,1)S(1)} %collective-permute-done.3.refs_3_) | copy-start | bytes 786436
  27.7 11.3 %collective-permute-start.7 = (bf16[2,128,512]{2,1,0:T(8,128)(2,1)}, bf16[2,128,512]{2,1,0:T(8,128)(2,1)}, u32[]{:S(2)}, u32[]{:S(2)}) collective-permute-start(bf16[2,128,512]{2,1,0:T(8,128)(2,1)} %get-tuple-element.65), channel_id=1, source_target_pairs={{0,3},{1,2},{2,1},{3,0},{4,7},{5,6},{6,5},{7,4},{8,11},{9,10},{10,... | collective-permute-start | bytes 786440 | tf_op jit(solution)/shard_map/ppermute | solution.py:363
  31.6 13.0 %collective-permute-start.6 = (bf16[2,128,512]{2,1,0:T(8,128)(2,1)}, bf16[2,128,512]{2,1,0:T(8,128)(2,1)}, u32[]{:S(2)}, u32[]{:S(2)}) collective-permute-start(bf16[2,128,512]{2,1,0:T(8,128)(2,1)} %get-tuple-element.63), channel_id=1, source_target_pairs={{0,2},{1,3},{2,0},{3,1},{4,6},{5,7},{6,4},{7,5},{8,10},{9,11},{10,... | collective-permute-start | bytes 786440 | tf_op jit(solution)/shard_map/ppermute | solution.py:363
  32.1 14.5 %collective-permute-start.5 = (bf16[2,128,512]{2,1,0:T(8,128)(2,1)S(1)}, bf16[2,128,512]{2,1,0:T(8,128)(2,1)}, u32[]{:S(2)}, u32[]{:S(2)}) collective-permute-start(bf16[2,128,512]{2,1,0:T(8,128)(2,1)S(1)} %get-tuple-element.61), channel_id=1, source_target_pairs={{0,1},{1,0},{2,3},{3,2},{4,5},{5,4},{6,7},{7,6},{8,9},{9,8},{10,11... | collective-permute-start | bytes 786440 | tf_op jit(solution)/shard_map/ppermute | solution.py:363
  36.3 13.9 %copy-start.5 = (bf16[4,128,512]{2,1,0:T(8,128)(2,1)}, bf16[4,128,512]{2,1,0:T(8,128)(2,1)S(1)}, u32[]{:S(2)}) copy-start(bf16[4,128,512]{2,1,0:T(8,128)(2,1)S(1)} %collective-permute-done.8.tile_ref.refs_8_) | copy-start | bytes 1572868
  36.3 14.4 %collective-permute-start.12 = (bf16[4,128,512]{2,1,0:T(8,128)(2,1)S(1)}, bf16[4,128,512]{2,1,0:T(8,128)(2,1)S(1)}, u32[]{:S(2)}, u32[]{:S(2)}) collective-permute-start(bf16[4,128,512]{2,1,0:T(8,128)(2,1)S(1)} %collective-permute-done.8.tile_ref.refs_8_), channel_id=1, source_target_pairs={{0,4},{1,5},{2,6},{3,7},{4,0},{5,1},{6,2},{7,3},{8,12},{9,13},{10,... | collective-permute-start | bytes 1572872 | tf_op jit(solution)/shard_map/ppermute | solution.py:352
  39.0 12.3 %collective-permute-start.11 = (bf16[2,128,512]{2,1,0:T(8,128)(2,1)S(1)}, bf16[2,128,512]{2,1,0:T(8,128)(2,1)S(1)}, u32[]{:S(2)}, u32[]{:S(2)}) collective-permute-start(bf16[2,128,512]{2,1,0:T(8,128)(2,1)S(1)} %get-tuple-element.73), channel_id=1, source_target_pairs={{0,3},{1,2},{2,1},{3,0},{4,7},{5,6},{6,5},{7,4},{8,11},{9,10},{10,... | collective-permute-start | bytes 786440 | tf_op jit(solution)/shard_map/ppermute | solution.py:363
  44.6 11.2 %collective-permute-start.10 = (bf16[2,128,512]{2,1,0:T(8,128)(2,1)S(1)}, bf16[2,128,512]{2,1,0:T(8,128)(2,1)S(1)}, u32[]{:S(2)}, u32[]{:S(2)}) collective-permute-start(bf16[2,128,512]{2,1,0:T(8,128)(2,1)S(1)} %get-tuple-element.71), channel_id=1, source_target_pairs={{0,2},{1,3},{2,0},{3,1},{4,6},{5,7},{6,4},{7,5},{8,10},{9,11},{10,... | collective-permute-start | bytes 786440 | tf_op jit(solution)/shard_map/ppermute | solution.py:363
  46.6 12.7 %copy-start.11 = (bf16[1,512,768]{2,1,0:T(8,128)(2,1)S(1)}, bf16[1,512,768]{2,1,0:T(8,128)(2,1)}, u32[]{:S(2)}) copy-start(bf16[1,512,768]{2,1,0:T(8,128)(2,1)} %param.8) | copy-start | bytes 2359300
  46.6 11.2 %collective-permute-start.9 = (bf16[2,128,512]{2,1,0:T(8,128)(2,1)S(1)}, bf16[2,128,512]{2,1,0:T(8,128)(2,1)S(1)}, u32[]{:S(2)}, u32[]{:S(2)}) collective-permute-start(bf16[2,128,512]{2,1,0:T(8,128)(2,1)S(1)} %get-tuple-element.69), channel_id=1, source_target_pairs={{0,1},{1,0},{2,3},{3,2},{4,5},{5,4},{6,7},{7,6},{8,9},{9,8},{10,11... | collective-permute-start | bytes 786440 | tf_op jit(solution)/shard_map/ppermute | solution.py:363
  50.7 10.3 %copy-start.6 = (bf16[4,128,512]{2,1,0:T(8,128)(2,1)}, bf16[4,128,512]{2,1,0:T(8,128)(2,1)S(1)}, u32[]{:S(2)}) copy-start(bf16[4,128,512]{2,1,0:T(8,128)(2,1)S(1)} %collective-permute-done.12.tile_ref.refs_12_) | copy-start | bytes 1572868
  51.3 9.7 %copy-start.23 = (bf16[2,128,512]{2,1,0:T(8,128)(2,1)}, bf16[2,128,512]{2,1,0:T(8,128)(2,1)S(1)}, u32[]{:S(2)}) copy-start(bf16[2,128,512]{2,1,0:T(8,128)(2,1)S(1)} %collective-permute-done.11.refs_11_) | copy-start | bytes 786436
  51.3 10.3 %collective-permute-start.15 = (bf16[2,128,512]{2,1,0:T(8,128)(2,1)S(1)}, bf16[2,128,512]{2,1,0:T(8,128)(2,1)S(1)}, u32[]{:S(2)}, u32[]{:S(2)}) collective-permute-start(bf16[2,128,512]{2,1,0:T(8,128)(2,1)S(1)} %get-tuple-element.79), channel_id=1, source_target_pairs={{0,3},{1,2},{2,1},{3,0},{4,7},{5,6},{6,5},{7,4},{8,11},{9,10},{10,... | collective-permute-start | bytes 786440 | tf_op jit(solution)/shard_map/ppermute | solution.py:363
  55.7 11.0 %collective-permute-start.14 = (bf16[2,128,512]{2,1,0:T(8,128)(2,1)S(1)}, bf16[2,128,512]{2,1,0:T(8,128)(2,1)S(1)}, u32[]{:S(2)}, u32[]{:S(2)}) collective-permute-start(bf16[2,128,512]{2,1,0:T(8,128)(2,1)S(1)} %get-tuple-element.77), channel_id=1, source_target_pairs={{0,2},{1,3},{2,0},{3,1},{4,6},{5,7},{6,4},{7,5},{8,10},{9,11},{10,... | collective-permute-start | bytes 786440 | tf_op jit(solution)/shard_map/ppermute | solution.py:363
  57.8 9.2 %collective-permute-start.13 = (bf16[2,128,512]{2,1,0:T(8,128)(2,1)S(1)}, bf16[2,128,512]{2,1,0:T(8,128)(2,1)S(1)}, u32[]{:S(2)}, u32[]{:S(2)}) collective-permute-start(bf16[2,128,512]{2,1,0:T(8,128)(2,1)S(1)} %get-tuple-element.75), channel_id=1, source_target_pairs={{0,1},{1,0},{2,3},{3,2},{4,5},{5,4},{6,7},{7,6},{8,9},{9,8},{10,11... | collective-permute-start | bytes 786440 | tf_op jit(solution)/shard_map/ppermute | solution.py:363
  84.9 34.6 %copy-start.7 = (bf16[2,128,512]{2,1,0:T(8,128)(2,1)S(1)}, bf16[2,128,512]{2,1,0:T(8,128)(2,1)}, u32[]{:S(2)}) copy-start(bf16[2,128,512]{2,1,0:T(8,128)(2,1)} %get-tuple-element.81.refs_0_) | copy-start | bytes 786436
  84.9 9.5 %collective-permute-start.19 = (bf16[2,128,512]{2,1,0:T(8,128)(2,1)}, bf16[2,128,512]{2,1,0:T(8,128)(2,1)S(1)}, u32[]{:S(2)}, u32[]{:S(2)}) collective-permute-start(bf16[2,128,512]{2,1,0:T(8,128)(2,1)} %get-tuple-element.86), channel_id=1, source_target_pairs={{0,1},{1,0},{2,3},{3,2},{4,5},{5,4},{6,7},{7,6},{8,9},{9,8},{10,11... | collective-permute-start | bytes 786440 | tf_op jit(solution)/shard_map/ppermute | solution.py:363
  86.6 13.8 %collective-permute-start.20 = (bf16[2,128,512]{2,1,0:T(8,128)(2,1)}, bf16[2,128,512]{2,1,0:T(8,128)(2,1)S(1)}, u32[]{:S(2)}, u32[]{:S(2)}) collective-permute-start(bf16[2,128,512]{2,1,0:T(8,128)(2,1)} %get-tuple-element.87), channel_id=1, source_target_pairs={{0,2},{1,3},{2,0},{3,1},{4,6},{5,7},{6,4},{7,5},{8,10},{9,11},{10,... | collective-permute-start | bytes 786440 | tf_op jit(solution)/shard_map/ppermute | solution.py:363
  88.1 12.3 %collective-permute-start.21 = (bf16[2,128,512]{2,1,0:T(8,128)(2,1)}, bf16[2,128,512]{2,1,0:T(8,128)(2,1)S(1)}, u32[]{:S(2)}, u32[]{:S(2)}) collective-permute-start(bf16[2,128,512]{2,1,0:T(8,128)(2,1)} %get-tuple-element.88), channel_id=1, source_target_pairs={{0,3},{1,2},{2,1},{3,0},{4,7},{5,6},{6,5},{7,4},{8,11},{9,10},{10,... | collective-permute-start | bytes 786440 | tf_op jit(solution)/shard_map/ppermute | solution.py:363
  101.3 10.4 %copy-start.22 = (bf16[2,128,512]{2,1,0:T(8,128)(2,1)S(1)}, bf16[2,128,512]{2,1,0:T(8,128)(2,1)}, u32[]{:S(2)}) copy-start(bf16[2,128,512]{2,1,0:T(8,128)(2,1)} %get-tuple-element.91) | copy-start | bytes 786436
  102.1 17.4 %collective-permute-start.22 = (bf16[4,128,512]{2,1,0:T(8,128)(2,1)S(1)}, bf16[4,128,512]{2,1,0:T(8,128)(2,1)S(1)}, u32[]{:S(2)}, u32[]{:S(2)}) collective-permute-start(bf16[4,128,512]{2,1,0:T(8,128)(2,1)S(1)} %owner_sum.4), channel_id=1, source_target_pairs={{0,4},{1,5},{2,6},{3,7},{4,0},{5,1},{6,2},{7,3},{8,12},{9,13},{10,... | collective-permute-start | bytes 1572872 | tf_op jit(solution)/shard_map/ppermute | solution.py:352
  102.2 9.5 %collective-permute-start.16 = (bf16[2,128,512]{2,1,0:T(8,128)(2,1)}, bf16[2,128,512]{2,1,0:T(8,128)(2,1)S(1)}, u32[]{:S(2)}, u32[]{:S(2)}) collective-permute-start(bf16[2,128,512]{2,1,0:T(8,128)(2,1)} %get-tuple-element.82), channel_id=1, source_target_pairs={{0,1},{1,0},{2,3},{3,2},{4,5},{5,4},{6,7},{7,6},{8,9},{9,8},{10,11... | collective-permute-start | bytes 786440 | tf_op jit(solution)/shard_map/ppermute | solution.py:363
  103.5 12.3 %collective-permute-start.17 = (bf16[2,128,512]{2,1,0:T(8,128)(2,1)}, bf16[2,128,512]{2,1,0:T(8,128)(2,1)S(1)}, u32[]{:S(2)}, u32[]{:S(2)}) collective-permute-start(bf16[2,128,512]{2,1,0:T(8,128)(2,1)} %get-tuple-element.83), channel_id=1, source_target_pairs={{0,2},{1,3},{2,0},{3,1},{4,6},{5,7},{6,4},{7,5},{8,10},{9,11},{10,... | collective-permute-start | bytes 786440 | tf_op jit(solution)/shard_map/ppermute | solution.py:363
  104.3 14.0 %collective-permute-start.18 = (bf16[2,128,512]{2,1,0:T(8,128)(2,1)}, bf16[2,128,512]{2,1,0:T(8,128)(2,1)S(1)}, u32[]{:S(2)}, u32[]{:S(2)}) collective-permute-start(bf16[2,128,512]{2,1,0:T(8,128)(2,1)} %get-tuple-element.84), channel_id=1, source_target_pairs={{0,3},{1,2},{2,1},{3,0},{4,7},{5,6},{6,5},{7,4},{8,11},{9,10},{10,... | collective-permute-start | bytes 786440 | tf_op jit(solution)/shard_map/ppermute | solution.py:363
  106.3 14.2 %copy-start.29 = (bf16[768,512]{1,0:T(8,128)(2,1)S(1)}, bf16[768,512]{1,0:T(8,128)(2,1)}, u32[]{:S(2)}) copy-start(bf16[768,512]{1,0:T(8,128)(2,1)} %get-tuple-element.103) | copy-start | bytes 2359300
  111.7 16.2 %collective-permute-start.23 = (bf16[2,128,512]{2,1,0:T(8,128)(2,1)S(1)}, bf16[2,128,512]{2,1,0:T(8,128)(2,1)S(1)}, u32[]{:S(2)}, u32[]{:S(2)}) collective-permute-start(bf16[2,128,512]{2,1,0:T(8,128)(2,1)S(1)} %copy-done.22), channel_id=1, source_target_pairs={{0,1},{1,0},{2,3},{3,2},{4,5},{5,4},{6,7},{7,6},{8,9},{9,8},{10,11... | collective-permute-start | bytes 786440 | tf_op jit(solution)/shard_map/ppermute | solution.py:363
  115.7 12.2 %collective-permute-start.25 = (bf16[2,128,512]{2,1,0:T(8,128)(2,1)}, bf16[2,128,512]{2,1,0:T(8,128)(2,1)S(1)}, u32[]{:S(2)}, u32[]{:S(2)}) collective-permute-start(bf16[2,128,512]{2,1,0:T(8,128)(2,1)} %get-tuple-element.96), channel_id=1, source_target_pairs={{0,2},{1,3},{2,0},{3,1},{4,6},{5,7},{6,4},{7,5},{8,10},{9,11},{10,... | collective-permute-start | bytes 786440 | tf_op jit(solution)/shard_map/ppermute | solution.py:363
  118.3 9.2 %collective-permute-start.27 = (bf16[2,128,512]{2,1,0:T(8,128)(2,1)}, bf16[2,128,512]{2,1,0:T(8,128)(2,1)S(1)}, u32[]{:S(2)}, u32[]{:S(2)}) collective-permute-start(bf16[2,128,512]{2,1,0:T(8,128)(2,1)} %get-tuple-element.101), channel_id=1, source_target_pairs={{0,3},{1,2},{2,1},{3,0},{4,7},{5,6},{6,5},{7,4},{8,11},{9,10},{10,... | collective-permute-start | bytes 786440 | tf_op jit(solution)/shard_map/ppermute | solution.py:363
  120.4 26.2 %collective-permute-start.31 = (bf16[4,128,512]{2,1,0:T(8,128)(2,1)S(1)}, bf16[4,128,512]{2,1,0:T(8,128)(2,1)S(1)}, u32[]{:S(2)}, u32[]{:S(2)}) collective-permute-start(bf16[4,128,512]{2,1,0:T(8,128)(2,1)S(1)} %owner_sum.5), channel_id=1, source_target_pairs={{0,24},{1,25},{2,26},{3,27},{4,28},{5,29},{6,30},{7,31},{8,16},{9,... | collective-permute-start | bytes 1572872 | tf_op jit(solution)/shard_map/ppermute | solution.py:352
  120.6 9.6 %copy-start.16 = (bf16[2,128,512]{2,1,0:T(8,128)(2,1)S(1)}, bf16[2,128,512]{2,1,0:T(8,128)(2,1)}, u32[]{:S(2)}) copy-start(bf16[2,128,512]{2,1,0:T(8,128)(2,1)} %get-tuple-element.102) | copy-start | bytes 786436
  120.6 10.9 %copy-start.15 = (bf16[768,768]{1,0:T(8,128)(2,1)S(1)}, bf16[768,768]{1,0:T(8,128)(2,1)}, u32[]{:S(2)}) copy-start(bf16[768,768]{1,0:T(8,128)(2,1)} %param.13) | copy-start | bytes 3538948
  120.6 10.9 %copy-start.30 = (bf16[768,512]{1,0:T(8,128)(2,1)S(1)}, bf16[768,512]{1,0:T(8,128)(2,1)}, u32[]{:S(2)}) copy-start(bf16[768,512]{1,0:T(8,128)(2,1)} %get-tuple-element.104) | copy-start | bytes 2359300
  128.0 8.5 %collective-permute-start.24 = (bf16[2,128,512]{2,1,0:T(8,128)(2,1)S(1)}, bf16[2,128,512]{2,1,0:T(8,128)(2,1)S(1)}, u32[]{:S(2)}, u32[]{:S(2)}) collective-permute-start(bf16[2,128,512]{2,1,0:T(8,128)(2,1)S(1)} %copy-done.20), channel_id=1, source_target_pairs={{0,1},{1,0},{2,3},{3,2},{4,5},{5,4},{6,7},{7,6},{8,9},{9,8},{10,11... | collective-permute-start | bytes 786440 | tf_op jit(solution)/shard_map/ppermute | solution.py:363
  128.3 11.4 %collective-permute-start.26 = (bf16[2,128,512]{2,1,0:T(8,128)(2,1)S(1)}, bf16[2,128,512]{2,1,0:T(8,128)(2,1)S(1)}, u32[]{:S(2)}, u32[]{:S(2)}) collective-permute-start(bf16[2,128,512]{2,1,0:T(8,128)(2,1)S(1)} %copy-done.18), channel_id=1, source_target_pairs={{0,2},{1,3},{2,0},{3,1},{4,6},{5,7},{6,4},{7,5},{8,10},{9,11},{10,... | collective-permute-start | bytes 786440 | tf_op jit(solution)/shard_map/ppermute | solution.py:363
  130.2 9.5 %collective-permute-start.28 = (bf16[2,128,512]{2,1,0:T(8,128)(2,1)S(1)}, bf16[2,128,512]{2,1,0:T(8,128)(2,1)S(1)}, u32[]{:S(2)}, u32[]{:S(2)}) collective-permute-start(bf16[2,128,512]{2,1,0:T(8,128)(2,1)S(1)} %copy-done.16), channel_id=1, source_target_pairs={{0,3},{1,2},{2,1},{3,0},{4,7},{5,6},{6,5},{7,4},{8,11},{9,10},{10,... | collective-permute-start | bytes 786440 | tf_op jit(solution)/shard_map/ppermute | solution.py:363
  134.0 12.6 %copy-start.1 = (bf16[768,256]{1,0:T(8,128)(2,1)S(1)}, bf16[768,256]{1,0:T(8,128)(2,1)}, u32[]{:S(2)}) copy-start(bf16[768,256]{1,0:T(8,128)(2,1)} %refs_3_.3) | copy-start | bytes 1179652
  134.1 12.6 %copy-start.2 = (bf16[768,256]{1,0:T(8,128)(2,1)S(1)}, bf16[768,256]{1,0:T(8,128)(2,1)}, u32[]{:S(2)}) copy-start(bf16[768,256]{1,0:T(8,128)(2,1)} %refs_4_.1) | copy-start | bytes 1179652
  134.1 24.0 %collective-permute-start.29 = (bf16[4,128,512]{2,1,0:T(8,128)(2,1)S(1)}, bf16[4,128,512]{2,1,0:T(8,128)(2,1)S(1)}, u32[]{:S(2)}, u32[]{:S(2)}) collective-permute-start(bf16[4,128,512]{2,1,0:T(8,128)(2,1)S(1)} %owner_sum.6), channel_id=1, source_target_pairs={{0,20},{1,21},{2,22},{3,23},{4,16},{5,17},{6,18},{7,19},{8,28},{9,... | collective-permute-start | bytes 1572872 | tf_op jit(solution)/shard_map/ppermute | solution.py:352
  140.5 17.6 %collective-permute-start.30 = (bf16[4,128,512]{2,1,0:T(8,128)(2,1)S(1)}, bf16[4,128,512]{2,1,0:T(8,128)(2,1)S(1)}, u32[]{:S(2)}, u32[]{:S(2)}) collective-permute-start(bf16[4,128,512]{2,1,0:T(8,128)(2,1)S(1)} %owner_sum.7), channel_id=1, source_target_pairs={{0,16},{1,17},{2,18},{3,19},{4,20},{5,21},{6,22},{7,23},{8,24},{9,... | collective-permute-start | bytes 1572872 | tf_op jit(solution)/shard_map/ppermute | solution.py:352
  (15 other events, 64.1 us)

commit v11 on v10

--- a/solution.py
+++ b/solution.py
@@ -16,6 +16,7 @@
 KV = KV_HEADS * HEAD_DIM
 PAIR = 2 * HEAD_DIM
 CODE = 16
+FAR_SUM_FLOPS = 8_000_000_000
 FAR_FLOPS = 30_000_000_000
 MAJOR = 4
 TEMPER = HEAD_DIM ** (-0.5)
@@ -233,51 +234,107 @@
     )(gets, puts, queries, normed_grad, *arrived)
 
 
-def project_kernel(tokens_hbm, wk_hbm, wv_hbm, out_ref, tokens, wk, wv, sems):
-    moves = ((wk_hbm, wk), (tokens_hbm, tokens), (wv_hbm, wv))
-    copies = [pltpu.make_async_copy(src, dst, sems.at[i]) for i, (src, dst) in enumerate(moves)]
+def plan(plane, list_len, my_tile, tiles, picks, gets, puts, wanted, counts):
+    entries = gets.shape[0]
+    block_count = entries // list_len
+    my_row, my_place = lax.div(my_tile, plane), lax.rem(my_tile, plane)
+    spare = MAJOR * plane * CAP
+
+    def clear(i, carry):
+        wanted[i] = -1
+        return carry
+
+    lax.fori_loop(0, spare + 1, clear, 0)
+
+    def one_asker(p, carry):
+        asker = my_row * plane + (my_place ^ p)
+
+        def zero(t, carry):
+            counts[t] = 0
+            return carry
+
+        lax.fori_loop(0, counts.shape[0], zero, 0)
+        for e in range(entries):
+            row = asker * block_count + e // list_len
+            tile, pick = tiles[0, row, e % list_len], picks[0, row, e % list_len]
+            rank = counts[tile]
+            counts[tile] = rank + 1
+            group, column = lax.div(tile, plane) ^ my_row, lax.rem(tile, plane)
+            mine = column == my_place
+            wanted[jnp.where(mine, (group * plane + p) * CAP + rank, spare)] = pick
+
+            @pl.when(p == 0)
+            def _():
+                code = (group * plane + (column ^ my_place)) * CODE
+                puts[e] = code + rank
+                gets[e] = code + jnp.where(mine, pick, rank)
+
+        return carry
+
+    lax.fori_loop(0, plane, one_asker, 0)
+
+
+def project_kernel(
+    plane, list_len, my_tile, tiles, picks, tokens_hbm, wk_hbm, wv_hbm,
+    out_ref, gets, puts, wanted, tokens, wk, wv, counts, sems,
+):
+    copies = []
+    for src, dst, pieces in ((wk_hbm, wk, 2), (tokens_hbm, tokens, 4), (wv_hbm, wv, 2)):
+        size = src.shape[0] // pieces
+        for i in range(pieces):
+            part = pl.ds(i * size, size)
+            copies.append(
+                pltpu.make_async_copy(src.at[part], dst.at[part], sems.at[len(copies)])
+            )
     for copy in copies:
         copy.start()
-    copies[0].wait()
-    copies[1].wait()
+    plan(plane, list_len, my_tile[0], tiles, picks, gets, puts, wanted, counts)
+    for copy in copies[:6]:
+        copy.wait()
     keys = jnp.dot(tokens[...], wk[...], preferred_element_type=F32)
     out_ref[:, :KV] = keys.astype(BF16)
-    copies[2].wait()
+    for copy in copies[6:]:
+        copy.wait()
     values = jnp.dot(tokens[...], wv[...], preferred_element_type=F32)
     out_ref[:, KV:] = values.astype(BF16)
 
 
-def project(tokens, w_key, w_value):
+def project(plane, my_tile, key_tiles, key_blocks, tokens, w_key, w_value):
+    list_len = key_tiles.shape[2]
+    rows = tokens.shape[0]
+    entries = rows // BLK * list_len
+    smem = pl.BlockSpec(memory_space=pltpu.SMEM)
     args = (tokens, w_key, w_value)
+    slots = MAJOR * plane * CAP + 1
     return pl.pallas_call(
-        project_kernel,
-        in_specs=[pl.BlockSpec(memory_space=pl.ANY)] * 3,
-        out_specs=WHOLE,
-        out_shape=jax.ShapeDtypeStruct((tokens.shape[0], 2 * KV), BF16),
+        functools.partial(project_kernel, plane, list_len),
+        in_specs=[smem] * 3 + [pl.BlockSpec(memory_space=pl.ANY)] * 3,
+        out_specs=[WHOLE] + [smem] * 3,
+        out_shape=[jax.ShapeDtypeStruct((rows, 2 * KV), BF16)]
+        + [jax.ShapeDtypeStruct((n,), jnp.int32) for n in (entries, entries, slots)],
         scratch_shapes=[pltpu.VMEM(x.shape, BF16) for x in args]
-        + [pltpu.SemaphoreType.DMA((3,))],
+        + [pltpu.SMEM((MAJOR * plane,), jnp.int32), pltpu.SemaphoreType.DMA((8,))],
         compiler_params=params(56),
         name="project",
-    )(*args)
-
-
-def pack_kernel(picked_ref, tile_ref, *outs):
+    )(my_tile.reshape(1), key_tiles, key_blocks, *args)
+
+
+def pack_kernel(first, wanted_ref, tile_ref, *outs):
     for i, out in enumerate(outs):
         for s in range(CAP):
-            out[s] = tile_ref[picked_ref[i * CAP + s]]
-
-
-def pack(picked, tile):
-    peers = picked.shape[0] // CAP
+            out[s] = tile_ref[jnp.maximum(wanted_ref[first + (i + 1) * CAP + s], 0)]
+
+
+def pack(group, plane, wanted, tile):
     shape = (CAP,) + tile.shape[1:]
     return pl.pallas_call(
-        pack_kernel,
+        functools.partial(pack_kernel, group * plane * CAP),
         in_specs=[pl.BlockSpec(memory_space=pltpu.SMEM), WHOLE],
-        out_specs=[WHOLE] * peers,
-        out_shape=[jax.ShapeDtypeStruct(shape, BF16)] * peers,
+        out_specs=[WHOLE] * (plane - 1),
+        out_shape=[jax.ShapeDtypeStruct(shape, BF16)] * (plane - 1),
         compiler_params=params(16),
         name="pack",
-    )(picked, tile)
+    )(wanted, tile)
 
 
 def finish_kernel(parts, *refs):
@@ -304,32 +361,34 @@
     )(*parts, term, w_key, w_value)
 
 
-def owner_kernel(peers, wanted_ref, *refs):
-    parts, extra, (out_ref, total) = refs[:peers], refs[peers:-2], refs[-2:]
-    total[...] = extra[0][...].astype(F32) if extra else jnp.zeros_like(total)
+def owner_kernel(first, wanted_ref, *refs):
+    parts, (out_ref, total) = refs[:-2], refs[-2:]
+    total[...] = jnp.zeros_like(total)
     for p, part in enumerate(parts):
         for s in range(CAP):
-            block = wanted_ref[p * CAP + s]
+            block = wanted_ref[first + p * CAP + s]
 
             @pl.when(block >= 0)
             def _():
                 total[block] += part[s].astype(F32)
 
-    out_ref[...] = total[...].astype(BF16)
-
-
-def owner_sum(wanted, parts, blocks, *extra):
+    out_ref[...] = total[...].astype(out_ref.dtype)
+
+
+def owner_sum(group, wanted, parts, blocks, kind, flops):
     shape = (blocks,) + parts[0].shape[1:]
-    args = (*parts, *extra)
     return pl.pallas_call(
-        functools.partial(owner_kernel, len(parts)),
-        in_specs=[pl.BlockSpec(memory_space=pltpu.SMEM)] + [WHOLE] * len(args),
+        functools.partial(owner_kernel, group * len(parts) * CAP),
+        in_specs=[pl.BlockSpec(memory_space=pltpu.SMEM)] + [WHOLE] * len(parts),
         out_specs=WHOLE,
-        out_shape=jax.ShapeDtypeStruct(shape, BF16),
+        out_shape=jax.ShapeDtypeStruct(shape, kind),
         scratch_shapes=[pltpu.VMEM(shape, F32)],
         compiler_params=params(16),
+        cost_estimate=pl.CostEstimate(
+            flops=flops, bytes_accessed=4 * parts[0].size, transcendentals=0
+        ),
         name="owner_sum",
-    )(wanted, *args)
+    )(wanted, *parts)
 
 
 def shards(patches, out_grad, w_query, w_key, w_value, w_out, key_tiles, key_blocks):
@@ -338,10 +397,8 @@
     tile_count = lax.axis_size("tile")
     plane = tile_count // MAJOR
     my_tile = lax.axis_index("tile")
-    my_row, my_place = my_tile // plane, my_tile % plane
     block_count = rows // BLK
     list_len = key_tiles.shape[2]
-    entry_count = block_count * list_len
 
     def swap(value, d, cross):
         pairs = [
@@ -363,38 +420,18 @@
             moved.append(lax.ppermute(value, "tile", pairs))
         return moved
 
-    def plane_rows(table):
-        table = table[0].reshape(MAJOR, plane, entry_count)
-        return lax.dynamic_index_in_dim(table, my_row, 0, keepdims=False)
-
-    def mine_of(table):
-        return lax.dynamic_index_in_dim(table, my_place, 0, keepdims=False)
-
-    tiles, picks = plane_rows(key_tiles), plane_rows(key_blocks)
-    earlier = jnp.arange(entry_count)[:, None] > jnp.arange(entry_count)[None, :]
-    same = (tiles[:, :, None] == tiles[:, None, :]) & earlier[None]
-    ranks = jnp.sum(same.astype(jnp.int32), axis=2)
-    groups, columns = (tiles // plane) ^ my_row, tiles % plane
-    my_source = mine_of(groups) * plane + (mine_of(columns) ^ my_place)
-    puts = my_source * CODE + mine_of(ranks)
-    gets = jnp.where(my_source % plane == 0, my_source * CODE + mine_of(picks), puts)
-    ids = jnp.arange(MAJOR * CAP, dtype=jnp.int32)
-    slots = groups * CAP + ranks
-    hits = (slots[:, None, :] == ids[None, :, None]) & (columns == my_place)[:, None, :]
-    wanted = jnp.sum(jnp.where(hits, picks[:, None, :] + 1, 0), axis=2) - 1
-    wanted = wanted[jnp.arange(plane) ^ my_place].reshape(plane, MAJOR, CAP)
-    wanted = wanted.transpose(1, 0, 2).reshape(MAJOR, plane * CAP)
-    picked = jnp.maximum(wanted[:, CAP:], 0)
-
-    mine = project(tokens, w_key, w_value).reshape(block_count, BLK, 2 * KV)
+    mine, gets, puts, wanted = project(
+        plane, my_tile, key_tiles, key_blocks, tokens, w_key, w_value
+    )
+    mine = mine.reshape(block_count, BLK, 2 * KV)
     next_tile = swap(mine, 1, 1)
     own_tile = swap(mine, 0, 1)
     far_tile = swap(after(mine, own_tile), 2, 1)
-    own = spread(pack(picked[0], own_tile))
-    beside = spread(pack(picked[1], next_tile), own)
+    own = spread(pack(0, plane, wanted, own_tile))
+    beside = spread(pack(1, plane, wanted, next_tile), own)
     last_tile = swap(after(far_tile, own[-1]), 1, 0)
-    far = spread(pack(picked[2], after(far_tile, own[-1])), beside)
-    last = spread(pack(picked[3], last_tile), far)
+    far = spread(pack(2, plane, wanted, after(far_tile, own[-1])), beside)
+    last = spread(pack(3, plane, wanted, last_tile), far)
     arrived = [own_tile, *own, next_tile, *beside, far_tile, *far, last_tile, *last]
     queries = lax.dot_general(
         w_query, tokens, (((0,), (1,)), ((), ())), preferred_element_type=F32
@@ -409,14 +446,16 @@
         query_grad, w_query, (((0,), (1,)), ((), ())), preferred_element_type=F32
     )
     last = spread(back[3][1:])
-    far = spread(back[2][1:])
+    last[0], query_term, layer_out = lax.optimization_barrier((last[0], query_term, layer_out))
+    far = spread(back[2][1:], last)
     beside = spread(back[1][1:], far)
-    last_sum = swap(owner_sum(wanted[3], [back[3][0], *last], block_count), 1, 0)
-    far_sum = owner_sum(wanted[2], [back[2][0], *far], block_count, last_sum)
-    own = spread([after(x, far_sum) for x in back[0][1:]], beside)
-    next_sum = owner_sum(wanted[1], [back[1][0], *beside], block_count)
-    *own, query_term, layer_out = lax.optimization_barrier((*own, query_term, layer_out))
-    own_sum = owner_sum(wanted[0], [back[0][0], *own], block_count)
+    last_sum = owner_sum(3, wanted, [back[3][0], *last], block_count, BF16, 0)
+    last_sum = swap(last_sum, 1, 0).astype(F32)
+    far_sum = owner_sum(2, wanted, [back[2][0], *far], block_count, F32, FAR_SUM_FLOPS)
+    far_sum = (far_sum + last_sum).astype(BF16)
+    next_sum = owner_sum(1, wanted, [back[1][0], *beside], block_count, BF16, 0)
+    own = spread([after(after(x, far_sum), next_sum) for x in back[0][1:]], beside)
+    own_sum = owner_sum(0, wanted, [back[0][0], *own], block_count, BF16, 0)
     far_grad = swap(far_sum, 2, 1).reshape(rows, 2 * KV)
     near_grads = [x.reshape(rows, 2 * KV) for x in (swap(next_sum, 1, 1), swap(own_sum, 0, 1))]
     query_term = finish([far_grad], query_term, w_key, w_value, F32, FAR_FLOPS)

time: 160 us -> 158 us (0.988)
  other arithmetic: 2.88 us -> 0.17 us
    ppermute x24, waiting for transfers between devices: 44.7 us -> 49 us  [spread(): moved.append(lax.ppermute(value, 'tile', pairs))]
    ppermute x8, waiting for transfers between devices: 31.1 us -> 27.1 us  [swap(): return lax.ppermute(value, ('vintage', 'tile'), pairs)]
    unnamed x64 -> x78, local copies, waits for them, and re-layouts: 1.95 us -> 4.4 us
  transfers between devices with their start and end apart: 32 -> 32, of which waited for: 20 -> 15; matrix products, arithmetic and copies ran while one was open for 8% -> 5% of each run, Pallas kernels for 4% -> 4%
where the time goes in v11:
time: 158 us
  waiting for transfers between devices  76.1 us (48%)
  starting transfers between devices  38.7 us (24%)
  Pallas kernels  30.3 us (19%)
  matrix products  7.41 us (5%)
  local copies, waits for them, and re-layouts  4.4 us (3%)
    ppermute x24, waiting for transfers between devices, spread(): moved.append(lax.ppermute(value, 'tile', pairs))  49 us
    ppermute x24, starting transfers between devices, spread(): moved.append(lax.ppermute(value, 'tile', pairs))  31.9 us
    ppermute x8, waiting for transfers between devices, swap(): return lax.ppermute(value, ('vintage', 'tile'), pairs)  27.1 us
    pallas_call x1, Pallas kernels, attention(): pl.pallas_call(functools.partial(attention_kernel, list_len, per_step), g...  17.3 us
    ppermute x8, starting transfers between devices, swap(): return lax.ppermute(value, ('vintage', 'tile'), pairs)  6.78 us
    pallas_call x1, Pallas kernels, project(): pl.pallas_call(functools.partial(project_kernel, plane, list_len), in_spe...  5.19 us
    unnamed x78, local copies, waits for them, and re-layouts  4.4 us
    pallas_call x4, Pallas kernels, owner_sum(): pl.pallas_call(functools.partial(owner_kernel, group * len(parts) * CAP),...  3.32 us
  transfers between devices with their start and end apart: 32, of which 15 were waited for; matrix products, arithmetic and copies ran while one was open for 5% of the time, Pallas kernels for 4%

profile of v11, /device:TPU:0, one launch (start us, length us, event | category | flops | bytes accessed | tf_op | source)
XLA Modules:
  0.0 158.1 jit_solution(6657058246519021014)
XLA Ops:
  0.6 1.5 copy.10.tiles
  2.1 1.4 copy.11.picks
  3.5 5.2 %project.1 = (bf16[512,512]{1,0:T(8,128)(2,1)}, s32[16]{0:T(128)}, s32[16]{0:T(128)}, s32[33]{0:T(128)}) custom-call(s32[1]{0:T(128)} %bitcast.my_tile, s32[1,64,4]{2,1,0:T(8,128)} %copy.10.tiles, s32[1,64,4]{2,1,0:T(8,128)} %copy.11.picks, bf16[512,768]{1,0:T(8,128)(2,1)} %bitcast.23, bf16[768,256]{1,0:T(8,128)(2,1)} %refs_3_.3, bf16[768,256]{1,0:T(8,128)(2,1)} %refs_4_.1), custom_call_target="tpu_custom_call" | custom-call | tf_op jit(solution)/shard_map/project/pallas_call | solution.py:309
  9.2 2.7 %collective-permute-start.4 = (bf16[4,128,512]{2,1,0:T(8,128)(2,1)}, bf16[4,128,512]{2,1,0:T(8,128)(2,1)S(1)}, u32[]{:S(2)}, u32[]{:S(2)}) collective-permute-start(bf16[4,128,512]{2,1,0:T(8,128)(2,1)} %bitcast.25), channel_id=1, source_target_pairs={{0,20},{1,21},{2,22},{3,23},{4,16},{5,17},{6,18},{7,19},{8,28},{9,... | collective-permute-start | bytes 1572872 | tf_op jit(solution)/shard_map/ppermute | solution.py:409
  11.9 2.7 %collective-permute-start.8 = (bf16[4,128,512]{2,1,0:T(8,128)(2,1)}, bf16[4,128,512]{2,1,0:T(8,128)(2,1)S(1)}, u32[]{:S(2)}, u32[]{:S(2)}) collective-permute-start(bf16[4,128,512]{2,1,0:T(8,128)(2,1)} %bitcast.26), channel_id=1, source_target_pairs={{0,24},{1,25},{2,26},{3,27},{4,28},{5,29},{6,30},{7,31},{8,16},{9,... | collective-permute-start | bytes 1572872 | tf_op jit(solution)/shard_map/ppermute | solution.py:409
  15.9 2.5 %collective-permute-start.3 = (bf16[2,128,512]{2,1,0:T(8,128)(2,1)S(1)}, bf16[2,128,512]{2,1,0:T(8,128)(2,1)S(1)}, u32[]{:S(2)}, u32[]{:S(2)}) collective-permute-start(bf16[2,128,512]{2,1,0:T(8,128)(2,1)S(1)} %get-tuple-element.71), channel_id=1, source_target_pairs={{0,3},{1,2},{2,1},{3,0},{4,7},{5,6},{6,5},{7,4},{8,11},{9,10},{10,... | collective-permute-start | bytes 786440 | tf_op jit(solution)/shard_map/ppermute | solution.py:420
  19.4 15.6 %collective-permute-done.4.tile_ref.refs_4_ = bf16[4,128,512]{2,1,0:T(8,128)(2,1)S(1)} collective-permute-done((bf16[4,128,512]{2,1,0:T(8,128)(2,1)}, bf16[4,128,512]{2,1,0:T(8,128)(2,1)S(1)}, u32[]{:S(2)}, u32[]{:S(2)}) %collective-permute-start.4) | collective-permute-done | bytes 524320 | tf_op jit(solution)/shard_map/ppermute | solution.py:409
  35.6 2.0 %collective-permute-start.7 = (bf16[2,128,512]{2,1,0:T(8,128)(2,1)S(1)}, bf16[2,128,512]{2,1,0:T(8,128)(2,1)S(1)}, u32[]{:S(2)}, u32[]{:S(2)}) collective-permute-start(bf16[2,128,512]{2,1,0:T(8,128)(2,1)S(1)} %get-tuple-element.77), channel_id=1, source_target_pairs={{0,3},{1,2},{2,1},{3,0},{4,7},{5,6},{6,5},{7,4},{8,11},{9,10},{10,... | collective-permute-start | bytes 786440 | tf_op jit(solution)/shard_map/ppermute | solution.py:420
  38.2 1.0 collective-permute-start.5
  40.4 5.3 %collective-permute-done.7.refs_7_ = bf16[2,128,512]{2,1,0:T(8,128)(2,1)S(1)} collective-permute-done((bf16[2,128,512]{2,1,0:T(8,128)(2,1)S(1)}, bf16[2,128,512]{2,1,0:T(8,128)(2,1)S(1)}, u32[]{:S(2)}, u32[]{:S(2)}) %collective-permute-start.7) | collective-permute-done | bytes 262176 | tf_op jit(solution)/shard_map/ppermute | solution.py:420
  45.8 2.0 %collective-permute-start.11 = (bf16[2,128,512]{2,1,0:T(8,128)(2,1)S(1)}, bf16[2,128,512]{2,1,0:T(8,128)(2,1)S(1)}, u32[]{:S(2)}, u32[]{:S(2)}) collective-permute-start(bf16[2,128,512]{2,1,0:T(8,128)(2,1)S(1)} %get-tuple-element.85), channel_id=1, source_target_pairs={{0,3},{1,2},{2,1},{3,0},{4,7},{5,6},{6,5},{7,4},{8,11},{9,10},{10,... | collective-permute-start | bytes 786440 | tf_op jit(solution)/shard_map/ppermute | solution.py:420
  47.8 3.5 %collective-permute-done.6.refs_6_ = bf16[2,128,512]{2,1,0:T(8,128)(2,1)S(1)} collective-permute-done((bf16[2,128,512]{2,1,0:T(8,128)(2,1)S(1)}, bf16[2,128,512]{2,1,0:T(8,128)(2,1)S(1)}, u32[]{:S(2)}, u32[]{:S(2)}) %collective-permute-start.6) | collective-permute-done | bytes 262176 | tf_op jit(solution)/shard_map/ppermute | solution.py:420
  51.3 1.1 collective-permute-start.10
  52.4 0.7 collective-permute-start.9
  53.1 2.0 %fusion.ng_ref = f32[768,512]{1,0:T(8,128)} fusion(bf16[768,768]{1,0:T(8,128)(2,1)S(1)} %copy-done.14, bf16[1,512,768]{2,1,0:T(8,128)(2,1)S(1)} %copy-done.15), kind=kOutput, calls=%fused_computation.3 | convolution fusion | flops 603979776 | bytes 3538944 | tf_op jit(solution)/shard_map/dot_general | solution.py:34
  55.8 1.2 collective-permute-done.11.refs_11_
  57.1 2.0 %collective-permute-start.15 = (bf16[2,128,512]{2,1,0:T(8,128)(2,1)S(1)}, bf16[2,128,512]{2,1,0:T(8,128)(2,1)S(1)}, u32[]{:S(2)}, u32[]{:S(2)}) collective-permute-start(bf16[2,128,512]{2,1,0:T(8,128)(2,1)S(1)} %get-tuple-element.91), channel_id=1, source_target_pairs={{0,3},{1,2},{2,1},{3,0},{4,7},{5,6},{6,5},{7,4},{8,11},{9,10},{10,... | collective-permute-start | bytes 786440 | tf_op jit(solution)/shard_map/ppermute | solution.py:420
  59.1 3.5 %collective-permute-done.10.refs_10_ = bf16[2,128,512]{2,1,0:T(8,128)(2,1)S(1)} collective-permute-done((bf16[2,128,512]{2,1,0:T(8,128)(2,1)S(1)}, bf16[2,128,512]{2,1,0:T(8,128)(2,1)S(1)}, u32[]{:S(2)}, u32[]{:S(2)}) %collective-permute-start.10) | collective-permute-done | bytes 262176 | tf_op jit(solution)/shard_map/ppermute | solution.py:420
  62.6 1.1 collective-permute-start.14
  63.7 1.5 collective-permute-start.13
  65.2 1.7 %convolution_convert_fusion.1.q_ref = bf16[768,512]{1,0:T(8,128)(2,1)} fusion(bf16[768,768]{1,0:T(8,128)(2,1)S(1)} %copy-done, bf16[1,512,768]{2,1,0:T(8,128)(2,1)S(1)} %copy-done.13), kind=kOutput, calls=%fused_computation.1 | convolution fusion | flops 604372992 | bytes 2752512 | tf_op jit(solution)/shard_map/dot_general | solution.py:436
  66.9 1.5 collective-permute-done.15.refs_15_
  68.3 5.0 %collective-permute-done.14.refs_14_ = bf16[2,128,512]{2,1,0:T(8,128)(2,1)S(1)} collective-permute-done((bf16[2,128,512]{2,1,0:T(8,128)(2,1)S(1)}, bf16[2,128,512]{2,1,0:T(8,128)(2,1)S(1)}, u32[]{:S(2)}, u32[]{:S(2)}) %collective-permute-start.14) | collective-permute-done | bytes 262176 | tf_op jit(solution)/shard_map/ppermute | solution.py:420
  73.4 0.7 copy-done.35
  74.2 17.3 %attention.1 = (bf16[768,512]{1,0:T(8,128)(2,1)}, bf16[768,512]{1,0:T(8,128)(2,1)}, bf16[2,128,512]{2,1,0:T(8,128)(2,1)}, bf16[2,128,512]{2,1,0:T(8,128)(2,1)}, ...) custom-call(s32[16]{0:T(128)} %get-tuple-element.65.get_ref, ...), custom_call_target="tpu_custom_call" | custom-call | flops 2415919104 | bytes 6291456 | tf_op jit(solution)/shard_map/attention/pallas_call | solution.py:212
  91.5 1.3 collective-permute-start.16
  92.8 1.5 collective-permute-start.19
  95.0 2.0 %fusion.3.refs_1_ = f32[512,768]{1,0:T(8,128)S(1)} fusion(bf16[768,512]{1,0:T(8,128)(2,1)} %get-tuple-element.93, bf16[768,768]{1,0:T(8,128)(2,1)S(1)} %copy-done), kind=kOutput, calls=%fused_computation.6 | convolution fusion | flops 603979776 | bytes 3538944 | tf_op jit(solution)/shard_map/dot_general | solution.py:445
  97.1 1.7 %convolution_convert_fusion = bf16[512,768]{1,0:T(8,128)(2,1)} fusion(bf16[768,512]{1,0:T(8,128)(2,1)S(1)} %copy-done.37, bf16[768,768]{1,0:T(8,128)(2,1)S(1)} %copy-done.14), kind=kOutput, calls=%fused_computation | convolution fusion | flops 604372992 | bytes 2752512 | tf_op jit(solution)/shard_map/dot_general | solution.py:38
  98.8 7.9 %collective-permute-done.19.refs_2_ = bf16[2,128,512]{2,1,0:T(8,128)(2,1)S(1)} collective-permute-done((bf16[2,128,512]{2,1,0:T(8,128)(2,1)}, bf16[2,128,512]{2,1,0:T(8,128)(2,1)S(1)}, u32[]{:S(2)}, u32[]{:S(2)}) %collective-permute-start.19) | collective-permute-done | bytes 262176 | tf_op jit(solution)/shard_map/ppermute | solution.py:420
  106.7 2.4 %collective-permute-start.20 = (bf16[2,128,512]{2,1,0:T(8,128)(2,1)S(1)}, bf16[2,128,512]{2,1,0:T(8,128)(2,1)S(1)}, u32[]{:S(2)}, u32[]{:S(2)}) collective-permute-start(bf16[2,128,512]{2,1,0:T(8,128)(2,1)S(1)} %copy-done.32), channel_id=1, source_target_pairs={{0,2},{1,3},{2,0},{3,1},{4,6},{5,7},{6,4},{7,5},{8,10},{9,11},{10,... | collective-permute-start | bytes 786440 | tf_op jit(solution)/shard_map/ppermute | solution.py:420
  109.1 1.5 collective-permute-start.17
  110.6 0.9 owner_sum.6
  111.7 6.3 %collective-permute-done.20.refs_2_ = bf16[2,128,512]{2,1,0:T(8,128)(2,1)S(1)} collective-permute-done((bf16[2,128,512]{2,1,0:T(8,128)(2,1)S(1)}, bf16[2,128,512]{2,1,0:T(8,128)(2,1)S(1)}, u32[]{:S(2)}, u32[]{:S(2)}) %collective-permute-start.20) | collective-permute-done | bytes 262176 | tf_op jit(solution)/shard_map/ppermute | solution.py:420
  118.0 2.4 %collective-permute-start.21 = (bf16[2,128,512]{2,1,0:T(8,128)(2,1)S(1)}, bf16[2,128,512]{2,1,0:T(8,128)(2,1)S(1)}, u32[]{:S(2)}, u32[]{:S(2)}) collective-permute-start(bf16[2,128,512]{2,1,0:T(8,128)(2,1)S(1)} %copy-done.26), channel_id=1, source_target_pairs={{0,2},{1,3},{2,0},{3,1},{4,6},{5,7},{6,4},{7,5},{8,10},{9,11},{10,... | collective-permute-start | bytes 786440 | tf_op jit(solution)/shard_map/ppermute | solution.py:420
  120.4 2.4 %collective-permute-start.24 = (bf16[2,128,512]{2,1,0:T(8,128)(2,1)S(1)}, bf16[2,128,512]{2,1,0:T(8,128)(2,1)S(1)}, u32[]{:S(2)}, u32[]{:S(2)}) collective-permute-start(bf16[2,128,512]{2,1,0:T(8,128)(2,1)S(1)} %copy-done.25), channel_id=1, source_target_pairs={{0,3},{1,2},{2,1},{3,0},{4,7},{5,6},{6,5},{7,4},{8,11},{9,10},{10,... | collective-permute-start | bytes 786440 | tf_op jit(solution)/shard_map/ppermute | solution.py:420
  123.1 0.8 owner_sum.5
  124.2 4.9 %collective-permute-done.21.refs_2_ = bf16[2,128,512]{2,1,0:T(8,128)(2,1)S(1)} collective-permute-done((bf16[2,128,512]{2,1,0:T(8,128)(2,1)S(1)}, bf16[2,128,512]{2,1,0:T(8,128)(2,1)S(1)}, u32[]{:S(2)}, u32[]{:S(2)}) %collective-permute-start.21) | collective-permute-done | bytes 262176 | tf_op jit(solution)/shard_map/ppermute | solution.py:420
  129.1 2.2 %collective-permute-done.18.refs_1_ = bf16[2,128,512]{2,1,0:T(8,128)(2,1)S(1)} collective-permute-done((bf16[2,128,512]{2,1,0:T(8,128)(2,1)S(1)}, bf16[2,128,512]{2,1,0:T(8,128)(2,1)S(1)}, u32[]{:S(2)}, u32[]{:S(2)}) %collective-permute-start.18) | collective-permute-done | bytes 262176 | tf_op jit(solution)/shard_map/ppermute | solution.py:420
  131.2 0.8 owner_sum.4
  132.0 2.3 %collective-permute-start.27 = (bf16[2,128,512]{2,1,0:T(8,128)(2,1)S(1)}, bf16[2,128,512]{2,1,0:T(8,128)(2,1)S(1)}, u32[]{:S(2)}, u32[]{:S(2)}) collective-permute-start(bf16[2,128,512]{2,1,0:T(8,128)(2,1)S(1)} %copy-done.20), channel_id=1, source_target_pairs={{0,1},{1,0},{2,3},{3,2},{4,5},{5,4},{6,7},{7,6},{8,9},{9,8},{10,11... | collective-permute-start | bytes 786440 | tf_op jit(solution)/shard_map/ppermute | solution.py:420
  134.4 1.2 collective-permute-start.28
  135.9 3.4 %collective-permute-done.27.refs_1_ = bf16[2,128,512]{2,1,0:T(8,128)(2,1)S(1)} collective-permute-done((bf16[2,128,512]{2,1,0:T(8,128)(2,1)S(1)}, bf16[2,128,512]{2,1,0:T(8,128)(2,1)S(1)}, u32[]{:S(2)}, u32[]{:S(2)}) %collective-permute-start.27) | collective-permute-done | bytes 262176 | tf_op jit(solution)/shard_map/ppermute | solution.py:420
  139.3 4.2 %collective-permute-done.28.refs_2_ = bf16[2,128,512]{2,1,0:T(8,128)(2,1)S(1)} collective-permute-done((bf16[2,128,512]{2,1,0:T(8,128)(2,1)S(1)}, bf16[2,128,512]{2,1,0:T(8,128)(2,1)S(1)}, u32[]{:S(2)}, u32[]{:S(2)}) %collective-permute-start.28) | collective-permute-done | bytes 262176 | tf_op jit(solution)/shard_map/ppermute | solution.py:420
  143.6 0.8 owner_sum.7
  144.4 3.3 %collective-permute-done.31 = bf16[4,128,512]{2,1,0:T(8,128)(2,1)S(1)} collective-permute-done((bf16[4,128,512]{2,1,0:T(8,128)(2,1)S(1)}, bf16[4,128,512]{2,1,0:T(8,128)(2,1)S(1)}, u32[]{:S(2)}, u32[]{:S(2)}) %collective-permute-start.31) | collective-permute-done | bytes 524320 | tf_op jit(solution)/shard_map/ppermute | solution.py:409
  148.4 8.2 %collective-permute-done.25 = bf16[4,128,512]{2,1,0:T(8,128)(2,1)S(1)} collective-permute-done((bf16[4,128,512]{2,1,0:T(8,128)(2,1)S(1)}, bf16[4,128,512]{2,1,0:T(8,128)(2,1)S(1)}, u32[]{:S(2)}, u32[]{:S(2)}) %collective-permute-start.25) | collective-permute-done | bytes 524320 | tf_op jit(solution)/shard_map/ppermute | solution.py:409
  156.6 1.5 finish.3
  (111 shorter events, 8.2 us)
Async XLA Ops:
  0.6 64.5 %copy-start = (bf16[768,768]{1,0:T(8,128)(2,1)S(1)}, bf16[768,768]{1,0:T(8,128)(2,1)}, u32[]{:S(2)}) copy-start(bf16[768,768]{1,0:T(8,128)(2,1)} %param.10) | copy-start | bytes 3538948
  3.5 49.6 %copy-start.14 = (bf16[768,768]{1,0:T(8,128)(2,1)S(1)}, bf16[768,768]{1,0:T(8,128)(2,1)}, u32[]{:S(2)}) copy-start(bf16[768,768]{1,0:T(8,128)(2,1)} %param.13) | copy-start | bytes 3538948
  8.7 3.2 %collective-permute-start = (bf16[4,128,512]{2,1,0:T(8,128)(2,1)}, bf16[4,128,512]{2,1,0:T(8,128)(2,1)S(1)}, u32[]{:S(2)}, u32[]{:S(2)}) collective-permute-start(bf16[4,128,512]{2,1,0:T(8,128)(2,1)} %bitcast.24), channel_id=1, source_target_pairs={{0,16},{1,17},{2,18},{3,19},{4,20},{5,21},{6,22},{7,23},{8,24},{9,... | collective-permute-start | bytes 1572872 | tf_op jit(solution)/shard_map/ppermute | solution.py:409
  9.2 25.8 %collective-permute-start.4 = (bf16[4,128,512]{2,1,0:T(8,128)(2,1)}, bf16[4,128,512]{2,1,0:T(8,128)(2,1)S(1)}, u32[]{:S(2)}, u32[]{:S(2)}) collective-permute-start(bf16[4,128,512]{2,1,0:T(8,128)(2,1)} %bitcast.25), channel_id=1, source_target_pairs={{0,20},{1,21},{2,22},{3,23},{4,16},{5,17},{6,18},{7,19},{8,28},{9,... | collective-permute-start | bytes 1572872 | tf_op jit(solution)/shard_map/ppermute | solution.py:409
  11.9 43.2 %copy-start.3 = (bf16[4,128,512]{2,1,0:T(8,128)(2,1)}, bf16[4,128,512]{2,1,0:T(8,128)(2,1)S(1)}, u32[]{:S(2)}) copy-start(bf16[4,128,512]{2,1,0:T(8,128)(2,1)S(1)} %collective-permute-done.tile_ref.refs_0_) | copy-start | bytes 1572868
  11.9 27.3 %collective-permute-start.8 = (bf16[4,128,512]{2,1,0:T(8,128)(2,1)}, bf16[4,128,512]{2,1,0:T(8,128)(2,1)S(1)}, u32[]{:S(2)}, u32[]{:S(2)}) collective-permute-start(bf16[4,128,512]{2,1,0:T(8,128)(2,1)} %bitcast.26), channel_id=1, source_target_pairs={{0,24},{1,25},{2,26},{3,27},{4,28},{5,29},{6,30},{7,31},{8,16},{9,... | collective-permute-start | bytes 1572872 | tf_op jit(solution)/shard_map/ppermute | solution.py:409
  15.3 37.9 %copy-start.15 = (bf16[1,512,768]{2,1,0:T(8,128)(2,1)S(1)}, bf16[1,512,768]{2,1,0:T(8,128)(2,1)}, u32[]{:S(2)}) copy-start(bf16[1,512,768]{2,1,0:T(8,128)(2,1)} %param.9) | copy-start | bytes 2359300
  15.9 19.8 %collective-permute-start.3 = (bf16[2,128,512]{2,1,0:T(8,128)(2,1)S(1)}, bf16[2,128,512]{2,1,0:T(8,128)(2,1)S(1)}, u32[]{:S(2)}, u32[]{:S(2)}) collective-permute-start(bf16[2,128,512]{2,1,0:T(8,128)(2,1)S(1)} %get-tuple-element.71), channel_id=1, source_target_pairs={{0,3},{1,2},{2,1},{3,0},{4,7},{5,6},{6,5},{7,4},{8,11},{9,10},{10,... | collective-permute-start | bytes 786440 | tf_op jit(solution)/shard_map/ppermute | solution.py:420
  18.4 19.3 %collective-permute-start.2 = (bf16[2,128,512]{2,1,0:T(8,128)(2,1)S(1)}, bf16[2,128,512]{2,1,0:T(8,128)(2,1)S(1)}, u32[]{:S(2)}, u32[]{:S(2)}) collective-permute-start(bf16[2,128,512]{2,1,0:T(8,128)(2,1)S(1)} %get-tuple-element.70), channel_id=1, source_target_pairs={{0,2},{1,3},{2,0},{3,1},{4,6},{5,7},{6,4},{7,5},{8,10},{9,11},{10,... | collective-permute-start | bytes 786440 | tf_op jit(solution)/shard_map/ppermute | solution.py:420
  18.9 19.3 %collective-permute-start.1 = (bf16[2,128,512]{2,1,0:T(8,128)(2,1)S(1)}, bf16[2,128,512]{2,1,0:T(8,128)(2,1)S(1)}, u32[]{:S(2)}, u32[]{:S(2)}) collective-permute-start(bf16[2,128,512]{2,1,0:T(8,128)(2,1)S(1)} %get-tuple-element.69), channel_id=1, source_target_pairs={{0,1},{1,0},{2,3},{3,2},{4,5},{5,4},{6,7},{7,6},{8,9},{9,8},{10,11... | collective-permute-start | bytes 786440 | tf_op jit(solution)/shard_map/ppermute | solution.py:420
  35.0 20.1 %copy-start.4 = (bf16[4,128,512]{2,1,0:T(8,128)(2,1)}, bf16[4,128,512]{2,1,0:T(8,128)(2,1)S(1)}, u32[]{:S(2)}) copy-start(bf16[4,128,512]{2,1,0:T(8,128)(2,1)S(1)} %collective-permute-done.4.tile_ref.refs_4_) | copy-start | bytes 1572868
  35.6 19.5 %copy-start.17 = (bf16[2,128,512]{2,1,0:T(8,128)(2,1)}, bf16[2,128,512]{2,1,0:T(8,128)(2,1)S(1)}, u32[]{:S(2)}) copy-start(bf16[2,128,512]{2,1,0:T(8,128)(2,1)S(1)} %collective-permute-done.3.refs_3_) | copy-start | bytes 786436
  35.6 10.1 %collective-permute-start.7 = (bf16[2,128,512]{2,1,0:T(8,128)(2,1)S(1)}, bf16[2,128,512]{2,1,0:T(8,128)(2,1)S(1)}, u32[]{:S(2)}, u32[]{:S(2)}) collective-permute-start(bf16[2,128,512]{2,1,0:T(8,128)(2,1)S(1)} %get-tuple-element.77), channel_id=1, source_target_pairs={{0,3},{1,2},{2,1},{3,0},{4,7},{5,6},{6,5},{7,4},{8,11},{9,10},{10,... | collective-permute-start | bytes 786440 | tf_op jit(solution)/shard_map/ppermute | solution.py:420
  37.7 17.5 %copy-start.19 = (bf16[2,128,512]{2,1,0:T(8,128)(2,1)}, bf16[2,128,512]{2,1,0:T(8,128)(2,1)S(1)}, u32[]{:S(2)}) copy-start(bf16[2,128,512]{2,1,0:T(8,128)(2,1)S(1)} %collective-permute-done.2.refs_2_) | copy-start | bytes 786436
  37.7 13.7 %collective-permute-start.6 = (bf16[2,128,512]{2,1,0:T(8,128)(2,1)S(1)}, bf16[2,128,512]{2,1,0:T(8,128)(2,1)S(1)}, u32[]{:S(2)}, u32[]{:S(2)}) collective-permute-start(bf16[2,128,512]{2,1,0:T(8,128)(2,1)S(1)} %get-tuple-element.75), channel_id=1, source_target_pairs={{0,2},{1,3},{2,0},{3,1},{4,6},{5,7},{6,4},{7,5},{8,10},{9,11},{10,... | collective-permute-start | bytes 786440 | tf_op jit(solution)/shard_map/ppermute | solution.py:420
  38.2 17.0 %copy-start.21 = (bf16[2,128,512]{2,1,0:T(8,128)(2,1)}, bf16[2,128,512]{2,1,0:T(8,128)(2,1)S(1)}, u32[]{:S(2)}) copy-start(bf16[2,128,512]{2,1,0:T(8,128)(2,1)S(1)} %collective-permute-done.1.refs_1_) | copy-start | bytes 786436
  38.2 14.2 %collective-permute-start.5 = (bf16[2,128,512]{2,1,0:T(8,128)(2,1)S(1)}, bf16[2,128,512]{2,1,0:T(8,128)(2,1)S(1)}, u32[]{:S(2)}, u32[]{:S(2)}) collective-permute-start(bf16[2,128,512]{2,1,0:T(8,128)(2,1)S(1)} %get-tuple-element.73), channel_id=1, source_target_pairs={{0,1},{1,0},{2,3},{3,2},{4,5},{5,4},{6,7},{7,6},{8,9},{9,8},{10,11... | collective-permute-start | bytes 786440 | tf_op jit(solution)/shard_map/ppermute | solution.py:420
  39.2 15.9 %copy-start.5 = (bf16[4,128,512]{2,1,0:T(8,128)(2,1)}, bf16[4,128,512]{2,1,0:T(8,128)(2,1)S(1)}, u32[]{:S(2)}) copy-start(bf16[4,128,512]{2,1,0:T(8,128)(2,1)S(1)} %collective-permute-done.8.tile_ref.refs_8_) | copy-start | bytes 1572868
  39.2 16.0 %collective-permute-start.12 = (bf16[4,128,512]{2,1,0:T(8,128)(2,1)S(1)}, bf16[4,128,512]{2,1,0:T(8,128)(2,1)S(1)}, u32[]{:S(2)}, u32[]{:S(2)}) collective-permute-start(bf16[4,128,512]{2,1,0:T(8,128)(2,1)S(1)} %collective-permute-done.8.tile_ref.refs_8_), channel_id=1, source_target_pairs={{0,4},{1,5},{2,6},{3,7},{4,0},{5,1},{6,2},{7,3},{8,12},{9,13},{10,... | collective-permute-start | bytes 1572872 | tf_op jit(solution)/shard_map/ppermute | solution.py:409
  45.8 11.3 %collective-permute-start.11 = (bf16[2,128,512]{2,1,0:T(8,128)(2,1)S(1)}, bf16[2,128,512]{2,1,0:T(8,128)(2,1)S(1)}, u32[]{:S(2)}, u32[]{:S(2)}) collective-permute-start(bf16[2,128,512]{2,1,0:T(8,128)(2,1)S(1)} %get-tuple-element.85), channel_id=1, source_target_pairs={{0,3},{1,2},{2,1},{3,0},{4,7},{5,6},{6,5},{7,4},{8,11},{9,10},{10,... | collective-permute-start | bytes 786440 | tf_op jit(solution)/shard_map/ppermute | solution.py:420
  51.3 11.3 %collective-permute-start.10 = (bf16[2,128,512]{2,1,0:T(8,128)(2,1)S(1)}, bf16[2,128,512]{2,1,0:T(8,128)(2,1)S(1)}, u32[]{:S(2)}, u32[]{:S(2)}) collective-permute-start(bf16[2,128,512]{2,1,0:T(8,128)(2,1)S(1)} %get-tuple-element.83), channel_id=1, source_target_pairs={{0,2},{1,3},{2,0},{3,1},{4,6},{5,7},{6,4},{7,5},{8,10},{9,11},{10,... | collective-permute-start | bytes 786440 | tf_op jit(solution)/shard_map/ppermute | solution.py:420
  52.4 11.3 %collective-permute-start.9 = (bf16[2,128,512]{2,1,0:T(8,128)(2,1)S(1)}, bf16[2,128,512]{2,1,0:T(8,128)(2,1)S(1)}, u32[]{:S(2)}, u32[]{:S(2)}) collective-permute-start(bf16[2,128,512]{2,1,0:T(8,128)(2,1)S(1)} %get-tuple-element.81), channel_id=1, source_target_pairs={{0,1},{1,0},{2,3},{3,2},{4,5},{5,4},{6,7},{7,6},{8,9},{9,8},{10,11... | collective-permute-start | bytes 786440 | tf_op jit(solution)/shard_map/ppermute | solution.py:420
  57.1 11.3 %collective-permute-start.15 = (bf16[2,128,512]{2,1,0:T(8,128)(2,1)S(1)}, bf16[2,128,512]{2,1,0:T(8,128)(2,1)S(1)}, u32[]{:S(2)}, u32[]{:S(2)}) collective-permute-start(bf16[2,128,512]{2,1,0:T(8,128)(2,1)S(1)} %get-tuple-element.91), channel_id=1, source_target_pairs={{0,3},{1,2},{2,1},{3,0},{4,7},{5,6},{6,5},{7,4},{8,11},{9,10},{10,... | collective-permute-start | bytes 786440 | tf_op jit(solution)/shard_map/ppermute | solution.py:420
  62.6 10.8 %collective-permute-start.14 = (bf16[2,128,512]{2,1,0:T(8,128)(2,1)S(1)}, bf16[2,128,512]{2,1,0:T(8,128)(2,1)S(1)}, u32[]{:S(2)}, u32[]{:S(2)}) collective-permute-start(bf16[2,128,512]{2,1,0:T(8,128)(2,1)S(1)} %get-tuple-element.89), channel_id=1, source_target_pairs={{0,2},{1,3},{2,0},{3,1},{4,6},{5,7},{6,4},{7,5},{8,10},{9,11},{10,... | collective-permute-start | bytes 786440 | tf_op jit(solution)/shard_map/ppermute | solution.py:420
  63.7 9.7 %collective-permute-start.13 = (bf16[2,128,512]{2,1,0:T(8,128)(2,1)S(1)}, bf16[2,128,512]{2,1,0:T(8,128)(2,1)S(1)}, u32[]{:S(2)}, u32[]{:S(2)}) collective-permute-start(bf16[2,128,512]{2,1,0:T(8,128)(2,1)S(1)} %get-tuple-element.87), channel_id=1, source_target_pairs={{0,1},{1,0},{2,3},{3,2},{4,5},{5,4},{6,7},{7,6},{8,9},{9,8},{10,11... | collective-permute-start | bytes 786440 | tf_op jit(solution)/shard_map/ppermute | solution.py:420
  91.5 17.6 %collective-permute-start.16 = (bf16[2,128,512]{2,1,0:T(8,128)(2,1)}, bf16[2,128,512]{2,1,0:T(8,128)(2,1)S(1)}, u32[]{:S(2)}, u32[]{:S(2)}) collective-permute-start(bf16[2,128,512]{2,1,0:T(8,128)(2,1)} %get-tuple-element.92), channel_id=1, source_target_pairs={{0,1},{1,0},{2,3},{3,2},{4,5},{5,4},{6,7},{7,6},{8,9},{9,8},{10,11... | collective-permute-start | bytes 786440 | tf_op jit(solution)/shard_map/ppermute | solution.py:420
  92.8 13.9 %collective-permute-start.19 = (bf16[2,128,512]{2,1,0:T(8,128)(2,1)}, bf16[2,128,512]{2,1,0:T(8,128)(2,1)S(1)}, u32[]{:S(2)}, u32[]{:S(2)}) collective-permute-start(bf16[2,128,512]{2,1,0:T(8,128)(2,1)} %get-tuple-element.104), channel_id=1, source_target_pairs={{0,2},{1,3},{2,0},{3,1},{4,6},{5,7},{6,4},{7,5},{8,10},{9,11},{10,... | collective-permute-start | bytes 786440 | tf_op jit(solution)/shard_map/ppermute | solution.py:420
  94.4 14.7 %collective-permute-start.22 = (bf16[2,128,512]{2,1,0:T(8,128)(2,1)}, bf16[2,128,512]{2,1,0:T(8,128)(2,1)S(1)}, u32[]{:S(2)}, u32[]{:S(2)}) collective-permute-start(bf16[2,128,512]{2,1,0:T(8,128)(2,1)} %get-tuple-element.109), channel_id=1, source_target_pairs={{0,3},{1,2},{2,1},{3,0},{4,7},{5,6},{6,5},{7,4},{8,11},{9,10},{10,... | collective-permute-start | bytes 786440 | tf_op jit(solution)/shard_map/ppermute | solution.py:420
  98.8 19.1 %copy-start.26 = (bf16[2,128,512]{2,1,0:T(8,128)(2,1)S(1)}, bf16[2,128,512]{2,1,0:T(8,128)(2,1)}, u32[]{:S(2)}) copy-start(bf16[2,128,512]{2,1,0:T(8,128)(2,1)} %get-tuple-element.106) | copy-start | bytes 786436
  98.8 21.6 %copy-start.25 = (bf16[2,128,512]{2,1,0:T(8,128)(2,1)S(1)}, bf16[2,128,512]{2,1,0:T(8,128)(2,1)}, u32[]{:S(2)}) copy-start(bf16[2,128,512]{2,1,0:T(8,128)(2,1)} %get-tuple-element.111) | copy-start | bytes 786436
  98.8 24.0 %copy-start.23 = (bf16[2,128,512]{2,1,0:T(8,128)(2,1)S(1)}, bf16[2,128,512]{2,1,0:T(8,128)(2,1)}, u32[]{:S(2)}) copy-start(bf16[2,128,512]{2,1,0:T(8,128)(2,1)} %get-tuple-element.101) | copy-start | bytes 786436
  98.8 24.2 %copy-start.12 = (bf16[2,128,512]{2,1,0:T(8,128)(2,1)S(1)}, bf16[2,128,512]{2,1,0:T(8,128)(2,1)}, u32[]{:S(2)}) copy-start(bf16[2,128,512]{2,1,0:T(8,128)(2,1)} %get-tuple-element.114.refs_0_) | copy-start | bytes 786436
  106.7 11.3 %collective-permute-start.20 = (bf16[2,128,512]{2,1,0:T(8,128)(2,1)S(1)}, bf16[2,128,512]{2,1,0:T(8,128)(2,1)S(1)}, u32[]{:S(2)}, u32[]{:S(2)}) collective-permute-start(bf16[2,128,512]{2,1,0:T(8,128)(2,1)S(1)} %copy-done.32), channel_id=1, source_target_pairs={{0,2},{1,3},{2,0},{3,1},{4,6},{5,7},{6,4},{7,5},{8,10},{9,11},{10,... | collective-permute-start | bytes 786440 | tf_op jit(solution)/shard_map/ppermute | solution.py:420
  109.1 11.3 %collective-permute-start.23 = (bf16[2,128,512]{2,1,0:T(8,128)(2,1)S(1)}, bf16[2,128,512]{2,1,0:T(8,128)(2,1)S(1)}, u32[]{:S(2)}, u32[]{:S(2)}) collective-permute-start(bf16[2,128,512]{2,1,0:T(8,128)(2,1)S(1)} %copy-done.31), channel_id=1, source_target_pairs={{0,3},{1,2},{2,1},{3,0},{4,7},{5,6},{6,5},{7,4},{8,11},{9,10},{10,... | collective-permute-start | bytes 786440 | tf_op jit(solution)/shard_map/ppermute | solution.py:420
  109.1 13.7 %collective-permute-start.17 = (bf16[2,128,512]{2,1,0:T(8,128)(2,1)S(1)}, bf16[2,128,512]{2,1,0:T(8,128)(2,1)S(1)}, u32[]{:S(2)}, u32[]{:S(2)}) collective-permute-start(bf16[2,128,512]{2,1,0:T(8,128)(2,1)S(1)} %copy-done.29), channel_id=1, source_target_pairs={{0,1},{1,0},{2,3},{3,2},{4,5},{5,4},{6,7},{7,6},{8,9},{9,8},{10,11... | collective-permute-start | bytes 786440 | tf_op jit(solution)/shard_map/ppermute | solution.py:420
  111.6 12.3 %collective-permute-start.26 = (bf16[4,128,512]{2,1,0:T(8,128)(2,1)S(1)}, bf16[4,128,512]{2,1,0:T(8,128)(2,1)S(1)}, u32[]{:S(2)}, u32[]{:S(2)}) collective-permute-start(bf16[4,128,512]{2,1,0:T(8,128)(2,1)S(1)} %owner_sum.6), channel_id=1, source_target_pairs={{0,4},{1,5},{2,6},{3,7},{4,0},{5,1},{6,2},{7,3},{8,12},{9,13},{10,... | collective-permute-start | bytes 1572872 | tf_op jit(solution)/shard_map/ppermute | solution.py:409
  118.0 11.1 %collective-permute-start.21 = (bf16[2,128,512]{2,1,0:T(8,128)(2,1)S(1)}, bf16[2,128,512]{2,1,0:T(8,128)(2,1)S(1)}, u32[]{:S(2)}, u32[]{:S(2)}) collective-permute-start(bf16[2,128,512]{2,1,0:T(8,128)(2,1)S(1)} %copy-done.26), channel_id=1, source_target_pairs={{0,2},{1,3},{2,0},{3,1},{4,6},{5,7},{6,4},{7,5},{8,10},{9,11},{10,... | collective-permute-start | bytes 786440 | tf_op jit(solution)/shard_map/ppermute | solution.py:420
  120.4 8.7 %collective-permute-start.24 = (bf16[2,128,512]{2,1,0:T(8,128)(2,1)S(1)}, bf16[2,128,512]{2,1,0:T(8,128)(2,1)S(1)}, u32[]{:S(2)}, u32[]{:S(2)}) collective-permute-start(bf16[2,128,512]{2,1,0:T(8,128)(2,1)S(1)} %copy-done.25), channel_id=1, source_target_pairs={{0,3},{1,2},{2,1},{3,0},{4,7},{5,6},{6,5},{7,4},{8,11},{9,10},{10,... | collective-permute-start | bytes 786440 | tf_op jit(solution)/shard_map/ppermute | solution.py:420
  122.8 8.4 %collective-permute-start.18 = (bf16[2,128,512]{2,1,0:T(8,128)(2,1)S(1)}, bf16[2,128,512]{2,1,0:T(8,128)(2,1)S(1)}, u32[]{:S(2)}, u32[]{:S(2)}) collective-permute-start(bf16[2,128,512]{2,1,0:T(8,128)(2,1)S(1)} %copy-done.23), channel_id=1, source_target_pairs={{0,1},{1,0},{2,3},{3,2},{4,5},{5,4},{6,7},{7,6},{8,9},{9,8},{10,11... | collective-permute-start | bytes 786440 | tf_op jit(solution)/shard_map/ppermute | solution.py:420
  124.1 19.5 %copy-start.7 = (bf16[2,128,512]{2,1,0:T(8,128)(2,1)S(1)}, bf16[2,128,512]{2,1,0:T(8,128)(2,1)}, u32[]{:S(2)}) copy-start(bf16[2,128,512]{2,1,0:T(8,128)(2,1)} %get-tuple-element.112.refs_0_) | copy-start | bytes 786436
  124.1 23.7 %collective-permute-start.31 = (bf16[4,128,512]{2,1,0:T(8,128)(2,1)S(1)}, bf16[4,128,512]{2,1,0:T(8,128)(2,1)S(1)}, u32[]{:S(2)}, u32[]{:S(2)}) collective-permute-start(bf16[4,128,512]{2,1,0:T(8,128)(2,1)S(1)} %add_convert_fusion), channel_id=1, source_target_pairs={{0,24},{1,25},{2,26},{3,27},{4,28},{5,29},{6,30},{7,31},{8,16},{9,... | collective-permute-start | bytes 1572872 | tf_op jit(solution)/shard_map/ppermute | solution.py:409
  132.0 15.8 %copy-start.1 = (bf16[768,256]{1,0:T(8,128)(2,1)S(1)}, bf16[768,256]{1,0:T(8,128)(2,1)}, u32[]{:S(2)}) copy-start(bf16[768,256]{1,0:T(8,128)(2,1)} %refs_3_.3) | copy-start | bytes 1179652
  132.0 15.7 %copy-start.2 = (bf16[768,256]{1,0:T(8,128)(2,1)S(1)}, bf16[768,256]{1,0:T(8,128)(2,1)}, u32[]{:S(2)}) copy-start(bf16[768,256]{1,0:T(8,128)(2,1)} %refs_4_.1) | copy-start | bytes 1179652
  132.0 7.3 %collective-permute-start.27 = (bf16[2,128,512]{2,1,0:T(8,128)(2,1)S(1)}, bf16[2,128,512]{2,1,0:T(8,128)(2,1)S(1)}, u32[]{:S(2)}, u32[]{:S(2)}) collective-permute-start(bf16[2,128,512]{2,1,0:T(8,128)(2,1)S(1)} %copy-done.20), channel_id=1, source_target_pairs={{0,1},{1,0},{2,3},{3,2},{4,5},{5,4},{6,7},{7,6},{8,9},{9,8},{10,11... | collective-permute-start | bytes 786440 | tf_op jit(solution)/shard_map/ppermute | solution.py:420
  134.4 9.2 %collective-permute-start.28 = (bf16[2,128,512]{2,1,0:T(8,128)(2,1)S(1)}, bf16[2,128,512]{2,1,0:T(8,128)(2,1)S(1)}, u32[]{:S(2)}, u32[]{:S(2)}) collective-permute-start(bf16[2,128,512]{2,1,0:T(8,128)(2,1)S(1)} %copy-done.18), channel_id=1, source_target_pairs={{0,2},{1,3},{2,0},{3,1},{4,6},{5,7},{6,4},{7,5},{8,10},{9,11},{10,... | collective-permute-start | bytes 786440 | tf_op jit(solution)/shard_map/ppermute | solution.py:420
  135.6 8.0 %collective-permute-start.29 = (bf16[2,128,512]{2,1,0:T(8,128)(2,1)S(1)}, bf16[2,128,512]{2,1,0:T(8,128)(2,1)S(1)}, u32[]{:S(2)}, u32[]{:S(2)}) collective-permute-start(bf16[2,128,512]{2,1,0:T(8,128)(2,1)S(1)} %copy-done.16), channel_id=1, source_target_pairs={{0,3},{1,2},{2,1},{3,0},{4,7},{5,6},{6,5},{7,4},{8,11},{9,10},{10,... | collective-permute-start | bytes 786440 | tf_op jit(solution)/shard_map/ppermute | solution.py:420
  135.9 20.7 %collective-permute-start.25 = (bf16[4,128,512]{2,1,0:T(8,128)(2,1)S(1)}, bf16[4,128,512]{2,1,0:T(8,128)(2,1)S(1)}, u32[]{:S(2)}, u32[]{:S(2)}) collective-permute-start(bf16[4,128,512]{2,1,0:T(8,128)(2,1)S(1)} %owner_sum.4), channel_id=1, source_target_pairs={{0,20},{1,21},{2,22},{3,23},{4,16},{5,17},{6,18},{7,19},{8,28},{9,... | collective-permute-start | bytes 1572872 | tf_op jit(solution)/shard_map/ppermute | solution.py:409
  144.4 12.2 %collective-permute-start.30 = (bf16[4,128,512]{2,1,0:T(8,128)(2,1)S(1)}, bf16[4,128,512]{2,1,0:T(8,128)(2,1)S(1)}, u32[]{:S(2)}, u32[]{:S(2)}) collective-permute-start(bf16[4,128,512]{2,1,0:T(8,128)(2,1)S(1)} %owner_sum.7), channel_id=1, source_target_pairs={{0,16},{1,17},{2,18},{3,19},{4,20},{5,21},{6,22},{7,23},{8,24},{9,... | collective-permute-start | bytes 1572872 | tf_op jit(solution)/shard_map/ppermute | solution.py:409
  (22 other events, 164.7 us)

commit v12 on v11

--- a/solution.py
+++ b/solution.py
@@ -16,8 +16,9 @@
 KV = KV_HEADS * HEAD_DIM
 PAIR = 2 * HEAD_DIM
 CODE = 16
-FAR_SUM_FLOPS = 8_000_000_000
-FAR_FLOPS = 30_000_000_000
+NEXT_FLOPS = 10_000_000_000
+FAR_SUM_FLOPS = 5_000_000_000
+FAR_FLOPS = 20_000_000_000
 MAJOR = 4
 TEMPER = HEAD_DIM ** (-0.5)
 EPSILON = 1e-06
@@ -102,8 +103,6 @@
         start(fetch, get_ref, 0, entries)
 
     first = step * per_step * list_len
-    for i in range(per_step * list_len):
-        fetch(first + i, 0, 0).wait()
     pairs = range(KV // PAIR)
     keys, values, wide, scores, exact, scales, grads, overlap, prob_grads = (
         {} for _ in range(9)
@@ -114,9 +113,11 @@
         return pl.ds(pl.multiple_of((step * per_step + b) * size, size), size)
 
     def cols_at(b):
-        return slice(b * BLK, (b + 1) * BLK)
+        return pl.ds(pl.multiple_of((step * per_step + b) * BLK, BLK), BLK)
 
     def score(b):
+        for i in range(list_len):
+            fetch(first + b * list_len + i, 0, 0).wait()
         here = rows_at(b)
         queries = q_ref[:, cols_at(b)] * jnp.asarray(TEMPER, BF16)
         for j in pairs:
@@ -177,16 +178,19 @@
         parts_scr[here, j * PAIR : (j + 1) * PAIR] = key_part.astype(BF16)
         parts_scr[here, KV + j * PAIR : KV + (j + 1) * PAIR] = value_part.astype(BF16)
 
-    for b in range(per_step):
-        score(b)
+    score(0)
     for j in pairs:
         soften(0, j)
+    if per_step > 1:
+        score(1)
     normalise(0)
     for b in range(per_step):
         for j in pairs:
             regrade(b, j)
             if b + 1 < per_step:
                 soften(b + 1, j)
+        if b + 2 < per_step:
+            score(b + 2)
         for j in pairs:
             finish_pair(b, j)
             if b + 1 < per_step and j == 0:
@@ -204,9 +208,9 @@
     slot_shape = (CAP,) + arrived[0].shape[1:]
     blocks = rows // BLK
     entries = blocks * list_len
-    per_step = 2 if list_len <= 4 and blocks % 2 == 0 else 1
-    row_spec = pl.BlockSpec((width, per_step * BLK), lambda r, g, p: (0, r))
-    anywhere = pl.BlockSpec(memory_space=pl.ANY)
+    resident = list_len <= 4
+    per_step = blocks if resident else 1
+    place = WHOLE if resident else pl.BlockSpec(memory_space=pl.ANY)
     keys = list_len * BLK
     pairs = HEADS * rows * keys
     return pl.pallas_call(
@@ -214,8 +218,8 @@
         grid_spec=pltpu.PrefetchScalarGridSpec(
             num_scalar_prefetch=2,
             grid=(blocks // per_step,),
-            in_specs=[row_spec, row_spec] + [anywhere] * len(arrived),
-            out_specs=[row_spec, row_spec] + [anywhere] * len(arrived),
+            in_specs=[WHOLE] * 2 + [place] * len(arrived),
+            out_specs=[WHOLE] * 2 + [place] * len(arrived),
             scratch_shapes=[
                 pltpu.VMEM((per_step, KV // PAIR, keys, 2 * GROUP * BLK), BF16),
                 pltpu.VMEM((entries * BLK, 2 * KV), BF16),
@@ -226,7 +230,7 @@
         ),
         out_shape=[jax.ShapeDtypeStruct((width, rows), BF16)] * 2
         + [jax.ShapeDtypeStruct(slot_shape, BF16)] * len(arrived),
-        compiler_params=params(56),
+        compiler_params=params(40 if resident else 56),
         cost_estimate=pl.CostEstimate(
             flops=12 * pairs * HEAD_DIM, bytes_accessed=16 * rows * width, transcendentals=pairs
         ),
@@ -234,50 +238,7 @@
     )(gets, puts, queries, normed_grad, *arrived)
 
 
-def plan(plane, list_len, my_tile, tiles, picks, gets, puts, wanted, counts):
-    entries = gets.shape[0]
-    block_count = entries // list_len
-    my_row, my_place = lax.div(my_tile, plane), lax.rem(my_tile, plane)
-    spare = MAJOR * plane * CAP
-
-    def clear(i, carry):
-        wanted[i] = -1
-        return carry
-
-    lax.fori_loop(0, spare + 1, clear, 0)
-
-    def one_asker(p, carry):
-        asker = my_row * plane + (my_place ^ p)
-
-        def zero(t, carry):
-            counts[t] = 0
-            return carry
-
-        lax.fori_loop(0, counts.shape[0], zero, 0)
-        for e in range(entries):
-            row = asker * block_count + e // list_len
-            tile, pick = tiles[0, row, e % list_len], picks[0, row, e % list_len]
-            rank = counts[tile]
-            counts[tile] = rank + 1
-            group, column = lax.div(tile, plane) ^ my_row, lax.rem(tile, plane)
-            mine = column == my_place
-            wanted[jnp.where(mine, (group * plane + p) * CAP + rank, spare)] = pick
-
-            @pl.when(p == 0)
-            def _():
-                code = (group * plane + (column ^ my_place)) * CODE
-                puts[e] = code + rank
-                gets[e] = code + jnp.where(mine, pick, rank)
-
-        return carry
-
-    lax.fori_loop(0, plane, one_asker, 0)
-
-
-def project_kernel(
-    plane, list_len, my_tile, tiles, picks, tokens_hbm, wk_hbm, wv_hbm,
-    out_ref, gets, puts, wanted, tokens, wk, wv, counts, sems,
-):
+def project_kernel(tokens_hbm, wk_hbm, wv_hbm, out_ref, tokens, wk, wv, sems):
     copies = []
     for src, dst, pieces in ((wk_hbm, wk, 2), (tokens_hbm, tokens, 4), (wv_hbm, wv, 2)):
         size = src.shape[0] // pieces
@@ -288,7 +249,6 @@
             )
     for copy in copies:
         copy.start()
-    plan(plane, list_len, my_tile[0], tiles, picks, gets, puts, wanted, counts)
     for copy in copies[:6]:
         copy.wait()
     keys = jnp.dot(tokens[...], wk[...], preferred_element_type=F32)
@@ -299,24 +259,18 @@
     out_ref[:, KV:] = values.astype(BF16)
 
 
-def project(plane, my_tile, key_tiles, key_blocks, tokens, w_key, w_value):
-    list_len = key_tiles.shape[2]
-    rows = tokens.shape[0]
-    entries = rows // BLK * list_len
-    smem = pl.BlockSpec(memory_space=pltpu.SMEM)
+def project(tokens, w_key, w_value):
     args = (tokens, w_key, w_value)
-    slots = MAJOR * plane * CAP + 1
     return pl.pallas_call(
-        functools.partial(project_kernel, plane, list_len),
-        in_specs=[smem] * 3 + [pl.BlockSpec(memory_space=pl.ANY)] * 3,
-        out_specs=[WHOLE] + [smem] * 3,
-        out_shape=[jax.ShapeDtypeStruct((rows, 2 * KV), BF16)]
-        + [jax.ShapeDtypeStruct((n,), jnp.int32) for n in (entries, entries, slots)],
+        project_kernel,
+        in_specs=[pl.BlockSpec(memory_space=pl.ANY)] * 3,
+        out_specs=WHOLE,
+        out_shape=jax.ShapeDtypeStruct((tokens.shape[0], 2 * KV), BF16),
         scratch_shapes=[pltpu.VMEM(x.shape, BF16) for x in args]
-        + [pltpu.SMEM((MAJOR * plane,), jnp.int32), pltpu.SemaphoreType.DMA((8,))],
+        + [pltpu.SemaphoreType.DMA((8,))],
         compiler_params=params(56),
         name="project",
-    )(my_tile.reshape(1), key_tiles, key_blocks, *args)
+    )(*args)
 
 
 def pack_kernel(first, wanted_ref, tile_ref, *outs):
@@ -397,8 +351,10 @@
     tile_count = lax.axis_size("tile")
     plane = tile_count // MAJOR
     my_tile = lax.axis_index("tile")
+    my_row, my_place = my_tile // plane, my_tile % plane
     block_count = rows // BLK
     list_len = key_tiles.shape[2]
+    entry_count = block_count * list_len
 
     def swap(value, d, cross):
         pairs = [
@@ -420,10 +376,29 @@
             moved.append(lax.ppermute(value, "tile", pairs))
         return moved
 
-    mine, gets, puts, wanted = project(
-        plane, my_tile, key_tiles, key_blocks, tokens, w_key, w_value
-    )
-    mine = mine.reshape(block_count, BLK, 2 * KV)
+    def plane_rows(table):
+        table = table[0].reshape(MAJOR, plane, entry_count)
+        return lax.dynamic_index_in_dim(table, my_row, 0, keepdims=False)
+
+    def mine_of(table):
+        return lax.dynamic_index_in_dim(table, my_place, 0, keepdims=False)
+
+    tiles, picks = plane_rows(key_tiles), plane_rows(key_blocks)
+    earlier = jnp.arange(entry_count)[:, None] > jnp.arange(entry_count)[None, :]
+    same = (tiles[:, :, None] == tiles[:, None, :]) & earlier[None]
+    ranks = jnp.sum(same.astype(jnp.int32), axis=2)
+    groups, columns = (tiles // plane) ^ my_row, tiles % plane
+    my_source = mine_of(groups) * plane + (mine_of(columns) ^ my_place)
+    puts = my_source * CODE + mine_of(ranks)
+    gets = jnp.where(my_source % plane == 0, my_source * CODE + mine_of(picks), puts)
+    ids = jnp.arange(MAJOR * CAP, dtype=jnp.int32)
+    slots = groups * CAP + ranks
+    hits = (slots[:, None, :] == ids[None, :, None]) & (columns == my_place)[:, None, :]
+    wanted = jnp.sum(jnp.where(hits, picks[:, None, :] + 1, 0), axis=2) - 1
+    wanted = wanted[jnp.arange(plane) ^ my_place].reshape(plane, MAJOR, CAP)
+    wanted = wanted.transpose(1, 0, 2).reshape(-1)
+
+    mine = project(tokens, w_key, w_value).reshape(block_count, BLK, 2 * KV)
     next_tile = swap(mine, 1, 1)
     own_tile = swap(mine, 0, 1)
     far_tile = swap(after(mine, own_tile), 2, 1)
@@ -453,13 +428,15 @@
     last_sum = swap(last_sum, 1, 0).astype(F32)
     far_sum = owner_sum(2, wanted, [back[2][0], *far], block_count, F32, FAR_SUM_FLOPS)
     far_sum = (far_sum + last_sum).astype(BF16)
+    beside[0] = after(beside[0], far_sum)
     next_sum = owner_sum(1, wanted, [back[1][0], *beside], block_count, BF16, 0)
     own = spread([after(after(x, far_sum), next_sum) for x in back[0][1:]], beside)
     own_sum = owner_sum(0, wanted, [back[0][0], *own], block_count, BF16, 0)
-    far_grad = swap(far_sum, 2, 1).reshape(rows, 2 * KV)
-    near_grads = [x.reshape(rows, 2 * KV) for x in (swap(next_sum, 1, 1), swap(own_sum, 0, 1))]
+    sums = (swap(far_sum, 2, 1), swap(next_sum, 1, 1), swap(own_sum, 0, 1))
+    far_grad, next_grad, own_grad = (x.reshape(rows, 2 * KV) for x in sums)
     query_term = finish([far_grad], query_term, w_key, w_value, F32, FAR_FLOPS)
-    input_grad = finish(near_grads, query_term, w_key, w_value, BF16, 800_000_000)
+    query_term = finish([next_grad], query_term, w_key, w_value, F32, NEXT_FLOPS)
+    input_grad = finish([own_grad], query_term, w_key, w_value, BF16, 800_000_000)
     return (layer_out[None], input_grad[None])
 
 

time: 158 us -> 162 us (1.025)
  Pallas kernels: 30.3 us -> 35.3 us
  other arithmetic: 0.17 us -> 2.44 us
  waiting for transfers between devices: 76.1 us -> 73.9 us
  matrix products: 7.41 us -> 5.64 us
    pallas_call x1, Pallas kernels: 17.3 us -> 22.7 us  [attention(): pl.pallas_call(functools.partial(attention_kernel, list_len, per_step), g...]
    ppermute x8, waiting for transfers between devices: 27.1 us -> 23.4 us  [swap(): return lax.ppermute(value, ('vintage', 'tile'), pairs)]
    ppermute x24, starting transfers between devices: 31.9 us -> 34.3 us  [spread(): moved.append(lax.ppermute(value, 'tile', pairs))]
    unnamed x78 -> x24, local copies, waits for them, and re-layouts: 4.4 us -> 2.07 us
    pallas_call x1, Pallas kernels: 5.19 us -> 3.4 us  [project(): pl.pallas_call(project_kernel, in_specs=[pl.BlockSpec(memory_space=pl.ANY...]
  transfers between devices with their start and end apart: 32 -> 32, of which waited for: 15 -> 16; matrix products, arithmetic and copies ran while one was open for 5% -> 6% of each run, Pallas kernels for 4% -> 5%
where the time goes in v12:
time: 162 us; the launch traced here: 161 us
  waiting for transfers between devices  73.9 us (46%)
  starting transfers between devices  40.1 us (25%)
  Pallas kernels  35.3 us (22%)
  matrix products  5.64 us (3%)
  local copies, waits for them, and re-layouts  3.08 us (2%)
  other arithmetic  2.44 us (2%)
    ppermute x24, waiting for transfers between devices, spread(): moved.append(lax.ppermute(value, 'tile', pairs))  50.5 us
    ppermute x24, starting transfers between devices, spread(): moved.append(lax.ppermute(value, 'tile', pairs))  34.3 us
    ppermute x8, waiting for transfers between devices, swap(): return lax.ppermute(value, ('vintage', 'tile'), pairs)  23.4 us
    pallas_call x1, Pallas kernels, attention(): pl.pallas_call(functools.partial(attention_kernel, list_len, per_step), g...  22.7 us
    ppermute x8, starting transfers between devices, swap(): return lax.ppermute(value, ('vintage', 'tile'), pairs)  5.82 us
    pallas_call x1, Pallas kernels, project(): pl.pallas_call(project_kernel, in_specs=[pl.BlockSpec(memory_space=pl.ANY...  3.4 us
    pallas_call x4, Pallas kernels, pack(): pl.pallas_call(functools.partial(pack_kernel, group * plane * CAP), in_sp...  3.3 us
  transfers between devices with their start and end apart: 32, of which 16 were waited for; matrix products, arithmetic and copies ran while one was open for 6% of the time, Pallas kernels for 5%

profile of v12, /device:TPU:0, one launch (start us, length us, event | category | flops | bytes accessed | tf_op | source)
XLA Modules:
  0.0 161.3 jit_solution(16353566511891556908)
XLA Ops:
  0.7 3.4 %project.1 = bf16[512,512]{1,0:T(8,128)(2,1)} custom-call(bf16[512,768]{1,0:T(8,128)(2,1)} %bitcast.51, bf16[768,256]{1,0:T(8,128)(2,1)} %refs_2_.5, bf16[768,256]{1,0:T(8,128)(2,1)} %refs_3_.5), custom_call_target="tpu_custom_call" | custom-call | tf_op jit(solution)/shard_map/project/pallas_call | solution.py:264
  4.1 2.5 %collective-permute-start.4 = (bf16[4,128,512]{2,1,0:T(8,128)(2,1)}, bf16[4,128,512]{2,1,0:T(8,128)(2,1)S(1)}, u32[]{:S(2)}, u32[]{:S(2)}) collective-permute-start(bf16[4,128,512]{2,1,0:T(8,128)(2,1)} %bitcast.52), channel_id=1, source_target_pairs={{0,20},{1,21},{2,22},{3,23},{4,16},{5,17},{6,18},{7,19},{8,28},{9,... | collective-permute-start | bytes 1572872 | tf_op jit(solution)/shard_map/ppermute | solution.py:365
  9.2 2.4 %collective-permute-start.8 = (bf16[4,128,512]{2,1,0:T(8,128)(2,1)}, bf16[4,128,512]{2,1,0:T(8,128)(2,1)S(1)}, u32[]{:S(2)}, u32[]{:S(2)}) collective-permute-start(bf16[4,128,512]{2,1,0:T(8,128)(2,1)} %bitcast.54), channel_id=1, source_target_pairs={{0,24},{1,25},{2,26},{3,27},{4,28},{5,29},{6,30},{7,31},{8,16},{9,... | collective-permute-start | bytes 1572872 | tf_op jit(solution)/shard_map/ppermute | solution.py:365
  13.1 2.5 %collective-permute-start.3 = (bf16[2,128,512]{2,1,0:T(8,128)(2,1)S(1)}, bf16[2,128,512]{2,1,0:T(8,128)(2,1)S(1)}, u32[]{:S(2)}, u32[]{:S(2)}) collective-permute-start(bf16[2,128,512]{2,1,0:T(8,128)(2,1)S(1)} %get-tuple-element.64), channel_id=1, source_target_pairs={{0,3},{1,2},{2,1},{3,0},{4,7},{5,6},{6,5},{7,4},{8,11},{9,10},{10,... | collective-permute-start | bytes 786440 | tf_op jit(solution)/shard_map/ppermute | solution.py:376
  16.6 10.6 %collective-permute-done.4.tile_ref.refs_4_ = bf16[4,128,512]{2,1,0:T(8,128)(2,1)S(1)} collective-permute-done((bf16[4,128,512]{2,1,0:T(8,128)(2,1)}, bf16[4,128,512]{2,1,0:T(8,128)(2,1)S(1)}, u32[]{:S(2)}, u32[]{:S(2)}) %collective-permute-start.4) | collective-permute-done | bytes 524320 | tf_op jit(solution)/shard_map/ppermute | solution.py:365
  27.2 1.5 pack.5
  28.7 3.9 %collective-permute-start.7 = (bf16[2,128,512]{2,1,0:T(8,128)(2,1)}, bf16[2,128,512]{2,1,0:T(8,128)(2,1)}, u32[]{:S(2)}, u32[]{:S(2)}) collective-permute-start(bf16[2,128,512]{2,1,0:T(8,128)(2,1)} %get-tuple-element.70), channel_id=1, source_target_pairs={{0,3},{1,2},{2,1},{3,0},{4,7},{5,6},{6,5},{7,4},{8,11},{9,10},{10,... | collective-permute-start | bytes 786440 | tf_op jit(solution)/shard_map/ppermute | solution.py:376
  32.5 0.7 copy-done.3
  33.7 0.7 copy-done.5
  34.5 1.1 collective-permute-done.8.tile_ref.refs_8_
  35.7 0.7 compare_select_fusion.3
  37.0 3.0 %collective-permute-done.7.refs_7_ = bf16[2,128,512]{2,1,0:T(8,128)(2,1)} collective-permute-done((bf16[2,128,512]{2,1,0:T(8,128)(2,1)}, bf16[2,128,512]{2,1,0:T(8,128)(2,1)}, u32[]{:S(2)}, u32[]{:S(2)}) %collective-permute-start.7) | collective-permute-done | bytes 262176 | tf_op jit(solution)/shard_map/ppermute | solution.py:376
  40.0 3.0 %collective-permute-start.11 = (bf16[2,128,512]{2,1,0:T(8,128)(2,1)S(1)}, bf16[2,128,512]{2,1,0:T(8,128)(2,1)S(1)}, u32[]{:S(2)}, u32[]{:S(2)}) collective-permute-start(bf16[2,128,512]{2,1,0:T(8,128)(2,1)S(1)} %get-tuple-element.78), channel_id=1, source_target_pairs={{0,3},{1,2},{2,1},{3,0},{4,7},{5,6},{6,5},{7,4},{8,11},{9,10},{10,... | collective-permute-start | bytes 786440 | tf_op jit(solution)/shard_map/ppermute | solution.py:376
  42.9 2.6 %collective-permute-done.6.refs_6_ = bf16[2,128,512]{2,1,0:T(8,128)(2,1)} collective-permute-done((bf16[2,128,512]{2,1,0:T(8,128)(2,1)}, bf16[2,128,512]{2,1,0:T(8,128)(2,1)}, u32[]{:S(2)}, u32[]{:S(2)}) %collective-permute-start.6) | collective-permute-done | bytes 262176 | tf_op jit(solution)/shard_map/ppermute | solution.py:376
  45.5 2.0 %collective-permute-start.10 = (bf16[2,128,512]{2,1,0:T(8,128)(2,1)S(1)}, bf16[2,128,512]{2,1,0:T(8,128)(2,1)S(1)}, u32[]{:S(2)}, u32[]{:S(2)}) collective-permute-start(bf16[2,128,512]{2,1,0:T(8,128)(2,1)S(1)} %get-tuple-element.76), channel_id=1, source_target_pairs={{0,2},{1,3},{2,0},{3,1},{4,6},{5,7},{6,4},{7,5},{8,10},{9,11},{10,... | collective-permute-start | bytes 786440 | tf_op jit(solution)/shard_map/ppermute | solution.py:376
  47.5 1.1 collective-permute-start.9
  48.6 2.3 %fusion.ng_ref = f32[768,512]{1,0:T(8,128)S(1)} fusion(bf16[768,768]{1,0:T(8,128)(2,1)} %param.13, bf16[1,512,768]{2,1,0:T(8,128)(2,1)} %param.9), kind=kOutput, calls=%fused_computation.4 | convolution fusion | flops 603979776 | bytes 3538944 | tf_op jit(solution)/shard_map/dot_general | solution.py:35
  51.6 2.5 %collective-permute-start.15 = (bf16[2,128,512]{2,1,0:T(8,128)(2,1)S(1)}, bf16[2,128,512]{2,1,0:T(8,128)(2,1)S(1)}, u32[]{:S(2)}, u32[]{:S(2)}) collective-permute-start(bf16[2,128,512]{2,1,0:T(8,128)(2,1)S(1)} %get-tuple-element.84), channel_id=1, source_target_pairs={{0,3},{1,2},{2,1},{3,0},{4,7},{5,6},{6,5},{7,4},{8,11},{9,10},{10,... | collective-permute-start | bytes 786440 | tf_op jit(solution)/shard_map/ppermute | solution.py:376
  54.1 2.6 %collective-permute-done.10.refs_10_ = bf16[2,128,512]{2,1,0:T(8,128)(2,1)S(1)} collective-permute-done((bf16[2,128,512]{2,1,0:T(8,128)(2,1)S(1)}, bf16[2,128,512]{2,1,0:T(8,128)(2,1)S(1)}, u32[]{:S(2)}, u32[]{:S(2)}) %collective-permute-start.10) | collective-permute-done | bytes 262176 | tf_op jit(solution)/shard_map/ppermute | solution.py:376
  56.7 2.1 %collective-permute-start.14 = (bf16[2,128,512]{2,1,0:T(8,128)(2,1)S(1)}, bf16[2,128,512]{2,1,0:T(8,128)(2,1)S(1)}, u32[]{:S(2)}, u32[]{:S(2)}) collective-permute-start(bf16[2,128,512]{2,1,0:T(8,128)(2,1)S(1)} %get-tuple-element.82), channel_id=1, source_target_pairs={{0,2},{1,3},{2,0},{3,1},{4,6},{5,7},{6,4},{7,5},{8,10},{9,11},{10,... | collective-permute-start | bytes 786440 | tf_op jit(solution)/shard_map/ppermute | solution.py:376
  58.7 1.5 collective-permute-start.13
  60.2 0.8 convolution_convert_fusion.1.q_ref
  61.1 1.4 collective-permute-done.15.refs_15_
  62.4 5.2 %collective-permute-done.14.refs_14_ = bf16[2,128,512]{2,1,0:T(8,128)(2,1)S(1)} collective-permute-done((bf16[2,128,512]{2,1,0:T(8,128)(2,1)S(1)}, bf16[2,128,512]{2,1,0:T(8,128)(2,1)S(1)}, u32[]{:S(2)}, u32[]{:S(2)}) %collective-permute-start.14) | collective-permute-done | bytes 262176 | tf_op jit(solution)/shard_map/ppermute | solution.py:376
  67.9 22.7 %attention.1 = (bf16[768,512]{1,0:T(8,128)(2,1)S(1)}, bf16[768,512]{1,0:T(8,128)(2,1)S(1)}, bf16[2,128,512]{2,1,0:T(8,128)(2,1)S(1)}, bf16[2,128,512]{2,1,0:T(8,...) custom-call(s32[16]{0:T(128)S(1)} %get-tuple-element.127.get_ref, ...), custom_call_target="tpu_custom_call" | custom-call | flops 2415919104 | bytes 6291456 | tf_op jit(solution)/shard_map/attention/pallas_call | solution.py:216
  90.6 1.6 collective-permute-start.16
  92.2 1.5 collective-permute-start.18
  94.2 0.8 fusion.17.refs_1_
  95.5 1.7 %convolution_convert_fusion = bf16[512,768]{1,0:T(8,128)(2,1)} fusion(bf16[768,512]{1,0:T(8,128)(2,1)S(1)} %get-tuple-element.87, bf16[768,768]{1,0:T(8,128)(2,1)S(1)} %copy-done.10), kind=kOutput, calls=%fused_computation.1 | convolution fusion | flops 604372992 | bytes 2752512 | tf_op jit(solution)/shard_map/dot_general | solution.py:39
  97.2 8.6 %collective-permute-done.18.refs_2_ = bf16[2,128,512]{2,1,0:T(8,128)(2,1)S(1)} collective-permute-done((bf16[2,128,512]{2,1,0:T(8,128)(2,1)S(1)}, bf16[2,128,512]{2,1,0:T(8,128)(2,1)S(1)}, u32[]{:S(2)}, u32[]{:S(2)}) %collective-permute-start.18) | collective-permute-done | bytes 262176 | tf_op jit(solution)/shard_map/ppermute | solution.py:376
  105.7 1.5 collective-permute-start.19
  107.4 1.8 %collective-permute-start.17 = (bf16[2,128,512]{2,1,0:T(8,128)(2,1)S(1)}, bf16[2,128,512]{2,1,0:T(8,128)(2,1)S(1)}, u32[]{:S(2)}, u32[]{:S(2)}) collective-permute-start(bf16[2,128,512]{2,1,0:T(8,128)(2,1)S(1)} %get-tuple-element.94), channel_id=1, source_target_pairs={{0,1},{1,0},{2,3},{3,2},{4,5},{5,4},{6,7},{7,6},{8,9},{9,8},{10,11... | collective-permute-start | bytes 786440 | tf_op jit(solution)/shard_map/ppermute | solution.py:376
  109.2 0.8 owner_sum.5
  110.1 8.0 %collective-permute-done.19.refs_2_ = bf16[2,128,512]{2,1,0:T(8,128)(2,1)S(1)} collective-permute-done((bf16[2,128,512]{2,1,0:T(8,128)(2,1)S(1)}, bf16[2,128,512]{2,1,0:T(8,128)(2,1)S(1)}, u32[]{:S(2)}, u32[]{:S(2)}) %collective-permute-start.19) | collective-permute-done | bytes 262176 | tf_op jit(solution)/shard_map/ppermute | solution.py:376
  118.1 1.7 %collective-permute-start.24 = (bf16[2,128,512]{2,1,0:T(8,128)(2,1)S(1)}, bf16[2,128,512]{2,1,0:T(8,128)(2,1)S(1)}, u32[]{:S(2)}, u32[]{:S(2)}) collective-permute-start(bf16[2,128,512]{2,1,0:T(8,128)(2,1)S(1)} %get-tuple-element.108), channel_id=1, source_target_pairs={{0,2},{1,3},{2,0},{3,1},{4,6},{5,7},{6,4},{7,5},{8,10},{9,11},{10,... | collective-permute-start | bytes 786440 | tf_op jit(solution)/shard_map/ppermute | solution.py:376
  120.4 1.2 collective-permute-start.23
  121.6 0.8 owner_sum.4
  122.7 9.5 %collective-permute-done.23.refs_1_ = bf16[2,128,512]{2,1,0:T(8,128)(2,1)S(1)} collective-permute-done((bf16[2,128,512]{2,1,0:T(8,128)(2,1)S(1)}, bf16[2,128,512]{2,1,0:T(8,128)(2,1)S(1)}, u32[]{:S(2)}, u32[]{:S(2)}) %collective-permute-start.23) | collective-permute-done | bytes 262176 | tf_op jit(solution)/shard_map/ppermute | solution.py:376
  132.2 0.8 owner_sum.6
  133.7 1.2 collective-permute-start.27
  134.9 1.7 %collective-permute-start.28 = (bf16[2,128,512]{2,1,0:T(8,128)(2,1)S(1)}, bf16[2,128,512]{2,1,0:T(8,128)(2,1)S(1)}, u32[]{:S(2)}, u32[]{:S(2)}) collective-permute-start(bf16[2,128,512]{2,1,0:T(8,128)(2,1)S(1)} %get-tuple-element.120), channel_id=1, source_target_pairs={{0,3},{1,2},{2,1},{3,0},{4,7},{5,6},{6,5},{7,4},{8,11},{9,10},{10,... | collective-permute-start | bytes 786440 | tf_op jit(solution)/shard_map/ppermute | solution.py:376
  136.6 5.4 %collective-permute-done.26.refs_1_ = bf16[2,128,512]{2,1,0:T(8,128)(2,1)S(1)} collective-permute-done((bf16[2,128,512]{2,1,0:T(8,128)(2,1)S(1)}, bf16[2,128,512]{2,1,0:T(8,128)(2,1)S(1)}, u32[]{:S(2)}, u32[]{:S(2)}) %collective-permute-start.26) | collective-permute-done | bytes 262176 | tf_op jit(solution)/shard_map/ppermute | solution.py:376
  142.0 2.2 %collective-permute-done.27.refs_2_ = bf16[2,128,512]{2,1,0:T(8,128)(2,1)S(1)} collective-permute-done((bf16[2,128,512]{2,1,0:T(8,128)(2,1)S(1)}, bf16[2,128,512]{2,1,0:T(8,128)(2,1)S(1)}, u32[]{:S(2)}, u32[]{:S(2)}) %collective-permute-start.27) | collective-permute-done | bytes 262176 | tf_op jit(solution)/shard_map/ppermute | solution.py:376
  144.2 1.8 %collective-permute-done.28.refs_3_ = bf16[2,128,512]{2,1,0:T(8,128)(2,1)S(1)} collective-permute-done((bf16[2,128,512]{2,1,0:T(8,128)(2,1)S(1)}, bf16[2,128,512]{2,1,0:T(8,128)(2,1)S(1)}, u32[]{:S(2)}, u32[]{:S(2)}) %collective-permute-start.28) | collective-permute-done | bytes 262176 | tf_op jit(solution)/shard_map/ppermute | solution.py:376
  146.0 0.8 owner_sum.7
  146.9 1.2 collective-permute-done.31
  148.7 10.5 %collective-permute-done.30 = bf16[4,128,512]{2,1,0:T(8,128)(2,1)S(1)} collective-permute-done((bf16[4,128,512]{2,1,0:T(8,128)(2,1)S(1)}, bf16[4,128,512]{2,1,0:T(8,128)(2,1)S(1)}, u32[]{:S(2)}, u32[]{:S(2)}) %collective-permute-start.30) | collective-permute-done | bytes 524320 | tf_op jit(solution)/shard_map/ppermute | solution.py:365
  159.9 1.5 finish.5
  (74 shorter events, 11.1 us)
Async XLA Ops:
  0.6 59.6 %copy-start = (bf16[768,768]{1,0:T(8,128)(2,1)S(1)}, bf16[768,768]{1,0:T(8,128)(2,1)}, u32[]{:S(2)}) copy-start(bf16[768,768]{1,0:T(8,128)(2,1)} %param.10) | copy-start | bytes 3538948
  0.6 6.6 %copy-start.8 = (s32[1,64,4]{1,2,0:T(4,128)S(1)}, s32[1,64,4]{1,2,0:T(4,128)}, u32[]{:S(2)}) copy-start(s32[1,64,4]{1,2,0:T(4,128)} %param.14) | copy-start | bytes 3076
  0.7 6.8 %copy-start.9 = (s32[1,64,4]{1,2,0:T(4,128)S(1)}, s32[1,64,4]{1,2,0:T(4,128)}, u32[]{:S(2)}) copy-start(s32[1,64,4]{1,2,0:T(4,128)} %param.15) | copy-start | bytes 3076
  4.1 23.1 %collective-permute-start.4 = (bf16[4,128,512]{2,1,0:T(8,128)(2,1)}, bf16[4,128,512]{2,1,0:T(8,128)(2,1)S(1)}, u32[]{:S(2)}, u32[]{:S(2)}) collective-permute-start(bf16[4,128,512]{2,1,0:T(8,128)(2,1)} %bitcast.52), channel_id=1, source_target_pairs={{0,20},{1,21},{2,22},{3,23},{4,16},{5,17},{6,18},{7,19},{8,28},{9,... | collective-permute-start | bytes 1572872 | tf_op jit(solution)/shard_map/ppermute | solution.py:365
  6.6 2.6 %collective-permute-start = (bf16[4,128,512]{2,1,0:T(8,128)(2,1)}, bf16[4,128,512]{2,1,0:T(8,128)(2,1)S(1)}, u32[]{:S(2)}, u32[]{:S(2)}) collective-permute-start(bf16[4,128,512]{2,1,0:T(8,128)(2,1)} %bitcast.53), channel_id=1, source_target_pairs={{0,16},{1,17},{2,18},{3,19},{4,20},{5,21},{6,22},{7,23},{8,24},{9,... | collective-permute-start | bytes 1572872 | tf_op jit(solution)/shard_map/ppermute | solution.py:365
  9.2 26.4 %collective-permute-start.8 = (bf16[4,128,512]{2,1,0:T(8,128)(2,1)}, bf16[4,128,512]{2,1,0:T(8,128)(2,1)S(1)}, u32[]{:S(2)}, u32[]{:S(2)}) collective-permute-start(bf16[4,128,512]{2,1,0:T(8,128)(2,1)} %bitcast.54), channel_id=1, source_target_pairs={{0,24},{1,25},{2,26},{3,27},{4,28},{5,29},{6,30},{7,31},{8,16},{9,... | collective-permute-start | bytes 1572872 | tf_op jit(solution)/shard_map/ppermute | solution.py:365
  13.1 15.6 %collective-permute-start.3 = (bf16[2,128,512]{2,1,0:T(8,128)(2,1)S(1)}, bf16[2,128,512]{2,1,0:T(8,128)(2,1)S(1)}, u32[]{:S(2)}, u32[]{:S(2)}) collective-permute-start(bf16[2,128,512]{2,1,0:T(8,128)(2,1)S(1)} %get-tuple-element.64), channel_id=1, source_target_pairs={{0,3},{1,2},{2,1},{3,0},{4,7},{5,6},{6,5},{7,4},{8,11},{9,10},{10,... | collective-permute-start | bytes 786440 | tf_op jit(solution)/shard_map/ppermute | solution.py:376
  15.6 17.0 %collective-permute-start.2 = (bf16[2,128,512]{2,1,0:T(8,128)(2,1)S(1)}, bf16[2,128,512]{2,1,0:T(8,128)(2,1)S(1)}, u32[]{:S(2)}, u32[]{:S(2)}) collective-permute-start(bf16[2,128,512]{2,1,0:T(8,128)(2,1)S(1)} %get-tuple-element.63), channel_id=1, source_target_pairs={{0,2},{1,3},{2,0},{3,1},{4,6},{5,7},{6,4},{7,5},{8,10},{9,11},{10,... | collective-permute-start | bytes 786440 | tf_op jit(solution)/shard_map/ppermute | solution.py:376
  16.1 17.7 %collective-permute-start.1 = (bf16[2,128,512]{2,1,0:T(8,128)(2,1)S(1)}, bf16[2,128,512]{2,1,0:T(8,128)(2,1)S(1)}, u32[]{:S(2)}, u32[]{:S(2)}) collective-permute-start(bf16[2,128,512]{2,1,0:T(8,128)(2,1)S(1)} %get-tuple-element.62), channel_id=1, source_target_pairs={{0,1},{1,0},{2,3},{3,2},{4,5},{5,4},{6,7},{7,6},{8,9},{9,8},{10,11... | collective-permute-start | bytes 786440 | tf_op jit(solution)/shard_map/ppermute | solution.py:376
  28.7 11.3 %collective-permute-start.7 = (bf16[2,128,512]{2,1,0:T(8,128)(2,1)}, bf16[2,128,512]{2,1,0:T(8,128)(2,1)}, u32[]{:S(2)}, u32[]{:S(2)}) collective-permute-start(bf16[2,128,512]{2,1,0:T(8,128)(2,1)} %get-tuple-element.70), channel_id=1, source_target_pairs={{0,3},{1,2},{2,1},{3,0},{4,7},{5,6},{6,5},{7,4},{8,11},{9,10},{10,... | collective-permute-start | bytes 786440 | tf_op jit(solution)/shard_map/ppermute | solution.py:376
  32.5 0.7 copy-start.3
  33.2 12.3 %collective-permute-start.6 = (bf16[2,128,512]{2,1,0:T(8,128)(2,1)}, bf16[2,128,512]{2,1,0:T(8,128)(2,1)}, u32[]{:S(2)}, u32[]{:S(2)}) collective-permute-start(bf16[2,128,512]{2,1,0:T(8,128)(2,1)} %get-tuple-element.68), channel_id=1, source_target_pairs={{0,2},{1,3},{2,0},{3,1},{4,6},{5,7},{6,4},{7,5},{8,10},{9,11},{10,... | collective-permute-start | bytes 786440 | tf_op jit(solution)/shard_map/ppermute | solution.py:376
  33.7 0.7 copy-start.5
  34.5 13.1 %collective-permute-start.5 = (bf16[2,128,512]{2,1,0:T(8,128)(2,1)}, bf16[2,128,512]{2,1,0:T(8,128)(2,1)}, u32[]{:S(2)}, u32[]{:S(2)}) collective-permute-start(bf16[2,128,512]{2,1,0:T(8,128)(2,1)} %get-tuple-element.66), channel_id=1, source_target_pairs={{0,1},{1,0},{2,3},{3,2},{4,5},{5,4},{6,7},{7,6},{8,9},{9,8},{10,11... | collective-permute-start | bytes 786440 | tf_op jit(solution)/shard_map/ppermute | solution.py:376
  35.6 15.3 %collective-permute-start.12 = (bf16[4,128,512]{2,1,0:T(8,128)(2,1)S(1)}, bf16[4,128,512]{2,1,0:T(8,128)(2,1)S(1)}, u32[]{:S(2)}, u32[]{:S(2)}) collective-permute-start(bf16[4,128,512]{2,1,0:T(8,128)(2,1)S(1)} %collective-permute-done.8.tile_ref.refs_8_), channel_id=1, source_target_pairs={{0,4},{1,5},{2,6},{3,7},{4,0},{5,1},{6,2},{7,3},{8,12},{9,13},{10,... | collective-permute-start | bytes 1572872 | tf_op jit(solution)/shard_map/ppermute | solution.py:365
  40.0 11.6 %collective-permute-start.11 = (bf16[2,128,512]{2,1,0:T(8,128)(2,1)S(1)}, bf16[2,128,512]{2,1,0:T(8,128)(2,1)S(1)}, u32[]{:S(2)}, u32[]{:S(2)}) collective-permute-start(bf16[2,128,512]{2,1,0:T(8,128)(2,1)S(1)} %get-tuple-element.78), channel_id=1, source_target_pairs={{0,3},{1,2},{2,1},{3,0},{4,7},{5,6},{6,5},{7,4},{8,11},{9,10},{10,... | collective-permute-start | bytes 786440 | tf_op jit(solution)/shard_map/ppermute | solution.py:376
  45.5 11.2 %collective-permute-start.10 = (bf16[2,128,512]{2,1,0:T(8,128)(2,1)S(1)}, bf16[2,128,512]{2,1,0:T(8,128)(2,1)S(1)}, u32[]{:S(2)}, u32[]{:S(2)}) collective-permute-start(bf16[2,128,512]{2,1,0:T(8,128)(2,1)S(1)} %get-tuple-element.76), channel_id=1, source_target_pairs={{0,2},{1,3},{2,0},{3,1},{4,6},{5,7},{6,4},{7,5},{8,10},{9,11},{10,... | collective-permute-start | bytes 786440 | tf_op jit(solution)/shard_map/ppermute | solution.py:376
  47.5 12.7 %copy-start.7 = (bf16[1,512,768]{2,1,0:T(8,128)(2,1)S(1)}, bf16[1,512,768]{2,1,0:T(8,128)(2,1)}, u32[]{:S(2)}) copy-start(bf16[1,512,768]{2,1,0:T(8,128)(2,1)} %param.8) | copy-start | bytes 2359300
  47.5 11.2 %collective-permute-start.9 = (bf16[2,128,512]{2,1,0:T(8,128)(2,1)S(1)}, bf16[2,128,512]{2,1,0:T(8,128)(2,1)S(1)}, u32[]{:S(2)}, u32[]{:S(2)}) collective-permute-start(bf16[2,128,512]{2,1,0:T(8,128)(2,1)S(1)} %get-tuple-element.74), channel_id=1, source_target_pairs={{0,1},{1,0},{2,3},{3,2},{4,5},{5,4},{6,7},{7,6},{8,9},{9,8},{10,11... | collective-permute-start | bytes 786440 | tf_op jit(solution)/shard_map/ppermute | solution.py:376
  51.6 10.9 %collective-permute-start.15 = (bf16[2,128,512]{2,1,0:T(8,128)(2,1)S(1)}, bf16[2,128,512]{2,1,0:T(8,128)(2,1)S(1)}, u32[]{:S(2)}, u32[]{:S(2)}) collective-permute-start(bf16[2,128,512]{2,1,0:T(8,128)(2,1)S(1)} %get-tuple-element.84), channel_id=1, source_target_pairs={{0,3},{1,2},{2,1},{3,0},{4,7},{5,6},{6,5},{7,4},{8,11},{9,10},{10,... | collective-permute-start | bytes 786440 | tf_op jit(solution)/shard_map/ppermute | solution.py:376
  56.7 11.0 %collective-permute-start.14 = (bf16[2,128,512]{2,1,0:T(8,128)(2,1)S(1)}, bf16[2,128,512]{2,1,0:T(8,128)(2,1)S(1)}, u32[]{:S(2)}, u32[]{:S(2)}) collective-permute-start(bf16[2,128,512]{2,1,0:T(8,128)(2,1)S(1)} %get-tuple-element.82), channel_id=1, source_target_pairs={{0,2},{1,3},{2,0},{3,1},{4,6},{5,7},{6,4},{7,5},{8,10},{9,11},{10,... | collective-permute-start | bytes 786440 | tf_op jit(solution)/shard_map/ppermute | solution.py:376
  58.7 9.2 %copy-start.4 = (bf16[2,128,512]{2,1,0:T(8,128)(2,1)S(1)}, bf16[2,128,512]{2,1,0:T(8,128)(2,1)}, u32[]{:S(2)}) copy-start(bf16[2,128,512]{2,1,0:T(8,128)(2,1)} %copy-done.3) | copy-start | bytes 786436
  58.7 9.2 %copy-start.6 = (bf16[2,128,512]{2,1,0:T(8,128)(2,1)S(1)}, bf16[2,128,512]{2,1,0:T(8,128)(2,1)}, u32[]{:S(2)}) copy-start(bf16[2,128,512]{2,1,0:T(8,128)(2,1)} %copy-done.5) | copy-start | bytes 786436
  58.7 9.2 %collective-permute-start.13 = (bf16[2,128,512]{2,1,0:T(8,128)(2,1)S(1)}, bf16[2,128,512]{2,1,0:T(8,128)(2,1)S(1)}, u32[]{:S(2)}, u32[]{:S(2)}) collective-permute-start(bf16[2,128,512]{2,1,0:T(8,128)(2,1)S(1)} %get-tuple-element.80), channel_id=1, source_target_pairs={{0,1},{1,0},{2,3},{3,2},{4,5},{5,4},{6,7},{7,6},{8,9},{9,8},{10,11... | collective-permute-start | bytes 786440 | tf_op jit(solution)/shard_map/ppermute | solution.py:376
  90.6 16.7 %collective-permute-start.16 = (bf16[2,128,512]{2,1,0:T(8,128)(2,1)S(1)}, bf16[2,128,512]{2,1,0:T(8,128)(2,1)S(1)}, u32[]{:S(2)}, u32[]{:S(2)}) collective-permute-start(bf16[2,128,512]{2,1,0:T(8,128)(2,1)S(1)} %get-tuple-element.85), channel_id=1, source_target_pairs={{0,1},{1,0},{2,3},{3,2},{4,5},{5,4},{6,7},{7,6},{8,9},{9,8},{10,11... | collective-permute-start | bytes 786440 | tf_op jit(solution)/shard_map/ppermute | solution.py:376
  92.2 13.5 %collective-permute-start.18 = (bf16[2,128,512]{2,1,0:T(8,128)(2,1)S(1)}, bf16[2,128,512]{2,1,0:T(8,128)(2,1)S(1)}, u32[]{:S(2)}, u32[]{:S(2)}) collective-permute-start(bf16[2,128,512]{2,1,0:T(8,128)(2,1)S(1)} %get-tuple-element.96), channel_id=1, source_target_pairs={{0,2},{1,3},{2,0},{3,1},{4,6},{5,7},{6,4},{7,5},{8,10},{9,11},{10,... | collective-permute-start | bytes 786440 | tf_op jit(solution)/shard_map/ppermute | solution.py:376
  93.7 13.5 %collective-permute-start.20 = (bf16[2,128,512]{2,1,0:T(8,128)(2,1)S(1)}, bf16[2,128,512]{2,1,0:T(8,128)(2,1)S(1)}, u32[]{:S(2)}, u32[]{:S(2)}) collective-permute-start(bf16[2,128,512]{2,1,0:T(8,128)(2,1)S(1)} %get-tuple-element.99), channel_id=1, source_target_pairs={{0,3},{1,2},{2,1},{3,0},{4,7},{5,6},{6,5},{7,4},{8,11},{9,10},{10,... | collective-permute-start | bytes 786440 | tf_op jit(solution)/shard_map/ppermute | solution.py:376
  94.2 1.3 copy-start.10
  105.7 12.4 %collective-permute-start.19 = (bf16[2,128,512]{2,1,0:T(8,128)(2,1)S(1)}, bf16[2,128,512]{2,1,0:T(8,128)(2,1)S(1)}, u32[]{:S(2)}, u32[]{:S(2)}) collective-permute-start(bf16[2,128,512]{2,1,0:T(8,128)(2,1)S(1)} %get-tuple-element.97), channel_id=1, source_target_pairs={{0,2},{1,3},{2,0},{3,1},{4,6},{5,7},{6,4},{7,5},{8,10},{9,11},{10,... | collective-permute-start | bytes 786440 | tf_op jit(solution)/shard_map/ppermute | solution.py:376
  107.2 12.6 %collective-permute-start.21 = (bf16[2,128,512]{2,1,0:T(8,128)(2,1)S(1)}, bf16[2,128,512]{2,1,0:T(8,128)(2,1)S(1)}, u32[]{:S(2)}, u32[]{:S(2)}) collective-permute-start(bf16[2,128,512]{2,1,0:T(8,128)(2,1)S(1)} %get-tuple-element.100), channel_id=1, source_target_pairs={{0,3},{1,2},{2,1},{3,0},{4,7},{5,6},{6,5},{7,4},{8,11},{9,10},{10,... | collective-permute-start | bytes 786440 | tf_op jit(solution)/shard_map/ppermute | solution.py:376
  107.4 13.0 %collective-permute-start.17 = (bf16[2,128,512]{2,1,0:T(8,128)(2,1)S(1)}, bf16[2,128,512]{2,1,0:T(8,128)(2,1)S(1)}, u32[]{:S(2)}, u32[]{:S(2)}) collective-permute-start(bf16[2,128,512]{2,1,0:T(8,128)(2,1)S(1)} %get-tuple-element.94), channel_id=1, source_target_pairs={{0,1},{1,0},{2,3},{3,2},{4,5},{5,4},{6,7},{7,6},{8,9},{9,8},{10,11... | collective-permute-start | bytes 786440 | tf_op jit(solution)/shard_map/ppermute | solution.py:376
  110.0 12.4 %collective-permute-start.22 = (bf16[4,128,512]{2,1,0:T(8,128)(2,1)S(1)}, bf16[4,128,512]{2,1,0:T(8,128)(2,1)S(1)}, u32[]{:S(2)}, u32[]{:S(2)}) collective-permute-start(bf16[4,128,512]{2,1,0:T(8,128)(2,1)S(1)} %owner_sum.5), channel_id=1, source_target_pairs={{0,4},{1,5},{2,6},{3,7},{4,0},{5,1},{6,2},{7,3},{8,12},{9,13},{10,... | collective-permute-start | bytes 1572872 | tf_op jit(solution)/shard_map/ppermute | solution.py:365
  118.1 14.1 %collective-permute-start.24 = (bf16[2,128,512]{2,1,0:T(8,128)(2,1)S(1)}, bf16[2,128,512]{2,1,0:T(8,128)(2,1)S(1)}, u32[]{:S(2)}, u32[]{:S(2)}) collective-permute-start(bf16[2,128,512]{2,1,0:T(8,128)(2,1)S(1)} %get-tuple-element.108), channel_id=1, source_target_pairs={{0,2},{1,3},{2,0},{3,1},{4,6},{5,7},{6,4},{7,5},{8,10},{9,11},{10,... | collective-permute-start | bytes 786440 | tf_op jit(solution)/shard_map/ppermute | solution.py:376
  119.8 12.4 %collective-permute-start.25 = (bf16[2,128,512]{2,1,0:T(8,128)(2,1)S(1)}, bf16[2,128,512]{2,1,0:T(8,128)(2,1)S(1)}, u32[]{:S(2)}, u32[]{:S(2)}) collective-permute-start(bf16[2,128,512]{2,1,0:T(8,128)(2,1)S(1)} %get-tuple-element.110), channel_id=1, source_target_pairs={{0,3},{1,2},{2,1},{3,0},{4,7},{5,6},{6,5},{7,4},{8,11},{9,10},{10,... | collective-permute-start | bytes 786440 | tf_op jit(solution)/shard_map/ppermute | solution.py:376
  120.4 11.8 %collective-permute-start.23 = (bf16[2,128,512]{2,1,0:T(8,128)(2,1)S(1)}, bf16[2,128,512]{2,1,0:T(8,128)(2,1)S(1)}, u32[]{:S(2)}, u32[]{:S(2)}) collective-permute-start(bf16[2,128,512]{2,1,0:T(8,128)(2,1)S(1)} %get-tuple-element.105), channel_id=1, source_target_pairs={{0,1},{1,0},{2,3},{3,2},{4,5},{5,4},{6,7},{7,6},{8,9},{9,8},{10,11... | collective-permute-start | bytes 786440 | tf_op jit(solution)/shard_map/ppermute | solution.py:376
  122.6 25.5 %collective-permute-start.31 = (bf16[4,128,512]{2,1,0:T(8,128)(2,1)S(1)}, bf16[4,128,512]{2,1,0:T(8,128)(2,1)S(1)}, u32[]{:S(2)}, u32[]{:S(2)}) collective-permute-start(bf16[4,128,512]{2,1,0:T(8,128)(2,1)S(1)} %add_convert_fusion), channel_id=1, source_target_pairs={{0,24},{1,25},{2,26},{3,27},{4,28},{5,29},{6,30},{7,31},{8,16},{9,... | collective-permute-start | bytes 1572872 | tf_op jit(solution)/shard_map/ppermute | solution.py:365
  133.0 15.1 %copy-start.1 = (bf16[768,256]{1,0:T(8,128)(2,1)S(1)}, bf16[768,256]{1,0:T(8,128)(2,1)}, u32[]{:S(2)}) copy-start(bf16[768,256]{1,0:T(8,128)(2,1)} %refs_2_.5) | copy-start | bytes 1179652
  133.0 15.1 %copy-start.2 = (bf16[768,256]{1,0:T(8,128)(2,1)S(1)}, bf16[768,256]{1,0:T(8,128)(2,1)}, u32[]{:S(2)}) copy-start(bf16[768,256]{1,0:T(8,128)(2,1)} %refs_3_.5) | copy-start | bytes 1179652
  133.0 8.9 %collective-permute-start.26 = (bf16[2,128,512]{2,1,0:T(8,128)(2,1)S(1)}, bf16[2,128,512]{2,1,0:T(8,128)(2,1)S(1)}, u32[]{:S(2)}, u32[]{:S(2)}) collective-permute-start(bf16[2,128,512]{2,1,0:T(8,128)(2,1)S(1)} %get-tuple-element.112), channel_id=1, source_target_pairs={{0,1},{1,0},{2,3},{3,2},{4,5},{5,4},{6,7},{7,6},{8,9},{9,8},{10,11... | collective-permute-start | bytes 786440 | tf_op jit(solution)/shard_map/ppermute | solution.py:376
  133.7 10.5 %collective-permute-start.27 = (bf16[2,128,512]{2,1,0:T(8,128)(2,1)S(1)}, bf16[2,128,512]{2,1,0:T(8,128)(2,1)S(1)}, u32[]{:S(2)}, u32[]{:S(2)}) collective-permute-start(bf16[2,128,512]{2,1,0:T(8,128)(2,1)S(1)} %get-tuple-element.116), channel_id=1, source_target_pairs={{0,2},{1,3},{2,0},{3,1},{4,6},{5,7},{6,4},{7,5},{8,10},{9,11},{10,... | collective-permute-start | bytes 786440 | tf_op jit(solution)/shard_map/ppermute | solution.py:376
  134.9 11.1 %collective-permute-start.28 = (bf16[2,128,512]{2,1,0:T(8,128)(2,1)S(1)}, bf16[2,128,512]{2,1,0:T(8,128)(2,1)S(1)}, u32[]{:S(2)}, u32[]{:S(2)}) collective-permute-start(bf16[2,128,512]{2,1,0:T(8,128)(2,1)S(1)} %get-tuple-element.120), channel_id=1, source_target_pairs={{0,3},{1,2},{2,1},{3,0},{4,7},{5,6},{6,5},{7,4},{8,11},{9,10},{10,... | collective-permute-start | bytes 786440 | tf_op jit(solution)/shard_map/ppermute | solution.py:376
  136.6 22.6 %collective-permute-start.30 = (bf16[4,128,512]{2,1,0:T(8,128)(2,1)S(1)}, bf16[4,128,512]{2,1,0:T(8,128)(2,1)S(1)}, u32[]{:S(2)}, u32[]{:S(2)}) collective-permute-start(bf16[4,128,512]{2,1,0:T(8,128)(2,1)S(1)} %owner_sum.6), channel_id=1, source_target_pairs={{0,20},{1,21},{2,22},{3,23},{4,16},{5,17},{6,18},{7,19},{8,28},{9,... | collective-permute-start | bytes 1572872 | tf_op jit(solution)/shard_map/ppermute | solution.py:365
  146.8 13.1 %collective-permute-start.29 = (bf16[4,128,512]{2,1,0:T(8,128)(2,1)S(1)}, bf16[4,128,512]{2,1,0:T(8,128)(2,1)S(1)}, u32[]{:S(2)}, u32[]{:S(2)}) collective-permute-start(bf16[4,128,512]{2,1,0:T(8,128)(2,1)S(1)} %owner_sum.7), channel_id=1, source_target_pairs={{0,16},{1,17},{2,18},{3,19},{4,20},{5,21},{6,22},{7,23},{8,24},{9,... | collective-permute-start | bytes 1572872 | tf_op jit(solution)/shard_map/ppermute | solution.py:365

commit v13 on v12

--- a/solution.py
+++ b/solution.py
@@ -15,8 +15,7 @@
 GROUP = HEADS // KV_HEADS
 KV = KV_HEADS * HEAD_DIM
 PAIR = 2 * HEAD_DIM
-CODE = 16
-NEXT_FLOPS = 10_000_000_000
+CODE = 64
 FAR_SUM_FLOPS = 5_000_000_000
 FAR_FLOPS = 20_000_000_000
 MAJOR = 4
@@ -63,11 +62,10 @@
     return jnp.concatenate(heads, axis=0)
 
 
-def attention_kernel(list_len, per_step, get_ref, put_ref, q_ref, ng_ref, *refs):
+def attention_kernel(list_len, per_step, sources, get_ref, put_ref, q_ref, ng_ref, *refs):
     expo_scr, kv_scr, parts_scr, in_sems, out_sems = refs[-5:]
-    sources = (len(refs) - 7) // 2
     arrived, (normed_ref, qg_ref) = refs[:sources], refs[sources : sources + 2]
-    back = refs[sources + 2 : 2 * sources + 2]
+    back = refs[sources + 2 : -5]
     step = pl.program_id(0)
     entries = in_sems.shape[0]
 
@@ -84,11 +82,11 @@
             parts_scr.at[rows_of(e)], back[source].at[slot], out_sems.at[e]
         )
 
-    def start(copy, code_ref, begin, count):
+    def start(copy, places, code_ref, begin, count):
         def one(i, carry):
             e = begin + i
             code = code_ref[e]
-            for source in range(sources):
+            for source in range(places):
 
                 @pl.when(code // CODE == source)
                 def _():
@@ -100,7 +98,7 @@
 
     @pl.when(step == 0)
     def _():
-        start(fetch, get_ref, 0, entries)
+        start(fetch, len(arrived), get_ref, 0, entries)
 
     first = step * per_step * list_len
     pairs = range(KV // PAIR)
@@ -195,7 +193,7 @@
             finish_pair(b, j)
             if b + 1 < per_step and j == 0:
                 normalise(b + 1)
-    start(give, put_ref, first, per_step * list_len)
+    start(give, len(back), put_ref, first, per_step * list_len)
 
     @pl.when(step == pl.num_programs(0) - 1)
     def _():
@@ -203,23 +201,22 @@
             give(e, 0, 0).wait()
 
 
-def attention(gets, puts, queries, normed_grad, arrived, list_len):
+def attention(gets, puts, queries, normed_grad, arrived, list_len, back_shapes):
     width, rows = queries.shape
-    slot_shape = (CAP,) + arrived[0].shape[1:]
     blocks = rows // BLK
     entries = blocks * list_len
     resident = list_len <= 4
-    per_step = blocks if resident else 1
+    per_step = 1
     place = WHOLE if resident else pl.BlockSpec(memory_space=pl.ANY)
     keys = list_len * BLK
     pairs = HEADS * rows * keys
     return pl.pallas_call(
-        functools.partial(attention_kernel, list_len, per_step),
+        functools.partial(attention_kernel, list_len, per_step, len(arrived)),
         grid_spec=pltpu.PrefetchScalarGridSpec(
             num_scalar_prefetch=2,
             grid=(blocks // per_step,),
             in_specs=[WHOLE] * 2 + [place] * len(arrived),
-            out_specs=[WHOLE] * 2 + [place] * len(arrived),
+            out_specs=[WHOLE] * 2 + [place] * len(back_shapes),
             scratch_shapes=[
                 pltpu.VMEM((per_step, KV // PAIR, keys, 2 * GROUP * BLK), BF16),
                 pltpu.VMEM((entries * BLK, 2 * KV), BF16),
@@ -229,7 +226,7 @@
             ],
         ),
         out_shape=[jax.ShapeDtypeStruct((width, rows), BF16)] * 2
-        + [jax.ShapeDtypeStruct(slot_shape, BF16)] * len(arrived),
+        + [jax.ShapeDtypeStruct(shape, BF16) for shape in back_shapes],
         compiler_params=params(40 if resident else 56),
         cost_estimate=pl.CostEstimate(
             flops=12 * pairs * HEAD_DIM, bytes_accessed=16 * rows * width, transcendentals=pairs
@@ -376,27 +373,40 @@
             moved.append(lax.ppermute(value, "tile", pairs))
         return moved
 
-    def plane_rows(table):
+    def plane_rows(table, row):
         table = table[0].reshape(MAJOR, plane, entry_count)
-        return lax.dynamic_index_in_dim(table, my_row, 0, keepdims=False)
+        return lax.dynamic_index_in_dim(table, row, 0, keepdims=False)
 
     def mine_of(table):
         return lax.dynamic_index_in_dim(table, my_place, 0, keepdims=False)
 
-    tiles, picks = plane_rows(key_tiles), plane_rows(key_blocks)
     earlier = jnp.arange(entry_count)[:, None] > jnp.arange(entry_count)[None, :]
-    same = (tiles[:, :, None] == tiles[:, None, :]) & earlier[None]
-    ranks = jnp.sum(same.astype(jnp.int32), axis=2)
+
+    def ranked(tiles):
+        same = (tiles[:, :, None] == tiles[:, None, :]) & earlier[None]
+        return jnp.sum(same.astype(jnp.int32), axis=2)
+
+    def asked(slots, count, picks, valid):
+        ids = jnp.arange(count, dtype=jnp.int32)
+        hits = (slots[:, None, :] == ids[None, :, None]) & valid[:, None, :]
+        found = jnp.sum(jnp.where(hits, picks[:, None, :] + 1, 0), axis=2) - 1
+        return found[jnp.arange(plane) ^ my_place]
+
+    tiles, picks = plane_rows(key_tiles, my_row), plane_rows(key_blocks, my_row)
+    ranks = ranked(tiles)
     groups, columns = (tiles // plane) ^ my_row, tiles % plane
-    my_source = mine_of(groups) * plane + (mine_of(columns) ^ my_place)
-    puts = my_source * CODE + mine_of(ranks)
-    gets = jnp.where(my_source % plane == 0, my_source * CODE + mine_of(picks), puts)
-    ids = jnp.arange(MAJOR * CAP, dtype=jnp.int32)
-    slots = groups * CAP + ranks
-    hits = (slots[:, None, :] == ids[None, :, None]) & (columns == my_place)[:, None, :]
-    wanted = jnp.sum(jnp.where(hits, picks[:, None, :] + 1, 0), axis=2) - 1
-    wanted = wanted[jnp.arange(plane) ^ my_place].reshape(plane, MAJOR, CAP)
-    wanted = wanted.transpose(1, 0, 2).reshape(-1)
+    my_group, my_peer, my_rank = mine_of(groups), mine_of(columns) ^ my_place, mine_of(ranks)
+    gets = (my_group * plane + my_peer) * CODE + jnp.where(my_peer == 0, mine_of(picks), my_rank)
+    puts = jnp.where(
+        my_group == 1,
+        3 * plane * CODE + my_peer * CAP + my_rank,
+        (jnp.maximum(my_group - 1, 0) * plane + my_peer) * CODE + my_rank,
+    )
+    wanted = asked(groups * CAP + ranks, MAJOR * CAP, picks, columns == my_place)
+    wanted = wanted.reshape(plane, MAJOR, CAP).transpose(1, 0, 2).reshape(-1)
+    tiles, picks = plane_rows(key_tiles, my_row ^ 1), plane_rows(key_blocks, my_row ^ 1)
+    beside_wanted = asked(ranked(tiles), CAP, picks, tiles == my_tile).reshape(-1)
+    own_wanted = jnp.concatenate([wanted[: plane * CAP], beside_wanted])
 
     mine = project(tokens, w_key, w_value).reshape(block_count, BLK, 2 * KV)
     next_tile = swap(mine, 1, 1)
@@ -412,31 +422,35 @@
         w_query, tokens, (((0,), (1,)), ((), ())), preferred_element_type=F32
     ).astype(BF16)
     normed_grad = dot_nt(w_out, out_grad[0])
+    slot_shape = (CAP, BLK, 2 * KV)
+    back_shapes = [slot_shape] * (3 * plane) + [(plane * CAP, BLK, 2 * KV)]
     normed_low, query_grad, *back = attention(
-        gets, puts, queries, normed_grad, arrived, list_len
-    )
-    back = [back[d * plane : (d + 1) * plane] for d in range(MAJOR)]
+        gets, puts, queries, normed_grad, arrived, list_len, back_shapes
+    )
+    hopped = swap(back[3 * plane], 1, 0)
+    back = [back[d * plane : (d + 1) * plane] for d in range(3)]
     layer_out = dot_tn(normed_low, w_out).astype(BF16)
     query_term = lax.dot_general(
         query_grad, w_query, (((0,), (1,)), ((), ())), preferred_element_type=F32
     )
-    last = spread(back[3][1:])
+    last = spread(back[2][1:])
     last[0], query_term, layer_out = lax.optimization_barrier((last[0], query_term, layer_out))
-    far = spread(back[2][1:], last)
-    beside = spread(back[1][1:], far)
-    last_sum = owner_sum(3, wanted, [back[3][0], *last], block_count, BF16, 0)
+    far = spread(back[1][1:], last)
+    last_sum = owner_sum(3, wanted, [back[2][0], *last], block_count, BF16, 0)
     last_sum = swap(last_sum, 1, 0).astype(F32)
-    far_sum = owner_sum(2, wanted, [back[2][0], *far], block_count, F32, FAR_SUM_FLOPS)
+    far_sum = owner_sum(2, wanted, [back[1][0], *far], block_count, F32, FAR_SUM_FLOPS)
     far_sum = (far_sum + last_sum).astype(BF16)
-    beside[0] = after(beside[0], far_sum)
-    next_sum = owner_sum(1, wanted, [back[1][0], *beside], block_count, BF16, 0)
-    own = spread([after(after(x, far_sum), next_sum) for x in back[0][1:]], beside)
-    own_sum = owner_sum(0, wanted, [back[0][0], *own], block_count, BF16, 0)
-    sums = (swap(far_sum, 2, 1), swap(next_sum, 1, 1), swap(own_sum, 0, 1))
-    far_grad, next_grad, own_grad = (x.reshape(rows, 2 * KV) for x in sums)
-    query_term = finish([far_grad], query_term, w_key, w_value, F32, FAR_FLOPS)
-    query_term = finish([next_grad], query_term, w_key, w_value, F32, NEXT_FLOPS)
-    input_grad = finish([own_grad], query_term, w_key, w_value, BF16, 800_000_000)
+    own = spread(back[0][1:], far)
+    beside = [hopped[p * CAP : (p + 1) * CAP] for p in range(plane)]
+    beside = [beside[0], *spread([after(x, far_sum) for x in beside[1:]], own)]
+    own_sum = owner_sum(0, own_wanted, [back[0][0], *own, *beside], block_count, BF16, 0)
+    far_grad, own_grad = swap(far_sum, 2, 1), swap(own_sum, 0, 1)
+    query_term = finish(
+        [far_grad.reshape(rows, 2 * KV)], query_term, w_key, w_value, F32, FAR_FLOPS
+    )
+    input_grad = finish(
+        [own_grad.reshape(rows, 2 * KV)], query_term, w_key, w_value, BF16, 800_000_000
+    )
     return (layer_out[None], input_grad[None])
 
 

time: 162 us -> 163 us (level)
  waiting for transfers between devices: 73.9 us -> 59.1 us
  local copies, waits for them, and re-layouts: 3.08 us -> 12.5 us
  other arithmetic: 2.44 us -> 5.69 us
    ppermute x24, waiting for transfers between devices: 50.5 us -> 40.7 us  [spread(): moved.append(lax.ppermute(value, 'tile', pairs))]
    unnamed x24 -> x72, local copies, waits for them, and re-layouts: 2.07 us -> 8.33 us
    ppermute x8, waiting for transfers between devices: 23.4 us -> 18.3 us  [swap(): return lax.ppermute(value, ('vintage', 'tile'), pairs)]
    slice x0 -> x4, local copies, waits for them, and re-layouts: none -> 2.27 us  [the longest x1 2.09 us: shards(): beside = [hopped[p * CAP:(p + 1) * CAP] for p in range(plane)]]
    convert_element_type x1, other arithmetic: 0.17 us -> 2.04 us  [shards(): far_sum = (far_sum + last_sum).astype(BF16)]
    pallas_call x1, Pallas kernels: 22.7 us -> 24.4 us  [attention(): pl.pallas_call(functools.partial(attention_kernel, list_len, per_step, le...]
  transfers between devices with their start and end apart: 32 -> 32, of which waited for: 16 -> 16; matrix products, arithmetic and copies ran while one was open for 6% -> 10% of each run, Pallas kernels for 5% -> 5%
where the time goes in v13:
time: 163 us; the launch traced here: 162 us
  waiting for transfers between devices  59.1 us (36%)
  starting transfers between devices  40.2 us (25%)
  Pallas kernels  36.8 us (23%)
  local copies, waits for them, and re-layouts  12.5 us (8%)
  matrix products  6.81 us (4%)
  other arithmetic  5.69 us (3%)
    ppermute x24, waiting for transfers between devices, spread(): moved.append(lax.ppermute(value, 'tile', pairs))  40.7 us
    ppermute x24, starting transfers between devices, spread(): moved.append(lax.ppermute(value, 'tile', pairs))  34.2 us
    pallas_call x1, Pallas kernels, attention(): pl.pallas_call(functools.partial(attention_kernel, list_len, per_step, le...  24.4 us
    ppermute x8, waiting for transfers between devices, swap(): return lax.ppermute(value, ('vintage', 'tile'), pairs)  18.3 us
    unnamed x72, local copies, waits for them, and re-layouts  8.33 us
    ppermute x8, starting transfers between devices, swap(): return lax.ppermute(value, ('vintage', 'tile'), pairs)  6 us
    pallas_call x1, Pallas kernels, project(): pl.pallas_call(project_kernel, in_specs=[pl.BlockSpec(memory_space=pl.ANY...  3.4 us
    pallas_call x4, Pallas kernels, pack(): pl.pallas_call(functools.partial(pack_kernel, group * plane * CAP), in_sp...  3.31 us
  transfers between devices with their start and end apart: 32, of which 16 were waited for; matrix products, arithmetic and copies ran while one was open for 10% of the time, Pallas kernels for 5%

profile of v13, /device:TPU:0, one launch (start us, length us, event | category | flops | bytes accessed | tf_op | source)
XLA Modules:
  0.0 162.1 jit_solution(1974080577131605455)
XLA Ops:
  0.7 3.4 %project.1 = bf16[512,512]{1,0:T(8,128)(2,1)} custom-call(bf16[512,768]{1,0:T(8,128)(2,1)} %bitcast.60, bf16[768,256]{1,0:T(8,128)(2,1)} %refs_2_.3, bf16[768,256]{1,0:T(8,128)(2,1)} %refs_3_.3), custom_call_target="tpu_custom_call" | custom-call | tf_op jit(solution)/shard_map/project/pallas_call | solution.py:261
  4.1 2.5 %collective-permute-start.4 = (bf16[4,128,512]{2,1,0:T(8,128)(2,1)}, bf16[4,128,512]{2,1,0:T(8,128)(2,1)S(1)}, u32[]{:S(2)}, u32[]{:S(2)}) collective-permute-start(bf16[4,128,512]{2,1,0:T(8,128)(2,1)} %bitcast.61), channel_id=1, source_target_pairs={{0,20},{1,21},{2,22},{3,23},{4,16},{5,17},{6,18},{7,19},{8,28},{9,... | collective-permute-start | bytes 1572872 | tf_op jit(solution)/shard_map/ppermute | solution.py:362
  10.4 2.3 %collective-permute-start.8 = (bf16[4,128,512]{2,1,0:T(8,128)(2,1)}, bf16[4,128,512]{2,1,0:T(8,128)(2,1)S(1)}, u32[]{:S(2)}, u32[]{:S(2)}) collective-permute-start(bf16[4,128,512]{2,1,0:T(8,128)(2,1)} %bitcast.63), channel_id=1, source_target_pairs={{0,24},{1,25},{2,26},{3,27},{4,28},{5,29},{6,30},{7,31},{8,16},{9,... | collective-permute-start | bytes 1572872 | tf_op jit(solution)/shard_map/ppermute | solution.py:362
  14.1 2.5 %collective-permute-start.3 = (bf16[2,128,512]{2,1,0:T(8,128)(2,1)S(1)}, bf16[2,128,512]{2,1,0:T(8,128)(2,1)S(1)}, u32[]{:S(2)}, u32[]{:S(2)}) collective-permute-start(bf16[2,128,512]{2,1,0:T(8,128)(2,1)S(1)} %get-tuple-element.57), channel_id=1, source_target_pairs={{0,3},{1,2},{2,1},{3,0},{4,7},{5,6},{6,5},{7,4},{8,11},{9,10},{10,... | collective-permute-start | bytes 786440 | tf_op jit(solution)/shard_map/ppermute | solution.py:373
  17.7 8.3 %collective-permute-done.4.tile_ref.refs_4_ = bf16[4,128,512]{2,1,0:T(8,128)(2,1)S(1)} collective-permute-done((bf16[4,128,512]{2,1,0:T(8,128)(2,1)}, bf16[4,128,512]{2,1,0:T(8,128)(2,1)S(1)}, u32[]{:S(2)}, u32[]{:S(2)}) %collective-permute-start.4) | collective-permute-done | bytes 524320 | tf_op jit(solution)/shard_map/ppermute | solution.py:362
  26.0 1.5 pack.5
  28.2 3.9 %collective-permute-start.7 = (bf16[2,128,512]{2,1,0:T(8,128)(2,1)}, bf16[2,128,512]{2,1,0:T(8,128)(2,1)S(1)}, u32[]{:S(2)}, u32[]{:S(2)}) collective-permute-start(bf16[2,128,512]{2,1,0:T(8,128)(2,1)} %get-tuple-element.63), channel_id=1, source_target_pairs={{0,3},{1,2},{2,1},{3,0},{4,7},{5,6},{6,5},{7,4},{8,11},{9,10},{10,... | collective-permute-start | bytes 786440 | tf_op jit(solution)/shard_map/ppermute | solution.py:373
  34.1 2.8 %collective-permute-done.8.tile_ref.refs_8_ = bf16[4,128,512]{2,1,0:T(8,128)(2,1)S(1)} collective-permute-done((bf16[4,128,512]{2,1,0:T(8,128)(2,1)}, bf16[4,128,512]{2,1,0:T(8,128)(2,1)S(1)}, u32[]{:S(2)}, u32[]{:S(2)}) %collective-permute-start.8) | collective-permute-done | bytes 524320 | tf_op jit(solution)/shard_map/ppermute | solution.py:362
  38.2 1.3 collective-permute-done.7.refs_7_
  39.4 3.0 %collective-permute-start.11 = (bf16[2,128,512]{2,1,0:T(8,128)(2,1)S(1)}, bf16[2,128,512]{2,1,0:T(8,128)(2,1)S(1)}, u32[]{:S(2)}, u32[]{:S(2)}) collective-permute-start(bf16[2,128,512]{2,1,0:T(8,128)(2,1)S(1)} %get-tuple-element.71), channel_id=1, source_target_pairs={{0,3},{1,2},{2,1},{3,0},{4,7},{5,6},{6,5},{7,4},{8,11},{9,10},{10,... | collective-permute-start | bytes 786440 | tf_op jit(solution)/shard_map/ppermute | solution.py:373
  42.4 2.7 %collective-permute-done.6.refs_6_ = bf16[2,128,512]{2,1,0:T(8,128)(2,1)} collective-permute-done((bf16[2,128,512]{2,1,0:T(8,128)(2,1)}, bf16[2,128,512]{2,1,0:T(8,128)(2,1)}, u32[]{:S(2)}, u32[]{:S(2)}) %collective-permute-start.6) | collective-permute-done | bytes 262176 | tf_op jit(solution)/shard_map/ppermute | solution.py:373
  45.0 2.0 %collective-permute-start.10 = (bf16[2,128,512]{2,1,0:T(8,128)(2,1)S(1)}, bf16[2,128,512]{2,1,0:T(8,128)(2,1)S(1)}, u32[]{:S(2)}, u32[]{:S(2)}) collective-permute-start(bf16[2,128,512]{2,1,0:T(8,128)(2,1)S(1)} %get-tuple-element.69), channel_id=1, source_target_pairs={{0,2},{1,3},{2,0},{3,1},{4,6},{5,7},{6,4},{7,5},{8,10},{9,11},{10,... | collective-permute-start | bytes 786440 | tf_op jit(solution)/shard_map/ppermute | solution.py:373
  47.1 1.1 collective-permute-start.9
  48.2 2.3 %fusion.ng_ref = f32[768,512]{1,0:T(8,128)S(1)} fusion(bf16[768,768]{1,0:T(8,128)(2,1)} %param.13, bf16[1,512,768]{2,1,0:T(8,128)(2,1)} %param.9), kind=kOutput, calls=%fused_computation.5 | convolution fusion | flops 603979776 | bytes 3538944 | tf_op jit(solution)/shard_map/dot_general | solution.py:34
  51.6 2.5 %collective-permute-start.15 = (bf16[2,128,512]{2,1,0:T(8,128)(2,1)S(1)}, bf16[2,128,512]{2,1,0:T(8,128)(2,1)S(1)}, u32[]{:S(2)}, u32[]{:S(2)}) collective-permute-start(bf16[2,128,512]{2,1,0:T(8,128)(2,1)S(1)} %get-tuple-element.77), channel_id=1, source_target_pairs={{0,3},{1,2},{2,1},{3,0},{4,7},{5,6},{6,5},{7,4},{8,11},{9,10},{10,... | collective-permute-start | bytes 786440 | tf_op jit(solution)/shard_map/ppermute | solution.py:373
  54.2 2.1 %collective-permute-done.10.refs_10_ = bf16[2,128,512]{2,1,0:T(8,128)(2,1)S(1)} collective-permute-done((bf16[2,128,512]{2,1,0:T(8,128)(2,1)S(1)}, bf16[2,128,512]{2,1,0:T(8,128)(2,1)S(1)}, u32[]{:S(2)}, u32[]{:S(2)}) %collective-permute-start.10) | collective-permute-done | bytes 262176 | tf_op jit(solution)/shard_map/ppermute | solution.py:373
  56.2 2.1 %collective-permute-start.14 = (bf16[2,128,512]{2,1,0:T(8,128)(2,1)S(1)}, bf16[2,128,512]{2,1,0:T(8,128)(2,1)S(1)}, u32[]{:S(2)}, u32[]{:S(2)}) collective-permute-start(bf16[2,128,512]{2,1,0:T(8,128)(2,1)S(1)} %get-tuple-element.75), channel_id=1, source_target_pairs={{0,2},{1,3},{2,0},{3,1},{4,6},{5,7},{6,4},{7,5},{8,10},{9,11},{10,... | collective-permute-start | bytes 786440 | tf_op jit(solution)/shard_map/ppermute | solution.py:373
  58.3 1.5 collective-permute-start.13
  59.8 0.8 convolution_convert_fusion.1.q_ref
  60.7 1.3 collective-permute-done.15.refs_15_
  62.0 5.2 %collective-permute-done.14.refs_14_ = bf16[2,128,512]{2,1,0:T(8,128)(2,1)S(1)} collective-permute-done((bf16[2,128,512]{2,1,0:T(8,128)(2,1)S(1)}, bf16[2,128,512]{2,1,0:T(8,128)(2,1)S(1)}, u32[]{:S(2)}, u32[]{:S(2)}) %collective-permute-start.14) | collective-permute-done | bytes 262176 | tf_op jit(solution)/shard_map/ppermute | solution.py:373
  67.5 24.4 %attention.1 = (bf16[768,512]{1,0:T(8,128)(2,1)S(1)}, bf16[768,512]{1,0:T(8,128)(2,1)S(1)}, bf16[2,128,512]{2,1,0:T(8,128)(2,1)S(1)}, bf16[2,128,512]{2,1,0:T(8,...) custom-call(s32[16]{0:T(128)S(1)} %get-tuple-element.126.get_ref, ...), custom_call_target="tpu_custom_call" | custom-call | flops 2415919104 | bytes 6291456 | tf_op jit(solution)/shard_map/attention/pallas_call | solution.py:213
  91.9 1.6 %collective-permute-start.16 = (bf16[2,128,512]{2,1,0:T(8,128)(2,1)S(1)}, bf16[2,128,512]{2,1,0:T(8,128)(2,1)S(1)}, u32[]{:S(2)}, u32[]{:S(2)}) collective-permute-start(bf16[2,128,512]{2,1,0:T(8,128)(2,1)S(1)} %get-tuple-element.78), channel_id=1, source_target_pairs={{0,1},{1,0},{2,3},{3,2},{4,5},{5,4},{6,7},{7,6},{8,9},{9,8},{10,11... | collective-permute-start | bytes 786440 | tf_op jit(solution)/shard_map/ppermute | solution.py:373
  93.6 1.4 collective-permute-start.19
  95.5 2.0 %fusion.14.refs_1_ = f32[512,768]{1,0:T(8,128)} fusion(bf16[768,512]{1,0:T(8,128)(2,1)S(1)} %get-tuple-element.79, bf16[768,768]{1,0:T(8,128)(2,1)S(1)} %copy-done), kind=kOutput, calls=%fused_computation.52 | convolution fusion | flops 603979776 | bytes 3538944 | tf_op jit(solution)/shard_map/dot_general | solution.py:433
  97.5 1.7 %convolution_convert_fusion = bf16[512,768]{1,0:T(8,128)(2,1)} fusion(bf16[768,512]{1,0:T(8,128)(2,1)S(1)} %get-tuple-element.80, bf16[768,768]{1,0:T(8,128)(2,1)S(1)} %copy-done.34), kind=kOutput, calls=%fused_computation.2 | convolution fusion | flops 604372992 | bytes 2752512 | tf_op jit(solution)/shard_map/dot_general | solution.py:38
  99.3 7.7 %collective-permute-done.19.refs_2_ = bf16[2,128,512]{2,1,0:T(8,128)(2,1)S(1)} collective-permute-done((bf16[2,128,512]{2,1,0:T(8,128)(2,1)S(1)}, bf16[2,128,512]{2,1,0:T(8,128)(2,1)S(1)}, u32[]{:S(2)}, u32[]{:S(2)}) %collective-permute-start.19) | collective-permute-done | bytes 262176 | tf_op jit(solution)/shard_map/ppermute | solution.py:373
  107.0 1.5 collective-permute-start.20
  108.7 1.8 %collective-permute-start.17 = (bf16[2,128,512]{2,1,0:T(8,128)(2,1)}, bf16[2,128,512]{2,1,0:T(8,128)(2,1)S(1)}, u32[]{:S(2)}, u32[]{:S(2)}) collective-permute-start(bf16[2,128,512]{2,1,0:T(8,128)(2,1)} %get-tuple-element.86), channel_id=1, source_target_pairs={{0,1},{1,0},{2,3},{3,2},{4,5},{5,4},{6,7},{7,6},{8,9},{9,8},{10,11... | collective-permute-start | bytes 786440 | tf_op jit(solution)/shard_map/ppermute | solution.py:373
  111.7 8.1 %collective-permute-done.20.refs_2_ = bf16[2,128,512]{2,1,0:T(8,128)(2,1)S(1)} collective-permute-done((bf16[2,128,512]{2,1,0:T(8,128)(2,1)}, bf16[2,128,512]{2,1,0:T(8,128)(2,1)S(1)}, u32[]{:S(2)}, u32[]{:S(2)}) %collective-permute-start.20) | collective-permute-done | bytes 262176 | tf_op jit(solution)/shard_map/ppermute | solution.py:373
  120.5 1.7 %collective-permute-start.21 = (bf16[2,128,512]{2,1,0:T(8,128)(2,1)S(1)}, bf16[2,128,512]{2,1,0:T(8,128)(2,1)S(1)}, u32[]{:S(2)}, u32[]{:S(2)}) collective-permute-start(bf16[2,128,512]{2,1,0:T(8,128)(2,1)S(1)} %copy-done.14), channel_id=1, source_target_pairs={{0,2},{1,3},{2,0},{3,1},{4,6},{5,7},{6,4},{7,5},{8,10},{9,11},{10,... | collective-permute-start | bytes 786440 | tf_op jit(solution)/shard_map/ppermute | solution.py:373
  124.0 1.4 collective-permute-start.18
  125.4 0.9 copy-done.18
  126.4 0.9 copy-done.20
  127.3 0.9 copy-done.22
  128.3 0.9 copy-done.25
  129.2 0.8 owner_sum.3
  130.0 1.1 collective-permute-done.26
  131.1 2.0 %add_convert_fusion = bf16[4,128,512]{2,1,0:T(8,128)(2,1)} fusion(f32[4,128,512]{2,1,0:T(8,128)S(1)} %owner_sum.3, bf16[4,128,512]{2,1,0:T(8,128)(2,1)} %collective-permute-done.26), kind=kLoop, calls=%fused_computation.4 | loop fusion | flops 786432 | bytes 2097152 | tf_op jit(solution)/shard_map/convert_element_type | solution.py:442
  133.1 2.1 %fusion.13 = (bf16[2,128,512]{2,1,0:T(8,128)(2,1)}, bf16[2,128,512]{2,1,0:T(8,128)(2,1)}, bf16[2,128,512]{2,1,0:T(8,128)(2,1)}, bf16[2,128,512]{2,1,0:T(8,128)(2,1)S(1)}) fusion(bf16[8,128,512]{2,1,0:T(8,128)(2,1)} %collective-permute-done.25), kind=kLoop, calls=%fused_computation.51 | loop fusion | bytes 2097152 | tf_op jit(solution)/shard_map/slice | solution.py:444
  135.4 1.5 collective-permute-start.27
  136.9 1.5 collective-permute-start.28
  139.9 4.5 %collective-permute-done.27.refs_5_ = bf16[2,128,512]{2,1,0:T(8,128)(2,1)S(1)} collective-permute-done((bf16[2,128,512]{2,1,0:T(8,128)(2,1)}, bf16[2,128,512]{2,1,0:T(8,128)(2,1)S(1)}, u32[]{:S(2)}, u32[]{:S(2)}) %collective-permute-start.27) | collective-permute-done | bytes 262176 | tf_op jit(solution)/shard_map/ppermute | solution.py:373
  144.4 7.4 %collective-permute-done.28.refs_6_ = bf16[2,128,512]{2,1,0:T(8,128)(2,1)S(1)} collective-permute-done((bf16[2,128,512]{2,1,0:T(8,128)(2,1)}, bf16[2,128,512]{2,1,0:T(8,128)(2,1)S(1)}, u32[]{:S(2)}, u32[]{:S(2)}) %collective-permute-start.28) | collective-permute-done | bytes 262176 | tf_op jit(solution)/shard_map/ppermute | solution.py:373
  151.8 0.9 owner_sum.5
  153.2 5.7 %collective-permute-done.31 = bf16[4,128,512]{2,1,0:T(8,128)(2,1)} collective-permute-done((bf16[4,128,512]{2,1,0:T(8,128)(2,1)}, bf16[4,128,512]{2,1,0:T(8,128)(2,1)}, u32[]{:S(2)}, u32[]{:S(2)}) %collective-permute-start.31) | collective-permute-done | bytes 524320 | tf_op jit(solution)/shard_map/ppermute | solution.py:362
  158.9 1.6 %finish.2.refs_1_ = f32[512,768]{1,0:T(8,128)S(1)} custom-call(bf16[512,512]{1,0:T(8,128)(2,1)} %bitcast.20.refs_0_, f32[512,768]{1,0:T(8,128)S(1)} %copy-done.23, bf16[768,256]{1,0:T(8,128)(2,1)S(1)} %copy-done.1, bf16[768,256]{1,0:T(8,128)(2,1)S(1)} %copy-done.2), custom_call_target="tpu_custom_call" | custom-call | flops 20000000000 | bytes 1572864 | tf_op jit(solution)/shard_map/finish/pallas_call | solution.py:302
  160.6 1.5 finish.3
  (130 shorter events, 18.0 us)
Async XLA Ops:
  0.6 59.2 %copy-start = (bf16[768,768]{1,0:T(8,128)(2,1)S(1)}, bf16[768,768]{1,0:T(8,128)(2,1)}, u32[]{:S(2)}) copy-start(bf16[768,768]{1,0:T(8,128)(2,1)} %param.10) | copy-start | bytes 3538948
  4.1 21.9 %collective-permute-start.4 = (bf16[4,128,512]{2,1,0:T(8,128)(2,1)}, bf16[4,128,512]{2,1,0:T(8,128)(2,1)S(1)}, u32[]{:S(2)}, u32[]{:S(2)}) collective-permute-start(bf16[4,128,512]{2,1,0:T(8,128)(2,1)} %bitcast.61), channel_id=1, source_target_pairs={{0,20},{1,21},{2,22},{3,23},{4,16},{5,17},{6,18},{7,19},{8,28},{9,... | collective-permute-start | bytes 1572872 | tf_op jit(solution)/shard_map/ppermute | solution.py:362
  6.6 3.8 %collective-permute-start = (bf16[4,128,512]{2,1,0:T(8,128)(2,1)}, bf16[4,128,512]{2,1,0:T(8,128)(2,1)S(1)}, u32[]{:S(2)}, u32[]{:S(2)}) collective-permute-start(bf16[4,128,512]{2,1,0:T(8,128)(2,1)} %bitcast.62), channel_id=1, source_target_pairs={{0,16},{1,17},{2,18},{3,19},{4,20},{5,21},{6,22},{7,23},{8,24},{9,... | collective-permute-start | bytes 1572872 | tf_op jit(solution)/shard_map/ppermute | solution.py:362
  10.4 26.4 %collective-permute-start.8 = (bf16[4,128,512]{2,1,0:T(8,128)(2,1)}, bf16[4,128,512]{2,1,0:T(8,128)(2,1)S(1)}, u32[]{:S(2)}, u32[]{:S(2)}) collective-permute-start(bf16[4,128,512]{2,1,0:T(8,128)(2,1)} %bitcast.63), channel_id=1, source_target_pairs={{0,24},{1,25},{2,26},{3,27},{4,28},{5,29},{6,30},{7,31},{8,16},{9,... | collective-permute-start | bytes 1572872 | tf_op jit(solution)/shard_map/ppermute | solution.py:362
  14.1 13.4 %collective-permute-start.3 = (bf16[2,128,512]{2,1,0:T(8,128)(2,1)S(1)}, bf16[2,128,512]{2,1,0:T(8,128)(2,1)S(1)}, u32[]{:S(2)}, u32[]{:S(2)}) collective-permute-start(bf16[2,128,512]{2,1,0:T(8,128)(2,1)S(1)} %get-tuple-element.57), channel_id=1, source_target_pairs={{0,3},{1,2},{2,1},{3,0},{4,7},{5,6},{6,5},{7,4},{8,11},{9,10},{10,... | collective-permute-start | bytes 786440 | tf_op jit(solution)/shard_map/ppermute | solution.py:373
  16.7 15.4 %collective-permute-start.2 = (bf16[2,128,512]{2,1,0:T(8,128)(2,1)S(1)}, bf16[2,128,512]{2,1,0:T(8,128)(2,1)S(1)}, u32[]{:S(2)}, u32[]{:S(2)}) collective-permute-start(bf16[2,128,512]{2,1,0:T(8,128)(2,1)S(1)} %get-tuple-element.56), channel_id=1, source_target_pairs={{0,2},{1,3},{2,0},{3,1},{4,6},{5,7},{6,4},{7,5},{8,10},{9,11},{10,... | collective-permute-start | bytes 786440 | tf_op jit(solution)/shard_map/ppermute | solution.py:373
  17.2 16.1 %collective-permute-start.1 = (bf16[2,128,512]{2,1,0:T(8,128)(2,1)S(1)}, bf16[2,128,512]{2,1,0:T(8,128)(2,1)S(1)}, u32[]{:S(2)}, u32[]{:S(2)}) collective-permute-start(bf16[2,128,512]{2,1,0:T(8,128)(2,1)S(1)} %get-tuple-element.55), channel_id=1, source_target_pairs={{0,1},{1,0},{2,3},{3,2},{4,5},{5,4},{6,7},{7,6},{8,9},{9,8},{10,11... | collective-permute-start | bytes 786440 | tf_op jit(solution)/shard_map/ppermute | solution.py:373
  28.2 11.2 %collective-permute-start.7 = (bf16[2,128,512]{2,1,0:T(8,128)(2,1)}, bf16[2,128,512]{2,1,0:T(8,128)(2,1)S(1)}, u32[]{:S(2)}, u32[]{:S(2)}) collective-permute-start(bf16[2,128,512]{2,1,0:T(8,128)(2,1)} %get-tuple-element.63), channel_id=1, source_target_pairs={{0,3},{1,2},{2,1},{3,0},{4,7},{5,6},{6,5},{7,4},{8,11},{9,10},{10,... | collective-permute-start | bytes 786440 | tf_op jit(solution)/shard_map/ppermute | solution.py:373
  32.8 12.3 %collective-permute-start.6 = (bf16[2,128,512]{2,1,0:T(8,128)(2,1)}, bf16[2,128,512]{2,1,0:T(8,128)(2,1)}, u32[]{:S(2)}, u32[]{:S(2)}) collective-permute-start(bf16[2,128,512]{2,1,0:T(8,128)(2,1)} %get-tuple-element.61), channel_id=1, source_target_pairs={{0,2},{1,3},{2,0},{3,1},{4,6},{5,7},{6,4},{7,5},{8,10},{9,11},{10,... | collective-permute-start | bytes 786440 | tf_op jit(solution)/shard_map/ppermute | solution.py:373
  34.0 13.1 %collective-permute-start.5 = (bf16[2,128,512]{2,1,0:T(8,128)(2,1)}, bf16[2,128,512]{2,1,0:T(8,128)(2,1)}, u32[]{:S(2)}, u32[]{:S(2)}) collective-permute-start(bf16[2,128,512]{2,1,0:T(8,128)(2,1)} %get-tuple-element.59), channel_id=1, source_target_pairs={{0,1},{1,0},{2,3},{3,2},{4,5},{5,4},{6,7},{7,6},{8,9},{9,8},{10,11... | collective-permute-start | bytes 786440 | tf_op jit(solution)/shard_map/ppermute | solution.py:373
  36.8 14.2 %collective-permute-start.12 = (bf16[4,128,512]{2,1,0:T(8,128)(2,1)S(1)}, bf16[4,128,512]{2,1,0:T(8,128)(2,1)S(1)}, u32[]{:S(2)}, u32[]{:S(2)}) collective-permute-start(bf16[4,128,512]{2,1,0:T(8,128)(2,1)S(1)} %collective-permute-done.8.tile_ref.refs_8_), channel_id=1, source_target_pairs={{0,4},{1,5},{2,6},{3,7},{4,0},{5,1},{6,2},{7,3},{8,12},{9,13},{10,... | collective-permute-start | bytes 1572872 | tf_op jit(solution)/shard_map/ppermute | solution.py:362
  39.4 11.1 %copy-start.9 = (bf16[2,128,512]{2,1,0:T(8,128)(2,1)}, bf16[2,128,512]{2,1,0:T(8,128)(2,1)S(1)}, u32[]{:S(2)}) copy-start(bf16[2,128,512]{2,1,0:T(8,128)(2,1)S(1)} %collective-permute-done.7.refs_7_) | copy-start | bytes 786436
  39.4 12.2 %collective-permute-start.11 = (bf16[2,128,512]{2,1,0:T(8,128)(2,1)S(1)}, bf16[2,128,512]{2,1,0:T(8,128)(2,1)S(1)}, u32[]{:S(2)}, u32[]{:S(2)}) collective-permute-start(bf16[2,128,512]{2,1,0:T(8,128)(2,1)S(1)} %get-tuple-element.71), channel_id=1, source_target_pairs={{0,3},{1,2},{2,1},{3,0},{4,7},{5,6},{6,5},{7,4},{8,11},{9,10},{10,... | collective-permute-start | bytes 786440 | tf_op jit(solution)/shard_map/ppermute | solution.py:373
  45.0 11.2 %collective-permute-start.10 = (bf16[2,128,512]{2,1,0:T(8,128)(2,1)S(1)}, bf16[2,128,512]{2,1,0:T(8,128)(2,1)S(1)}, u32[]{:S(2)}, u32[]{:S(2)}) collective-permute-start(bf16[2,128,512]{2,1,0:T(8,128)(2,1)S(1)} %get-tuple-element.69), channel_id=1, source_target_pairs={{0,2},{1,3},{2,0},{3,1},{4,6},{5,7},{6,4},{7,5},{8,10},{9,11},{10,... | collective-permute-start | bytes 786440 | tf_op jit(solution)/shard_map/ppermute | solution.py:373
  47.1 12.8 %copy-start.26 = (bf16[1,512,768]{2,1,0:T(8,128)(2,1)S(1)}, bf16[1,512,768]{2,1,0:T(8,128)(2,1)}, u32[]{:S(2)}) copy-start(bf16[1,512,768]{2,1,0:T(8,128)(2,1)} %param.8) | copy-start | bytes 2359300
  47.1 11.2 %collective-permute-start.9 = (bf16[2,128,512]{2,1,0:T(8,128)(2,1)S(1)}, bf16[2,128,512]{2,1,0:T(8,128)(2,1)S(1)}, u32[]{:S(2)}, u32[]{:S(2)}) collective-permute-start(bf16[2,128,512]{2,1,0:T(8,128)(2,1)S(1)} %get-tuple-element.67), channel_id=1, source_target_pairs={{0,1},{1,0},{2,3},{3,2},{4,5},{5,4},{6,7},{7,6},{8,9},{9,8},{10,11... | collective-permute-start | bytes 786440 | tf_op jit(solution)/shard_map/ppermute | solution.py:373
  51.6 10.3 %collective-permute-start.15 = (bf16[2,128,512]{2,1,0:T(8,128)(2,1)S(1)}, bf16[2,128,512]{2,1,0:T(8,128)(2,1)S(1)}, u32[]{:S(2)}, u32[]{:S(2)}) collective-permute-start(bf16[2,128,512]{2,1,0:T(8,128)(2,1)S(1)} %get-tuple-element.77), channel_id=1, source_target_pairs={{0,3},{1,2},{2,1},{3,0},{4,7},{5,6},{6,5},{7,4},{8,11},{9,10},{10,... | collective-permute-start | bytes 786440 | tf_op jit(solution)/shard_map/ppermute | solution.py:373
  56.2 11.0 %collective-permute-start.14 = (bf16[2,128,512]{2,1,0:T(8,128)(2,1)S(1)}, bf16[2,128,512]{2,1,0:T(8,128)(2,1)S(1)}, u32[]{:S(2)}, u32[]{:S(2)}) collective-permute-start(bf16[2,128,512]{2,1,0:T(8,128)(2,1)S(1)} %get-tuple-element.75), channel_id=1, source_target_pairs={{0,2},{1,3},{2,0},{3,1},{4,6},{5,7},{6,4},{7,5},{8,10},{9,11},{10,... | collective-permute-start | bytes 786440 | tf_op jit(solution)/shard_map/ppermute | solution.py:373
  58.3 9.2 %copy-start.4 = (bf16[2,128,512]{2,1,0:T(8,128)(2,1)S(1)}, bf16[2,128,512]{2,1,0:T(8,128)(2,1)}, u32[]{:S(2)}) copy-start(bf16[2,128,512]{2,1,0:T(8,128)(2,1)} %copy-done.3) | copy-start | bytes 786436
  58.3 9.2 %copy-start.6 = (bf16[2,128,512]{2,1,0:T(8,128)(2,1)S(1)}, bf16[2,128,512]{2,1,0:T(8,128)(2,1)}, u32[]{:S(2)}) copy-start(bf16[2,128,512]{2,1,0:T(8,128)(2,1)} %copy-done.5) | copy-start | bytes 786436
  58.3 9.2 %copy-start.8 = (bf16[2,128,512]{2,1,0:T(8,128)(2,1)S(1)}, bf16[2,128,512]{2,1,0:T(8,128)(2,1)}, u32[]{:S(2)}) copy-start(bf16[2,128,512]{2,1,0:T(8,128)(2,1)} %copy-done.7) | copy-start | bytes 786436
  58.3 9.2 %copy-start.10 = (bf16[2,128,512]{2,1,0:T(8,128)(2,1)S(1)}, bf16[2,128,512]{2,1,0:T(8,128)(2,1)}, u32[]{:S(2)}) copy-start(bf16[2,128,512]{2,1,0:T(8,128)(2,1)} %copy-done.9) | copy-start | bytes 786436
  58.3 9.2 %collective-permute-start.13 = (bf16[2,128,512]{2,1,0:T(8,128)(2,1)S(1)}, bf16[2,128,512]{2,1,0:T(8,128)(2,1)S(1)}, u32[]{:S(2)}, u32[]{:S(2)}) collective-permute-start(bf16[2,128,512]{2,1,0:T(8,128)(2,1)S(1)} %get-tuple-element.73), channel_id=1, source_target_pairs={{0,1},{1,0},{2,3},{3,2},{4,5},{5,4},{6,7},{7,6},{8,9},{9,8},{10,11... | collective-permute-start | bytes 786440 | tf_op jit(solution)/shard_map/ppermute | solution.py:373
  91.9 16.7 %collective-permute-start.16 = (bf16[2,128,512]{2,1,0:T(8,128)(2,1)S(1)}, bf16[2,128,512]{2,1,0:T(8,128)(2,1)S(1)}, u32[]{:S(2)}, u32[]{:S(2)}) collective-permute-start(bf16[2,128,512]{2,1,0:T(8,128)(2,1)S(1)} %get-tuple-element.78), channel_id=1, source_target_pairs={{0,1},{1,0},{2,3},{3,2},{4,5},{5,4},{6,7},{7,6},{8,9},{9,8},{10,11... | collective-permute-start | bytes 786440 | tf_op jit(solution)/shard_map/ppermute | solution.py:373
  93.6 13.4 %collective-permute-start.19 = (bf16[2,128,512]{2,1,0:T(8,128)(2,1)S(1)}, bf16[2,128,512]{2,1,0:T(8,128)(2,1)S(1)}, u32[]{:S(2)}, u32[]{:S(2)}) collective-permute-start(bf16[2,128,512]{2,1,0:T(8,128)(2,1)S(1)} %get-tuple-element.90), channel_id=1, source_target_pairs={{0,2},{1,3},{2,0},{3,1},{4,6},{5,7},{6,4},{7,5},{8,10},{9,11},{10,... | collective-permute-start | bytes 786440 | tf_op jit(solution)/shard_map/ppermute | solution.py:373
  95.0 13.6 %collective-permute-start.22 = (bf16[2,128,512]{2,1,0:T(8,128)(2,1)S(1)}, bf16[2,128,512]{2,1,0:T(8,128)(2,1)S(1)}, u32[]{:S(2)}, u32[]{:S(2)}) collective-permute-start(bf16[2,128,512]{2,1,0:T(8,128)(2,1)S(1)} %get-tuple-element.95), channel_id=1, source_target_pairs={{0,3},{1,2},{2,1},{3,0},{4,7},{5,6},{6,5},{7,4},{8,11},{9,10},{10,... | collective-permute-start | bytes 786440 | tf_op jit(solution)/shard_map/ppermute | solution.py:373
  95.5 37.6 %collective-permute-start.25 = (bf16[8,128,512]{2,1,0:T(8,128)(2,1)}, bf16[8,128,512]{2,1,0:T(8,128)(2,1)}, u32[]{:S(2)}, u32[]{:S(2)}) collective-permute-start(bf16[8,128,512]{2,1,0:T(8,128)(2,1)} %get-tuple-element.98), channel_id=1, source_target_pairs={{0,4},{1,5},{2,6},{3,7},{4,0},{5,1},{6,2},{7,3},{8,12},{9,13},{10,... | collective-permute-start | bytes 3145736 | tf_op jit(solution)/shard_map/ppermute | solution.py:362
  99.2 12.2 %copy-start.28 = (s32[4,16]{1,0:T(4,128)S(1)}, s32[4,16]{1,0:T(4,128)}, u32[]{:S(2)}) copy-start(s32[4,16]{1,0:T(4,128)} %get-tuple-element.108) | copy-start | bytes 772
  99.2 12.2 %copy-start.29 = (s32[4,16]{1,0:T(4,128)S(1)}, s32[4,16]{1,0:T(4,128)}, u32[]{:S(2)}) copy-start(s32[4,16]{1,0:T(4,128)} %get-tuple-element.121) | copy-start | bytes 772
  99.2 12.2 %copy-start.33 = (pred[4,16]{1,0:T(4,128)(4,1)S(1)}, pred[4,16]{1,0:T(4,128)(4,1)}, u32[]{:S(2)}) copy-start(pred[4,16]{1,0:T(4,128)(4,1)} %get-tuple-element.123) | copy-start | bytes 196
  99.2 21.3 %copy-start.14 = (bf16[2,128,512]{2,1,0:T(8,128)(2,1)S(1)}, bf16[2,128,512]{2,1,0:T(8,128)(2,1)}, u32[]{:S(2)}) copy-start(bf16[2,128,512]{2,1,0:T(8,128)(2,1)} %copy-done.13) | copy-start | bytes 786436
  99.2 23.7 %copy-start.16 = (bf16[2,128,512]{2,1,0:T(8,128)(2,1)S(1)}, bf16[2,128,512]{2,1,0:T(8,128)(2,1)}, u32[]{:S(2)}) copy-start(bf16[2,128,512]{2,1,0:T(8,128)(2,1)} %copy-done.15) | copy-start | bytes 786436
  99.3 24.7 %copy-start.12 = (bf16[2,128,512]{2,1,0:T(8,128)(2,1)S(1)}, bf16[2,128,512]{2,1,0:T(8,128)(2,1)}, u32[]{:S(2)}) copy-start(bf16[2,128,512]{2,1,0:T(8,128)(2,1)} %copy-done.11) | copy-start | bytes 786436
  107.0 12.8 %collective-permute-start.20 = (bf16[2,128,512]{2,1,0:T(8,128)(2,1)}, bf16[2,128,512]{2,1,0:T(8,128)(2,1)S(1)}, u32[]{:S(2)}, u32[]{:S(2)}) collective-permute-start(bf16[2,128,512]{2,1,0:T(8,128)(2,1)} %get-tuple-element.91), channel_id=1, source_target_pairs={{0,2},{1,3},{2,0},{3,1},{4,6},{5,7},{6,4},{7,5},{8,10},{9,11},{10,... | collective-permute-start | bytes 786440 | tf_op jit(solution)/shard_map/ppermute | solution.py:373
  108.5 13.7 %collective-permute-start.23 = (bf16[2,128,512]{2,1,0:T(8,128)(2,1)}, bf16[2,128,512]{2,1,0:T(8,128)(2,1)S(1)}, u32[]{:S(2)}, u32[]{:S(2)}) collective-permute-start(bf16[2,128,512]{2,1,0:T(8,128)(2,1)} %get-tuple-element.96), channel_id=1, source_target_pairs={{0,3},{1,2},{2,1},{3,0},{4,7},{5,6},{6,5},{7,4},{8,11},{9,10},{10,... | collective-permute-start | bytes 786440 | tf_op jit(solution)/shard_map/ppermute | solution.py:373
  108.7 14.6 %collective-permute-start.17 = (bf16[2,128,512]{2,1,0:T(8,128)(2,1)}, bf16[2,128,512]{2,1,0:T(8,128)(2,1)S(1)}, u32[]{:S(2)}, u32[]{:S(2)}) collective-permute-start(bf16[2,128,512]{2,1,0:T(8,128)(2,1)} %get-tuple-element.86), channel_id=1, source_target_pairs={{0,1},{1,0},{2,3},{3,2},{4,5},{5,4},{6,7},{7,6},{8,9},{9,8},{10,11... | collective-permute-start | bytes 786440 | tf_op jit(solution)/shard_map/ppermute | solution.py:373
  111.3 19.8 %collective-permute-start.26 = (bf16[4,128,512]{2,1,0:T(8,128)(2,1)S(1)}, bf16[4,128,512]{2,1,0:T(8,128)(2,1)}, u32[]{:S(2)}, u32[]{:S(2)}) collective-permute-start(bf16[4,128,512]{2,1,0:T(8,128)(2,1)S(1)} %owner_sum.4), channel_id=1, source_target_pairs={{0,4},{1,5},{2,6},{3,7},{4,0},{5,1},{6,2},{7,3},{8,12},{9,13},{10,... | collective-permute-start | bytes 1572872 | tf_op jit(solution)/shard_map/ppermute | solution.py:362
  120.5 14.7 %collective-permute-start.21 = (bf16[2,128,512]{2,1,0:T(8,128)(2,1)S(1)}, bf16[2,128,512]{2,1,0:T(8,128)(2,1)S(1)}, u32[]{:S(2)}, u32[]{:S(2)}) collective-permute-start(bf16[2,128,512]{2,1,0:T(8,128)(2,1)S(1)} %copy-done.14), channel_id=1, source_target_pairs={{0,2},{1,3},{2,0},{3,1},{4,6},{5,7},{6,4},{7,5},{8,10},{9,11},{10,... | collective-permute-start | bytes 786440 | tf_op jit(solution)/shard_map/ppermute | solution.py:373
  123.0 12.3 %collective-permute-start.24 = (bf16[2,128,512]{2,1,0:T(8,128)(2,1)S(1)}, bf16[2,128,512]{2,1,0:T(8,128)(2,1)S(1)}, u32[]{:S(2)}, u32[]{:S(2)}) collective-permute-start(bf16[2,128,512]{2,1,0:T(8,128)(2,1)S(1)} %copy-done.16), channel_id=1, source_target_pairs={{0,3},{1,2},{2,1},{3,0},{4,7},{5,6},{6,5},{7,4},{8,11},{9,10},{10,... | collective-permute-start | bytes 786440 | tf_op jit(solution)/shard_map/ppermute | solution.py:373
  124.0 11.5 %collective-permute-start.18 = (bf16[2,128,512]{2,1,0:T(8,128)(2,1)S(1)}, bf16[2,128,512]{2,1,0:T(8,128)(2,1)S(1)}, u32[]{:S(2)}, u32[]{:S(2)}) collective-permute-start(bf16[2,128,512]{2,1,0:T(8,128)(2,1)S(1)} %copy-done.12), channel_id=1, source_target_pairs={{0,1},{1,0},{2,3},{3,2},{4,5},{5,4},{6,7},{7,6},{8,9},{9,8},{10,11... | collective-permute-start | bytes 786440 | tf_op jit(solution)/shard_map/ppermute | solution.py:373
  133.1 25.8 %collective-permute-start.31 = (bf16[4,128,512]{2,1,0:T(8,128)(2,1)}, bf16[4,128,512]{2,1,0:T(8,128)(2,1)}, u32[]{:S(2)}, u32[]{:S(2)}) collective-permute-start(bf16[4,128,512]{2,1,0:T(8,128)(2,1)} %add_convert_fusion), channel_id=1, source_target_pairs={{0,24},{1,25},{2,26},{3,27},{4,28},{5,29},{6,30},{7,31},{8,16},{9,... | collective-permute-start | bytes 1572872 | tf_op jit(solution)/shard_map/ppermute | solution.py:362
  135.4 9.0 %collective-permute-start.27 = (bf16[2,128,512]{2,1,0:T(8,128)(2,1)}, bf16[2,128,512]{2,1,0:T(8,128)(2,1)S(1)}, u32[]{:S(2)}, u32[]{:S(2)}) collective-permute-start(bf16[2,128,512]{2,1,0:T(8,128)(2,1)} %get-tuple-element.102), channel_id=1, source_target_pairs={{0,1},{1,0},{2,3},{3,2},{4,5},{5,4},{6,7},{7,6},{8,9},{9,8},{10,11... | collective-permute-start | bytes 786440 | tf_op jit(solution)/shard_map/ppermute | solution.py:373
  136.9 14.9 %collective-permute-start.28 = (bf16[2,128,512]{2,1,0:T(8,128)(2,1)}, bf16[2,128,512]{2,1,0:T(8,128)(2,1)S(1)}, u32[]{:S(2)}, u32[]{:S(2)}) collective-permute-start(bf16[2,128,512]{2,1,0:T(8,128)(2,1)} %get-tuple-element.104), channel_id=1, source_target_pairs={{0,2},{1,3},{2,0},{3,1},{4,6},{5,7},{6,4},{7,5},{8,10},{9,11},{10,... | collective-permute-start | bytes 786440 | tf_op jit(solution)/shard_map/ppermute | solution.py:373
  138.5 13.3 %collective-permute-start.29 = (bf16[2,128,512]{2,1,0:T(8,128)(2,1)}, bf16[2,128,512]{2,1,0:T(8,128)(2,1)S(1)}, u32[]{:S(2)}, u32[]{:S(2)}) collective-permute-start(bf16[2,128,512]{2,1,0:T(8,128)(2,1)} %get-tuple-element.106), channel_id=1, source_target_pairs={{0,3},{1,2},{2,1},{3,0},{4,7},{5,6},{6,5},{7,4},{8,11},{9,10},{10,... | collective-permute-start | bytes 786440 | tf_op jit(solution)/shard_map/ppermute | solution.py:373
  151.8 7.1 %copy-start.1 = (bf16[768,256]{1,0:T(8,128)(2,1)S(1)}, bf16[768,256]{1,0:T(8,128)(2,1)}, u32[]{:S(2)}) copy-start(bf16[768,256]{1,0:T(8,128)(2,1)} %refs_2_.3) | copy-start | bytes 1179652
  151.8 7.1 %copy-start.2 = (bf16[768,256]{1,0:T(8,128)(2,1)S(1)}, bf16[768,256]{1,0:T(8,128)(2,1)}, u32[]{:S(2)}) copy-start(bf16[768,256]{1,0:T(8,128)(2,1)} %refs_3_.3) | copy-start | bytes 1179652
  151.8 7.1 %copy-start.23 = (f32[512,768]{1,0:T(8,128)S(1)}, f32[512,768]{1,0:T(8,128)}, u32[]{:S(2)}) copy-start(f32[512,768]{1,0:T(8,128)} %fusion.14.refs_1_) | copy-start | bytes 4718596
  152.7 7.8 %collective-permute-start.30 = (bf16[4,128,512]{2,1,0:T(8,128)(2,1)S(1)}, bf16[4,128,512]{2,1,0:T(8,128)(2,1)S(1)}, u32[]{:S(2)}, u32[]{:S(2)}) collective-permute-start(bf16[4,128,512]{2,1,0:T(8,128)(2,1)S(1)} %owner_sum.5), channel_id=1, source_target_pairs={{0,16},{1,17},{2,18},{3,19},{4,20},{5,21},{6,22},{7,23},{8,24},{9,... | collective-permute-start | bytes 1572872 | tf_op jit(solution)/shard_map/ppermute | solution.py:362
  (19 other events, 53.4 us)

commit v14 on v12

--- a/solution.py
+++ b/solution.py
@@ -16,9 +16,8 @@
 KV = KV_HEADS * HEAD_DIM
 PAIR = 2 * HEAD_DIM
 CODE = 16
-NEXT_FLOPS = 10_000_000_000
-FAR_SUM_FLOPS = 5_000_000_000
-FAR_FLOPS = 20_000_000_000
+FAR_SUM_FLOPS = 8_000_000_000
+FAR_FLOPS = 30_000_000_000
 MAJOR = 4
 TEMPER = HEAD_DIM ** (-0.5)
 EPSILON = 1e-06
@@ -103,6 +102,8 @@
         start(fetch, get_ref, 0, entries)
 
     first = step * per_step * list_len
+    for i in range(per_step * list_len):
+        fetch(first + i, 0, 0).wait()
     pairs = range(KV // PAIR)
     keys, values, wide, scores, exact, scales, grads, overlap, prob_grads = (
         {} for _ in range(9)
@@ -113,11 +114,9 @@
         return pl.ds(pl.multiple_of((step * per_step + b) * size, size), size)
 
     def cols_at(b):
-        return pl.ds(pl.multiple_of((step * per_step + b) * BLK, BLK), BLK)
+        return slice(b * BLK, (b + 1) * BLK)
 
     def score(b):
-        for i in range(list_len):
-            fetch(first + b * list_len + i, 0, 0).wait()
         here = rows_at(b)
         queries = q_ref[:, cols_at(b)] * jnp.asarray(TEMPER, BF16)
         for j in pairs:
@@ -178,19 +177,16 @@
         parts_scr[here, j * PAIR : (j + 1) * PAIR] = key_part.astype(BF16)
         parts_scr[here, KV + j * PAIR : KV + (j + 1) * PAIR] = value_part.astype(BF16)
 
-    score(0)
+    for b in range(per_step):
+        score(b)
     for j in pairs:
         soften(0, j)
-    if per_step > 1:
-        score(1)
     normalise(0)
     for b in range(per_step):
         for j in pairs:
             regrade(b, j)
             if b + 1 < per_step:
                 soften(b + 1, j)
-        if b + 2 < per_step:
-            score(b + 2)
         for j in pairs:
             finish_pair(b, j)
             if b + 1 < per_step and j == 0:
@@ -208,9 +204,9 @@
     slot_shape = (CAP,) + arrived[0].shape[1:]
     blocks = rows // BLK
     entries = blocks * list_len
-    resident = list_len <= 4
-    per_step = blocks if resident else 1
-    place = WHOLE if resident else pl.BlockSpec(memory_space=pl.ANY)
+    per_step = 2 if list_len <= 4 and blocks % 2 == 0 else 1
+    row_spec = pl.BlockSpec((width, per_step * BLK), lambda r, g, p: (0, r))
+    anywhere = pl.BlockSpec(memory_space=pl.ANY)
     keys = list_len * BLK
     pairs = HEADS * rows * keys
     return pl.pallas_call(
@@ -218,8 +214,8 @@
         grid_spec=pltpu.PrefetchScalarGridSpec(
             num_scalar_prefetch=2,
             grid=(blocks // per_step,),
-            in_specs=[WHOLE] * 2 + [place] * len(arrived),
-            out_specs=[WHOLE] * 2 + [place] * len(arrived),
+            in_specs=[row_spec, row_spec] + [anywhere] * len(arrived),
+            out_specs=[row_spec, row_spec] + [anywhere] * len(arrived),
             scratch_shapes=[
                 pltpu.VMEM((per_step, KV // PAIR, keys, 2 * GROUP * BLK), BF16),
                 pltpu.VMEM((entries * BLK, 2 * KV), BF16),
@@ -230,7 +226,7 @@
         ),
         out_shape=[jax.ShapeDtypeStruct((width, rows), BF16)] * 2
         + [jax.ShapeDtypeStruct(slot_shape, BF16)] * len(arrived),
-        compiler_params=params(40 if resident else 56),
+        compiler_params=params(56),
         cost_estimate=pl.CostEstimate(
             flops=12 * pairs * HEAD_DIM, bytes_accessed=16 * rows * width, transcendentals=pairs
         ),
@@ -428,15 +424,13 @@
     last_sum = swap(last_sum, 1, 0).astype(F32)
     far_sum = owner_sum(2, wanted, [back[2][0], *far], block_count, F32, FAR_SUM_FLOPS)
     far_sum = (far_sum + last_sum).astype(BF16)
-    beside[0] = after(beside[0], far_sum)
     next_sum = owner_sum(1, wanted, [back[1][0], *beside], block_count, BF16, 0)
     own = spread([after(after(x, far_sum), next_sum) for x in back[0][1:]], beside)
     own_sum = owner_sum(0, wanted, [back[0][0], *own], block_count, BF16, 0)
-    sums = (swap(far_sum, 2, 1), swap(next_sum, 1, 1), swap(own_sum, 0, 1))
-    far_grad, next_grad, own_grad = (x.reshape(rows, 2 * KV) for x in sums)
+    far_grad = swap(far_sum, 2, 1).reshape(rows, 2 * KV)
+    near_grads = [x.reshape(rows, 2 * KV) for x in (swap(next_sum, 1, 1), swap(own_sum, 0, 1))]
     query_term = finish([far_grad], query_term, w_key, w_value, F32, FAR_FLOPS)
-    query_term = finish([next_grad], query_term, w_key, w_value, F32, NEXT_FLOPS)
-    input_grad = finish([own_grad], query_term, w_key, w_value, BF16, 800_000_000)
+    input_grad = finish(near_grads, query_term, w_key, w_value, BF16, 800_000_000)
     return (layer_out[None], input_grad[None])
 
 

time: 162 us -> 157 us (0.969)
  Pallas kernels: 35.3 us -> 29.7 us
  matrix products: 5.64 us -> 9.04 us
    pallas_call x1, Pallas kernels: 22.7 us -> 17.7 us  [attention(): pl.pallas_call(functools.partial(attention_kernel, list_len, per_step), g...]
    ppermute x24, waiting for transfers between devices: 50.5 us -> 48 us  [spread(): moved.append(lax.ppermute(value, 'tile', pairs))]
    ppermute x8, waiting for transfers between devices: 23.4 us -> 25.2 us  [swap(): return lax.ppermute(value, ('vintage', 'tile'), pairs)]
  transfers between devices with their start and end apart: 32 -> 32, of which waited for: 16 -> 17; matrix products, arithmetic and copies ran while one was open for 6% -> 8% of each run, Pallas kernels for 5% -> 5%
where the time goes in v14:
time: 157 us
  waiting for transfers between devices  73.2 us (47%)
  starting transfers between devices  39 us (25%)
  Pallas kernels  29.7 us (19%)
  matrix products  9.04 us (6%)
  other arithmetic  2.97 us (2%)
  local copies, waits for them, and re-layouts  2.04 us (1%)
    ppermute x24, waiting for transfers between devices, spread(): moved.append(lax.ppermute(value, 'tile', pairs))  48 us
    ppermute x24, starting transfers between devices, spread(): moved.append(lax.ppermute(value, 'tile', pairs))  33.1 us
    ppermute x8, waiting for transfers between devices, swap(): return lax.ppermute(value, ('vintage', 'tile'), pairs)  25.2 us
    pallas_call x1, Pallas kernels, attention(): pl.pallas_call(functools.partial(attention_kernel, list_len, per_step), g...  17.7 us
    ppermute x8, starting transfers between devices, swap(): return lax.ppermute(value, ('vintage', 'tile'), pairs)  5.87 us
    dot_general x1, matrix products, dot_nt(): lax.dot_general(a, b, (((1,), (1,)), ((), ())), preferred_element_type=F32)  3.53 us
    pallas_call x1, Pallas kernels, project(): pl.pallas_call(project_kernel, in_specs=[pl.BlockSpec(memory_space=pl.ANY...  3.4 us
    pallas_call x4, Pallas kernels, owner_sum(): pl.pallas_call(functools.partial(owner_kernel, group * len(parts) * CAP),...  3.35 us
  transfers between devices with their start and end apart: 32, of which 17 were waited for; matrix products, arithmetic and copies ran while one was open for 8% of the time, Pallas kernels for 5%

profile of v14, /device:TPU:0, one launch (start us, length us, event | category | flops | bytes accessed | tf_op | source)
XLA Modules:
  0.0 157.0 jit_solution(17219921102877635002)
XLA Ops:
  0.7 3.4 %project.1 = bf16[512,512]{1,0:T(8,128)(2,1)} custom-call(bf16[512,768]{1,0:T(8,128)(2,1)} %bitcast.51, bf16[768,256]{1,0:T(8,128)(2,1)} %refs_3_.3, bf16[768,256]{1,0:T(8,128)(2,1)} %refs_4_.1), custom_call_target="tpu_custom_call" | custom-call | tf_op jit(solution)/shard_map/project/pallas_call | solution.py:260
  4.1 2.5 %collective-permute-start.4 = (bf16[4,128,512]{2,1,0:T(8,128)(2,1)}, bf16[4,128,512]{2,1,0:T(8,128)(2,1)S(1)}, u32[]{:S(2)}, u32[]{:S(2)}) collective-permute-start(bf16[4,128,512]{2,1,0:T(8,128)(2,1)} %bitcast.52), channel_id=1, source_target_pairs={{0,20},{1,21},{2,22},{3,23},{4,16},{5,17},{6,18},{7,19},{8,28},{9,... | collective-permute-start | bytes 1572872 | tf_op jit(solution)/shard_map/ppermute | solution.py:361
  6.6 0.7 collective-permute-start
  9.2 2.4 %collective-permute-start.8 = (bf16[4,128,512]{2,1,0:T(8,128)(2,1)}, bf16[4,128,512]{2,1,0:T(8,128)(2,1)S(1)}, u32[]{:S(2)}, u32[]{:S(2)}) collective-permute-start(bf16[4,128,512]{2,1,0:T(8,128)(2,1)} %bitcast.54), channel_id=1, source_target_pairs={{0,24},{1,25},{2,26},{3,27},{4,28},{5,29},{6,30},{7,31},{8,16},{9,... | collective-permute-start | bytes 1572872 | tf_op jit(solution)/shard_map/ppermute | solution.py:361
  13.1 2.5 %collective-permute-start.3 = (bf16[2,128,512]{2,1,0:T(8,128)(2,1)S(1)}, bf16[2,128,512]{2,1,0:T(8,128)(2,1)S(1)}, u32[]{:S(2)}, u32[]{:S(2)}) collective-permute-start(bf16[2,128,512]{2,1,0:T(8,128)(2,1)S(1)} %get-tuple-element.63), channel_id=1, source_target_pairs={{0,3},{1,2},{2,1},{3,0},{4,7},{5,6},{6,5},{7,4},{8,11},{9,10},{10,... | collective-permute-start | bytes 786440 | tf_op jit(solution)/shard_map/ppermute | solution.py:372
  16.6 10.5 %collective-permute-done.4.tile_ref.refs_4_ = bf16[4,128,512]{2,1,0:T(8,128)(2,1)S(1)} collective-permute-done((bf16[4,128,512]{2,1,0:T(8,128)(2,1)}, bf16[4,128,512]{2,1,0:T(8,128)(2,1)S(1)}, u32[]{:S(2)}, u32[]{:S(2)}) %collective-permute-start.4) | collective-permute-done | bytes 524320 | tf_op jit(solution)/shard_map/ppermute | solution.py:361
  27.2 1.4 pack.5
  28.6 3.9 %collective-permute-start.7 = (bf16[2,128,512]{2,1,0:T(8,128)(2,1)}, bf16[2,128,512]{2,1,0:T(8,128)(2,1)}, u32[]{:S(2)}, u32[]{:S(2)}) collective-permute-start(bf16[2,128,512]{2,1,0:T(8,128)(2,1)} %get-tuple-element.69), channel_id=1, source_target_pairs={{0,3},{1,2},{2,1},{3,0},{4,7},{5,6},{6,5},{7,4},{8,11},{9,10},{10,... | collective-permute-start | bytes 786440 | tf_op jit(solution)/shard_map/ppermute | solution.py:372
  33.1 2.5 %collective-permute-done.8.tile_ref.refs_8_ = bf16[4,128,512]{2,1,0:T(8,128)(2,1)S(1)} collective-permute-done((bf16[4,128,512]{2,1,0:T(8,128)(2,1)}, bf16[4,128,512]{2,1,0:T(8,128)(2,1)S(1)}, u32[]{:S(2)}, u32[]{:S(2)}) %collective-permute-start.8) | collective-permute-done | bytes 524320 | tf_op jit(solution)/shard_map/ppermute | solution.py:361
  35.8 1.2 compare_select_fusion.3
  37.6 2.3 %collective-permute-done.7.refs_7_ = bf16[2,128,512]{2,1,0:T(8,128)(2,1)} collective-permute-done((bf16[2,128,512]{2,1,0:T(8,128)(2,1)}, bf16[2,128,512]{2,1,0:T(8,128)(2,1)}, u32[]{:S(2)}, u32[]{:S(2)}) %collective-permute-start.7) | collective-permute-done | bytes 262176 | tf_op jit(solution)/shard_map/ppermute | solution.py:372
  39.9 3.0 %collective-permute-start.11 = (bf16[2,128,512]{2,1,0:T(8,128)(2,1)S(1)}, bf16[2,128,512]{2,1,0:T(8,128)(2,1)S(1)}, u32[]{:S(2)}, u32[]{:S(2)}) collective-permute-start(bf16[2,128,512]{2,1,0:T(8,128)(2,1)S(1)} %get-tuple-element.77), channel_id=1, source_target_pairs={{0,3},{1,2},{2,1},{3,0},{4,7},{5,6},{6,5},{7,4},{8,11},{9,10},{10,... | collective-permute-start | bytes 786440 | tf_op jit(solution)/shard_map/ppermute | solution.py:372
  42.9 2.6 %collective-permute-done.6.refs_6_ = bf16[2,128,512]{2,1,0:T(8,128)(2,1)} collective-permute-done((bf16[2,128,512]{2,1,0:T(8,128)(2,1)}, bf16[2,128,512]{2,1,0:T(8,128)(2,1)}, u32[]{:S(2)}, u32[]{:S(2)}) %collective-permute-start.6) | collective-permute-done | bytes 262176 | tf_op jit(solution)/shard_map/ppermute | solution.py:372
  45.4 2.0 %collective-permute-start.10 = (bf16[2,128,512]{2,1,0:T(8,128)(2,1)S(1)}, bf16[2,128,512]{2,1,0:T(8,128)(2,1)S(1)}, u32[]{:S(2)}, u32[]{:S(2)}) collective-permute-start(bf16[2,128,512]{2,1,0:T(8,128)(2,1)S(1)} %get-tuple-element.75), channel_id=1, source_target_pairs={{0,2},{1,3},{2,0},{3,1},{4,6},{5,7},{6,4},{7,5},{8,10},{9,11},{10,... | collective-permute-start | bytes 786440 | tf_op jit(solution)/shard_map/ppermute | solution.py:372
  47.6 3.5 %fusion.ng_ref = f32[768,512]{1,0:T(8,128)} fusion(bf16[768,768]{1,0:T(8,128)(2,1)} %param.13, bf16[1,512,768]{2,1,0:T(8,128)(2,1)} %param.9), kind=kOutput, calls=%fused_computation.4 | convolution fusion | flops 603979776 | bytes 3538944 | tf_op jit(solution)/shard_map/dot_general | solution.py:34
  51.8 2.3 %collective-permute-start.15 = (bf16[2,128,512]{2,1,0:T(8,128)(2,1)S(1)}, bf16[2,128,512]{2,1,0:T(8,128)(2,1)S(1)}, u32[]{:S(2)}, u32[]{:S(2)}) collective-permute-start(bf16[2,128,512]{2,1,0:T(8,128)(2,1)S(1)} %get-tuple-element.83), channel_id=1, source_target_pairs={{0,3},{1,2},{2,1},{3,0},{4,7},{5,6},{6,5},{7,4},{8,11},{9,10},{10,... | collective-permute-start | bytes 786440 | tf_op jit(solution)/shard_map/ppermute | solution.py:372
  54.0 2.6 %collective-permute-done.10.refs_10_ = bf16[2,128,512]{2,1,0:T(8,128)(2,1)S(1)} collective-permute-done((bf16[2,128,512]{2,1,0:T(8,128)(2,1)S(1)}, bf16[2,128,512]{2,1,0:T(8,128)(2,1)S(1)}, u32[]{:S(2)}, u32[]{:S(2)}) %collective-permute-start.10) | collective-permute-done | bytes 262176 | tf_op jit(solution)/shard_map/ppermute | solution.py:372
  56.6 2.1 %collective-permute-start.14 = (bf16[2,128,512]{2,1,0:T(8,128)(2,1)S(1)}, bf16[2,128,512]{2,1,0:T(8,128)(2,1)S(1)}, u32[]{:S(2)}, u32[]{:S(2)}) collective-permute-start(bf16[2,128,512]{2,1,0:T(8,128)(2,1)S(1)} %get-tuple-element.81), channel_id=1, source_target_pairs={{0,2},{1,3},{2,0},{3,1},{4,6},{5,7},{6,4},{7,5},{8,10},{9,11},{10,... | collective-permute-start | bytes 786440 | tf_op jit(solution)/shard_map/ppermute | solution.py:372
  58.7 1.5 collective-permute-start.13
  60.1 1.7 %convolution_convert_fusion.1.q_ref = bf16[768,512]{1,0:T(8,128)(2,1)} fusion(bf16[768,768]{1,0:T(8,128)(2,1)S(1)} %copy-done, bf16[1,512,768]{2,1,0:T(8,128)(2,1)S(1)} %copy-done.11), kind=kOutput, calls=%fused_computation.2 | convolution fusion | flops 604372992 | bytes 2752512 | tf_op jit(solution)/shard_map/dot_general | solution.py:407
  62.3 5.2 %collective-permute-done.14.refs_14_ = bf16[2,128,512]{2,1,0:T(8,128)(2,1)S(1)} collective-permute-done((bf16[2,128,512]{2,1,0:T(8,128)(2,1)S(1)}, bf16[2,128,512]{2,1,0:T(8,128)(2,1)S(1)}, u32[]{:S(2)}, u32[]{:S(2)}) %collective-permute-start.14) | collective-permute-done | bytes 262176 | tf_op jit(solution)/shard_map/ppermute | solution.py:372
  68.5 17.7 %attention.1 = (bf16[768,512]{1,0:T(8,128)(2,1)}, bf16[768,512]{1,0:T(8,128)(2,1)}, bf16[2,128,512]{2,1,0:T(8,128)(2,1)}, bf16[2,128,512]{2,1,0:T(8,128)(2,1)}, ...) custom-call(s32[16]{0:T(128)} %get-tuple-element.125.get_ref, ...), custom_call_target="tpu_custom_call" | custom-call | flops 2415919104 | bytes 6291456 | tf_op jit(solution)/shard_map/attention/pallas_call | solution.py:212
  86.2 1.6 %collective-permute-start.16 = (bf16[2,128,512]{2,1,0:T(8,128)(2,1)}, bf16[2,128,512]{2,1,0:T(8,128)(2,1)S(1)}, u32[]{:S(2)}, u32[]{:S(2)}) collective-permute-start(bf16[2,128,512]{2,1,0:T(8,128)(2,1)} %get-tuple-element.84), channel_id=1, source_target_pairs={{0,1},{1,0},{2,3},{3,2},{4,5},{5,4},{6,7},{7,6},{8,9},{9,8},{10,11... | collective-permute-start | bytes 786440 | tf_op jit(solution)/shard_map/ppermute | solution.py:372
  87.8 1.5 collective-permute-start.19
  89.8 2.1 %fusion.17.refs_1_ = f32[512,768]{1,0:T(8,128)S(1)} fusion(bf16[768,512]{1,0:T(8,128)(2,1)} %get-tuple-element.85, bf16[768,768]{1,0:T(8,128)(2,1)S(1)} %copy-done), kind=kOutput, calls=%fused_computation.46 | convolution fusion | flops 603979776 | bytes 3538944 | tf_op jit(solution)/shard_map/dot_general | solution.py:416
  91.9 1.7 %convolution_convert_fusion = bf16[512,768]{1,0:T(8,128)(2,1)} fusion(bf16[768,512]{1,0:T(8,128)(2,1)S(1)} %copy-done.33, bf16[768,768]{1,0:T(8,128)(2,1)S(1)} %copy-done.14), kind=kOutput, calls=%fused_computation.1 | convolution fusion | flops 604372992 | bytes 2752512 | tf_op jit(solution)/shard_map/dot_general | solution.py:38
  93.6 8.0 %collective-permute-done.19.refs_2_ = bf16[2,128,512]{2,1,0:T(8,128)(2,1)S(1)} collective-permute-done((bf16[2,128,512]{2,1,0:T(8,128)(2,1)}, bf16[2,128,512]{2,1,0:T(8,128)(2,1)S(1)}, u32[]{:S(2)}, u32[]{:S(2)}) %collective-permute-start.19) | collective-permute-done | bytes 262176 | tf_op jit(solution)/shard_map/ppermute | solution.py:372
  101.7 1.5 collective-permute-start.20
  103.2 2.0 %collective-permute-start.17 = (bf16[2,128,512]{2,1,0:T(8,128)(2,1)S(1)}, bf16[2,128,512]{2,1,0:T(8,128)(2,1)S(1)}, u32[]{:S(2)}, u32[]{:S(2)}) collective-permute-start(bf16[2,128,512]{2,1,0:T(8,128)(2,1)S(1)} %copy-done.25), channel_id=1, source_target_pairs={{0,1},{1,0},{2,3},{3,2},{4,5},{5,4},{6,7},{7,6},{8,9},{9,8},{10,11... | collective-permute-start | bytes 786440 | tf_op jit(solution)/shard_map/ppermute | solution.py:372
  105.2 1.0 owner_sum.6
  106.2 7.9 %collective-permute-done.20.refs_2_ = bf16[2,128,512]{2,1,0:T(8,128)(2,1)S(1)} collective-permute-done((bf16[2,128,512]{2,1,0:T(8,128)(2,1)S(1)}, bf16[2,128,512]{2,1,0:T(8,128)(2,1)S(1)}, u32[]{:S(2)}, u32[]{:S(2)}) %collective-permute-start.20) | collective-permute-done | bytes 262176 | tf_op jit(solution)/shard_map/ppermute | solution.py:372
  114.1 1.7 %collective-permute-start.21 = (bf16[2,128,512]{2,1,0:T(8,128)(2,1)S(1)}, bf16[2,128,512]{2,1,0:T(8,128)(2,1)S(1)}, u32[]{:S(2)}, u32[]{:S(2)}) collective-permute-start(bf16[2,128,512]{2,1,0:T(8,128)(2,1)S(1)} %copy-done.23), channel_id=1, source_target_pairs={{0,2},{1,3},{2,0},{3,1},{4,6},{5,7},{6,4},{7,5},{8,10},{9,11},{10,... | collective-permute-start | bytes 786440 | tf_op jit(solution)/shard_map/ppermute | solution.py:372
  115.9 0.7 collective-permute-start.24
  116.6 1.1 collective-permute-start.18
  117.6 0.8 owner_sum.5
  118.7 8.2 %collective-permute-done.21.refs_2_ = bf16[2,128,512]{2,1,0:T(8,128)(2,1)S(1)} collective-permute-done((bf16[2,128,512]{2,1,0:T(8,128)(2,1)S(1)}, bf16[2,128,512]{2,1,0:T(8,128)(2,1)S(1)}, u32[]{:S(2)}, u32[]{:S(2)}) %collective-permute-start.21) | collective-permute-done | bytes 262176 | tf_op jit(solution)/shard_map/ppermute | solution.py:372
  126.9 1.3 collective-permute-done.18.refs_1_
  128.2 0.8 owner_sum.4
  129.1 0.6 collective-permute-start.27
  129.7 1.2 collective-permute-start.28
  130.9 1.7 %collective-permute-start.29 = (bf16[2,128,512]{2,1,0:T(8,128)(2,1)S(1)}, bf16[2,128,512]{2,1,0:T(8,128)(2,1)S(1)}, u32[]{:S(2)}, u32[]{:S(2)}) collective-permute-start(bf16[2,128,512]{2,1,0:T(8,128)(2,1)S(1)} %copy-done.18), channel_id=1, source_target_pairs={{0,3},{1,2},{2,1},{3,0},{4,7},{5,6},{6,5},{7,4},{8,11},{9,10},{10,... | collective-permute-start | bytes 786440 | tf_op jit(solution)/shard_map/ppermute | solution.py:372
  132.6 5.4 %collective-permute-done.27.refs_1_ = bf16[2,128,512]{2,1,0:T(8,128)(2,1)S(1)} collective-permute-done((bf16[2,128,512]{2,1,0:T(8,128)(2,1)S(1)}, bf16[2,128,512]{2,1,0:T(8,128)(2,1)S(1)}, u32[]{:S(2)}, u32[]{:S(2)}) %collective-permute-start.27) | collective-permute-done | bytes 262176 | tf_op jit(solution)/shard_map/ppermute | solution.py:372
  138.0 2.1 %collective-permute-done.28.refs_2_ = bf16[2,128,512]{2,1,0:T(8,128)(2,1)S(1)} collective-permute-done((bf16[2,128,512]{2,1,0:T(8,128)(2,1)S(1)}, bf16[2,128,512]{2,1,0:T(8,128)(2,1)S(1)}, u32[]{:S(2)}, u32[]{:S(2)}) %collective-permute-start.28) | collective-permute-done | bytes 262176 | tf_op jit(solution)/shard_map/ppermute | solution.py:372
  140.1 1.8 %collective-permute-done.29.refs_3_ = bf16[2,128,512]{2,1,0:T(8,128)(2,1)S(1)} collective-permute-done((bf16[2,128,512]{2,1,0:T(8,128)(2,1)S(1)}, bf16[2,128,512]{2,1,0:T(8,128)(2,1)S(1)}, u32[]{:S(2)}, u32[]{:S(2)}) %collective-permute-start.29) | collective-permute-done | bytes 262176 | tf_op jit(solution)/shard_map/ppermute | solution.py:372
  141.9 0.8 owner_sum.7
  142.8 1.6 %collective-permute-done.31 = bf16[4,128,512]{2,1,0:T(8,128)(2,1)S(1)} collective-permute-done((bf16[4,128,512]{2,1,0:T(8,128)(2,1)S(1)}, bf16[4,128,512]{2,1,0:T(8,128)(2,1)S(1)}, u32[]{:S(2)}, u32[]{:S(2)}) %collective-permute-start.31) | collective-permute-done | bytes 524320 | tf_op jit(solution)/shard_map/ppermute | solution.py:361
  145.0 10.5 %collective-permute-done.25 = bf16[4,128,512]{2,1,0:T(8,128)(2,1)S(1)} collective-permute-done((bf16[4,128,512]{2,1,0:T(8,128)(2,1)S(1)}, bf16[4,128,512]{2,1,0:T(8,128)(2,1)S(1)}, u32[]{:S(2)}, u32[]{:S(2)}) %collective-permute-start.25) | collective-permute-done | bytes 524320 | tf_op jit(solution)/shard_map/ppermute | solution.py:361
  155.5 1.5 finish.3
  (119 shorter events, 9.5 us)
Async XLA Ops:
  0.6 59.5 %copy-start = (bf16[768,768]{1,0:T(8,128)(2,1)S(1)}, bf16[768,768]{1,0:T(8,128)(2,1)}, u32[]{:S(2)}) copy-start(bf16[768,768]{1,0:T(8,128)(2,1)} %param.10) | copy-start | bytes 3538948
  4.1 23.1 %collective-permute-start.4 = (bf16[4,128,512]{2,1,0:T(8,128)(2,1)}, bf16[4,128,512]{2,1,0:T(8,128)(2,1)S(1)}, u32[]{:S(2)}, u32[]{:S(2)}) collective-permute-start(bf16[4,128,512]{2,1,0:T(8,128)(2,1)} %bitcast.52), channel_id=1, source_target_pairs={{0,20},{1,21},{2,22},{3,23},{4,16},{5,17},{6,18},{7,19},{8,28},{9,... | collective-permute-start | bytes 1572872 | tf_op jit(solution)/shard_map/ppermute | solution.py:361
  6.6 2.6 %collective-permute-start = (bf16[4,128,512]{2,1,0:T(8,128)(2,1)}, bf16[4,128,512]{2,1,0:T(8,128)(2,1)S(1)}, u32[]{:S(2)}, u32[]{:S(2)}) collective-permute-start(bf16[4,128,512]{2,1,0:T(8,128)(2,1)} %bitcast.53), channel_id=1, source_target_pairs={{0,16},{1,17},{2,18},{3,19},{4,20},{5,21},{6,22},{7,23},{8,24},{9,... | collective-permute-start | bytes 1572872 | tf_op jit(solution)/shard_map/ppermute | solution.py:361
  9.2 41.9 %copy-start.4 = (bf16[4,128,512]{2,1,0:T(8,128)(2,1)}, bf16[4,128,512]{2,1,0:T(8,128)(2,1)S(1)}, u32[]{:S(2)}) copy-start(bf16[4,128,512]{2,1,0:T(8,128)(2,1)S(1)} %collective-permute-done.tile_ref.refs_0_) | copy-start | bytes 1572868
  9.2 26.4 %collective-permute-start.8 = (bf16[4,128,512]{2,1,0:T(8,128)(2,1)}, bf16[4,128,512]{2,1,0:T(8,128)(2,1)S(1)}, u32[]{:S(2)}, u32[]{:S(2)}) collective-permute-start(bf16[4,128,512]{2,1,0:T(8,128)(2,1)} %bitcast.54), channel_id=1, source_target_pairs={{0,24},{1,25},{2,26},{3,27},{4,28},{5,29},{6,30},{7,31},{8,16},{9,... | collective-permute-start | bytes 1572872 | tf_op jit(solution)/shard_map/ppermute | solution.py:361
  13.1 15.5 %collective-permute-start.3 = (bf16[2,128,512]{2,1,0:T(8,128)(2,1)S(1)}, bf16[2,128,512]{2,1,0:T(8,128)(2,1)S(1)}, u32[]{:S(2)}, u32[]{:S(2)}) collective-permute-start(bf16[2,128,512]{2,1,0:T(8,128)(2,1)S(1)} %get-tuple-element.63), channel_id=1, source_target_pairs={{0,3},{1,2},{2,1},{3,0},{4,7},{5,6},{6,5},{7,4},{8,11},{9,10},{10,... | collective-permute-start | bytes 786440 | tf_op jit(solution)/shard_map/ppermute | solution.py:372
  15.6 16.9 %collective-permute-start.2 = (bf16[2,128,512]{2,1,0:T(8,128)(2,1)S(1)}, bf16[2,128,512]{2,1,0:T(8,128)(2,1)S(1)}, u32[]{:S(2)}, u32[]{:S(2)}) collective-permute-start(bf16[2,128,512]{2,1,0:T(8,128)(2,1)S(1)} %get-tuple-element.62), channel_id=1, source_target_pairs={{0,2},{1,3},{2,0},{3,1},{4,6},{5,7},{6,4},{7,5},{8,10},{9,11},{10,... | collective-permute-start | bytes 786440 | tf_op jit(solution)/shard_map/ppermute | solution.py:372
  16.1 16.9 %collective-permute-start.1 = (bf16[2,128,512]{2,1,0:T(8,128)(2,1)S(1)}, bf16[2,128,512]{2,1,0:T(8,128)(2,1)S(1)}, u32[]{:S(2)}, u32[]{:S(2)}) collective-permute-start(bf16[2,128,512]{2,1,0:T(8,128)(2,1)S(1)} %get-tuple-element.61), channel_id=1, source_target_pairs={{0,1},{1,0},{2,3},{3,2},{4,5},{5,4},{6,7},{7,6},{8,9},{9,8},{10,11... | collective-permute-start | bytes 786440 | tf_op jit(solution)/shard_map/ppermute | solution.py:372
  27.2 24.0 %copy-start.3 = (bf16[4,128,512]{2,1,0:T(8,128)(2,1)}, bf16[4,128,512]{2,1,0:T(8,128)(2,1)S(1)}, u32[]{:S(2)}) copy-start(bf16[4,128,512]{2,1,0:T(8,128)(2,1)S(1)} %collective-permute-done.4.tile_ref.refs_4_) | copy-start | bytes 1572868
  28.6 11.3 %collective-permute-start.7 = (bf16[2,128,512]{2,1,0:T(8,128)(2,1)}, bf16[2,128,512]{2,1,0:T(8,128)(2,1)}, u32[]{:S(2)}, u32[]{:S(2)}) collective-permute-start(bf16[2,128,512]{2,1,0:T(8,128)(2,1)} %get-tuple-element.69), channel_id=1, source_target_pairs={{0,3},{1,2},{2,1},{3,0},{4,7},{5,6},{6,5},{7,4},{8,11},{9,10},{10,... | collective-permute-start | bytes 786440 | tf_op jit(solution)/shard_map/ppermute | solution.py:372
  32.5 13.0 %collective-permute-start.6 = (bf16[2,128,512]{2,1,0:T(8,128)(2,1)}, bf16[2,128,512]{2,1,0:T(8,128)(2,1)}, u32[]{:S(2)}, u32[]{:S(2)}) collective-permute-start(bf16[2,128,512]{2,1,0:T(8,128)(2,1)} %get-tuple-element.67), channel_id=1, source_target_pairs={{0,2},{1,3},{2,0},{3,1},{4,6},{5,7},{6,4},{7,5},{8,10},{9,11},{10,... | collective-permute-start | bytes 786440 | tf_op jit(solution)/shard_map/ppermute | solution.py:372
  33.0 14.5 %collective-permute-start.5 = (bf16[2,128,512]{2,1,0:T(8,128)(2,1)S(1)}, bf16[2,128,512]{2,1,0:T(8,128)(2,1)}, u32[]{:S(2)}, u32[]{:S(2)}) collective-permute-start(bf16[2,128,512]{2,1,0:T(8,128)(2,1)S(1)} %get-tuple-element.65), channel_id=1, source_target_pairs={{0,1},{1,0},{2,3},{3,2},{4,5},{5,4},{6,7},{7,6},{8,9},{9,8},{10,11... | collective-permute-start | bytes 786440 | tf_op jit(solution)/shard_map/ppermute | solution.py:372
  35.7 15.5 %copy-start.5 = (bf16[4,128,512]{2,1,0:T(8,128)(2,1)}, bf16[4,128,512]{2,1,0:T(8,128)(2,1)S(1)}, u32[]{:S(2)}) copy-start(bf16[4,128,512]{2,1,0:T(8,128)(2,1)S(1)} %collective-permute-done.8.tile_ref.refs_8_) | copy-start | bytes 1572868
  35.7 15.4 %collective-permute-start.12 = (bf16[4,128,512]{2,1,0:T(8,128)(2,1)S(1)}, bf16[4,128,512]{2,1,0:T(8,128)(2,1)S(1)}, u32[]{:S(2)}, u32[]{:S(2)}) collective-permute-start(bf16[4,128,512]{2,1,0:T(8,128)(2,1)S(1)} %collective-permute-done.8.tile_ref.refs_8_), channel_id=1, source_target_pairs={{0,4},{1,5},{2,6},{3,7},{4,0},{5,1},{6,2},{7,3},{8,12},{9,13},{10,... | collective-permute-start | bytes 1572872 | tf_op jit(solution)/shard_map/ppermute | solution.py:361
  39.9 11.9 %collective-permute-start.11 = (bf16[2,128,512]{2,1,0:T(8,128)(2,1)S(1)}, bf16[2,128,512]{2,1,0:T(8,128)(2,1)S(1)}, u32[]{:S(2)}, u32[]{:S(2)}) collective-permute-start(bf16[2,128,512]{2,1,0:T(8,128)(2,1)S(1)} %get-tuple-element.77), channel_id=1, source_target_pairs={{0,3},{1,2},{2,1},{3,0},{4,7},{5,6},{6,5},{7,4},{8,11},{9,10},{10,... | collective-permute-start | bytes 786440 | tf_op jit(solution)/shard_map/ppermute | solution.py:372
  45.4 11.2 %collective-permute-start.10 = (bf16[2,128,512]{2,1,0:T(8,128)(2,1)S(1)}, bf16[2,128,512]{2,1,0:T(8,128)(2,1)S(1)}, u32[]{:S(2)}, u32[]{:S(2)}) collective-permute-start(bf16[2,128,512]{2,1,0:T(8,128)(2,1)S(1)} %get-tuple-element.75), channel_id=1, source_target_pairs={{0,2},{1,3},{2,0},{3,1},{4,6},{5,7},{6,4},{7,5},{8,10},{9,11},{10,... | collective-permute-start | bytes 786440 | tf_op jit(solution)/shard_map/ppermute | solution.py:372
  47.5 12.7 %copy-start.11 = (bf16[1,512,768]{2,1,0:T(8,128)(2,1)S(1)}, bf16[1,512,768]{2,1,0:T(8,128)(2,1)}, u32[]{:S(2)}) copy-start(bf16[1,512,768]{2,1,0:T(8,128)(2,1)} %param.8) | copy-start | bytes 2359300
  47.5 11.2 %collective-permute-start.9 = (bf16[2,128,512]{2,1,0:T(8,128)(2,1)S(1)}, bf16[2,128,512]{2,1,0:T(8,128)(2,1)S(1)}, u32[]{:S(2)}, u32[]{:S(2)}) collective-permute-start(bf16[2,128,512]{2,1,0:T(8,128)(2,1)S(1)} %get-tuple-element.73), channel_id=1, source_target_pairs={{0,1},{1,0},{2,3},{3,2},{4,5},{5,4},{6,7},{7,6},{8,9},{9,8},{10,11... | collective-permute-start | bytes 786440 | tf_op jit(solution)/shard_map/ppermute | solution.py:372
  51.8 10.6 %collective-permute-start.15 = (bf16[2,128,512]{2,1,0:T(8,128)(2,1)S(1)}, bf16[2,128,512]{2,1,0:T(8,128)(2,1)S(1)}, u32[]{:S(2)}, u32[]{:S(2)}) collective-permute-start(bf16[2,128,512]{2,1,0:T(8,128)(2,1)S(1)} %get-tuple-element.83), channel_id=1, source_target_pairs={{0,3},{1,2},{2,1},{3,0},{4,7},{5,6},{6,5},{7,4},{8,11},{9,10},{10,... | collective-permute-start | bytes 786440 | tf_op jit(solution)/shard_map/ppermute | solution.py:372
  56.6 11.0 %collective-permute-start.14 = (bf16[2,128,512]{2,1,0:T(8,128)(2,1)S(1)}, bf16[2,128,512]{2,1,0:T(8,128)(2,1)S(1)}, u32[]{:S(2)}, u32[]{:S(2)}) collective-permute-start(bf16[2,128,512]{2,1,0:T(8,128)(2,1)S(1)} %get-tuple-element.81), channel_id=1, source_target_pairs={{0,2},{1,3},{2,0},{3,1},{4,6},{5,7},{6,4},{7,5},{8,10},{9,11},{10,... | collective-permute-start | bytes 786440 | tf_op jit(solution)/shard_map/ppermute | solution.py:372
  58.7 9.2 %collective-permute-start.13 = (bf16[2,128,512]{2,1,0:T(8,128)(2,1)S(1)}, bf16[2,128,512]{2,1,0:T(8,128)(2,1)S(1)}, u32[]{:S(2)}, u32[]{:S(2)}) collective-permute-start(bf16[2,128,512]{2,1,0:T(8,128)(2,1)S(1)} %get-tuple-element.79), channel_id=1, source_target_pairs={{0,1},{1,0},{2,3},{3,2},{4,5},{5,4},{6,7},{7,6},{8,9},{9,8},{10,11... | collective-permute-start | bytes 786440 | tf_op jit(solution)/shard_map/ppermute | solution.py:372
  86.2 17.0 %collective-permute-start.16 = (bf16[2,128,512]{2,1,0:T(8,128)(2,1)}, bf16[2,128,512]{2,1,0:T(8,128)(2,1)S(1)}, u32[]{:S(2)}, u32[]{:S(2)}) collective-permute-start(bf16[2,128,512]{2,1,0:T(8,128)(2,1)} %get-tuple-element.84), channel_id=1, source_target_pairs={{0,1},{1,0},{2,3},{3,2},{4,5},{5,4},{6,7},{7,6},{8,9},{9,8},{10,11... | collective-permute-start | bytes 786440 | tf_op jit(solution)/shard_map/ppermute | solution.py:372
  87.8 13.9 %collective-permute-start.19 = (bf16[2,128,512]{2,1,0:T(8,128)(2,1)}, bf16[2,128,512]{2,1,0:T(8,128)(2,1)S(1)}, u32[]{:S(2)}, u32[]{:S(2)}) collective-permute-start(bf16[2,128,512]{2,1,0:T(8,128)(2,1)} %get-tuple-element.96), channel_id=1, source_target_pairs={{0,2},{1,3},{2,0},{3,1},{4,6},{5,7},{6,4},{7,5},{8,10},{9,11},{10,... | collective-permute-start | bytes 786440 | tf_op jit(solution)/shard_map/ppermute | solution.py:372
  89.3 13.8 %collective-permute-start.22 = (bf16[2,128,512]{2,1,0:T(8,128)(2,1)}, bf16[2,128,512]{2,1,0:T(8,128)(2,1)S(1)}, u32[]{:S(2)}, u32[]{:S(2)}) collective-permute-start(bf16[2,128,512]{2,1,0:T(8,128)(2,1)} %get-tuple-element.101), channel_id=1, source_target_pairs={{0,3},{1,2},{2,1},{3,0},{4,7},{5,6},{6,5},{7,4},{8,11},{9,10},{10,... | collective-permute-start | bytes 786440 | tf_op jit(solution)/shard_map/ppermute | solution.py:372
  91.9 11.2 %copy-start.27 = (bf16[2,128,512]{2,1,0:T(8,128)(2,1)S(1)}, bf16[2,128,512]{2,1,0:T(8,128)(2,1)}, u32[]{:S(2)}) copy-start(bf16[2,128,512]{2,1,0:T(8,128)(2,1)} %get-tuple-element.102) | copy-start | bytes 786436
  91.9 11.3 %copy-start.25 = (bf16[2,128,512]{2,1,0:T(8,128)(2,1)S(1)}, bf16[2,128,512]{2,1,0:T(8,128)(2,1)}, u32[]{:S(2)}) copy-start(bf16[2,128,512]{2,1,0:T(8,128)(2,1)} %get-tuple-element.92) | copy-start | bytes 786436
  91.9 13.3 %copy-start.9 = (bf16[2,128,512]{2,1,0:T(8,128)(2,1)S(1)}, bf16[2,128,512]{2,1,0:T(8,128)(2,1)}, u32[]{:S(2)}) copy-start(bf16[2,128,512]{2,1,0:T(8,128)(2,1)} %get-tuple-element.107.refs_0_) | copy-start | bytes 786436
  93.6 20.5 %copy-start.23 = (bf16[2,128,512]{2,1,0:T(8,128)(2,1)S(1)}, bf16[2,128,512]{2,1,0:T(8,128)(2,1)}, u32[]{:S(2)}) copy-start(bf16[2,128,512]{2,1,0:T(8,128)(2,1)} %get-tuple-element.98) | copy-start | bytes 786436
  93.6 22.2 %copy-start.22 = (bf16[2,128,512]{2,1,0:T(8,128)(2,1)S(1)}, bf16[2,128,512]{2,1,0:T(8,128)(2,1)}, u32[]{:S(2)}) copy-start(bf16[2,128,512]{2,1,0:T(8,128)(2,1)} %get-tuple-element.103) | copy-start | bytes 786436
  93.6 22.9 %copy-start.21 = (bf16[2,128,512]{2,1,0:T(8,128)(2,1)S(1)}, bf16[2,128,512]{2,1,0:T(8,128)(2,1)}, u32[]{:S(2)}) copy-start(bf16[2,128,512]{2,1,0:T(8,128)(2,1)} %get-tuple-element.93) | copy-start | bytes 786436
  93.6 24.0 %copy-start.10 = (bf16[2,128,512]{2,1,0:T(8,128)(2,1)S(1)}, bf16[2,128,512]{2,1,0:T(8,128)(2,1)}, u32[]{:S(2)}) copy-start(bf16[2,128,512]{2,1,0:T(8,128)(2,1)} %get-tuple-element.106.refs_0_) | copy-start | bytes 786436
  101.7 12.4 %collective-permute-start.20 = (bf16[2,128,512]{2,1,0:T(8,128)(2,1)S(1)}, bf16[2,128,512]{2,1,0:T(8,128)(2,1)S(1)}, u32[]{:S(2)}, u32[]{:S(2)}) collective-permute-start(bf16[2,128,512]{2,1,0:T(8,128)(2,1)S(1)} %copy-done.28), channel_id=1, source_target_pairs={{0,2},{1,3},{2,0},{3,1},{4,6},{5,7},{6,4},{7,5},{8,10},{9,11},{10,... | collective-permute-start | bytes 786440 | tf_op jit(solution)/shard_map/ppermute | solution.py:372
  103.1 12.7 %collective-permute-start.23 = (bf16[2,128,512]{2,1,0:T(8,128)(2,1)S(1)}, bf16[2,128,512]{2,1,0:T(8,128)(2,1)S(1)}, u32[]{:S(2)}, u32[]{:S(2)}) collective-permute-start(bf16[2,128,512]{2,1,0:T(8,128)(2,1)S(1)} %copy-done.27), channel_id=1, source_target_pairs={{0,3},{1,2},{2,1},{3,0},{4,7},{5,6},{6,5},{7,4},{8,11},{9,10},{10,... | collective-permute-start | bytes 786440 | tf_op jit(solution)/shard_map/ppermute | solution.py:372
  103.2 13.4 %collective-permute-start.17 = (bf16[2,128,512]{2,1,0:T(8,128)(2,1)S(1)}, bf16[2,128,512]{2,1,0:T(8,128)(2,1)S(1)}, u32[]{:S(2)}, u32[]{:S(2)}) collective-permute-start(bf16[2,128,512]{2,1,0:T(8,128)(2,1)S(1)} %copy-done.25), channel_id=1, source_target_pairs={{0,1},{1,0},{2,3},{3,2},{4,5},{5,4},{6,7},{7,6},{8,9},{9,8},{10,11... | collective-permute-start | bytes 786440 | tf_op jit(solution)/shard_map/ppermute | solution.py:372
  106.2 12.3 %collective-permute-start.26 = (bf16[4,128,512]{2,1,0:T(8,128)(2,1)S(1)}, bf16[4,128,512]{2,1,0:T(8,128)(2,1)S(1)}, u32[]{:S(2)}, u32[]{:S(2)}) collective-permute-start(bf16[4,128,512]{2,1,0:T(8,128)(2,1)S(1)} %owner_sum.6), channel_id=1, source_target_pairs={{0,4},{1,5},{2,6},{3,7},{4,0},{5,1},{6,2},{7,3},{8,12},{9,13},{10,... | collective-permute-start | bytes 1572872 | tf_op jit(solution)/shard_map/ppermute | solution.py:361
  114.1 12.8 %collective-permute-start.21 = (bf16[2,128,512]{2,1,0:T(8,128)(2,1)S(1)}, bf16[2,128,512]{2,1,0:T(8,128)(2,1)S(1)}, u32[]{:S(2)}, u32[]{:S(2)}) collective-permute-start(bf16[2,128,512]{2,1,0:T(8,128)(2,1)S(1)} %copy-done.23), channel_id=1, source_target_pairs={{0,2},{1,3},{2,0},{3,1},{4,6},{5,7},{6,4},{7,5},{8,10},{9,11},{10,... | collective-permute-start | bytes 786440 | tf_op jit(solution)/shard_map/ppermute | solution.py:372
  115.9 11.0 %collective-permute-start.24 = (bf16[2,128,512]{2,1,0:T(8,128)(2,1)S(1)}, bf16[2,128,512]{2,1,0:T(8,128)(2,1)S(1)}, u32[]{:S(2)}, u32[]{:S(2)}) collective-permute-start(bf16[2,128,512]{2,1,0:T(8,128)(2,1)S(1)} %copy-done.22), channel_id=1, source_target_pairs={{0,3},{1,2},{2,1},{3,0},{4,7},{5,6},{6,5},{7,4},{8,11},{9,10},{10,... | collective-permute-start | bytes 786440 | tf_op jit(solution)/shard_map/ppermute | solution.py:372
  116.6 11.7 %collective-permute-start.18 = (bf16[2,128,512]{2,1,0:T(8,128)(2,1)S(1)}, bf16[2,128,512]{2,1,0:T(8,128)(2,1)S(1)}, u32[]{:S(2)}, u32[]{:S(2)}) collective-permute-start(bf16[2,128,512]{2,1,0:T(8,128)(2,1)S(1)} %copy-done.21), channel_id=1, source_target_pairs={{0,1},{1,0},{2,3},{3,2},{4,5},{5,4},{6,7},{7,6},{8,9},{9,8},{10,11... | collective-permute-start | bytes 786440 | tf_op jit(solution)/shard_map/ppermute | solution.py:372
  118.6 12.2 %copy-start.18 = (bf16[2,128,512]{2,1,0:T(8,128)(2,1)S(1)}, bf16[2,128,512]{2,1,0:T(8,128)(2,1)}, u32[]{:S(2)}) copy-start(bf16[2,128,512]{2,1,0:T(8,128)(2,1)} %get-tuple-element.118) | copy-start | bytes 786436
  118.7 23.2 %copy-start.7 = (bf16[2,128,512]{2,1,0:T(8,128)(2,1)S(1)}, bf16[2,128,512]{2,1,0:T(8,128)(2,1)}, u32[]{:S(2)}) copy-start(bf16[2,128,512]{2,1,0:T(8,128)(2,1)} %get-tuple-element.104.refs_0_) | copy-start | bytes 786436
  118.7 25.7 %collective-permute-start.31 = (bf16[4,128,512]{2,1,0:T(8,128)(2,1)S(1)}, bf16[4,128,512]{2,1,0:T(8,128)(2,1)S(1)}, u32[]{:S(2)}, u32[]{:S(2)}) collective-permute-start(bf16[4,128,512]{2,1,0:T(8,128)(2,1)S(1)} %add_convert_fusion), channel_id=1, source_target_pairs={{0,24},{1,25},{2,26},{3,27},{4,28},{5,29},{6,30},{7,31},{8,16},{9,... | collective-permute-start | bytes 1572872 | tf_op jit(solution)/shard_map/ppermute | solution.py:361
  129.0 15.4 %copy-start.1 = (bf16[768,256]{1,0:T(8,128)(2,1)S(1)}, bf16[768,256]{1,0:T(8,128)(2,1)}, u32[]{:S(2)}) copy-start(bf16[768,256]{1,0:T(8,128)(2,1)} %refs_3_.3) | copy-start | bytes 1179652
  129.0 15.4 %copy-start.2 = (bf16[768,256]{1,0:T(8,128)(2,1)S(1)}, bf16[768,256]{1,0:T(8,128)(2,1)}, u32[]{:S(2)}) copy-start(bf16[768,256]{1,0:T(8,128)(2,1)} %refs_4_.1) | copy-start | bytes 1179652
  129.1 9.0 %collective-permute-start.27 = (bf16[2,128,512]{2,1,0:T(8,128)(2,1)S(1)}, bf16[2,128,512]{2,1,0:T(8,128)(2,1)S(1)}, u32[]{:S(2)}, u32[]{:S(2)}) collective-permute-start(bf16[2,128,512]{2,1,0:T(8,128)(2,1)S(1)} %copy-done.20), channel_id=1, source_target_pairs={{0,1},{1,0},{2,3},{3,2},{4,5},{5,4},{6,7},{7,6},{8,9},{9,8},{10,11... | collective-permute-start | bytes 786440 | tf_op jit(solution)/shard_map/ppermute | solution.py:372
  129.7 10.4 %collective-permute-start.28 = (bf16[2,128,512]{2,1,0:T(8,128)(2,1)S(1)}, bf16[2,128,512]{2,1,0:T(8,128)(2,1)S(1)}, u32[]{:S(2)}, u32[]{:S(2)}) collective-permute-start(bf16[2,128,512]{2,1,0:T(8,128)(2,1)S(1)} %copy-done.19), channel_id=1, source_target_pairs={{0,2},{1,3},{2,0},{3,1},{4,6},{5,7},{6,4},{7,5},{8,10},{9,11},{10,... | collective-permute-start | bytes 786440 | tf_op jit(solution)/shard_map/ppermute | solution.py:372
  130.9 11.0 %collective-permute-start.29 = (bf16[2,128,512]{2,1,0:T(8,128)(2,1)S(1)}, bf16[2,128,512]{2,1,0:T(8,128)(2,1)S(1)}, u32[]{:S(2)}, u32[]{:S(2)}) collective-permute-start(bf16[2,128,512]{2,1,0:T(8,128)(2,1)S(1)} %copy-done.18), channel_id=1, source_target_pairs={{0,3},{1,2},{2,1},{3,0},{4,7},{5,6},{6,5},{7,4},{8,11},{9,10},{10,... | collective-permute-start | bytes 786440 | tf_op jit(solution)/shard_map/ppermute | solution.py:372
  132.6 22.9 %collective-permute-start.25 = (bf16[4,128,512]{2,1,0:T(8,128)(2,1)S(1)}, bf16[4,128,512]{2,1,0:T(8,128)(2,1)S(1)}, u32[]{:S(2)}, u32[]{:S(2)}) collective-permute-start(bf16[4,128,512]{2,1,0:T(8,128)(2,1)S(1)} %owner_sum.4), channel_id=1, source_target_pairs={{0,20},{1,21},{2,22},{3,23},{4,16},{5,17},{6,18},{7,19},{8,28},{9,... | collective-permute-start | bytes 1572872 | tf_op jit(solution)/shard_map/ppermute | solution.py:361
  142.7 12.8 %collective-permute-start.30 = (bf16[4,128,512]{2,1,0:T(8,128)(2,1)S(1)}, bf16[4,128,512]{2,1,0:T(8,128)(2,1)S(1)}, u32[]{:S(2)}, u32[]{:S(2)}) collective-permute-start(bf16[4,128,512]{2,1,0:T(8,128)(2,1)S(1)} %owner_sum.7), channel_id=1, source_target_pairs={{0,16},{1,17},{2,18},{3,19},{4,20},{5,21},{6,22},{7,23},{8,24},{9,... | collective-permute-start | bytes 1572872 | tf_op jit(solution)/shard_map/ppermute | solution.py:361
  (18 other events, 108.0 us)

commit v15 on v13

--- a/solution.py
+++ b/solution.py
@@ -101,6 +101,8 @@
         start(fetch, len(arrived), get_ref, 0, entries)
 
     first = step * per_step * list_len
+    for i in range(per_step * list_len):
+        fetch(first + i, 0, 0).wait()
     pairs = range(KV // PAIR)
     keys, values, wide, scores, exact, scales, grads, overlap, prob_grads = (
         {} for _ in range(9)
@@ -111,11 +113,9 @@
         return pl.ds(pl.multiple_of((step * per_step + b) * size, size), size)
 
     def cols_at(b):
-        return pl.ds(pl.multiple_of((step * per_step + b) * BLK, BLK), BLK)
+        return slice(b * BLK, (b + 1) * BLK)
 
     def score(b):
-        for i in range(list_len):
-            fetch(first + b * list_len + i, 0, 0).wait()
         here = rows_at(b)
         queries = q_ref[:, cols_at(b)] * jnp.asarray(TEMPER, BF16)
         for j in pairs:
@@ -176,19 +176,16 @@
         parts_scr[here, j * PAIR : (j + 1) * PAIR] = key_part.astype(BF16)
         parts_scr[here, KV + j * PAIR : KV + (j + 1) * PAIR] = value_part.astype(BF16)
 
-    score(0)
+    for b in range(per_step):
+        score(b)
     for j in pairs:
         soften(0, j)
-    if per_step > 1:
-        score(1)
     normalise(0)
     for b in range(per_step):
         for j in pairs:
             regrade(b, j)
             if b + 1 < per_step:
                 soften(b + 1, j)
-        if b + 2 < per_step:
-            score(b + 2)
         for j in pairs:
             finish_pair(b, j)
             if b + 1 < per_step and j == 0:
@@ -205,9 +202,9 @@
     width, rows = queries.shape
     blocks = rows // BLK
     entries = blocks * list_len
-    resident = list_len <= 4
-    per_step = 1
-    place = WHOLE if resident else pl.BlockSpec(memory_space=pl.ANY)
+    per_step = 2 if list_len <= 4 and blocks % 2 == 0 else 1
+    row_spec = pl.BlockSpec((width, per_step * BLK), lambda r, g, p: (0, r))
+    anywhere = pl.BlockSpec(memory_space=pl.ANY)
     keys = list_len * BLK
     pairs = HEADS * rows * keys
     return pl.pallas_call(
@@ -215,8 +212,8 @@
         grid_spec=pltpu.PrefetchScalarGridSpec(
             num_scalar_prefetch=2,
             grid=(blocks // per_step,),
-            in_specs=[WHOLE] * 2 + [place] * len(arrived),
-            out_specs=[WHOLE] * 2 + [place] * len(back_shapes),
+            in_specs=[row_spec, row_spec] + [anywhere] * len(arrived),
+            out_specs=[row_spec, row_spec] + [anywhere] * len(back_shapes),
             scratch_shapes=[
                 pltpu.VMEM((per_step, KV // PAIR, keys, 2 * GROUP * BLK), BF16),
                 pltpu.VMEM((entries * BLK, 2 * KV), BF16),
@@ -227,7 +224,7 @@
         ),
         out_shape=[jax.ShapeDtypeStruct((width, rows), BF16)] * 2
         + [jax.ShapeDtypeStruct(shape, BF16) for shape in back_shapes],
-        compiler_params=params(40 if resident else 56),
+        compiler_params=params(56),
         cost_estimate=pl.CostEstimate(
             flops=12 * pairs * HEAD_DIM, bytes_accessed=16 * rows * width, transcendentals=pairs
         ),

time: 163 us -> 155 us (0.951)
  local copies, waits for them, and re-layouts: 12.5 us -> 5.16 us
  Pallas kernels: 36.8 us -> 29.7 us
  matrix products: 6.81 us -> 10.2 us
  waiting for transfers between devices: 59.1 us -> 62 us
    ppermute x8, waiting for transfers between devices: 18.3 us -> 27.2 us  [swap(): return lax.ppermute(value, ('vintage', 'tile'), pairs)]
    unnamed x72 -> x62, local copies, waits for them, and re-layouts: 8.33 us -> 1.01 us
    pallas_call x1, Pallas kernels: 24.4 us -> 17.3 us  [attention(): pl.pallas_call(functools.partial(attention_kernel, list_len, per_step, le...]
    ppermute x24, waiting for transfers between devices: 40.7 us -> 34.8 us  [spread(): moved.append(lax.ppermute(value, 'tile', pairs))]
    ppermute x8, starting transfers between devices: 6 us -> 7.69 us  [swap(): return lax.ppermute(value, ('vintage', 'tile'), pairs)]
  transfers between devices with their start and end apart: 32 -> 32, of which waited for: 16 -> 14; matrix products, arithmetic and copies ran while one was open for 10% -> 13% of each run, Pallas kernels for 5% -> 5%
where the time goes in v15:
time: 155 us
  waiting for transfers between devices  62 us (40%)
  starting transfers between devices  40.7 us (26%)
  Pallas kernels  29.7 us (19%)
  matrix products  10.2 us (7%)
  other arithmetic  6.22 us (4%)
  local copies, waits for them, and re-layouts  5.16 us (3%)
    ppermute x24, waiting for transfers between devices, spread(): moved.append(lax.ppermute(value, 'tile', pairs))  34.8 us
    ppermute x24, starting transfers between devices, spread(): moved.append(lax.ppermute(value, 'tile', pairs))  33 us
    ppermute x8, waiting for transfers between devices, swap(): return lax.ppermute(value, ('vintage', 'tile'), pairs)  27.2 us
    pallas_call x1, Pallas kernels, attention(): pl.pallas_call(functools.partial(attention_kernel, list_len, per_step, le...  17.3 us
    ppermute x8, starting transfers between devices, swap(): return lax.ppermute(value, ('vintage', 'tile'), pairs)  7.69 us
    dot_general x1, matrix products, dot_nt(): lax.dot_general(a, b, (((1,), (1,)), ((), ())), preferred_element_type=F32)  3.54 us
    pallas_call x1, Pallas kernels, project(): pl.pallas_call(project_kernel, in_specs=[pl.BlockSpec(memory_space=pl.ANY...  3.4 us
    dot_general x1, matrix products, shards(): lax.dot_general(query_grad, w_query, (((0,), (1,)), ((), ())), preferred_...  3.28 us
  transfers between devices with their start and end apart: 32, of which 14 were waited for; matrix products, arithmetic and copies ran while one was open for 13% of the time, Pallas kernels for 5%

profile of v15, /device:TPU:0, one launch (start us, length us, event | category | flops | bytes accessed | tf_op | source)
XLA Modules:
  0.0 155.0 jit_solution(15407498961252313164)
XLA Ops:
  0.7 3.4 %project.1 = bf16[512,512]{1,0:T(8,128)(2,1)} custom-call(bf16[512,768]{1,0:T(8,128)(2,1)} %bitcast.60, bf16[768,256]{1,0:T(8,128)(2,1)} %refs_2_.3, bf16[768,256]{1,0:T(8,128)(2,1)} %refs_3_.3), custom_call_target="tpu_custom_call" | custom-call | tf_op jit(solution)/shard_map/project/pallas_call | solution.py:258
  4.1 2.5 %collective-permute-start.4 = (bf16[4,128,512]{2,1,0:T(8,128)(2,1)}, bf16[4,128,512]{2,1,0:T(8,128)(2,1)S(1)}, u32[]{:S(2)}, u32[]{:S(2)}) collective-permute-start(bf16[4,128,512]{2,1,0:T(8,128)(2,1)} %bitcast.61), channel_id=1, source_target_pairs={{0,20},{1,21},{2,22},{3,23},{4,16},{5,17},{6,18},{7,19},{8,28},{9,... | collective-permute-start | bytes 1572872 | tf_op jit(solution)/shard_map/ppermute | solution.py:359
  8.8 0.8 convert_reduce_fusion
  10.4 2.3 %collective-permute-start.8 = (bf16[4,128,512]{2,1,0:T(8,128)(2,1)}, bf16[4,128,512]{2,1,0:T(8,128)(2,1)S(1)}, u32[]{:S(2)}, u32[]{:S(2)}) collective-permute-start(bf16[4,128,512]{2,1,0:T(8,128)(2,1)} %bitcast.63), channel_id=1, source_target_pairs={{0,24},{1,25},{2,26},{3,27},{4,28},{5,29},{6,30},{7,31},{8,16},{9,... | collective-permute-start | bytes 1572872 | tf_op jit(solution)/shard_map/ppermute | solution.py:359
  14.1 2.5 %collective-permute-start.3 = (bf16[2,128,512]{2,1,0:T(8,128)(2,1)S(1)}, bf16[2,128,512]{2,1,0:T(8,128)(2,1)S(1)}, u32[]{:S(2)}, u32[]{:S(2)}) collective-permute-start(bf16[2,128,512]{2,1,0:T(8,128)(2,1)S(1)} %get-tuple-element.57), channel_id=1, source_target_pairs={{0,3},{1,2},{2,1},{3,0},{4,7},{5,6},{6,5},{7,4},{8,11},{9,10},{10,... | collective-permute-start | bytes 786440 | tf_op jit(solution)/shard_map/ppermute | solution.py:370
  17.7 8.3 %collective-permute-done.4.tile_ref.refs_4_ = bf16[4,128,512]{2,1,0:T(8,128)(2,1)S(1)} collective-permute-done((bf16[4,128,512]{2,1,0:T(8,128)(2,1)}, bf16[4,128,512]{2,1,0:T(8,128)(2,1)S(1)}, u32[]{:S(2)}, u32[]{:S(2)}) %collective-permute-start.4) | collective-permute-done | bytes 524320 | tf_op jit(solution)/shard_map/ppermute | solution.py:359
  26.0 1.4 pack.5
  27.4 3.9 %collective-permute-start.7 = (bf16[2,128,512]{2,1,0:T(8,128)(2,1)}, bf16[2,128,512]{2,1,0:T(8,128)(2,1)}, u32[]{:S(2)}, u32[]{:S(2)}) collective-permute-start(bf16[2,128,512]{2,1,0:T(8,128)(2,1)} %get-tuple-element.63), channel_id=1, source_target_pairs={{0,3},{1,2},{2,1},{3,0},{4,7},{5,6},{6,5},{7,4},{8,11},{9,10},{10,... | collective-permute-start | bytes 786440 | tf_op jit(solution)/shard_map/ppermute | solution.py:370
  32.0 4.9 %collective-permute-done.8.tile_ref.refs_8_ = bf16[4,128,512]{2,1,0:T(8,128)(2,1)S(1)} collective-permute-done((bf16[4,128,512]{2,1,0:T(8,128)(2,1)}, bf16[4,128,512]{2,1,0:T(8,128)(2,1)S(1)}, u32[]{:S(2)}, u32[]{:S(2)}) %collective-permute-start.8) | collective-permute-done | bytes 524320 | tf_op jit(solution)/shard_map/ppermute | solution.py:359
  36.9 1.3 bitcast_select_fusion
  38.9 2.8 %collective-permute-start.11 = (bf16[2,128,512]{2,1,0:T(8,128)(2,1)S(1)}, bf16[2,128,512]{2,1,0:T(8,128)(2,1)S(1)}, u32[]{:S(2)}, u32[]{:S(2)}) collective-permute-start(bf16[2,128,512]{2,1,0:T(8,128)(2,1)S(1)} %get-tuple-element.71), channel_id=1, source_target_pairs={{0,3},{1,2},{2,1},{3,0},{4,7},{5,6},{6,5},{7,4},{8,11},{9,10},{10,... | collective-permute-start | bytes 786440 | tf_op jit(solution)/shard_map/ppermute | solution.py:370
  41.7 2.6 %collective-permute-done.6.refs_6_ = bf16[2,128,512]{2,1,0:T(8,128)(2,1)} collective-permute-done((bf16[2,128,512]{2,1,0:T(8,128)(2,1)}, bf16[2,128,512]{2,1,0:T(8,128)(2,1)}, u32[]{:S(2)}, u32[]{:S(2)}) %collective-permute-start.6) | collective-permute-done | bytes 262176 | tf_op jit(solution)/shard_map/ppermute | solution.py:370
  44.2 2.0 %collective-permute-start.10 = (bf16[2,128,512]{2,1,0:T(8,128)(2,1)S(1)}, bf16[2,128,512]{2,1,0:T(8,128)(2,1)S(1)}, u32[]{:S(2)}, u32[]{:S(2)}) collective-permute-start(bf16[2,128,512]{2,1,0:T(8,128)(2,1)S(1)} %get-tuple-element.69), channel_id=1, source_target_pairs={{0,2},{1,3},{2,0},{3,1},{4,6},{5,7},{6,4},{7,5},{8,10},{9,11},{10,... | collective-permute-start | bytes 786440 | tf_op jit(solution)/shard_map/ppermute | solution.py:370
  46.4 3.5 %fusion.ng_ref = f32[768,512]{1,0:T(8,128)} fusion(bf16[768,768]{1,0:T(8,128)(2,1)} %param.13, bf16[1,512,768]{2,1,0:T(8,128)(2,1)} %param.9), kind=kOutput, calls=%fused_computation.5 | convolution fusion | flops 603979776 | bytes 3538944 | tf_op jit(solution)/shard_map/dot_general | solution.py:34
  50.0 1.2 collective-permute-done.12.tile_ref.refs_12_
  51.8 2.5 %collective-permute-start.15 = (bf16[2,128,512]{2,1,0:T(8,128)(2,1)S(1)}, bf16[2,128,512]{2,1,0:T(8,128)(2,1)S(1)}, u32[]{:S(2)}, u32[]{:S(2)}) collective-permute-start(bf16[2,128,512]{2,1,0:T(8,128)(2,1)S(1)} %get-tuple-element.77), channel_id=1, source_target_pairs={{0,3},{1,2},{2,1},{3,0},{4,7},{5,6},{6,5},{7,4},{8,11},{9,10},{10,... | collective-permute-start | bytes 786440 | tf_op jit(solution)/shard_map/ppermute | solution.py:370
  54.3 0.8 collective-permute-done.10.refs_10_
  55.1 1.9 %collective-permute-start.14 = (bf16[2,128,512]{2,1,0:T(8,128)(2,1)S(1)}, bf16[2,128,512]{2,1,0:T(8,128)(2,1)S(1)}, u32[]{:S(2)}, u32[]{:S(2)}) collective-permute-start(bf16[2,128,512]{2,1,0:T(8,128)(2,1)S(1)} %get-tuple-element.75), channel_id=1, source_target_pairs={{0,2},{1,3},{2,0},{3,1},{4,6},{5,7},{6,4},{7,5},{8,10},{9,11},{10,... | collective-permute-start | bytes 786440 | tf_op jit(solution)/shard_map/ppermute | solution.py:370
  57.0 1.5 collective-permute-start.13
  58.5 1.7 %convolution_convert_fusion.1.q_ref = bf16[768,512]{1,0:T(8,128)(2,1)} fusion(bf16[768,768]{1,0:T(8,128)(2,1)S(1)} %copy-done, bf16[1,512,768]{2,1,0:T(8,128)(2,1)S(1)} %copy-done.11), kind=kOutput, calls=%fused_computation.3 | convolution fusion | flops 604372992 | bytes 2752512 | tf_op jit(solution)/shard_map/dot_general | solution.py:418
  60.2 1.8 %collective-permute-done.15.refs_15_ = bf16[2,128,512]{2,1,0:T(8,128)(2,1)S(1)} collective-permute-done((bf16[2,128,512]{2,1,0:T(8,128)(2,1)S(1)}, bf16[2,128,512]{2,1,0:T(8,128)(2,1)S(1)}, u32[]{:S(2)}, u32[]{:S(2)}) %collective-permute-start.15) | collective-permute-done | bytes 262176 | tf_op jit(solution)/shard_map/ppermute | solution.py:370
  62.0 4.3 %collective-permute-done.14.refs_14_ = bf16[2,128,512]{2,1,0:T(8,128)(2,1)S(1)} collective-permute-done((bf16[2,128,512]{2,1,0:T(8,128)(2,1)S(1)}, bf16[2,128,512]{2,1,0:T(8,128)(2,1)S(1)}, u32[]{:S(2)}, u32[]{:S(2)}) %collective-permute-start.14) | collective-permute-done | bytes 262176 | tf_op jit(solution)/shard_map/ppermute | solution.py:370
  67.4 17.3 %attention.1 = (bf16[768,512]{1,0:T(8,128)(2,1)}, bf16[768,512]{1,0:T(8,128)(2,1)}, bf16[2,128,512]{2,1,0:T(8,128)(2,1)}, bf16[2,128,512]{2,1,0:T(8,128)(2,1)}, ...) custom-call(s32[16]{0:T(128)} %get-tuple-element.126.get_ref, ...), custom_call_target="tpu_custom_call" | custom-call | flops 2415919104 | bytes 6291456 | tf_op jit(solution)/shard_map/attention/pallas_call | solution.py:210
  84.7 1.5 collective-permute-start.16
  86.2 1.6 %collective-permute-start.19 = (bf16[2,128,512]{2,1,0:T(8,128)(2,1)}, bf16[2,128,512]{2,1,0:T(8,128)(2,1)S(1)}, u32[]{:S(2)}, u32[]{:S(2)}) collective-permute-start(bf16[2,128,512]{2,1,0:T(8,128)(2,1)} %get-tuple-element.90), channel_id=1, source_target_pairs={{0,2},{1,3},{2,0},{3,1},{4,6},{5,7},{6,4},{7,5},{8,10},{9,11},{10,... | collective-permute-start | bytes 786440 | tf_op jit(solution)/shard_map/ppermute | solution.py:370
  88.7 3.3 %fusion.14.refs_1_ = f32[512,768]{1,0:T(8,128)} fusion(bf16[768,512]{1,0:T(8,128)(2,1)} %get-tuple-element.79, bf16[768,768]{1,0:T(8,128)(2,1)S(1)} %copy-done), kind=kOutput, calls=%fused_computation.52 | convolution fusion | flops 603979776 | bytes 3538944 | tf_op jit(solution)/shard_map/dot_general | solution.py:430
  92.0 1.7 %convolution_convert_fusion = bf16[512,768]{1,0:T(8,128)(2,1)} fusion(bf16[768,512]{1,0:T(8,128)(2,1)S(1)} %copy-done.29, bf16[768,768]{1,0:T(8,128)(2,1)S(1)} %copy-done.19), kind=kOutput, calls=%fused_computation.2 | convolution fusion | flops 604372992 | bytes 2752512 | tf_op jit(solution)/shard_map/dot_general | solution.py:38
  93.7 6.3 %collective-permute-done.19.refs_2_ = bf16[2,128,512]{2,1,0:T(8,128)(2,1)S(1)} collective-permute-done((bf16[2,128,512]{2,1,0:T(8,128)(2,1)}, bf16[2,128,512]{2,1,0:T(8,128)(2,1)S(1)}, u32[]{:S(2)}, u32[]{:S(2)}) %collective-permute-start.19) | collective-permute-done | bytes 262176 | tf_op jit(solution)/shard_map/ppermute | solution.py:370
  100.0 1.5 collective-permute-start.20
  101.7 1.8 %collective-permute-start.17 = (bf16[2,128,512]{2,1,0:T(8,128)(2,1)}, bf16[2,128,512]{2,1,0:T(8,128)(2,1)S(1)}, u32[]{:S(2)}, u32[]{:S(2)}) collective-permute-start(bf16[2,128,512]{2,1,0:T(8,128)(2,1)} %get-tuple-element.86), channel_id=1, source_target_pairs={{0,1},{1,0},{2,3},{3,2},{4,5},{5,4},{6,7},{7,6},{8,9},{9,8},{10,11... | collective-permute-start | bytes 786440 | tf_op jit(solution)/shard_map/ppermute | solution.py:370
  103.5 1.0 owner_sum.4
  104.4 1.1 collective-permute-start.26
  105.8 6.9 %collective-permute-done.20.refs_2_ = bf16[2,128,512]{2,1,0:T(8,128)(2,1)S(1)} collective-permute-done((bf16[2,128,512]{2,1,0:T(8,128)(2,1)}, bf16[2,128,512]{2,1,0:T(8,128)(2,1)S(1)}, u32[]{:S(2)}, u32[]{:S(2)}) %collective-permute-start.20) | collective-permute-done | bytes 262176 | tf_op jit(solution)/shard_map/ppermute | solution.py:370
  112.7 1.7 %collective-permute-start.21 = (bf16[2,128,512]{2,1,0:T(8,128)(2,1)}, bf16[2,128,512]{2,1,0:T(8,128)(2,1)S(1)}, u32[]{:S(2)}, u32[]{:S(2)}) collective-permute-start(bf16[2,128,512]{2,1,0:T(8,128)(2,1)} %get-tuple-element.92), channel_id=1, source_target_pairs={{0,2},{1,3},{2,0},{3,1},{4,6},{5,7},{6,4},{7,5},{8,10},{9,11},{10,... | collective-permute-start | bytes 786440 | tf_op jit(solution)/shard_map/ppermute | solution.py:370
  114.5 0.8 collective-permute-start.24
  115.2 1.0 collective-permute-start.18
  116.2 0.8 owner_sum.3
  117.0 6.8 %collective-permute-done.26 = bf16[4,128,512]{2,1,0:T(8,128)(2,1)} collective-permute-done((bf16[4,128,512]{2,1,0:T(8,128)(2,1)S(1)}, bf16[4,128,512]{2,1,0:T(8,128)(2,1)}, u32[]{:S(2)}, u32[]{:S(2)}) %collective-permute-start.26) | collective-permute-done | bytes 524320 | tf_op jit(solution)/shard_map/ppermute | solution.py:359
  123.9 2.0 %add_convert_fusion = bf16[4,128,512]{2,1,0:T(8,128)(2,1)} fusion(f32[4,128,512]{2,1,0:T(8,128)S(1)} %owner_sum.3, bf16[4,128,512]{2,1,0:T(8,128)(2,1)} %collective-permute-done.26), kind=kLoop, calls=%fused_computation.4 | loop fusion | flops 786432 | bytes 2097152 | tf_op jit(solution)/shard_map/convert_element_type | solution.py:439
  125.9 2.1 %fusion.13 = (bf16[2,128,512]{2,1,0:T(8,128)(2,1)S(1)}, bf16[2,128,512]{2,1,0:T(8,128)(2,1)}, bf16[2,128,512]{2,1,0:T(8,128)(2,1)}, bf16[2,128,512]{2,1,0:T(8,128)(2,1)S(1)}) fusion(bf16[8,128,512]{2,1,0:T(8,128)(2,1)} %collective-permute-done.25), kind=kLoop, calls=%fused_computation.51 | loop fusion | bytes 2097152 | tf_op jit(solution)/shard_map/slice | solution.py:441
  128.0 1.7 %collective-permute-start.27 = (bf16[2,128,512]{2,1,0:T(8,128)(2,1)}, bf16[2,128,512]{2,1,0:T(8,128)(2,1)S(1)}, u32[]{:S(2)}, u32[]{:S(2)}) collective-permute-start(bf16[2,128,512]{2,1,0:T(8,128)(2,1)} %get-tuple-element.102), channel_id=1, source_target_pairs={{0,1},{1,0},{2,3},{3,2},{4,5},{5,4},{6,7},{7,6},{8,9},{9,8},{10,11... | collective-permute-start | bytes 786440 | tf_op jit(solution)/shard_map/ppermute | solution.py:370
  129.7 1.5 collective-permute-start.28
  132.6 4.1 %collective-permute-done.27.refs_5_ = bf16[2,128,512]{2,1,0:T(8,128)(2,1)S(1)} collective-permute-done((bf16[2,128,512]{2,1,0:T(8,128)(2,1)}, bf16[2,128,512]{2,1,0:T(8,128)(2,1)S(1)}, u32[]{:S(2)}, u32[]{:S(2)}) %collective-permute-start.27) | collective-permute-done | bytes 262176 | tf_op jit(solution)/shard_map/ppermute | solution.py:370
  136.7 7.7 %collective-permute-done.28.refs_6_ = bf16[2,128,512]{2,1,0:T(8,128)(2,1)S(1)} collective-permute-done((bf16[2,128,512]{2,1,0:T(8,128)(2,1)}, bf16[2,128,512]{2,1,0:T(8,128)(2,1)S(1)}, u32[]{:S(2)}, u32[]{:S(2)}) %collective-permute-start.28) | collective-permute-done | bytes 262176 | tf_op jit(solution)/shard_map/ppermute | solution.py:370
  144.4 0.9 owner_sum.5
  145.9 5.9 %collective-permute-done.31 = bf16[4,128,512]{2,1,0:T(8,128)(2,1)} collective-permute-done((bf16[4,128,512]{2,1,0:T(8,128)(2,1)}, bf16[4,128,512]{2,1,0:T(8,128)(2,1)}, u32[]{:S(2)}, u32[]{:S(2)}) %collective-permute-start.31) | collective-permute-done | bytes 524320 | tf_op jit(solution)/shard_map/ppermute | solution.py:359
  151.9 1.6 %finish.2.refs_1_ = f32[512,768]{1,0:T(8,128)S(1)} custom-call(bf16[512,512]{1,0:T(8,128)(2,1)} %bitcast.20.refs_0_, f32[512,768]{1,0:T(8,128)S(1)} %copy-done.9, bf16[768,256]{1,0:T(8,128)(2,1)S(1)} %copy-done.1, bf16[768,256]{1,0:T(8,128)(2,1)S(1)} %copy-done.2), custom_call_target="tpu_custom_call" | custom-call | flops 20000000000 | bytes 1572864 | tf_op jit(solution)/shard_map/finish/pallas_call | solution.py:299
  153.5 1.5 finish.3
  (120 shorter events, 11.8 us)
Async XLA Ops:
  0.6 57.9 %copy-start = (bf16[768,768]{1,0:T(8,128)(2,1)S(1)}, bf16[768,768]{1,0:T(8,128)(2,1)}, u32[]{:S(2)}) copy-start(bf16[768,768]{1,0:T(8,128)(2,1)} %param.10) | copy-start | bytes 3538948
  4.1 21.9 %collective-permute-start.4 = (bf16[4,128,512]{2,1,0:T(8,128)(2,1)}, bf16[4,128,512]{2,1,0:T(8,128)(2,1)S(1)}, u32[]{:S(2)}, u32[]{:S(2)}) collective-permute-start(bf16[4,128,512]{2,1,0:T(8,128)(2,1)} %bitcast.61), channel_id=1, source_target_pairs={{0,20},{1,21},{2,22},{3,23},{4,16},{5,17},{6,18},{7,19},{8,28},{9,... | collective-permute-start | bytes 1572872 | tf_op jit(solution)/shard_map/ppermute | solution.py:359
  6.6 3.8 %collective-permute-start = (bf16[4,128,512]{2,1,0:T(8,128)(2,1)}, bf16[4,128,512]{2,1,0:T(8,128)(2,1)S(1)}, u32[]{:S(2)}, u32[]{:S(2)}) collective-permute-start(bf16[4,128,512]{2,1,0:T(8,128)(2,1)} %bitcast.62), channel_id=1, source_target_pairs={{0,16},{1,17},{2,18},{3,19},{4,20},{5,21},{6,22},{7,23},{8,24},{9,... | collective-permute-start | bytes 1572872 | tf_op jit(solution)/shard_map/ppermute | solution.py:359
  10.4 39.6 %copy-start.4 = (bf16[4,128,512]{2,1,0:T(8,128)(2,1)}, bf16[4,128,512]{2,1,0:T(8,128)(2,1)S(1)}, u32[]{:S(2)}) copy-start(bf16[4,128,512]{2,1,0:T(8,128)(2,1)S(1)} %collective-permute-done.tile_ref.refs_0_) | copy-start | bytes 1572868
  10.4 26.4 %collective-permute-start.8 = (bf16[4,128,512]{2,1,0:T(8,128)(2,1)}, bf16[4,128,512]{2,1,0:T(8,128)(2,1)S(1)}, u32[]{:S(2)}, u32[]{:S(2)}) collective-permute-start(bf16[4,128,512]{2,1,0:T(8,128)(2,1)} %bitcast.63), channel_id=1, source_target_pairs={{0,24},{1,25},{2,26},{3,27},{4,28},{5,29},{6,30},{7,31},{8,16},{9,... | collective-permute-start | bytes 1572872 | tf_op jit(solution)/shard_map/ppermute | solution.py:359
  14.1 13.3 %collective-permute-start.3 = (bf16[2,128,512]{2,1,0:T(8,128)(2,1)S(1)}, bf16[2,128,512]{2,1,0:T(8,128)(2,1)S(1)}, u32[]{:S(2)}, u32[]{:S(2)}) collective-permute-start(bf16[2,128,512]{2,1,0:T(8,128)(2,1)S(1)} %get-tuple-element.57), channel_id=1, source_target_pairs={{0,3},{1,2},{2,1},{3,0},{4,7},{5,6},{6,5},{7,4},{8,11},{9,10},{10,... | collective-permute-start | bytes 786440 | tf_op jit(solution)/shard_map/ppermute | solution.py:370
  16.6 14.7 %collective-permute-start.2 = (bf16[2,128,512]{2,1,0:T(8,128)(2,1)S(1)}, bf16[2,128,512]{2,1,0:T(8,128)(2,1)S(1)}, u32[]{:S(2)}, u32[]{:S(2)}) collective-permute-start(bf16[2,128,512]{2,1,0:T(8,128)(2,1)S(1)} %get-tuple-element.56), channel_id=1, source_target_pairs={{0,2},{1,3},{2,0},{3,1},{4,6},{5,7},{6,4},{7,5},{8,10},{9,11},{10,... | collective-permute-start | bytes 786440 | tf_op jit(solution)/shard_map/ppermute | solution.py:370
  17.1 14.7 %collective-permute-start.1 = (bf16[2,128,512]{2,1,0:T(8,128)(2,1)S(1)}, bf16[2,128,512]{2,1,0:T(8,128)(2,1)S(1)}, u32[]{:S(2)}, u32[]{:S(2)}) collective-permute-start(bf16[2,128,512]{2,1,0:T(8,128)(2,1)S(1)} %get-tuple-element.55), channel_id=1, source_target_pairs={{0,1},{1,0},{2,3},{3,2},{4,5},{5,4},{6,7},{7,6},{8,9},{9,8},{10,11... | collective-permute-start | bytes 786440 | tf_op jit(solution)/shard_map/ppermute | solution.py:370
  26.0 23.9 %copy-start.3 = (bf16[4,128,512]{2,1,0:T(8,128)(2,1)}, bf16[4,128,512]{2,1,0:T(8,128)(2,1)S(1)}, u32[]{:S(2)}) copy-start(bf16[4,128,512]{2,1,0:T(8,128)(2,1)S(1)} %collective-permute-done.4.tile_ref.refs_4_) | copy-start | bytes 1572868
  27.4 9.4 %copy-start.20 = (bf16[2,128,512]{2,1,0:T(8,128)(2,1)}, bf16[2,128,512]{2,1,0:T(8,128)(2,1)S(1)}, u32[]{:S(2)}) copy-start(bf16[2,128,512]{2,1,0:T(8,128)(2,1)S(1)} %collective-permute-done.3.refs_3_) | copy-start | bytes 786436
  27.4 11.4 %collective-permute-start.7 = (bf16[2,128,512]{2,1,0:T(8,128)(2,1)}, bf16[2,128,512]{2,1,0:T(8,128)(2,1)}, u32[]{:S(2)}, u32[]{:S(2)}) collective-permute-start(bf16[2,128,512]{2,1,0:T(8,128)(2,1)} %get-tuple-element.63), channel_id=1, source_target_pairs={{0,3},{1,2},{2,1},{3,0},{4,7},{5,6},{6,5},{7,4},{8,11},{9,10},{10,... | collective-permute-start | bytes 786440 | tf_op jit(solution)/shard_map/ppermute | solution.py:370
  31.3 13.0 %collective-permute-start.6 = (bf16[2,128,512]{2,1,0:T(8,128)(2,1)}, bf16[2,128,512]{2,1,0:T(8,128)(2,1)}, u32[]{:S(2)}, u32[]{:S(2)}) collective-permute-start(bf16[2,128,512]{2,1,0:T(8,128)(2,1)} %get-tuple-element.61), channel_id=1, source_target_pairs={{0,2},{1,3},{2,0},{3,1},{4,6},{5,7},{6,4},{7,5},{8,10},{9,11},{10,... | collective-permute-start | bytes 786440 | tf_op jit(solution)/shard_map/ppermute | solution.py:370
  31.8 14.5 %collective-permute-start.5 = (bf16[2,128,512]{2,1,0:T(8,128)(2,1)S(1)}, bf16[2,128,512]{2,1,0:T(8,128)(2,1)}, u32[]{:S(2)}, u32[]{:S(2)}) collective-permute-start(bf16[2,128,512]{2,1,0:T(8,128)(2,1)S(1)} %get-tuple-element.59), channel_id=1, source_target_pairs={{0,1},{1,0},{2,3},{3,2},{4,5},{5,4},{6,7},{7,6},{8,9},{9,8},{10,11... | collective-permute-start | bytes 786440 | tf_op jit(solution)/shard_map/ppermute | solution.py:370
  36.8 13.1 %copy-start.5 = (bf16[4,128,512]{2,1,0:T(8,128)(2,1)}, bf16[4,128,512]{2,1,0:T(8,128)(2,1)S(1)}, u32[]{:S(2)}) copy-start(bf16[4,128,512]{2,1,0:T(8,128)(2,1)S(1)} %collective-permute-done.8.tile_ref.refs_8_) | copy-start | bytes 1572868
  36.8 14.4 %collective-permute-start.12 = (bf16[4,128,512]{2,1,0:T(8,128)(2,1)S(1)}, bf16[4,128,512]{2,1,0:T(8,128)(2,1)S(1)}, u32[]{:S(2)}, u32[]{:S(2)}) collective-permute-start(bf16[4,128,512]{2,1,0:T(8,128)(2,1)S(1)} %collective-permute-done.8.tile_ref.refs_8_), channel_id=1, source_target_pairs={{0,4},{1,5},{2,6},{3,7},{4,0},{5,1},{6,2},{7,3},{8,12},{9,13},{10,... | collective-permute-start | bytes 1572872 | tf_op jit(solution)/shard_map/ppermute | solution.py:359
  38.9 13.0 %collective-permute-start.11 = (bf16[2,128,512]{2,1,0:T(8,128)(2,1)S(1)}, bf16[2,128,512]{2,1,0:T(8,128)(2,1)S(1)}, u32[]{:S(2)}, u32[]{:S(2)}) collective-permute-start(bf16[2,128,512]{2,1,0:T(8,128)(2,1)S(1)} %get-tuple-element.71), channel_id=1, source_target_pairs={{0,3},{1,2},{2,1},{3,0},{4,7},{5,6},{6,5},{7,4},{8,11},{9,10},{10,... | collective-permute-start | bytes 786440 | tf_op jit(solution)/shard_map/ppermute | solution.py:370
  44.2 10.9 %collective-permute-start.10 = (bf16[2,128,512]{2,1,0:T(8,128)(2,1)S(1)}, bf16[2,128,512]{2,1,0:T(8,128)(2,1)S(1)}, u32[]{:S(2)}, u32[]{:S(2)}) collective-permute-start(bf16[2,128,512]{2,1,0:T(8,128)(2,1)S(1)} %get-tuple-element.69), channel_id=1, source_target_pairs={{0,2},{1,3},{2,0},{3,1},{4,6},{5,7},{6,4},{7,5},{8,10},{9,11},{10,... | collective-permute-start | bytes 786440 | tf_op jit(solution)/shard_map/ppermute | solution.py:370
  46.3 12.2 %copy-start.11 = (bf16[1,512,768]{2,1,0:T(8,128)(2,1)S(1)}, bf16[1,512,768]{2,1,0:T(8,128)(2,1)}, u32[]{:S(2)}) copy-start(bf16[1,512,768]{2,1,0:T(8,128)(2,1)} %param.8) | copy-start | bytes 2359300
  46.3 10.7 %collective-permute-start.9 = (bf16[2,128,512]{2,1,0:T(8,128)(2,1)S(1)}, bf16[2,128,512]{2,1,0:T(8,128)(2,1)S(1)}, u32[]{:S(2)}, u32[]{:S(2)}) collective-permute-start(bf16[2,128,512]{2,1,0:T(8,128)(2,1)S(1)} %get-tuple-element.67), channel_id=1, source_target_pairs={{0,1},{1,0},{2,3},{3,2},{4,5},{5,4},{6,7},{7,6},{8,9},{9,8},{10,11... | collective-permute-start | bytes 786440 | tf_op jit(solution)/shard_map/ppermute | solution.py:370
  51.2 9.0 %copy-start.6 = (bf16[4,128,512]{2,1,0:T(8,128)(2,1)}, bf16[4,128,512]{2,1,0:T(8,128)(2,1)S(1)}, u32[]{:S(2)}) copy-start(bf16[4,128,512]{2,1,0:T(8,128)(2,1)S(1)} %collective-permute-done.12.tile_ref.refs_12_) | copy-start | bytes 1572868
  51.8 8.4 %copy-start.23 = (bf16[2,128,512]{2,1,0:T(8,128)(2,1)}, bf16[2,128,512]{2,1,0:T(8,128)(2,1)S(1)}, u32[]{:S(2)}) copy-start(bf16[2,128,512]{2,1,0:T(8,128)(2,1)S(1)} %collective-permute-done.11.refs_11_) | copy-start | bytes 786436
  51.8 10.2 %collective-permute-start.15 = (bf16[2,128,512]{2,1,0:T(8,128)(2,1)S(1)}, bf16[2,128,512]{2,1,0:T(8,128)(2,1)S(1)}, u32[]{:S(2)}, u32[]{:S(2)}) collective-permute-start(bf16[2,128,512]{2,1,0:T(8,128)(2,1)S(1)} %get-tuple-element.77), channel_id=1, source_target_pairs={{0,3},{1,2},{2,1},{3,0},{4,7},{5,6},{6,5},{7,4},{8,11},{9,10},{10,... | collective-permute-start | bytes 786440 | tf_op jit(solution)/shard_map/ppermute | solution.py:370
  55.1 11.3 %collective-permute-start.14 = (bf16[2,128,512]{2,1,0:T(8,128)(2,1)S(1)}, bf16[2,128,512]{2,1,0:T(8,128)(2,1)S(1)}, u32[]{:S(2)}, u32[]{:S(2)}) collective-permute-start(bf16[2,128,512]{2,1,0:T(8,128)(2,1)S(1)} %get-tuple-element.75), channel_id=1, source_target_pairs={{0,2},{1,3},{2,0},{3,1},{4,6},{5,7},{6,4},{7,5},{8,10},{9,11},{10,... | collective-permute-start | bytes 786440 | tf_op jit(solution)/shard_map/ppermute | solution.py:370
  57.0 9.7 %collective-permute-start.13 = (bf16[2,128,512]{2,1,0:T(8,128)(2,1)S(1)}, bf16[2,128,512]{2,1,0:T(8,128)(2,1)S(1)}, u32[]{:S(2)}, u32[]{:S(2)}) collective-permute-start(bf16[2,128,512]{2,1,0:T(8,128)(2,1)S(1)} %get-tuple-element.73), channel_id=1, source_target_pairs={{0,1},{1,0},{2,3},{3,2},{4,5},{5,4},{6,7},{7,6},{8,9},{9,8},{10,11... | collective-permute-start | bytes 786440 | tf_op jit(solution)/shard_map/ppermute | solution.py:370
  84.7 17.0 %collective-permute-start.16 = (bf16[2,128,512]{2,1,0:T(8,128)(2,1)}, bf16[2,128,512]{2,1,0:T(8,128)(2,1)S(1)}, u32[]{:S(2)}, u32[]{:S(2)}) collective-permute-start(bf16[2,128,512]{2,1,0:T(8,128)(2,1)} %get-tuple-element.78), channel_id=1, source_target_pairs={{0,1},{1,0},{2,3},{3,2},{4,5},{5,4},{6,7},{7,6},{8,9},{9,8},{10,11... | collective-permute-start | bytes 786440 | tf_op jit(solution)/shard_map/ppermute | solution.py:370
  86.2 13.8 %collective-permute-start.19 = (bf16[2,128,512]{2,1,0:T(8,128)(2,1)}, bf16[2,128,512]{2,1,0:T(8,128)(2,1)S(1)}, u32[]{:S(2)}, u32[]{:S(2)}) collective-permute-start(bf16[2,128,512]{2,1,0:T(8,128)(2,1)} %get-tuple-element.90), channel_id=1, source_target_pairs={{0,2},{1,3},{2,0},{3,1},{4,6},{5,7},{6,4},{7,5},{8,10},{9,11},{10,... | collective-permute-start | bytes 786440 | tf_op jit(solution)/shard_map/ppermute | solution.py:370
  87.8 13.7 %collective-permute-start.22 = (bf16[2,128,512]{2,1,0:T(8,128)(2,1)}, bf16[2,128,512]{2,1,0:T(8,128)(2,1)S(1)}, u32[]{:S(2)}, u32[]{:S(2)}) collective-permute-start(bf16[2,128,512]{2,1,0:T(8,128)(2,1)} %get-tuple-element.95), channel_id=1, source_target_pairs={{0,3},{1,2},{2,1},{3,0},{4,7},{5,6},{6,5},{7,4},{8,11},{9,10},{10,... | collective-permute-start | bytes 786440 | tf_op jit(solution)/shard_map/ppermute | solution.py:370
  88.2 37.6 %collective-permute-start.25 = (bf16[8,128,512]{2,1,0:T(8,128)(2,1)}, bf16[8,128,512]{2,1,0:T(8,128)(2,1)}, u32[]{:S(2)}, u32[]{:S(2)}) collective-permute-start(bf16[8,128,512]{2,1,0:T(8,128)(2,1)} %get-tuple-element.98), channel_id=1, source_target_pairs={{0,4},{1,5},{2,6},{3,7},{4,0},{5,1},{6,2},{7,3},{8,12},{9,13},{10,... | collective-permute-start | bytes 3145736 | tf_op jit(solution)/shard_map/ppermute | solution.py:359
  92.0 11.5 %copy-start.7 = (bf16[2,128,512]{2,1,0:T(8,128)(2,1)S(1)}, bf16[2,128,512]{2,1,0:T(8,128)(2,1)}, u32[]{:S(2)}) copy-start(bf16[2,128,512]{2,1,0:T(8,128)(2,1)} %get-tuple-element.100.refs_0_) | copy-start | bytes 786436
  93.7 11.9 %copy-start.13 = (s32[4,16]{1,0:T(4,128)S(1)}, s32[4,16]{1,0:T(4,128)}, u32[]{:S(2)}) copy-start(s32[4,16]{1,0:T(4,128)} %get-tuple-element.108) | copy-start | bytes 772
  93.7 11.9 %copy-start.14 = (s32[4,16]{1,0:T(4,128)S(1)}, s32[4,16]{1,0:T(4,128)}, u32[]{:S(2)}) copy-start(s32[4,16]{1,0:T(4,128)} %get-tuple-element.121) | copy-start | bytes 772
  93.7 11.9 %copy-start.18 = (pred[4,16]{1,0:T(4,128)(4,1)S(1)}, pred[4,16]{1,0:T(4,128)(4,1)}, u32[]{:S(2)}) copy-start(pred[4,16]{1,0:T(4,128)(4,1)} %get-tuple-element.123) | copy-start | bytes 196
  93.7 22.5 %copy-start.10 = (bf16[2,128,512]{2,1,0:T(8,128)(2,1)S(1)}, bf16[2,128,512]{2,1,0:T(8,128)(2,1)}, u32[]{:S(2)}) copy-start(bf16[2,128,512]{2,1,0:T(8,128)(2,1)} %get-tuple-element.99.refs_0_) | copy-start | bytes 786436
  100.0 12.7 %collective-permute-start.20 = (bf16[2,128,512]{2,1,0:T(8,128)(2,1)}, bf16[2,128,512]{2,1,0:T(8,128)(2,1)S(1)}, u32[]{:S(2)}, u32[]{:S(2)}) collective-permute-start(bf16[2,128,512]{2,1,0:T(8,128)(2,1)} %get-tuple-element.91), channel_id=1, source_target_pairs={{0,2},{1,3},{2,0},{3,1},{4,6},{5,7},{6,4},{7,5},{8,10},{9,11},{10,... | collective-permute-start | bytes 786440 | tf_op jit(solution)/shard_map/ppermute | solution.py:370
  101.5 12.9 %collective-permute-start.23 = (bf16[2,128,512]{2,1,0:T(8,128)(2,1)}, bf16[2,128,512]{2,1,0:T(8,128)(2,1)S(1)}, u32[]{:S(2)}, u32[]{:S(2)}) collective-permute-start(bf16[2,128,512]{2,1,0:T(8,128)(2,1)} %get-tuple-element.96), channel_id=1, source_target_pairs={{0,3},{1,2},{2,1},{3,0},{4,7},{5,6},{6,5},{7,4},{8,11},{9,10},{10,... | collective-permute-start | bytes 786440 | tf_op jit(solution)/shard_map/ppermute | solution.py:370
  101.7 13.6 %collective-permute-start.17 = (bf16[2,128,512]{2,1,0:T(8,128)(2,1)}, bf16[2,128,512]{2,1,0:T(8,128)(2,1)S(1)}, u32[]{:S(2)}, u32[]{:S(2)}) collective-permute-start(bf16[2,128,512]{2,1,0:T(8,128)(2,1)} %get-tuple-element.86), channel_id=1, source_target_pairs={{0,1},{1,0},{2,3},{3,2},{4,5},{5,4},{6,7},{7,6},{8,9},{9,8},{10,11... | collective-permute-start | bytes 786440 | tf_op jit(solution)/shard_map/ppermute | solution.py:370
  104.4 19.4 %collective-permute-start.26 = (bf16[4,128,512]{2,1,0:T(8,128)(2,1)S(1)}, bf16[4,128,512]{2,1,0:T(8,128)(2,1)}, u32[]{:S(2)}, u32[]{:S(2)}) collective-permute-start(bf16[4,128,512]{2,1,0:T(8,128)(2,1)S(1)} %owner_sum.4), channel_id=1, source_target_pairs={{0,4},{1,5},{2,6},{3,7},{4,0},{5,1},{6,2},{7,3},{8,12},{9,13},{10,... | collective-permute-start | bytes 1572872 | tf_op jit(solution)/shard_map/ppermute | solution.py:359
  112.7 15.3 %collective-permute-start.21 = (bf16[2,128,512]{2,1,0:T(8,128)(2,1)}, bf16[2,128,512]{2,1,0:T(8,128)(2,1)S(1)}, u32[]{:S(2)}, u32[]{:S(2)}) collective-permute-start(bf16[2,128,512]{2,1,0:T(8,128)(2,1)} %get-tuple-element.92), channel_id=1, source_target_pairs={{0,2},{1,3},{2,0},{3,1},{4,6},{5,7},{6,4},{7,5},{8,10},{9,11},{10,... | collective-permute-start | bytes 786440 | tf_op jit(solution)/shard_map/ppermute | solution.py:370
  114.5 13.5 %collective-permute-start.24 = (bf16[2,128,512]{2,1,0:T(8,128)(2,1)}, bf16[2,128,512]{2,1,0:T(8,128)(2,1)S(1)}, u32[]{:S(2)}, u32[]{:S(2)}) collective-permute-start(bf16[2,128,512]{2,1,0:T(8,128)(2,1)} %get-tuple-element.97), channel_id=1, source_target_pairs={{0,3},{1,2},{2,1},{3,0},{4,7},{5,6},{6,5},{7,4},{8,11},{9,10},{10,... | collective-permute-start | bytes 786440 | tf_op jit(solution)/shard_map/ppermute | solution.py:370
  115.2 12.8 %collective-permute-start.18 = (bf16[2,128,512]{2,1,0:T(8,128)(2,1)}, bf16[2,128,512]{2,1,0:T(8,128)(2,1)S(1)}, u32[]{:S(2)}, u32[]{:S(2)}) collective-permute-start(bf16[2,128,512]{2,1,0:T(8,128)(2,1)} %get-tuple-element.87), channel_id=1, source_target_pairs={{0,1},{1,0},{2,3},{3,2},{4,5},{5,4},{6,7},{7,6},{8,9},{9,8},{10,11... | collective-permute-start | bytes 786440 | tf_op jit(solution)/shard_map/ppermute | solution.py:370
  125.8 18.6 %copy-start.8 = (bf16[2,128,512]{2,1,0:T(8,128)(2,1)S(1)}, bf16[2,128,512]{2,1,0:T(8,128)(2,1)}, u32[]{:S(2)}) copy-start(bf16[2,128,512]{2,1,0:T(8,128)(2,1)} %get-tuple-element.82.refs_0_) | copy-start | bytes 786436
  125.9 26.0 %collective-permute-start.31 = (bf16[4,128,512]{2,1,0:T(8,128)(2,1)}, bf16[4,128,512]{2,1,0:T(8,128)(2,1)}, u32[]{:S(2)}, u32[]{:S(2)}) collective-permute-start(bf16[4,128,512]{2,1,0:T(8,128)(2,1)} %add_convert_fusion), channel_id=1, source_target_pairs={{0,24},{1,25},{2,26},{3,27},{4,28},{5,29},{6,30},{7,31},{8,16},{9,... | collective-permute-start | bytes 1572872 | tf_op jit(solution)/shard_map/ppermute | solution.py:359
  128.0 8.7 %collective-permute-start.27 = (bf16[2,128,512]{2,1,0:T(8,128)(2,1)}, bf16[2,128,512]{2,1,0:T(8,128)(2,1)S(1)}, u32[]{:S(2)}, u32[]{:S(2)}) collective-permute-start(bf16[2,128,512]{2,1,0:T(8,128)(2,1)} %get-tuple-element.102), channel_id=1, source_target_pairs={{0,1},{1,0},{2,3},{3,2},{4,5},{5,4},{6,7},{7,6},{8,9},{9,8},{10,11... | collective-permute-start | bytes 786440 | tf_op jit(solution)/shard_map/ppermute | solution.py:370
  129.7 14.7 %collective-permute-start.28 = (bf16[2,128,512]{2,1,0:T(8,128)(2,1)}, bf16[2,128,512]{2,1,0:T(8,128)(2,1)S(1)}, u32[]{:S(2)}, u32[]{:S(2)}) collective-permute-start(bf16[2,128,512]{2,1,0:T(8,128)(2,1)} %get-tuple-element.104), channel_id=1, source_target_pairs={{0,2},{1,3},{2,0},{3,1},{4,6},{5,7},{6,4},{7,5},{8,10},{9,11},{10,... | collective-permute-start | bytes 786440 | tf_op jit(solution)/shard_map/ppermute | solution.py:370
  131.2 13.2 %collective-permute-start.29 = (bf16[2,128,512]{2,1,0:T(8,128)(2,1)S(1)}, bf16[2,128,512]{2,1,0:T(8,128)(2,1)S(1)}, u32[]{:S(2)}, u32[]{:S(2)}) collective-permute-start(bf16[2,128,512]{2,1,0:T(8,128)(2,1)S(1)} %get-tuple-element.106), channel_id=1, source_target_pairs={{0,3},{1,2},{2,1},{3,0},{4,7},{5,6},{6,5},{7,4},{8,11},{9,10},{10,... | collective-permute-start | bytes 786440 | tf_op jit(solution)/shard_map/ppermute | solution.py:370
  144.4 7.4 %copy-start.1 = (bf16[768,256]{1,0:T(8,128)(2,1)S(1)}, bf16[768,256]{1,0:T(8,128)(2,1)}, u32[]{:S(2)}) copy-start(bf16[768,256]{1,0:T(8,128)(2,1)} %refs_2_.3) | copy-start | bytes 1179652
  144.4 7.4 %copy-start.2 = (bf16[768,256]{1,0:T(8,128)(2,1)S(1)}, bf16[768,256]{1,0:T(8,128)(2,1)}, u32[]{:S(2)}) copy-start(bf16[768,256]{1,0:T(8,128)(2,1)} %refs_3_.3) | copy-start | bytes 1179652
  145.4 8.1 %collective-permute-start.30 = (bf16[4,128,512]{2,1,0:T(8,128)(2,1)S(1)}, bf16[4,128,512]{2,1,0:T(8,128)(2,1)S(1)}, u32[]{:S(2)}, u32[]{:S(2)}) collective-permute-start(bf16[4,128,512]{2,1,0:T(8,128)(2,1)S(1)} %owner_sum.5), channel_id=1, source_target_pairs={{0,16},{1,17},{2,18},{3,19},{4,20},{5,21},{6,22},{7,23},{8,24},{9,... | collective-permute-start | bytes 1572872 | tf_op jit(solution)/shard_map/ppermute | solution.py:359
  (14 other events, 56.1 us)

commit v16 on v15

--- a/solution.py
+++ b/solution.py
@@ -435,10 +435,11 @@
     far = spread(back[1][1:], last)
     last_sum = owner_sum(3, wanted, [back[2][0], *last], block_count, BF16, 0)
     last_sum = swap(last_sum, 1, 0).astype(F32)
-    far_sum = owner_sum(2, wanted, [back[1][0], *far], block_count, F32, FAR_SUM_FLOPS)
-    far_sum = (far_sum + last_sum).astype(BF16)
+    beside = [hopped[p * CAP : (p + 1) * CAP] for p in range(plane)]
+    far[0], *beside = lax.optimization_barrier((far[0], *beside))
+    far_sum = owner_sum(2, wanted, [back[1][0], *far], block_count, BF16, FAR_SUM_FLOPS)
+    far_sum = (far_sum.astype(F32) + last_sum).astype(BF16)
     own = spread(back[0][1:], far)
-    beside = [hopped[p * CAP : (p + 1) * CAP] for p in range(plane)]
     beside = [beside[0], *spread([after(x, far_sum) for x in beside[1:]], own)]
     own_sum = owner_sum(0, own_wanted, [back[0][0], *own, *beside], block_count, BF16, 0)
     far_grad, own_grad = swap(far_sum, 2, 1), swap(own_sum, 0, 1)

time: 155 us -> 152 us (0.981)
  waiting for transfers between devices: 62 us -> 56.2 us
  starting transfers between devices: 40.7 us -> 44.8 us
    ppermute x8, waiting for transfers between devices: 27.2 us -> 23.7 us  [swap(): return lax.ppermute(value, ('vintage', 'tile'), pairs)]
    ppermute x8, starting transfers between devices: 7.69 us -> 10.8 us  [swap(): return lax.ppermute(value, ('vintage', 'tile'), pairs)]
    ppermute x24, waiting for transfers between devices: 34.8 us -> 32.5 us  [spread(): moved.append(lax.ppermute(value, 'tile', pairs))]
  transfers between devices with their start and end apart: 32 -> 32, of which waited for: 14 -> 15; matrix products, arithmetic and copies ran while one was open for 13% -> 12% of each run, Pallas kernels for 5% -> 5%
where the time goes in v16:
time: 152 us
  waiting for transfers between devices  56.2 us (37%)
  starting transfers between devices  44.8 us (29%)
  Pallas kernels  30.2 us (20%)
  matrix products  10.2 us (7%)
  other arithmetic  5.22 us (3%)
  local copies, waits for them, and re-layouts  3.93 us (3%)
    ppermute x24, starting transfers between devices, spread(): moved.append(lax.ppermute(value, 'tile', pairs))  34 us
    ppermute x24, waiting for transfers between devices, spread(): moved.append(lax.ppermute(value, 'tile', pairs))  32.5 us
    ppermute x8, waiting for transfers between devices, swap(): return lax.ppermute(value, ('vintage', 'tile'), pairs)  23.7 us
    pallas_call x1, Pallas kernels, attention(): pl.pallas_call(functools.partial(attention_kernel, list_len, per_step, le...  17.6 us
    ppermute x8, starting transfers between devices, swap(): return lax.ppermute(value, ('vintage', 'tile'), pairs)  10.8 us
    dot_general x1, matrix products, dot_nt(): lax.dot_general(a, b, (((1,), (1,)), ((), ())), preferred_element_type=F32)  3.54 us
    pallas_call x1, Pallas kernels, project(): pl.pallas_call(project_kernel, in_specs=[pl.BlockSpec(memory_space=pl.ANY...  3.4 us
    dot_general x1, matrix products, shards(): lax.dot_general(query_grad, w_query, (((0,), (1,)), ((), ())), preferred_...  3.29 us
  transfers between devices with their start and end apart: 32, of which 15 were waited for; matrix products, arithmetic and copies ran while one was open for 12% of the time, Pallas kernels for 5%

profile of v16, /device:TPU:0, one launch (start us, length us, event | category | flops | bytes accessed | tf_op | source)
XLA Modules:
  0.0 151.6 jit_solution(10200822247971793845)
XLA Ops:
  0.7 3.4 %project.1 = bf16[512,512]{1,0:T(8,128)(2,1)} custom-call(bf16[512,768]{1,0:T(8,128)(2,1)} %bitcast.60, bf16[768,256]{1,0:T(8,128)(2,1)} %refs_2_.3, bf16[768,256]{1,0:T(8,128)(2,1)} %refs_3_.3), custom_call_target="tpu_custom_call" | custom-call | tf_op jit(solution)/shard_map/project/pallas_call | solution.py:258
  4.1 2.5 %collective-permute-start.4 = (bf16[4,128,512]{2,1,0:T(8,128)(2,1)}, bf16[4,128,512]{2,1,0:T(8,128)(2,1)S(1)}, u32[]{:S(2)}, u32[]{:S(2)}) collective-permute-start(bf16[4,128,512]{2,1,0:T(8,128)(2,1)} %bitcast.61), channel_id=1, source_target_pairs={{0,20},{1,21},{2,22},{3,23},{4,16},{5,17},{6,18},{7,19},{8,28},{9,... | collective-permute-start | bytes 1572872 | tf_op jit(solution)/shard_map/ppermute | solution.py:359
  8.8 0.8 convert_reduce_fusion
  10.4 2.3 %collective-permute-start.8 = (bf16[4,128,512]{2,1,0:T(8,128)(2,1)}, bf16[4,128,512]{2,1,0:T(8,128)(2,1)S(1)}, u32[]{:S(2)}, u32[]{:S(2)}) collective-permute-start(bf16[4,128,512]{2,1,0:T(8,128)(2,1)} %bitcast.63), channel_id=1, source_target_pairs={{0,24},{1,25},{2,26},{3,27},{4,28},{5,29},{6,30},{7,31},{8,16},{9,... | collective-permute-start | bytes 1572872 | tf_op jit(solution)/shard_map/ppermute | solution.py:359
  14.2 2.5 %collective-permute-start.3 = (bf16[2,128,512]{2,1,0:T(8,128)(2,1)S(1)}, bf16[2,128,512]{2,1,0:T(8,128)(2,1)S(1)}, u32[]{:S(2)}, u32[]{:S(2)}) collective-permute-start(bf16[2,128,512]{2,1,0:T(8,128)(2,1)S(1)} %get-tuple-element.62), channel_id=1, source_target_pairs={{0,3},{1,2},{2,1},{3,0},{4,7},{5,6},{6,5},{7,4},{8,11},{9,10},{10,... | collective-permute-start | bytes 786440 | tf_op jit(solution)/shard_map/ppermute | solution.py:370
  17.7 8.2 %collective-permute-done.4.tile_ref.refs_4_ = bf16[4,128,512]{2,1,0:T(8,128)(2,1)S(1)} collective-permute-done((bf16[4,128,512]{2,1,0:T(8,128)(2,1)}, bf16[4,128,512]{2,1,0:T(8,128)(2,1)S(1)}, u32[]{:S(2)}, u32[]{:S(2)}) %collective-permute-start.4) | collective-permute-done | bytes 524320 | tf_op jit(solution)/shard_map/ppermute | solution.py:359
  25.9 1.4 pack.5
  27.4 3.9 %collective-permute-start.7 = (bf16[2,128,512]{2,1,0:T(8,128)(2,1)}, bf16[2,128,512]{2,1,0:T(8,128)(2,1)}, u32[]{:S(2)}, u32[]{:S(2)}) collective-permute-start(bf16[2,128,512]{2,1,0:T(8,128)(2,1)} %get-tuple-element.68), channel_id=1, source_target_pairs={{0,3},{1,2},{2,1},{3,0},{4,7},{5,6},{6,5},{7,4},{8,11},{9,10},{10,... | collective-permute-start | bytes 786440 | tf_op jit(solution)/shard_map/ppermute | solution.py:370
  31.9 5.0 %collective-permute-done.8.tile_ref.refs_8_ = bf16[4,128,512]{2,1,0:T(8,128)(2,1)S(1)} collective-permute-done((bf16[4,128,512]{2,1,0:T(8,128)(2,1)}, bf16[4,128,512]{2,1,0:T(8,128)(2,1)S(1)}, u32[]{:S(2)}, u32[]{:S(2)}) %collective-permute-start.8) | collective-permute-done | bytes 524320 | tf_op jit(solution)/shard_map/ppermute | solution.py:359
  37.0 1.3 bitcast_select_fusion
  38.9 2.7 %collective-permute-start.11 = (bf16[2,128,512]{2,1,0:T(8,128)(2,1)S(1)}, bf16[2,128,512]{2,1,0:T(8,128)(2,1)S(1)}, u32[]{:S(2)}, u32[]{:S(2)}) collective-permute-start(bf16[2,128,512]{2,1,0:T(8,128)(2,1)S(1)} %get-tuple-element.76), channel_id=1, source_target_pairs={{0,3},{1,2},{2,1},{3,0},{4,7},{5,6},{6,5},{7,4},{8,11},{9,10},{10,... | collective-permute-start | bytes 786440 | tf_op jit(solution)/shard_map/ppermute | solution.py:370
  41.6 2.6 %collective-permute-done.6.refs_6_ = bf16[2,128,512]{2,1,0:T(8,128)(2,1)} collective-permute-done((bf16[2,128,512]{2,1,0:T(8,128)(2,1)}, bf16[2,128,512]{2,1,0:T(8,128)(2,1)}, u32[]{:S(2)}, u32[]{:S(2)}) %collective-permute-start.6) | collective-permute-done | bytes 262176 | tf_op jit(solution)/shard_map/ppermute | solution.py:370
  44.2 2.0 %collective-permute-start.10 = (bf16[2,128,512]{2,1,0:T(8,128)(2,1)S(1)}, bf16[2,128,512]{2,1,0:T(8,128)(2,1)S(1)}, u32[]{:S(2)}, u32[]{:S(2)}) collective-permute-start(bf16[2,128,512]{2,1,0:T(8,128)(2,1)S(1)} %get-tuple-element.74), channel_id=1, source_target_pairs={{0,2},{1,3},{2,0},{3,1},{4,6},{5,7},{6,4},{7,5},{8,10},{9,11},{10,... | collective-permute-start | bytes 786440 | tf_op jit(solution)/shard_map/ppermute | solution.py:370
  46.4 3.5 %fusion.ng_ref = f32[768,512]{1,0:T(8,128)} fusion(bf16[768,768]{1,0:T(8,128)(2,1)} %param.13, bf16[1,512,768]{2,1,0:T(8,128)(2,1)} %param.9), kind=kOutput, calls=%fused_computation.5 | convolution fusion | flops 603979776 | bytes 3538944 | tf_op jit(solution)/shard_map/dot_general | solution.py:34
  49.9 1.4 collective-permute-done.12.tile_ref.refs_12_
  51.9 2.5 %collective-permute-start.15 = (bf16[2,128,512]{2,1,0:T(8,128)(2,1)S(1)}, bf16[2,128,512]{2,1,0:T(8,128)(2,1)S(1)}, u32[]{:S(2)}, u32[]{:S(2)}) collective-permute-start(bf16[2,128,512]{2,1,0:T(8,128)(2,1)S(1)} %get-tuple-element.82), channel_id=1, source_target_pairs={{0,3},{1,2},{2,1},{3,0},{4,7},{5,6},{6,5},{7,4},{8,11},{9,10},{10,... | collective-permute-start | bytes 786440 | tf_op jit(solution)/shard_map/ppermute | solution.py:370
  55.1 1.8 %collective-permute-start.14 = (bf16[2,128,512]{2,1,0:T(8,128)(2,1)S(1)}, bf16[2,128,512]{2,1,0:T(8,128)(2,1)S(1)}, u32[]{:S(2)}, u32[]{:S(2)}) collective-permute-start(bf16[2,128,512]{2,1,0:T(8,128)(2,1)S(1)} %get-tuple-element.80), channel_id=1, source_target_pairs={{0,2},{1,3},{2,0},{3,1},{4,6},{5,7},{6,4},{7,5},{8,10},{9,11},{10,... | collective-permute-start | bytes 786440 | tf_op jit(solution)/shard_map/ppermute | solution.py:370
  56.8 1.5 collective-permute-start.13
  58.3 1.7 %convolution_convert_fusion.1.q_ref = bf16[768,512]{1,0:T(8,128)(2,1)} fusion(bf16[768,768]{1,0:T(8,128)(2,1)S(1)} %copy-done, bf16[1,512,768]{2,1,0:T(8,128)(2,1)S(1)} %copy-done.11), kind=kOutput, calls=%fused_computation.3 | convolution fusion | flops 604372992 | bytes 2752512 | tf_op jit(solution)/shard_map/dot_general | solution.py:418
  60.1 2.0 %collective-permute-done.15.refs_15_ = bf16[2,128,512]{2,1,0:T(8,128)(2,1)S(1)} collective-permute-done((bf16[2,128,512]{2,1,0:T(8,128)(2,1)S(1)}, bf16[2,128,512]{2,1,0:T(8,128)(2,1)S(1)}, u32[]{:S(2)}, u32[]{:S(2)}) %collective-permute-start.15) | collective-permute-done | bytes 262176 | tf_op jit(solution)/shard_map/ppermute | solution.py:370
  62.1 4.3 %collective-permute-done.14.refs_14_ = bf16[2,128,512]{2,1,0:T(8,128)(2,1)S(1)} collective-permute-done((bf16[2,128,512]{2,1,0:T(8,128)(2,1)S(1)}, bf16[2,128,512]{2,1,0:T(8,128)(2,1)S(1)}, u32[]{:S(2)}, u32[]{:S(2)}) %collective-permute-start.14) | collective-permute-done | bytes 262176 | tf_op jit(solution)/shard_map/ppermute | solution.py:370
  67.3 17.6 %attention.1 = (bf16[768,512]{1,0:T(8,128)(2,1)}, bf16[768,512]{1,0:T(8,128)(2,1)}, bf16[2,128,512]{2,1,0:T(8,128)(2,1)}, bf16[2,128,512]{2,1,0:T(8,128)(2,1)}, ...) custom-call(s32[16]{0:T(128)} %get-tuple-element.136.get_ref, ...), custom_call_target="tpu_custom_call" | custom-call | flops 2415919104 | bytes 6291456 | tf_op jit(solution)/shard_map/attention/pallas_call | solution.py:210
  85.6 1.5 %collective-permute-start.16 = (bf16[2,128,512]{2,1,0:T(8,128)(2,1)}, bf16[2,128,512]{2,1,0:T(8,128)(2,1)S(1)}, u32[]{:S(2)}, u32[]{:S(2)}) collective-permute-start(bf16[2,128,512]{2,1,0:T(8,128)(2,1)} %get-tuple-element.83), channel_id=1, source_target_pairs={{0,1},{1,0},{2,3},{3,2},{4,5},{5,4},{6,7},{7,6},{8,9},{9,8},{10,11... | collective-permute-start | bytes 786440 | tf_op jit(solution)/shard_map/ppermute | solution.py:370
  87.1 1.5 %collective-permute-start.20 = (bf16[2,128,512]{2,1,0:T(8,128)(2,1)}, bf16[2,128,512]{2,1,0:T(8,128)(2,1)S(1)}, u32[]{:S(2)}, u32[]{:S(2)}) collective-permute-start(bf16[2,128,512]{2,1,0:T(8,128)(2,1)} %get-tuple-element.97), channel_id=1, source_target_pairs={{0,2},{1,3},{2,0},{3,1},{4,6},{5,7},{6,4},{7,5},{8,10},{9,11},{10,... | collective-permute-start | bytes 786440 | tf_op jit(solution)/shard_map/ppermute | solution.py:370
  89.1 3.3 %fusion.14.refs_1_ = f32[512,768]{1,0:T(8,128)} fusion(bf16[768,512]{1,0:T(8,128)(2,1)} %get-tuple-element.84, bf16[768,768]{1,0:T(8,128)(2,1)S(1)} %copy-done), kind=kOutput, calls=%fused_computation.52 | convolution fusion | flops 603979776 | bytes 3538944 | tf_op jit(solution)/shard_map/dot_general | solution.py:430
  92.4 8.7 %collective-permute-done.20.refs_2_ = bf16[2,128,512]{2,1,0:T(8,128)(2,1)S(1)} collective-permute-done((bf16[2,128,512]{2,1,0:T(8,128)(2,1)}, bf16[2,128,512]{2,1,0:T(8,128)(2,1)S(1)}, u32[]{:S(2)}, u32[]{:S(2)}) %collective-permute-start.20) | collective-permute-done | bytes 262176 | tf_op jit(solution)/shard_map/ppermute | solution.py:370
  101.1 2.2 %collective-permute-start.21 = (bf16[2,128,512]{2,1,0:T(8,128)(2,1)S(1)}, bf16[2,128,512]{2,1,0:T(8,128)(2,1)S(1)}, u32[]{:S(2)}, u32[]{:S(2)}) collective-permute-start(bf16[2,128,512]{2,1,0:T(8,128)(2,1)S(1)} %copy-done.29), channel_id=1, source_target_pairs={{0,2},{1,3},{2,0},{3,1},{4,6},{5,7},{6,4},{7,5},{8,10},{9,11},{10,... | collective-permute-start | bytes 786440 | tf_op jit(solution)/shard_map/ppermute | solution.py:370
  103.3 1.7 %convolution_convert_fusion = bf16[512,768]{1,0:T(8,128)(2,1)} fusion(bf16[768,512]{1,0:T(8,128)(2,1)S(1)} %copy-done.34, bf16[768,768]{1,0:T(8,128)(2,1)S(1)} %copy-done.19), kind=kOutput, calls=%fused_computation.2 | convolution fusion | flops 604372992 | bytes 2752512 | tf_op jit(solution)/shard_map/dot_general | solution.py:38
  105.0 1.6 %collective-permute-start.17 = (bf16[2,128,512]{2,1,0:T(8,128)(2,1)S(1)}, bf16[2,128,512]{2,1,0:T(8,128)(2,1)S(1)}, u32[]{:S(2)}, u32[]{:S(2)}) collective-permute-start(bf16[2,128,512]{2,1,0:T(8,128)(2,1)S(1)} %copy-done.25), channel_id=1, source_target_pairs={{0,1},{1,0},{2,3},{3,2},{4,5},{5,4},{6,7},{7,6},{8,9},{9,8},{10,11... | collective-permute-start | bytes 786440 | tf_op jit(solution)/shard_map/ppermute | solution.py:370
  106.6 1.1 owner_sum.4
  107.7 4.3 %collective-permute-start.26 = (bf16[4,128,512]{2,1,0:T(8,128)(2,1)S(1)}, bf16[4,128,512]{2,1,0:T(8,128)(2,1)S(1)}, u32[]{:S(2)}, u32[]{:S(2)}) collective-permute-start(bf16[4,128,512]{2,1,0:T(8,128)(2,1)S(1)} %owner_sum.4), channel_id=1, source_target_pairs={{0,4},{1,5},{2,6},{3,7},{4,0},{5,1},{6,2},{7,3},{8,12},{9,13},{10,... | collective-permute-start | bytes 1572872 | tf_op jit(solution)/shard_map/ppermute | solution.py:359
  112.0 1.1 collective-permute-done.21.refs_2_
  113.1 3.0 %collective-permute-start.22 = (bf16[2,128,512]{2,1,0:T(8,128)(2,1)S(1)}, bf16[2,128,512]{2,1,0:T(8,128)(2,1)S(1)}, u32[]{:S(2)}, u32[]{:S(2)}) collective-permute-start(bf16[2,128,512]{2,1,0:T(8,128)(2,1)S(1)} %copy-done.24), channel_id=1, source_target_pairs={{0,2},{1,3},{2,0},{3,1},{4,6},{5,7},{6,4},{7,5},{8,10},{9,11},{10,... | collective-permute-start | bytes 786440 | tf_op jit(solution)/shard_map/ppermute | solution.py:370
  116.1 0.9 fusion.13
  117.0 1.5 %collective-permute-start.19 = (bf16[2,128,512]{2,1,0:T(8,128)(2,1)S(1)}, bf16[2,128,512]{2,1,0:T(8,128)(2,1)S(1)}, u32[]{:S(2)}, u32[]{:S(2)}) collective-permute-start(bf16[2,128,512]{2,1,0:T(8,128)(2,1)S(1)} %copy-done.23), channel_id=1, source_target_pairs={{0,1},{1,0},{2,3},{3,2},{4,5},{5,4},{6,7},{7,6},{8,9},{9,8},{10,11... | collective-permute-start | bytes 786440 | tf_op jit(solution)/shard_map/ppermute | solution.py:370
  118.5 0.8 owner_sum.3
  119.3 2.0 %collective-permute-done.26 = bf16[4,128,512]{2,1,0:T(8,128)(2,1)S(1)} collective-permute-done((bf16[4,128,512]{2,1,0:T(8,128)(2,1)S(1)}, bf16[4,128,512]{2,1,0:T(8,128)(2,1)S(1)}, u32[]{:S(2)}, u32[]{:S(2)}) %collective-permute-start.26) | collective-permute-done | bytes 524320 | tf_op jit(solution)/shard_map/ppermute | solution.py:359
  121.4 0.9 add_convert_fusion
  122.6 1.0 collective-permute-done.25.refs_3_
  123.6 1.7 %collective-permute-start.28 = (bf16[2,128,512]{2,1,0:T(8,128)(2,1)}, bf16[2,128,512]{2,1,0:T(8,128)(2,1)S(1)}, u32[]{:S(2)}, u32[]{:S(2)}) collective-permute-start(bf16[2,128,512]{2,1,0:T(8,128)(2,1)} %get-tuple-element.113), channel_id=1, source_target_pairs={{0,2},{1,3},{2,0},{3,1},{4,6},{5,7},{6,4},{7,5},{8,10},{9,11},{10,... | collective-permute-start | bytes 786440 | tf_op jit(solution)/shard_map/ppermute | solution.py:370
  125.3 0.9 collective-permute-start.29
  126.2 0.9 collective-permute-start.27
  128.1 10.2 %collective-permute-done.28.refs_6_ = bf16[2,128,512]{2,1,0:T(8,128)(2,1)S(1)} collective-permute-done((bf16[2,128,512]{2,1,0:T(8,128)(2,1)}, bf16[2,128,512]{2,1,0:T(8,128)(2,1)S(1)}, u32[]{:S(2)}, u32[]{:S(2)}) %collective-permute-start.28) | collective-permute-done | bytes 262176 | tf_op jit(solution)/shard_map/ppermute | solution.py:370
  138.3 1.7 %collective-permute-done.27.refs_5_ = bf16[2,128,512]{2,1,0:T(8,128)(2,1)S(1)} collective-permute-done((bf16[2,128,512]{2,1,0:T(8,128)(2,1)S(1)}, bf16[2,128,512]{2,1,0:T(8,128)(2,1)S(1)}, u32[]{:S(2)}, u32[]{:S(2)}) %collective-permute-start.27) | collective-permute-done | bytes 262176 | tf_op jit(solution)/shard_map/ppermute | solution.py:370
  140.0 0.9 owner_sum.5
  141.3 7.1 %collective-permute-done.31 = bf16[4,128,512]{2,1,0:T(8,128)(2,1)} collective-permute-done((bf16[4,128,512]{2,1,0:T(8,128)(2,1)}, bf16[4,128,512]{2,1,0:T(8,128)(2,1)}, u32[]{:S(2)}, u32[]{:S(2)}) %collective-permute-start.31) | collective-permute-done | bytes 524320 | tf_op jit(solution)/shard_map/ppermute | solution.py:359
  148.4 1.7 %finish.2.refs_1_ = f32[512,768]{1,0:T(8,128)S(1)} custom-call(bf16[512,512]{1,0:T(8,128)(2,1)} %bitcast.20.refs_0_, f32[512,768]{1,0:T(8,128)S(1)} %copy-done.9, bf16[768,256]{1,0:T(8,128)(2,1)S(1)} %copy-done.1, bf16[768,256]{1,0:T(8,128)(2,1)S(1)} %copy-done.2), custom_call_target="tpu_custom_call" | custom-call | flops 20000000000 | bytes 1572864 | tf_op jit(solution)/shard_map/finish/pallas_call | solution.py:299
  150.1 1.5 finish.3
  (130 shorter events, 11.9 us)
Async XLA Ops:
  0.6 57.7 %copy-start = (bf16[768,768]{1,0:T(8,128)(2,1)S(1)}, bf16[768,768]{1,0:T(8,128)(2,1)}, u32[]{:S(2)}) copy-start(bf16[768,768]{1,0:T(8,128)(2,1)} %param.10) | copy-start | bytes 3538948
  4.1 21.9 %collective-permute-start.4 = (bf16[4,128,512]{2,1,0:T(8,128)(2,1)}, bf16[4,128,512]{2,1,0:T(8,128)(2,1)S(1)}, u32[]{:S(2)}, u32[]{:S(2)}) collective-permute-start(bf16[4,128,512]{2,1,0:T(8,128)(2,1)} %bitcast.61), channel_id=1, source_target_pairs={{0,20},{1,21},{2,22},{3,23},{4,16},{5,17},{6,18},{7,19},{8,28},{9,... | collective-permute-start | bytes 1572872 | tf_op jit(solution)/shard_map/ppermute | solution.py:359
  6.6 3.8 %collective-permute-start = (bf16[4,128,512]{2,1,0:T(8,128)(2,1)}, bf16[4,128,512]{2,1,0:T(8,128)(2,1)S(1)}, u32[]{:S(2)}, u32[]{:S(2)}) collective-permute-start(bf16[4,128,512]{2,1,0:T(8,128)(2,1)} %bitcast.62), channel_id=1, source_target_pairs={{0,16},{1,17},{2,18},{3,19},{4,20},{5,21},{6,22},{7,23},{8,24},{9,... | collective-permute-start | bytes 1572872 | tf_op jit(solution)/shard_map/ppermute | solution.py:359
  10.4 39.5 %copy-start.4 = (bf16[4,128,512]{2,1,0:T(8,128)(2,1)}, bf16[4,128,512]{2,1,0:T(8,128)(2,1)S(1)}, u32[]{:S(2)}) copy-start(bf16[4,128,512]{2,1,0:T(8,128)(2,1)S(1)} %collective-permute-done.tile_ref.refs_0_) | copy-start | bytes 1572868
  10.4 26.4 %collective-permute-start.8 = (bf16[4,128,512]{2,1,0:T(8,128)(2,1)}, bf16[4,128,512]{2,1,0:T(8,128)(2,1)S(1)}, u32[]{:S(2)}, u32[]{:S(2)}) collective-permute-start(bf16[4,128,512]{2,1,0:T(8,128)(2,1)} %bitcast.63), channel_id=1, source_target_pairs={{0,24},{1,25},{2,26},{3,27},{4,28},{5,29},{6,30},{7,31},{8,16},{9,... | collective-permute-start | bytes 1572872 | tf_op jit(solution)/shard_map/ppermute | solution.py:359
  14.2 13.2 %collective-permute-start.3 = (bf16[2,128,512]{2,1,0:T(8,128)(2,1)S(1)}, bf16[2,128,512]{2,1,0:T(8,128)(2,1)S(1)}, u32[]{:S(2)}, u32[]{:S(2)}) collective-permute-start(bf16[2,128,512]{2,1,0:T(8,128)(2,1)S(1)} %get-tuple-element.62), channel_id=1, source_target_pairs={{0,3},{1,2},{2,1},{3,0},{4,7},{5,6},{6,5},{7,4},{8,11},{9,10},{10,... | collective-permute-start | bytes 786440 | tf_op jit(solution)/shard_map/ppermute | solution.py:370
  16.7 14.5 %collective-permute-start.2 = (bf16[2,128,512]{2,1,0:T(8,128)(2,1)S(1)}, bf16[2,128,512]{2,1,0:T(8,128)(2,1)S(1)}, u32[]{:S(2)}, u32[]{:S(2)}) collective-permute-start(bf16[2,128,512]{2,1,0:T(8,128)(2,1)S(1)} %get-tuple-element.61), channel_id=1, source_target_pairs={{0,2},{1,3},{2,0},{3,1},{4,6},{5,7},{6,4},{7,5},{8,10},{9,11},{10,... | collective-permute-start | bytes 786440 | tf_op jit(solution)/shard_map/ppermute | solution.py:370
  17.2 14.6 %collective-permute-start.1 = (bf16[2,128,512]{2,1,0:T(8,128)(2,1)S(1)}, bf16[2,128,512]{2,1,0:T(8,128)(2,1)S(1)}, u32[]{:S(2)}, u32[]{:S(2)}) collective-permute-start(bf16[2,128,512]{2,1,0:T(8,128)(2,1)S(1)} %get-tuple-element.60), channel_id=1, source_target_pairs={{0,1},{1,0},{2,3},{3,2},{4,5},{5,4},{6,7},{7,6},{8,9},{9,8},{10,11... | collective-permute-start | bytes 786440 | tf_op jit(solution)/shard_map/ppermute | solution.py:370
  25.9 24.0 %copy-start.3 = (bf16[4,128,512]{2,1,0:T(8,128)(2,1)}, bf16[4,128,512]{2,1,0:T(8,128)(2,1)S(1)}, u32[]{:S(2)}) copy-start(bf16[4,128,512]{2,1,0:T(8,128)(2,1)S(1)} %collective-permute-done.4.tile_ref.refs_4_) | copy-start | bytes 1572868
  27.4 9.5 %copy-start.20 = (bf16[2,128,512]{2,1,0:T(8,128)(2,1)}, bf16[2,128,512]{2,1,0:T(8,128)(2,1)S(1)}, u32[]{:S(2)}) copy-start(bf16[2,128,512]{2,1,0:T(8,128)(2,1)S(1)} %collective-permute-done.3.refs_3_) | copy-start | bytes 786436
  27.4 11.5 %collective-permute-start.7 = (bf16[2,128,512]{2,1,0:T(8,128)(2,1)}, bf16[2,128,512]{2,1,0:T(8,128)(2,1)}, u32[]{:S(2)}, u32[]{:S(2)}) collective-permute-start(bf16[2,128,512]{2,1,0:T(8,128)(2,1)} %get-tuple-element.68), channel_id=1, source_target_pairs={{0,3},{1,2},{2,1},{3,0},{4,7},{5,6},{6,5},{7,4},{8,11},{9,10},{10,... | collective-permute-start | bytes 786440 | tf_op jit(solution)/shard_map/ppermute | solution.py:370
  31.2 13.0 %collective-permute-start.6 = (bf16[2,128,512]{2,1,0:T(8,128)(2,1)}, bf16[2,128,512]{2,1,0:T(8,128)(2,1)}, u32[]{:S(2)}, u32[]{:S(2)}) collective-permute-start(bf16[2,128,512]{2,1,0:T(8,128)(2,1)} %get-tuple-element.66), channel_id=1, source_target_pairs={{0,2},{1,3},{2,0},{3,1},{4,6},{5,7},{6,4},{7,5},{8,10},{9,11},{10,... | collective-permute-start | bytes 786440 | tf_op jit(solution)/shard_map/ppermute | solution.py:370
  31.8 14.5 %collective-permute-start.5 = (bf16[2,128,512]{2,1,0:T(8,128)(2,1)S(1)}, bf16[2,128,512]{2,1,0:T(8,128)(2,1)}, u32[]{:S(2)}, u32[]{:S(2)}) collective-permute-start(bf16[2,128,512]{2,1,0:T(8,128)(2,1)S(1)} %get-tuple-element.64), channel_id=1, source_target_pairs={{0,1},{1,0},{2,3},{3,2},{4,5},{5,4},{6,7},{7,6},{8,9},{9,8},{10,11... | collective-permute-start | bytes 786440 | tf_op jit(solution)/shard_map/ppermute | solution.py:370
  36.9 13.0 %copy-start.5 = (bf16[4,128,512]{2,1,0:T(8,128)(2,1)}, bf16[4,128,512]{2,1,0:T(8,128)(2,1)S(1)}, u32[]{:S(2)}) copy-start(bf16[4,128,512]{2,1,0:T(8,128)(2,1)S(1)} %collective-permute-done.8.tile_ref.refs_8_) | copy-start | bytes 1572868
  36.9 14.4 %collective-permute-start.12 = (bf16[4,128,512]{2,1,0:T(8,128)(2,1)S(1)}, bf16[4,128,512]{2,1,0:T(8,128)(2,1)S(1)}, u32[]{:S(2)}, u32[]{:S(2)}) collective-permute-start(bf16[4,128,512]{2,1,0:T(8,128)(2,1)S(1)} %collective-permute-done.8.tile_ref.refs_8_), channel_id=1, source_target_pairs={{0,4},{1,5},{2,6},{3,7},{4,0},{5,1},{6,2},{7,3},{8,12},{9,13},{10,... | collective-permute-start | bytes 1572872 | tf_op jit(solution)/shard_map/ppermute | solution.py:359
  38.9 13.0 %collective-permute-start.11 = (bf16[2,128,512]{2,1,0:T(8,128)(2,1)S(1)}, bf16[2,128,512]{2,1,0:T(8,128)(2,1)S(1)}, u32[]{:S(2)}, u32[]{:S(2)}) collective-permute-start(bf16[2,128,512]{2,1,0:T(8,128)(2,1)S(1)} %get-tuple-element.76), channel_id=1, source_target_pairs={{0,3},{1,2},{2,1},{3,0},{4,7},{5,6},{6,5},{7,4},{8,11},{9,10},{10,... | collective-permute-start | bytes 786440 | tf_op jit(solution)/shard_map/ppermute | solution.py:370
  44.2 10.9 %collective-permute-start.10 = (bf16[2,128,512]{2,1,0:T(8,128)(2,1)S(1)}, bf16[2,128,512]{2,1,0:T(8,128)(2,1)S(1)}, u32[]{:S(2)}, u32[]{:S(2)}) collective-permute-start(bf16[2,128,512]{2,1,0:T(8,128)(2,1)S(1)} %get-tuple-element.74), channel_id=1, source_target_pairs={{0,2},{1,3},{2,0},{3,1},{4,6},{5,7},{6,4},{7,5},{8,10},{9,11},{10,... | collective-permute-start | bytes 786440 | tf_op jit(solution)/shard_map/ppermute | solution.py:370
  46.2 12.1 %copy-start.11 = (bf16[1,512,768]{2,1,0:T(8,128)(2,1)S(1)}, bf16[1,512,768]{2,1,0:T(8,128)(2,1)}, u32[]{:S(2)}) copy-start(bf16[1,512,768]{2,1,0:T(8,128)(2,1)} %param.8) | copy-start | bytes 2359300
  46.2 10.6 %collective-permute-start.9 = (bf16[2,128,512]{2,1,0:T(8,128)(2,1)S(1)}, bf16[2,128,512]{2,1,0:T(8,128)(2,1)S(1)}, u32[]{:S(2)}, u32[]{:S(2)}) collective-permute-start(bf16[2,128,512]{2,1,0:T(8,128)(2,1)S(1)} %get-tuple-element.72), channel_id=1, source_target_pairs={{0,1},{1,0},{2,3},{3,2},{4,5},{5,4},{6,7},{7,6},{8,9},{9,8},{10,11... | collective-permute-start | bytes 786440 | tf_op jit(solution)/shard_map/ppermute | solution.py:370
  51.3 8.8 %copy-start.6 = (bf16[4,128,512]{2,1,0:T(8,128)(2,1)}, bf16[4,128,512]{2,1,0:T(8,128)(2,1)S(1)}, u32[]{:S(2)}) copy-start(bf16[4,128,512]{2,1,0:T(8,128)(2,1)S(1)} %collective-permute-done.12.tile_ref.refs_12_) | copy-start | bytes 1572868
  51.9 10.2 %collective-permute-start.15 = (bf16[2,128,512]{2,1,0:T(8,128)(2,1)S(1)}, bf16[2,128,512]{2,1,0:T(8,128)(2,1)S(1)}, u32[]{:S(2)}, u32[]{:S(2)}) collective-permute-start(bf16[2,128,512]{2,1,0:T(8,128)(2,1)S(1)} %get-tuple-element.82), channel_id=1, source_target_pairs={{0,3},{1,2},{2,1},{3,0},{4,7},{5,6},{6,5},{7,4},{8,11},{9,10},{10,... | collective-permute-start | bytes 786440 | tf_op jit(solution)/shard_map/ppermute | solution.py:370
  55.1 11.3 %collective-permute-start.14 = (bf16[2,128,512]{2,1,0:T(8,128)(2,1)S(1)}, bf16[2,128,512]{2,1,0:T(8,128)(2,1)S(1)}, u32[]{:S(2)}, u32[]{:S(2)}) collective-permute-start(bf16[2,128,512]{2,1,0:T(8,128)(2,1)S(1)} %get-tuple-element.80), channel_id=1, source_target_pairs={{0,2},{1,3},{2,0},{3,1},{4,6},{5,7},{6,4},{7,5},{8,10},{9,11},{10,... | collective-permute-start | bytes 786440 | tf_op jit(solution)/shard_map/ppermute | solution.py:370
  56.8 9.8 %collective-permute-start.13 = (bf16[2,128,512]{2,1,0:T(8,128)(2,1)S(1)}, bf16[2,128,512]{2,1,0:T(8,128)(2,1)S(1)}, u32[]{:S(2)}, u32[]{:S(2)}) collective-permute-start(bf16[2,128,512]{2,1,0:T(8,128)(2,1)S(1)} %get-tuple-element.78), channel_id=1, source_target_pairs={{0,1},{1,0},{2,3},{3,2},{4,5},{5,4},{6,7},{7,6},{8,9},{9,8},{10,11... | collective-permute-start | bytes 786440 | tf_op jit(solution)/shard_map/ppermute | solution.py:370
  84.9 31.2 %collective-permute-start.18 = (bf16[8,128,512]{2,1,0:T(8,128)(2,1)}, bf16[8,128,512]{2,1,0:T(8,128)(2,1)S(1)}, u32[]{:S(2)}, u32[]{:S(2)}) collective-permute-start(bf16[8,128,512]{2,1,0:T(8,128)(2,1)} %get-tuple-element.92), channel_id=1, source_target_pairs={{0,4},{1,5},{2,6},{3,7},{4,0},{5,1},{6,2},{7,3},{8,12},{9,13},{10,... | collective-permute-start | bytes 3145736 | tf_op jit(solution)/shard_map/ppermute | solution.py:359
  85.6 19.4 %collective-permute-start.16 = (bf16[2,128,512]{2,1,0:T(8,128)(2,1)}, bf16[2,128,512]{2,1,0:T(8,128)(2,1)S(1)}, u32[]{:S(2)}, u32[]{:S(2)}) collective-permute-start(bf16[2,128,512]{2,1,0:T(8,128)(2,1)} %get-tuple-element.83), channel_id=1, source_target_pairs={{0,1},{1,0},{2,3},{3,2},{4,5},{5,4},{6,7},{7,6},{8,9},{9,8},{10,11... | collective-permute-start | bytes 786440 | tf_op jit(solution)/shard_map/ppermute | solution.py:370
  87.1 13.9 %collective-permute-start.20 = (bf16[2,128,512]{2,1,0:T(8,128)(2,1)}, bf16[2,128,512]{2,1,0:T(8,128)(2,1)S(1)}, u32[]{:S(2)}, u32[]{:S(2)}) collective-permute-start(bf16[2,128,512]{2,1,0:T(8,128)(2,1)} %get-tuple-element.97), channel_id=1, source_target_pairs={{0,2},{1,3},{2,0},{3,1},{4,6},{5,7},{6,4},{7,5},{8,10},{9,11},{10,... | collective-permute-start | bytes 786440 | tf_op jit(solution)/shard_map/ppermute | solution.py:370
  88.7 14.6 %collective-permute-start.23 = (bf16[2,128,512]{2,1,0:T(8,128)(2,1)}, bf16[2,128,512]{2,1,0:T(8,128)(2,1)S(1)}, u32[]{:S(2)}, u32[]{:S(2)}) collective-permute-start(bf16[2,128,512]{2,1,0:T(8,128)(2,1)} %get-tuple-element.102), channel_id=1, source_target_pairs={{0,3},{1,2},{2,1},{3,0},{4,7},{5,6},{6,5},{7,4},{8,11},{9,10},{10,... | collective-permute-start | bytes 786440 | tf_op jit(solution)/shard_map/ppermute | solution.py:370
  89.1 12.0 %copy-start.29 = (bf16[2,128,512]{2,1,0:T(8,128)(2,1)S(1)}, bf16[2,128,512]{2,1,0:T(8,128)(2,1)}, u32[]{:S(2)}) copy-start(bf16[2,128,512]{2,1,0:T(8,128)(2,1)} %get-tuple-element.98) | copy-start | bytes 786436
  89.1 14.2 %copy-start.27 = (bf16[2,128,512]{2,1,0:T(8,128)(2,1)S(1)}, bf16[2,128,512]{2,1,0:T(8,128)(2,1)}, u32[]{:S(2)}) copy-start(bf16[2,128,512]{2,1,0:T(8,128)(2,1)} %get-tuple-element.103) | copy-start | bytes 786436
  89.1 14.2 %copy-start.19 = (bf16[768,768]{1,0:T(8,128)(2,1)S(1)}, bf16[768,768]{1,0:T(8,128)(2,1)}, u32[]{:S(2)}) copy-start(bf16[768,768]{1,0:T(8,128)(2,1)} %param.13) | copy-start | bytes 3538948
  89.1 14.2 %copy-start.34 = (bf16[768,512]{1,0:T(8,128)(2,1)S(1)}, bf16[768,512]{1,0:T(8,128)(2,1)}, u32[]{:S(2)}) copy-start(bf16[768,512]{1,0:T(8,128)(2,1)} %get-tuple-element.85) | copy-start | bytes 2359300
  101.1 12.1 %collective-permute-start.21 = (bf16[2,128,512]{2,1,0:T(8,128)(2,1)S(1)}, bf16[2,128,512]{2,1,0:T(8,128)(2,1)S(1)}, u32[]{:S(2)}, u32[]{:S(2)}) collective-permute-start(bf16[2,128,512]{2,1,0:T(8,128)(2,1)S(1)} %copy-done.29), channel_id=1, source_target_pairs={{0,2},{1,3},{2,0},{3,1},{4,6},{5,7},{6,4},{7,5},{8,10},{9,11},{10,... | collective-permute-start | bytes 786440 | tf_op jit(solution)/shard_map/ppermute | solution.py:370
  103.3 12.8 %collective-permute-start.24 = (bf16[2,128,512]{2,1,0:T(8,128)(2,1)S(1)}, bf16[2,128,512]{2,1,0:T(8,128)(2,1)S(1)}, u32[]{:S(2)}, u32[]{:S(2)}) collective-permute-start(bf16[2,128,512]{2,1,0:T(8,128)(2,1)S(1)} %copy-done.27), channel_id=1, source_target_pairs={{0,3},{1,2},{2,1},{3,0},{4,7},{5,6},{6,5},{7,4},{8,11},{9,10},{10,... | collective-permute-start | bytes 786440 | tf_op jit(solution)/shard_map/ppermute | solution.py:370
  105.0 11.9 %collective-permute-start.17 = (bf16[2,128,512]{2,1,0:T(8,128)(2,1)S(1)}, bf16[2,128,512]{2,1,0:T(8,128)(2,1)S(1)}, u32[]{:S(2)}, u32[]{:S(2)}) collective-permute-start(bf16[2,128,512]{2,1,0:T(8,128)(2,1)S(1)} %copy-done.25), channel_id=1, source_target_pairs={{0,1},{1,0},{2,3},{3,2},{4,5},{5,4},{6,7},{7,6},{8,9},{9,8},{10,11... | collective-permute-start | bytes 786440 | tf_op jit(solution)/shard_map/ppermute | solution.py:370
  107.7 9.3 %copy-start.23 = (bf16[2,128,512]{2,1,0:T(8,128)(2,1)S(1)}, bf16[2,128,512]{2,1,0:T(8,128)(2,1)}, u32[]{:S(2)}) copy-start(bf16[2,128,512]{2,1,0:T(8,128)(2,1)} %get-tuple-element.94) | copy-start | bytes 786436
  107.7 10.8 %copy-start.10 = (bf16[2,128,512]{2,1,0:T(8,128)(2,1)S(1)}, bf16[2,128,512]{2,1,0:T(8,128)(2,1)}, u32[]{:S(2)}) copy-start(bf16[2,128,512]{2,1,0:T(8,128)(2,1)} %get-tuple-element.107.refs_0_) | copy-start | bytes 786436
  107.7 13.7 %collective-permute-start.26 = (bf16[4,128,512]{2,1,0:T(8,128)(2,1)S(1)}, bf16[4,128,512]{2,1,0:T(8,128)(2,1)S(1)}, u32[]{:S(2)}, u32[]{:S(2)}) collective-permute-start(bf16[4,128,512]{2,1,0:T(8,128)(2,1)S(1)} %owner_sum.4), channel_id=1, source_target_pairs={{0,4},{1,5},{2,6},{3,7},{4,0},{5,1},{6,2},{7,3},{8,12},{9,13},{10,... | collective-permute-start | bytes 1572872 | tf_op jit(solution)/shard_map/ppermute | solution.py:359
  113.1 10.5 %collective-permute-start.22 = (bf16[2,128,512]{2,1,0:T(8,128)(2,1)S(1)}, bf16[2,128,512]{2,1,0:T(8,128)(2,1)S(1)}, u32[]{:S(2)}, u32[]{:S(2)}) collective-permute-start(bf16[2,128,512]{2,1,0:T(8,128)(2,1)S(1)} %copy-done.24), channel_id=1, source_target_pairs={{0,2},{1,3},{2,0},{3,1},{4,6},{5,7},{6,4},{7,5},{8,10},{9,11},{10,... | collective-permute-start | bytes 786440 | tf_op jit(solution)/shard_map/ppermute | solution.py:370
  116.1 7.5 %collective-permute-start.25 = (bf16[2,128,512]{2,1,0:T(8,128)(2,1)}, bf16[2,128,512]{2,1,0:T(8,128)(2,1)S(1)}, u32[]{:S(2)}, u32[]{:S(2)}) collective-permute-start(bf16[2,128,512]{2,1,0:T(8,128)(2,1)} %get-tuple-element.104), channel_id=1, source_target_pairs={{0,3},{1,2},{2,1},{3,0},{4,7},{5,6},{6,5},{7,4},{8,11},{9,10},{10,... | collective-permute-start | bytes 786440 | tf_op jit(solution)/shard_map/ppermute | solution.py:370
  117.0 9.2 %collective-permute-start.19 = (bf16[2,128,512]{2,1,0:T(8,128)(2,1)S(1)}, bf16[2,128,512]{2,1,0:T(8,128)(2,1)S(1)}, u32[]{:S(2)}, u32[]{:S(2)}) collective-permute-start(bf16[2,128,512]{2,1,0:T(8,128)(2,1)S(1)} %copy-done.23), channel_id=1, source_target_pairs={{0,1},{1,0},{2,3},{3,2},{4,5},{5,4},{6,7},{7,6},{8,9},{9,8},{10,11... | collective-permute-start | bytes 786440 | tf_op jit(solution)/shard_map/ppermute | solution.py:370
  119.3 20.7 %copy-start.8 = (bf16[2,128,512]{2,1,0:T(8,128)(2,1)S(1)}, bf16[2,128,512]{2,1,0:T(8,128)(2,1)}, u32[]{:S(2)}) copy-start(bf16[2,128,512]{2,1,0:T(8,128)(2,1)} %get-tuple-element.87.refs_0_) | copy-start | bytes 786436
  122.3 26.1 %collective-permute-start.31 = (bf16[4,128,512]{2,1,0:T(8,128)(2,1)}, bf16[4,128,512]{2,1,0:T(8,128)(2,1)}, u32[]{:S(2)}, u32[]{:S(2)}) collective-permute-start(bf16[4,128,512]{2,1,0:T(8,128)(2,1)} %add_convert_fusion), channel_id=1, source_target_pairs={{0,24},{1,25},{2,26},{3,27},{4,28},{5,29},{6,30},{7,31},{8,16},{9,... | collective-permute-start | bytes 1572872 | tf_op jit(solution)/shard_map/ppermute | solution.py:359
  123.6 14.7 %collective-permute-start.28 = (bf16[2,128,512]{2,1,0:T(8,128)(2,1)}, bf16[2,128,512]{2,1,0:T(8,128)(2,1)S(1)}, u32[]{:S(2)}, u32[]{:S(2)}) collective-permute-start(bf16[2,128,512]{2,1,0:T(8,128)(2,1)} %get-tuple-element.113), channel_id=1, source_target_pairs={{0,2},{1,3},{2,0},{3,1},{4,6},{5,7},{6,4},{7,5},{8,10},{9,11},{10,... | collective-permute-start | bytes 786440 | tf_op jit(solution)/shard_map/ppermute | solution.py:370
  125.3 13.0 %collective-permute-start.29 = (bf16[2,128,512]{2,1,0:T(8,128)(2,1)}, bf16[2,128,512]{2,1,0:T(8,128)(2,1)S(1)}, u32[]{:S(2)}, u32[]{:S(2)}) collective-permute-start(bf16[2,128,512]{2,1,0:T(8,128)(2,1)} %get-tuple-element.116), channel_id=1, source_target_pairs={{0,3},{1,2},{2,1},{3,0},{4,7},{5,6},{6,5},{7,4},{8,11},{9,10},{10,... | collective-permute-start | bytes 786440 | tf_op jit(solution)/shard_map/ppermute | solution.py:370
  126.2 13.8 %collective-permute-start.27 = (bf16[2,128,512]{2,1,0:T(8,128)(2,1)S(1)}, bf16[2,128,512]{2,1,0:T(8,128)(2,1)S(1)}, u32[]{:S(2)}, u32[]{:S(2)}) collective-permute-start(bf16[2,128,512]{2,1,0:T(8,128)(2,1)S(1)} %get-tuple-element.110), channel_id=1, source_target_pairs={{0,1},{1,0},{2,3},{3,2},{4,5},{5,4},{6,7},{7,6},{8,9},{9,8},{10,11... | collective-permute-start | bytes 786440 | tf_op jit(solution)/shard_map/ppermute | solution.py:370
  140.0 8.4 %copy-start.2 = (bf16[768,256]{1,0:T(8,128)(2,1)S(1)}, bf16[768,256]{1,0:T(8,128)(2,1)}, u32[]{:S(2)}) copy-start(bf16[768,256]{1,0:T(8,128)(2,1)} %refs_3_.3) | copy-start | bytes 1179652
  140.0 8.4 %copy-start.9 = (f32[512,768]{1,0:T(8,128)S(1)}, f32[512,768]{1,0:T(8,128)}, u32[]{:S(2)}) copy-start(f32[512,768]{1,0:T(8,128)} %fusion.14.refs_1_) | copy-start | bytes 4718596
  141.0 9.1 %collective-permute-start.30 = (bf16[4,128,512]{2,1,0:T(8,128)(2,1)S(1)}, bf16[4,128,512]{2,1,0:T(8,128)(2,1)S(1)}, u32[]{:S(2)}, u32[]{:S(2)}) collective-permute-start(bf16[4,128,512]{2,1,0:T(8,128)(2,1)S(1)} %owner_sum.5), channel_id=1, source_target_pairs={{0,16},{1,17},{2,18},{3,19},{4,20},{5,21},{6,22},{7,23},{8,24},{9,... | collective-permute-start | bytes 1572872 | tf_op jit(solution)/shard_map/ppermute | solution.py:359
  (19 other events, 80.8 us)

commit v17 on v16

--- a/solution.py
+++ b/solution.py
@@ -431,7 +431,7 @@
         query_grad, w_query, (((0,), (1,)), ((), ())), preferred_element_type=F32
     )
     last = spread(back[2][1:])
-    last[0], query_term, layer_out = lax.optimization_barrier((last[0], query_term, layer_out))
+    last[1], query_term, layer_out = lax.optimization_barrier((last[1], query_term, layer_out))
     far = spread(back[1][1:], last)
     last_sum = owner_sum(3, wanted, [back[2][0], *last], block_count, BF16, 0)
     last_sum = swap(last_sum, 1, 0).astype(F32)

time: 152 us -> 152 us (level)
  waiting for transfers between devices: 56.2 us -> 59.8 us
  starting transfers between devices: 44.8 us -> 41.3 us
    ppermute x24, waiting for transfers between devices: 32.5 us -> 36.2 us  [spread(): moved.append(lax.ppermute(value, 'tile', pairs))]
    ppermute x8, starting transfers between devices: 10.8 us -> 8.18 us  [swap(): return lax.ppermute(value, ('vintage', 'tile'), pairs)]
  transfers between devices with their start and end apart: 32 -> 32, of which waited for: 15 -> 16; matrix products, arithmetic and copies ran while one was open for 12% -> 12% of each run, Pallas kernels for 5% -> 5%
where the time goes in v17:
time: 152 us
  waiting for transfers between devices  59.8 us (39%)
  starting transfers between devices  41.3 us (27%)
  Pallas kernels  30.1 us (20%)
  matrix products  10.2 us (7%)
  other arithmetic  5.22 us (3%)
  local copies, waits for them, and re-layouts  3.93 us (3%)
    ppermute x24, waiting for transfers between devices, spread(): moved.append(lax.ppermute(value, 'tile', pairs))  36.2 us
    ppermute x24, starting transfers between devices, spread(): moved.append(lax.ppermute(value, 'tile', pairs))  33.2 us
    ppermute x8, waiting for transfers between devices, swap(): return lax.ppermute(value, ('vintage', 'tile'), pairs)  23.6 us
    pallas_call x1, Pallas kernels, attention(): pl.pallas_call(functools.partial(attention_kernel, list_len, per_step, le...  17.6 us
    ppermute x8, starting transfers between devices, swap(): return lax.ppermute(value, ('vintage', 'tile'), pairs)  8.18 us
    dot_general x1, matrix products, dot_nt(): lax.dot_general(a, b, (((1,), (1,)), ((), ())), preferred_element_type=F32)  3.54 us
    pallas_call x1, Pallas kernels, project(): pl.pallas_call(project_kernel, in_specs=[pl.BlockSpec(memory_space=pl.ANY...  3.4 us
    dot_general x1, matrix products, shards(): lax.dot_general(query_grad, w_query, (((0,), (1,)), ((), ())), preferred_...  3.28 us
  transfers between devices with their start and end apart: 32, of which 16 were waited for; matrix products, arithmetic and copies ran while one was open for 12% of the time, Pallas kernels for 5%

profile of v17, /device:TPU:0, one launch (start us, length us, event | category | flops | bytes accessed | tf_op | source)
XLA Modules:
  0.0 151.6 jit_solution(1939749703570040842)
XLA Ops:
  0.7 3.4 %project.1 = bf16[512,512]{1,0:T(8,128)(2,1)} custom-call(bf16[512,768]{1,0:T(8,128)(2,1)} %bitcast.60, bf16[768,256]{1,0:T(8,128)(2,1)} %refs_2_.3, bf16[768,256]{1,0:T(8,128)(2,1)} %refs_3_.3), custom_call_target="tpu_custom_call" | custom-call | tf_op jit(solution)/shard_map/project/pallas_call | solution.py:258
  4.1 2.5 %collective-permute-start.4 = (bf16[4,128,512]{2,1,0:T(8,128)(2,1)}, bf16[4,128,512]{2,1,0:T(8,128)(2,1)S(1)}, u32[]{:S(2)}, u32[]{:S(2)}) collective-permute-start(bf16[4,128,512]{2,1,0:T(8,128)(2,1)} %bitcast.61), channel_id=1, source_target_pairs={{0,20},{1,21},{2,22},{3,23},{4,16},{5,17},{6,18},{7,19},{8,28},{9,... | collective-permute-start | bytes 1572872 | tf_op jit(solution)/shard_map/ppermute | solution.py:359
  8.8 0.8 convert_reduce_fusion
  10.4 2.3 %collective-permute-start.8 = (bf16[4,128,512]{2,1,0:T(8,128)(2,1)}, bf16[4,128,512]{2,1,0:T(8,128)(2,1)S(1)}, u32[]{:S(2)}, u32[]{:S(2)}) collective-permute-start(bf16[4,128,512]{2,1,0:T(8,128)(2,1)} %bitcast.63), channel_id=1, source_target_pairs={{0,24},{1,25},{2,26},{3,27},{4,28},{5,29},{6,30},{7,31},{8,16},{9,... | collective-permute-start | bytes 1572872 | tf_op jit(solution)/shard_map/ppermute | solution.py:359
  14.2 2.5 %collective-permute-start.3 = (bf16[2,128,512]{2,1,0:T(8,128)(2,1)S(1)}, bf16[2,128,512]{2,1,0:T(8,128)(2,1)S(1)}, u32[]{:S(2)}, u32[]{:S(2)}) collective-permute-start(bf16[2,128,512]{2,1,0:T(8,128)(2,1)S(1)} %get-tuple-element.62), channel_id=1, source_target_pairs={{0,3},{1,2},{2,1},{3,0},{4,7},{5,6},{6,5},{7,4},{8,11},{9,10},{10,... | collective-permute-start | bytes 786440 | tf_op jit(solution)/shard_map/ppermute | solution.py:370
  17.7 8.2 %collective-permute-done.4.tile_ref.refs_4_ = bf16[4,128,512]{2,1,0:T(8,128)(2,1)S(1)} collective-permute-done((bf16[4,128,512]{2,1,0:T(8,128)(2,1)}, bf16[4,128,512]{2,1,0:T(8,128)(2,1)S(1)}, u32[]{:S(2)}, u32[]{:S(2)}) %collective-permute-start.4) | collective-permute-done | bytes 524320 | tf_op jit(solution)/shard_map/ppermute | solution.py:359
  25.9 1.4 pack.5
  27.4 3.9 %collective-permute-start.7 = (bf16[2,128,512]{2,1,0:T(8,128)(2,1)}, bf16[2,128,512]{2,1,0:T(8,128)(2,1)}, u32[]{:S(2)}, u32[]{:S(2)}) collective-permute-start(bf16[2,128,512]{2,1,0:T(8,128)(2,1)} %get-tuple-element.68), channel_id=1, source_target_pairs={{0,3},{1,2},{2,1},{3,0},{4,7},{5,6},{6,5},{7,4},{8,11},{9,10},{10,... | collective-permute-start | bytes 786440 | tf_op jit(solution)/shard_map/ppermute | solution.py:370
  31.9 5.0 %collective-permute-done.8.tile_ref.refs_8_ = bf16[4,128,512]{2,1,0:T(8,128)(2,1)S(1)} collective-permute-done((bf16[4,128,512]{2,1,0:T(8,128)(2,1)}, bf16[4,128,512]{2,1,0:T(8,128)(2,1)S(1)}, u32[]{:S(2)}, u32[]{:S(2)}) %collective-permute-start.8) | collective-permute-done | bytes 524320 | tf_op jit(solution)/shard_map/ppermute | solution.py:359
  37.0 1.3 bitcast_select_fusion
  38.9 2.7 %collective-permute-start.11 = (bf16[2,128,512]{2,1,0:T(8,128)(2,1)S(1)}, bf16[2,128,512]{2,1,0:T(8,128)(2,1)S(1)}, u32[]{:S(2)}, u32[]{:S(2)}) collective-permute-start(bf16[2,128,512]{2,1,0:T(8,128)(2,1)S(1)} %get-tuple-element.76), channel_id=1, source_target_pairs={{0,3},{1,2},{2,1},{3,0},{4,7},{5,6},{6,5},{7,4},{8,11},{9,10},{10,... | collective-permute-start | bytes 786440 | tf_op jit(solution)/shard_map/ppermute | solution.py:370
  41.6 2.6 %collective-permute-done.6.refs_6_ = bf16[2,128,512]{2,1,0:T(8,128)(2,1)} collective-permute-done((bf16[2,128,512]{2,1,0:T(8,128)(2,1)}, bf16[2,128,512]{2,1,0:T(8,128)(2,1)}, u32[]{:S(2)}, u32[]{:S(2)}) %collective-permute-start.6) | collective-permute-done | bytes 262176 | tf_op jit(solution)/shard_map/ppermute | solution.py:370
  44.2 2.0 %collective-permute-start.10 = (bf16[2,128,512]{2,1,0:T(8,128)(2,1)S(1)}, bf16[2,128,512]{2,1,0:T(8,128)(2,1)S(1)}, u32[]{:S(2)}, u32[]{:S(2)}) collective-permute-start(bf16[2,128,512]{2,1,0:T(8,128)(2,1)S(1)} %get-tuple-element.74), channel_id=1, source_target_pairs={{0,2},{1,3},{2,0},{3,1},{4,6},{5,7},{6,4},{7,5},{8,10},{9,11},{10,... | collective-permute-start | bytes 786440 | tf_op jit(solution)/shard_map/ppermute | solution.py:370
  46.4 3.5 %fusion.ng_ref = f32[768,512]{1,0:T(8,128)} fusion(bf16[768,768]{1,0:T(8,128)(2,1)} %param.13, bf16[1,512,768]{2,1,0:T(8,128)(2,1)} %param.9), kind=kOutput, calls=%fused_computation.5 | convolution fusion | flops 603979776 | bytes 3538944 | tf_op jit(solution)/shard_map/dot_general | solution.py:34
  49.9 1.4 collective-permute-done.12.tile_ref.refs_12_
  51.9 2.5 %collective-permute-start.15 = (bf16[2,128,512]{2,1,0:T(8,128)(2,1)S(1)}, bf16[2,128,512]{2,1,0:T(8,128)(2,1)S(1)}, u32[]{:S(2)}, u32[]{:S(2)}) collective-permute-start(bf16[2,128,512]{2,1,0:T(8,128)(2,1)S(1)} %get-tuple-element.82), channel_id=1, source_target_pairs={{0,3},{1,2},{2,1},{3,0},{4,7},{5,6},{6,5},{7,4},{8,11},{9,10},{10,... | collective-permute-start | bytes 786440 | tf_op jit(solution)/shard_map/ppermute | solution.py:370
  55.1 1.8 %collective-permute-start.14 = (bf16[2,128,512]{2,1,0:T(8,128)(2,1)S(1)}, bf16[2,128,512]{2,1,0:T(8,128)(2,1)S(1)}, u32[]{:S(2)}, u32[]{:S(2)}) collective-permute-start(bf16[2,128,512]{2,1,0:T(8,128)(2,1)S(1)} %get-tuple-element.80), channel_id=1, source_target_pairs={{0,2},{1,3},{2,0},{3,1},{4,6},{5,7},{6,4},{7,5},{8,10},{9,11},{10,... | collective-permute-start | bytes 786440 | tf_op jit(solution)/shard_map/ppermute | solution.py:370
  56.8 1.5 collective-permute-start.13
  58.3 1.7 %convolution_convert_fusion.1.q_ref = bf16[768,512]{1,0:T(8,128)(2,1)} fusion(bf16[768,768]{1,0:T(8,128)(2,1)S(1)} %copy-done, bf16[1,512,768]{2,1,0:T(8,128)(2,1)S(1)} %copy-done.11), kind=kOutput, calls=%fused_computation.3 | convolution fusion | flops 604372992 | bytes 2752512 | tf_op jit(solution)/shard_map/dot_general | solution.py:418
  60.1 2.0 %collective-permute-done.15.refs_15_ = bf16[2,128,512]{2,1,0:T(8,128)(2,1)S(1)} collective-permute-done((bf16[2,128,512]{2,1,0:T(8,128)(2,1)S(1)}, bf16[2,128,512]{2,1,0:T(8,128)(2,1)S(1)}, u32[]{:S(2)}, u32[]{:S(2)}) %collective-permute-start.15) | collective-permute-done | bytes 262176 | tf_op jit(solution)/shard_map/ppermute | solution.py:370
  62.1 4.3 %collective-permute-done.14.refs_14_ = bf16[2,128,512]{2,1,0:T(8,128)(2,1)S(1)} collective-permute-done((bf16[2,128,512]{2,1,0:T(8,128)(2,1)S(1)}, bf16[2,128,512]{2,1,0:T(8,128)(2,1)S(1)}, u32[]{:S(2)}, u32[]{:S(2)}) %collective-permute-start.14) | collective-permute-done | bytes 262176 | tf_op jit(solution)/shard_map/ppermute | solution.py:370
  67.3 17.6 %attention.1 = (bf16[768,512]{1,0:T(8,128)(2,1)}, bf16[768,512]{1,0:T(8,128)(2,1)}, bf16[2,128,512]{2,1,0:T(8,128)(2,1)}, bf16[2,128,512]{2,1,0:T(8,128)(2,1)}, ...) custom-call(s32[16]{0:T(128)} %get-tuple-element.136.get_ref, ...), custom_call_target="tpu_custom_call" | custom-call | flops 2415919104 | bytes 6291456 | tf_op jit(solution)/shard_map/attention/pallas_call | solution.py:210
  85.6 1.5 %collective-permute-start.16 = (bf16[2,128,512]{2,1,0:T(8,128)(2,1)}, bf16[2,128,512]{2,1,0:T(8,128)(2,1)S(1)}, u32[]{:S(2)}, u32[]{:S(2)}) collective-permute-start(bf16[2,128,512]{2,1,0:T(8,128)(2,1)} %get-tuple-element.83), channel_id=1, source_target_pairs={{0,2},{1,3},{2,0},{3,1},{4,6},{5,7},{6,4},{7,5},{8,10},{9,11},{10,... | collective-permute-start | bytes 786440 | tf_op jit(solution)/shard_map/ppermute | solution.py:370
  87.1 1.5 collective-permute-start.17
  89.1 3.3 %fusion.14.refs_1_ = f32[512,768]{1,0:T(8,128)} fusion(bf16[768,512]{1,0:T(8,128)(2,1)} %get-tuple-element.84, bf16[768,768]{1,0:T(8,128)(2,1)S(1)} %copy-done), kind=kOutput, calls=%fused_computation.52 | convolution fusion | flops 603979776 | bytes 3538944 | tf_op jit(solution)/shard_map/dot_general | solution.py:430
  92.4 1.7 %convolution_convert_fusion = bf16[512,768]{1,0:T(8,128)(2,1)} fusion(bf16[768,512]{1,0:T(8,128)(2,1)S(1)} %copy-done.34, bf16[768,768]{1,0:T(8,128)(2,1)S(1)} %copy-done.19), kind=kOutput, calls=%fused_computation.2 | convolution fusion | flops 604372992 | bytes 2752512 | tf_op jit(solution)/shard_map/dot_general | solution.py:38
  94.1 6.4 %collective-permute-done.23.refs_3_ = bf16[2,128,512]{2,1,0:T(8,128)(2,1)S(1)} collective-permute-done((bf16[2,128,512]{2,1,0:T(8,128)(2,1)}, bf16[2,128,512]{2,1,0:T(8,128)(2,1)S(1)}, u32[]{:S(2)}, u32[]{:S(2)}) %collective-permute-start.23) | collective-permute-done | bytes 262176 | tf_op jit(solution)/shard_map/ppermute | solution.py:370
  100.5 2.5 %collective-permute-start.24 = (bf16[2,128,512]{2,1,0:T(8,128)(2,1)S(1)}, bf16[2,128,512]{2,1,0:T(8,128)(2,1)S(1)}, u32[]{:S(2)}, u32[]{:S(2)}) collective-permute-start(bf16[2,128,512]{2,1,0:T(8,128)(2,1)S(1)} %copy-done.29), channel_id=1, source_target_pairs={{0,3},{1,2},{2,1},{3,0},{4,7},{5,6},{6,5},{7,4},{8,11},{9,10},{10,... | collective-permute-start | bytes 786440 | tf_op jit(solution)/shard_map/ppermute | solution.py:370
  104.0 1.0 owner_sum.4
  105.0 1.3 collective-permute-start.26
  106.4 4.3 %collective-permute-done.24.refs_3_ = bf16[2,128,512]{2,1,0:T(8,128)(2,1)S(1)} collective-permute-done((bf16[2,128,512]{2,1,0:T(8,128)(2,1)S(1)}, bf16[2,128,512]{2,1,0:T(8,128)(2,1)S(1)}, u32[]{:S(2)}, u32[]{:S(2)}) %collective-permute-start.24) | collective-permute-done | bytes 262176 | tf_op jit(solution)/shard_map/ppermute | solution.py:370
  110.7 2.4 %collective-permute-start.25 = (bf16[2,128,512]{2,1,0:T(8,128)(2,1)}, bf16[2,128,512]{2,1,0:T(8,128)(2,1)S(1)}, u32[]{:S(2)}, u32[]{:S(2)}) collective-permute-start(bf16[2,128,512]{2,1,0:T(8,128)(2,1)} %get-tuple-element.104), channel_id=1, source_target_pairs={{0,3},{1,2},{2,1},{3,0},{4,7},{5,6},{6,5},{7,4},{8,11},{9,10},{10,... | collective-permute-start | bytes 786440 | tf_op jit(solution)/shard_map/ppermute | solution.py:370
  113.1 3.1 %collective-permute-done.21.refs_2_ = bf16[2,128,512]{2,1,0:T(8,128)(2,1)S(1)} collective-permute-done((bf16[2,128,512]{2,1,0:T(8,128)(2,1)S(1)}, bf16[2,128,512]{2,1,0:T(8,128)(2,1)S(1)}, u32[]{:S(2)}, u32[]{:S(2)}) %collective-permute-start.21) | collective-permute-done | bytes 262176 | tf_op jit(solution)/shard_map/ppermute | solution.py:370
  116.3 1.5 collective-permute-start.22
  117.8 0.9 fusion.13
  118.7 0.8 owner_sum.3
  119.5 1.9 %collective-permute-done.26 = bf16[4,128,512]{2,1,0:T(8,128)(2,1)S(1)} collective-permute-done((bf16[4,128,512]{2,1,0:T(8,128)(2,1)S(1)}, bf16[4,128,512]{2,1,0:T(8,128)(2,1)S(1)}, u32[]{:S(2)}, u32[]{:S(2)}) %collective-permute-start.26) | collective-permute-done | bytes 524320 | tf_op jit(solution)/shard_map/ppermute | solution.py:359
  121.4 0.9 add_convert_fusion
  123.1 1.9 %collective-permute-done.22.refs_2_ = bf16[2,128,512]{2,1,0:T(8,128)(2,1)S(1)} collective-permute-done((bf16[2,128,512]{2,1,0:T(8,128)(2,1)S(1)}, bf16[2,128,512]{2,1,0:T(8,128)(2,1)S(1)}, u32[]{:S(2)}, u32[]{:S(2)}) %collective-permute-start.22) | collective-permute-done | bytes 262176 | tf_op jit(solution)/shard_map/ppermute | solution.py:370
  125.0 1.6 %collective-permute-start.28 = (bf16[2,128,512]{2,1,0:T(8,128)(2,1)}, bf16[2,128,512]{2,1,0:T(8,128)(2,1)S(1)}, u32[]{:S(2)}, u32[]{:S(2)}) collective-permute-start(bf16[2,128,512]{2,1,0:T(8,128)(2,1)} %get-tuple-element.113), channel_id=1, source_target_pairs={{0,2},{1,3},{2,0},{3,1},{4,6},{5,7},{6,4},{7,5},{8,10},{9,11},{10,... | collective-permute-start | bytes 786440 | tf_op jit(solution)/shard_map/ppermute | solution.py:370
  126.6 1.4 collective-permute-start.29
  128.5 0.7 gather_fusion.1
  129.6 9.2 %collective-permute-done.28.refs_6_ = bf16[2,128,512]{2,1,0:T(8,128)(2,1)S(1)} collective-permute-done((bf16[2,128,512]{2,1,0:T(8,128)(2,1)}, bf16[2,128,512]{2,1,0:T(8,128)(2,1)S(1)}, u32[]{:S(2)}, u32[]{:S(2)}) %collective-permute-start.28) | collective-permute-done | bytes 262176 | tf_op jit(solution)/shard_map/ppermute | solution.py:370
  138.8 1.4 collective-permute-done.27.refs_5_
  140.2 0.9 owner_sum.5
  141.2 7.2 %collective-permute-done.31 = bf16[4,128,512]{2,1,0:T(8,128)(2,1)} collective-permute-done((bf16[4,128,512]{2,1,0:T(8,128)(2,1)}, bf16[4,128,512]{2,1,0:T(8,128)(2,1)}, u32[]{:S(2)}, u32[]{:S(2)}) %collective-permute-start.31) | collective-permute-done | bytes 524320 | tf_op jit(solution)/shard_map/ppermute | solution.py:359
  148.4 1.7 %finish.2.refs_1_ = f32[512,768]{1,0:T(8,128)S(1)} custom-call(bf16[512,512]{1,0:T(8,128)(2,1)} %bitcast.20.refs_0_, f32[512,768]{1,0:T(8,128)S(1)} %copy-done.9, bf16[768,256]{1,0:T(8,128)(2,1)S(1)} %copy-done.1, bf16[768,256]{1,0:T(8,128)(2,1)S(1)} %copy-done.2), custom_call_target="tpu_custom_call" | custom-call | flops 20000000000 | bytes 1572864 | tf_op jit(solution)/shard_map/finish/pallas_call | solution.py:299
  150.1 1.5 finish.3
  (130 shorter events, 13.1 us)
Async XLA Ops:
  0.6 57.7 %copy-start = (bf16[768,768]{1,0:T(8,128)(2,1)S(1)}, bf16[768,768]{1,0:T(8,128)(2,1)}, u32[]{:S(2)}) copy-start(bf16[768,768]{1,0:T(8,128)(2,1)} %param.10) | copy-start | bytes 3538948
  4.1 21.9 %collective-permute-start.4 = (bf16[4,128,512]{2,1,0:T(8,128)(2,1)}, bf16[4,128,512]{2,1,0:T(8,128)(2,1)S(1)}, u32[]{:S(2)}, u32[]{:S(2)}) collective-permute-start(bf16[4,128,512]{2,1,0:T(8,128)(2,1)} %bitcast.61), channel_id=1, source_target_pairs={{0,20},{1,21},{2,22},{3,23},{4,16},{5,17},{6,18},{7,19},{8,28},{9,... | collective-permute-start | bytes 1572872 | tf_op jit(solution)/shard_map/ppermute | solution.py:359
  6.6 3.8 %collective-permute-start = (bf16[4,128,512]{2,1,0:T(8,128)(2,1)}, bf16[4,128,512]{2,1,0:T(8,128)(2,1)S(1)}, u32[]{:S(2)}, u32[]{:S(2)}) collective-permute-start(bf16[4,128,512]{2,1,0:T(8,128)(2,1)} %bitcast.62), channel_id=1, source_target_pairs={{0,16},{1,17},{2,18},{3,19},{4,20},{5,21},{6,22},{7,23},{8,24},{9,... | collective-permute-start | bytes 1572872 | tf_op jit(solution)/shard_map/ppermute | solution.py:359
  10.4 39.5 %copy-start.4 = (bf16[4,128,512]{2,1,0:T(8,128)(2,1)}, bf16[4,128,512]{2,1,0:T(8,128)(2,1)S(1)}, u32[]{:S(2)}) copy-start(bf16[4,128,512]{2,1,0:T(8,128)(2,1)S(1)} %collective-permute-done.tile_ref.refs_0_) | copy-start | bytes 1572868
  10.4 26.4 %collective-permute-start.8 = (bf16[4,128,512]{2,1,0:T(8,128)(2,1)}, bf16[4,128,512]{2,1,0:T(8,128)(2,1)S(1)}, u32[]{:S(2)}, u32[]{:S(2)}) collective-permute-start(bf16[4,128,512]{2,1,0:T(8,128)(2,1)} %bitcast.63), channel_id=1, source_target_pairs={{0,24},{1,25},{2,26},{3,27},{4,28},{5,29},{6,30},{7,31},{8,16},{9,... | collective-permute-start | bytes 1572872 | tf_op jit(solution)/shard_map/ppermute | solution.py:359
  14.2 13.2 %collective-permute-start.3 = (bf16[2,128,512]{2,1,0:T(8,128)(2,1)S(1)}, bf16[2,128,512]{2,1,0:T(8,128)(2,1)S(1)}, u32[]{:S(2)}, u32[]{:S(2)}) collective-permute-start(bf16[2,128,512]{2,1,0:T(8,128)(2,1)S(1)} %get-tuple-element.62), channel_id=1, source_target_pairs={{0,3},{1,2},{2,1},{3,0},{4,7},{5,6},{6,5},{7,4},{8,11},{9,10},{10,... | collective-permute-start | bytes 786440 | tf_op jit(solution)/shard_map/ppermute | solution.py:370
  16.7 14.5 %collective-permute-start.2 = (bf16[2,128,512]{2,1,0:T(8,128)(2,1)S(1)}, bf16[2,128,512]{2,1,0:T(8,128)(2,1)S(1)}, u32[]{:S(2)}, u32[]{:S(2)}) collective-permute-start(bf16[2,128,512]{2,1,0:T(8,128)(2,1)S(1)} %get-tuple-element.61), channel_id=1, source_target_pairs={{0,2},{1,3},{2,0},{3,1},{4,6},{5,7},{6,4},{7,5},{8,10},{9,11},{10,... | collective-permute-start | bytes 786440 | tf_op jit(solution)/shard_map/ppermute | solution.py:370
  17.2 14.6 %collective-permute-start.1 = (bf16[2,128,512]{2,1,0:T(8,128)(2,1)S(1)}, bf16[2,128,512]{2,1,0:T(8,128)(2,1)S(1)}, u32[]{:S(2)}, u32[]{:S(2)}) collective-permute-start(bf16[2,128,512]{2,1,0:T(8,128)(2,1)S(1)} %get-tuple-element.60), channel_id=1, source_target_pairs={{0,1},{1,0},{2,3},{3,2},{4,5},{5,4},{6,7},{7,6},{8,9},{9,8},{10,11... | collective-permute-start | bytes 786440 | tf_op jit(solution)/shard_map/ppermute | solution.py:370
  25.9 24.0 %copy-start.3 = (bf16[4,128,512]{2,1,0:T(8,128)(2,1)}, bf16[4,128,512]{2,1,0:T(8,128)(2,1)S(1)}, u32[]{:S(2)}) copy-start(bf16[4,128,512]{2,1,0:T(8,128)(2,1)S(1)} %collective-permute-done.4.tile_ref.refs_4_) | copy-start | bytes 1572868
  27.4 9.5 %copy-start.20 = (bf16[2,128,512]{2,1,0:T(8,128)(2,1)}, bf16[2,128,512]{2,1,0:T(8,128)(2,1)S(1)}, u32[]{:S(2)}) copy-start(bf16[2,128,512]{2,1,0:T(8,128)(2,1)S(1)} %collective-permute-done.3.refs_3_) | copy-start | bytes 786436
  27.4 11.5 %collective-permute-start.7 = (bf16[2,128,512]{2,1,0:T(8,128)(2,1)}, bf16[2,128,512]{2,1,0:T(8,128)(2,1)}, u32[]{:S(2)}, u32[]{:S(2)}) collective-permute-start(bf16[2,128,512]{2,1,0:T(8,128)(2,1)} %get-tuple-element.68), channel_id=1, source_target_pairs={{0,3},{1,2},{2,1},{3,0},{4,7},{5,6},{6,5},{7,4},{8,11},{9,10},{10,... | collective-permute-start | bytes 786440 | tf_op jit(solution)/shard_map/ppermute | solution.py:370
  31.2 13.0 %collective-permute-start.6 = (bf16[2,128,512]{2,1,0:T(8,128)(2,1)}, bf16[2,128,512]{2,1,0:T(8,128)(2,1)}, u32[]{:S(2)}, u32[]{:S(2)}) collective-permute-start(bf16[2,128,512]{2,1,0:T(8,128)(2,1)} %get-tuple-element.66), channel_id=1, source_target_pairs={{0,2},{1,3},{2,0},{3,1},{4,6},{5,7},{6,4},{7,5},{8,10},{9,11},{10,... | collective-permute-start | bytes 786440 | tf_op jit(solution)/shard_map/ppermute | solution.py:370
  31.8 14.5 %collective-permute-start.5 = (bf16[2,128,512]{2,1,0:T(8,128)(2,1)S(1)}, bf16[2,128,512]{2,1,0:T(8,128)(2,1)}, u32[]{:S(2)}, u32[]{:S(2)}) collective-permute-start(bf16[2,128,512]{2,1,0:T(8,128)(2,1)S(1)} %get-tuple-element.64), channel_id=1, source_target_pairs={{0,1},{1,0},{2,3},{3,2},{4,5},{5,4},{6,7},{7,6},{8,9},{9,8},{10,11... | collective-permute-start | bytes 786440 | tf_op jit(solution)/shard_map/ppermute | solution.py:370
  36.9 13.0 %copy-start.5 = (bf16[4,128,512]{2,1,0:T(8,128)(2,1)}, bf16[4,128,512]{2,1,0:T(8,128)(2,1)S(1)}, u32[]{:S(2)}) copy-start(bf16[4,128,512]{2,1,0:T(8,128)(2,1)S(1)} %collective-permute-done.8.tile_ref.refs_8_) | copy-start | bytes 1572868
  36.9 14.4 %collective-permute-start.12 = (bf16[4,128,512]{2,1,0:T(8,128)(2,1)S(1)}, bf16[4,128,512]{2,1,0:T(8,128)(2,1)S(1)}, u32[]{:S(2)}, u32[]{:S(2)}) collective-permute-start(bf16[4,128,512]{2,1,0:T(8,128)(2,1)S(1)} %collective-permute-done.8.tile_ref.refs_8_), channel_id=1, source_target_pairs={{0,4},{1,5},{2,6},{3,7},{4,0},{5,1},{6,2},{7,3},{8,12},{9,13},{10,... | collective-permute-start | bytes 1572872 | tf_op jit(solution)/shard_map/ppermute | solution.py:359
  38.9 13.0 %collective-permute-start.11 = (bf16[2,128,512]{2,1,0:T(8,128)(2,1)S(1)}, bf16[2,128,512]{2,1,0:T(8,128)(2,1)S(1)}, u32[]{:S(2)}, u32[]{:S(2)}) collective-permute-start(bf16[2,128,512]{2,1,0:T(8,128)(2,1)S(1)} %get-tuple-element.76), channel_id=1, source_target_pairs={{0,3},{1,2},{2,1},{3,0},{4,7},{5,6},{6,5},{7,4},{8,11},{9,10},{10,... | collective-permute-start | bytes 786440 | tf_op jit(solution)/shard_map/ppermute | solution.py:370
  44.2 10.9 %collective-permute-start.10 = (bf16[2,128,512]{2,1,0:T(8,128)(2,1)S(1)}, bf16[2,128,512]{2,1,0:T(8,128)(2,1)S(1)}, u32[]{:S(2)}, u32[]{:S(2)}) collective-permute-start(bf16[2,128,512]{2,1,0:T(8,128)(2,1)S(1)} %get-tuple-element.74), channel_id=1, source_target_pairs={{0,2},{1,3},{2,0},{3,1},{4,6},{5,7},{6,4},{7,5},{8,10},{9,11},{10,... | collective-permute-start | bytes 786440 | tf_op jit(solution)/shard_map/ppermute | solution.py:370
  46.2 12.1 %copy-start.11 = (bf16[1,512,768]{2,1,0:T(8,128)(2,1)S(1)}, bf16[1,512,768]{2,1,0:T(8,128)(2,1)}, u32[]{:S(2)}) copy-start(bf16[1,512,768]{2,1,0:T(8,128)(2,1)} %param.8) | copy-start | bytes 2359300
  46.2 10.6 %collective-permute-start.9 = (bf16[2,128,512]{2,1,0:T(8,128)(2,1)S(1)}, bf16[2,128,512]{2,1,0:T(8,128)(2,1)S(1)}, u32[]{:S(2)}, u32[]{:S(2)}) collective-permute-start(bf16[2,128,512]{2,1,0:T(8,128)(2,1)S(1)} %get-tuple-element.72), channel_id=1, source_target_pairs={{0,1},{1,0},{2,3},{3,2},{4,5},{5,4},{6,7},{7,6},{8,9},{9,8},{10,11... | collective-permute-start | bytes 786440 | tf_op jit(solution)/shard_map/ppermute | solution.py:370
  51.3 8.8 %copy-start.6 = (bf16[4,128,512]{2,1,0:T(8,128)(2,1)}, bf16[4,128,512]{2,1,0:T(8,128)(2,1)S(1)}, u32[]{:S(2)}) copy-start(bf16[4,128,512]{2,1,0:T(8,128)(2,1)S(1)} %collective-permute-done.12.tile_ref.refs_12_) | copy-start | bytes 1572868
  51.9 10.2 %collective-permute-start.15 = (bf16[2,128,512]{2,1,0:T(8,128)(2,1)S(1)}, bf16[2,128,512]{2,1,0:T(8,128)(2,1)S(1)}, u32[]{:S(2)}, u32[]{:S(2)}) collective-permute-start(bf16[2,128,512]{2,1,0:T(8,128)(2,1)S(1)} %get-tuple-element.82), channel_id=1, source_target_pairs={{0,3},{1,2},{2,1},{3,0},{4,7},{5,6},{6,5},{7,4},{8,11},{9,10},{10,... | collective-permute-start | bytes 786440 | tf_op jit(solution)/shard_map/ppermute | solution.py:370
  55.1 11.3 %collective-permute-start.14 = (bf16[2,128,512]{2,1,0:T(8,128)(2,1)S(1)}, bf16[2,128,512]{2,1,0:T(8,128)(2,1)S(1)}, u32[]{:S(2)}, u32[]{:S(2)}) collective-permute-start(bf16[2,128,512]{2,1,0:T(8,128)(2,1)S(1)} %get-tuple-element.80), channel_id=1, source_target_pairs={{0,2},{1,3},{2,0},{3,1},{4,6},{5,7},{6,4},{7,5},{8,10},{9,11},{10,... | collective-permute-start | bytes 786440 | tf_op jit(solution)/shard_map/ppermute | solution.py:370
  56.8 9.8 %collective-permute-start.13 = (bf16[2,128,512]{2,1,0:T(8,128)(2,1)S(1)}, bf16[2,128,512]{2,1,0:T(8,128)(2,1)S(1)}, u32[]{:S(2)}, u32[]{:S(2)}) collective-permute-start(bf16[2,128,512]{2,1,0:T(8,128)(2,1)S(1)} %get-tuple-element.78), channel_id=1, source_target_pairs={{0,1},{1,0},{2,3},{3,2},{4,5},{5,4},{6,7},{7,6},{8,9},{9,8},{10,11... | collective-permute-start | bytes 786440 | tf_op jit(solution)/shard_map/ppermute | solution.py:370
  84.9 32.8 %collective-permute-start.19 = (bf16[8,128,512]{2,1,0:T(8,128)(2,1)}, bf16[8,128,512]{2,1,0:T(8,128)(2,1)S(1)}, u32[]{:S(2)}, u32[]{:S(2)}) collective-permute-start(bf16[8,128,512]{2,1,0:T(8,128)(2,1)} %get-tuple-element.92), channel_id=1, source_target_pairs={{0,4},{1,5},{2,6},{3,7},{4,0},{5,1},{6,2},{7,3},{8,12},{9,13},{10,... | collective-permute-start | bytes 3145736 | tf_op jit(solution)/shard_map/ppermute | solution.py:359
  85.6 17.4 %collective-permute-start.16 = (bf16[2,128,512]{2,1,0:T(8,128)(2,1)}, bf16[2,128,512]{2,1,0:T(8,128)(2,1)S(1)}, u32[]{:S(2)}, u32[]{:S(2)}) collective-permute-start(bf16[2,128,512]{2,1,0:T(8,128)(2,1)} %get-tuple-element.83), channel_id=1, source_target_pairs={{0,2},{1,3},{2,0},{3,1},{4,6},{5,7},{6,4},{7,5},{8,10},{9,11},{10,... | collective-permute-start | bytes 786440 | tf_op jit(solution)/shard_map/ppermute | solution.py:370
  87.1 16.4 %collective-permute-start.17 = (bf16[2,128,512]{2,1,0:T(8,128)(2,1)}, bf16[2,128,512]{2,1,0:T(8,128)(2,1)S(1)}, u32[]{:S(2)}, u32[]{:S(2)}) collective-permute-start(bf16[2,128,512]{2,1,0:T(8,128)(2,1)} %get-tuple-element.90), channel_id=1, source_target_pairs={{0,1},{1,0},{2,3},{3,2},{4,5},{5,4},{6,7},{7,6},{8,9},{9,8},{10,11... | collective-permute-start | bytes 786440 | tf_op jit(solution)/shard_map/ppermute | solution.py:370
  88.6 11.9 %collective-permute-start.23 = (bf16[2,128,512]{2,1,0:T(8,128)(2,1)}, bf16[2,128,512]{2,1,0:T(8,128)(2,1)S(1)}, u32[]{:S(2)}, u32[]{:S(2)}) collective-permute-start(bf16[2,128,512]{2,1,0:T(8,128)(2,1)} %get-tuple-element.102), channel_id=1, source_target_pairs={{0,3},{1,2},{2,1},{3,0},{4,7},{5,6},{6,5},{7,4},{8,11},{9,10},{10,... | collective-permute-start | bytes 786440 | tf_op jit(solution)/shard_map/ppermute | solution.py:370
  92.4 10.6 %copy-start.27 = (bf16[2,128,512]{2,1,0:T(8,128)(2,1)S(1)}, bf16[2,128,512]{2,1,0:T(8,128)(2,1)}, u32[]{:S(2)}) copy-start(bf16[2,128,512]{2,1,0:T(8,128)(2,1)} %get-tuple-element.98) | copy-start | bytes 786436
  92.4 11.2 %copy-start.25 = (bf16[2,128,512]{2,1,0:T(8,128)(2,1)S(1)}, bf16[2,128,512]{2,1,0:T(8,128)(2,1)}, u32[]{:S(2)}) copy-start(bf16[2,128,512]{2,1,0:T(8,128)(2,1)} %get-tuple-element.91) | copy-start | bytes 786436
  92.4 11.7 %copy-start.7 = (bf16[2,128,512]{2,1,0:T(8,128)(2,1)S(1)}, bf16[2,128,512]{2,1,0:T(8,128)(2,1)}, u32[]{:S(2)}) copy-start(bf16[2,128,512]{2,1,0:T(8,128)(2,1)} %get-tuple-element.108.refs_0_) | copy-start | bytes 786436
  94.1 22.2 %copy-start.24 = (bf16[2,128,512]{2,1,0:T(8,128)(2,1)S(1)}, bf16[2,128,512]{2,1,0:T(8,128)(2,1)}, u32[]{:S(2)}) copy-start(bf16[2,128,512]{2,1,0:T(8,128)(2,1)} %get-tuple-element.99) | copy-start | bytes 786436
  100.5 10.2 %collective-permute-start.24 = (bf16[2,128,512]{2,1,0:T(8,128)(2,1)S(1)}, bf16[2,128,512]{2,1,0:T(8,128)(2,1)S(1)}, u32[]{:S(2)}, u32[]{:S(2)}) collective-permute-start(bf16[2,128,512]{2,1,0:T(8,128)(2,1)S(1)} %copy-done.29), channel_id=1, source_target_pairs={{0,3},{1,2},{2,1},{3,0},{4,7},{5,6},{6,5},{7,4},{8,11},{9,10},{10,... | collective-permute-start | bytes 786440 | tf_op jit(solution)/shard_map/ppermute | solution.py:370
  103.0 13.3 %collective-permute-start.21 = (bf16[2,128,512]{2,1,0:T(8,128)(2,1)S(1)}, bf16[2,128,512]{2,1,0:T(8,128)(2,1)S(1)}, u32[]{:S(2)}, u32[]{:S(2)}) collective-permute-start(bf16[2,128,512]{2,1,0:T(8,128)(2,1)S(1)} %copy-done.27), channel_id=1, source_target_pairs={{0,2},{1,3},{2,0},{3,1},{4,6},{5,7},{6,4},{7,5},{8,10},{9,11},{10,... | collective-permute-start | bytes 786440 | tf_op jit(solution)/shard_map/ppermute | solution.py:370
  103.5 15.1 %collective-permute-start.18 = (bf16[2,128,512]{2,1,0:T(8,128)(2,1)S(1)}, bf16[2,128,512]{2,1,0:T(8,128)(2,1)S(1)}, u32[]{:S(2)}, u32[]{:S(2)}) collective-permute-start(bf16[2,128,512]{2,1,0:T(8,128)(2,1)S(1)} %copy-done.25), channel_id=1, source_target_pairs={{0,1},{1,0},{2,3},{3,2},{4,5},{5,4},{6,7},{7,6},{8,9},{9,8},{10,11... | collective-permute-start | bytes 786440 | tf_op jit(solution)/shard_map/ppermute | solution.py:370
  105.0 13.6 %copy-start.23 = (bf16[2,128,512]{2,1,0:T(8,128)(2,1)S(1)}, bf16[2,128,512]{2,1,0:T(8,128)(2,1)}, u32[]{:S(2)}) copy-start(bf16[2,128,512]{2,1,0:T(8,128)(2,1)} %get-tuple-element.94) | copy-start | bytes 786436
  105.0 13.6 %copy-start.10 = (bf16[2,128,512]{2,1,0:T(8,128)(2,1)S(1)}, bf16[2,128,512]{2,1,0:T(8,128)(2,1)}, u32[]{:S(2)}) copy-start(bf16[2,128,512]{2,1,0:T(8,128)(2,1)} %get-tuple-element.107.refs_0_) | copy-start | bytes 786436
  105.0 16.3 %collective-permute-start.26 = (bf16[4,128,512]{2,1,0:T(8,128)(2,1)S(1)}, bf16[4,128,512]{2,1,0:T(8,128)(2,1)S(1)}, u32[]{:S(2)}, u32[]{:S(2)}) collective-permute-start(bf16[4,128,512]{2,1,0:T(8,128)(2,1)S(1)} %owner_sum.4), channel_id=1, source_target_pairs={{0,4},{1,5},{2,6},{3,7},{4,0},{5,1},{6,2},{7,3},{8,12},{9,13},{10,... | collective-permute-start | bytes 1572872 | tf_op jit(solution)/shard_map/ppermute | solution.py:359
  110.7 12.4 %collective-permute-start.25 = (bf16[2,128,512]{2,1,0:T(8,128)(2,1)}, bf16[2,128,512]{2,1,0:T(8,128)(2,1)S(1)}, u32[]{:S(2)}, u32[]{:S(2)}) collective-permute-start(bf16[2,128,512]{2,1,0:T(8,128)(2,1)} %get-tuple-element.104), channel_id=1, source_target_pairs={{0,3},{1,2},{2,1},{3,0},{4,7},{5,6},{6,5},{7,4},{8,11},{9,10},{10,... | collective-permute-start | bytes 786440 | tf_op jit(solution)/shard_map/ppermute | solution.py:370
  116.3 8.8 %collective-permute-start.22 = (bf16[2,128,512]{2,1,0:T(8,128)(2,1)S(1)}, bf16[2,128,512]{2,1,0:T(8,128)(2,1)S(1)}, u32[]{:S(2)}, u32[]{:S(2)}) collective-permute-start(bf16[2,128,512]{2,1,0:T(8,128)(2,1)S(1)} %copy-done.24), channel_id=1, source_target_pairs={{0,2},{1,3},{2,0},{3,1},{4,6},{5,7},{6,4},{7,5},{8,10},{9,11},{10,... | collective-permute-start | bytes 786440 | tf_op jit(solution)/shard_map/ppermute | solution.py:370
  118.6 9.4 %collective-permute-start.20 = (bf16[2,128,512]{2,1,0:T(8,128)(2,1)S(1)}, bf16[2,128,512]{2,1,0:T(8,128)(2,1)S(1)}, u32[]{:S(2)}, u32[]{:S(2)}) collective-permute-start(bf16[2,128,512]{2,1,0:T(8,128)(2,1)S(1)} %copy-done.23), channel_id=1, source_target_pairs={{0,1},{1,0},{2,3},{3,2},{4,5},{5,4},{6,7},{7,6},{8,9},{9,8},{10,11... | collective-permute-start | bytes 786440 | tf_op jit(solution)/shard_map/ppermute | solution.py:370
  119.5 20.7 %copy-start.8 = (bf16[2,128,512]{2,1,0:T(8,128)(2,1)S(1)}, bf16[2,128,512]{2,1,0:T(8,128)(2,1)}, u32[]{:S(2)}) copy-start(bf16[2,128,512]{2,1,0:T(8,128)(2,1)} %get-tuple-element.87.refs_0_) | copy-start | bytes 786436
  122.3 26.1 %collective-permute-start.31 = (bf16[4,128,512]{2,1,0:T(8,128)(2,1)}, bf16[4,128,512]{2,1,0:T(8,128)(2,1)}, u32[]{:S(2)}, u32[]{:S(2)}) collective-permute-start(bf16[4,128,512]{2,1,0:T(8,128)(2,1)} %add_convert_fusion), channel_id=1, source_target_pairs={{0,24},{1,25},{2,26},{3,27},{4,28},{5,29},{6,30},{7,31},{8,16},{9,... | collective-permute-start | bytes 1572872 | tf_op jit(solution)/shard_map/ppermute | solution.py:359
  125.0 13.7 %collective-permute-start.28 = (bf16[2,128,512]{2,1,0:T(8,128)(2,1)}, bf16[2,128,512]{2,1,0:T(8,128)(2,1)S(1)}, u32[]{:S(2)}, u32[]{:S(2)}) collective-permute-start(bf16[2,128,512]{2,1,0:T(8,128)(2,1)} %get-tuple-element.113), channel_id=1, source_target_pairs={{0,2},{1,3},{2,0},{3,1},{4,6},{5,7},{6,4},{7,5},{8,10},{9,11},{10,... | collective-permute-start | bytes 786440 | tf_op jit(solution)/shard_map/ppermute | solution.py:370
  126.6 12.1 %collective-permute-start.29 = (bf16[2,128,512]{2,1,0:T(8,128)(2,1)}, bf16[2,128,512]{2,1,0:T(8,128)(2,1)S(1)}, u32[]{:S(2)}, u32[]{:S(2)}) collective-permute-start(bf16[2,128,512]{2,1,0:T(8,128)(2,1)} %get-tuple-element.116), channel_id=1, source_target_pairs={{0,3},{1,2},{2,1},{3,0},{4,7},{5,6},{6,5},{7,4},{8,11},{9,10},{10,... | collective-permute-start | bytes 786440 | tf_op jit(solution)/shard_map/ppermute | solution.py:370
  128.1 12.1 %collective-permute-start.27 = (bf16[2,128,512]{2,1,0:T(8,128)(2,1)S(1)}, bf16[2,128,512]{2,1,0:T(8,128)(2,1)S(1)}, u32[]{:S(2)}, u32[]{:S(2)}) collective-permute-start(bf16[2,128,512]{2,1,0:T(8,128)(2,1)S(1)} %get-tuple-element.110), channel_id=1, source_target_pairs={{0,1},{1,0},{2,3},{3,2},{4,5},{5,4},{6,7},{7,6},{8,9},{9,8},{10,11... | collective-permute-start | bytes 786440 | tf_op jit(solution)/shard_map/ppermute | solution.py:370
  140.2 8.2 %copy-start.2 = (bf16[768,256]{1,0:T(8,128)(2,1)S(1)}, bf16[768,256]{1,0:T(8,128)(2,1)}, u32[]{:S(2)}) copy-start(bf16[768,256]{1,0:T(8,128)(2,1)} %refs_3_.3) | copy-start | bytes 1179652
  140.2 8.2 %copy-start.9 = (f32[512,768]{1,0:T(8,128)S(1)}, f32[512,768]{1,0:T(8,128)}, u32[]{:S(2)}) copy-start(f32[512,768]{1,0:T(8,128)} %fusion.14.refs_1_) | copy-start | bytes 4718596
  141.1 9.0 %collective-permute-start.30 = (bf16[4,128,512]{2,1,0:T(8,128)(2,1)S(1)}, bf16[4,128,512]{2,1,0:T(8,128)(2,1)S(1)}, u32[]{:S(2)}, u32[]{:S(2)}) collective-permute-start(bf16[4,128,512]{2,1,0:T(8,128)(2,1)S(1)} %owner_sum.5), channel_id=1, source_target_pairs={{0,16},{1,17},{2,18},{3,19},{4,20},{5,21},{6,22},{7,23},{8,24},{9,... | collective-permute-start | bytes 1572872 | tf_op jit(solution)/shard_map/ppermute | solution.py:359
  (19 other events, 83.5 us)

commit v18 on v17

--- a/solution.py
+++ b/solution.py
@@ -232,41 +232,6 @@
     )(gets, puts, queries, normed_grad, *arrived)
 
 
-def project_kernel(tokens_hbm, wk_hbm, wv_hbm, out_ref, tokens, wk, wv, sems):
-    copies = []
-    for src, dst, pieces in ((wk_hbm, wk, 2), (tokens_hbm, tokens, 4), (wv_hbm, wv, 2)):
-        size = src.shape[0] // pieces
-        for i in range(pieces):
-            part = pl.ds(i * size, size)
-            copies.append(
-                pltpu.make_async_copy(src.at[part], dst.at[part], sems.at[len(copies)])
-            )
-    for copy in copies:
-        copy.start()
-    for copy in copies[:6]:
-        copy.wait()
-    keys = jnp.dot(tokens[...], wk[...], preferred_element_type=F32)
-    out_ref[:, :KV] = keys.astype(BF16)
-    for copy in copies[6:]:
-        copy.wait()
-    values = jnp.dot(tokens[...], wv[...], preferred_element_type=F32)
-    out_ref[:, KV:] = values.astype(BF16)
-
-
-def project(tokens, w_key, w_value):
-    args = (tokens, w_key, w_value)
-    return pl.pallas_call(
-        project_kernel,
-        in_specs=[pl.BlockSpec(memory_space=pl.ANY)] * 3,
-        out_specs=WHOLE,
-        out_shape=jax.ShapeDtypeStruct((tokens.shape[0], 2 * KV), BF16),
-        scratch_shapes=[pltpu.VMEM(x.shape, BF16) for x in args]
-        + [pltpu.SemaphoreType.DMA((8,))],
-        compiler_params=params(56),
-        name="project",
-    )(*args)
-
-
 def pack_kernel(first, wanted_ref, tile_ref, *outs):
     for i, out in enumerate(outs):
         for s in range(CAP):
@@ -405,7 +370,9 @@
     beside_wanted = asked(ranked(tiles), CAP, picks, tiles == my_tile).reshape(-1)
     own_wanted = jnp.concatenate([wanted[: plane * CAP], beside_wanted])
 
-    mine = project(tokens, w_key, w_value).reshape(block_count, BLK, 2 * KV)
+    keys = jnp.dot(tokens, w_key, preferred_element_type=F32).astype(BF16)
+    values = jnp.dot(tokens, w_value, preferred_element_type=F32).astype(BF16)
+    mine = jnp.concatenate([keys, values], axis=-1).reshape(block_count, BLK, 2 * KV)
     next_tile = swap(mine, 1, 1)
     own_tile = swap(mine, 0, 1)
     far_tile = swap(after(mine, own_tile), 2, 1)

time: 152 us -> 153 us (level)
  waiting for transfers between devices: 59.8 us -> 62.9 us
  other arithmetic: 5.22 us -> 2.24 us
  Pallas kernels: 30.1 us -> 27.7 us
  matrix products: 10.2 us -> 12.4 us
    ppermute x24, waiting for transfers between devices: 36.2 us -> 41.4 us  [spread(): moved.append(lax.ppermute(value, 'tile', pairs))]
    pallas_call x1 -> x0, Pallas kernels: 3.4 us -> none  [project(): pl.pallas_call(project_kernel, in_specs=[pl.BlockSpec(memory_space=pl.ANY...]
    dot_general x0 -> x2, matrix products: none -> 2.22 us  [the longest x1 1.8 us: shards(): keys = jnp.dot(tokens, w_key, preferred_element_type=F32).astype(BF16)]
    ppermute x8, waiting for transfers between devices: 23.6 us -> 21.5 us  [swap(): return lax.ppermute(value, ('vintage', 'tile'), pairs)]
  transfers between devices with their start and end apart: 32 -> 32, of which waited for: 16 -> 17; matrix products, arithmetic and copies ran while one was open for 12% -> 10% of each run, Pallas kernels for 5% -> 6%
where the time goes in v18:
time: 153 us
  waiting for transfers between devices  62.9 us (41%)
  starting transfers between devices  41.6 us (27%)
  Pallas kernels  27.7 us (18%)
  matrix products  12.4 us (8%)
  local copies, waits for them, and re-layouts  4.88 us (3%)
  other arithmetic  2.24 us (1%)
    ppermute x24, waiting for transfers between devices, spread(): moved.append(lax.ppermute(value, 'tile', pairs))  41.4 us
    ppermute x24, starting transfers between devices, spread(): moved.append(lax.ppermute(value, 'tile', pairs))  33.2 us
    ppermute x8, waiting for transfers between devices, swap(): return lax.ppermute(value, ('vintage', 'tile'), pairs)  21.5 us
    pallas_call x1, Pallas kernels, attention(): pl.pallas_call(functools.partial(attention_kernel, list_len, per_step, le...  17.8 us
    ppermute x8, starting transfers between devices, swap(): return lax.ppermute(value, ('vintage', 'tile'), pairs)  8.36 us
    pallas_call x4, Pallas kernels, pack(): pl.pallas_call(functools.partial(pack_kernel, group * plane * CAP), in_sp...  3.72 us
    dot_general x1, matrix products, dot_nt(): lax.dot_general(a, b, (((1,), (1,)), ((), ())), preferred_element_type=F32)  3.54 us
    dot_general x1, matrix products, shards(): lax.dot_general(query_grad, w_query, (((0,), (1,)), ((), ())), preferred_...  3.27 us
  transfers between devices with their start and end apart: 32, of which 17 were waited for; matrix products, arithmetic and copies ran while one was open for 10% of the time, Pallas kernels for 6%

profile of v18, /device:TPU:0, one launch (start us, length us, event | category | flops | bytes accessed | tf_op | source)
XLA Modules:
  0.0 152.7 jit_solution(11061783388021160717)
XLA Ops:
  0.7 1.8 %convolution_convert_fusion.3 = bf16[512,256]{0,1:T(8,128)(2,1)S(1)} fusion(bf16[768,256]{1,0:T(8,128)(2,1)} %refs_2_.3, bf16[1,512,768]{2,1,0:T(8,128)(2,1)} %param.8), kind=kOutput, calls=%fused_computation.5 | convolution fusion | flops 201457664 | bytes 1441792 | tf_op jit(solution)/shard_map/dot_general | solution.py:373
  3.0 1.0 copy.22
  4.0 2.5 %collective-permute-start.4 = (bf16[4,128,512]{2,1,0:T(8,128)(2,1)}, bf16[4,128,512]{2,1,0:T(8,128)(2,1)S(1)}, u32[]{:S(2)}, u32[]{:S(2)}) collective-permute-start(bf16[4,128,512]{2,1,0:T(8,128)(2,1)} %bitcast.10), channel_id=1, source_target_pairs={{0,20},{1,21},{2,22},{3,23},{4,16},{5,17},{6,18},{7,19},{8,28},{9,... | collective-permute-start | bytes 1572872 | tf_op jit(solution)/shard_map/ppermute | solution.py:324
  8.0 0.9 collective-permute-done.tile_ref.refs_0_
  8.9 2.6 %collective-permute-start.8 = (bf16[4,128,512]{2,1,0:T(8,128)(2,1)}, bf16[4,128,512]{2,1,0:T(8,128)(2,1)S(1)}, u32[]{:S(2)}, u32[]{:S(2)}) collective-permute-start(bf16[4,128,512]{2,1,0:T(8,128)(2,1)} %bitcast.10), channel_id=1, source_target_pairs={{0,24},{1,25},{2,26},{3,27},{4,28},{5,29},{6,30},{7,31},{8,16},{9,... | collective-permute-start | bytes 1572872 | tf_op jit(solution)/shard_map/ppermute | solution.py:324
  12.9 2.5 %collective-permute-start.3 = (bf16[2,128,512]{2,1,0:T(8,128)(2,1)S(1)}, bf16[2,128,512]{2,1,0:T(8,128)(2,1)S(1)}, u32[]{:S(2)}, u32[]{:S(2)}) collective-permute-start(bf16[2,128,512]{2,1,0:T(8,128)(2,1)S(1)} %get-tuple-element.62), channel_id=1, source_target_pairs={{0,3},{1,2},{2,1},{3,0},{4,7},{5,6},{6,5},{7,4},{8,11},{9,10},{10,... | collective-permute-start | bytes 786440 | tf_op jit(solution)/shard_map/ppermute | solution.py:335
  16.5 10.8 %collective-permute-done.4.tile_ref.refs_4_ = bf16[4,128,512]{2,1,0:T(8,128)(2,1)S(1)} collective-permute-done((bf16[4,128,512]{2,1,0:T(8,128)(2,1)}, bf16[4,128,512]{2,1,0:T(8,128)(2,1)S(1)}, u32[]{:S(2)}, u32[]{:S(2)}) %collective-permute-start.4) | collective-permute-done | bytes 524320 | tf_op jit(solution)/shard_map/ppermute | solution.py:324
  27.3 1.4 pack.5
  28.7 3.9 %collective-permute-start.7 = (bf16[2,128,512]{2,1,0:T(8,128)(2,1)}, bf16[2,128,512]{2,1,0:T(8,128)(2,1)}, u32[]{:S(2)}, u32[]{:S(2)}) collective-permute-start(bf16[2,128,512]{2,1,0:T(8,128)(2,1)} %get-tuple-element.68), channel_id=1, source_target_pairs={{0,3},{1,2},{2,1},{3,0},{4,7},{5,6},{6,5},{7,4},{8,11},{9,10},{10,... | collective-permute-start | bytes 786440 | tf_op jit(solution)/shard_map/ppermute | solution.py:335
  33.2 1.8 %collective-permute-done.8.tile_ref.refs_8_ = bf16[4,128,512]{2,1,0:T(8,128)(2,1)S(1)} collective-permute-done((bf16[4,128,512]{2,1,0:T(8,128)(2,1)}, bf16[4,128,512]{2,1,0:T(8,128)(2,1)S(1)}, u32[]{:S(2)}, u32[]{:S(2)}) %collective-permute-start.8) | collective-permute-done | bytes 524320 | tf_op jit(solution)/shard_map/ppermute | solution.py:324
  36.5 3.5 %collective-permute-done.7.refs_7_ = bf16[2,128,512]{2,1,0:T(8,128)(2,1)} collective-permute-done((bf16[2,128,512]{2,1,0:T(8,128)(2,1)}, bf16[2,128,512]{2,1,0:T(8,128)(2,1)}, u32[]{:S(2)}, u32[]{:S(2)}) %collective-permute-start.7) | collective-permute-done | bytes 262176 | tf_op jit(solution)/shard_map/ppermute | solution.py:335
  40.0 3.0 %collective-permute-start.11 = (bf16[2,128,512]{2,1,0:T(8,128)(2,1)S(1)}, bf16[2,128,512]{2,1,0:T(8,128)(2,1)S(1)}, u32[]{:S(2)}, u32[]{:S(2)}) collective-permute-start(bf16[2,128,512]{2,1,0:T(8,128)(2,1)S(1)} %get-tuple-element.76), channel_id=1, source_target_pairs={{0,3},{1,2},{2,1},{3,0},{4,7},{5,6},{6,5},{7,4},{8,11},{9,10},{10,... | collective-permute-start | bytes 786440 | tf_op jit(solution)/shard_map/ppermute | solution.py:335
  43.0 2.6 %collective-permute-done.6.refs_6_ = bf16[2,128,512]{2,1,0:T(8,128)(2,1)} collective-permute-done((bf16[2,128,512]{2,1,0:T(8,128)(2,1)}, bf16[2,128,512]{2,1,0:T(8,128)(2,1)}, u32[]{:S(2)}, u32[]{:S(2)}) %collective-permute-start.6) | collective-permute-done | bytes 262176 | tf_op jit(solution)/shard_map/ppermute | solution.py:335
  45.6 2.0 %collective-permute-start.10 = (bf16[2,128,512]{2,1,0:T(8,128)(2,1)S(1)}, bf16[2,128,512]{2,1,0:T(8,128)(2,1)S(1)}, u32[]{:S(2)}, u32[]{:S(2)}) collective-permute-start(bf16[2,128,512]{2,1,0:T(8,128)(2,1)S(1)} %get-tuple-element.74), channel_id=1, source_target_pairs={{0,2},{1,3},{2,0},{3,1},{4,6},{5,7},{6,4},{7,5},{8,10},{9,11},{10,... | collective-permute-start | bytes 786440 | tf_op jit(solution)/shard_map/ppermute | solution.py:335
  47.7 3.5 %fusion.ng_ref = f32[768,512]{1,0:T(8,128)} fusion(bf16[768,768]{1,0:T(8,128)(2,1)} %param.13, bf16[1,512,768]{2,1,0:T(8,128)(2,1)} %param.9), kind=kOutput, calls=%fused_computation.7 | convolution fusion | flops 603979776 | bytes 3538944 | tf_op jit(solution)/shard_map/dot_general | solution.py:34
  51.3 1.1 pack.7
  52.4 1.8 %collective-permute-start.15 = (bf16[2,128,512]{2,1,0:T(8,128)(2,1)S(1)}, bf16[2,128,512]{2,1,0:T(8,128)(2,1)S(1)}, u32[]{:S(2)}, u32[]{:S(2)}) collective-permute-start(bf16[2,128,512]{2,1,0:T(8,128)(2,1)S(1)} %get-tuple-element.82), channel_id=1, source_target_pairs={{0,3},{1,2},{2,1},{3,0},{4,7},{5,6},{6,5},{7,4},{8,11},{9,10},{10,... | collective-permute-start | bytes 786440 | tf_op jit(solution)/shard_map/ppermute | solution.py:335
  54.2 2.6 %collective-permute-done.10.refs_10_ = bf16[2,128,512]{2,1,0:T(8,128)(2,1)S(1)} collective-permute-done((bf16[2,128,512]{2,1,0:T(8,128)(2,1)S(1)}, bf16[2,128,512]{2,1,0:T(8,128)(2,1)S(1)}, u32[]{:S(2)}, u32[]{:S(2)}) %collective-permute-start.10) | collective-permute-done | bytes 262176 | tf_op jit(solution)/shard_map/ppermute | solution.py:335
  56.7 2.0 %collective-permute-start.14 = (bf16[2,128,512]{2,1,0:T(8,128)(2,1)S(1)}, bf16[2,128,512]{2,1,0:T(8,128)(2,1)S(1)}, u32[]{:S(2)}, u32[]{:S(2)}) collective-permute-start(bf16[2,128,512]{2,1,0:T(8,128)(2,1)S(1)} %get-tuple-element.80), channel_id=1, source_target_pairs={{0,2},{1,3},{2,0},{3,1},{4,6},{5,7},{6,4},{7,5},{8,10},{9,11},{10,... | collective-permute-start | bytes 786440 | tf_op jit(solution)/shard_map/ppermute | solution.py:335
  58.8 1.5 collective-permute-start.13
  60.3 1.7 %convolution_convert_fusion.1.q_ref = bf16[768,512]{1,0:T(8,128)(2,1)} fusion(bf16[768,768]{1,0:T(8,128)(2,1)S(1)} %copy-done, bf16[1,512,768]{2,1,0:T(8,128)(2,1)S(1)} %copy-done.11), kind=kOutput, calls=%fused_computation.3 | convolution fusion | flops 604372992 | bytes 2752512 | tf_op jit(solution)/shard_map/dot_general | solution.py:385
  62.7 5.0 %collective-permute-done.14.refs_14_ = bf16[2,128,512]{2,1,0:T(8,128)(2,1)S(1)} collective-permute-done((bf16[2,128,512]{2,1,0:T(8,128)(2,1)S(1)}, bf16[2,128,512]{2,1,0:T(8,128)(2,1)S(1)}, u32[]{:S(2)}, u32[]{:S(2)}) %collective-permute-start.14) | collective-permute-done | bytes 262176 | tf_op jit(solution)/shard_map/ppermute | solution.py:335
  68.6 17.8 %attention.1 = (bf16[768,512]{1,0:T(8,128)(2,1)}, bf16[768,512]{1,0:T(8,128)(2,1)}, bf16[2,128,512]{2,1,0:T(8,128)(2,1)}, bf16[2,128,512]{2,1,0:T(8,128)(2,1)}, ...) custom-call(s32[16]{0:T(128)} %get-tuple-element.136.get_ref, ...), custom_call_target="tpu_custom_call" | custom-call | flops 2415919104 | bytes 6291456 | tf_op jit(solution)/shard_map/attention/pallas_call | solution.py:210
  86.5 1.6 %collective-permute-start.16 = (bf16[2,128,512]{2,1,0:T(8,128)(2,1)}, bf16[2,128,512]{2,1,0:T(8,128)(2,1)S(1)}, u32[]{:S(2)}, u32[]{:S(2)}) collective-permute-start(bf16[2,128,512]{2,1,0:T(8,128)(2,1)} %get-tuple-element.83), channel_id=1, source_target_pairs={{0,2},{1,3},{2,0},{3,1},{4,6},{5,7},{6,4},{7,5},{8,10},{9,11},{10,... | collective-permute-start | bytes 786440 | tf_op jit(solution)/shard_map/ppermute | solution.py:335
  88.1 1.4 collective-permute-start.17
  90.1 3.3 %fusion.16.refs_1_ = f32[512,768]{1,0:T(8,128)} fusion(bf16[768,512]{1,0:T(8,128)(2,1)} %get-tuple-element.84, bf16[768,768]{1,0:T(8,128)(2,1)S(1)} %copy-done), kind=kOutput, calls=%fused_computation.57 | convolution fusion | flops 603979776 | bytes 3538944 | tf_op jit(solution)/shard_map/dot_general | solution.py:397
  93.4 1.7 %convolution_convert_fusion = bf16[512,768]{1,0:T(8,128)(2,1)} fusion(bf16[768,512]{1,0:T(8,128)(2,1)S(1)} %copy-done.29, bf16[768,768]{1,0:T(8,128)(2,1)S(1)} %copy-done.14), kind=kOutput, calls=%fused_computation.2 | convolution fusion | flops 604372992 | bytes 2752512 | tf_op jit(solution)/shard_map/dot_general | solution.py:38
  95.1 6.6 %collective-permute-done.23.refs_3_ = bf16[2,128,512]{2,1,0:T(8,128)(2,1)S(1)} collective-permute-done((bf16[2,128,512]{2,1,0:T(8,128)(2,1)}, bf16[2,128,512]{2,1,0:T(8,128)(2,1)S(1)}, u32[]{:S(2)}, u32[]{:S(2)}) %collective-permute-start.23) | collective-permute-done | bytes 262176 | tf_op jit(solution)/shard_map/ppermute | solution.py:335
  101.7 2.6 %collective-permute-start.24 = (bf16[2,128,512]{2,1,0:T(8,128)(2,1)S(1)}, bf16[2,128,512]{2,1,0:T(8,128)(2,1)S(1)}, u32[]{:S(2)}, u32[]{:S(2)}) collective-permute-start(bf16[2,128,512]{2,1,0:T(8,128)(2,1)S(1)} %copy-done.24), channel_id=1, source_target_pairs={{0,3},{1,2},{2,1},{3,0},{4,7},{5,6},{6,5},{7,4},{8,11},{9,10},{10,... | collective-permute-start | bytes 786440 | tf_op jit(solution)/shard_map/ppermute | solution.py:335
  105.2 0.8 owner_sum.4
  106.0 1.6 %collective-permute-start.26 = (bf16[4,128,512]{2,1,0:T(8,128)(2,1)S(1)}, bf16[4,128,512]{2,1,0:T(8,128)(2,1)S(1)}, u32[]{:S(2)}, u32[]{:S(2)}) collective-permute-start(bf16[4,128,512]{2,1,0:T(8,128)(2,1)S(1)} %owner_sum.4), channel_id=1, source_target_pairs={{0,4},{1,5},{2,6},{3,7},{4,0},{5,1},{6,2},{7,3},{8,12},{9,13},{10,... | collective-permute-start | bytes 1572872 | tf_op jit(solution)/shard_map/ppermute | solution.py:324
  107.6 4.2 %collective-permute-done.24.refs_3_ = bf16[2,128,512]{2,1,0:T(8,128)(2,1)S(1)} collective-permute-done((bf16[2,128,512]{2,1,0:T(8,128)(2,1)S(1)}, bf16[2,128,512]{2,1,0:T(8,128)(2,1)S(1)}, u32[]{:S(2)}, u32[]{:S(2)}) %collective-permute-start.24) | collective-permute-done | bytes 262176 | tf_op jit(solution)/shard_map/ppermute | solution.py:335
  111.9 2.5 %collective-permute-start.25 = (bf16[2,128,512]{2,1,0:T(8,128)(2,1)S(1)}, bf16[2,128,512]{2,1,0:T(8,128)(2,1)S(1)}, u32[]{:S(2)}, u32[]{:S(2)}) collective-permute-start(bf16[2,128,512]{2,1,0:T(8,128)(2,1)S(1)} %copy-done.19), channel_id=1, source_target_pairs={{0,3},{1,2},{2,1},{3,0},{4,7},{5,6},{6,5},{7,4},{8,11},{9,10},{10,... | collective-permute-start | bytes 786440 | tf_op jit(solution)/shard_map/ppermute | solution.py:335
  114.4 3.0 %collective-permute-done.21.refs_2_ = bf16[2,128,512]{2,1,0:T(8,128)(2,1)S(1)} collective-permute-done((bf16[2,128,512]{2,1,0:T(8,128)(2,1)S(1)}, bf16[2,128,512]{2,1,0:T(8,128)(2,1)S(1)}, u32[]{:S(2)}, u32[]{:S(2)}) %collective-permute-start.21) | collective-permute-done | bytes 262176 | tf_op jit(solution)/shard_map/ppermute | solution.py:335
  117.4 1.6 %collective-permute-start.22 = (bf16[2,128,512]{2,1,0:T(8,128)(2,1)S(1)}, bf16[2,128,512]{2,1,0:T(8,128)(2,1)S(1)}, u32[]{:S(2)}, u32[]{:S(2)}) collective-permute-start(bf16[2,128,512]{2,1,0:T(8,128)(2,1)S(1)} %copy-done.18), channel_id=1, source_target_pairs={{0,2},{1,3},{2,0},{3,1},{4,6},{5,7},{6,4},{7,5},{8,10},{9,11},{10,... | collective-permute-start | bytes 786440 | tf_op jit(solution)/shard_map/ppermute | solution.py:335
  119.0 0.9 fusion.15
  120.0 0.8 owner_sum.3
  120.8 2.0 %collective-permute-done.26 = bf16[4,128,512]{2,1,0:T(8,128)(2,1)S(1)} collective-permute-done((bf16[4,128,512]{2,1,0:T(8,128)(2,1)S(1)}, bf16[4,128,512]{2,1,0:T(8,128)(2,1)S(1)}, u32[]{:S(2)}, u32[]{:S(2)}) %collective-permute-start.26) | collective-permute-done | bytes 524320 | tf_op jit(solution)/shard_map/ppermute | solution.py:324
  122.8 0.9 add_convert_fusion
  124.6 1.9 %collective-permute-done.22.refs_2_ = bf16[2,128,512]{2,1,0:T(8,128)(2,1)S(1)} collective-permute-done((bf16[2,128,512]{2,1,0:T(8,128)(2,1)S(1)}, bf16[2,128,512]{2,1,0:T(8,128)(2,1)S(1)}, u32[]{:S(2)}, u32[]{:S(2)}) %collective-permute-start.22) | collective-permute-done | bytes 262176 | tf_op jit(solution)/shard_map/ppermute | solution.py:335
  126.5 1.7 %collective-permute-start.28 = (bf16[2,128,512]{2,1,0:T(8,128)(2,1)}, bf16[2,128,512]{2,1,0:T(8,128)(2,1)S(1)}, u32[]{:S(2)}, u32[]{:S(2)}) collective-permute-start(bf16[2,128,512]{2,1,0:T(8,128)(2,1)} %get-tuple-element.113), channel_id=1, source_target_pairs={{0,2},{1,3},{2,0},{3,1},{4,6},{5,7},{6,4},{7,5},{8,10},{9,11},{10,... | collective-permute-start | bytes 786440 | tf_op jit(solution)/shard_map/ppermute | solution.py:335
  128.2 1.4 collective-permute-start.29
  130.9 9.7 %collective-permute-done.28.refs_6_ = bf16[2,128,512]{2,1,0:T(8,128)(2,1)S(1)} collective-permute-done((bf16[2,128,512]{2,1,0:T(8,128)(2,1)}, bf16[2,128,512]{2,1,0:T(8,128)(2,1)S(1)}, u32[]{:S(2)}, u32[]{:S(2)}) %collective-permute-start.28) | collective-permute-done | bytes 262176 | tf_op jit(solution)/shard_map/ppermute | solution.py:335
  140.6 1.4 collective-permute-done.27.refs_5_
  141.9 1.5 owner_sum.5
  143.5 6.1 %collective-permute-done.31 = bf16[4,128,512]{2,1,0:T(8,128)(2,1)} collective-permute-done((bf16[4,128,512]{2,1,0:T(8,128)(2,1)}, bf16[4,128,512]{2,1,0:T(8,128)(2,1)}, u32[]{:S(2)}, u32[]{:S(2)}) %collective-permute-start.31) | collective-permute-done | bytes 524320 | tf_op jit(solution)/shard_map/ppermute | solution.py:324
  149.5 1.7 %finish.2.refs_1_ = f32[512,768]{1,0:T(8,128)S(1)} custom-call(bf16[512,512]{1,0:T(8,128)(2,1)} %bitcast.20.refs_0_, f32[512,768]{1,0:T(8,128)S(1)} %copy-done.8, bf16[768,256]{1,0:T(8,128)(2,1)S(1)} %copy-done.2, bf16[768,256]{1,0:T(8,128)(2,1)S(1)} %copy-done.1), custom_call_target="tpu_custom_call" | custom-call | flops 20000000000 | bytes 1572864 | tf_op jit(solution)/shard_map/finish/pallas_call | solution.py:264
  151.2 1.5 finish.3
  (123 shorter events, 12.2 us)
Async XLA Ops:
  0.6 59.6 %copy-start = (bf16[768,768]{1,0:T(8,128)(2,1)S(1)}, bf16[768,768]{1,0:T(8,128)(2,1)}, u32[]{:S(2)}) copy-start(bf16[768,768]{1,0:T(8,128)(2,1)} %param.10) | copy-start | bytes 3538948
  4.0 23.3 %collective-permute-start.4 = (bf16[4,128,512]{2,1,0:T(8,128)(2,1)}, bf16[4,128,512]{2,1,0:T(8,128)(2,1)S(1)}, u32[]{:S(2)}, u32[]{:S(2)}) collective-permute-start(bf16[4,128,512]{2,1,0:T(8,128)(2,1)} %bitcast.10), channel_id=1, source_target_pairs={{0,20},{1,21},{2,22},{3,23},{4,16},{5,17},{6,18},{7,19},{8,28},{9,... | collective-permute-start | bytes 1572872 | tf_op jit(solution)/shard_map/ppermute | solution.py:324
  6.5 2.4 %collective-permute-start = (bf16[4,128,512]{2,1,0:T(8,128)(2,1)}, bf16[4,128,512]{2,1,0:T(8,128)(2,1)S(1)}, u32[]{:S(2)}, u32[]{:S(2)}) collective-permute-start(bf16[4,128,512]{2,1,0:T(8,128)(2,1)} %bitcast.10), channel_id=1, source_target_pairs={{0,16},{1,17},{2,18},{3,19},{4,20},{5,21},{6,22},{7,23},{8,24},{9,... | collective-permute-start | bytes 1572872 | tf_op jit(solution)/shard_map/ppermute | solution.py:324
  8.9 42.4 %copy-start.4 = (bf16[4,128,512]{2,1,0:T(8,128)(2,1)}, bf16[4,128,512]{2,1,0:T(8,128)(2,1)S(1)}, u32[]{:S(2)}) copy-start(bf16[4,128,512]{2,1,0:T(8,128)(2,1)S(1)} %collective-permute-done.tile_ref.refs_0_) | copy-start | bytes 1572868
  8.9 26.2 %collective-permute-start.8 = (bf16[4,128,512]{2,1,0:T(8,128)(2,1)}, bf16[4,128,512]{2,1,0:T(8,128)(2,1)S(1)}, u32[]{:S(2)}, u32[]{:S(2)}) collective-permute-start(bf16[4,128,512]{2,1,0:T(8,128)(2,1)} %bitcast.10), channel_id=1, source_target_pairs={{0,24},{1,25},{2,26},{3,27},{4,28},{5,29},{6,30},{7,31},{8,16},{9,... | collective-permute-start | bytes 1572872 | tf_op jit(solution)/shard_map/ppermute | solution.py:324
  12.9 15.8 %collective-permute-start.3 = (bf16[2,128,512]{2,1,0:T(8,128)(2,1)S(1)}, bf16[2,128,512]{2,1,0:T(8,128)(2,1)S(1)}, u32[]{:S(2)}, u32[]{:S(2)}) collective-permute-start(bf16[2,128,512]{2,1,0:T(8,128)(2,1)S(1)} %get-tuple-element.62), channel_id=1, source_target_pairs={{0,3},{1,2},{2,1},{3,0},{4,7},{5,6},{6,5},{7,4},{8,11},{9,10},{10,... | collective-permute-start | bytes 786440 | tf_op jit(solution)/shard_map/ppermute | solution.py:335
  15.4 17.2 %collective-permute-start.2 = (bf16[2,128,512]{2,1,0:T(8,128)(2,1)S(1)}, bf16[2,128,512]{2,1,0:T(8,128)(2,1)S(1)}, u32[]{:S(2)}, u32[]{:S(2)}) collective-permute-start(bf16[2,128,512]{2,1,0:T(8,128)(2,1)S(1)} %get-tuple-element.61), channel_id=1, source_target_pairs={{0,2},{1,3},{2,0},{3,1},{4,6},{5,7},{6,4},{7,5},{8,10},{9,11},{10,... | collective-permute-start | bytes 786440 | tf_op jit(solution)/shard_map/ppermute | solution.py:335
  15.9 17.2 %collective-permute-start.1 = (bf16[2,128,512]{2,1,0:T(8,128)(2,1)S(1)}, bf16[2,128,512]{2,1,0:T(8,128)(2,1)S(1)}, u32[]{:S(2)}, u32[]{:S(2)}) collective-permute-start(bf16[2,128,512]{2,1,0:T(8,128)(2,1)S(1)} %get-tuple-element.60), channel_id=1, source_target_pairs={{0,1},{1,0},{2,3},{3,2},{4,5},{5,4},{6,7},{7,6},{8,9},{9,8},{10,11... | collective-permute-start | bytes 786440 | tf_op jit(solution)/shard_map/ppermute | solution.py:335
  27.3 24.0 %copy-start.3 = (bf16[4,128,512]{2,1,0:T(8,128)(2,1)}, bf16[4,128,512]{2,1,0:T(8,128)(2,1)S(1)}, u32[]{:S(2)}) copy-start(bf16[4,128,512]{2,1,0:T(8,128)(2,1)S(1)} %collective-permute-done.4.tile_ref.refs_4_) | copy-start | bytes 1572868
  28.7 11.3 %collective-permute-start.7 = (bf16[2,128,512]{2,1,0:T(8,128)(2,1)}, bf16[2,128,512]{2,1,0:T(8,128)(2,1)}, u32[]{:S(2)}, u32[]{:S(2)}) collective-permute-start(bf16[2,128,512]{2,1,0:T(8,128)(2,1)} %get-tuple-element.68), channel_id=1, source_target_pairs={{0,3},{1,2},{2,1},{3,0},{4,7},{5,6},{6,5},{7,4},{8,11},{9,10},{10,... | collective-permute-start | bytes 786440 | tf_op jit(solution)/shard_map/ppermute | solution.py:335
  32.6 13.0 %collective-permute-start.6 = (bf16[2,128,512]{2,1,0:T(8,128)(2,1)}, bf16[2,128,512]{2,1,0:T(8,128)(2,1)}, u32[]{:S(2)}, u32[]{:S(2)}) collective-permute-start(bf16[2,128,512]{2,1,0:T(8,128)(2,1)} %get-tuple-element.66), channel_id=1, source_target_pairs={{0,2},{1,3},{2,0},{3,1},{4,6},{5,7},{6,4},{7,5},{8,10},{9,11},{10,... | collective-permute-start | bytes 786440 | tf_op jit(solution)/shard_map/ppermute | solution.py:335
  33.1 14.5 %collective-permute-start.5 = (bf16[2,128,512]{2,1,0:T(8,128)(2,1)S(1)}, bf16[2,128,512]{2,1,0:T(8,128)(2,1)}, u32[]{:S(2)}, u32[]{:S(2)}) collective-permute-start(bf16[2,128,512]{2,1,0:T(8,128)(2,1)S(1)} %get-tuple-element.64), channel_id=1, source_target_pairs={{0,1},{1,0},{2,3},{3,2},{4,5},{5,4},{6,7},{7,6},{8,9},{9,8},{10,11... | collective-permute-start | bytes 786440 | tf_op jit(solution)/shard_map/ppermute | solution.py:335
  35.0 16.2 %copy-start.5 = (bf16[4,128,512]{2,1,0:T(8,128)(2,1)}, bf16[4,128,512]{2,1,0:T(8,128)(2,1)S(1)}, u32[]{:S(2)}) copy-start(bf16[4,128,512]{2,1,0:T(8,128)(2,1)S(1)} %collective-permute-done.8.tile_ref.refs_8_) | copy-start | bytes 1572868
  35.1 16.2 %collective-permute-start.12 = (bf16[4,128,512]{2,1,0:T(8,128)(2,1)S(1)}, bf16[4,128,512]{2,1,0:T(8,128)(2,1)}, u32[]{:S(2)}, u32[]{:S(2)}) collective-permute-start(bf16[4,128,512]{2,1,0:T(8,128)(2,1)S(1)} %collective-permute-done.8.tile_ref.refs_8_), channel_id=1, source_target_pairs={{0,4},{1,5},{2,6},{3,7},{4,0},{5,1},{6,2},{7,3},{8,12},{9,13},{10,... | collective-permute-start | bytes 1572872 | tf_op jit(solution)/shard_map/ppermute | solution.py:324
  40.0 12.4 %collective-permute-start.11 = (bf16[2,128,512]{2,1,0:T(8,128)(2,1)S(1)}, bf16[2,128,512]{2,1,0:T(8,128)(2,1)S(1)}, u32[]{:S(2)}, u32[]{:S(2)}) collective-permute-start(bf16[2,128,512]{2,1,0:T(8,128)(2,1)S(1)} %get-tuple-element.76), channel_id=1, source_target_pairs={{0,3},{1,2},{2,1},{3,0},{4,7},{5,6},{6,5},{7,4},{8,11},{9,10},{10,... | collective-permute-start | bytes 786440 | tf_op jit(solution)/shard_map/ppermute | solution.py:335
  45.6 11.2 %collective-permute-start.10 = (bf16[2,128,512]{2,1,0:T(8,128)(2,1)S(1)}, bf16[2,128,512]{2,1,0:T(8,128)(2,1)S(1)}, u32[]{:S(2)}, u32[]{:S(2)}) collective-permute-start(bf16[2,128,512]{2,1,0:T(8,128)(2,1)S(1)} %get-tuple-element.74), channel_id=1, source_target_pairs={{0,2},{1,3},{2,0},{3,1},{4,6},{5,7},{6,4},{7,5},{8,10},{9,11},{10,... | collective-permute-start | bytes 786440 | tf_op jit(solution)/shard_map/ppermute | solution.py:335
  47.6 12.7 %copy-start.11 = (bf16[1,512,768]{2,1,0:T(8,128)(2,1)S(1)}, bf16[1,512,768]{2,1,0:T(8,128)(2,1)}, u32[]{:S(2)}) copy-start(bf16[1,512,768]{2,1,0:T(8,128)(2,1)} %param.8) | copy-start | bytes 2359300
  47.6 11.2 %collective-permute-start.9 = (bf16[2,128,512]{2,1,0:T(8,128)(2,1)S(1)}, bf16[2,128,512]{2,1,0:T(8,128)(2,1)S(1)}, u32[]{:S(2)}, u32[]{:S(2)}) collective-permute-start(bf16[2,128,512]{2,1,0:T(8,128)(2,1)S(1)} %get-tuple-element.72), channel_id=1, source_target_pairs={{0,1},{1,0},{2,3},{3,2},{4,5},{5,4},{6,7},{7,6},{8,9},{9,8},{10,11... | collective-permute-start | bytes 786440 | tf_op jit(solution)/shard_map/ppermute | solution.py:335
  52.4 9.6 %copy-start.21 = (bf16[2,128,512]{2,1,0:T(8,128)(2,1)}, bf16[2,128,512]{2,1,0:T(8,128)(2,1)S(1)}, u32[]{:S(2)}) copy-start(bf16[2,128,512]{2,1,0:T(8,128)(2,1)S(1)} %collective-permute-done.11.refs_11_) | copy-start | bytes 786436
  52.4 10.3 %collective-permute-start.15 = (bf16[2,128,512]{2,1,0:T(8,128)(2,1)S(1)}, bf16[2,128,512]{2,1,0:T(8,128)(2,1)S(1)}, u32[]{:S(2)}, u32[]{:S(2)}) collective-permute-start(bf16[2,128,512]{2,1,0:T(8,128)(2,1)S(1)} %get-tuple-element.82), channel_id=1, source_target_pairs={{0,3},{1,2},{2,1},{3,0},{4,7},{5,6},{6,5},{7,4},{8,11},{9,10},{10,... | collective-permute-start | bytes 786440 | tf_op jit(solution)/shard_map/ppermute | solution.py:335
  56.7 11.0 %collective-permute-start.14 = (bf16[2,128,512]{2,1,0:T(8,128)(2,1)S(1)}, bf16[2,128,512]{2,1,0:T(8,128)(2,1)S(1)}, u32[]{:S(2)}, u32[]{:S(2)}) collective-permute-start(bf16[2,128,512]{2,1,0:T(8,128)(2,1)S(1)} %get-tuple-element.80), channel_id=1, source_target_pairs={{0,2},{1,3},{2,0},{3,1},{4,6},{5,7},{6,4},{7,5},{8,10},{9,11},{10,... | collective-permute-start | bytes 786440 | tf_op jit(solution)/shard_map/ppermute | solution.py:335
  58.8 9.2 %collective-permute-start.13 = (bf16[2,128,512]{2,1,0:T(8,128)(2,1)S(1)}, bf16[2,128,512]{2,1,0:T(8,128)(2,1)S(1)}, u32[]{:S(2)}, u32[]{:S(2)}) collective-permute-start(bf16[2,128,512]{2,1,0:T(8,128)(2,1)S(1)} %get-tuple-element.78), channel_id=1, source_target_pairs={{0,1},{1,0},{2,3},{3,2},{4,5},{5,4},{6,7},{7,6},{8,9},{9,8},{10,11... | collective-permute-start | bytes 786440 | tf_op jit(solution)/shard_map/ppermute | solution.py:335
  86.4 32.6 %collective-permute-start.19 = (bf16[8,128,512]{2,1,0:T(8,128)(2,1)}, bf16[8,128,512]{2,1,0:T(8,128)(2,1)S(1)}, u32[]{:S(2)}, u32[]{:S(2)}) collective-permute-start(bf16[8,128,512]{2,1,0:T(8,128)(2,1)} %get-tuple-element.92), channel_id=1, source_target_pairs={{0,4},{1,5},{2,6},{3,7},{4,0},{5,1},{6,2},{7,3},{8,12},{9,13},{10,... | collective-permute-start | bytes 3145736 | tf_op jit(solution)/shard_map/ppermute | solution.py:324
  86.5 17.8 %collective-permute-start.16 = (bf16[2,128,512]{2,1,0:T(8,128)(2,1)}, bf16[2,128,512]{2,1,0:T(8,128)(2,1)S(1)}, u32[]{:S(2)}, u32[]{:S(2)}) collective-permute-start(bf16[2,128,512]{2,1,0:T(8,128)(2,1)} %get-tuple-element.83), channel_id=1, source_target_pairs={{0,2},{1,3},{2,0},{3,1},{4,6},{5,7},{6,4},{7,5},{8,10},{9,11},{10,... | collective-permute-start | bytes 786440 | tf_op jit(solution)/shard_map/ppermute | solution.py:335
  88.1 16.6 %collective-permute-start.17 = (bf16[2,128,512]{2,1,0:T(8,128)(2,1)}, bf16[2,128,512]{2,1,0:T(8,128)(2,1)S(1)}, u32[]{:S(2)}, u32[]{:S(2)}) collective-permute-start(bf16[2,128,512]{2,1,0:T(8,128)(2,1)} %get-tuple-element.90), channel_id=1, source_target_pairs={{0,1},{1,0},{2,3},{3,2},{4,5},{5,4},{6,7},{7,6},{8,9},{9,8},{10,11... | collective-permute-start | bytes 786440 | tf_op jit(solution)/shard_map/ppermute | solution.py:335
  89.6 12.1 %collective-permute-start.23 = (bf16[2,128,512]{2,1,0:T(8,128)(2,1)}, bf16[2,128,512]{2,1,0:T(8,128)(2,1)S(1)}, u32[]{:S(2)}, u32[]{:S(2)}) collective-permute-start(bf16[2,128,512]{2,1,0:T(8,128)(2,1)} %get-tuple-element.102), channel_id=1, source_target_pairs={{0,3},{1,2},{2,1},{3,0},{4,7},{5,6},{6,5},{7,4},{8,11},{9,10},{10,... | collective-permute-start | bytes 786440 | tf_op jit(solution)/shard_map/ppermute | solution.py:335
  93.3 8.3 %copy-start.24 = (bf16[2,128,512]{2,1,0:T(8,128)(2,1)S(1)}, bf16[2,128,512]{2,1,0:T(8,128)(2,1)}, u32[]{:S(2)}) copy-start(bf16[2,128,512]{2,1,0:T(8,128)(2,1)} %get-tuple-element.103) | copy-start | bytes 786436
  93.3 10.9 %copy-start.22 = (bf16[2,128,512]{2,1,0:T(8,128)(2,1)S(1)}, bf16[2,128,512]{2,1,0:T(8,128)(2,1)}, u32[]{:S(2)}) copy-start(bf16[2,128,512]{2,1,0:T(8,128)(2,1)} %get-tuple-element.98) | copy-start | bytes 786436
  93.3 11.4 %copy-start.20 = (bf16[2,128,512]{2,1,0:T(8,128)(2,1)S(1)}, bf16[2,128,512]{2,1,0:T(8,128)(2,1)}, u32[]{:S(2)}) copy-start(bf16[2,128,512]{2,1,0:T(8,128)(2,1)} %get-tuple-element.91) | copy-start | bytes 786436
  93.4 11.8 %copy-start.6 = (bf16[2,128,512]{2,1,0:T(8,128)(2,1)S(1)}, bf16[2,128,512]{2,1,0:T(8,128)(2,1)}, u32[]{:S(2)}) copy-start(bf16[2,128,512]{2,1,0:T(8,128)(2,1)} %get-tuple-element.108.refs_0_) | copy-start | bytes 786436
  95.1 16.8 %copy-start.19 = (bf16[2,128,512]{2,1,0:T(8,128)(2,1)S(1)}, bf16[2,128,512]{2,1,0:T(8,128)(2,1)}, u32[]{:S(2)}) copy-start(bf16[2,128,512]{2,1,0:T(8,128)(2,1)} %get-tuple-element.104) | copy-start | bytes 786436
  95.1 22.3 %copy-start.18 = (bf16[2,128,512]{2,1,0:T(8,128)(2,1)S(1)}, bf16[2,128,512]{2,1,0:T(8,128)(2,1)}, u32[]{:S(2)}) copy-start(bf16[2,128,512]{2,1,0:T(8,128)(2,1)} %get-tuple-element.99) | copy-start | bytes 786436
  101.7 10.2 %collective-permute-start.24 = (bf16[2,128,512]{2,1,0:T(8,128)(2,1)S(1)}, bf16[2,128,512]{2,1,0:T(8,128)(2,1)S(1)}, u32[]{:S(2)}, u32[]{:S(2)}) collective-permute-start(bf16[2,128,512]{2,1,0:T(8,128)(2,1)S(1)} %copy-done.24), channel_id=1, source_target_pairs={{0,3},{1,2},{2,1},{3,0},{4,7},{5,6},{6,5},{7,4},{8,11},{9,10},{10,... | collective-permute-start | bytes 786440 | tf_op jit(solution)/shard_map/ppermute | solution.py:335
  104.3 13.1 %collective-permute-start.21 = (bf16[2,128,512]{2,1,0:T(8,128)(2,1)S(1)}, bf16[2,128,512]{2,1,0:T(8,128)(2,1)S(1)}, u32[]{:S(2)}, u32[]{:S(2)}) collective-permute-start(bf16[2,128,512]{2,1,0:T(8,128)(2,1)S(1)} %copy-done.22), channel_id=1, source_target_pairs={{0,2},{1,3},{2,0},{3,1},{4,6},{5,7},{6,4},{7,5},{8,10},{9,11},{10,... | collective-permute-start | bytes 786440 | tf_op jit(solution)/shard_map/ppermute | solution.py:335
  104.7 15.2 %collective-permute-start.18 = (bf16[2,128,512]{2,1,0:T(8,128)(2,1)S(1)}, bf16[2,128,512]{2,1,0:T(8,128)(2,1)S(1)}, u32[]{:S(2)}, u32[]{:S(2)}) collective-permute-start(bf16[2,128,512]{2,1,0:T(8,128)(2,1)S(1)} %copy-done.20), channel_id=1, source_target_pairs={{0,1},{1,0},{2,3},{3,2},{4,5},{5,4},{6,7},{7,6},{8,9},{9,8},{10,11... | collective-permute-start | bytes 786440 | tf_op jit(solution)/shard_map/ppermute | solution.py:335
  106.0 14.0 %copy-start.9 = (bf16[2,128,512]{2,1,0:T(8,128)(2,1)S(1)}, bf16[2,128,512]{2,1,0:T(8,128)(2,1)}, u32[]{:S(2)}) copy-start(bf16[2,128,512]{2,1,0:T(8,128)(2,1)} %get-tuple-element.107.refs_0_) | copy-start | bytes 786436
  106.0 16.8 %collective-permute-start.26 = (bf16[4,128,512]{2,1,0:T(8,128)(2,1)S(1)}, bf16[4,128,512]{2,1,0:T(8,128)(2,1)S(1)}, u32[]{:S(2)}, u32[]{:S(2)}) collective-permute-start(bf16[4,128,512]{2,1,0:T(8,128)(2,1)S(1)} %owner_sum.4), channel_id=1, source_target_pairs={{0,4},{1,5},{2,6},{3,7},{4,0},{5,1},{6,2},{7,3},{8,12},{9,13},{10,... | collective-permute-start | bytes 1572872 | tf_op jit(solution)/shard_map/ppermute | solution.py:324
  111.9 12.7 %collective-permute-start.25 = (bf16[2,128,512]{2,1,0:T(8,128)(2,1)S(1)}, bf16[2,128,512]{2,1,0:T(8,128)(2,1)S(1)}, u32[]{:S(2)}, u32[]{:S(2)}) collective-permute-start(bf16[2,128,512]{2,1,0:T(8,128)(2,1)S(1)} %copy-done.19), channel_id=1, source_target_pairs={{0,3},{1,2},{2,1},{3,0},{4,7},{5,6},{6,5},{7,4},{8,11},{9,10},{10,... | collective-permute-start | bytes 786440 | tf_op jit(solution)/shard_map/ppermute | solution.py:335
  117.4 9.1 %collective-permute-start.22 = (bf16[2,128,512]{2,1,0:T(8,128)(2,1)S(1)}, bf16[2,128,512]{2,1,0:T(8,128)(2,1)S(1)}, u32[]{:S(2)}, u32[]{:S(2)}) collective-permute-start(bf16[2,128,512]{2,1,0:T(8,128)(2,1)S(1)} %copy-done.18), channel_id=1, source_target_pairs={{0,2},{1,3},{2,0},{3,1},{4,6},{5,7},{6,4},{7,5},{8,10},{9,11},{10,... | collective-permute-start | bytes 786440 | tf_op jit(solution)/shard_map/ppermute | solution.py:335
  120.0 9.6 %collective-permute-start.20 = (bf16[2,128,512]{2,1,0:T(8,128)(2,1)}, bf16[2,128,512]{2,1,0:T(8,128)(2,1)S(1)}, u32[]{:S(2)}, u32[]{:S(2)}) collective-permute-start(bf16[2,128,512]{2,1,0:T(8,128)(2,1)} %get-tuple-element.94), channel_id=1, source_target_pairs={{0,1},{1,0},{2,3},{3,2},{4,5},{5,4},{6,7},{7,6},{8,9},{9,8},{10,11... | collective-permute-start | bytes 786440 | tf_op jit(solution)/shard_map/ppermute | solution.py:335
  120.8 21.2 %copy-start.7 = (bf16[2,128,512]{2,1,0:T(8,128)(2,1)S(1)}, bf16[2,128,512]{2,1,0:T(8,128)(2,1)}, u32[]{:S(2)}) copy-start(bf16[2,128,512]{2,1,0:T(8,128)(2,1)} %get-tuple-element.87.refs_0_) | copy-start | bytes 786436
  123.7 25.8 %collective-permute-start.31 = (bf16[4,128,512]{2,1,0:T(8,128)(2,1)}, bf16[4,128,512]{2,1,0:T(8,128)(2,1)}, u32[]{:S(2)}, u32[]{:S(2)}) collective-permute-start(bf16[4,128,512]{2,1,0:T(8,128)(2,1)} %add_convert_fusion), channel_id=1, source_target_pairs={{0,24},{1,25},{2,26},{3,27},{4,28},{5,29},{6,30},{7,31},{8,16},{9,... | collective-permute-start | bytes 1572872 | tf_op jit(solution)/shard_map/ppermute | solution.py:324
  126.5 14.1 %collective-permute-start.28 = (bf16[2,128,512]{2,1,0:T(8,128)(2,1)}, bf16[2,128,512]{2,1,0:T(8,128)(2,1)S(1)}, u32[]{:S(2)}, u32[]{:S(2)}) collective-permute-start(bf16[2,128,512]{2,1,0:T(8,128)(2,1)} %get-tuple-element.113), channel_id=1, source_target_pairs={{0,2},{1,3},{2,0},{3,1},{4,6},{5,7},{6,4},{7,5},{8,10},{9,11},{10,... | collective-permute-start | bytes 786440 | tf_op jit(solution)/shard_map/ppermute | solution.py:335
  128.2 12.4 %collective-permute-start.29 = (bf16[2,128,512]{2,1,0:T(8,128)(2,1)}, bf16[2,128,512]{2,1,0:T(8,128)(2,1)S(1)}, u32[]{:S(2)}, u32[]{:S(2)}) collective-permute-start(bf16[2,128,512]{2,1,0:T(8,128)(2,1)} %get-tuple-element.116), channel_id=1, source_target_pairs={{0,3},{1,2},{2,1},{3,0},{4,7},{5,6},{6,5},{7,4},{8,11},{9,10},{10,... | collective-permute-start | bytes 786440 | tf_op jit(solution)/shard_map/ppermute | solution.py:335
  129.5 12.4 %collective-permute-start.27 = (bf16[2,128,512]{2,1,0:T(8,128)(2,1)}, bf16[2,128,512]{2,1,0:T(8,128)(2,1)}, u32[]{:S(2)}, u32[]{:S(2)}) collective-permute-start(bf16[2,128,512]{2,1,0:T(8,128)(2,1)} %get-tuple-element.110), channel_id=1, source_target_pairs={{0,1},{1,0},{2,3},{3,2},{4,5},{5,4},{6,7},{7,6},{8,9},{9,8},{10,11... | collective-permute-start | bytes 786440 | tf_op jit(solution)/shard_map/ppermute | solution.py:335
  141.9 7.6 %copy-start.2 = (bf16[768,256]{1,0:T(8,128)(2,1)S(1)}, bf16[768,256]{1,0:T(8,128)(2,1)}, u32[]{:S(2)}) copy-start(bf16[768,256]{1,0:T(8,128)(2,1)} %refs_2_.3) | copy-start | bytes 1179652
  141.9 7.6 %copy-start.8 = (f32[512,768]{1,0:T(8,128)S(1)}, f32[512,768]{1,0:T(8,128)}, u32[]{:S(2)}) copy-start(f32[512,768]{1,0:T(8,128)} %fusion.16.refs_1_) | copy-start | bytes 4718596
  143.4 7.8 %collective-permute-start.30 = (bf16[4,128,512]{2,1,0:T(8,128)(2,1)S(1)}, bf16[4,128,512]{2,1,0:T(8,128)(2,1)S(1)}, u32[]{:S(2)}, u32[]{:S(2)}) collective-permute-start(bf16[4,128,512]{2,1,0:T(8,128)(2,1)S(1)} %owner_sum.5), channel_id=1, source_target_pairs={{0,16},{1,17},{2,18},{3,19},{4,20},{5,21},{6,22},{7,23},{8,24},{9,... | collective-permute-start | bytes 1572872 | tf_op jit(solution)/shard_map/ppermute | solution.py:324
  (14 other events, 44.8 us)
